TPU v7x, 128 devices: a whole 4x4x4 slice. The times are simulated.
128 devices in a mesh: grp: 4 (over y_lo, core), lat: 32 (over z, x, y_hi).
Axes of the slice: x: 4, y: 4 (y_hi: 2, y_lo: 2; y = y_hi * 2 + y_lo), z: 4, core: 2. Of those that a mesh axis runs over, the one named last changes fastest.
Arguments:
- eigvecs: bfloat16 [256, 32, 6, 16384], P('grp', None, None, 'lat'), may hold values from -6 to 6
- solutions: bfloat16 [4, 32, 32, 6, 16384], P('grp', None, None, None, 'lat'), may hold values from -6 to 6
- source_index: int32 [4], replicated, may hold values from 0 to 255
- source_time: int32 [1], replicated, may hold values from 0 to 31
- dilution: int32 [4, 4], replicated, may hold values from 0 to 3, each once within a row
Outputs:
- perambulator: float32 [32, 256, 256], P('lat', 'grp')
- sources: bfloat16 [4, 4, 4, 6, 16384], P('grp', None, None, None, 'lat')
Inputs may be any that keep to these rules, and one draw needn't show every extreme that they name: `dilution`: each row is a permutation of 0 to 3.
All inputs are finite; a program needn't handle non-finite values.
Results may differ from a plain program's by a relative error of at most 0.001.
Values may be sent and summed in bfloat16 or wider, within the bound.
No kernel may reach another device: no remote copies, remote signals or barrier semaphores. Data moves between devices by JAX's collectives and lax.ppermute only.
A program may use at most 256 MiB of HBM per device.

v0:
```python
import math

import jax
import jax.numpy as jnp
from jax import lax
from jax.sharding import PartitionSpec as P

MASS = 2


def spread_2(value, axis, source):
    kept = jnp.where(lax.axis_index(axis) == source, value, 0).astype(value.dtype)
    return lax.psum(kept, axis)


def make_columns(block):
    groups, count, times, comps, sites = block.shape
    parts = block.reshape(groups, count, times, comps // 2, 2, sites)
    turned = jnp.stack([parts[:, :, :, :, 1, :], -parts[:, :, :, :, 0, :]], axis=4)
    both = jnp.stack([parts, turned], axis=2)
    return both.reshape(groups, count * 2, times, comps, sites)


def reorder(tau, dilution, masses):
    times, vecs, groups, width = tau.shape
    nsources = dilution.shape[0]
    view = tau.reshape(times, vecs, groups, masses, nsources, width // (masses * nsources))
    spin_grid = jnp.arange(groups, dtype=jnp.int32)
    mask = jnp.transpose(dilution)[None, :, :] == spin_grid[:, None, None]
    picked = jnp.where(
        mask[None, None, :, :, None, :, None], view[:, :, None], jnp.zeros((), jnp.float32)
    )
    return jnp.sum(picked, axis=3).reshape(times, vecs, groups * width)


def local(eigvecs, solutions, source_index, source_time, dilution):
    owned = eigvecs.shape[0]
    lattice = lax.axis_size("lat")
    group = lax.axis_index("grp")
    nsources = source_index.shape[0]
    spins = dilution.shape[1]
    scale = 1.0 / math.sqrt(eigvecs.shape[2] * eigvecs.shape[3] * lattice)
    slice_now = lax.dynamic_index_in_dim(eigvecs, source_time[0], 1, keepdims=False)
    owners = source_index // owned
    local_rows = source_index - owners * owned
    picked = jnp.take(slice_now, local_rows, axis=0)
    vectors = []
    for source in range(nsources):
        vectors.append(spread_2(picked[source], "grp", owners[source]))
    chosen = jnp.stack(vectors)
    my_spins = lax.dynamic_index_in_dim(dilution, group, 1, keepdims=False)
    spin_mask = jnp.arange(spins, dtype=jnp.int32)[None, :] == my_spins[:, None]
    sources = jnp.where(
        spin_mask[:, :, None, None], chosen[:, None, :, :], jnp.zeros((), jnp.bfloat16)
    )
    sources = sources[None]
    mine = make_columns(solutions)[0]
    part = jnp.einsum(
        "jtkx,ntkx->tjn",
        lax.all_gather(eigvecs, "grp", axis=0, tiled=True),
        mine,
        preferred_element_type=jnp.float32,
    )
    spread = lax.all_to_all(part[:, :, None, :], "grp", split_axis=1, concat_axis=2, tiled=True)
    sums = lax.psum_scatter(spread, "lat", scatter_dimension=0, tiled=True)
    return (reorder(sums, dilution, MASS) * scale, sources)


def solution(mesh):
    return jax.shard_map(
        local,
        mesh=mesh,
        in_specs=(P("grp", None, None, "lat"), P("grp", None, None, None, "lat"), P(), P(), P()),
        out_specs=(P("lat", "grp", None), P("grp", None, None, None, "lat")),
        check_vma=False,
    )
```

profile of v0, /device:TPU:0, one launch (start us, length us, event | category | flops | bytes accessed | tf_op | source)
XLA Modules:
  0.0 736.5 jit_solution(10460614324809678353)
XLA Ops:
  7.2 0.0 all-gather.2.cloned.1.call-start
  7.2 14.5 %copy.41 = bf16[64,32,6,512]{3,0,2,1:T(8,128)(2,1)} copy(bf16[64,32,6,512]{3,1,2,0:T(8,128)(2,1)} %param.5) | data formatting | bytes 25165824 | tf_op args[0]
  21.7 0.0 all-gather.2.cloned.1.call-update
  21.7 0.0 reduce-scatter.2.cloned.1.call-start
  21.8 0.0 slice-start
  21.8 3.4 fusion.5
  25.2 0.0 slice-start.1
  25.2 0.6 maximum_bitcast_fusion
  25.8 0.0 slice-done
  25.8 1.1 slice-done.1
  27.0 5.4 pad_maximum_fusion
  32.3 420.8 %all-gather.2.cloned.1.call-done = bf16[256,32,6,512]{3,0,2,1:T(8,128)(2,1)} async-done(((bf16[64,32,6,512]{3,0,2,1:T(8,128)(2,1)}), bf16[256,32,6,512]{3,0,2,1:T(8,128)(2,1)}) %all-gather.2.cloned.1.call-update) | async-done | bytes 50331664 | tf_op jit(solution)/shard_map/all_gather | solution.py:60
  453.1 22.8 %fusion.2 = f32[32,256,1,64]{1,3,0,2:T(8,128)S(1)} fusion(bf16[256,32,6,512]{3,0,2,1:T(8,128)(2,1)} %all-gather.2.cloned.1.call-done, bf16[64,32,6,512]{3,1,2,0:T(8,128)(2,1)} %bitcast.34), kind=kOutput, calls=%fused_computation.7 | convolution fusion | flops 3221225472 | bytes 65011712 | tf_op jit(solution)/shard_map/jtkx,ntkx->tjn/dot_general | solution.py:58
  475.9 4.5 copy.42
  480.4 4.5 reshape.100
  484.9 29.5 %all_to_all.18 = f32[4,1,131072]{2,1,0:T(1,128)} all-to-all(f32[4,1,131072]{2,1,0:T(1,128)S(1)} %reshape.100), channel_id=1, replica_groups=mesh['grp'=4,'lat'=32] {'grp'}, dimensions={0} | all-to-all | bytes 4194304 | tf_op jit(solution)/shard_map/all_to_all | solution.py:64
  514.4 0.5 broadcast.125
  514.9 7.7 %reduce.3 = f32[4,131072]{1,0:T(4,128)S(1)} reduce(f32[4,1,131072]{2,1,0:T(1,128)} %all_to_all.18, f32[]{:T(128)} %broadcast.125), dimensions={1}, to_apply=%all_to_all.13.reduce_sub_computation | reduce | bytes 4194308 | tf_op jit(solution)/shard_map/all_to_all | solution.py:64
  522.6 4.0 reshape.101
  526.6 0.0 copy-start.1
  526.6 0.0 copy-start
  526.6 6.6 copy.55
  533.2 0.0 reduce-scatter.2.cloned.1.call-update
  533.8 1.0 dynamic-slice_bitcast_fusion
  534.9 0.2 copy.46
  535.1 0.0 copy-done.1
  535.1 0.7 fusion.6
  538.3 0.0 copy-done
  538.3 0.2 dynamic-slice_reduce_fusion
  538.5 0.1 copy.39
  538.6 0.5 gather_fusion
  539.2 0.1 broadcast_select_fusion.1
  539.3 10.7 %all-reduce = (bf16[1,6,512]{2,1,0:T(8,128)(2,1)S(1)}, bf16[1,6,512]{2,1,0:T(8,128)(2,1)S(1)}, bf16[1,6,512]{2,1,0:T(8,128)(2,1)S(1)}, bf16[1,6,512]{2,1,0:T(8,128)(2,1)S(1)}) all-reduce(bf16[1,6,512]{2,1,0:T(8,128)(2,1)S(1)} %get-tuple-element.20, ...), channel_id=1, replica_groups=mesh['grp'=4,'lat'=32] {'grp'}, use_global_device_ids=true, to_apply=%region_5.6 | all-reduce | flops 12288 | bytes 49152 | tf_op jit(solution)/shard_map/psum | solution.py:13
  550.0 0.1 iota_compare_fusion.1
  550.1 0.7 broadcast_select_fusion
  550.9 176.9 %reduce-scatter.2.cloned.1.call-done = f32[1,64,4,64]{3,1,2,0:T(8,128)} async-done(((f32[32,64,4,64]{3,1,2,0:T(8,128)}), f32[1,64,4,64]{3,1,2,0:T(8,128)}) %reduce-scatter.2.cloned.1.call-update) | async-done | bytes 65552 | tf_op jit(solution)/shard_map/reduce_scatter | solution.py:65
  727.8 1.0 copy.44
  728.8 0.1 select_reduce_fusion
  729.0 0.7 copy.47
  (7 shorter events, 0.1 us)
Async XLA Ops:
  7.2 445.9 %all-gather.2.cloned.1.call-start = ((), (), s32[]{:S(2)}) async-start(), calls=%async_computation.2 | async-start | bytes 62914560 | tf_op jit(solution)/shard_map/all_gather | solution.py:60
  21.7 706.1 %reduce-scatter.2.cloned.1.call-start = ((), (), s32[]{:S(2)}) async-start(), calls=%async_computation.3 | async-start | bytes 4325376 | tf_op jit(solution)/shard_map/reduce_scatter | solution.py:65
  21.8 4.1 slice-start
  25.2 1.8 slice-start.1
  526.6 8.5 %copy-start.1 = (s32[4]{0:T(128)S(1)}, s32[4]{0:T(128)}, u32[]{:S(2)}) copy-start(s32[4]{0:T(128)} %param.7) | copy-start | bytes 52
  526.6 11.8 %copy-start = (s32[4,4]{1,0:T(4,128)S(1)}, s32[4,4]{1,0:T(4,128)}, u32[]{:S(2)}) copy-start(s32[4,4]{1,0:T(4,128)} %param.9) | copy-start | bytes 196
Sparse Core Ops, SparseCore 0:
  21.8 431.2 all-gather.1
  533.3 194.4 reduce-scatter.1
where the time goes:
time: 737 us
  waiting for transfers between devices  598 us (81%)
  blocking collectives  40.2 us (5%)
  local copies, waits for them, and re-layouts  40.1 us (5%)
  matrix products  22.8 us (3%)
  other arithmetic  18.2 us (2%)
  between operations  17.4 us (2%)
    all_gather x1, waiting for transfers between devices, local(): lax.all_gather(eigvecs, 'grp', axis=0, tiled=True)  421 us
    reduce_scatter x1, waiting for transfers between devices, local(): sums = lax.psum_scatter(spread, 'lat', scatter_dimension=0, tiled=True)  177 us
    all_to_all x1, blocking collectives, local(): lax.all_to_all(part[:, :, None, :], 'grp', split_axis=1, concat_axis=2, t...  29.5 us
    unnamed x12, local copies, waits for them, and re-layouts  24.8 us
    dot_general x1, matrix products, local(): jnp.einsum('jtkx,ntkx->tjn', lax.all_gather(eigvecs, 'grp', axis=0, tiled...  22.8 us
  transfers between devices with their start and end apart: 2, of which 2 were waited for; matrix products, arithmetic and copies ran while one was open for 2% of the time, Pallas kernels for 0%

commit v1 on v0

v1 whole, which is shorter than its diff:
```python
import functools
import math

import jax
import jax.numpy as jnp
from jax import lax
from jax.experimental import pallas as pl
from jax.experimental.pallas import tpu as pltpu
from jax.sharding import Mesh
from jax.sharding import PartitionSpec as P

MASS = 2
RAW = 8
SWAP = [(0, 1), (1, 0)]


def tie(value, *after):
    return lax.optimization_barrier((value, *after))[0]


def swap(value, axis):
    return lax.ppermute(value, axis, SWAP)


def by_time(block):
    n, _, comps, sites = block.shape
    parts = block.reshape(n, 4, 4, 2, comps, sites).transpose(2, 1, 3, 4, 0, 5)
    return parts.reshape(4, 8, comps // 2, 2 * n, sites)


def dot_kernel(count, *refs):
    cols, (own, other), outs = refs[:count], refs[count : count + 2], refs[count + 2 :]
    width = own.shape[3] // 2
    for at in range(own.shape[1]):
        for col, out in zip(cols, outs):
            n = col.shape[3] // 2
            halves = []
            for vecs in (own, other):
                total = None
                for colour in range(vecs.shape[2]):
                    term = lax.dot_general(
                        col[0, at, colour],
                        vecs[0, at, colour],
                        (((1,), (1,)), ((), ())),
                        preferred_element_type=jnp.float32,
                    )
                    total = term if total is None else total + term
                real = total[:n, :width] + total[n:, width:]
                imag = total[n:, :width] - total[:n, width:]
                halves.append((real, imag))
            for part in range(2):
                out[0, at, part] = jnp.concatenate([halves[0][part], halves[1][part]], axis=1)


def project(cols, own, other, first, size, step):
    _, inner, colours, rows, sites = own.shape
    spec = lambda n, off: pl.BlockSpec(
        (1, step, colours, n, sites), lambda i, j, off=off: (i + off, j, 0, 0, 0)
    )
    in_specs = [spec(c.shape[3], 0) for c in cols] + [spec(rows, first)] * 2
    out_specs = [
        pl.BlockSpec((1, step, 2, c.shape[3] // 2, rows), lambda i, j: (i, j, 0, 0, 0))
        for c in cols
    ]
    out_shape = [
        jax.ShapeDtypeStruct((size, inner, 2, c.shape[3] // 2, rows), jnp.float32) for c in cols
    ]
    total = sum(c.shape[3] for c in cols)
    return pl.pallas_call(
        functools.partial(dot_kernel, len(cols)),
        grid=(size, inner // step),
        in_specs=in_specs,
        out_specs=out_specs,
        out_shape=out_shape,
        compiler_params=pltpu.CompilerParams(vmem_limit_bytes=48 * 2**20),
        cost_estimate=pl.CostEstimate(
            flops=2 * size * inner * colours * sites * total * 2 * rows,
            bytes_accessed=2 * size * inner * colours * sites * (total + 2 * rows),
            transcendentals=0,
        ),
        name="project",
    )(*cols, own, other)


def pick(value, index):
    return lax.dynamic_index_in_dim(value, index, 0, keepdims=False)


def sum_z(part):
    me = lax.axis_index("z")
    slabs = jnp.swapaxes(part, 0, 1)
    total = pick(slabs, me)
    got = [
        lax.ppermute(pick(slabs, (me + k) % 4), "z", [(i, (i + k) % 4) for i in range(4)])
        for k in (1, 3, 2)
    ]
    return total + got[0] + got[1] + got[2]


def sum_x(part, first, size):
    me = lax.axis_index("x")
    clip = lambda i: jnp.clip(i - first, 0, size - 1)
    total = pick(part, clip(me)) if size > 1 else part[0]
    for k in (1, 3, 2):
        send = pick(part, clip((me + k) % 4)) if size > 1 else part[0]
        pairs = [(i, (i + k) % 4) for i in range(4) if first <= (i + k) % 4 < first + size]
        total = total + lax.ppermute(send, "x", pairs)
    return total


def sum_yh(part):
    me = lax.axis_index("yh")
    return pick(part, me) + swap(pick(part, 1 - me), "yh")


def local(eigvecs, solutions, source_index, source_time, dilution):
    owned, times, comps, sites = eigvecs.shape
    count = solutions.shape[1]
    nsources, spins = dilution.shape
    scale = 1.0 / math.sqrt(comps * sites * 32)
    core = lax.axis_index("c")
    group = 2 * lax.axis_index("yl") + core
    sols = solutions[0]

    raw = swap(sols[:RAW], "yl")
    mine = by_time(sols)
    late = by_time(sols[RAW:])
    send = [late[x] for x in range(4)]
    got = [swap(send[0], "yl")]
    got.append(swap(tie(send[1], raw), "yl"))
    got.append(swap(tie(send[2], got[0]), "yl"))
    got.append(swap(tie(send[3], got[1]), "yl"))

    own = by_time(eigvecs)
    other = swap(own, "c")

    def rows(part):
        x, inner, _, n, lanes = part.shape
        return part.reshape(x, 4, 2, 2 * n, lanes)

    a, b = project([mine, by_time(raw)], own, other, 0, 4, 4)
    first = sum_x(sum_z(jnp.concatenate([rows(a), rows(b)], axis=3)), 0, 4)
    tail = []
    mid = [project([got[x][None]], own, other, x, 1, 4)[0] for x in range(3)]
    mid = sum_x(sum_z(rows(jnp.concatenate(mid, axis=0))), 0, 3)
    last = project([got[3][None]], own, other, 3, 1, 4)[0]
    last = sum_x(sum_z(rows(last)), 3, 1)

    main = sum_yh(jnp.concatenate([first, mid], axis=1))
    main_c = swap(main, "c")
    last = sum_yh(last)
    last_c = swap(last, "c")
    is_last = lax.axis_index("x") == 3

    def assemble(main, last, half):
        main = main[:, half * owned : (half + 1) * owned]
        last = last[:, half * owned : (half + 1) * owned]
        n0, n1 = 2 * count, 2 * count + 2 * RAW
        home = main[:n0].reshape(2, count, owned)
        early = main[n0:n1].reshape(2, RAW, owned)
        rest = jnp.where(is_last, last, main[n1:]).reshape(2, count - RAW, owned)
        return home, jnp.concatenate([early, rest], axis=1)

    h0, y0 = assemble(main, last, 0)
    h1, y1 = assemble(main_c, last_c, 1)
    tau = jnp.stack([h0, h1, y0, y1])
    order = jnp.stack([group, group ^ 1, group ^ 2, group ^ 3])
    spin_of = jnp.take(jnp.transpose(dilution), order, axis=0)
    mask = spin_of[:, None, :] == jnp.arange(spins, dtype=jnp.int32)[None, :, None]
    view = tau.reshape(4, 1, 2, MASS, nsources, count // (MASS * nsources), owned)
    picked = jnp.where(mask[:, :, None, None, :, None, None], view, 0.0)
    result = jnp.sum(picked, axis=0).reshape(spins, 2, count, owned) * scale
    result = result.transpose(3, 0, 2, 1).reshape(1, owned, spins * count * 2)

    slice_now = lax.dynamic_index_in_dim(eigvecs, source_time[0], 1, keepdims=False)
    owners = source_index // owned
    chosen = jnp.take(slice_now, source_index - owners * owned, axis=0)
    chosen = jnp.where((owners == group)[:, None, None], chosen, 0).astype(jnp.bfloat16)
    chosen = chosen + swap(chosen, "c")
    chosen = chosen + swap(chosen, "yl")
    my_spins = lax.dynamic_index_in_dim(dilution, group, 1, keepdims=False)
    spin_mask = jnp.arange(spins, dtype=jnp.int32)[None, :] == my_spins[:, None]
    sources = jnp.where(
        spin_mask[:, :, None, None], chosen[:, None, :, :], jnp.zeros((), jnp.bfloat16)
    )
    return result, sources[None]


def solution(mesh):
    split = Mesh(mesh.devices.reshape(2, 2, 4, 4, 2), ("yl", "c", "z", "x", "yh"))
    grp, lat = ("yl", "c"), ("z", "x", "yh")
    return jax.shard_map(
        local,
        mesh=split,
        in_specs=(P(grp, None, None, lat), P(grp, None, None, None, lat), P(), P(), P()),
        out_specs=(P(lat, grp, None), P(grp, None, None, None, lat)),
        check_vma=False,
    )
```

time: 737 us -> 277 us (0.38)
  waiting for transfers between devices: 598 us -> 99 us
  starting transfers between devices: 0.08 us -> 45.6 us
  local copies, waits for them, and re-layouts: 40.1 us -> 85.3 us
  blocking collectives: 40.2 us -> 0 us
  Pallas kernels: 0 us -> 37.2 us
  matrix products: 22.8 us -> 0 us
  between operations: 17.4 us -> 1.71 us
  other arithmetic: 18.2 us -> 5.55 us
    all_gather x1 -> x0, waiting for transfers between devices: 421 us -> none  [local(): lax.all_gather(eigvecs, 'grp', axis=0, tiled=True)]
    reduce_scatter x1 -> x0, waiting for transfers between devices: 177 us -> none  [local(): sums = lax.psum_scatter(spread, 'lat', scatter_dimension=0, tiled=True)]
    ppermute x0 -> x30, waiting for transfers between devices: none -> 99 us  [the longest x12 88.6 us: swap(): return lax.ppermute(value, axis, SWAP)]
    reshape x0 -> x8, local copies, waits for them, and re-layouts: none -> 52.7 us  [the longest x6 52.6 us: by_time(): parts = block.reshape(n, 4, 4, 2, comps, sites).transpose(2, 1, 3, 4, 0, 5)]
    ppermute x0 -> x30, starting transfers between devices: none -> 45.6 us  [the longest x9 19.3 us: sum_x(): total = total + lax.ppermute(send, 'x', pairs)]
    pallas_call x0 -> x5, Pallas kernels: none -> 37.2 us  [project(): pl.pallas_call(functools.partial(dot_kernel, len(cols)), grid=(size, inne...]
    all_to_all x1 -> x0, blocking collectives: 29.5 us -> none  [local(): lax.all_to_all(part[:, :, None, :], 'grp', split_axis=1, concat_axis=2, t...]
    unnamed x12, local copies, waits for them, and re-layouts: 24.8 us -> 0.83 us
  transfers between devices with their start and end apart: 2 -> 30, of which waited for: 2 -> 10; matrix products, arithmetic and copies ran while one was open for 2% -> 20% of each run, Pallas kernels for 0% -> 14%
where the time goes in v1:
time: 277 us; the launch traced here: 274 us
  waiting for transfers between devices  99 us (36%)
  local copies, waits for them, and re-layouts  85.3 us (31%)
  starting transfers between devices  45.6 us (16%)
  Pallas kernels  37.2 us (13%)
  other arithmetic  5.55 us (2%)
    ppermute x12, waiting for transfers between devices, swap(): return lax.ppermute(value, axis, SWAP)  88.6 us
    reshape x6, local copies, waits for them, and re-layouts, by_time(): parts = block.reshape(n, 4, 4, 2, comps, sites).transpose(2, 1, 3, 4, 0, 5)  52.6 us
    pallas_call x5, Pallas kernels, project(): pl.pallas_call(functools.partial(dot_kernel, len(cols)), grid=(size, inne...  37.2 us
    ppermute x9, starting transfers between devices, sum_x(): total = total + lax.ppermute(send, 'x', pairs)  19.3 us
    another operation x2, local copies, waits for them, and re-layouts, by_time(): parts = block.reshape(n, 4, 4, 2, comps, sites).transpose(2, 1, 3, 4, 0, 5)  19.2 us
    ppermute x12, starting transfers between devices, swap(): return lax.ppermute(value, axis, SWAP)  13.2 us
    ppermute x9, starting transfers between devices, sum_z(): lax.ppermute(pick(slabs, (me + k) % 4), 'z', [(i, (i + k) % 4) for i in r...  13.1 us
    ppermute x9, waiting for transfers between devices, sum_x(): total = total + lax.ppermute(send, 'x', pairs)  5.63 us
  transfers between devices with their start and end apart: 30, of which 10 were waited for; matrix products, arithmetic and copies ran while one was open for 20% of the time, Pallas kernels for 14%

profile of v1, /device:TPU:0, one launch (start us, length us, event | category | flops | bytes accessed | tf_op | source)
XLA Modules:
  0.0 274.4 jit_solution(10385336976357343064)
XLA Ops:
  0.6 19.0 %reshape.317 = bf16[64,4,4,2,6,512]{5,3,2,1,4,0:T(2,128)(2,1)} reshape(bf16[64,32,6,512]{3,1,2,0:T(8,128)(2,1)} %param.5) | data formatting | bytes 25165824 | tf_op jit(solution)/shard_map/reshape | solution.py:27
  19.6 14.6 %copy.23 = bf16[64,4,4,2,6,512]{5,0,4,3,1,2:T(8,128)(2,1)} copy(bf16[64,4,4,2,6,512]{5,3,2,1,4,0:T(2,128)(2,1)} %reshape.317) | data formatting | bytes 25165824 | tf_op jit(solution)/shard_map/reshape | solution.py:27
  34.3 1.2 slice_bitcast_fusion
  35.5 1.7 collective-permute-start
  37.2 2.6 slice.60
  39.8 8.1 %reshape.321 = bf16[24,4,4,2,6,512]{5,3,2,1,4,0:T(2,128)(2,1)} reshape(bf16[1,24,32,6,512]{4,2,3,1,0:T(8,128)(2,1)} %slice.60) | data formatting | bytes 9437184 | tf_op jit(solution)/shard_map/reshape | solution.py:27
  47.9 5.0 %copy.33 = bf16[24,4,4,2,6,512]{5,0,4,3,1,2:T(8,128)(2,1)S(1)} copy(bf16[24,4,4,2,6,512]{5,3,2,1,4,0:T(2,128)(2,1)} %reshape.321) | data formatting | bytes 9437184 | tf_op jit(solution)/shard_map/reshape | solution.py:27
  52.9 1.9 fusion.27
  54.7 0.4 collective-permute-start.8
  55.8 17.2 %collective-permute-done = bf16[8,32,6,512]{3,1,2,0:T(8,128)(2,1)} collective-permute-done((bf16[8,32,6,512]{3,1,2,0:T(8,128)(2,1)}, bf16[8,32,6,512]{3,1,2,0:T(8,128)(2,1)}, u32[]{:S(2)}, u32[]{:S(2)}) %collective-permute-start) | collective-permute-done | bytes 1572896 | tf_op jit(solution)/shard_map/ppermute | solution.py:22
  73.0 1.7 collective-permute-start.9
  74.7 2.7 constant_dynamic-slice_fusion
  77.4 1.0 copy.34
  78.4 2.2 gather_fusion.1
  80.6 1.5 select_select_fusion
  82.0 0.1 copy.20
  82.2 0.6 gather_fusion
  82.9 15.2 %collective-permute-done.8 = bf16[8,3,48,512]{3,2,1,0:T(8,128)(2,1)S(1)} collective-permute-done((bf16[8,3,48,512]{3,2,1,0:T(8,128)(2,1)S(1)}, bf16[8,3,48,512]{3,2,1,0:T(8,128)(2,1)S(1)}, u32[]{:S(2)}, u32[]{:S(2)}) %collective-permute-start.8) | collective-permute-done | bytes 1179680 | tf_op jit(solution)/shard_map/ppermute | solution.py:22
  98.2 1.7 collective-permute-start.10
  99.8 23.6 %collective-permute-done.9 = bf16[8,3,48,512]{3,2,1,0:T(8,128)(2,1)S(1)} collective-permute-done((bf16[8,3,48,512]{3,2,1,0:T(8,128)(2,1)}, bf16[8,3,48,512]{3,2,1,0:T(8,128)(2,1)S(1)}, u32[]{:S(2)}, u32[]{:S(2)}) %collective-permute-start.9) | collective-permute-done | bytes 1179680 | tf_op jit(solution)/shard_map/ppermute | solution.py:22
  123.5 1.7 collective-permute-start.19
  125.1 0.2 fusion.25
  125.3 1.5 fusion.28
  126.8 0.4 collective-permute-start.29
  127.2 10.2 %reshape_squeeze.3 = bf16[32,4,4,2,6,512]{5,3,2,1,4,0:T(2,128)(2,1)} reshape(bf16[1,32,32,6,512]{4,2,3,1,0:T(8,128)(2,1)} %param.6) | data formatting | bytes 12582912 | tf_op jit(solution)/shard_map/reshape;squeeze | solution.py:27
  137.4 9.0 %copy.21 = bf16[32,4,4,2,6,512]{5,0,4,3,1,2:T(8,128)(2,1)} copy(bf16[32,4,4,2,6,512]{5,3,2,1,4,0:T(2,128)(2,1)} %reshape_squeeze.3) | data formatting | bytes 12582912 | tf_op jit(solution)/shard_map/reshape;squeeze | solution.py:27
  146.4 28.0 %collective-permute-done.29 = bf16[4,6,512]{2,1,0:T(8,128)(2,1)} collective-permute-done((bf16[4,6,512]{2,1,0:T(8,128)(2,1)}, bf16[4,6,512]{2,1,0:T(8,128)(2,1)}, u32[]{:S(2)}, u32[]{:S(2)}) %collective-permute-start.29) | collective-permute-done | bytes 24608 | tf_op jit(solution)/shard_map/ppermute | solution.py:22
  174.4 0.8 add.241
  175.2 0.7 broadcast_select_fusion
  176.0 3.6 %reshape.315 = bf16[8,4,4,2,6,512]{5,3,2,1,4,0:T(2,128)(2,1)} reshape(bf16[8,32,6,512]{3,1,2,0:T(8,128)(2,1)} %collective-permute-done) | data formatting | bytes 3145728 | tf_op jit(solution)/shard_map/reshape | solution.py:27
  179.6 2.3 copy.22
  181.9 19.1 %project.5 = (f32[4,8,2,32,128]{4,3,2,1,0:T(8,128)S(1)}, f32[4,8,2,8,128]{4,3,2,1,0:T(8,128)S(1)}) custom-call(bf16[4,8,3,64,512]{4,3,2,1,0:T(8,128)(2,1)} %bitcast.163, bf16[4,8,3,16,512]{4,3,2,1,0:T(8,128)(2,1)S(1)} %bitcast.153, bf16[4,8,3,128,512]{4,3,2,1,0:T(8,128)(2,1)} %bitcast.16.refs_2_.refs_1_, ...), custom_call_target="tpu_custom_call" | custom-call | flops 2013265920 | bytes 33030144 | tf_op jit(solution)/shard_map/project/pallas_call | solution.py:69
  201.1 4.0 %collective-permute-start.4 = (f32[4,2,80,128]{3,2,1,0:T(8,128)S(1)}, f32[4,2,80,128]{3,2,1,0:T(8,128)S(1)}, u32[]{:S(2)}, u32[]{:S(2)}) collective-permute-start(f32[4,2,80,128]{3,2,1,0:T(8,128)S(1)} %get-tuple-element.26), channel_id=1, source_target_pairs={{0,16},{8,24},{16,0},{24,8},{1,17},{9,25},{17,1},{25,9},{2,18},{10... | collective-permute-start | bytes 983048 | tf_op jit(solution)/shard_map/ppermute | solution.py:94
  205.2 0.7 collective-permute-start.3
  205.9 4.6 %project.9 = f32[1,8,2,24,128]{4,3,2,1,0:T(8,128)S(1)} custom-call(bf16[1,8,3,48,512]{4,3,2,1,0:T(8,128)(2,1)} %bitcast.50.refs_0_, bf16[4,8,3,128,512]{4,3,2,1,0:T(8,128)(2,1)} %bitcast.16.refs_2_.refs_1_, bf16[4,8,3,128,512]{4,3,2,1,0:T(8,128)(2,1)} %collective-permute-done.1.refs_3_.refs_2_), custom_call_target="tpu_custom_call" | custom-call | flops 301989888 | bytes 7471104 | tf_op jit(solution)/shard_map/project/pallas_call | solution.py:69
  210.6 2.5 collective-permute-start.22
  213.0 1.6 collective-permute-start.21
  214.7 0.4 collective-permute-start.20
  215.1 4.5 %project.8 = f32[1,8,2,24,128]{4,3,2,1,0:T(8,128)S(1)} custom-call(bf16[1,8,3,48,512]{4,3,2,1,0:T(8,128)(2,1)S(1)} %bitcast.158, bf16[4,8,3,128,512]{4,3,2,1,0:T(8,128)(2,1)} %bitcast.16.refs_2_.refs_1_, bf16[4,8,3,128,512]{4,3,2,1,0:T(8,128)(2,1)} %collective-permute-done.1.refs_3_.refs_2_), custom_call_target="tpu_custom_call" | custom-call | flops 301989888 | bytes 7471104 | tf_op jit(solution)/shard_map/project/pallas_call | solution.py:69
  219.5 4.5 %project.7 = f32[1,8,2,24,128]{4,3,2,1,0:T(8,128)S(1)} custom-call(bf16[1,8,3,48,512]{4,3,2,1,0:T(8,128)(2,1)S(1)} %bitcast.157, bf16[4,8,3,128,512]{4,3,2,1,0:T(8,128)(2,1)} %bitcast.16.refs_2_.refs_1_, bf16[4,8,3,128,512]{4,3,2,1,0:T(8,128)(2,1)} %collective-permute-done.1.refs_3_.refs_2_), custom_call_target="tpu_custom_call" | custom-call | flops 301989888 | bytes 7471104 | tf_op jit(solution)/shard_map/project/pallas_call | solution.py:69
  224.0 4.5 %project.6 = f32[1,8,2,24,128]{4,3,2,1,0:T(8,128)S(1)} custom-call(bf16[1,8,3,48,512]{4,3,2,1,0:T(8,128)(2,1)S(1)} %bitcast.156, bf16[4,8,3,128,512]{4,3,2,1,0:T(8,128)(2,1)} %bitcast.16.refs_2_.refs_1_, bf16[4,8,3,128,512]{4,3,2,1,0:T(8,128)(2,1)} %collective-permute-done.1.refs_3_.refs_2_), custom_call_target="tpu_custom_call" | custom-call | flops 301989888 | bytes 7471104 | tf_op jit(solution)/shard_map/project/pallas_call | solution.py:69
  228.6 0.7 collective-permute-start.25
  229.3 5.3 %collective-permute-start.24 = (f32[2,48,128]{2,1,0:T(8,128)S(1)}, f32[2,48,128]{2,1,0:T(8,128)S(1)}, u32[]{:S(2)}, u32[]{:S(2)}) collective-permute-start(f32[2,48,128]{2,1,0:T(8,128)S(1)} %fusion.22), channel_id=1, source_target_pairs={{0,6},{1,7},{8,14},{9,15},{16,22},{17,23},{24,30},{25,31},{32,38},... | collective-permute-start | bytes 147464 | tf_op jit(solution)/shard_map/ppermute | solution.py:107
  234.6 0.7 collective-permute-start.23
  235.3 1.2 collective-permute-start.13
  236.5 2.6 collective-permute-start.12
  239.2 3.5 %collective-permute-done.13 = f32[3,2,48,128]{3,2,1,0:T(8,128)S(1)} collective-permute-done((f32[3,2,48,128]{3,2,1,0:T(8,128)S(1)}, f32[3,2,48,128]{3,2,1,0:T(8,128)S(1)}, u32[]{:S(2)}, u32[]{:S(2)}) %collective-permute-start.13) | collective-permute-done | bytes 147488 | tf_op jit(solution)/shard_map/ppermute | solution.py:94
  242.7 1.3 collective-permute-done.12
  244.0 3.2 %collective-permute-start.26 = (f32[48,128]{1,0:T(8,128)S(1)}, f32[48,128]{1,0:T(8,128)S(1)}, u32[]{:S(2)}, u32[]{:S(2)}) collective-permute-start(f32[48,128]{1,0:T(8,128)S(1)} %dynamic-slice_bitcast_fusion.12), channel_id=1, source_target_pairs={{0,1},{1,0},{2,3},{3,2},{4,5},{5,4},{6,7},{7,6},{8,9},{9,8},{10,11... | collective-permute-start | bytes 73736 | tf_op jit(solution)/shard_map/ppermute | solution.py:22
  247.3 4.1 %collective-permute-start.16 = (f32[2,48,128]{2,1,0:T(8,128)S(1)}, f32[2,48,128]{2,1,0:T(8,128)S(1)}, u32[]{:S(2)}, u32[]{:S(2)}) collective-permute-start(f32[2,48,128]{2,1,0:T(8,128)S(1)} %get-tuple-element.37), channel_id=1, source_target_pairs={{0,4},{4,0},{6,2},{1,5},{5,1},{7,3},{8,12},{12,8},{14,10},{9,13},{... | collective-permute-start | bytes 147464 | tf_op jit(solution)/shard_map/ppermute | solution.py:107
  251.4 1.3 collective-permute-start.15
  252.7 4.6 %collective-permute-start.14 = (f32[2,48,128]{2,1,0:T(8,128)S(1)}, f32[2,48,128]{2,1,0:T(8,128)S(1)}, u32[]{:S(2)}, u32[]{:S(2)}) collective-permute-start(f32[2,48,128]{2,1,0:T(8,128)S(1)} %get-tuple-element.36), channel_id=1, source_target_pairs={{0,2},{2,4},{6,0},{1,3},{3,5},{7,1},{8,10},{10,12},{14,8},{9,11},{... | collective-permute-start | bytes 147464 | tf_op jit(solution)/shard_map/ppermute | solution.py:107
  257.3 0.1 collective-permute-start.7
  257.5 2.7 collective-permute-start.6
  260.2 3.2 %collective-permute-done.7 = f32[2,80,128]{2,1,0:T(8,128)S(1)} collective-permute-done((f32[2,80,128]{2,1,0:T(8,128)S(1)}, f32[2,80,128]{2,1,0:T(8,128)S(1)}, u32[]{:S(2)}, u32[]{:S(2)}) %collective-permute-start.7) | collective-permute-done | bytes 81952 | tf_op jit(solution)/shard_map/ppermute | solution.py:107
  263.4 2.4 collective-permute-done.5
  265.8 2.5 collective-permute-start.17
  268.3 0.1 collective-permute-start.27
  268.4 3.3 %collective-permute-done.17 = f32[128,128]{1,0:T(8,128)S(1)} collective-permute-done((f32[128,128]{1,0:T(8,128)S(1)}, f32[128,128]{1,0:T(8,128)S(1)}, u32[]{:S(2)}, u32[]{:S(2)}) %collective-permute-start.17) | collective-permute-done | bytes 65568 | tf_op jit(solution)/shard_map/ppermute | solution.py:22
  271.7 0.1 collective-permute-start.18
  271.8 1.2 collective-permute-done.18
  273.3 0.2 select_reduce_fusion
  273.6 0.1 copy.25
  273.7 0.7 copy.28
  (70 shorter events, 1.2 us)
Async XLA Ops:
  19.6 14.6 %copy-start = (bf16[1,32,32,6,512]{4,2,3,1,0:T(8,128)(2,1)S(1)}, bf16[1,32,32,6,512]{4,2,3,1,0:T(8,128)(2,1)}, u32[]{:S(2)}) copy-start(bf16[1,32,32,6,512]{4,2,3,1,0:T(8,128)(2,1)} %param.6) | copy-start | bytes 18874372
  34.3 147.6 %collective-permute-start.1 = (bf16[4,8,3,128,512]{4,3,2,1,0:T(8,128)(2,1)}, bf16[4,8,3,128,512]{4,3,2,1,0:T(8,128)(2,1)}, u32[]{:S(2)}, u32[]{:S(2)}) collective-permute-start(bf16[4,8,3,128,512]{4,3,2,1,0:T(8,128)(2,1)} %bitcast.16.refs_2_.refs_1_), channel_id=1, source_target_pairs={{0,32},{32,0},{1,33},{33,1},{2,34},{34,2},{3,35},{35,3},{4,36},{36... | collective-permute-start | bytes 37748744 | tf_op jit(solution)/shard_map/ppermute | solution.py:22
  35.5 37.5 %collective-permute-start = (bf16[8,32,6,512]{3,1,2,0:T(8,128)(2,1)}, bf16[8,32,6,512]{3,1,2,0:T(8,128)(2,1)}, u32[]{:S(2)}, u32[]{:S(2)}) collective-permute-start(bf16[8,32,6,512]{3,1,2,0:T(8,128)(2,1)} %slice_bitcast_fusion), channel_id=1, source_target_pairs={{0,64},{64,0},{1,65},{65,1},{2,66},{66,2},{3,67},{67,3},{4,68},{68... | collective-permute-start | bytes 4718600 | tf_op jit(solution)/shard_map/ppermute | solution.py:22
  52.8 2.9 %copy-start.4 = (s32[4]{0:T(128)S(1)}, s32[4]{0:T(128)}, u32[]{:S(2)}) copy-start(s32[4]{0:T(128)} %param.7) | copy-start | bytes 52
  54.7 43.5 %collective-permute-start.8 = (bf16[8,3,48,512]{3,2,1,0:T(8,128)(2,1)S(1)}, bf16[8,3,48,512]{3,2,1,0:T(8,128)(2,1)S(1)}, u32[]{:S(2)}, u32[]{:S(2)}) collective-permute-start(bf16[8,3,48,512]{3,2,1,0:T(8,128)(2,1)S(1)} %bitcast.169), channel_id=1, source_target_pairs={{0,64},{64,0},{1,65},{65,1},{2,66},{66,2},{3,67},{67,3},{4,68},{68... | collective-permute-start | bytes 3538952 | tf_op jit(solution)/shard_map/ppermute | solution.py:22
  55.8 24.8 %copy-start.2 = (pred[4]{0:T(512)(128)(4,1)}, pred[4]{0:T(512)(128)(4,1)S(1)}, u32[]{:S(2)}) copy-start(pred[4]{0:T(512)(128)(4,1)S(1)} %get-tuple-element.16) | copy-start | bytes 16
  73.0 9.0 %copy-start.1 = (s32[4,4]{1,0:T(4,128)S(1)}, s32[4,4]{1,0:T(4,128)}, u32[]{:S(2)}) copy-start(s32[4,4]{1,0:T(4,128)} %param.9) | copy-start | bytes 196
  73.0 50.5 %collective-permute-start.9 = (bf16[8,3,48,512]{3,2,1,0:T(8,128)(2,1)}, bf16[8,3,48,512]{3,2,1,0:T(8,128)(2,1)S(1)}, u32[]{:S(2)}, u32[]{:S(2)}) collective-permute-start(bf16[8,3,48,512]{3,2,1,0:T(8,128)(2,1)} %bitcast.31), channel_id=1, source_target_pairs={{0,64},{64,0},{1,65},{65,1},{2,66},{66,2},{3,67},{67,3},{4,68},{68... | collective-permute-start | bytes 3538952 | tf_op jit(solution)/shard_map/ppermute | solution.py:22
  78.4 3.8 %copy-start.3 = (pred[4]{0:T(512)(128)(4,1)}, pred[4]{0:T(512)(128)(4,1)S(1)}, u32[]{:S(2)}) copy-start(pred[4]{0:T(512)(128)(4,1)S(1)} %get-tuple-element.18) | copy-start | bytes 16
  82.0 43.3 %collective-permute-start.28 = (bf16[4,6,512]{2,1,0:T(8,128)(2,1)}, bf16[4,6,512]{2,1,0:T(8,128)(2,1)}, u32[]{:S(2)}, u32[]{:S(2)}) collective-permute-start(bf16[4,6,512]{2,1,0:T(8,128)(2,1)} %select_select_fusion), channel_id=1, source_target_pairs={{0,32},{32,0},{1,33},{33,1},{2,34},{34,2},{3,35},{35,3},{4,36},{36... | collective-permute-start | bytes 73736 | tf_op jit(solution)/shard_map/ppermute | solution.py:22
  98.2 116.5 %collective-permute-start.10 = (bf16[8,3,48,512]{3,2,1,0:T(8,128)(2,1)}, bf16[8,3,48,512]{3,2,1,0:T(8,128)(2,1)S(1)}, u32[]{:S(2)}, u32[]{:S(2)}) collective-permute-start(bf16[8,3,48,512]{3,2,1,0:T(8,128)(2,1)} %bitcast.167), channel_id=1, source_target_pairs={{0,64},{64,0},{1,65},{65,1},{2,66},{66,2},{3,67},{67,3},{4,68},{68... | collective-permute-start | bytes 3538952 | tf_op jit(solution)/shard_map/ppermute | solution.py:22
  123.5 82.4 %collective-permute-start.19 = (bf16[8,3,48,512]{3,2,1,0:T(8,128)(2,1)}, bf16[8,3,48,512]{3,2,1,0:T(8,128)(2,1)}, u32[]{:S(2)}, u32[]{:S(2)}) collective-permute-start(bf16[8,3,48,512]{3,2,1,0:T(8,128)(2,1)} %bitcast.168), channel_id=1, source_target_pairs={{0,64},{64,0},{1,65},{65,1},{2,66},{66,2},{3,67},{67,3},{4,68},{68... | collective-permute-start | bytes 3538952 | tf_op jit(solution)/shard_map/ppermute | solution.py:22
  126.8 47.6 %collective-permute-start.29 = (bf16[4,6,512]{2,1,0:T(8,128)(2,1)}, bf16[4,6,512]{2,1,0:T(8,128)(2,1)}, u32[]{:S(2)}, u32[]{:S(2)}) collective-permute-start(bf16[4,6,512]{2,1,0:T(8,128)(2,1)} %fusion.28), channel_id=1, source_target_pairs={{0,64},{64,0},{1,65},{65,1},{2,66},{66,2},{3,67},{67,3},{4,68},{68... | collective-permute-start | bytes 73736 | tf_op jit(solution)/shard_map/ppermute | solution.py:22
  201.1 50.2 %collective-permute-start.4 = (f32[4,2,80,128]{3,2,1,0:T(8,128)S(1)}, f32[4,2,80,128]{3,2,1,0:T(8,128)S(1)}, u32[]{:S(2)}, u32[]{:S(2)}) collective-permute-start(f32[4,2,80,128]{3,2,1,0:T(8,128)S(1)} %get-tuple-element.26), channel_id=1, source_target_pairs={{0,16},{8,24},{16,0},{24,8},{1,17},{9,25},{17,1},{25,9},{2,18},{10... | collective-permute-start | bytes 983048 | tf_op jit(solution)/shard_map/ppermute | solution.py:94
  205.2 47.5 %collective-permute-start.3 = (f32[4,2,80,128]{3,2,1,0:T(8,128)S(1)}, f32[4,2,80,128]{3,2,1,0:T(8,128)S(1)}, u32[]{:S(2)}, u32[]{:S(2)}) collective-permute-start(f32[4,2,80,128]{3,2,1,0:T(8,128)S(1)} %get-tuple-element.25), channel_id=1, source_target_pairs={{0,24},{8,0},{16,8},{24,16},{1,25},{9,1},{17,9},{25,17},{2,26},{10... | collective-permute-start | bytes 983048 | tf_op jit(solution)/shard_map/ppermute | solution.py:94
  210.6 18.0 %collective-permute-start.22 = (f32[1,2,48,128]{3,2,1,0:T(8,128)S(1)}, f32[1,2,48,128]{3,2,1,0:T(8,128)S(1)}, u32[]{:S(2)}, u32[]{:S(2)}) collective-permute-start(f32[1,2,48,128]{3,2,1,0:T(8,128)S(1)} %get-tuple-element.34), channel_id=1, source_target_pairs={{0,16},{8,24},{16,0},{24,8},{1,17},{9,25},{17,1},{25,9},{2,18},{10... | collective-permute-start | bytes 147464 | tf_op jit(solution)/shard_map/ppermute | solution.py:94
  213.0 15.5 %collective-permute-start.21 = (f32[1,2,48,128]{3,2,1,0:T(8,128)S(1)}, f32[1,2,48,128]{3,2,1,0:T(8,128)S(1)}, u32[]{:S(2)}, u32[]{:S(2)}) collective-permute-start(f32[1,2,48,128]{3,2,1,0:T(8,128)S(1)} %get-tuple-element.35), channel_id=1, source_target_pairs={{0,24},{8,0},{16,8},{24,16},{1,25},{9,1},{17,9},{25,17},{2,26},{10... | collective-permute-start | bytes 147464 | tf_op jit(solution)/shard_map/ppermute | solution.py:94
  214.7 13.9 %collective-permute-start.20 = (f32[1,2,48,128]{3,2,1,0:T(8,128)S(1)}, f32[1,2,48,128]{3,2,1,0:T(8,128)S(1)}, u32[]{:S(2)}, u32[]{:S(2)}) collective-permute-start(f32[1,2,48,128]{3,2,1,0:T(8,128)S(1)} %get-tuple-element.33), channel_id=1, source_target_pairs={{0,8},{8,16},{16,24},{24,0},{1,9},{9,17},{17,25},{25,1},{2,10},{10... | collective-permute-start | bytes 147464 | tf_op jit(solution)/shard_map/ppermute | solution.py:94
  228.6 6.7 %collective-permute-start.25 = (f32[2,48,128]{2,1,0:T(8,128)S(1)}, f32[2,48,128]{2,1,0:T(8,128)S(1)}, u32[]{:S(2)}, u32[]{:S(2)}) collective-permute-start(f32[2,48,128]{2,1,0:T(8,128)S(1)} %fusion.22), channel_id=1, source_target_pairs={{2,6},{3,7},{10,14},{11,15},{18,22},{19,23},{26,30},{27,31},{34,38... | collective-permute-start | bytes 147464 | tf_op jit(solution)/shard_map/ppermute | solution.py:107
  229.3 7.3 %collective-permute-start.24 = (f32[2,48,128]{2,1,0:T(8,128)S(1)}, f32[2,48,128]{2,1,0:T(8,128)S(1)}, u32[]{:S(2)}, u32[]{:S(2)}) collective-permute-start(f32[2,48,128]{2,1,0:T(8,128)S(1)} %fusion.22), channel_id=1, source_target_pairs={{0,6},{1,7},{8,14},{9,15},{16,22},{17,23},{24,30},{25,31},{32,38},... | collective-permute-start | bytes 147464 | tf_op jit(solution)/shard_map/ppermute | solution.py:107
  234.6 4.6 %collective-permute-start.23 = (f32[2,48,128]{2,1,0:T(8,128)S(1)}, f32[2,48,128]{2,1,0:T(8,128)S(1)}, u32[]{:S(2)}, u32[]{:S(2)}) collective-permute-start(f32[2,48,128]{2,1,0:T(8,128)S(1)} %fusion.22), channel_id=1, source_target_pairs={{4,6},{5,7},{12,14},{13,15},{20,22},{21,23},{28,30},{29,31},{36,38... | collective-permute-start | bytes 147464 | tf_op jit(solution)/shard_map/ppermute | solution.py:107
  235.3 7.4 %collective-permute-start.13 = (f32[3,2,48,128]{3,2,1,0:T(8,128)S(1)}, f32[3,2,48,128]{3,2,1,0:T(8,128)S(1)}, u32[]{:S(2)}, u32[]{:S(2)}) collective-permute-start(f32[3,2,48,128]{3,2,1,0:T(8,128)S(1)} %get-tuple-element.28), channel_id=1, source_target_pairs={{0,16},{8,24},{16,0},{24,8},{1,17},{9,25},{17,1},{25,9},{2,18},{10... | collective-permute-start | bytes 442376 | tf_op jit(solution)/shard_map/ppermute | solution.py:94
  236.5 7.4 %collective-permute-start.12 = (f32[3,2,48,128]{3,2,1,0:T(8,128)S(1)}, f32[3,2,48,128]{3,2,1,0:T(8,128)S(1)}, u32[]{:S(2)}, u32[]{:S(2)}) collective-permute-start(f32[3,2,48,128]{3,2,1,0:T(8,128)S(1)} %get-tuple-element.29), channel_id=1, source_target_pairs={{0,24},{8,0},{16,8},{24,16},{1,25},{9,1},{17,9},{25,17},{2,26},{10... | collective-permute-start | bytes 442376 | tf_op jit(solution)/shard_map/ppermute | solution.py:94
  239.1 8.1 %collective-permute-start.11 = (f32[3,2,48,128]{3,2,1,0:T(8,128)S(1)}, f32[3,2,48,128]{3,2,1,0:T(8,128)S(1)}, u32[]{:S(2)}, u32[]{:S(2)}) collective-permute-start(f32[3,2,48,128]{3,2,1,0:T(8,128)S(1)} %get-tuple-element.27), channel_id=1, source_target_pairs={{0,8},{8,16},{16,24},{24,0},{1,9},{9,17},{17,25},{25,1},{2,10},{10... | collective-permute-start | bytes 442376 | tf_op jit(solution)/shard_map/ppermute | solution.py:94
  242.7 14.5 %collective-permute-start.2 = (f32[4,2,80,128]{3,2,1,0:T(8,128)S(1)}, f32[4,2,80,128]{3,2,1,0:T(8,128)S(1)}, u32[]{:S(2)}, u32[]{:S(2)}) collective-permute-start(f32[4,2,80,128]{3,2,1,0:T(8,128)S(1)} %get-tuple-element.24), channel_id=1, source_target_pairs={{0,8},{8,16},{16,24},{24,0},{1,9},{9,17},{17,25},{25,1},{2,10},{10... | collective-permute-start | bytes 983048 | tf_op jit(solution)/shard_map/ppermute | solution.py:94
  244.0 24.3 %collective-permute-start.26 = (f32[48,128]{1,0:T(8,128)S(1)}, f32[48,128]{1,0:T(8,128)S(1)}, u32[]{:S(2)}, u32[]{:S(2)}) collective-permute-start(f32[48,128]{1,0:T(8,128)S(1)} %dynamic-slice_bitcast_fusion.12), channel_id=1, source_target_pairs={{0,1},{1,0},{2,3},{3,2},{4,5},{5,4},{6,7},{7,6},{8,9},{9,8},{10,11... | collective-permute-start | bytes 73736 | tf_op jit(solution)/shard_map/ppermute | solution.py:22
  247.3 10.2 %collective-permute-start.16 = (f32[2,48,128]{2,1,0:T(8,128)S(1)}, f32[2,48,128]{2,1,0:T(8,128)S(1)}, u32[]{:S(2)}, u32[]{:S(2)}) collective-permute-start(f32[2,48,128]{2,1,0:T(8,128)S(1)} %get-tuple-element.37), channel_id=1, source_target_pairs={{0,4},{4,0},{6,2},{1,5},{5,1},{7,3},{8,12},{12,8},{14,10},{9,13},{... | collective-permute-start | bytes 147464 | tf_op jit(solution)/shard_map/ppermute | solution.py:107
  251.4 8.8 %collective-permute-start.15 = (f32[2,48,128]{2,1,0:T(8,128)S(1)}, f32[2,48,128]{2,1,0:T(8,128)S(1)}, u32[]{:S(2)}, u32[]{:S(2)}) collective-permute-start(f32[2,48,128]{2,1,0:T(8,128)S(1)} %get-tuple-element.38), channel_id=1, source_target_pairs={{2,0},{4,2},{6,4},{3,1},{5,3},{7,5},{10,8},{12,10},{14,12},{11,9},... | collective-permute-start | bytes 147464 | tf_op jit(solution)/shard_map/ppermute | solution.py:107
  252.7 7.5 %collective-permute-start.14 = (f32[2,48,128]{2,1,0:T(8,128)S(1)}, f32[2,48,128]{2,1,0:T(8,128)S(1)}, u32[]{:S(2)}, u32[]{:S(2)}) collective-permute-start(f32[2,48,128]{2,1,0:T(8,128)S(1)} %get-tuple-element.36), channel_id=1, source_target_pairs={{0,2},{2,4},{6,0},{1,3},{3,5},{7,1},{8,10},{10,12},{14,8},{9,11},{... | collective-permute-start | bytes 147464 | tf_op jit(solution)/shard_map/ppermute | solution.py:107
  257.3 6.0 %collective-permute-start.7 = (f32[2,80,128]{2,1,0:T(8,128)S(1)}, f32[2,80,128]{2,1,0:T(8,128)S(1)}, u32[]{:S(2)}, u32[]{:S(2)}) collective-permute-start(f32[2,80,128]{2,1,0:T(8,128)S(1)} %get-tuple-element.31), channel_id=1, source_target_pairs={{0,4},{2,6},{4,0},{6,2},{1,5},{3,7},{5,1},{7,3},{8,12},{10,14},{12... | collective-permute-start | bytes 245768 | tf_op jit(solution)/shard_map/ppermute | solution.py:107
  257.5 5.9 %collective-permute-start.6 = (f32[2,80,128]{2,1,0:T(8,128)S(1)}, f32[2,80,128]{2,1,0:T(8,128)S(1)}, u32[]{:S(2)}, u32[]{:S(2)}) collective-permute-start(f32[2,80,128]{2,1,0:T(8,128)S(1)} %get-tuple-element.32), channel_id=1, source_target_pairs={{0,6},{2,0},{4,2},{6,4},{1,7},{3,1},{5,3},{7,5},{8,14},{10,8},{12,... | collective-permute-start | bytes 245768 | tf_op jit(solution)/shard_map/ppermute | solution.py:107
  260.1 5.7 %collective-permute-start.5 = (f32[2,80,128]{2,1,0:T(8,128)S(1)}, f32[2,80,128]{2,1,0:T(8,128)S(1)}, u32[]{:S(2)}, u32[]{:S(2)}) collective-permute-start(f32[2,80,128]{2,1,0:T(8,128)S(1)} %get-tuple-element.30), channel_id=1, source_target_pairs={{0,2},{2,4},{4,6},{6,0},{1,3},{3,5},{5,7},{7,1},{8,10},{10,12},{12... | collective-permute-start | bytes 245768 | tf_op jit(solution)/shard_map/ppermute | solution.py:107
  265.8 5.8 %collective-permute-start.17 = (f32[128,128]{1,0:T(8,128)S(1)}, f32[128,128]{1,0:T(8,128)S(1)}, u32[]{:S(2)}, u32[]{:S(2)}) collective-permute-start(f32[128,128]{1,0:T(8,128)S(1)} %fusion.16), channel_id=1, source_target_pairs={{0,1},{1,0},{2,3},{3,2},{4,5},{5,4},{6,7},{7,6},{8,9},{9,8},{10,11... | collective-permute-start | bytes 196616 | tf_op jit(solution)/shard_map/ppermute | solution.py:22
  268.3 4.8 %collective-permute-start.27 = (f32[48,128]{1,0:T(8,128)S(1)}, f32[48,128]{1,0:T(8,128)S(1)}, u32[]{:S(2)}, u32[]{:S(2)}) collective-permute-start(f32[48,128]{1,0:T(8,128)S(1)} %bitcast_add_fusion.4), channel_id=1, source_target_pairs={{0,32},{32,0},{1,33},{33,1},{2,34},{34,2},{3,35},{35,3},{4,36},{36... | collective-permute-start | bytes 73736 | tf_op jit(solution)/shard_map/ppermute | solution.py:22
  271.7 1.3 collective-permute-start.18

commit v2 on v1

--- a/solution.py
+++ b/solution.py
@@ -14,22 +14,101 @@
 SWAP = [(0, 1), (1, 0)]
 
 
-def tie(value, *after):
-    return lax.optimization_barrier((value, *after))[0]
-
-
 def swap(value, axis):
     return lax.ppermute(value, axis, SWAP)
 
 
-def by_time(block):
-    n, _, comps, sites = block.shape
-    parts = block.reshape(n, 4, 4, 2, comps, sites).transpose(2, 1, 3, 4, 0, 5)
-    return parts.reshape(4, 8, comps // 2, 2 * n, sites)
+HINT = pl.CostEstimate(flops=1000, bytes_accessed=1000, transcendentals=0)
+
+
+def by_time_kernel(cuts, block, *outs):
+    for k in range(block.shape[1]):
+        turned = jnp.swapaxes(block[:, k], 0, 1)
+        for t in range(turned.shape[0]):
+            for (low, high), out in zip(cuts, outs):
+                out[t // 2, 0, t % 2, k] = turned[t, low:high]
+
+
+def by_time(block, cuts):
+    n, comps, times, sites = block.shape
+    return pl.pallas_call(
+        functools.partial(by_time_kernel, cuts),
+        grid=(4,),
+        in_specs=[pl.BlockSpec((n, comps, times // 4, sites), lambda z: (0, 0, z, 0))],
+        out_specs=[
+            pl.BlockSpec((4, 1, 2, comps, h - l, sites), lambda z: (0, z, 0, 0, 0, 0))
+            for l, h in cuts
+        ],
+        out_shape=[
+            jax.ShapeDtypeStruct((4, 4, 2, comps, h - l, sites), block.dtype) for l, h in cuts
+        ],
+        compiler_params=pltpu.CompilerParams(vmem_limit_bytes=48 * 2**20),
+        cost_estimate=HINT,
+        name="by_time",
+    )(block)
+
+
+def rows_of(block):
+    x, z, yh, comps, n, sites = block.shape
+    return block.reshape(x, z * yh, comps // 2, 2 * n, sites)
+
+
+ANY = pl.BlockSpec(memory_space=pl.ANY)
+
+
+def carve_kernel(block, *refs):
+    refs[-1][...] = block[0]
+
+
+def carve(late, x, *after):
+    _, inner, colours, n, sites = late.shape
+    return pl.pallas_call(
+        carve_kernel,
+        grid=(4,),
+        in_specs=[pl.BlockSpec((1, inner // 4, colours, n, sites), lambda i: (x, i, 0, 0, 0))]
+        + [ANY] * len(after),
+        out_specs=pl.BlockSpec((inner // 4, colours, n, sites), lambda i: (i, 0, 0, 0)),
+        out_shape=jax.ShapeDtypeStruct((inner, colours, n, sites), late.dtype),
+        compiler_params=pltpu.CompilerParams(vmem_limit_bytes=60 * 2**20),
+        cost_estimate=HINT,
+        name="carve",
+    )(late, *after)
+
+
+def choose_kernel(owned, rows, at, block, *refs):
+    group, time, index = at[0], at[1], at[2 + pl.program_id(0)]
+    row = lax.broadcasted_iota(jnp.int32, block.shape[1:], 1)
+    here = jnp.where(index // owned == group, time % rows, -1)
+    kept = jnp.where(row == here, block[0].astype(jnp.float32), 0.0)
+    refs[-1][0] = jnp.sum(kept, axis=1).astype(block.dtype)
+
+
+def choose(vecs, source_index, source_time, group, after):
+    owned, comps, _, sites = vecs.shape
+    rows = 16
+    at = jnp.concatenate([group[None], source_time, source_index])
+    return pl.pallas_call(
+        functools.partial(choose_kernel, owned, rows),
+        grid_spec=pltpu.PrefetchScalarGridSpec(
+            num_scalar_prefetch=1,
+            grid=(source_index.shape[0],),
+            in_specs=[
+                pl.BlockSpec(
+                    (1, comps, rows, sites), lambda i, at: (at[2 + i] % owned, 0, at[1] // rows, 0)
+                ),
+                ANY,
+            ],
+            out_specs=pl.BlockSpec((1, comps, sites), lambda i, at: (i, 0, 0)),
+        ),
+        out_shape=jax.ShapeDtypeStruct((source_index.shape[0], comps, sites), vecs.dtype),
+        compiler_params=pltpu.CompilerParams(vmem_limit_bytes=60 * 2**20),
+        cost_estimate=HINT,
+        name="choose",
+    )(at, vecs, after)
 
 
 def dot_kernel(count, *refs):
-    cols, (own, other), outs = refs[:count], refs[count : count + 2], refs[count + 2 :]
+    cols, (own, other), outs = refs[:count], refs[count : count + 2], refs[-count:]
     width = own.shape[3] // 2
     for at in range(own.shape[1]):
         for col, out in zip(cols, outs):
@@ -52,12 +131,12 @@
                 out[0, at, part] = jnp.concatenate([halves[0][part], halves[1][part]], axis=1)
 
 
-def project(cols, own, other, first, size, step):
+def project(cols, own, other, first, size, step, *after):
     _, inner, colours, rows, sites = own.shape
     spec = lambda n, off: pl.BlockSpec(
         (1, step, colours, n, sites), lambda i, j, off=off: (i + off, j, 0, 0, 0)
     )
-    in_specs = [spec(c.shape[3], 0) for c in cols] + [spec(rows, first)] * 2
+    in_specs = [spec(c.shape[3], 0) for c in cols] + [spec(rows, first)] * 2 + [ANY] * len(after)
     out_specs = [
         pl.BlockSpec((1, step, 2, c.shape[3] // 2, rows), lambda i, j: (i, j, 0, 0, 0))
         for c in cols
@@ -65,7 +144,6 @@
     out_shape = [
         jax.ShapeDtypeStruct((size, inner, 2, c.shape[3] // 2, rows), jnp.float32) for c in cols
     ]
-    total = sum(c.shape[3] for c in cols)
     return pl.pallas_call(
         functools.partial(dot_kernel, len(cols)),
         grid=(size, inner // step),
@@ -73,13 +151,9 @@
         out_specs=out_specs,
         out_shape=out_shape,
         compiler_params=pltpu.CompilerParams(vmem_limit_bytes=48 * 2**20),
-        cost_estimate=pl.CostEstimate(
-            flops=2 * size * inner * colours * sites * total * 2 * rows,
-            bytes_accessed=2 * size * inner * colours * sites * (total + 2 * rows),
-            transcendentals=0,
-        ),
+        cost_estimate=HINT,
         name="project",
-    )(*cols, own, other)
+    )(*cols, own, other, *after)
 
 
 def pick(value, index):
@@ -120,46 +194,58 @@
     scale = 1.0 / math.sqrt(comps * sites * 32)
     core = lax.axis_index("c")
     group = 2 * lax.axis_index("yl") + core
-    sols = solutions[0]
+    sols = solutions[0].transpose(0, 2, 1, 3)
+    vecs = eigvecs.transpose(0, 2, 1, 3)
 
     raw = swap(sols[:RAW], "yl")
-    mine = by_time(sols)
-    late = by_time(sols[RAW:])
-    send = [late[x] for x in range(4)]
-    got = [swap(send[0], "yl")]
-    got.append(swap(tie(send[1], raw), "yl"))
-    got.append(swap(tie(send[2], got[0]), "yl"))
-    got.append(swap(tie(send[3], got[1]), "yl"))
-
-    own = by_time(eigvecs)
-    other = swap(own, "c")
+    other = swap(vecs, "c")
+    early, late = by_time(sols, ((0, RAW), (RAW, count)))
+    late = rows_of(late)
+    send = [carve(late, 0), carve(late, 1, raw)]
+    got = [swap(send[0], "yl"), swap(send[1], "yl")]
+    send.append(carve(late, 2, got[0]))
+    got.append(swap(send[2], "yl"))
+    send.append(carve(late, 3, got[1]))
+    got.append(swap(send[3], "yl"))
+
+    whole = ((0, owned),)
+    own = rows_of(by_time(vecs, whole)[0])
+    other = rows_of(by_time(other, whole)[0])
+    raw = rows_of(by_time(raw, ((0, RAW),))[0])
 
     def rows(part):
         x, inner, _, n, lanes = part.shape
         return part.reshape(x, 4, 2, 2 * n, lanes)
 
-    a, b = project([mine, by_time(raw)], own, other, 0, 4, 4)
-    first = sum_x(sum_z(jnp.concatenate([rows(a), rows(b)], axis=3)), 0, 4)
-    tail = []
-    mid = [project([got[x][None]], own, other, x, 1, 4)[0] for x in range(3)]
-    mid = sum_x(sum_z(rows(jnp.concatenate(mid, axis=0))), 0, 3)
-    last = project([got[3][None]], own, other, 3, 1, 4)[0]
-    last = sum_x(sum_z(rows(last)), 3, 1)
-
+    def against(x, *after):
+        return rows(project([got[x][None]], own, other, x, 1, 4, *after)[0])
+
+    parts = project([rows_of(early), late, raw], own, other, 0, 4, 4)
+    first_z = sum_z(jnp.concatenate([rows(p) for p in parts], axis=3))
+    chosen = choose(vecs, source_index, source_time, group, first_z)
+    first = sum_x(first_z, 0, 4)
+    mid = [against(0, first_z, send[2])]
+    mid.append(against(1, first, mid[0], send[3]))
+    mid_z = sum_z(jnp.concatenate(mid, axis=0))
+    last = [against(2, mid_z)]
+    mid = sum_x(mid_z, 0, 2)
     main = sum_yh(jnp.concatenate([first, mid], axis=1))
     main_c = swap(main, "c")
+    last.append(against(3, main_c, last[0]))
+    last = sum_x(sum_z(jnp.concatenate(last, axis=0)), 2, 2)
     last = sum_yh(last)
     last_c = swap(last, "c")
-    is_last = lax.axis_index("x") == 3
+    is_last = lax.axis_index("x") >= 2
 
     def assemble(main, last, half):
         main = main[:, half * owned : (half + 1) * owned]
         last = last[:, half * owned : (half + 1) * owned]
-        n0, n1 = 2 * count, 2 * count + 2 * RAW
-        home = main[:n0].reshape(2, count, owned)
-        early = main[n0:n1].reshape(2, RAW, owned)
-        rest = jnp.where(is_last, last, main[n1:]).reshape(2, count - RAW, owned)
-        return home, jnp.concatenate([early, rest], axis=1)
+        cut = [2 * RAW, 2 * count, 2 * (count + RAW)]
+        view = lambda v: v.reshape(2, -1, owned)
+        home = jnp.concatenate([view(main[: cut[0]]), view(main[cut[0] : cut[1]])], axis=1)
+        rest = jnp.where(is_last, last, main[cut[2] :])
+        away = jnp.concatenate([view(main[cut[1] : cut[2]]), view(rest)], axis=1)
+        return home, away
 
     h0, y0 = assemble(main, last, 0)
     h1, y1 = assemble(main_c, last_c, 1)
@@ -172,10 +258,6 @@
     result = jnp.sum(picked, axis=0).reshape(spins, 2, count, owned) * scale
     result = result.transpose(3, 0, 2, 1).reshape(1, owned, spins * count * 2)
 
-    slice_now = lax.dynamic_index_in_dim(eigvecs, source_time[0], 1, keepdims=False)
-    owners = source_index // owned
-    chosen = jnp.take(slice_now, source_index - owners * owned, axis=0)
-    chosen = jnp.where((owners == group)[:, None, None], chosen, 0).astype(jnp.bfloat16)
     chosen = chosen + swap(chosen, "c")
     chosen = chosen + swap(chosen, "yl")
     my_spins = lax.dynamic_index_in_dim(dilution, group, 1, keepdims=False)

time: 277 us -> 236 us (0.85)
  local copies, waits for them, and re-layouts: 85.3 us -> 9.04 us
  Pallas kernels: 37.2 us -> 89.3 us
  waiting for transfers between devices: 99 us -> 84.7 us
    reshape x8 -> x2, local copies, waits for them, and re-layouts: 52.7 us -> 0.08 us  [assemble(): view = lambda v: v.reshape(2, -1, owned)]
    pallas_call x0 -> x9, Pallas kernels: none -> 45 us  [the longest x4 27.6 us: by_time(): pl.pallas_call(functools.partial(by_time_kernel, cuts), grid=(4,), in_spe...]
    ppermute x12, waiting for transfers between devices: 88.6 us -> 61.9 us  [swap(): return lax.ppermute(value, axis, SWAP)]
    another operation x2 -> x0, local copies, waits for them, and re-layouts: 19.2 us -> none  [by_time(): parts = block.reshape(n, 4, 4, 2, comps, sites).transpose(2, 1, 3, 4, 0, 5)]
    ppermute x9, waiting for transfers between devices: 4.82 us -> 19.4 us  [sum_z(): lax.ppermute(pick(slabs, (me + k) % 4), 'z', [(i, (i + k) % 4) for i in r...]
    pallas_call x5, Pallas kernels: 37.2 us -> 44.3 us  [project(): pl.pallas_call(functools.partial(dot_kernel, len(cols)), grid=(size, inne...]
    unnamed x12 -> x26, local copies, waits for them, and re-layouts: 0.83 us -> 5.48 us
    slice x4 -> x0, local copies, waits for them, and re-layouts: 4.56 us -> none  [the longest x1 2.63 us: local(): late = by_time(sols[RAW:])]
  transfers between devices with their start and end apart: 30 -> 30, of which waited for: 10 -> 15; matrix products, arithmetic and copies ran while one was open for 20% -> 3% of each run, Pallas kernels for 14% -> 34%
where the time goes in v2:
time: 236 us; the launch traced here: 232 us
  Pallas kernels  89.3 us (38%)
  waiting for transfers between devices  84.7 us (36%)
  starting transfers between devices  43.4 us (18%)
  local copies, waits for them, and re-layouts  9.04 us (4%)
  other arithmetic  4.19 us (2%)
    ppermute x12, waiting for transfers between devices, swap(): return lax.ppermute(value, axis, SWAP)  61.9 us
    pallas_call x5, Pallas kernels, project(): pl.pallas_call(functools.partial(dot_kernel, len(cols)), grid=(size, inne...  44.3 us
    pallas_call x4, Pallas kernels, by_time(): pl.pallas_call(functools.partial(by_time_kernel, cuts), grid=(4,), in_spe...  27.6 us
    ppermute x9, waiting for transfers between devices, sum_z(): lax.ppermute(pick(slabs, (me + k) % 4), 'z', [(i, (i + k) % 4) for i in r...  19.4 us
    ppermute x9, starting transfers between devices, sum_x(): total = total + lax.ppermute(send, 'x', pairs)  17.9 us
    ppermute x9, starting transfers between devices, sum_z(): lax.ppermute(pick(slabs, (me + k) % 4), 'z', [(i, (i + k) % 4) for i in r...  14.6 us
    pallas_call x4, Pallas kernels, carve(): pl.pallas_call(carve_kernel, grid=(4,), in_specs=[pl.BlockSpec((1, inner...  13.6 us
    ppermute x12, starting transfers between devices, swap(): return lax.ppermute(value, axis, SWAP)  10.9 us
  transfers between devices with their start and end apart: 30, of which 15 were waited for; matrix products, arithmetic and copies ran while one was open for 3% of the time, Pallas kernels for 34%

profile of v2, /device:TPU:0, one launch (start us, length us, event | category | flops | bytes accessed | tf_op | source)
XLA Modules:
  0.0 232.4 jit_solution(15158120890530542210)
XLA Ops:
  0.7 1.6 slice.56
  2.3 1.7 collective-permute-start
  4.0 6.0 %by_time.4 = (bf16[4,4,2,6,8,512]{5,4,3,2,1,0:T(8,128)(2,1)S(1)}, bf16[4,4,2,6,24,512]{5,4,3,2,1,0:T(8,128)(2,1)}) custom-call(bf16[32,6,32,512]{3,2,1,0:T(8,128)(2,1)} %bitcast.190), custom_call_target="tpu_custom_call" | custom-call | flops 1000 | bytes 1000 | tf_op jit(solution)/shard_map/by_time/pallas_call | solution.py:34
  10.1 1.2 copy-done.8
  11.2 3.4 %carve.4 = bf16[8,3,48,512]{3,2,1,0:T(8,128)(2,1)} custom-call(bf16[4,8,3,48,512]{4,3,2,1,0:T(8,128)(2,1)} %bitcast.181), custom_call_target="tpu_custom_call" | custom-call | flops 1000 | bytes 1000 | tf_op jit(solution)/shard_map/carve/pallas_call | solution.py:65
  14.6 0.4 collective-permute-start.8
  15.0 24.6 %collective-permute-done.block.refs_0_ = bf16[8,6,32,512]{3,2,1,0:T(8,128)(2,1)S(1)} collective-permute-done((bf16[8,6,32,512]{3,2,1,0:T(8,128)(2,1)S(1)}, bf16[8,6,32,512]{3,2,1,0:T(8,128)(2,1)S(1)}, u32[]{:S(2)}, u32[]{:S(2)}) %collective-permute-start) | collective-permute-done | bytes 1572896 | tf_op jit(solution)/shard_map/ppermute | solution.py:18
  39.6 1.1 copy-done
  40.7 3.4 %carve.6 = bf16[8,3,48,512]{3,2,1,0:T(8,128)(2,1)} custom-call(bf16[4,8,3,48,512]{4,3,2,1,0:T(8,128)(2,1)} %bitcast.182, bf16[8,6,32,512]{3,2,1,0:T(8,128)(2,1)} %copy-done), custom_call_target="tpu_custom_call" | custom-call | flops 1000 | bytes 1000 | tf_op jit(solution)/shard_map/carve/pallas_call | solution.py:65
  44.1 1.7 collective-permute-start.9
  45.8 10.3 %by_time.6 = bf16[4,4,2,6,64,512]{5,4,3,2,1,0:T(8,128)(2,1)} custom-call(bf16[64,6,32,512]{3,2,1,0:T(8,128)(2,1)} %bitcast.187), custom_call_target="tpu_custom_call" | custom-call | flops 1000 | bytes 1000 | tf_op jit(solution)/shard_map/by_time/pallas_call | solution.py:34
  56.1 0.7 by_time.5
  56.8 10.5 %by_time.7 = bf16[4,4,2,6,64,512]{5,4,3,2,1,0:T(8,128)(2,1)} custom-call(bf16[64,6,32,512]{3,2,1,0:T(8,128)(2,1)} %collective-permute-done.1.block), custom_call_target="tpu_custom_call" | custom-call | flops 1000 | bytes 1000 | tf_op jit(solution)/shard_map/by_time/pallas_call | solution.py:34
  67.4 25.6 %project.5 = (f32[4,8,2,8,128]{4,3,2,1,0:T(8,128)S(1)}, f32[4,8,2,24,128]{4,3,2,1,0:T(8,128)S(1)}, f32[4,8,2,8,128]{4,3,2,1,0:T(8,128)S(1)}) custom-call(bf16[4,8,3,16,512]{4,3,2,1,0:T(8,128)(2,1)S(1)} %bitcast.167, bf16[4,8,3,48,512]{4,3,2,1,0:T(8,128)(2,1)} %bitcast.183, bf16[4,8,3,16,512]{4,3,2,1,0:T(8,128)(2,1)S(1)} %bitcast.155, ...), custom_call_target="tpu_custom_call" | custom-call | flops 1000 | bytes 1000 | tf_op jit(solution)/shard_map/project/pallas_call | solution.py:147
  93.1 1.0 dynamic-slice_bitcast_fusion.2
  94.1 1.9 collective-permute-start.2
  96.0 2.1 collective-permute-start.3
  98.1 1.9 collective-permute-start.4
  100.2 0.6 gather_fusion
  100.7 5.3 %collective-permute-done.2 = f32[4,2,80,128]{3,2,1,0:T(8,128)S(1)} collective-permute-done((f32[4,2,80,128]{3,2,1,0:T(8,128)}, f32[4,2,80,128]{3,2,1,0:T(8,128)S(1)}, u32[]{:S(2)}, u32[]{:S(2)}) %collective-permute-start.2) | collective-permute-done | bytes 327712 | tf_op jit(solution)/shard_map/ppermute | solution.py:168
  106.1 5.6 %collective-permute-done.3 = f32[4,2,80,128]{3,2,1,0:T(8,128)S(1)} collective-permute-done((f32[4,2,80,128]{3,2,1,0:T(8,128)}, f32[4,2,80,128]{3,2,1,0:T(8,128)S(1)}, u32[]{:S(2)}, u32[]{:S(2)}) %collective-permute-start.3) | collective-permute-done | bytes 327712 | tf_op jit(solution)/shard_map/ppermute | solution.py:168
  111.7 1.9 collective-permute-done.4
  113.5 1.0 fusion.1.refs_3_.refs_0_
  114.6 1.6 collective-permute-start.5
  116.2 1.7 collective-permute-start.6
  117.9 1.8 collective-permute-start.7
  119.8 3.4 %carve.5.refs_4_ = bf16[8,3,48,512]{3,2,1,0:T(8,128)(2,1)} custom-call(bf16[4,8,3,48,512]{4,3,2,1,0:T(8,128)(2,1)} %bitcast.184, bf16[8,3,48,512]{3,2,1,0:T(8,128)(2,1)} %collective-permute-done.8.refs_0_), custom_call_target="tpu_custom_call" | custom-call | flops 1000 | bytes 1000 | tf_op jit(solution)/shard_map/carve/pallas_call | solution.py:65
  123.2 1.1 copy-done.3
  124.3 3.4 %carve.7.refs_5_ = bf16[8,3,48,512]{3,2,1,0:T(8,128)(2,1)} custom-call(bf16[4,8,3,48,512]{4,3,2,1,0:T(8,128)(2,1)} %bitcast.185, bf16[8,3,48,512]{3,2,1,0:T(8,128)(2,1)} %copy-done.3), custom_call_target="tpu_custom_call" | custom-call | flops 1000 | bytes 1000 | tf_op jit(solution)/shard_map/carve/pallas_call | solution.py:65
  127.7 1.3 copy-done.6
  129.0 4.8 %project.6 = f32[1,8,2,24,128]{4,3,2,1,0:T(8,128)S(1)} custom-call(bf16[1,8,3,48,512]{4,3,2,1,0:T(8,128)(2,1)} %bitcast.30.refs_0_, bf16[4,8,3,128,512]{4,3,2,1,0:T(8,128)(2,1)} %bitcast.172, bf16[4,8,3,128,512]{4,3,2,1,0:T(8,128)(2,1)} %bitcast.177, f32[4,2,80,128]{3,2,1,0:T(8,128)S(1)} %fusion.1.refs_3_.refs_0_, bf16[8,3,48,512]{3,2,1,0:T(8,128)(2,1)S(1)} %copy-done.6), custom_call_target="tpu_custom_call" | custom-call | flops 1000 | bytes 1000 | tf_op jit(solution)/shard_map/project/pallas_call | solution.py:147
  133.9 4.6 %project.7 = f32[1,8,2,24,128]{4,3,2,1,0:T(8,128)S(1)} custom-call(bf16[1,8,3,48,512]{4,3,2,1,0:T(8,128)(2,1)S(1)} %bitcast.156, bf16[4,8,3,128,512]{4,3,2,1,0:T(8,128)(2,1)} %bitcast.173, bf16[4,8,3,128,512]{4,3,2,1,0:T(8,128)(2,1)} %bitcast.178, f32[2,80,128]{2,1,0:T(8,128)S(1)} %fusion.25.refs_3_, f32[1,4,2,48,128]{4,3,2,1,0:T(8,128)S(1)} %bitcast.157, ...), custom_call_target="tpu_custom_call" | custom-call | flops 1000 | bytes 1000 | tf_op jit(solution)/shard_map/project/pallas_call | solution.py:147
  138.5 1.2 collective-permute-start.10
  139.7 2.1 collective-permute-start.11
  142.6 0.6 collective-permute-start.18
  143.2 1.5 collective-permute-start.19
  145.0 2.9 %collective-permute-done.12 = f32[2,2,48,128]{3,2,1,0:T(8,128)S(1)} collective-permute-done((f32[2,2,48,128]{3,2,1,0:T(8,128)S(1)}, f32[2,2,48,128]{3,2,1,0:T(8,128)S(1)}, u32[]{:S(2)}, u32[]{:S(2)}) %collective-permute-start.12) | collective-permute-done | bytes 98336 | tf_op jit(solution)/shard_map/ppermute | solution.py:168
  148.0 2.5 %collective-permute-start.13 = (f32[2,48,128]{2,1,0:T(8,128)S(1)}, f32[2,48,128]{2,1,0:T(8,128)S(1)}, u32[]{:S(2)}, u32[]{:S(2)}) collective-permute-start(f32[2,48,128]{2,1,0:T(8,128)S(1)} %get-tuple-element.31), channel_id=1, source_target_pairs={{0,2},{6,0},{1,3},{7,1},{8,10},{14,8},{9,11},{15,9},{16,18},{22,16... | collective-permute-start | bytes 147464 | tf_op jit(solution)/shard_map/ppermute | solution.py:181
  150.5 1.3 collective-permute-start.14
  151.8 1.3 collective-permute-start.15
  153.1 0.6 pad_add_fusion.at
  153.7 3.8 %choose.1 = bf16[4,6,512]{2,1,0:T(8,128)(2,1)} custom-call(s32[6]{0:T(128)} %pad_add_fusion.at, bf16[64,6,32,512]{3,2,1,0:T(8,128)(2,1)} %bitcast.188, f32[4,2,80,128]{3,2,1,0:T(8,128)} %copy-done.2), custom_call_target="tpu_custom_call" | custom-call | flops 1000 | bytes 1000 | tf_op jit(solution)/shard_map/choose/pallas_call | solution.py:90
  157.5 1.8 collective-permute-done.15
  159.3 3.0 %collective-permute-start.16 = (f32[128,128]{1,0:T(8,128)S(1)}, f32[128,128]{1,0:T(8,128)S(1)}, u32[]{:S(2)}, u32[]{:S(2)}) collective-permute-start(f32[128,128]{1,0:T(8,128)S(1)} %fusion.27), channel_id=1, source_target_pairs={{0,1},{1,0},{2,3},{3,2},{4,5},{5,4},{6,7},{7,6},{8,9},{9,8},{10,11... | collective-permute-start | bytes 196616 | tf_op jit(solution)/shard_map/ppermute | solution.py:18
  162.5 0.8 add.242
  163.3 0.4 collective-permute-start.29
  163.7 32.2 %collective-permute-done.16 = f32[128,128]{1,0:T(8,128)S(1)} collective-permute-done((f32[128,128]{1,0:T(8,128)S(1)}, f32[128,128]{1,0:T(8,128)S(1)}, u32[]{:S(2)}, u32[]{:S(2)}) %collective-permute-start.16) | collective-permute-done | bytes 65568 | tf_op jit(solution)/shard_map/ppermute | solution.py:18
  196.1 4.7 %project.8 = f32[1,8,2,24,128]{4,3,2,1,0:T(8,128)S(1)} custom-call(bf16[1,8,3,48,512]{4,3,2,1,0:T(8,128)(2,1)} %bitcast.53.refs_0_, bf16[4,8,3,128,512]{4,3,2,1,0:T(8,128)(2,1)} %bitcast.174, bf16[4,8,3,128,512]{4,3,2,1,0:T(8,128)(2,1)} %bitcast.179, f32[2,2,48,128]{3,2,1,0:T(8,128)S(1)} %fusion.19.refs_3_), custom_call_target="tpu_custom_call" | custom-call | flops 1000 | bytes 1000 | tf_op jit(solution)/shard_map/project/pallas_call | solution.py:147
  200.8 4.7 %project.9 = f32[1,8,2,24,128]{4,3,2,1,0:T(8,128)S(1)} custom-call(bf16[1,8,3,48,512]{4,3,2,1,0:T(8,128)(2,1)} %bitcast.55.refs_0_, bf16[4,8,3,128,512]{4,3,2,1,0:T(8,128)(2,1)} %bitcast.175, bf16[4,8,3,128,512]{4,3,2,1,0:T(8,128)(2,1)} %bitcast.180, f32[128,128]{1,0:T(8,128)S(1)} %collective-permute-done.17.refs_3_, f32[1,4,2,48,128]{4,3,2,1,0:T(8,128)S(1)} %bitcast.160), custom_call_target="tpu_custom_call" | custom-call | flops 1000 | bytes 1000 | tf_op jit(solution)/shard_map/project/pallas_call | solution.py:147
  205.5 0.9 collective-permute-start.20
  206.4 2.4 %collective-permute-start.21 = (f32[2,2,48,128]{3,2,1,0:T(8,128)S(1)}, f32[2,2,48,128]{3,2,1,0:T(8,128)S(1)}, u32[]{:S(2)}, u32[]{:S(2)}) collective-permute-start(f32[2,2,48,128]{3,2,1,0:T(8,128)S(1)} %get-tuple-element.20), channel_id=1, source_target_pairs={{0,24},{8,0},{16,8},{24,16},{1,25},{9,1},{17,9},{25,17},{2,26},{10... | collective-permute-start | bytes 294920 | tf_op jit(solution)/shard_map/ppermute | solution.py:168
  208.8 2.0 collective-permute-start.22
  210.9 0.7 broadcast_select_fusion
  211.6 0.4 collective-permute-done.20
  212.0 1.4 collective-permute-done.21
  213.4 1.6 collective-permute-done.22
  215.0 0.7 collective-permute-start.23
  215.7 3.7 %collective-permute-start.24 = (f32[2,48,128]{2,1,0:T(8,128)S(1)}, f32[2,48,128]{2,1,0:T(8,128)S(1)}, u32[]{:S(2)}, u32[]{:S(2)}) collective-permute-start(f32[2,48,128]{2,1,0:T(8,128)S(1)} %get-tuple-element.30), channel_id=1, source_target_pairs={{0,6},{6,4},{1,7},{7,5},{8,14},{14,12},{9,15},{15,13},{16,22},{22,... | collective-permute-start | bytes 147464 | tf_op jit(solution)/shard_map/ppermute | solution.py:181
  219.4 3.4 %collective-permute-start.25 = (f32[2,48,128]{2,1,0:T(8,128)S(1)}, f32[2,48,128]{2,1,0:T(8,128)S(1)}, u32[]{:S(2)}, u32[]{:S(2)}) collective-permute-start(f32[2,48,128]{2,1,0:T(8,128)S(1)} %get-tuple-element.29), channel_id=1, source_target_pairs={{0,4},{2,6},{1,5},{3,7},{8,12},{10,14},{9,13},{11,15},{16,20},{18,... | collective-permute-start | bytes 147464 | tf_op jit(solution)/shard_map/ppermute | solution.py:181
  222.8 1.7 collective-permute-done.25
  224.5 1.5 collective-permute-start.26
  226.0 3.9 %collective-permute-done.26 = f32[48,128]{1,0:T(8,128)S(1)} collective-permute-done((f32[48,128]{1,0:T(8,128)S(1)}, f32[48,128]{1,0:T(8,128)S(1)}, u32[]{:S(2)}, u32[]{:S(2)}) %collective-permute-start.26) | collective-permute-done | bytes 24608 | tf_op jit(solution)/shard_map/ppermute | solution.py:18
  230.0 1.2 collective-permute-done.27
  231.7 0.7 copy.25
  (76 shorter events, 2.2 us)
Async XLA Ops:
  0.6 56.2 %collective-permute-start.1 = (bf16[64,6,32,512]{3,2,1,0:T(8,128)(2,1)}, bf16[64,6,32,512]{3,2,1,0:T(8,128)(2,1)}, u32[]{:S(2)}, u32[]{:S(2)}) collective-permute-start(bf16[64,6,32,512]{3,2,1,0:T(8,128)(2,1)} %bitcast.186), channel_id=1, source_target_pairs={{0,32},{32,0},{1,33},{33,1},{2,34},{34,2},{3,35},{35,3},{4,36},{36... | collective-permute-start | bytes 37748744 | tf_op jit(solution)/shard_map/ppermute | solution.py:18
  2.3 37.3 %collective-permute-start = (bf16[8,6,32,512]{3,2,1,0:T(8,128)(2,1)S(1)}, bf16[8,6,32,512]{3,2,1,0:T(8,128)(2,1)S(1)}, u32[]{:S(2)}, u32[]{:S(2)}) collective-permute-start(bf16[8,6,32,512]{3,2,1,0:T(8,128)(2,1)S(1)} %slice.56), channel_id=1, source_target_pairs={{0,64},{64,0},{1,65},{65,1},{2,66},{66,2},{3,67},{67,3},{4,68},{68... | collective-permute-start | bytes 4718600 | tf_op jit(solution)/shard_map/ppermute | solution.py:18
  10.1 1.2 copy-start.8
  14.6 105.2 %collective-permute-start.8 = (bf16[8,3,48,512]{3,2,1,0:T(8,128)(2,1)}, bf16[8,3,48,512]{3,2,1,0:T(8,128)(2,1)}, u32[]{:S(2)}, u32[]{:S(2)}) collective-permute-start(bf16[8,3,48,512]{3,2,1,0:T(8,128)(2,1)} %carve.4), channel_id=1, source_target_pairs={{0,64},{64,0},{1,65},{65,1},{2,66},{66,2},{3,67},{67,3},{4,68},{68... | collective-permute-start | bytes 3538952 | tf_op jit(solution)/shard_map/ppermute | solution.py:18
  39.6 1.1 copy-start
  44.1 12.0 %copy-start.1 = (bf16[8,6,32,512]{3,2,1,0:T(8,128)(2,1)S(1)}, bf16[8,6,32,512]{3,2,1,0:T(8,128)(2,1)}, u32[]{:S(2)}) copy-start(bf16[8,6,32,512]{3,2,1,0:T(8,128)(2,1)} %copy-done) | copy-start | bytes 4718596
  44.1 79.1 %collective-permute-start.9 = (bf16[8,3,48,512]{3,2,1,0:T(8,128)(2,1)}, bf16[8,3,48,512]{3,2,1,0:T(8,128)(2,1)S(1)}, u32[]{:S(2)}, u32[]{:S(2)}) collective-permute-start(bf16[8,3,48,512]{3,2,1,0:T(8,128)(2,1)} %carve.6), channel_id=1, source_target_pairs={{0,64},{64,0},{1,65},{65,1},{2,66},{66,2},{3,67},{67,3},{4,68},{68... | collective-permute-start | bytes 3538952 | tf_op jit(solution)/shard_map/ppermute | solution.py:18
  56.8 10.6 %copy-start.9 = (bf16[4,4,2,6,8,512]{5,4,3,2,1,0:T(8,128)(2,1)S(1)}, bf16[4,4,2,6,8,512]{5,4,3,2,1,0:T(8,128)(2,1)}, u32[]{:S(2)}) copy-start(bf16[4,4,2,6,8,512]{5,4,3,2,1,0:T(8,128)(2,1)} %copy-done.8) | copy-start | bytes 4718596
  93.1 6.9 %copy-start.10 = (s32[4,4]{1,0:T(4,128)S(1)}, s32[4,4]{1,0:T(4,128)}, u32[]{:S(2)}) copy-start(s32[4,4]{1,0:T(4,128)} %param.9) | copy-start | bytes 196
  94.1 12.0 %collective-permute-start.2 = (f32[4,2,80,128]{3,2,1,0:T(8,128)}, f32[4,2,80,128]{3,2,1,0:T(8,128)S(1)}, u32[]{:S(2)}, u32[]{:S(2)}) collective-permute-start(f32[4,2,80,128]{3,2,1,0:T(8,128)} %get-tuple-element.16), channel_id=1, source_target_pairs={{0,8},{8,16},{16,24},{24,0},{1,9},{9,17},{17,25},{25,1},{2,10},{10... | collective-permute-start | bytes 983048 | tf_op jit(solution)/shard_map/ppermute | solution.py:168
  96.0 15.7 %collective-permute-start.3 = (f32[4,2,80,128]{3,2,1,0:T(8,128)}, f32[4,2,80,128]{3,2,1,0:T(8,128)S(1)}, u32[]{:S(2)}, u32[]{:S(2)}) collective-permute-start(f32[4,2,80,128]{3,2,1,0:T(8,128)} %get-tuple-element.17), channel_id=1, source_target_pairs={{0,24},{8,0},{16,8},{24,16},{1,25},{9,1},{17,9},{25,17},{2,26},{10... | collective-permute-start | bytes 983048 | tf_op jit(solution)/shard_map/ppermute | solution.py:168
  98.1 15.4 %collective-permute-start.4 = (f32[4,2,80,128]{3,2,1,0:T(8,128)S(1)}, f32[4,2,80,128]{3,2,1,0:T(8,128)}, u32[]{:S(2)}, u32[]{:S(2)}) collective-permute-start(f32[4,2,80,128]{3,2,1,0:T(8,128)S(1)} %get-tuple-element.18), channel_id=1, source_target_pairs={{0,16},{8,24},{16,0},{24,8},{1,17},{9,25},{17,1},{25,9},{2,18},{10... | collective-permute-start | bytes 983048 | tf_op jit(solution)/shard_map/ppermute | solution.py:168
  114.6 19.2 %copy-start.2 = (f32[4,2,80,128]{3,2,1,0:T(8,128)}, f32[4,2,80,128]{3,2,1,0:T(8,128)S(1)}, u32[]{:S(2)}) copy-start(f32[4,2,80,128]{3,2,1,0:T(8,128)S(1)} %fusion.1.refs_3_.refs_0_) | copy-start | bytes 983044
  114.6 19.2 %collective-permute-start.5 = (f32[2,80,128]{2,1,0:T(8,128)S(1)}, f32[2,80,128]{2,1,0:T(8,128)S(1)}, u32[]{:S(2)}, u32[]{:S(2)}) collective-permute-start(f32[2,80,128]{2,1,0:T(8,128)S(1)} %get-tuple-element.25), channel_id=1, source_target_pairs={{0,2},{2,4},{4,6},{6,0},{1,3},{3,5},{5,7},{7,1},{8,10},{10,12},{12... | collective-permute-start | bytes 245768 | tf_op jit(solution)/shard_map/ppermute | solution.py:181
  116.2 17.6 %collective-permute-start.6 = (f32[2,80,128]{2,1,0:T(8,128)S(1)}, f32[2,80,128]{2,1,0:T(8,128)S(1)}, u32[]{:S(2)}, u32[]{:S(2)}) collective-permute-start(f32[2,80,128]{2,1,0:T(8,128)S(1)} %get-tuple-element.27), channel_id=1, source_target_pairs={{0,6},{2,0},{4,2},{6,4},{1,7},{3,1},{5,3},{7,5},{8,14},{10,8},{12,... | collective-permute-start | bytes 245768 | tf_op jit(solution)/shard_map/ppermute | solution.py:181
  117.9 15.9 %collective-permute-start.7 = (f32[2,80,128]{2,1,0:T(8,128)S(1)}, f32[2,80,128]{2,1,0:T(8,128)S(1)}, u32[]{:S(2)}, u32[]{:S(2)}) collective-permute-start(f32[2,80,128]{2,1,0:T(8,128)S(1)} %get-tuple-element.26), channel_id=1, source_target_pairs={{0,4},{2,6},{4,0},{6,2},{1,5},{3,7},{5,1},{7,3},{8,12},{10,14},{12... | collective-permute-start | bytes 245768 | tf_op jit(solution)/shard_map/ppermute | solution.py:181
  123.2 1.1 copy-start.3
  127.7 1.3 copy-start.6
  129.0 4.9 %copy-start.4 = (bf16[8,3,48,512]{3,2,1,0:T(8,128)(2,1)S(1)}, bf16[8,3,48,512]{3,2,1,0:T(8,128)(2,1)}, u32[]{:S(2)}) copy-start(bf16[8,3,48,512]{3,2,1,0:T(8,128)(2,1)} %copy-done.3) | copy-start | bytes 3538948
  129.0 4.9 %copy-start.5 = (bf16[8,3,48,512]{3,2,1,0:T(8,128)(2,1)S(1)}, bf16[8,3,48,512]{3,2,1,0:T(8,128)(2,1)}, u32[]{:S(2)}) copy-start(bf16[8,3,48,512]{3,2,1,0:T(8,128)(2,1)} %carve.7.refs_5_) | copy-start | bytes 3538948
  133.9 8.7 %copy-start.7 = (bf16[8,3,48,512]{3,2,1,0:T(8,128)(2,1)S(1)}, bf16[8,3,48,512]{3,2,1,0:T(8,128)(2,1)}, u32[]{:S(2)}) copy-start(bf16[8,3,48,512]{3,2,1,0:T(8,128)(2,1)} %carve.5.refs_4_) | copy-start | bytes 3538948
  138.5 14.6 %copy-start.11 = (s32[4]{0:T(128)S(1)}, s32[4]{0:T(128)}, u32[]{:S(2)}) copy-start(s32[4]{0:T(128)} %param.7) | copy-start | bytes 52
  138.5 6.3 %collective-permute-start.10 = (f32[2,2,48,128]{3,2,1,0:T(8,128)S(1)}, f32[2,2,48,128]{3,2,1,0:T(8,128)S(1)}, u32[]{:S(2)}, u32[]{:S(2)}) collective-permute-start(f32[2,2,48,128]{3,2,1,0:T(8,128)S(1)} %get-tuple-element.22), channel_id=1, source_target_pairs={{0,8},{8,16},{16,24},{24,0},{1,9},{9,17},{17,25},{25,1},{2,10},{10... | collective-permute-start | bytes 294920 | tf_op jit(solution)/shard_map/ppermute | solution.py:168
  139.7 5.3 %collective-permute-start.11 = (f32[2,2,48,128]{3,2,1,0:T(8,128)S(1)}, f32[2,2,48,128]{3,2,1,0:T(8,128)S(1)}, u32[]{:S(2)}, u32[]{:S(2)}) collective-permute-start(f32[2,2,48,128]{3,2,1,0:T(8,128)S(1)} %get-tuple-element.23), channel_id=1, source_target_pairs={{0,24},{8,0},{16,8},{24,16},{1,25},{9,1},{17,9},{25,17},{2,26},{10... | collective-permute-start | bytes 294920 | tf_op jit(solution)/shard_map/ppermute | solution.py:168
  141.8 6.1 %collective-permute-start.12 = (f32[2,2,48,128]{3,2,1,0:T(8,128)S(1)}, f32[2,2,48,128]{3,2,1,0:T(8,128)S(1)}, u32[]{:S(2)}, u32[]{:S(2)}) collective-permute-start(f32[2,2,48,128]{3,2,1,0:T(8,128)S(1)} %get-tuple-element.24), channel_id=1, source_target_pairs={{0,16},{8,24},{16,0},{24,8},{1,17},{9,25},{17,1},{25,9},{2,18},{10... | collective-permute-start | bytes 294920 | tf_op jit(solution)/shard_map/ppermute | solution.py:168
  142.6 53.5 %collective-permute-start.18 = (bf16[8,3,48,512]{3,2,1,0:T(8,128)(2,1)S(1)}, bf16[8,3,48,512]{3,2,1,0:T(8,128)(2,1)}, u32[]{:S(2)}, u32[]{:S(2)}) collective-permute-start(bf16[8,3,48,512]{3,2,1,0:T(8,128)(2,1)S(1)} %copy-done.7), channel_id=1, source_target_pairs={{0,64},{64,0},{1,65},{65,1},{2,66},{66,2},{3,67},{67,3},{4,68},{68... | collective-permute-start | bytes 3538952 | tf_op jit(solution)/shard_map/ppermute | solution.py:18
  143.2 57.6 %collective-permute-start.19 = (bf16[8,3,48,512]{3,2,1,0:T(8,128)(2,1)S(1)}, bf16[8,3,48,512]{3,2,1,0:T(8,128)(2,1)}, u32[]{:S(2)}, u32[]{:S(2)}) collective-permute-start(bf16[8,3,48,512]{3,2,1,0:T(8,128)(2,1)S(1)} %copy-done.5), channel_id=1, source_target_pairs={{0,64},{64,0},{1,65},{65,1},{2,66},{66,2},{3,67},{67,3},{4,68},{68... | collective-permute-start | bytes 3538952 | tf_op jit(solution)/shard_map/ppermute | solution.py:18
  148.0 9.5 %collective-permute-start.13 = (f32[2,48,128]{2,1,0:T(8,128)S(1)}, f32[2,48,128]{2,1,0:T(8,128)S(1)}, u32[]{:S(2)}, u32[]{:S(2)}) collective-permute-start(f32[2,48,128]{2,1,0:T(8,128)S(1)} %get-tuple-element.31), channel_id=1, source_target_pairs={{0,2},{6,0},{1,3},{7,1},{8,10},{14,8},{9,11},{15,9},{16,18},{22,16... | collective-permute-start | bytes 147464 | tf_op jit(solution)/shard_map/ppermute | solution.py:181
  150.5 7.0 %collective-permute-start.14 = (f32[2,48,128]{2,1,0:T(8,128)S(1)}, f32[2,48,128]{2,1,0:T(8,128)S(1)}, u32[]{:S(2)}, u32[]{:S(2)}) collective-permute-start(f32[2,48,128]{2,1,0:T(8,128)S(1)} %get-tuple-element.33), channel_id=1, source_target_pairs={{2,0},{4,2},{3,1},{5,3},{10,8},{12,10},{11,9},{13,11},{18,16},{20,... | collective-permute-start | bytes 147464 | tf_op jit(solution)/shard_map/ppermute | solution.py:181
  151.8 7.5 %collective-permute-start.15 = (f32[2,48,128]{2,1,0:T(8,128)S(1)}, f32[2,48,128]{2,1,0:T(8,128)S(1)}, u32[]{:S(2)}, u32[]{:S(2)}) collective-permute-start(f32[2,48,128]{2,1,0:T(8,128)S(1)} %get-tuple-element.32), channel_id=1, source_target_pairs={{4,0},{6,2},{5,1},{7,3},{12,8},{14,10},{13,9},{15,11},{20,16},{22,... | collective-permute-start | bytes 147464 | tf_op jit(solution)/shard_map/ppermute | solution.py:181
  157.5 5.0 %collective-permute-start.28 = (bf16[4,6,512]{2,1,0:T(8,128)(2,1)}, bf16[4,6,512]{2,1,0:T(8,128)(2,1)S(1)}, u32[]{:S(2)}, u32[]{:S(2)}) collective-permute-start(bf16[4,6,512]{2,1,0:T(8,128)(2,1)} %choose.1), channel_id=1, source_target_pairs={{0,32},{32,0},{1,33},{33,1},{2,34},{34,2},{3,35},{35,3},{4,36},{36... | collective-permute-start | bytes 73736 | tf_op jit(solution)/shard_map/ppermute | solution.py:18
  159.3 36.6 %collective-permute-start.16 = (f32[128,128]{1,0:T(8,128)S(1)}, f32[128,128]{1,0:T(8,128)S(1)}, u32[]{:S(2)}, u32[]{:S(2)}) collective-permute-start(f32[128,128]{1,0:T(8,128)S(1)} %fusion.27), channel_id=1, source_target_pairs={{0,1},{1,0},{2,3},{3,2},{4,5},{5,4},{6,7},{7,6},{8,9},{9,8},{10,11... | collective-permute-start | bytes 196616 | tf_op jit(solution)/shard_map/ppermute | solution.py:18
  163.3 32.8 %collective-permute-start.29 = (bf16[4,6,512]{2,1,0:T(8,128)(2,1)S(1)}, bf16[4,6,512]{2,1,0:T(8,128)(2,1)S(1)}, u32[]{:S(2)}, u32[]{:S(2)}) collective-permute-start(bf16[4,6,512]{2,1,0:T(8,128)(2,1)S(1)} %add.242), channel_id=1, source_target_pairs={{0,64},{64,0},{1,65},{65,1},{2,66},{66,2},{3,67},{67,3},{4,68},{68... | collective-permute-start | bytes 73736 | tf_op jit(solution)/shard_map/ppermute | solution.py:18
  195.9 4.9 %collective-permute-start.17 = (f32[128,128]{1,0:T(8,128)S(1)}, f32[128,128]{1,0:T(8,128)S(1)}, u32[]{:S(2)}, u32[]{:S(2)}) collective-permute-start(f32[128,128]{1,0:T(8,128)S(1)} %fusion.30), channel_id=1, source_target_pairs={{0,32},{32,0},{1,33},{33,1},{2,34},{34,2},{3,35},{35,3},{4,36},{36... | collective-permute-start | bytes 196616 | tf_op jit(solution)/shard_map/ppermute | solution.py:18
  205.5 6.5 %collective-permute-start.20 = (f32[2,2,48,128]{3,2,1,0:T(8,128)S(1)}, f32[2,2,48,128]{3,2,1,0:T(8,128)S(1)}, u32[]{:S(2)}, u32[]{:S(2)}) collective-permute-start(f32[2,2,48,128]{3,2,1,0:T(8,128)S(1)} %get-tuple-element.19), channel_id=1, source_target_pairs={{0,8},{8,16},{16,24},{24,0},{1,9},{9,17},{17,25},{25,1},{2,10},{10... | collective-permute-start | bytes 294920 | tf_op jit(solution)/shard_map/ppermute | solution.py:168
  206.4 7.0 %collective-permute-start.21 = (f32[2,2,48,128]{3,2,1,0:T(8,128)S(1)}, f32[2,2,48,128]{3,2,1,0:T(8,128)S(1)}, u32[]{:S(2)}, u32[]{:S(2)}) collective-permute-start(f32[2,2,48,128]{3,2,1,0:T(8,128)S(1)} %get-tuple-element.20), channel_id=1, source_target_pairs={{0,24},{8,0},{16,8},{24,16},{1,25},{9,1},{17,9},{25,17},{2,26},{10... | collective-permute-start | bytes 294920 | tf_op jit(solution)/shard_map/ppermute | solution.py:168
  208.8 6.1 %collective-permute-start.22 = (f32[2,2,48,128]{3,2,1,0:T(8,128)S(1)}, f32[2,2,48,128]{3,2,1,0:T(8,128)S(1)}, u32[]{:S(2)}, u32[]{:S(2)}) collective-permute-start(f32[2,2,48,128]{3,2,1,0:T(8,128)S(1)} %get-tuple-element.21), channel_id=1, source_target_pairs={{0,16},{8,24},{16,0},{24,8},{1,17},{9,25},{17,1},{25,9},{2,18},{10... | collective-permute-start | bytes 294920 | tf_op jit(solution)/shard_map/ppermute | solution.py:168
  215.0 7.7 %collective-permute-start.23 = (f32[2,48,128]{2,1,0:T(8,128)S(1)}, f32[2,48,128]{2,1,0:T(8,128)S(1)}, u32[]{:S(2)}, u32[]{:S(2)}) collective-permute-start(f32[2,48,128]{2,1,0:T(8,128)S(1)} %get-tuple-element.28), channel_id=1, source_target_pairs={{2,4},{4,6},{3,5},{5,7},{10,12},{12,14},{11,13},{13,15},{18,20},{2... | collective-permute-start | bytes 147464 | tf_op jit(solution)/shard_map/ppermute | solution.py:181
  215.7 7.1 %collective-permute-start.24 = (f32[2,48,128]{2,1,0:T(8,128)S(1)}, f32[2,48,128]{2,1,0:T(8,128)S(1)}, u32[]{:S(2)}, u32[]{:S(2)}) collective-permute-start(f32[2,48,128]{2,1,0:T(8,128)S(1)} %get-tuple-element.30), channel_id=1, source_target_pairs={{0,6},{6,4},{1,7},{7,5},{8,14},{14,12},{9,15},{15,13},{16,22},{22,... | collective-permute-start | bytes 147464 | tf_op jit(solution)/shard_map/ppermute | solution.py:181
  219.4 5.1 %collective-permute-start.25 = (f32[2,48,128]{2,1,0:T(8,128)S(1)}, f32[2,48,128]{2,1,0:T(8,128)S(1)}, u32[]{:S(2)}, u32[]{:S(2)}) collective-permute-start(f32[2,48,128]{2,1,0:T(8,128)S(1)} %get-tuple-element.29), channel_id=1, source_target_pairs={{0,4},{2,6},{1,5},{3,7},{8,12},{10,14},{9,13},{11,15},{16,20},{18,... | collective-permute-start | bytes 147464 | tf_op jit(solution)/shard_map/ppermute | solution.py:181
  224.5 5.4 %collective-permute-start.26 = (f32[48,128]{1,0:T(8,128)S(1)}, f32[48,128]{1,0:T(8,128)S(1)}, u32[]{:S(2)}, u32[]{:S(2)}) collective-permute-start(f32[48,128]{1,0:T(8,128)S(1)} %dynamic-slice_bitcast_fusion.12), channel_id=1, source_target_pairs={{0,1},{1,0},{2,3},{3,2},{4,5},{5,4},{6,7},{7,6},{8,9},{9,8},{10,11... | collective-permute-start | bytes 73736 | tf_op jit(solution)/shard_map/ppermute | solution.py:18
  229.9 1.2 collective-permute-start.27

commit v3 on v2

--- a/solution.py
+++ b/solution.py
@@ -24,9 +24,9 @@
 def by_time_kernel(cuts, block, *outs):
     for k in range(block.shape[1]):
         turned = jnp.swapaxes(block[:, k], 0, 1)
-        for t in range(turned.shape[0]):
-            for (low, high), out in zip(cuts, outs):
-                out[t // 2, 0, t % 2, k] = turned[t, low:high]
+        for (low, high, first, size), out in zip(cuts, outs):
+            for t in range(2 * size):
+                out[t // 2, 0, t % 2, k] = turned[2 * first + t, low:high]
 
 
 def by_time(block, cuts):
@@ -36,13 +36,14 @@
         grid=(4,),
         in_specs=[pl.BlockSpec((n, comps, times // 4, sites), lambda z: (0, 0, z, 0))],
         out_specs=[
-            pl.BlockSpec((4, 1, 2, comps, h - l, sites), lambda z: (0, z, 0, 0, 0, 0))
-            for l, h in cuts
+            pl.BlockSpec((size, 1, 2, comps, high - low, sites), lambda z: (0, z, 0, 0, 0, 0))
+            for low, high, _, size in cuts
         ],
         out_shape=[
-            jax.ShapeDtypeStruct((4, 4, 2, comps, h - l, sites), block.dtype) for l, h in cuts
+            jax.ShapeDtypeStruct((size, 4, 2, comps, high - low, sites), block.dtype)
+            for low, high, _, size in cuts
         ],
-        compiler_params=pltpu.CompilerParams(vmem_limit_bytes=48 * 2**20),
+        compiler_params=pltpu.CompilerParams(vmem_limit_bytes=56 * 2**20),
         cost_estimate=HINT,
         name="by_time",
     )(block)
@@ -54,25 +55,6 @@
 
 
 ANY = pl.BlockSpec(memory_space=pl.ANY)
-
-
-def carve_kernel(block, *refs):
-    refs[-1][...] = block[0]
-
-
-def carve(late, x, *after):
-    _, inner, colours, n, sites = late.shape
-    return pl.pallas_call(
-        carve_kernel,
-        grid=(4,),
-        in_specs=[pl.BlockSpec((1, inner // 4, colours, n, sites), lambda i: (x, i, 0, 0, 0))]
-        + [ANY] * len(after),
-        out_specs=pl.BlockSpec((inner // 4, colours, n, sites), lambda i: (i, 0, 0, 0)),
-        out_shape=jax.ShapeDtypeStruct((inner, colours, n, sites), late.dtype),
-        compiler_params=pltpu.CompilerParams(vmem_limit_bytes=60 * 2**20),
-        cost_estimate=HINT,
-        name="carve",
-    )(late, *after)
 
 
 def choose_kernel(owned, rows, at, block, *refs):
@@ -111,24 +93,27 @@
     cols, (own, other), outs = refs[:count], refs[count : count + 2], refs[-count:]
     width = own.shape[3] // 2
     for at in range(own.shape[1]):
+        total = None
+        for colour in range(own.shape[2]):
+            term = lax.dot_general(
+                jnp.concatenate([col[0, at, colour] for col in cols], axis=0),
+                jnp.concatenate([own[0, at, colour], other[0, at, colour]], axis=0),
+                (((1,), (1,)), ((), ())),
+                preferred_element_type=jnp.float32,
+            )
+            total = term if total is None else total + term
+        row = 0
         for col, out in zip(cols, outs):
             n = col.shape[3] // 2
-            halves = []
-            for vecs in (own, other):
-                total = None
-                for colour in range(vecs.shape[2]):
-                    term = lax.dot_general(
-                        col[0, at, colour],
-                        vecs[0, at, colour],
-                        (((1,), (1,)), ((), ())),
-                        preferred_element_type=jnp.float32,
-                    )
-                    total = term if total is None else total + term
-                real = total[:n, :width] + total[n:, width:]
-                imag = total[n:, :width] - total[:n, width:]
-                halves.append((real, imag))
-            for part in range(2):
-                out[0, at, part] = jnp.concatenate([halves[0][part], halves[1][part]], axis=1)
+            re, im = total[row : row + n], total[row + n : row + 2 * n]
+            row += 2 * n
+            real, imag = [], []
+            for left in (0, 2 * width):
+                mid, right = left + width, left + 2 * width
+                real.append(re[:, left:mid] + im[:, mid:right])
+                imag.append(im[:, left:mid] - re[:, mid:right])
+            out[0, at, 0] = jnp.concatenate(real, axis=1)
+            out[0, at, 1] = jnp.concatenate(imag, axis=1)
 
 
 def project(cols, own, other, first, size, step, *after):
@@ -199,52 +184,43 @@
 
     raw = swap(sols[:RAW], "yl")
     other = swap(vecs, "c")
-    early, late = by_time(sols, ((0, RAW), (RAW, count)))
-    late = rows_of(late)
-    send = [carve(late, 0), carve(late, 1, raw)]
-    got = [swap(send[0], "yl"), swap(send[1], "yl")]
-    send.append(carve(late, 2, got[0]))
-    got.append(swap(send[2], "yl"))
-    send.append(carve(late, 3, got[1]))
-    got.append(swap(send[3], "yl"))
-
-    whole = ((0, owned),)
+    sent = ((RAW, count, 0, 2), (RAW, count, 2, 1), (RAW, count, 3, 1))
+    mine, *send = by_time(sols, ((0, count, 0, 4), *sent))
+    got = [swap(rows_of(part), "yl") for part in send]
+
+    whole = ((0, owned, 0, 4),)
     own = rows_of(by_time(vecs, whole)[0])
     other = rows_of(by_time(other, whole)[0])
-    raw = rows_of(by_time(raw, ((0, RAW),))[0])
+    raw = rows_of(by_time(raw, ((0, RAW, 0, 4),))[0])
 
     def rows(part):
         x, inner, _, n, lanes = part.shape
         return part.reshape(x, 4, 2, 2 * n, lanes)
 
-    def against(x, *after):
-        return rows(project([got[x][None]], own, other, x, 1, 4, *after)[0])
-
-    parts = project([rows_of(early), late, raw], own, other, 0, 4, 4)
+    def against(part, x, step, *after):
+        return rows(project([part], own, other, x, part.shape[0], step, *after)[0])
+
+    parts = project([rows_of(mine), raw], own, other, 0, 4, 8)
     first_z = sum_z(jnp.concatenate([rows(p) for p in parts], axis=3))
     chosen = choose(vecs, source_index, source_time, group, first_z)
     first = sum_x(first_z, 0, 4)
-    mid = [against(0, first_z, send[2])]
-    mid.append(against(1, first, mid[0], send[3]))
-    mid_z = sum_z(jnp.concatenate(mid, axis=0))
-    last = [against(2, mid_z)]
-    mid = sum_x(mid_z, 0, 2)
+    mid = [against(got[0], 0, 8, first_z)]
+    mid.append(against(got[1], 2, 4, first))
+    mid = sum_x(sum_z(jnp.concatenate(mid, axis=0)), 0, 3)
     main = sum_yh(jnp.concatenate([first, mid], axis=1))
     main_c = swap(main, "c")
-    last.append(against(3, main_c, last[0]))
-    last = sum_x(sum_z(jnp.concatenate(last, axis=0)), 2, 2)
-    last = sum_yh(last)
+    last = sum_yh(sum_x(sum_z(against(got[2], 3, 2, mid)), 3, 1))
     last_c = swap(last, "c")
-    is_last = lax.axis_index("x") >= 2
+    is_last = lax.axis_index("x") == 3
 
     def assemble(main, last, half):
         main = main[:, half * owned : (half + 1) * owned]
         last = last[:, half * owned : (half + 1) * owned]
-        cut = [2 * RAW, 2 * count, 2 * (count + RAW)]
         view = lambda v: v.reshape(2, -1, owned)
-        home = jnp.concatenate([view(main[: cut[0]]), view(main[cut[0] : cut[1]])], axis=1)
-        rest = jnp.where(is_last, last, main[cut[2] :])
-        away = jnp.concatenate([view(main[cut[1] : cut[2]]), view(rest)], axis=1)
+        cut = [2 * count, 2 * (count + RAW)]
+        home = view(main[: cut[0]])
+        rest = jnp.where(is_last, last, main[cut[1] :])
+        away = jnp.concatenate([view(main[cut[0] : cut[1]]), view(rest)], axis=1)
         return home, away
 
     h0, y0 = assemble(main, last, 0)

time: 236 us -> 187 us (0.79)
  waiting for transfers between devices: 84.7 us -> 55.2 us
  Pallas kernels: 89.3 us -> 66.1 us
  starting transfers between devices: 43.4 us -> 51.2 us
  local copies, waits for them, and re-layouts: 9.04 us -> 5.17 us
    ppermute x12 -> x11, waiting for transfers between devices: 61.9 us -> 38.9 us  [swap(): return lax.ppermute(value, axis, SWAP)]
    pallas_call x5 -> x4, Pallas kernels: 44.3 us -> 29.9 us  [project(): pl.pallas_call(functools.partial(dot_kernel, len(cols)), grid=(size, inne...]
    pallas_call x4 -> x0, Pallas kernels: 13.6 us -> none  [carve(): pl.pallas_call(carve_kernel, grid=(4,), in_specs=[pl.BlockSpec((1, inner...]
    ppermute x9, waiting for transfers between devices: 19.4 us -> 14 us  [sum_z(): lax.ppermute(pick(slabs, (me + k) % 4), 'z', [(i, (i + k) % 4) for i in r...]
    pallas_call x4, Pallas kernels: 27.6 us -> 32.3 us  [by_time(): pl.pallas_call(functools.partial(by_time_kernel, cuts), grid=(4,), in_spe...]
    unnamed x26 -> x16, local copies, waits for them, and re-layouts: 5.48 us -> 0.84 us
    ppermute x9, starting transfers between devices: 14.6 us -> 18.1 us  [sum_z(): lax.ppermute(pick(slabs, (me + k) % 4), 'z', [(i, (i + k) % 4) for i in r...]
    ppermute x9, starting transfers between devices: 17.9 us -> 20.7 us  [sum_x(): total = total + lax.ppermute(send, 'x', pairs)]
  transfers between devices with their start and end apart: 30 -> 29, of which waited for: 15 -> 11; matrix products, arithmetic and copies ran while one was open for 3% -> 5% of each run, Pallas kernels for 34% -> 33%
where the time goes in v3:
time: 187 us; the launch traced here: 184 us
  Pallas kernels  66.1 us (35%)
  waiting for transfers between devices  55.2 us (30%)
  starting transfers between devices  51.2 us (27%)
  local copies, waits for them, and re-layouts  5.17 us (3%)
  other arithmetic  4.6 us (2%)
    ppermute x11, waiting for transfers between devices, swap(): return lax.ppermute(value, axis, SWAP)  38.9 us
    pallas_call x4, Pallas kernels, by_time(): pl.pallas_call(functools.partial(by_time_kernel, cuts), grid=(4,), in_spe...  32.3 us
    pallas_call x4, Pallas kernels, project(): pl.pallas_call(functools.partial(dot_kernel, len(cols)), grid=(size, inne...  29.9 us
    ppermute x9, starting transfers between devices, sum_x(): total = total + lax.ppermute(send, 'x', pairs)  20.7 us
    ppermute x9, starting transfers between devices, sum_z(): lax.ppermute(pick(slabs, (me + k) % 4), 'z', [(i, (i + k) % 4) for i in r...  18.1 us
    ppermute x9, waiting for transfers between devices, sum_z(): lax.ppermute(pick(slabs, (me + k) % 4), 'z', [(i, (i + k) % 4) for i in r...  14 us
    ppermute x11, starting transfers between devices, swap(): return lax.ppermute(value, axis, SWAP)  12.4 us
    pallas_call x1, Pallas kernels, choose(): pl.pallas_call(functools.partial(choose_kernel, owned, rows), grid_spec=p...  3.92 us
  transfers between devices with their start and end apart: 29, of which 11 were waited for; matrix products, arithmetic and copies ran while one was open for 5% of the time, Pallas kernels for 33%

profile of v3, /device:TPU:0, one launch (start us, length us, event | category | flops | bytes accessed | tf_op | source)
XLA Modules:
  0.0 184.0 jit_solution(2826416836695208852)
XLA Ops:
  0.6 0.1 collective-permute-start.1
  0.7 2.8 %slice.46 = bf16[8,6,32,512]{3,2,1,0:T(8,128)(2,1)} slice(bf16[32,6,32,512]{3,2,1,0:T(8,128)(2,1)} %bitcast.153), slice={[0:8], [0:6], [0:32], [0:512]} | slice | bytes 3145728 | tf_op jit(solution)/shard_map/slice | solution.py:185
  3.5 1.7 collective-permute-start
  5.1 7.6 %by_time.4 = (bf16[4,4,2,6,32,512]{5,4,3,2,1,0:T(8,128)(2,1)}, bf16[2,4,2,6,24,512]{5,4,3,2,1,0:T(8,128)(2,1)}, bf16[1,4,2,6,24,512]{5,4,3,2,1,0:T(8,128)(2,1)}, bf16[1,4,2,6,24,512]{5,4,3,2,1,0:T(8,128)(2,1)}) custom-call(bf16[32,6,32,512]{3,2,1,0:T(8,128)(2,1)} %bitcast.154), custom_call_target="tpu_custom_call" | custom-call | flops 1000 | bytes 1000 | tf_op jit(solution)/shard_map/by_time/pallas_call | solution.py:34
  12.8 0.4 collective-permute-start.8
  13.2 1.7 collective-permute-start.9
  14.8 10.4 %by_time.6 = bf16[4,4,2,6,64,512]{5,4,3,2,1,0:T(8,128)(2,1)} custom-call(bf16[64,6,32,512]{3,2,1,0:T(8,128)(2,1)} %bitcast.151), custom_call_target="tpu_custom_call" | custom-call | flops 1000 | bytes 1000 | tf_op jit(solution)/shard_map/by_time/pallas_call | solution.py:34
  25.9 0.1 copy.14
  26.0 0.1 fusion.35
  26.0 0.6 gather_fusion
  26.6 0.6 pad_add_fusion.at
  27.2 13.8 %collective-permute-done.block = bf16[8,6,32,512]{3,2,1,0:T(8,128)(2,1)} collective-permute-done((bf16[8,6,32,512]{3,2,1,0:T(8,128)(2,1)}, bf16[8,6,32,512]{3,2,1,0:T(8,128)(2,1)}, u32[]{:S(2)}, u32[]{:S(2)}) %collective-permute-start) | collective-permute-done | bytes 1572896 | tf_op jit(solution)/shard_map/ppermute | solution.py:18
  41.0 3.7 %by_time.5 = bf16[4,4,2,6,8,512]{5,4,3,2,1,0:T(8,128)(2,1)} custom-call(bf16[8,6,32,512]{3,2,1,0:T(8,128)(2,1)} %collective-permute-done.block), custom_call_target="tpu_custom_call" | custom-call | flops 1000 | bytes 1000 | tf_op jit(solution)/shard_map/by_time/pallas_call | solution.py:34
  44.7 10.6 %by_time.7 = bf16[4,4,2,6,64,512]{5,4,3,2,1,0:T(8,128)(2,1)} custom-call(bf16[64,6,32,512]{3,2,1,0:T(8,128)(2,1)} %collective-permute-done.1.block), custom_call_target="tpu_custom_call" | custom-call | flops 1000 | bytes 1000 | tf_op jit(solution)/shard_map/by_time/pallas_call | solution.py:34
  55.3 13.4 %project.4 = (f32[4,8,2,32,128]{4,3,2,1,0:T(8,128)S(1)}, f32[4,8,2,8,128]{4,3,2,1,0:T(8,128)S(1)}) custom-call(bf16[4,8,3,64,512]{4,3,2,1,0:T(8,128)(2,1)} %bitcast.155, bf16[4,8,3,16,512]{4,3,2,1,0:T(8,128)(2,1)S(1)} %bitcast.131, bf16[4,8,3,128,512]{4,3,2,1,0:T(8,128)(2,1)} %bitcast.142, bf16[4,8,3,128,512]{4,3,2,1,0:T(8,128)(2,1)} %bitcast.146), custom_call_target="tpu_custom_call" | custom-call | flops 1000 | bytes 1000 | tf_op jit(solution)/shard_map/project/pallas_call | solution.py:132
  68.7 0.1 fusion.8
  68.8 2.1 %collective-permute-start.2 = (f32[4,2,80,128]{3,2,1,0:T(8,128)S(1)}, f32[4,2,80,128]{3,2,1,0:T(8,128)S(1)}, u32[]{:S(2)}, u32[]{:S(2)}) collective-permute-start(f32[4,2,80,128]{3,2,1,0:T(8,128)S(1)} %get-tuple-element.18), channel_id=1, source_target_pairs={{0,8},{8,16},{16,24},{24,0},{1,9},{9,17},{17,25},{25,1},{2,10},{10... | collective-permute-start | bytes 983048 | tf_op jit(solution)/shard_map/ppermute | solution.py:153
  70.9 2.2 %collective-permute-start.3 = (f32[4,2,80,128]{3,2,1,0:T(8,128)S(1)}, f32[4,2,80,128]{3,2,1,0:T(8,128)S(1)}, u32[]{:S(2)}, u32[]{:S(2)}) collective-permute-start(f32[4,2,80,128]{3,2,1,0:T(8,128)S(1)} %get-tuple-element.19), channel_id=1, source_target_pairs={{0,24},{8,0},{16,8},{24,16},{1,25},{9,1},{17,9},{25,17},{2,26},{10... | collective-permute-start | bytes 983048 | tf_op jit(solution)/shard_map/ppermute | solution.py:153
  73.1 1.8 collective-permute-start.4
  74.8 0.1 compare_and_fusion
  74.9 0.1 broadcast_select_fusion.1
  75.0 5.7 %collective-permute-done.2 = f32[4,2,80,128]{3,2,1,0:T(8,128)S(1)} collective-permute-done((f32[4,2,80,128]{3,2,1,0:T(8,128)S(1)}, f32[4,2,80,128]{3,2,1,0:T(8,128)S(1)}, u32[]{:S(2)}, u32[]{:S(2)}) %collective-permute-start.2) | collective-permute-done | bytes 327712 | tf_op jit(solution)/shard_map/ppermute | solution.py:153
  80.7 5.8 %collective-permute-done.3 = f32[4,2,80,128]{3,2,1,0:T(8,128)S(1)} collective-permute-done((f32[4,2,80,128]{3,2,1,0:T(8,128)S(1)}, f32[4,2,80,128]{3,2,1,0:T(8,128)S(1)}, u32[]{:S(2)}, u32[]{:S(2)}) %collective-permute-start.3) | collective-permute-done | bytes 327712 | tf_op jit(solution)/shard_map/ppermute | solution.py:153
  86.5 1.8 collective-permute-done.4
  88.4 0.8 fusion.6.refs_3_.refs_0_
  89.1 3.9 %choose.1 = bf16[4,6,512]{2,1,0:T(8,128)(2,1)} custom-call(s32[6]{0:T(128)} %pad_add_fusion.at, bf16[64,6,32,512]{3,2,1,0:T(8,128)(2,1)} %bitcast.152, f32[4,2,80,128]{3,2,1,0:T(8,128)} %fusion.6.refs_3_.refs_0_), custom_call_target="tpu_custom_call" | custom-call | flops 1000 | bytes 1000 | tf_op jit(solution)/shard_map/choose/pallas_call | solution.py:72
  93.1 1.6 collective-permute-start.5
  94.6 1.7 collective-permute-start.6
  96.4 1.8 collective-permute-start.7
  98.2 0.6 iota_compare_fusion
  98.8 0.7 fusion.34
  99.5 7.0 %project.5 = f32[2,8,2,24,128]{4,3,2,1,0:T(8,128)S(1)} custom-call(bf16[2,8,3,48,512]{4,3,2,1,0:T(8,128)(2,1)S(1)} %collective-permute-done.8.refs_0_, bf16[4,8,3,128,512]{4,3,2,1,0:T(8,128)(2,1)} %bitcast.143, bf16[4,8,3,128,512]{4,3,2,1,0:T(8,128)(2,1)} %bitcast.147, f32[4,2,80,128]{3,2,1,0:T(8,128)S(1)} %copy-done.1), custom_call_target="tpu_custom_call" | custom-call | flops 1000 | bytes 1000 | tf_op jit(solution)/shard_map/project/pallas_call | solution.py:132
  106.6 1.7 collective-permute-start.18
  108.2 0.5 collective-permute-start.28
  108.8 0.9 fusion.23.refs_3_
  109.7 7.1 %collective-permute-done.9.refs_0_ = bf16[1,8,3,48,512]{4,3,2,1,0:T(8,128)(2,1)} collective-permute-done((bf16[1,8,3,48,512]{4,3,2,1,0:T(8,128)(2,1)}, bf16[1,8,3,48,512]{4,3,2,1,0:T(8,128)(2,1)}, u32[]{:S(2)}, u32[]{:S(2)}) %collective-permute-start.9) | collective-permute-done | bytes 1179680 | tf_op jit(solution)/shard_map/ppermute | solution.py:18
  116.8 4.4 %project.6 = f32[1,8,2,24,128]{4,3,2,1,0:T(8,128)S(1)} custom-call(bf16[1,8,3,48,512]{4,3,2,1,0:T(8,128)(2,1)} %collective-permute-done.9.refs_0_, bf16[4,8,3,128,512]{4,3,2,1,0:T(8,128)(2,1)} %bitcast.144, bf16[4,8,3,128,512]{4,3,2,1,0:T(8,128)(2,1)} %bitcast.148, f32[2,80,128]{2,1,0:T(8,128)S(1)} %fusion.23.refs_3_), custom_call_target="tpu_custom_call" | custom-call | flops 1000 | bytes 1000 | tf_op jit(solution)/shard_map/project/pallas_call | solution.py:132
  121.3 2.1 %collective-permute-start.10 = (f32[3,2,48,128]{3,2,1,0:T(8,128)S(1)}, f32[3,2,48,128]{3,2,1,0:T(8,128)S(1)}, u32[]{:S(2)}, u32[]{:S(2)}) collective-permute-start(f32[3,2,48,128]{3,2,1,0:T(8,128)S(1)} %get-tuple-element.21), channel_id=1, source_target_pairs={{0,8},{8,16},{16,24},{24,0},{1,9},{9,17},{17,25},{25,1},{2,10},{10... | collective-permute-start | bytes 442376 | tf_op jit(solution)/shard_map/ppermute | solution.py:153
  123.4 2.2 %collective-permute-start.11 = (f32[3,2,48,128]{3,2,1,0:T(8,128)S(1)}, f32[3,2,48,128]{3,2,1,0:T(8,128)S(1)}, u32[]{:S(2)}, u32[]{:S(2)}) collective-permute-start(f32[3,2,48,128]{3,2,1,0:T(8,128)S(1)} %get-tuple-element.22), channel_id=1, source_target_pairs={{0,24},{8,0},{16,8},{24,16},{1,25},{9,1},{17,9},{25,17},{2,26},{10... | collective-permute-start | bytes 442376 | tf_op jit(solution)/shard_map/ppermute | solution.py:153
  125.6 1.8 collective-permute-start.12
  127.5 14.8 %collective-permute-done.28 = bf16[4,6,512]{2,1,0:T(8,128)(2,1)S(1)} collective-permute-done((bf16[4,6,512]{2,1,0:T(8,128)(2,1)S(1)}, bf16[4,6,512]{2,1,0:T(8,128)(2,1)S(1)}, u32[]{:S(2)}, u32[]{:S(2)}) %collective-permute-start.28) | collective-permute-done | bytes 24608 | tf_op jit(solution)/shard_map/ppermute | solution.py:18
  142.4 3.5 %collective-permute-start.13 = (f32[2,48,128]{2,1,0:T(8,128)S(1)}, f32[2,48,128]{2,1,0:T(8,128)S(1)}, u32[]{:S(2)}, u32[]{:S(2)}) collective-permute-start(f32[2,48,128]{2,1,0:T(8,128)S(1)} %get-tuple-element.30), channel_id=1, source_target_pairs={{0,2},{2,4},{6,0},{1,3},{3,5},{7,1},{8,10},{10,12},{14,8},{9,11},{... | collective-permute-start | bytes 147464 | tf_op jit(solution)/shard_map/ppermute | solution.py:166
  145.9 1.3 collective-permute-start.14
  147.2 6.1 %collective-permute-start.15 = (f32[2,48,128]{2,1,0:T(8,128)S(1)}, f32[2,48,128]{2,1,0:T(8,128)S(1)}, u32[]{:S(2)}, u32[]{:S(2)}) collective-permute-start(f32[2,48,128]{2,1,0:T(8,128)S(1)} %get-tuple-element.31), channel_id=1, source_target_pairs={{0,4},{4,0},{6,2},{1,5},{5,1},{7,3},{8,12},{12,8},{14,10},{9,13},{... | collective-permute-start | bytes 147464 | tf_op jit(solution)/shard_map/ppermute | solution.py:166
  153.3 0.7 broadcast_select_fusion
  154.1 1.3 collective-permute-done.15
  155.4 5.1 %project.7 = f32[1,8,2,24,128]{4,3,2,1,0:T(8,128)S(1)} custom-call(bf16[1,8,3,48,512]{4,3,2,1,0:T(8,128)(2,1)S(1)} %collective-permute-done.18.refs_0_, bf16[4,8,3,128,512]{4,3,2,1,0:T(8,128)(2,1)} %bitcast.145, bf16[4,8,3,128,512]{4,3,2,1,0:T(8,128)(2,1)} %bitcast.149, f32[2,48,128]{2,1,0:T(8,128)S(1)} %fusion.33.refs_3_), custom_call_target="tpu_custom_call" | custom-call | flops 1000 | bytes 1000 | tf_op jit(solution)/shard_map/project/pallas_call | solution.py:132
  160.5 2.0 %collective-permute-start.19 = (f32[1,2,48,128]{3,2,1,0:T(8,128)S(1)}, f32[1,2,48,128]{3,2,1,0:T(8,128)S(1)}, u32[]{:S(2)}, u32[]{:S(2)}) collective-permute-start(f32[1,2,48,128]{3,2,1,0:T(8,128)S(1)} %get-tuple-element.27), channel_id=1, source_target_pairs={{0,8},{8,16},{16,24},{24,0},{1,9},{9,17},{17,25},{25,1},{2,10},{10... | collective-permute-start | bytes 147464 | tf_op jit(solution)/shard_map/ppermute | solution.py:153
  162.5 2.2 %collective-permute-start.20 = (f32[1,2,48,128]{3,2,1,0:T(8,128)S(1)}, f32[1,2,48,128]{3,2,1,0:T(8,128)S(1)}, u32[]{:S(2)}, u32[]{:S(2)}) collective-permute-start(f32[1,2,48,128]{3,2,1,0:T(8,128)S(1)} %get-tuple-element.29), channel_id=1, source_target_pairs={{0,24},{8,0},{16,8},{24,16},{1,25},{9,1},{17,9},{25,17},{2,26},{10... | collective-permute-start | bytes 147464 | tf_op jit(solution)/shard_map/ppermute | solution.py:153
  164.7 1.8 collective-permute-start.21
  166.5 3.2 %collective-permute-start.16 = (f32[128,128]{1,0:T(8,128)S(1)}, f32[128,128]{1,0:T(8,128)S(1)}, u32[]{:S(2)}, u32[]{:S(2)}) collective-permute-start(f32[128,128]{1,0:T(8,128)S(1)} %fusion.25), channel_id=1, source_target_pairs={{0,1},{1,0},{2,3},{3,2},{4,5},{5,4},{6,7},{7,6},{8,9},{9,8},{10,11... | collective-permute-start | bytes 196616 | tf_op jit(solution)/shard_map/ppermute | solution.py:18
  169.7 0.6 collective-permute-done.21
  170.3 0.7 collective-permute-start.22
  171.0 3.3 %collective-permute-start.23 = (f32[2,48,128]{2,1,0:T(8,128)S(1)}, f32[2,48,128]{2,1,0:T(8,128)S(1)}, u32[]{:S(2)}, u32[]{:S(2)}) collective-permute-start(f32[2,48,128]{2,1,0:T(8,128)S(1)} %fusion.31), channel_id=1, source_target_pairs={{0,6},{1,7},{8,14},{9,15},{16,22},{17,23},{24,30},{25,31},{32,38},... | collective-permute-start | bytes 147464 | tf_op jit(solution)/shard_map/ppermute | solution.py:166
  174.3 0.7 collective-permute-start.24
  175.0 1.0 collective-permute-done.23
  176.1 3.3 %collective-permute-start.25 = (f32[48,128]{1,0:T(8,128)S(1)}, f32[48,128]{1,0:T(8,128)S(1)}, u32[]{:S(2)}, u32[]{:S(2)}) collective-permute-start(f32[48,128]{1,0:T(8,128)S(1)} %dynamic-slice_bitcast_fusion.9), channel_id=1, source_target_pairs={{0,1},{1,0},{2,3},{3,2},{4,5},{5,4},{6,7},{7,6},{8,9},{9,8},{10,11... | collective-permute-start | bytes 73736 | tf_op jit(solution)/shard_map/ppermute | solution.py:18
  179.4 2.1 %collective-permute-done.25 = f32[48,128]{1,0:T(8,128)S(1)} collective-permute-done((f32[48,128]{1,0:T(8,128)S(1)}, f32[48,128]{1,0:T(8,128)S(1)}, u32[]{:S(2)}, u32[]{:S(2)}) %collective-permute-start.25) | collective-permute-done | bytes 24608 | tf_op jit(solution)/shard_map/ppermute | solution.py:18
  181.6 0.1 slice.48
  181.7 1.0 collective-permute-done.26
  182.7 0.1 slice_select_fusion
  182.9 0.2 select_reduce_fusion
  183.1 0.1 copy.18
  183.3 0.7 copy.19
  (59 shorter events, 0.6 us)
Async XLA Ops:
  0.6 44.1 %collective-permute-start.1 = (bf16[64,6,32,512]{3,2,1,0:T(8,128)(2,1)}, bf16[64,6,32,512]{3,2,1,0:T(8,128)(2,1)}, u32[]{:S(2)}, u32[]{:S(2)}) collective-permute-start(bf16[64,6,32,512]{3,2,1,0:T(8,128)(2,1)} %bitcast.150), channel_id=1, source_target_pairs={{0,32},{32,0},{1,33},{33,1},{2,34},{34,2},{3,35},{35,3},{4,36},{36... | collective-permute-start | bytes 37748744 | tf_op jit(solution)/shard_map/ppermute | solution.py:18
  3.5 37.5 %collective-permute-start = (bf16[8,6,32,512]{3,2,1,0:T(8,128)(2,1)}, bf16[8,6,32,512]{3,2,1,0:T(8,128)(2,1)}, u32[]{:S(2)}, u32[]{:S(2)}) collective-permute-start(bf16[8,6,32,512]{3,2,1,0:T(8,128)(2,1)} %slice.46), channel_id=1, source_target_pairs={{0,64},{64,0},{1,65},{65,1},{2,66},{66,2},{3,67},{67,3},{4,68},{68... | collective-permute-start | bytes 4718600 | tf_op jit(solution)/shard_map/ppermute | solution.py:18
  12.8 83.6 %collective-permute-start.8 = (bf16[2,8,3,48,512]{4,3,2,1,0:T(8,128)(2,1)}, bf16[2,8,3,48,512]{4,3,2,1,0:T(8,128)(2,1)S(1)}, u32[]{:S(2)}, u32[]{:S(2)}) collective-permute-start(bf16[2,8,3,48,512]{4,3,2,1,0:T(8,128)(2,1)} %bitcast.165), channel_id=1, source_target_pairs={{0,64},{64,0},{1,65},{65,1},{2,66},{66,2},{3,67},{67,3},{4,68},{68... | collective-permute-start | bytes 7077896 | tf_op jit(solution)/shard_map/ppermute | solution.py:18
  13.2 12.7 %copy-start.4 = (s32[4,4]{1,0:T(4,128)S(1)}, s32[4,4]{1,0:T(4,128)}, u32[]{:S(2)}) copy-start(s32[4,4]{1,0:T(4,128)} %param.9) | copy-start | bytes 196
  13.2 13.4 %copy-start.5 = (s32[4]{0:T(128)S(1)}, s32[4]{0:T(128)}, u32[]{:S(2)}) copy-start(s32[4]{0:T(128)} %param.7) | copy-start | bytes 52
  13.2 103.7 %collective-permute-start.9 = (bf16[1,8,3,48,512]{4,3,2,1,0:T(8,128)(2,1)}, bf16[1,8,3,48,512]{4,3,2,1,0:T(8,128)(2,1)}, u32[]{:S(2)}, u32[]{:S(2)}) collective-permute-start(bf16[1,8,3,48,512]{4,3,2,1,0:T(8,128)(2,1)} %bitcast.166), channel_id=1, source_target_pairs={{0,64},{64,0},{1,65},{65,1},{2,66},{66,2},{3,67},{67,3},{4,68},{68... | collective-permute-start | bytes 3538952 | tf_op jit(solution)/shard_map/ppermute | solution.py:18
  44.7 10.6 %copy-start = (bf16[4,4,2,6,8,512]{5,4,3,2,1,0:T(8,128)(2,1)S(1)}, bf16[4,4,2,6,8,512]{5,4,3,2,1,0:T(8,128)(2,1)}, u32[]{:S(2)}) copy-start(bf16[4,4,2,6,8,512]{5,4,3,2,1,0:T(8,128)(2,1)} %by_time.5) | copy-start | bytes 4718596
  68.8 11.9 %collective-permute-start.2 = (f32[4,2,80,128]{3,2,1,0:T(8,128)S(1)}, f32[4,2,80,128]{3,2,1,0:T(8,128)S(1)}, u32[]{:S(2)}, u32[]{:S(2)}) collective-permute-start(f32[4,2,80,128]{3,2,1,0:T(8,128)S(1)} %get-tuple-element.18), channel_id=1, source_target_pairs={{0,8},{8,16},{16,24},{24,0},{1,9},{9,17},{17,25},{25,1},{2,10},{10... | collective-permute-start | bytes 983048 | tf_op jit(solution)/shard_map/ppermute | solution.py:153
  70.9 15.7 %collective-permute-start.3 = (f32[4,2,80,128]{3,2,1,0:T(8,128)S(1)}, f32[4,2,80,128]{3,2,1,0:T(8,128)S(1)}, u32[]{:S(2)}, u32[]{:S(2)}) collective-permute-start(f32[4,2,80,128]{3,2,1,0:T(8,128)S(1)} %get-tuple-element.19), channel_id=1, source_target_pairs={{0,24},{8,0},{16,8},{24,16},{1,25},{9,1},{17,9},{25,17},{2,26},{10... | collective-permute-start | bytes 983048 | tf_op jit(solution)/shard_map/ppermute | solution.py:153
  73.1 15.3 %collective-permute-start.4 = (f32[4,2,80,128]{3,2,1,0:T(8,128)S(1)}, f32[4,2,80,128]{3,2,1,0:T(8,128)S(1)}, u32[]{:S(2)}, u32[]{:S(2)}) collective-permute-start(f32[4,2,80,128]{3,2,1,0:T(8,128)S(1)} %get-tuple-element.20), channel_id=1, source_target_pairs={{0,16},{8,24},{16,0},{24,8},{1,17},{9,25},{17,1},{25,9},{2,18},{10... | collective-permute-start | bytes 983048 | tf_op jit(solution)/shard_map/ppermute | solution.py:153
  89.1 3.9 %copy-start.1 = (f32[4,2,80,128]{3,2,1,0:T(8,128)S(1)}, f32[4,2,80,128]{3,2,1,0:T(8,128)}, u32[]{:S(2)}) copy-start(f32[4,2,80,128]{3,2,1,0:T(8,128)} %fusion.6.refs_3_.refs_0_) | copy-start | bytes 983044
  93.0 13.5 %collective-permute-start.27 = (bf16[4,6,512]{2,1,0:T(8,128)(2,1)}, bf16[4,6,512]{2,1,0:T(8,128)(2,1)S(1)}, u32[]{:S(2)}, u32[]{:S(2)}) collective-permute-start(bf16[4,6,512]{2,1,0:T(8,128)(2,1)} %choose.1), channel_id=1, source_target_pairs={{0,32},{32,0},{1,33},{33,1},{2,34},{34,2},{3,35},{35,3},{4,36},{36... | collective-permute-start | bytes 73736 | tf_op jit(solution)/shard_map/ppermute | solution.py:18
  93.1 15.2 %collective-permute-start.5 = (f32[2,80,128]{2,1,0:T(8,128)S(1)}, f32[2,80,128]{2,1,0:T(8,128)S(1)}, u32[]{:S(2)}, u32[]{:S(2)}) collective-permute-start(f32[2,80,128]{2,1,0:T(8,128)S(1)} %get-tuple-element.24), channel_id=1, source_target_pairs={{0,2},{2,4},{4,6},{6,0},{1,3},{3,5},{5,7},{7,1},{8,10},{10,12},{12... | collective-permute-start | bytes 245768 | tf_op jit(solution)/shard_map/ppermute | solution.py:166
  94.6 14.1 %collective-permute-start.6 = (f32[2,80,128]{2,1,0:T(8,128)S(1)}, f32[2,80,128]{2,1,0:T(8,128)S(1)}, u32[]{:S(2)}, u32[]{:S(2)}) collective-permute-start(f32[2,80,128]{2,1,0:T(8,128)S(1)} %get-tuple-element.26), channel_id=1, source_target_pairs={{0,6},{2,0},{4,2},{6,4},{1,7},{3,1},{5,3},{7,5},{8,14},{10,8},{12,... | collective-permute-start | bytes 245768 | tf_op jit(solution)/shard_map/ppermute | solution.py:166
  96.4 12.4 %collective-permute-start.7 = (f32[2,80,128]{2,1,0:T(8,128)S(1)}, f32[2,80,128]{2,1,0:T(8,128)}, u32[]{:S(2)}, u32[]{:S(2)}) collective-permute-start(f32[2,80,128]{2,1,0:T(8,128)S(1)} %get-tuple-element.25), channel_id=1, source_target_pairs={{0,4},{2,6},{4,0},{6,2},{1,5},{3,7},{5,1},{7,3},{8,12},{10,14},{12... | collective-permute-start | bytes 245768 | tf_op jit(solution)/shard_map/ppermute | solution.py:166
  99.5 8.7 %copy-start.2 = (bf16[4,6,512]{2,1,0:T(8,128)(2,1)S(1)}, bf16[4,6,512]{2,1,0:T(8,128)(2,1)}, u32[]{:S(2)}) copy-start(bf16[4,6,512]{2,1,0:T(8,128)(2,1)} %choose.1) | copy-start | bytes 73732
  106.6 48.8 %collective-permute-start.18 = (bf16[1,8,3,48,512]{4,3,2,1,0:T(8,128)(2,1)}, bf16[1,8,3,48,512]{4,3,2,1,0:T(8,128)(2,1)S(1)}, u32[]{:S(2)}, u32[]{:S(2)}) collective-permute-start(bf16[1,8,3,48,512]{4,3,2,1,0:T(8,128)(2,1)} %bitcast.46), channel_id=1, source_target_pairs={{0,64},{64,0},{1,65},{65,1},{2,66},{66,2},{3,67},{67,3},{4,68},{68... | collective-permute-start | bytes 3538952 | tf_op jit(solution)/shard_map/ppermute | solution.py:18
  108.2 34.1 %collective-permute-start.28 = (bf16[4,6,512]{2,1,0:T(8,128)(2,1)S(1)}, bf16[4,6,512]{2,1,0:T(8,128)(2,1)S(1)}, u32[]{:S(2)}, u32[]{:S(2)}) collective-permute-start(bf16[4,6,512]{2,1,0:T(8,128)(2,1)S(1)} %add.229), channel_id=1, source_target_pairs={{0,64},{64,0},{1,65},{65,1},{2,66},{66,2},{3,67},{67,3},{4,68},{68... | collective-permute-start | bytes 73736 | tf_op jit(solution)/shard_map/ppermute | solution.py:18
  109.7 17.7 %copy-start.6 = (s32[4]{0:T(128)S(1)}, s32[4]{0:T(128)}, u32[]{:S(2)}) copy-start(s32[4]{0:T(128)} %fusion.34) | copy-start | bytes 52
  121.3 21.0 %collective-permute-start.10 = (f32[3,2,48,128]{3,2,1,0:T(8,128)S(1)}, f32[3,2,48,128]{3,2,1,0:T(8,128)S(1)}, u32[]{:S(2)}, u32[]{:S(2)}) collective-permute-start(f32[3,2,48,128]{3,2,1,0:T(8,128)S(1)} %get-tuple-element.21), channel_id=1, source_target_pairs={{0,8},{8,16},{16,24},{24,0},{1,9},{9,17},{17,25},{25,1},{2,10},{10... | collective-permute-start | bytes 442376 | tf_op jit(solution)/shard_map/ppermute | solution.py:153
  123.4 18.9 %collective-permute-start.11 = (f32[3,2,48,128]{3,2,1,0:T(8,128)S(1)}, f32[3,2,48,128]{3,2,1,0:T(8,128)S(1)}, u32[]{:S(2)}, u32[]{:S(2)}) collective-permute-start(f32[3,2,48,128]{3,2,1,0:T(8,128)S(1)} %get-tuple-element.22), channel_id=1, source_target_pairs={{0,24},{8,0},{16,8},{24,16},{1,25},{9,1},{17,9},{25,17},{2,26},{10... | collective-permute-start | bytes 442376 | tf_op jit(solution)/shard_map/ppermute | solution.py:153
  125.6 16.7 %collective-permute-start.12 = (f32[3,2,48,128]{3,2,1,0:T(8,128)S(1)}, f32[3,2,48,128]{3,2,1,0:T(8,128)S(1)}, u32[]{:S(2)}, u32[]{:S(2)}) collective-permute-start(f32[3,2,48,128]{3,2,1,0:T(8,128)S(1)} %get-tuple-element.23), channel_id=1, source_target_pairs={{0,16},{8,24},{16,0},{24,8},{1,17},{9,25},{17,1},{25,9},{2,18},{10... | collective-permute-start | bytes 442376 | tf_op jit(solution)/shard_map/ppermute | solution.py:153
  142.4 11.6 %collective-permute-start.13 = (f32[2,48,128]{2,1,0:T(8,128)S(1)}, f32[2,48,128]{2,1,0:T(8,128)S(1)}, u32[]{:S(2)}, u32[]{:S(2)}) collective-permute-start(f32[2,48,128]{2,1,0:T(8,128)S(1)} %get-tuple-element.30), channel_id=1, source_target_pairs={{0,2},{2,4},{6,0},{1,3},{3,5},{7,1},{8,10},{10,12},{14,8},{9,11},{... | collective-permute-start | bytes 147464 | tf_op jit(solution)/shard_map/ppermute | solution.py:166
  145.9 8.1 %collective-permute-start.14 = (f32[2,48,128]{2,1,0:T(8,128)S(1)}, f32[2,48,128]{2,1,0:T(8,128)S(1)}, u32[]{:S(2)}, u32[]{:S(2)}) collective-permute-start(f32[2,48,128]{2,1,0:T(8,128)S(1)} %get-tuple-element.32), channel_id=1, source_target_pairs={{2,0},{4,2},{6,4},{3,1},{5,3},{7,5},{10,8},{12,10},{14,12},{11,9},... | collective-permute-start | bytes 147464 | tf_op jit(solution)/shard_map/ppermute | solution.py:166
  147.2 8.1 %collective-permute-start.15 = (f32[2,48,128]{2,1,0:T(8,128)S(1)}, f32[2,48,128]{2,1,0:T(8,128)S(1)}, u32[]{:S(2)}, u32[]{:S(2)}) collective-permute-start(f32[2,48,128]{2,1,0:T(8,128)S(1)} %get-tuple-element.31), channel_id=1, source_target_pairs={{0,4},{4,0},{6,2},{1,5},{5,1},{7,3},{8,12},{12,8},{14,10},{9,13},{... | collective-permute-start | bytes 147464 | tf_op jit(solution)/shard_map/ppermute | solution.py:166
  160.4 22.4 %copy-start.3 = (pred[4,4,4]{2,1,0:T(4,128)(4,1)S(1)}, pred[4,4,4]{2,1,0:T(4,128)(4,1)}, u32[]{:S(2)}) copy-start(pred[4,4,4]{2,1,0:T(4,128)(4,1)} %iota_compare_fusion) | copy-start | bytes 196
  160.5 9.2 %collective-permute-start.19 = (f32[1,2,48,128]{3,2,1,0:T(8,128)S(1)}, f32[1,2,48,128]{3,2,1,0:T(8,128)S(1)}, u32[]{:S(2)}, u32[]{:S(2)}) collective-permute-start(f32[1,2,48,128]{3,2,1,0:T(8,128)S(1)} %get-tuple-element.27), channel_id=1, source_target_pairs={{0,8},{8,16},{16,24},{24,0},{1,9},{9,17},{17,25},{25,1},{2,10},{10... | collective-permute-start | bytes 147464 | tf_op jit(solution)/shard_map/ppermute | solution.py:153
  162.5 7.2 %collective-permute-start.20 = (f32[1,2,48,128]{3,2,1,0:T(8,128)S(1)}, f32[1,2,48,128]{3,2,1,0:T(8,128)S(1)}, u32[]{:S(2)}, u32[]{:S(2)}) collective-permute-start(f32[1,2,48,128]{3,2,1,0:T(8,128)S(1)} %get-tuple-element.29), channel_id=1, source_target_pairs={{0,24},{8,0},{16,8},{24,16},{1,25},{9,1},{17,9},{25,17},{2,26},{10... | collective-permute-start | bytes 147464 | tf_op jit(solution)/shard_map/ppermute | solution.py:153
  164.7 5.6 %collective-permute-start.21 = (f32[1,2,48,128]{3,2,1,0:T(8,128)S(1)}, f32[1,2,48,128]{3,2,1,0:T(8,128)S(1)}, u32[]{:S(2)}, u32[]{:S(2)}) collective-permute-start(f32[1,2,48,128]{3,2,1,0:T(8,128)S(1)} %get-tuple-element.28), channel_id=1, source_target_pairs={{0,16},{8,24},{16,0},{24,8},{1,17},{9,25},{17,1},{25,9},{2,18},{10... | collective-permute-start | bytes 147464 | tf_op jit(solution)/shard_map/ppermute | solution.py:153
  166.5 8.5 %collective-permute-start.16 = (f32[128,128]{1,0:T(8,128)S(1)}, f32[128,128]{1,0:T(8,128)S(1)}, u32[]{:S(2)}, u32[]{:S(2)}) collective-permute-start(f32[128,128]{1,0:T(8,128)S(1)} %fusion.25), channel_id=1, source_target_pairs={{0,1},{1,0},{2,3},{3,2},{4,5},{5,4},{6,7},{7,6},{8,9},{9,8},{10,11... | collective-permute-start | bytes 196616 | tf_op jit(solution)/shard_map/ppermute | solution.py:18
  170.3 4.7 %collective-permute-start.22 = (f32[2,48,128]{2,1,0:T(8,128)S(1)}, f32[2,48,128]{2,1,0:T(8,128)S(1)}, u32[]{:S(2)}, u32[]{:S(2)}) collective-permute-start(f32[2,48,128]{2,1,0:T(8,128)S(1)} %fusion.31), channel_id=1, source_target_pairs={{4,6},{5,7},{12,14},{13,15},{20,22},{21,23},{28,30},{29,31},{36,38... | collective-permute-start | bytes 147464 | tf_op jit(solution)/shard_map/ppermute | solution.py:166
  171.0 5.1 %collective-permute-start.23 = (f32[2,48,128]{2,1,0:T(8,128)S(1)}, f32[2,48,128]{2,1,0:T(8,128)S(1)}, u32[]{:S(2)}, u32[]{:S(2)}) collective-permute-start(f32[2,48,128]{2,1,0:T(8,128)S(1)} %fusion.31), channel_id=1, source_target_pairs={{0,6},{1,7},{8,14},{9,15},{16,22},{17,23},{24,30},{25,31},{32,38},... | collective-permute-start | bytes 147464 | tf_op jit(solution)/shard_map/ppermute | solution.py:166
  174.3 1.7 collective-permute-start.24
  176.1 5.4 %collective-permute-start.25 = (f32[48,128]{1,0:T(8,128)S(1)}, f32[48,128]{1,0:T(8,128)S(1)}, u32[]{:S(2)}, u32[]{:S(2)}) collective-permute-start(f32[48,128]{1,0:T(8,128)S(1)} %dynamic-slice_bitcast_fusion.9), channel_id=1, source_target_pairs={{0,1},{1,0},{2,3},{3,2},{4,5},{5,4},{6,7},{7,6},{8,9},{9,8},{10,11... | collective-permute-start | bytes 73736 | tf_op jit(solution)/shard_map/ppermute | solution.py:18
  179.4 2.2 %collective-permute-start.17 = (f32[128,128]{1,0:T(8,128)S(1)}, f32[128,128]{1,0:T(8,128)S(1)}, u32[]{:S(2)}, u32[]{:S(2)}) collective-permute-start(f32[128,128]{1,0:T(8,128)S(1)} %fusion.28), channel_id=1, source_target_pairs={{0,32},{32,0},{1,33},{33,1},{2,34},{34,2},{3,35},{35,3},{4,36},{36... | collective-permute-start | bytes 196616 | tf_op jit(solution)/shard_map/ppermute | solution.py:18
  181.5 1.2 collective-permute-start.26

commit v4 on v3

--- a/solution.py
+++ b/solution.py
@@ -18,35 +18,39 @@
     return lax.ppermute(value, axis, SWAP)
 
 
+ANY = pl.BlockSpec(memory_space=pl.ANY)
 HINT = pl.CostEstimate(flops=1000, bytes_accessed=1000, transcendentals=0)
 
 
-def by_time_kernel(cuts, block, *outs):
+def by_time_kernel(cuts, block, *refs):
+    outs = refs[-len(cuts) :]
     for k in range(block.shape[1]):
         turned = jnp.swapaxes(block[:, k], 0, 1)
-        for (low, high, first, size), out in zip(cuts, outs):
-            for t in range(2 * size):
-                out[t // 2, 0, t % 2, k] = turned[2 * first + t, low:high]
-
-
-def by_time(block, cuts):
+        for (low, high, x, nx, y, ny), out in zip(cuts, outs):
+            for i in range(nx):
+                for j in range(ny):
+                    out[i, 0, j, k] = turned[2 * (x + i) + y + j, low:high]
+
+
+def by_time(block, cuts, *after):
     n, comps, times, sites = block.shape
     return pl.pallas_call(
         functools.partial(by_time_kernel, cuts),
         grid=(4,),
-        in_specs=[pl.BlockSpec((n, comps, times // 4, sites), lambda z: (0, 0, z, 0))],
+        in_specs=[pl.BlockSpec((n, comps, times // 4, sites), lambda z: (0, 0, z, 0))]
+        + [ANY] * len(after),
         out_specs=[
-            pl.BlockSpec((size, 1, 2, comps, high - low, sites), lambda z: (0, z, 0, 0, 0, 0))
-            for low, high, _, size in cuts
+            pl.BlockSpec((nx, 1, ny, comps, high - low, sites), lambda z: (0, z, 0, 0, 0, 0))
+            for low, high, _, nx, _, ny in cuts
         ],
         out_shape=[
-            jax.ShapeDtypeStruct((size, 4, 2, comps, high - low, sites), block.dtype)
-            for low, high, _, size in cuts
+            jax.ShapeDtypeStruct((nx, 4, ny, comps, high - low, sites), block.dtype)
+            for low, high, _, nx, _, ny in cuts
         ],
-        compiler_params=pltpu.CompilerParams(vmem_limit_bytes=56 * 2**20),
+        compiler_params=pltpu.CompilerParams(vmem_limit_bytes=(56 if n > RAW else 16) * 2**20),
         cost_estimate=HINT,
         name="by_time",
-    )(block)
+    )(block, *after)
 
 
 def rows_of(block):
@@ -54,18 +58,15 @@
     return block.reshape(x, z * yh, comps // 2, 2 * n, sites)
 
 
-ANY = pl.BlockSpec(memory_space=pl.ANY)
-
-
-def choose_kernel(owned, rows, at, block, *refs):
+def choose_kernel(owned, rows, at, block, out):
     group, time, index = at[0], at[1], at[2 + pl.program_id(0)]
     row = lax.broadcasted_iota(jnp.int32, block.shape[1:], 1)
     here = jnp.where(index // owned == group, time % rows, -1)
     kept = jnp.where(row == here, block[0].astype(jnp.float32), 0.0)
-    refs[-1][0] = jnp.sum(kept, axis=1).astype(block.dtype)
-
-
-def choose(vecs, source_index, source_time, group, after):
+    out[0] = jnp.sum(kept, axis=1).astype(block.dtype)
+
+
+def choose(vecs, source_index, source_time, group):
     owned, comps, _, sites = vecs.shape
     rows = 16
     at = jnp.concatenate([group[None], source_time, source_index])
@@ -77,8 +78,7 @@
             in_specs=[
                 pl.BlockSpec(
                     (1, comps, rows, sites), lambda i, at: (at[2 + i] % owned, 0, at[1] // rows, 0)
-                ),
-                ANY,
+                )
             ],
             out_specs=pl.BlockSpec((1, comps, sites), lambda i, at: (i, 0, 0)),
         ),
@@ -86,7 +86,7 @@
         compiler_params=pltpu.CompilerParams(vmem_limit_bytes=60 * 2**20),
         cost_estimate=HINT,
         name="choose",
-    )(at, vecs, after)
+    )(at, vecs)
 
 
 def dot_kernel(count, *refs):
@@ -116,12 +116,14 @@
             out[0, at, 1] = jnp.concatenate(imag, axis=1)
 
 
-def project(cols, own, other, first, size, step, *after):
-    _, inner, colours, rows, sites = own.shape
-    spec = lambda n, off: pl.BlockSpec(
-        (1, step, colours, n, sites), lambda i, j, off=off: (i + off, j, 0, 0, 0)
+def project(cols, own, other, x, y, step, *after):
+    size, inner, colours, _, sites = cols[0].shape
+    rows, stride = own.shape[3], own.shape[1] // inner
+    spec = lambda n, stride=1, x=0, y=0: pl.BlockSpec(
+        (1, step, colours, n, sites), lambda i, j: (i + x, j * stride + y, 0, 0, 0)
     )
-    in_specs = [spec(c.shape[3], 0) for c in cols] + [spec(rows, first)] * 2 + [ANY] * len(after)
+    in_specs = [spec(c.shape[3]) for c in cols] + [spec(rows, stride, x, y)] * 2
+    in_specs += [ANY] * len(after)
     out_specs = [
         pl.BlockSpec((1, step, 2, c.shape[3] // 2, rows), lambda i, j: (i, j, 0, 0, 0))
         for c in cols
@@ -184,32 +186,35 @@
 
     raw = swap(sols[:RAW], "yl")
     other = swap(vecs, "c")
-    sent = ((RAW, count, 0, 2), (RAW, count, 2, 1), (RAW, count, 3, 1))
-    mine, *send = by_time(sols, ((0, count, 0, 4), *sent))
+    chosen = choose(vecs, source_index, source_time, group)
+    sent = [(RAW, count, *cut) for cut in ((0, 2, 0, 2), (2, 1, 0, 2), (3, 1, 0, 1), (3, 1, 1, 1))]
+    mine, *send = by_time(sols, ((0, count, 0, 4, 0, 2), *sent), chosen)
     got = [swap(rows_of(part), "yl") for part in send]
 
-    whole = ((0, owned, 0, 4),)
-    own = rows_of(by_time(vecs, whole)[0])
+    chosen = lax.psum(chosen, ("yl", "c"))
+
+    whole = ((0, owned, 0, 4, 0, 2),)
+    own = rows_of(by_time(vecs, whole, chosen)[0])
     other = rows_of(by_time(other, whole)[0])
-    raw = rows_of(by_time(raw, ((0, RAW, 0, 4),))[0])
+    raw = rows_of(by_time(raw, ((0, RAW, 0, 4, 0, 2),), chosen)[0])
 
     def rows(part):
         x, inner, _, n, lanes = part.shape
-        return part.reshape(x, 4, 2, 2 * n, lanes)
-
-    def against(part, x, step, *after):
-        return rows(project([part], own, other, x, part.shape[0], step, *after)[0])
-
-    parts = project([rows_of(mine), raw], own, other, 0, 4, 8)
+        return part.reshape(x, 4, inner // 4, 2 * n, lanes)
+
+    def against(part, x, y, step, *after):
+        return rows(project([part], own, other, x, y, step, *after)[0])
+
+    parts = project([rows_of(mine), raw], own, other, 0, 0, 8)
     first_z = sum_z(jnp.concatenate([rows(p) for p in parts], axis=3))
-    chosen = choose(vecs, source_index, source_time, group, first_z)
     first = sum_x(first_z, 0, 4)
-    mid = [against(got[0], 0, 8, first_z)]
-    mid.append(against(got[1], 2, 4, first))
+    mid = [against(got[0], 0, 0, 8, first_z)]
+    mid.append(against(got[1], 2, 0, 4, first))
     mid = sum_x(sum_z(jnp.concatenate(mid, axis=0)), 0, 3)
     main = sum_yh(jnp.concatenate([first, mid], axis=1))
     main_c = swap(main, "c")
-    last = sum_yh(sum_x(sum_z(against(got[2], 3, 2, mid)), 3, 1))
+    last = [against(got[2], 3, 0, 1, mid), against(got[3], 3, 1, 1, mid)]
+    last = sum_yh(sum_x(sum_z(jnp.concatenate(last, axis=2)), 3, 1))
     last_c = swap(last, "c")
     is_last = lax.axis_index("x") == 3
 
@@ -234,8 +239,6 @@
     result = jnp.sum(picked, axis=0).reshape(spins, 2, count, owned) * scale
     result = result.transpose(3, 0, 2, 1).reshape(1, owned, spins * count * 2)
 
-    chosen = chosen + swap(chosen, "c")
-    chosen = chosen + swap(chosen, "yl")
     my_spins = lax.dynamic_index_in_dim(dilution, group, 1, keepdims=False)
     spin_mask = jnp.arange(spins, dtype=jnp.int32)[None, :] == my_spins[:, None]
     sources = jnp.where(

time: 187 us -> 234 us (1.25)
  blocking collectives: 0 us -> 80.6 us
  waiting for transfers between devices: 55.2 us -> 28.9 us
  starting transfers between devices: 51.2 us -> 42.7 us
    psum x0 -> x1, blocking collectives: none -> 80.6 us  [local(): chosen = lax.psum(chosen, ('yl', 'c'))]
    ppermute x11 -> x10, waiting for transfers between devices: 38.9 us -> 3.57 us  [swap(): return lax.ppermute(value, axis, SWAP)]
    ppermute x9, waiting for transfers between devices: 14 us -> 22.3 us  [sum_z(): lax.ppermute(pick(slabs, (me + k) % 4), 'z', [(i, (i + k) % 4) for i in r...]
    ppermute x9, starting transfers between devices: 18.1 us -> 12.6 us  [sum_z(): lax.ppermute(pick(slabs, (me + k) % 4), 'z', [(i, (i + k) % 4) for i in r...]
    pallas_call x4 -> x5, Pallas kernels: 29.9 us -> 32.4 us  [project(): pl.pallas_call(functools.partial(dot_kernel, len(cols)), grid=(size, inne...]
    ppermute x11 -> x10, starting transfers between devices: 12.4 us -> 10.4 us  [swap(): return lax.ppermute(value, axis, SWAP)]
  transfers between devices with their start and end apart: 29 -> 28, of which waited for: 11 -> 10; matrix products, arithmetic and copies ran while one was open for 5% -> 3% of each run, Pallas kernels for 33% -> 27%
where the time goes in v4:
time: 234 us; the launch traced here: 231 us
  blocking collectives  80.6 us (34%)
  Pallas kernels  67.1 us (29%)
  starting transfers between devices  42.7 us (18%)
  waiting for transfers between devices  28.9 us (12%)
  local copies, waits for them, and re-layouts  5.32 us (2%)
  other arithmetic  4.5 us (2%)
    psum x1, blocking collectives, local(): chosen = lax.psum(chosen, ('yl', 'c'))  80.6 us
    pallas_call x5, Pallas kernels, project(): pl.pallas_call(functools.partial(dot_kernel, len(cols)), grid=(size, inne...  32.4 us
    pallas_call x4, Pallas kernels, by_time(): pl.pallas_call(functools.partial(by_time_kernel, cuts), grid=(4,), in_spe...  30.9 us
    ppermute x9, waiting for transfers between devices, sum_z(): lax.ppermute(pick(slabs, (me + k) % 4), 'z', [(i, (i + k) % 4) for i in r...  22.3 us
    ppermute x9, starting transfers between devices, sum_x(): total = total + lax.ppermute(send, 'x', pairs)  19.7 us
    ppermute x9, starting transfers between devices, sum_z(): lax.ppermute(pick(slabs, (me + k) % 4), 'z', [(i, (i + k) % 4) for i in r...  12.6 us
    ppermute x10, starting transfers between devices, swap(): return lax.ppermute(value, axis, SWAP)  10.4 us
  transfers between devices with their start and end apart: 28, of which 10 were waited for; matrix products, arithmetic and copies ran while one was open for 3% of the time, Pallas kernels for 27%

profile of v4, /device:TPU:0, one launch (start us, length us, event | category | flops | bytes accessed | tf_op | source)
XLA Modules:
  0.0 230.8 jit_solution(9498030891549897387)
XLA Ops:
  0.6 0.1 collective-permute-start.1
  0.7 2.7 %slice.46 = bf16[8,6,32,512]{3,2,1,0:T(8,128)(2,1)} slice(bf16[32,6,32,512]{3,2,1,0:T(8,128)(2,1)} %bitcast.161), slice={[0:8], [0:6], [0:32], [0:512]} | slice | bytes 3145728 | tf_op jit(solution)/shard_map/slice | solution.py:187
  3.5 1.7 collective-permute-start
  5.8 0.6 pad_add_fusion.at
  6.4 3.8 %choose.1.refs_0_ = bf16[4,6,512]{2,1,0:T(8,128)(2,1)} custom-call(s32[6]{0:T(128)} %pad_add_fusion.at, bf16[64,6,32,512]{3,2,1,0:T(8,128)(2,1)} %bitcast.159), custom_call_target="tpu_custom_call" | custom-call | flops 1000 | bytes 1000 | tf_op jit(solution)/shard_map/choose/pallas_call | solution.py:73
  10.2 7.6 %by_time.4 = (bf16[4,4,2,6,32,512]{5,4,3,2,1,0:T(8,128)(2,1)}, bf16[2,4,2,6,24,512]{5,4,3,2,1,0:T(8,128)(2,1)}, bf16[1,4,2,6,24,512]{5,4,3,2,1,0:T(8,128)(2,1)},...) custom-call(bf16[32,6,32,512]{3,2,1,0:T(8,128)(2,1)} %bitcast.162, bf16[4,6,512]{2,1,0:T(8,128)(2,1)} %choose.1.refs_0_), custom_call_target="tpu_custom_call" | custom-call | flops 1000 | bytes 1000 | tf_op jit(solution)/shard_map/by_time/pallas_call | solution.py:37
  17.8 0.4 collective-permute-start.8
  18.2 80.6 %psum.7.refs_0_ = bf16[4,6,512]{2,1,0:T(8,128)(2,1)} all-reduce(bf16[4,6,512]{2,1,0:T(8,128)(2,1)S(1)} %copy-done.2), channel_id=1, replica_groups=mesh['yl'=2,'c'=2,'z'=4,'x'=4,'yh'=2] {'yl','c'}, use_global_device_ids=true, to_apply=%region_0.0 | all-reduce | flops 12288 | bytes 49152 | tf_op jit(solution)/shard_map/psum | solution.py:194
  98.8 0.4 collective-permute-start.9
  99.2 10.4 %by_time.6 = bf16[4,4,2,6,64,512]{5,4,3,2,1,0:T(8,128)(2,1)} custom-call(bf16[64,6,32,512]{3,2,1,0:T(8,128)(2,1)} %bitcast.160, bf16[4,6,512]{2,1,0:T(8,128)(2,1)} %psum.7.refs_0_), custom_call_target="tpu_custom_call" | custom-call | flops 1000 | bytes 1000 | tf_op jit(solution)/shard_map/by_time/pallas_call | solution.py:37
  109.6 0.1 copy.14
  109.7 0.2 fusion.43
  109.9 0.1 fusion.44
  110.0 0.1 iota_compare_fusion.1
  110.0 2.4 %by_time.5 = bf16[4,4,2,6,8,512]{5,4,3,2,1,0:T(8,128)(2,1)S(1)} custom-call(bf16[8,6,32,512]{3,2,1,0:T(8,128)(2,1)} %collective-permute-done.block, bf16[4,6,512]{2,1,0:T(8,128)(2,1)S(1)} %copy-done.1), custom_call_target="tpu_custom_call" | custom-call | flops 1000 | bytes 1000 | tf_op jit(solution)/shard_map/by_time/pallas_call | solution.py:37
  112.5 10.5 %by_time.7 = bf16[4,4,2,6,64,512]{5,4,3,2,1,0:T(8,128)(2,1)} custom-call(bf16[64,6,32,512]{3,2,1,0:T(8,128)(2,1)} %collective-permute-done.1.block), custom_call_target="tpu_custom_call" | custom-call | flops 1000 | bytes 1000 | tf_op jit(solution)/shard_map/by_time/pallas_call | solution.py:37
  122.9 13.4 %project.5 = (f32[4,8,2,32,128]{4,3,2,1,0:T(8,128)S(1)}, f32[4,8,2,8,128]{4,3,2,1,0:T(8,128)S(1)}) custom-call(bf16[4,8,3,64,512]{4,3,2,1,0:T(8,128)(2,1)} %bitcast.163, bf16[4,8,3,16,512]{4,3,2,1,0:T(8,128)(2,1)S(1)} %bitcast.135, bf16[4,8,3,128,512]{4,3,2,1,0:T(8,128)(2,1)} %bitcast.148, bf16[4,8,3,128,512]{4,3,2,1,0:T(8,128)(2,1)} %bitcast.153), custom_call_target="tpu_custom_call" | custom-call | flops 1000 | bytes 1000 | tf_op jit(solution)/shard_map/project/pallas_call | solution.py:134
  136.3 0.7 copy-done
  137.0 1.0 fusion.8
  138.1 2.0 collective-permute-start.2
  140.1 2.1 collective-permute-start.3
  142.2 1.9 collective-permute-start.4
  144.1 0.6 gather_fusion
  144.6 0.7 broadcast_select_fusion
  145.4 4.8 %collective-permute-done.2 = f32[4,2,80,128]{3,2,1,0:T(8,128)} collective-permute-done((f32[4,2,80,128]{3,2,1,0:T(8,128)}, f32[4,2,80,128]{3,2,1,0:T(8,128)}, u32[]{:S(2)}, u32[]{:S(2)}) %collective-permute-start.2) | collective-permute-done | bytes 327712 | tf_op jit(solution)/shard_map/ppermute | solution.py:155
  150.2 6.3 %collective-permute-done.3 = f32[4,2,80,128]{3,2,1,0:T(8,128)} collective-permute-done((f32[4,2,80,128]{3,2,1,0:T(8,128)}, f32[4,2,80,128]{3,2,1,0:T(8,128)}, u32[]{:S(2)}, u32[]{:S(2)}) %collective-permute-start.3) | collective-permute-done | bytes 327712 | tf_op jit(solution)/shard_map/ppermute | solution.py:155
  156.5 1.9 collective-permute-done.4
  158.4 1.2 fusion.6.refs_3_
  159.7 1.6 collective-permute-start.5
  161.2 1.7 collective-permute-start.6
  163.0 1.8 collective-permute-start.7
  164.8 0.1 compare_and_fusion
  164.9 0.4 collective-permute-start.19
  165.3 7.0 %project.6 = f32[2,8,2,24,128]{4,3,2,1,0:T(8,128)S(1)} custom-call(bf16[2,8,3,48,512]{4,3,2,1,0:T(8,128)(2,1)S(1)} %collective-permute-done.8.refs_0_, bf16[4,8,3,128,512]{4,3,2,1,0:T(8,128)(2,1)} %bitcast.149, bf16[4,8,3,128,512]{4,3,2,1,0:T(8,128)(2,1)} %bitcast.154, f32[4,2,80,128]{3,2,1,0:T(8,128)S(1)} %fusion.6.refs_3_), custom_call_target="tpu_custom_call" | custom-call | flops 1000 | bytes 1000 | tf_op jit(solution)/shard_map/project/pallas_call | solution.py:134
  172.3 1.8 collective-permute-start.18
  174.2 4.5 %project.7 = f32[1,8,2,24,128]{4,3,2,1,0:T(8,128)S(1)} custom-call(bf16[1,8,3,48,512]{4,3,2,1,0:T(8,128)(2,1)} %collective-permute-done.9.refs_0_, bf16[4,8,3,128,512]{4,3,2,1,0:T(8,128)(2,1)} %bitcast.150, bf16[4,8,3,128,512]{4,3,2,1,0:T(8,128)(2,1)} %bitcast.155, f32[2,80,128]{2,1,0:T(8,128)S(1)} %fusion.23.refs_3_), custom_call_target="tpu_custom_call" | custom-call | flops 1000 | bytes 1000 | tf_op jit(solution)/shard_map/project/pallas_call | solution.py:134
  178.7 1.2 collective-permute-start.10
  179.9 2.1 collective-permute-start.11
  182.0 0.1 broadcast_select_fusion.1
  182.1 4.1 %collective-permute-done.10 = f32[3,2,48,128]{3,2,1,0:T(8,128)S(1)} collective-permute-done((f32[3,2,48,128]{3,2,1,0:T(8,128)S(1)}, f32[3,2,48,128]{3,2,1,0:T(8,128)S(1)}, u32[]{:S(2)}, u32[]{:S(2)}) %collective-permute-start.10) | collective-permute-done | bytes 147488 | tf_op jit(solution)/shard_map/ppermute | solution.py:155
  186.3 2.4 %collective-permute-done.12 = f32[3,2,48,128]{3,2,1,0:T(8,128)S(1)} collective-permute-done((f32[3,2,48,128]{3,2,1,0:T(8,128)S(1)}, f32[3,2,48,128]{3,2,1,0:T(8,128)S(1)}, u32[]{:S(2)}, u32[]{:S(2)}) %collective-permute-start.12) | collective-permute-done | bytes 147488 | tf_op jit(solution)/shard_map/ppermute | solution.py:155
  188.7 2.5 %collective-permute-start.13 = (f32[2,48,128]{2,1,0:T(8,128)S(1)}, f32[2,48,128]{2,1,0:T(8,128)S(1)}, u32[]{:S(2)}, u32[]{:S(2)}) collective-permute-start(f32[2,48,128]{2,1,0:T(8,128)S(1)} %get-tuple-element.32), channel_id=1, source_target_pairs={{0,2},{2,4},{6,0},{1,3},{3,5},{7,1},{8,10},{10,12},{14,8},{9,11},{... | collective-permute-start | bytes 147464 | tf_op jit(solution)/shard_map/ppermute | solution.py:168
  191.2 1.3 collective-permute-start.14
  192.5 5.7 %collective-permute-start.15 = (f32[2,48,128]{2,1,0:T(8,128)S(1)}, f32[2,48,128]{2,1,0:T(8,128)S(1)}, u32[]{:S(2)}, u32[]{:S(2)}) collective-permute-start(f32[2,48,128]{2,1,0:T(8,128)S(1)} %get-tuple-element.33), channel_id=1, source_target_pairs={{0,4},{4,0},{6,2},{1,5},{5,1},{7,3},{8,12},{12,8},{14,10},{9,13},{... | collective-permute-start | bytes 147464 | tf_op jit(solution)/shard_map/ppermute | solution.py:168
  198.2 2.0 collective-permute-done.15
  200.3 3.7 %project.9 = f32[1,4,2,24,128]{4,3,2,1,0:T(8,128)S(1)} custom-call(bf16[1,4,3,48,512]{4,3,2,1,0:T(8,128)(2,1)S(1)} %collective-permute-done.19.refs_0_, bf16[4,8,3,128,512]{4,3,2,1,0:T(8,128)(2,1)} %bitcast.151, bf16[4,8,3,128,512]{4,3,2,1,0:T(8,128)(2,1)} %bitcast.156, f32[2,48,128]{2,1,0:T(8,128)S(1)} %fusion.42.refs_3_), custom_call_target="tpu_custom_call" | custom-call | flops 1000 | bytes 1000 | tf_op jit(solution)/shard_map/project/pallas_call | solution.py:134
  204.0 3.7 %project.8 = f32[1,4,2,24,128]{4,3,2,1,0:T(8,128)S(1)} custom-call(bf16[1,4,3,48,512]{4,3,2,1,0:T(8,128)(2,1)S(1)} %collective-permute-done.18.refs_0_, bf16[4,8,3,128,512]{4,3,2,1,0:T(8,128)(2,1)} %bitcast.152, bf16[4,8,3,128,512]{4,3,2,1,0:T(8,128)(2,1)} %bitcast.157, f32[2,48,128]{2,1,0:T(8,128)S(1)} %fusion.42.refs_3_), custom_call_target="tpu_custom_call" | custom-call | flops 1000 | bytes 1000 | tf_op jit(solution)/shard_map/project/pallas_call | solution.py:134
  207.8 0.1 collective-permute-start.20
  207.9 3.2 %collective-permute-start.21 = (f32[1,2,48,128]{3,2,1,0:T(8,128)S(1)}, f32[1,2,48,128]{3,2,1,0:T(8,128)S(1)}, u32[]{:S(2)}, u32[]{:S(2)}) collective-permute-start(f32[1,2,48,128]{3,2,1,0:T(8,128)S(1)} %get-tuple-element.30), channel_id=1, source_target_pairs={{0,24},{8,0},{16,8},{24,16},{1,25},{9,1},{17,9},{25,17},{2,26},{10... | collective-permute-start | bytes 147464 | tf_op jit(solution)/shard_map/ppermute | solution.py:155
  211.1 2.9 %collective-permute-start.16 = (f32[128,128]{1,0:T(8,128)S(1)}, f32[128,128]{1,0:T(8,128)S(1)}, u32[]{:S(2)}, u32[]{:S(2)}) collective-permute-start(f32[128,128]{1,0:T(8,128)S(1)} %fusion.25), channel_id=1, source_target_pairs={{0,1},{1,0},{2,3},{3,2},{4,5},{5,4},{6,7},{7,6},{8,9},{9,8},{10,11... | collective-permute-start | bytes 196616 | tf_op jit(solution)/shard_map/ppermute | solution.py:18
  214.0 2.7 %collective-permute-done.22 = f32[1,2,48,128]{3,2,1,0:T(8,128)S(1)} collective-permute-done((f32[1,2,48,128]{3,2,1,0:T(8,128)S(1)}, f32[1,2,48,128]{3,2,1,0:T(8,128)S(1)}, u32[]{:S(2)}, u32[]{:S(2)}) %collective-permute-start.22) | collective-permute-done | bytes 49184 | tf_op jit(solution)/shard_map/ppermute | solution.py:155
  216.7 0.7 collective-permute-start.23
  217.4 3.8 %collective-permute-start.24 = (f32[2,48,128]{2,1,0:T(8,128)S(1)}, f32[2,48,128]{2,1,0:T(8,128)S(1)}, u32[]{:S(2)}, u32[]{:S(2)}) collective-permute-start(f32[2,48,128]{2,1,0:T(8,128)S(1)} %fusion.36), channel_id=1, source_target_pairs={{0,6},{1,7},{8,14},{9,15},{16,22},{17,23},{24,30},{25,31},{32,38},... | collective-permute-start | bytes 147464 | tf_op jit(solution)/shard_map/ppermute | solution.py:168
  221.1 0.7 collective-permute-start.25
  221.9 1.0 collective-permute-done.24
  222.9 2.9 %collective-permute-start.26 = (f32[48,128]{1,0:T(8,128)S(1)}, f32[48,128]{1,0:T(8,128)S(1)}, u32[]{:S(2)}, u32[]{:S(2)}) collective-permute-start(f32[48,128]{1,0:T(8,128)S(1)} %dynamic-slice_bitcast_fusion.6), channel_id=1, source_target_pairs={{0,1},{1,0},{2,3},{3,2},{4,5},{5,4},{6,7},{7,6},{8,9},{9,8},{10,11... | collective-permute-start | bytes 73736 | tf_op jit(solution)/shard_map/ppermute | solution.py:18
  225.8 2.5 %collective-permute-done.26 = f32[48,128]{1,0:T(8,128)S(1)} collective-permute-done((f32[48,128]{1,0:T(8,128)S(1)}, f32[48,128]{1,0:T(8,128)S(1)}, u32[]{:S(2)}, u32[]{:S(2)}) %collective-permute-start.26) | collective-permute-done | bytes 24608 | tf_op jit(solution)/shard_map/ppermute | solution.py:18
  228.4 0.1 slice_bitcast_fusion
  228.4 0.1 slice.48
  228.5 1.0 collective-permute-done.27
  229.5 0.1 slice_select_fusion
  229.7 0.2 select_reduce_fusion
  229.9 0.1 copy.18
  230.1 0.7 copy.19
  (53 shorter events, 0.5 us)
Async XLA Ops:
  0.6 111.8 %collective-permute-start.1 = (bf16[64,6,32,512]{3,2,1,0:T(8,128)(2,1)}, bf16[64,6,32,512]{3,2,1,0:T(8,128)(2,1)}, u32[]{:S(2)}, u32[]{:S(2)}) collective-permute-start(bf16[64,6,32,512]{3,2,1,0:T(8,128)(2,1)} %bitcast.158), channel_id=1, source_target_pairs={{0,32},{32,0},{1,33},{33,1},{2,34},{34,2},{3,35},{35,3},{4,36},{36... | collective-permute-start | bytes 37748744 | tf_op jit(solution)/shard_map/ppermute | solution.py:18
  0.7 5.1 %copy-start.4 = (s32[4]{0:T(128)S(1)}, s32[4]{0:T(128)}, u32[]{:S(2)}) copy-start(s32[4]{0:T(128)} %param.7) | copy-start | bytes 52
  3.5 106.5 %collective-permute-start = (bf16[8,6,32,512]{3,2,1,0:T(8,128)(2,1)}, bf16[8,6,32,512]{3,2,1,0:T(8,128)(2,1)}, u32[]{:S(2)}, u32[]{:S(2)}) collective-permute-start(bf16[8,6,32,512]{3,2,1,0:T(8,128)(2,1)} %slice.46), channel_id=1, source_target_pairs={{0,64},{64,0},{1,65},{65,1},{2,66},{66,2},{3,67},{67,3},{4,68},{68... | collective-permute-start | bytes 4718600 | tf_op jit(solution)/shard_map/ppermute | solution.py:18
  10.2 8.0 %copy-start.2 = (bf16[4,6,512]{2,1,0:T(8,128)(2,1)S(1)}, bf16[4,6,512]{2,1,0:T(8,128)(2,1)}, u32[]{:S(2)}) copy-start(bf16[4,6,512]{2,1,0:T(8,128)(2,1)} %choose.1.refs_0_) | copy-start | bytes 73732
  17.8 147.1 %collective-permute-start.8 = (bf16[2,8,3,48,512]{4,3,2,1,0:T(8,128)(2,1)}, bf16[2,8,3,48,512]{4,3,2,1,0:T(8,128)(2,1)S(1)}, u32[]{:S(2)}, u32[]{:S(2)}) collective-permute-start(bf16[2,8,3,48,512]{4,3,2,1,0:T(8,128)(2,1)} %bitcast.173), channel_id=1, source_target_pairs={{0,64},{64,0},{1,65},{65,1},{2,66},{66,2},{3,67},{67,3},{4,68},{68... | collective-permute-start | bytes 7077896 | tf_op jit(solution)/shard_map/ppermute | solution.py:18
  98.8 10.8 %copy-start.3 = (s32[4,4]{1,0:T(4,128)S(1)}, s32[4,4]{1,0:T(4,128)}, u32[]{:S(2)}) copy-start(s32[4,4]{1,0:T(4,128)} %param.9) | copy-start | bytes 196
  98.8 11.2 %copy-start.1 = (bf16[4,6,512]{2,1,0:T(8,128)(2,1)S(1)}, bf16[4,6,512]{2,1,0:T(8,128)(2,1)}, u32[]{:S(2)}) copy-start(bf16[4,6,512]{2,1,0:T(8,128)(2,1)} %psum.7.refs_0_) | copy-start | bytes 73732
  98.8 75.3 %collective-permute-start.9 = (bf16[1,8,3,48,512]{4,3,2,1,0:T(8,128)(2,1)}, bf16[1,8,3,48,512]{4,3,2,1,0:T(8,128)(2,1)}, u32[]{:S(2)}, u32[]{:S(2)}) collective-permute-start(bf16[1,8,3,48,512]{4,3,2,1,0:T(8,128)(2,1)} %bitcast.174), channel_id=1, source_target_pairs={{0,64},{64,0},{1,65},{65,1},{2,66},{66,2},{3,67},{67,3},{4,68},{68... | collective-permute-start | bytes 3538952 | tf_op jit(solution)/shard_map/ppermute | solution.py:18
  136.3 0.7 copy-start
  138.1 12.1 %collective-permute-start.2 = (f32[4,2,80,128]{3,2,1,0:T(8,128)}, f32[4,2,80,128]{3,2,1,0:T(8,128)}, u32[]{:S(2)}, u32[]{:S(2)}) collective-permute-start(f32[4,2,80,128]{3,2,1,0:T(8,128)} %get-tuple-element.20), channel_id=1, source_target_pairs={{0,8},{8,16},{16,24},{24,0},{1,9},{9,17},{17,25},{25,1},{2,10},{10... | collective-permute-start | bytes 983048 | tf_op jit(solution)/shard_map/ppermute | solution.py:155
  140.1 16.5 %collective-permute-start.3 = (f32[4,2,80,128]{3,2,1,0:T(8,128)}, f32[4,2,80,128]{3,2,1,0:T(8,128)}, u32[]{:S(2)}, u32[]{:S(2)}) collective-permute-start(f32[4,2,80,128]{3,2,1,0:T(8,128)} %get-tuple-element.21), channel_id=1, source_target_pairs={{0,24},{8,0},{16,8},{24,16},{1,25},{9,1},{17,9},{25,17},{2,26},{10... | collective-permute-start | bytes 983048 | tf_op jit(solution)/shard_map/ppermute | solution.py:155
  142.2 16.2 %collective-permute-start.4 = (f32[4,2,80,128]{3,2,1,0:T(8,128)}, f32[4,2,80,128]{3,2,1,0:T(8,128)}, u32[]{:S(2)}, u32[]{:S(2)}) collective-permute-start(f32[4,2,80,128]{3,2,1,0:T(8,128)} %get-tuple-element.22), channel_id=1, source_target_pairs={{0,16},{8,24},{16,0},{24,8},{1,17},{9,25},{17,1},{25,9},{2,18},{10... | collective-permute-start | bytes 983048 | tf_op jit(solution)/shard_map/ppermute | solution.py:155
  159.7 12.7 %collective-permute-start.5 = (f32[2,80,128]{2,1,0:T(8,128)S(1)}, f32[2,80,128]{2,1,0:T(8,128)S(1)}, u32[]{:S(2)}, u32[]{:S(2)}) collective-permute-start(f32[2,80,128]{2,1,0:T(8,128)S(1)} %get-tuple-element.26), channel_id=1, source_target_pairs={{0,2},{2,4},{4,6},{6,0},{1,3},{3,5},{5,7},{7,1},{8,10},{10,12},{12... | collective-permute-start | bytes 245768 | tf_op jit(solution)/shard_map/ppermute | solution.py:168
  161.2 12.9 %collective-permute-start.6 = (f32[2,80,128]{2,1,0:T(8,128)S(1)}, f32[2,80,128]{2,1,0:T(8,128)S(1)}, u32[]{:S(2)}, u32[]{:S(2)}) collective-permute-start(f32[2,80,128]{2,1,0:T(8,128)S(1)} %get-tuple-element.28), channel_id=1, source_target_pairs={{0,6},{2,0},{4,2},{6,4},{1,7},{3,1},{5,3},{7,5},{8,14},{10,8},{12,... | collective-permute-start | bytes 245768 | tf_op jit(solution)/shard_map/ppermute | solution.py:168
  163.0 11.2 %collective-permute-start.7 = (f32[2,80,128]{2,1,0:T(8,128)S(1)}, f32[2,80,128]{2,1,0:T(8,128)S(1)}, u32[]{:S(2)}, u32[]{:S(2)}) collective-permute-start(f32[2,80,128]{2,1,0:T(8,128)S(1)} %get-tuple-element.27), channel_id=1, source_target_pairs={{0,4},{2,6},{4,0},{6,2},{1,5},{3,7},{5,1},{7,3},{8,12},{10,14},{12... | collective-permute-start | bytes 245768 | tf_op jit(solution)/shard_map/ppermute | solution.py:168
  164.9 35.4 %collective-permute-start.19 = (bf16[1,4,3,48,512]{4,3,2,1,0:T(8,128)(2,1)}, bf16[1,4,3,48,512]{4,3,2,1,0:T(8,128)(2,1)S(1)}, u32[]{:S(2)}, u32[]{:S(2)}) collective-permute-start(bf16[1,4,3,48,512]{4,3,2,1,0:T(8,128)(2,1)} %bitcast.48), channel_id=1, source_target_pairs={{0,64},{64,0},{1,65},{65,1},{2,66},{66,2},{3,67},{67,3},{4,68},{68... | collective-permute-start | bytes 1769480 | tf_op jit(solution)/shard_map/ppermute | solution.py:18
  172.3 31.7 %collective-permute-start.18 = (bf16[1,4,3,48,512]{4,3,2,1,0:T(8,128)(2,1)}, bf16[1,4,3,48,512]{4,3,2,1,0:T(8,128)(2,1)S(1)}, u32[]{:S(2)}, u32[]{:S(2)}) collective-permute-start(bf16[1,4,3,48,512]{4,3,2,1,0:T(8,128)(2,1)} %bitcast.46), channel_id=1, source_target_pairs={{0,64},{64,0},{1,65},{65,1},{2,66},{66,2},{3,67},{67,3},{4,68},{68... | collective-permute-start | bytes 1769480 | tf_op jit(solution)/shard_map/ppermute | solution.py:18
  178.7 7.6 %collective-permute-start.10 = (f32[3,2,48,128]{3,2,1,0:T(8,128)S(1)}, f32[3,2,48,128]{3,2,1,0:T(8,128)S(1)}, u32[]{:S(2)}, u32[]{:S(2)}) collective-permute-start(f32[3,2,48,128]{3,2,1,0:T(8,128)S(1)} %get-tuple-element.23), channel_id=1, source_target_pairs={{0,8},{8,16},{16,24},{24,0},{1,9},{9,17},{17,25},{25,1},{2,10},{10... | collective-permute-start | bytes 442376 | tf_op jit(solution)/shard_map/ppermute | solution.py:155
  179.9 6.4 %collective-permute-start.11 = (f32[3,2,48,128]{3,2,1,0:T(8,128)S(1)}, f32[3,2,48,128]{3,2,1,0:T(8,128)S(1)}, u32[]{:S(2)}, u32[]{:S(2)}) collective-permute-start(f32[3,2,48,128]{3,2,1,0:T(8,128)S(1)} %get-tuple-element.24), channel_id=1, source_target_pairs={{0,24},{8,0},{16,8},{24,16},{1,25},{9,1},{17,9},{25,17},{2,26},{10... | collective-permute-start | bytes 442376 | tf_op jit(solution)/shard_map/ppermute | solution.py:155
  182.0 6.6 %collective-permute-start.12 = (f32[3,2,48,128]{3,2,1,0:T(8,128)S(1)}, f32[3,2,48,128]{3,2,1,0:T(8,128)S(1)}, u32[]{:S(2)}, u32[]{:S(2)}) collective-permute-start(f32[3,2,48,128]{3,2,1,0:T(8,128)S(1)} %get-tuple-element.25), channel_id=1, source_target_pairs={{0,16},{8,24},{16,0},{24,8},{1,17},{9,25},{17,1},{25,9},{2,18},{10... | collective-permute-start | bytes 442376 | tf_op jit(solution)/shard_map/ppermute | solution.py:155
  188.7 9.5 %collective-permute-start.13 = (f32[2,48,128]{2,1,0:T(8,128)S(1)}, f32[2,48,128]{2,1,0:T(8,128)S(1)}, u32[]{:S(2)}, u32[]{:S(2)}) collective-permute-start(f32[2,48,128]{2,1,0:T(8,128)S(1)} %get-tuple-element.32), channel_id=1, source_target_pairs={{0,2},{2,4},{6,0},{1,3},{3,5},{7,1},{8,10},{10,12},{14,8},{9,11},{... | collective-permute-start | bytes 147464 | tf_op jit(solution)/shard_map/ppermute | solution.py:168
  191.2 7.0 %collective-permute-start.14 = (f32[2,48,128]{2,1,0:T(8,128)S(1)}, f32[2,48,128]{2,1,0:T(8,128)S(1)}, u32[]{:S(2)}, u32[]{:S(2)}) collective-permute-start(f32[2,48,128]{2,1,0:T(8,128)S(1)} %get-tuple-element.34), channel_id=1, source_target_pairs={{2,0},{4,2},{6,4},{3,1},{5,3},{7,5},{10,8},{12,10},{14,12},{11,9},... | collective-permute-start | bytes 147464 | tf_op jit(solution)/shard_map/ppermute | solution.py:168
  192.5 7.7 %collective-permute-start.15 = (f32[2,48,128]{2,1,0:T(8,128)S(1)}, f32[2,48,128]{2,1,0:T(8,128)S(1)}, u32[]{:S(2)}, u32[]{:S(2)}) collective-permute-start(f32[2,48,128]{2,1,0:T(8,128)S(1)} %get-tuple-element.33), channel_id=1, source_target_pairs={{0,4},{4,0},{6,2},{1,5},{5,1},{7,3},{8,12},{12,8},{14,10},{9,13},{... | collective-permute-start | bytes 147464 | tf_op jit(solution)/shard_map/ppermute | solution.py:168
  207.8 6.2 %collective-permute-start.20 = (f32[1,2,48,128]{3,2,1,0:T(8,128)S(1)}, f32[1,2,48,128]{3,2,1,0:T(8,128)S(1)}, u32[]{:S(2)}, u32[]{:S(2)}) collective-permute-start(f32[1,2,48,128]{3,2,1,0:T(8,128)S(1)} %get-tuple-element.29), channel_id=1, source_target_pairs={{0,8},{8,16},{16,24},{24,0},{1,9},{9,17},{17,25},{25,1},{2,10},{10... | collective-permute-start | bytes 147464 | tf_op jit(solution)/shard_map/ppermute | solution.py:155
  207.9 6.1 %collective-permute-start.21 = (f32[1,2,48,128]{3,2,1,0:T(8,128)S(1)}, f32[1,2,48,128]{3,2,1,0:T(8,128)S(1)}, u32[]{:S(2)}, u32[]{:S(2)}) collective-permute-start(f32[1,2,48,128]{3,2,1,0:T(8,128)S(1)} %get-tuple-element.30), channel_id=1, source_target_pairs={{0,24},{8,0},{16,8},{24,16},{1,25},{9,1},{17,9},{25,17},{2,26},{10... | collective-permute-start | bytes 147464 | tf_op jit(solution)/shard_map/ppermute | solution.py:155
  211.1 5.6 %collective-permute-start.22 = (f32[1,2,48,128]{3,2,1,0:T(8,128)S(1)}, f32[1,2,48,128]{3,2,1,0:T(8,128)S(1)}, u32[]{:S(2)}, u32[]{:S(2)}) collective-permute-start(f32[1,2,48,128]{3,2,1,0:T(8,128)S(1)} %get-tuple-element.31), channel_id=1, source_target_pairs={{0,16},{8,24},{16,0},{24,8},{1,17},{9,25},{17,1},{25,9},{2,18},{10... | collective-permute-start | bytes 147464 | tf_op jit(solution)/shard_map/ppermute | solution.py:155
  211.1 10.7 %collective-permute-start.16 = (f32[128,128]{1,0:T(8,128)S(1)}, f32[128,128]{1,0:T(8,128)S(1)}, u32[]{:S(2)}, u32[]{:S(2)}) collective-permute-start(f32[128,128]{1,0:T(8,128)S(1)} %fusion.25), channel_id=1, source_target_pairs={{0,1},{1,0},{2,3},{3,2},{4,5},{5,4},{6,7},{7,6},{8,9},{9,8},{10,11... | collective-permute-start | bytes 196616 | tf_op jit(solution)/shard_map/ppermute | solution.py:18
  216.7 5.1 %collective-permute-start.23 = (f32[2,48,128]{2,1,0:T(8,128)S(1)}, f32[2,48,128]{2,1,0:T(8,128)S(1)}, u32[]{:S(2)}, u32[]{:S(2)}) collective-permute-start(f32[2,48,128]{2,1,0:T(8,128)S(1)} %fusion.36), channel_id=1, source_target_pairs={{4,6},{5,7},{12,14},{13,15},{20,22},{21,23},{28,30},{29,31},{36,38... | collective-permute-start | bytes 147464 | tf_op jit(solution)/shard_map/ppermute | solution.py:168
  217.4 5.5 %collective-permute-start.24 = (f32[2,48,128]{2,1,0:T(8,128)S(1)}, f32[2,48,128]{2,1,0:T(8,128)S(1)}, u32[]{:S(2)}, u32[]{:S(2)}) collective-permute-start(f32[2,48,128]{2,1,0:T(8,128)S(1)} %fusion.36), channel_id=1, source_target_pairs={{0,6},{1,7},{8,14},{9,15},{16,22},{17,23},{24,30},{25,31},{32,38},... | collective-permute-start | bytes 147464 | tf_op jit(solution)/shard_map/ppermute | solution.py:168
  221.1 1.7 collective-permute-start.25
  222.9 5.4 %collective-permute-start.26 = (f32[48,128]{1,0:T(8,128)S(1)}, f32[48,128]{1,0:T(8,128)S(1)}, u32[]{:S(2)}, u32[]{:S(2)}) collective-permute-start(f32[48,128]{1,0:T(8,128)S(1)} %dynamic-slice_bitcast_fusion.6), channel_id=1, source_target_pairs={{0,1},{1,0},{2,3},{3,2},{4,5},{5,4},{6,7},{7,6},{8,9},{9,8},{10,11... | collective-permute-start | bytes 73736 | tf_op jit(solution)/shard_map/ppermute | solution.py:18
  225.8 2.6 %collective-permute-start.17 = (f32[128,128]{1,0:T(8,128)S(1)}, f32[128,128]{1,0:T(8,128)S(1)}, u32[]{:S(2)}, u32[]{:S(2)}) collective-permute-start(f32[128,128]{1,0:T(8,128)S(1)} %fusion.28), channel_id=1, source_target_pairs={{0,32},{32,0},{1,33},{33,1},{2,34},{34,2},{3,35},{35,3},{4,36},{36... | collective-permute-start | bytes 196616 | tf_op jit(solution)/shard_map/ppermute | solution.py:18
  228.3 1.2 collective-permute-start.27

commit v5 on v4

v5 whole, which is shorter than its diff:
```python
import functools
import math

import jax
import jax.numpy as jnp
from jax import lax
from jax.experimental import pallas as pl
from jax.experimental.pallas import tpu as pltpu
from jax.sharding import Mesh
from jax.sharding import PartitionSpec as P

MASS = 2
RAW = 8
SWAP = [(0, 1), (1, 0)]


def swap(value, axis):
    return lax.ppermute(value, axis, SWAP)


ANY = pl.BlockSpec(memory_space=pl.ANY)
HINT = pl.CostEstimate(flops=1000, bytes_accessed=1000, transcendentals=0)


def by_time_kernel(cuts, block, *refs):
    outs = refs[-len(cuts) :]
    comps = refs[-1].shape[3]
    for k in range(comps):
        if len(block.shape) == 4:
            part = block[:, k]
        else:
            part = jnp.stack([block[n * comps + k] for n in range(block.shape[0] // comps)])
        turned = jnp.swapaxes(part, 0, 1)
        for (low, high, x, nx, y, ny), out in zip(cuts, outs):
            for i in range(nx):
                for j in range(ny):
                    out[i, 0, j, k] = turned[2 * (x + i) + y + j, low:high]


def by_time(block, cuts, *after):
    if block.ndim == 4:
        n, comps, times, sites = block.shape
        spec = pl.BlockSpec((n, comps, times // 4, sites), lambda z: (0, 0, z, 0))
    else:
        n, comps = RAW, block.shape[0] // RAW
        _, times, sites = block.shape
        spec = pl.BlockSpec((n * comps, times // 4, sites), lambda z: (0, z, 0))
    return pl.pallas_call(
        functools.partial(by_time_kernel, cuts),
        grid=(4,),
        in_specs=[spec] + [ANY] * len(after),
        out_specs=[
            pl.BlockSpec((nx, 1, ny, comps, high - low, sites), lambda z: (0, z, 0, 0, 0, 0))
            for low, high, _, nx, _, ny in cuts
        ],
        out_shape=[
            jax.ShapeDtypeStruct((nx, 4, ny, comps, high - low, sites), block.dtype)
            for low, high, _, nx, _, ny in cuts
        ],
        compiler_params=pltpu.CompilerParams(vmem_limit_bytes=(56 if n > RAW else 16) * 2**20),
        cost_estimate=HINT,
        name="by_time",
    )(block, *after)


def rows_of(block):
    x, z, yh, comps, n, sites = block.shape
    return block.reshape(x, z * yh, comps // 2, 2 * n, sites)


def front_kernel(owned, at, sols, vecs, out, lines, slab, sems):
    count, comps, rows, _ = lines.shape
    whole = pltpu.make_async_copy(
        sols.at[pl.ds(0, RAW * comps)], out.at[pl.ds(0, RAW * comps)], sems.at[count]
    )
    whole.start()
    group, time = at[0], at[1]
    copies = []
    for s in range(count):
        copies.append(
            pltpu.make_async_copy(
                vecs.at[at[2 + s] % owned, :, pl.ds(pl.multiple_of(time // rows * rows, rows), rows)],
                lines.at[s],
                sems.at[s],
            )
        )
        copies[s].start()
    row = lax.broadcasted_iota(jnp.int32, lines.shape[1:], 1)
    for s in range(count):
        copies[s].wait()
        here = jnp.where(at[2 + s] // owned == group, time % rows, -1)
        kept = jnp.sum(jnp.where(row == here, lines[s].astype(jnp.float32), 0.0), axis=1)
        slab[s] = jnp.concatenate([kept, jnp.zeros_like(kept[:2])], axis=0).astype(slab.dtype)
    last = pltpu.make_async_copy(slab, out.at[RAW * comps], sems.at[count + 1])
    last.start()
    last.wait()
    whole.wait()


def front(sols, vecs, source_index, source_time, group):
    owned, comps, times, sites = vecs.shape
    count = source_index.shape[0]
    at = jnp.concatenate([group[None], source_time, source_index])
    out = pl.pallas_call(
        functools.partial(front_kernel, owned),
        in_specs=[pl.BlockSpec(memory_space=pltpu.SMEM), ANY, ANY],
        out_specs=ANY,
        out_shape=jax.ShapeDtypeStruct((RAW * comps + 1, count, times // count, sites), sols.dtype),
        scratch_shapes=[
            pltpu.VMEM((count, comps, 16, sites), sols.dtype),
            pltpu.VMEM((count, times // count, sites), sols.dtype),
            pltpu.SemaphoreType.DMA((count + 2,)),
        ],
        compiler_params=pltpu.CompilerParams(vmem_limit_bytes=56 * 2**20),
        cost_estimate=HINT,
        name="front",
    )(at, sols.reshape(-1, count, times // count, sites), vecs)
    return out.reshape(RAW * comps + 1, times, sites)


def product(cols, own, other):
    return lax.dot_general(
        jnp.concatenate(cols, axis=0),
        jnp.concatenate([own, other], axis=0),
        (((1,), (1,)), ((), ())),
        preferred_element_type=jnp.float32,
    )


def real_imag(total, row, n):
    width = total.shape[1] // 4
    re, im = total[row : row + n], total[row + n : row + 2 * n]
    real, imag = [], []
    for left in (0, 2 * width):
        mid, right = left + width, left + 2 * width
        real.append(re[:, left:mid] + im[:, mid:right])
        imag.append(im[:, left:mid] - re[:, mid:right])
    return jnp.concatenate(real, axis=1), jnp.concatenate(imag, axis=1)


def dot_kernel(count, *refs):
    cols, (own, other), outs = refs[:count], refs[count : count + 2], refs[-count:]
    for at in range(own.shape[1]):
        total = None
        for colour in range(own.shape[2]):
            term = product(
                [col[0, at, colour] for col in cols], own[0, at, colour], other[0, at, colour]
            )
            total = term if total is None else total + term
        row = 0
        for col, out in zip(cols, outs):
            n = col.shape[3] // 2
            out[0, at, 0], out[0, at, 1] = real_imag(total, row, n)
            row += 2 * n


def pieces_kernel(count, *refs):
    total = None
    for at in range(count):
        col, own, other = refs[3 * at : 3 * at + 3]
        for colour in range(own.shape[1]):
            term = product([col[0, colour]], own[0, colour], other[0, colour])
            total = term if total is None else total + term
    out = refs[-1]
    n = out.shape[2]
    parts = real_imag(total, 0, n)
    for part in range(2):
        if len(refs) == 3 * count + 1:
            out[0, part] = parts[part]
        else:
            out[0, part] = refs[3 * count][0, part] + parts[part]


def project_pieces(pieces, before=None):
    inner, colours, n2, sites = pieces[0][0].shape
    rows = pieces[0][1].shape[2]
    spec = lambda shape: pl.BlockSpec((1,) + shape[1:], lambda j: (j, 0, 0, 0))
    args = [array for piece in pieces for array in piece]
    if before is not None:
        args.append(before)
    out = (inner, 2, n2 // 2, rows)
    return pl.pallas_call(
        functools.partial(pieces_kernel, len(pieces)),
        grid=(inner,),
        in_specs=[spec(array.shape) for array in args],
        out_specs=spec(out),
        out_shape=jax.ShapeDtypeStruct(out, jnp.float32),
        compiler_params=pltpu.CompilerParams(vmem_limit_bytes=16 * 2**20),
        cost_estimate=HINT,
        name="project_pieces",
    )(*args)


def project(cols, own, other, x, y, step, *after):
    size, inner, colours, _, sites = cols[0].shape
    rows, stride = own.shape[3], own.shape[1] // inner
    spec = lambda n, stride=1, x=0, y=0: pl.BlockSpec(
        (1, step, colours, n, sites), lambda i, j: (i + x, j * stride + y, 0, 0, 0)
    )
    in_specs = [spec(c.shape[3]) for c in cols] + [spec(rows, stride, x, y)] * 2
    in_specs += [ANY] * len(after)
    out_specs = [
        pl.BlockSpec((1, step, 2, c.shape[3] // 2, rows), lambda i, j: (i, j, 0, 0, 0))
        for c in cols
    ]
    out_shape = [
        jax.ShapeDtypeStruct((size, inner, 2, c.shape[3] // 2, rows), jnp.float32) for c in cols
    ]
    return pl.pallas_call(
        functools.partial(dot_kernel, len(cols)),
        grid=(size, inner // step),
        in_specs=in_specs,
        out_specs=out_specs,
        out_shape=out_shape,
        compiler_params=pltpu.CompilerParams(vmem_limit_bytes=48 * 2**20),
        cost_estimate=HINT,
        name="project",
    )(*cols, own, other, *after)


def pick(value, index):
    return lax.dynamic_index_in_dim(value, index, 0, keepdims=False)


def share_z(slabs):
    me = lax.axis_index("z")
    got = [
        lax.ppermute(pick(slabs, (me + k) % 4), "z", [(i, (i + k) % 4) for i in range(4)])
        for k in (1, 3, 2)
    ]
    return [pick(slabs, me), *got]


def sum_z(part):
    got = share_z(jnp.swapaxes(part, 0, 1))
    return got[0] + got[1] + got[2] + got[3]


def sum_x(part, first, size):
    me = lax.axis_index("x")
    clip = lambda i: jnp.clip(i - first, 0, size - 1)
    total = pick(part, clip(me)) if size > 1 else part[0]
    for k in (1, 3, 2):
        send = pick(part, clip((me + k) % 4)) if size > 1 else part[0]
        pairs = [(i, (i + k) % 4) for i in range(4) if first <= (i + k) % 4 < first + size]
        total = total + lax.ppermute(send, "x", pairs)
    return total


def sum_yh(part):
    me = lax.axis_index("yh")
    return pick(part, me) + swap(pick(part, 1 - me), "yh")


def local(eigvecs, solutions, source_index, source_time, dilution):
    owned, times, comps, sites = eigvecs.shape
    count = solutions.shape[1]
    nsources, spins = dilution.shape
    scale = 1.0 / math.sqrt(comps * sites * 32)
    core = lax.axis_index("c")
    group = 2 * lax.axis_index("yl") + core
    sols = solutions[0].transpose(0, 2, 1, 3)
    vecs = eigvecs.transpose(0, 2, 1, 3)

    first_part = front(sols, vecs, source_index, source_time, group)
    raw = swap(first_part, "yl")
    other = swap(vecs, "c")
    sent = [(RAW, count, x, nx, 0, 2) for x, nx in ((0, 2), (2, 1), (3, 1))]
    mine, *send = by_time(sols, ((0, count, 0, 4, 0, 2), *sent), first_part)
    got = [swap(rows_of(part), "yl") for part in send[:2]]
    shared = [part.reshape(2, comps // 2, -1, sites) for part in share_z(send[2][0])]
    got_last = [swap(part, "yl") for part in shared]

    whole = (0, owned, 0, 4, 0, 2)
    late = (0, owned, 3, 1, 0, 2)
    own, own_late = by_time(vecs, (whole, late))
    other, other_late = by_time(other, (whole, late))
    own, other = rows_of(own), rows_of(other)
    lines = raw[RAW * comps] + first_part[RAW * comps]
    raw = rows_of(by_time(raw, ((0, RAW, 0, 4, 0, 2),), other)[0])

    mine_z = share_z(own_late[0])
    theirs_z = [pick(other_late[0], lax.axis_index("z"))] + [swap(p, "c") for p in mine_z[1:]]
    pieces = [
        (s, *(v.reshape(2, comps // 2, 2 * owned, sites) for v in pair))
        for s, *pair in zip(got_last, mine_z, theirs_z)
    ]

    def rows(part):
        x, inner, _, n, lanes = part.shape
        return part.reshape(x, 4, inner // 4, 2 * n, lanes)

    def against(part, x, y, step, *after):
        return rows(project([part], own, other, x, y, step, *after)[0])

    parts = project([rows_of(mine), raw], own, other, 0, 0, 8, *shared[1:], *mine_z[1:])
    first_z = sum_z(jnp.concatenate([rows(p) for p in parts], axis=3))
    first = sum_x(first_z, 0, 4)
    mid = [against(got[0], 0, 0, 8, first, *theirs_z[1:])]
    mid.append(against(got[1], 2, 0, 4, mid[0]))
    mid = sum_x(sum_z(jnp.concatenate(mid, axis=0)), 0, 3)
    last = project_pieces(pieces[3:], project_pieces(pieces[:3]))
    last = sum_x(last.reshape(1, 2, -1, 2 * owned), 3, 1)
    late = jnp.where(lax.axis_index("x") == 3, last, mid)
    here = sum_yh(jnp.concatenate([first, late], axis=1))
    there = swap(here, "c")

    def assemble(sums, half):
        sums = sums[:, half * owned : (half + 1) * owned]
        view = lambda v: v.reshape(2, -1, owned)
        cut = [2 * count, 2 * (count + RAW)]
        away = [view(sums[cut[0] : cut[1]]), view(sums[cut[1] :])]
        return view(sums[: cut[0]]), jnp.concatenate(away, axis=1)

    h0, y0 = assemble(here, 0)
    h1, y1 = assemble(there, 1)
    tau = jnp.stack([h0, h1, y0, y1])
    order = jnp.stack([group, group ^ 1, group ^ 2, group ^ 3])
    spin_of = jnp.take(jnp.transpose(dilution), order, axis=0)
    mask = spin_of[:, None, :] == jnp.arange(spins, dtype=jnp.int32)[None, :, None]
    view = tau.reshape(4, 1, 2, MASS, nsources, count // (MASS * nsources), owned)
    picked = jnp.where(mask[:, :, None, None, :, None, None], view, 0.0)
    result = jnp.sum(picked, axis=0).reshape(spins, 2, count, owned) * scale
    result = result.transpose(3, 0, 2, 1).reshape(1, owned, spins * count * 2)

    lines = lines + swap(lines, "c")
    chosen = lines.reshape(nsources, -1, sites)[:, :comps]
    my_spins = lax.dynamic_index_in_dim(dilution, group, 1, keepdims=False)
    spin_mask = jnp.arange(spins, dtype=jnp.int32)[None, :] == my_spins[:, None]
    sources = jnp.where(
        spin_mask[:, :, None, None], chosen[:, None, :, :], jnp.zeros((), jnp.bfloat16)
    )
    return result, sources[None]


def solution(mesh):
    split = Mesh(mesh.devices.reshape(2, 2, 4, 4, 2), ("yl", "c", "z", "x", "yh"))
    grp, lat = ("yl", "c"), ("z", "x", "yh")
    return jax.shard_map(
        local,
        mesh=split,
        in_specs=(P(grp, None, None, lat), P(grp, None, None, None, lat), P(), P(), P()),
        out_specs=(P(lat, grp, None), P(grp, None, None, None, lat)),
        check_vma=False,
    )
```

time: 234 us -> 242 us (1.034)
  blocking collectives: 80.6 us -> 0 us
  Pallas kernels: 67.1 us -> 111 us
  waiting for transfers between devices: 28.9 us -> 49.9 us
  local copies, waits for them, and re-layouts: 5.32 us -> 18.6 us
  starting transfers between devices: 42.7 us -> 51.9 us
    psum x1 -> x0, blocking collectives: 80.6 us -> none  [local(): chosen = lax.psum(chosen, ('yl', 'c'))]
    pallas_call x1 -> x3, Pallas kernels: 3.78 us -> 53.4 us  [the longest x1 49.5 us: front(): pl.pallas_call(functools.partial(front_kernel, owned), in_specs=[pl.Block...]
    ppermute x10 -> x14, waiting for transfers between devices: 3.57 us -> 15.9 us  [swap(): return lax.ppermute(value, axis, SWAP)]
    unnamed x12 -> x30, local copies, waits for them, and re-layouts: 1.51 us -> 10.8 us
    pallas_call x5 -> x3, Pallas kernels: 32.4 us -> 25.3 us  [project(): pl.pallas_call(functools.partial(dot_kernel, len(cols)), grid=(size, inne...]
    dynamic_slice x0 -> x3, local copies, waits for them, and re-layouts: none -> 6.68 us  [pick(): return lax.dynamic_index_in_dim(value, index, 0, keepdims=False)]
    ppermute x9 -> x12, starting transfers between devices: 12.6 us -> 19.2 us  [share_z(): lax.ppermute(pick(slabs, (me + k) % 4), 'z', [(i, (i + k) % 4) for i in r...]
    ppermute x9 -> x12, waiting for transfers between devices: 22.3 us -> 27.8 us  [share_z(): lax.ppermute(pick(slabs, (me + k) % 4), 'z', [(i, (i + k) % 4) for i in r...]
  transfers between devices with their start and end apart: 28 -> 35, of which waited for: 10 -> 14; matrix products, arithmetic and copies ran while one was open for 3% -> 6% of each run, Pallas kernels for 27% -> 46%
where the time goes in v5:
time: 242 us; the launch traced here: 240 us
  Pallas kernels  111 us (46%)
  starting transfers between devices  51.9 us (21%)
  waiting for transfers between devices  49.9 us (21%)
  local copies, waits for them, and re-layouts  18.6 us (8%)
  other arithmetic  6.68 us (3%)
    pallas_call x1, Pallas kernels, front(): pl.pallas_call(functools.partial(front_kernel, owned), in_specs=[pl.Block...  49.5 us
    pallas_call x4, Pallas kernels, by_time(): pl.pallas_call(functools.partial(by_time_kernel, cuts), grid=(4,), in_spe...  32.4 us
    ppermute x12, waiting for transfers between devices, share_z(): lax.ppermute(pick(slabs, (me + k) % 4), 'z', [(i, (i + k) % 4) for i in r...  27.8 us
    pallas_call x3, Pallas kernels, project(): pl.pallas_call(functools.partial(dot_kernel, len(cols)), grid=(size, inne...  25.3 us
    ppermute x9, starting transfers between devices, sum_x(): total = total + lax.ppermute(send, 'x', pairs)  19.9 us
    ppermute x12, starting transfers between devices, share_z(): lax.ppermute(pick(slabs, (me + k) % 4), 'z', [(i, (i + k) % 4) for i in r...  19.2 us
    ppermute x14, waiting for transfers between devices, swap(): return lax.ppermute(value, axis, SWAP)  15.9 us
    ppermute x14, starting transfers between devices, swap(): return lax.ppermute(value, axis, SWAP)  12.8 us
  transfers between devices with their start and end apart: 35, of which 14 were waited for; matrix products, arithmetic and copies ran while one was open for 6% of the time, Pallas kernels for 46%

profile of v5, /device:TPU:0, one launch (start us, length us, event | category | flops | bytes accessed | tf_op | source)
XLA Modules:
  0.0 240.0 jit_solution(3253242613468685293)
XLA Ops:
  1.4 1.2 pad_add_fusion.at
  2.6 49.5 %front.1 = bf16[49,4,8,512]{3,2,1,0:T(8,128)(2,1)} custom-call(s32[6]{0:T(128)} %pad_add_fusion.at, bf16[192,4,8,512]{3,2,1,0:T(8,128)(2,1)} %bitcast.174, bf16[64,6,32,512]{3,2,1,0:T(8,128)(2,1)} %bitcast.172), custom_call_target="tpu_custom_call" | custom-call | flops 1000 | bytes 1000 | tf_op jit(solution)/shard_map/front/pallas_call | solution.py:104
  52.1 1.7 collective-permute-start
  53.8 7.7 %by_time.4 = (bf16[4,4,2,6,32,512]{5,4,3,2,1,0:T(8,128)(2,1)}, bf16[2,4,2,6,24,512]{5,4,3,2,1,0:T(8,128)(2,1)}, bf16[1,4,2,6,24,512]{5,4,3,2,1,0:T(8,128)(2,1)}, bf16[1,4,2,6,24,512]{5,4,3,2,1,0:T(8,128)(2,1)}) custom-call(bf16[32,6,32,512]{3,2,1,0:T(8,128)(2,1)} %bitcast.175, bf16[49,32,512]{2,1,0:T(8,128)(2,1)} %bitcast.177), custom_call_target="tpu_custom_call" | custom-call | flops 1000 | bytes 1000 | tf_op jit(solution)/shard_map/by_time/pallas_call | solution.py:48
  61.5 2.2 constant_dynamic-slice_fusion.3
  63.7 3.9 %collective-permute-start.4 = (bf16[2,6,24,512]{3,2,1,0:T(8,128)(2,1)S(1)}, bf16[2,6,24,512]{3,2,1,0:T(8,128)(2,1)S(1)}, u32[]{:S(2)}, u32[]{:S(2)}) collective-permute-start(bf16[2,6,24,512]{3,2,1,0:T(8,128)(2,1)S(1)} %get-tuple-element.34), channel_id=1, source_target_pairs={{0,16},{8,24},{16,0},{24,8},{1,17},{9,25},{17,1},{25,9},{2,18},{10... | collective-permute-start | bytes 884744 | tf_op jit(solution)/shard_map/ppermute | solution.py:228
  67.6 0.7 collective-permute-start.3
  68.3 11.1 %by_time.7 = (bf16[4,4,2,6,64,512]{5,4,3,2,1,0:T(8,128)(2,1)}, bf16[1,4,2,6,64,512]{5,4,3,2,1,0:T(8,128)(2,1)}) custom-call(bf16[64,6,32,512]{3,2,1,0:T(8,128)(2,1)} %bitcast.173), custom_call_target="tpu_custom_call" | custom-call | flops 1000 | bytes 1000 | tf_op jit(solution)/shard_map/by_time/pallas_call | solution.py:48
  79.4 3.3 %constant_dynamic-slice_fusion.2 = (bf16[1,1,2,6,64,512]{5,4,3,2,1,0:T(8,128)(2,1)S(1)}, bf16[2,6,64,512]{3,2,1,0:T(8,128)(2,1)}, bf16[2,6,64,512]{3,2,1,0:T(8,128)(2,1)}, bf16[2,6,64,512]{3,2,1,0:T(8,128)(2,1)}) fusion(bf16[1,4,2,6,64,512]{5,4,3,2,1,0:T(8,128)(2,1)} %get-tuple-element.16, s32[]{:T(128)S(6)} %select_n.157, s32[]{:T(128)S(6)} %select_n.156, ...), kind=kLoop, calls=%fused_computation.79 | loop fusion | bytes 6291472 | tf_op jit(solution)/shard_map/jit(dynamic_index_in_dim)/dynamic_slice | solution.py:222
  82.7 2.4 collective-permute-start.7
  85.0 1.6 collective-permute-start.6
  86.7 0.7 copy-done.10
  87.8 2.2 collective-permute-done.block
  90.0 1.7 collective-permute-start.24
  91.6 1.9 collective-permute-start.2
  93.7 11.2 %by_time.5 = (bf16[4,4,2,6,64,512]{5,4,3,2,1,0:T(8,128)(2,1)}, bf16[1,4,2,6,64,512]{5,4,3,2,1,0:T(8,128)(2,1)}) custom-call(bf16[64,6,32,512]{3,2,1,0:T(8,128)(2,1)} %collective-permute-done.1.block), custom_call_target="tpu_custom_call" | custom-call | flops 1000 | bytes 1000 | tf_op jit(solution)/shard_map/by_time/pallas_call | solution.py:48
  104.8 4.6 %copy-done = bf16[4,4,2,6,64,512]{5,4,3,2,1,0:T(8,128)(2,1)S(1)} copy-done((bf16[4,4,2,6,64,512]{5,4,3,2,1,0:T(8,128)(2,1)S(1)}, bf16[4,4,2,6,64,512]{5,4,3,2,1,0:T(8,128)(2,1)}, u32[]{:S(2)}) %copy-start) | copy-done | bytes 12582936
  109.4 2.5 %by_time.6 = bf16[4,4,2,6,8,512]{5,4,3,2,1,0:T(8,128)(2,1)S(1)} custom-call(bf16[49,32,512]{2,1,0:T(8,128)(2,1)} %collective-permute-done.block, bf16[4,8,3,128,512]{4,3,2,1,0:T(8,128)(2,1)S(1)} %bitcast.144), custom_call_target="tpu_custom_call" | custom-call | flops 1000 | bytes 1000 | tf_op jit(solution)/shard_map/by_time/pallas_call | solution.py:48
  111.9 14.8 %collective-permute-done.2 = bf16[2,6,24,512]{3,2,1,0:T(8,128)(2,1)} collective-permute-done((bf16[2,6,24,512]{3,2,1,0:T(8,128)(2,1)}, bf16[2,6,24,512]{3,2,1,0:T(8,128)(2,1)}, u32[]{:S(2)}, u32[]{:S(2)}) %collective-permute-start.2) | collective-permute-done | bytes 294944 | tf_op jit(solution)/shard_map/ppermute | solution.py:228
  126.8 0.9 copy-done.1
  127.7 0.9 copy-done.4
  128.5 1.1 copy-done.2
  129.7 1.1 copy-done.5
  130.8 13.4 %project.3 = (f32[4,8,2,32,128]{4,3,2,1,0:T(8,128)S(1)}, f32[4,8,2,8,128]{4,3,2,1,0:T(8,128)S(1)}) custom-call(bf16[4,8,3,64,512]{4,3,2,1,0:T(8,128)(2,1)} %bitcast.178, bf16[4,8,3,16,512]{4,3,2,1,0:T(8,128)(2,1)S(1)} %bitcast.148, bf16[4,8,3,128,512]{4,3,2,1,0:T(8,128)(2,1)} %bitcast.168, bf16[4,8,3,128,512]{4,3,2,1,0:T(8,128)(2,1)} %bitcast.141, ...), custom_call_target="tpu_custom_call" | custom-call | flops 1000 | bytes 1000 | tf_op jit(solution)/shard_map/project/pallas_call | solution.py:209
  144.2 1.1 fusion.8
  145.3 0.9 collective-permute-start.8
  146.2 2.3 collective-permute-start.9
  149.2 1.2 collective-permute-start.10
  150.6 12.9 %collective-permute-done.8 = f32[4,2,80,128]{3,2,1,0:T(8,128)} collective-permute-done((f32[4,2,80,128]{3,2,1,0:T(8,128)}, f32[4,2,80,128]{3,2,1,0:T(8,128)}, u32[]{:S(2)}, u32[]{:S(2)}) %collective-permute-start.8) | collective-permute-done | bytes 327712 | tf_op jit(solution)/shard_map/ppermute | solution.py:228
  164.5 1.1 fusion.6
  165.7 0.7 copy-done.12
  166.4 1.5 collective-permute-start.11
  168.1 2.8 %collective-permute-start.13 = (f32[2,80,128]{2,1,0:T(8,128)S(1)}, f32[2,80,128]{2,1,0:T(8,128)S(1)}, u32[]{:S(2)}, u32[]{:S(2)}) collective-permute-start(f32[2,80,128]{2,1,0:T(8,128)S(1)} %get-tuple-element.41), channel_id=1, source_target_pairs={{0,4},{2,6},{4,0},{6,2},{1,5},{3,7},{5,1},{7,3},{8,12},{10,14},{12... | collective-permute-start | bytes 245768 | tf_op jit(solution)/shard_map/ppermute | solution.py:246
  170.9 1.2 collective-permute-done.11
  172.1 2.4 collective-permute-start.12
  174.7 1.6 collective-permute-start.16
  176.5 1.6 collective-permute-start.19
  178.1 0.9 fusion.23.refs_3_
  179.5 1.6 collective-permute-start.17
  181.1 7.4 %project.4 = f32[2,8,2,24,128]{4,3,2,1,0:T(8,128)S(1)} custom-call(bf16[2,8,3,48,512]{4,3,2,1,0:T(8,128)(2,1)} %collective-permute-done.24.refs_0_, bf16[4,8,3,128,512]{4,3,2,1,0:T(8,128)(2,1)} %bitcast.169, bf16[4,8,3,128,512]{4,3,2,1,0:T(8,128)(2,1)} %bitcast.142, f32[2,80,128]{2,1,0:T(8,128)S(1)} %fusion.23.refs_3_, ...), custom_call_target="tpu_custom_call" | custom-call | flops 1000 | bytes 1000 | tf_op jit(solution)/shard_map/project/pallas_call | solution.py:209
  188.6 3.0 %collective-permute-done.25.refs_0_ = bf16[1,8,3,48,512]{4,3,2,1,0:T(8,128)(2,1)} collective-permute-done((bf16[1,8,3,48,512]{4,3,2,1,0:T(8,128)(2,1)}, bf16[1,8,3,48,512]{4,3,2,1,0:T(8,128)(2,1)}, u32[]{:S(2)}, u32[]{:S(2)}) %collective-permute-start.25) | collective-permute-done | bytes 1179680 | tf_op jit(solution)/shard_map/ppermute | solution.py:18
  191.6 4.4 %project.5 = f32[1,8,2,24,128]{4,3,2,1,0:T(8,128)S(1)} custom-call(bf16[1,8,3,48,512]{4,3,2,1,0:T(8,128)(2,1)} %collective-permute-done.25.refs_0_, bf16[4,8,3,128,512]{4,3,2,1,0:T(8,128)(2,1)} %bitcast.170, bf16[4,8,3,128,512]{4,3,2,1,0:T(8,128)(2,1)} %bitcast.143, f32[2,4,2,48,128]{4,3,2,1,0:T(8,128)S(1)} %bitcast.145), custom_call_target="tpu_custom_call" | custom-call | flops 1000 | bytes 1000 | tf_op jit(solution)/shard_map/project/pallas_call | solution.py:209
  196.2 1.6 collective-permute-done.16.refs_0_
  197.8 1.6 collective-permute-start.27
  199.4 3.5 %collective-permute-done.19.refs_6_ = bf16[2,3,48,512]{3,2,1,0:T(8,128)(2,1)S(1)} collective-permute-done((bf16[2,3,48,512]{3,2,1,0:T(8,128)(2,1)}, bf16[2,3,48,512]{3,2,1,0:T(8,128)(2,1)S(1)}, u32[]{:S(2)}, u32[]{:S(2)}) %collective-permute-start.19) | collective-permute-done | bytes 294944 | tf_op jit(solution)/shard_map/ppermute | solution.py:18
  202.9 2.2 collective-permute-start.28
  205.1 0.8 fusion.32
  205.9 1.2 constant_dynamic-slice_fusion.1
  207.1 2.1 collective-permute-done.17.refs_3_
  209.3 3.0 %project_pieces.2.refs_3_ = f32[2,2,24,128]{3,2,1,0:T(8,128)S(1)} custom-call(bf16[2,3,48,512]{3,2,1,0:T(8,128)(2,1)S(1)} %collective-permute-done.16.refs_0_, bf16[2,3,128,512]{3,2,1,0:T(8,128)(2,1)S(1)} %bitcast.152, bf16[2,3,128,512]{3,2,1,0:T(8,128)(2,1)S(1)} %bitcast.151, bf16[2,3,48,512]{3,2,1,0:T(8,128)(2,1)S(1)} %collective-permute-done.17.refs_3_, ...), custom_call_target="tpu_custom_call" | custom-call | flops 1000 | bytes 1000 | tf_op jit(solution)/shard_map/project_pieces/pallas_call | solution.py:182
  212.3 1.0 project_pieces.3
  213.2 4.7 %collective-permute-start.22 = (f32[2,48,128]{2,1,0:T(8,128)S(1)}, f32[2,48,128]{2,1,0:T(8,128)S(1)}, u32[]{:S(2)}, u32[]{:S(2)}) collective-permute-start(f32[2,48,128]{2,1,0:T(8,128)S(1)} %bitcast.165), channel_id=1, source_target_pairs={{0,6},{1,7},{8,14},{9,15},{16,22},{17,23},{24,30},{25,31},{32,38},... | collective-permute-start | bytes 147464 | tf_op jit(solution)/shard_map/ppermute | solution.py:246
  217.9 0.7 collective-permute-start.23
  218.6 0.7 collective-permute-start.21
  219.4 3.4 %collective-permute-start.29 = (f32[2,48,128]{2,1,0:T(8,128)S(1)}, f32[2,48,128]{2,1,0:T(8,128)S(1)}, u32[]{:S(2)}, u32[]{:S(2)}) collective-permute-start(f32[2,48,128]{2,1,0:T(8,128)S(1)} %get-tuple-element.43), channel_id=1, source_target_pairs={{0,2},{2,4},{6,0},{1,3},{3,5},{7,1},{8,10},{10,12},{14,8},{9,11},{... | collective-permute-start | bytes 147464 | tf_op jit(solution)/shard_map/ppermute | solution.py:246
  222.8 2.5 %collective-permute-start.31 = (f32[2,48,128]{2,1,0:T(8,128)S(1)}, f32[2,48,128]{2,1,0:T(8,128)S(1)}, u32[]{:S(2)}, u32[]{:S(2)}) collective-permute-start(f32[2,48,128]{2,1,0:T(8,128)S(1)} %get-tuple-element.44), channel_id=1, source_target_pairs={{0,4},{4,0},{6,2},{1,5},{5,1},{7,3},{8,12},{12,8},{14,10},{9,13},{... | collective-permute-start | bytes 147464 | tf_op jit(solution)/shard_map/ppermute | solution.py:246
  225.3 1.3 collective-permute-start.30
  226.7 3.6 %collective-permute-done.31 = f32[2,48,128]{2,1,0:T(8,128)S(1)} collective-permute-done((f32[2,48,128]{2,1,0:T(8,128)S(1)}, f32[2,48,128]{2,1,0:T(8,128)S(1)}, u32[]{:S(2)}, u32[]{:S(2)}) %collective-permute-start.31) | collective-permute-done | bytes 49184 | tf_op jit(solution)/shard_map/ppermute | solution.py:246
  230.3 1.0 collective-permute-done.30
  231.4 3.0 %collective-permute-start.32 = (f32[128,128]{1,0:T(8,128)S(1)}, f32[128,128]{1,0:T(8,128)S(1)}, u32[]{:S(2)}, u32[]{:S(2)}) collective-permute-start(f32[128,128]{1,0:T(8,128)S(1)} %fusion.25), channel_id=1, source_target_pairs={{0,1},{1,0},{2,3},{3,2},{4,5},{5,4},{6,7},{7,6},{8,9},{9,8},{10,11... | collective-permute-start | bytes 196616 | tf_op jit(solution)/shard_map/ppermute | solution.py:18
  234.3 0.7 broadcast_select_fusion
  235.1 2.1 collective-permute-done.32
  237.4 1.2 collective-permute-done.33
  239.3 0.7 copy.12
  (83 shorter events, 4.7 us)
Async XLA Ops:
  0.6 91.0 %collective-permute-start.1 = (bf16[64,6,32,512]{3,2,1,0:T(8,128)(2,1)}, bf16[64,6,32,512]{3,2,1,0:T(8,128)(2,1)}, u32[]{:S(2)}, u32[]{:S(2)}) collective-permute-start(bf16[64,6,32,512]{3,2,1,0:T(8,128)(2,1)} %bitcast.171), channel_id=1, source_target_pairs={{0,32},{32,0},{1,33},{33,1},{2,34},{34,2},{3,35},{35,3},{4,36},{36... | collective-permute-start | bytes 37748744 | tf_op jit(solution)/shard_map/ppermute | solution.py:18
  52.1 37.9 %collective-permute-start = (bf16[49,32,512]{2,1,0:T(8,128)(2,1)}, bf16[49,32,512]{2,1,0:T(8,128)(2,1)}, u32[]{:S(2)}, u32[]{:S(2)}) collective-permute-start(bf16[49,32,512]{2,1,0:T(8,128)(2,1)} %bitcast.176), channel_id=1, source_target_pairs={{0,64},{64,0},{1,65},{65,1},{2,66},{66,2},{3,67},{67,3},{4,68},{68... | collective-permute-start | bytes 4816904 | tf_op jit(solution)/shard_map/ppermute | solution.py:18
  63.7 21.3 %collective-permute-start.4 = (bf16[2,6,24,512]{3,2,1,0:T(8,128)(2,1)S(1)}, bf16[2,6,24,512]{3,2,1,0:T(8,128)(2,1)S(1)}, u32[]{:S(2)}, u32[]{:S(2)}) collective-permute-start(bf16[2,6,24,512]{3,2,1,0:T(8,128)(2,1)S(1)} %get-tuple-element.34), channel_id=1, source_target_pairs={{0,16},{8,24},{16,0},{24,8},{1,17},{9,25},{17,1},{25,9},{2,18},{10... | collective-permute-start | bytes 884744 | tf_op jit(solution)/shard_map/ppermute | solution.py:228
  67.6 19.1 %collective-permute-start.3 = (bf16[2,6,24,512]{3,2,1,0:T(8,128)(2,1)S(1)}, bf16[2,6,24,512]{3,2,1,0:T(8,128)(2,1)S(1)}, u32[]{:S(2)}, u32[]{:S(2)}) collective-permute-start(bf16[2,6,24,512]{3,2,1,0:T(8,128)(2,1)S(1)} %get-tuple-element.35), channel_id=1, source_target_pairs={{0,24},{8,0},{16,8},{24,16},{1,25},{9,1},{17,9},{25,17},{2,26},{10... | collective-permute-start | bytes 884744 | tf_op jit(solution)/shard_map/ppermute | solution.py:228
  79.4 14.2 %copy-start.13 = (s32[4,4]{1,0:T(4,128)S(1)}, s32[4,4]{1,0:T(4,128)}, u32[]{:S(2)}) copy-start(s32[4,4]{1,0:T(4,128)} %param.9) | copy-start | bytes 196
  82.7 44.1 %collective-permute-start.7 = (bf16[2,6,64,512]{3,2,1,0:T(8,128)(2,1)}, bf16[2,6,64,512]{3,2,1,0:T(8,128)(2,1)S(1)}, u32[]{:S(2)}, u32[]{:S(2)}) collective-permute-start(bf16[2,6,64,512]{3,2,1,0:T(8,128)(2,1)} %get-tuple-element.27), channel_id=1, source_target_pairs={{0,16},{8,24},{16,0},{24,8},{1,17},{9,25},{17,1},{25,9},{2,18},{10... | collective-permute-start | bytes 2359304 | tf_op jit(solution)/shard_map/ppermute | solution.py:228
  85.0 19.8 %copy-start.8 = (bf16[2,6,24,512]{3,2,1,0:T(8,128)(2,1)}, bf16[2,6,24,512]{3,2,1,0:T(8,128)(2,1)S(1)}, u32[]{:S(2)}) copy-start(bf16[2,6,24,512]{3,2,1,0:T(8,128)(2,1)S(1)} %collective-permute-done.4) | copy-start | bytes 884740
  85.0 41.7 %collective-permute-start.6 = (bf16[2,6,64,512]{3,2,1,0:T(8,128)(2,1)}, bf16[2,6,64,512]{3,2,1,0:T(8,128)(2,1)S(1)}, u32[]{:S(2)}, u32[]{:S(2)}) collective-permute-start(bf16[2,6,64,512]{3,2,1,0:T(8,128)(2,1)} %get-tuple-element.28), channel_id=1, source_target_pairs={{0,24},{8,0},{16,8},{24,16},{1,25},{9,1},{17,9},{25,17},{2,26},{10... | collective-permute-start | bytes 2359304 | tf_op jit(solution)/shard_map/ppermute | solution.py:228
  86.7 0.7 copy-start.10
  87.4 40.3 %collective-permute-start.5 = (bf16[2,6,64,512]{3,2,1,0:T(8,128)(2,1)}, bf16[2,6,64,512]{3,2,1,0:T(8,128)(2,1)S(1)}, u32[]{:S(2)}, u32[]{:S(2)}) collective-permute-start(bf16[2,6,64,512]{3,2,1,0:T(8,128)(2,1)} %get-tuple-element.29), channel_id=1, source_target_pairs={{0,8},{8,16},{16,24},{24,0},{1,9},{9,17},{17,25},{25,1},{2,10},{10... | collective-permute-start | bytes 2359304 | tf_op jit(solution)/shard_map/ppermute | solution.py:228
  90.0 89.6 %collective-permute-start.24 = (bf16[2,8,3,48,512]{4,3,2,1,0:T(8,128)(2,1)}, bf16[2,8,3,48,512]{4,3,2,1,0:T(8,128)(2,1)}, u32[]{:S(2)}, u32[]{:S(2)}) collective-permute-start(bf16[2,8,3,48,512]{4,3,2,1,0:T(8,128)(2,1)} %bitcast.49), channel_id=1, source_target_pairs={{0,64},{64,0},{1,65},{65,1},{2,66},{66,2},{3,67},{67,3},{4,68},{68... | collective-permute-start | bytes 7077896 | tf_op jit(solution)/shard_map/ppermute | solution.py:18
  91.6 35.1 %collective-permute-start.2 = (bf16[2,6,24,512]{3,2,1,0:T(8,128)(2,1)}, bf16[2,6,24,512]{3,2,1,0:T(8,128)(2,1)}, u32[]{:S(2)}, u32[]{:S(2)}) collective-permute-start(bf16[2,6,24,512]{3,2,1,0:T(8,128)(2,1)} %get-tuple-element.36), channel_id=1, source_target_pairs={{0,8},{8,16},{16,24},{24,0},{1,9},{9,17},{17,25},{25,1},{2,10},{10... | collective-permute-start | bytes 884744 | tf_op jit(solution)/shard_map/ppermute | solution.py:228
  104.8 4.6 %copy-start = (bf16[4,4,2,6,64,512]{5,4,3,2,1,0:T(8,128)(2,1)S(1)}, bf16[4,4,2,6,64,512]{5,4,3,2,1,0:T(8,128)(2,1)}, u32[]{:S(2)}) copy-start(bf16[4,4,2,6,64,512]{5,4,3,2,1,0:T(8,128)(2,1)} %get-tuple-element.13) | copy-start | bytes 37748740
  109.4 19.1 %copy-start.9 = (bf16[2,6,24,512]{3,2,1,0:T(8,128)(2,1)S(1)}, bf16[2,6,24,512]{3,2,1,0:T(8,128)(2,1)}, u32[]{:S(2)}) copy-start(bf16[2,6,24,512]{3,2,1,0:T(8,128)(2,1)} %copy-done.8) | copy-start | bytes 884740
  109.4 19.1 %copy-start.11 = (bf16[2,6,24,512]{3,2,1,0:T(8,128)(2,1)S(1)}, bf16[2,6,24,512]{3,2,1,0:T(8,128)(2,1)}, u32[]{:S(2)}) copy-start(bf16[2,6,24,512]{3,2,1,0:T(8,128)(2,1)} %copy-done.10) | copy-start | bytes 884740
  126.8 0.9 copy-start.1
  127.7 0.9 copy-start.4
  128.5 1.1 copy-start.2
  129.7 1.1 copy-start.5
  144.2 4.4 %copy-start.7 = (f32[4,8,2,8,128]{4,3,2,1,0:T(8,128)}, f32[4,8,2,8,128]{4,3,2,1,0:T(8,128)S(1)}, u32[]{:S(2)}) copy-start(f32[4,8,2,8,128]{4,3,2,1,0:T(8,128)S(1)} %get-tuple-element.18) | copy-start | bytes 786436
  145.3 18.2 %collective-permute-start.8 = (f32[4,2,80,128]{3,2,1,0:T(8,128)}, f32[4,2,80,128]{3,2,1,0:T(8,128)}, u32[]{:S(2)}, u32[]{:S(2)}) collective-permute-start(f32[4,2,80,128]{3,2,1,0:T(8,128)} %get-tuple-element.30), channel_id=1, source_target_pairs={{0,8},{8,16},{16,24},{24,0},{1,9},{9,17},{17,25},{25,1},{2,10},{10... | collective-permute-start | bytes 983048 | tf_op jit(solution)/shard_map/ppermute | solution.py:228
  146.2 17.7 %collective-permute-start.9 = (f32[4,2,80,128]{3,2,1,0:T(8,128)}, f32[4,2,80,128]{3,2,1,0:T(8,128)}, u32[]{:S(2)}, u32[]{:S(2)}) collective-permute-start(f32[4,2,80,128]{3,2,1,0:T(8,128)} %get-tuple-element.31), channel_id=1, source_target_pairs={{0,24},{8,0},{16,8},{24,16},{1,25},{9,1},{17,9},{25,17},{2,26},{10... | collective-permute-start | bytes 983048 | tf_op jit(solution)/shard_map/ppermute | solution.py:228
  148.6 17.1 %collective-permute-start.15 = (bf16[2,6,64,512]{3,2,1,0:T(8,128)(2,1)S(1)}, bf16[2,6,64,512]{3,2,1,0:T(8,128)(2,1)S(1)}, u32[]{:S(2)}, u32[]{:S(2)}) collective-permute-start(bf16[2,6,64,512]{3,2,1,0:T(8,128)(2,1)S(1)} %collective-permute-done.7.refs_9_), channel_id=1, source_target_pairs={{0,32},{32,0},{1,33},{33,1},{2,34},{34,2},{3,35},{35,3},{4,36},{36... | collective-permute-start | bytes 2359304 | tf_op jit(solution)/shard_map/ppermute | solution.py:18
  149.2 14.8 %collective-permute-start.10 = (f32[4,2,80,128]{3,2,1,0:T(8,128)}, f32[4,2,80,128]{3,2,1,0:T(8,128)S(1)}, u32[]{:S(2)}, u32[]{:S(2)}) collective-permute-start(f32[4,2,80,128]{3,2,1,0:T(8,128)} %get-tuple-element.32), channel_id=1, source_target_pairs={{0,16},{8,24},{16,0},{24,8},{1,17},{9,25},{17,1},{25,9},{2,18},{10... | collective-permute-start | bytes 983048 | tf_op jit(solution)/shard_map/ppermute | solution.py:228
  163.5 28.1 %collective-permute-start.25 = (bf16[1,8,3,48,512]{4,3,2,1,0:T(8,128)(2,1)}, bf16[1,8,3,48,512]{4,3,2,1,0:T(8,128)(2,1)}, u32[]{:S(2)}, u32[]{:S(2)}) collective-permute-start(bf16[1,8,3,48,512]{4,3,2,1,0:T(8,128)(2,1)} %bitcast.190), channel_id=1, source_target_pairs={{0,64},{64,0},{1,65},{65,1},{2,66},{66,2},{3,67},{67,3},{4,68},{68... | collective-permute-start | bytes 3538952 | tf_op jit(solution)/shard_map/ppermute | solution.py:18
  164.0 4.2 %collective-permute-start.20 = (bf16[2,6,64,512]{3,2,1,0:T(8,128)(2,1)}, bf16[2,6,64,512]{3,2,1,0:T(8,128)(2,1)}, u32[]{:S(2)}, u32[]{:S(2)}) collective-permute-start(bf16[2,6,64,512]{3,2,1,0:T(8,128)(2,1)} %copy-done.1), channel_id=1, source_target_pairs={{0,32},{32,0},{1,33},{33,1},{2,34},{34,2},{3,35},{35,3},{4,36},{36... | collective-permute-start | bytes 2359304 | tf_op jit(solution)/shard_map/ppermute | solution.py:18
  164.0 15.0 %collective-permute-start.18 = (bf16[2,6,64,512]{3,2,1,0:T(8,128)(2,1)}, bf16[2,6,64,512]{3,2,1,0:T(8,128)(2,1)}, u32[]{:S(2)}, u32[]{:S(2)}) collective-permute-start(bf16[2,6,64,512]{3,2,1,0:T(8,128)(2,1)} %copy-done.4), channel_id=1, source_target_pairs={{0,32},{32,0},{1,33},{33,1},{2,34},{34,2},{3,35},{35,3},{4,36},{36... | collective-permute-start | bytes 2359304 | tf_op jit(solution)/shard_map/ppermute | solution.py:18
  165.7 0.7 copy-start.12
  166.4 5.7 %collective-permute-start.11 = (f32[2,80,128]{2,1,0:T(8,128)S(1)}, f32[2,80,128]{2,1,0:T(8,128)S(1)}, u32[]{:S(2)}, u32[]{:S(2)}) collective-permute-start(f32[2,80,128]{2,1,0:T(8,128)S(1)} %get-tuple-element.40), channel_id=1, source_target_pairs={{0,2},{2,4},{4,6},{6,0},{1,3},{3,5},{5,7},{7,1},{8,10},{10,12},{12... | collective-permute-start | bytes 245768 | tf_op jit(solution)/shard_map/ppermute | solution.py:246
  168.1 6.6 %collective-permute-start.13 = (f32[2,80,128]{2,1,0:T(8,128)S(1)}, f32[2,80,128]{2,1,0:T(8,128)S(1)}, u32[]{:S(2)}, u32[]{:S(2)}) collective-permute-start(f32[2,80,128]{2,1,0:T(8,128)S(1)} %get-tuple-element.41), channel_id=1, source_target_pairs={{0,4},{2,6},{4,0},{6,2},{1,5},{3,7},{5,1},{7,3},{8,12},{10,14},{12... | collective-permute-start | bytes 245768 | tf_op jit(solution)/shard_map/ppermute | solution.py:246
  172.1 4.4 %collective-permute-start.12 = (f32[2,80,128]{2,1,0:T(8,128)S(1)}, f32[2,80,128]{2,1,0:T(8,128)S(1)}, u32[]{:S(2)}, u32[]{:S(2)}) collective-permute-start(f32[2,80,128]{2,1,0:T(8,128)S(1)} %get-tuple-element.42), channel_id=1, source_target_pairs={{0,6},{2,0},{4,2},{6,4},{1,7},{3,1},{5,3},{7,5},{8,14},{10,8},{12,... | collective-permute-start | bytes 245768 | tf_op jit(solution)/shard_map/ppermute | solution.py:246
  174.7 23.0 %collective-permute-start.16 = (bf16[2,3,48,512]{3,2,1,0:T(8,128)(2,1)}, bf16[2,3,48,512]{3,2,1,0:T(8,128)(2,1)S(1)}, u32[]{:S(2)}, u32[]{:S(2)}) collective-permute-start(bf16[2,3,48,512]{3,2,1,0:T(8,128)(2,1)} %bitcast.181), channel_id=1, source_target_pairs={{0,64},{64,0},{1,65},{65,1},{2,66},{66,2},{3,67},{67,3},{4,68},{68... | collective-permute-start | bytes 884744 | tf_op jit(solution)/shard_map/ppermute | solution.py:18
  176.5 26.4 %collective-permute-start.19 = (bf16[2,3,48,512]{3,2,1,0:T(8,128)(2,1)}, bf16[2,3,48,512]{3,2,1,0:T(8,128)(2,1)S(1)}, u32[]{:S(2)}, u32[]{:S(2)}) collective-permute-start(bf16[2,3,48,512]{3,2,1,0:T(8,128)(2,1)} %bitcast.163), channel_id=1, source_target_pairs={{0,64},{64,0},{1,65},{65,1},{2,66},{66,2},{3,67},{67,3},{4,68},{68... | collective-permute-start | bytes 884744 | tf_op jit(solution)/shard_map/ppermute | solution.py:18
  179.0 33.3 %collective-permute-start.14 = (bf16[2,3,48,512]{3,2,1,0:T(8,128)(2,1)}, bf16[2,3,48,512]{3,2,1,0:T(8,128)(2,1)S(1)}, u32[]{:S(2)}, u32[]{:S(2)}) collective-permute-start(bf16[2,3,48,512]{3,2,1,0:T(8,128)(2,1)} %bitcast.161), channel_id=1, source_target_pairs={{0,64},{64,0},{1,65},{65,1},{2,66},{66,2},{3,67},{67,3},{4,68},{68... | collective-permute-start | bytes 884744 | tf_op jit(solution)/shard_map/ppermute | solution.py:18
  179.5 29.7 %collective-permute-start.17 = (bf16[2,3,48,512]{3,2,1,0:T(8,128)(2,1)}, bf16[2,3,48,512]{3,2,1,0:T(8,128)(2,1)S(1)}, u32[]{:S(2)}, u32[]{:S(2)}) collective-permute-start(bf16[2,3,48,512]{3,2,1,0:T(8,128)(2,1)} %bitcast.21.refs_4_), channel_id=1, source_target_pairs={{0,64},{64,0},{1,65},{65,1},{2,66},{66,2},{3,67},{67,3},{4,68},{68... | collective-permute-start | bytes 884744 | tf_op jit(solution)/shard_map/ppermute | solution.py:18
  196.0 13.2 %copy-start.3 = (bf16[2,6,64,512]{3,2,1,0:T(8,128)(2,1)S(1)}, bf16[2,6,64,512]{3,2,1,0:T(8,128)(2,1)}, u32[]{:S(2)}) copy-start(bf16[2,6,64,512]{3,2,1,0:T(8,128)(2,1)} %copy-done.1) | copy-start | bytes 2359300
  196.0 13.2 %copy-start.6 = (bf16[2,6,64,512]{3,2,1,0:T(8,128)(2,1)S(1)}, bf16[2,6,64,512]{3,2,1,0:T(8,128)(2,1)}, u32[]{:S(2)}) copy-start(bf16[2,6,64,512]{3,2,1,0:T(8,128)(2,1)} %copy-done.4) | copy-start | bytes 2359300
  196.1 21.8 %collective-permute-start.26 = (f32[3,2,48,128]{3,2,1,0:T(8,128)S(1)}, f32[3,2,48,128]{3,2,1,0:T(8,128)S(1)}, u32[]{:S(2)}, u32[]{:S(2)}) collective-permute-start(f32[3,2,48,128]{3,2,1,0:T(8,128)S(1)} %get-tuple-element.37), channel_id=1, source_target_pairs={{0,8},{8,16},{16,24},{24,0},{1,9},{9,17},{17,25},{25,1},{2,10},{10... | collective-permute-start | bytes 442376 | tf_op jit(solution)/shard_map/ppermute | solution.py:228
  197.8 20.8 %collective-permute-start.27 = (f32[3,2,48,128]{3,2,1,0:T(8,128)S(1)}, f32[3,2,48,128]{3,2,1,0:T(8,128)S(1)}, u32[]{:S(2)}, u32[]{:S(2)}) collective-permute-start(f32[3,2,48,128]{3,2,1,0:T(8,128)S(1)} %get-tuple-element.38), channel_id=1, source_target_pairs={{0,24},{8,0},{16,8},{24,16},{1,25},{9,1},{17,9},{25,17},{2,26},{10... | collective-permute-start | bytes 442376 | tf_op jit(solution)/shard_map/ppermute | solution.py:228
  202.9 16.3 %collective-permute-start.28 = (f32[3,2,48,128]{3,2,1,0:T(8,128)S(1)}, f32[3,2,48,128]{3,2,1,0:T(8,128)S(1)}, u32[]{:S(2)}, u32[]{:S(2)}) collective-permute-start(f32[3,2,48,128]{3,2,1,0:T(8,128)S(1)} %get-tuple-element.39), channel_id=1, source_target_pairs={{0,16},{8,24},{16,0},{24,8},{1,17},{9,25},{17,1},{25,9},{2,18},{10... | collective-permute-start | bytes 442376 | tf_op jit(solution)/shard_map/ppermute | solution.py:228
  209.3 13.5 %collective-permute-start.34 = (bf16[32,512]{1,0:T(8,128)(2,1)S(1)}, bf16[32,512]{1,0:T(8,128)(2,1)S(1)}, u32[]{:S(2)}, u32[]{:S(2)}) collective-permute-start(bf16[32,512]{1,0:T(8,128)(2,1)S(1)} %fusion.32), channel_id=1, source_target_pairs={{0,32},{32,0},{1,33},{33,1},{2,34},{34,2},{3,35},{35,3},{4,36},{36... | collective-permute-start | bytes 98312 | tf_op jit(solution)/shard_map/ppermute | solution.py:18
  213.2 12.1 %collective-permute-start.22 = (f32[2,48,128]{2,1,0:T(8,128)S(1)}, f32[2,48,128]{2,1,0:T(8,128)S(1)}, u32[]{:S(2)}, u32[]{:S(2)}) collective-permute-start(f32[2,48,128]{2,1,0:T(8,128)S(1)} %bitcast.165), channel_id=1, source_target_pairs={{0,6},{1,7},{8,14},{9,15},{16,22},{17,23},{24,30},{25,31},{32,38},... | collective-permute-start | bytes 147464 | tf_op jit(solution)/shard_map/ppermute | solution.py:246
  217.9 8.7 %collective-permute-start.23 = (f32[2,48,128]{2,1,0:T(8,128)S(1)}, f32[2,48,128]{2,1,0:T(8,128)S(1)}, u32[]{:S(2)}, u32[]{:S(2)}) collective-permute-start(f32[2,48,128]{2,1,0:T(8,128)S(1)} %bitcast.166), channel_id=1, source_target_pairs={{2,6},{3,7},{10,14},{11,15},{18,22},{19,23},{26,30},{27,31},{34,38... | collective-permute-start | bytes 147464 | tf_op jit(solution)/shard_map/ppermute | solution.py:246
  218.6 8.0 %collective-permute-start.21 = (f32[2,48,128]{2,1,0:T(8,128)S(1)}, f32[2,48,128]{2,1,0:T(8,128)S(1)}, u32[]{:S(2)}, u32[]{:S(2)}) collective-permute-start(f32[2,48,128]{2,1,0:T(8,128)S(1)} %bitcast.167), channel_id=1, source_target_pairs={{4,6},{5,7},{12,14},{13,15},{20,22},{21,23},{28,30},{29,31},{36,38... | collective-permute-start | bytes 147464 | tf_op jit(solution)/shard_map/ppermute | solution.py:246
  219.4 7.3 %collective-permute-start.29 = (f32[2,48,128]{2,1,0:T(8,128)S(1)}, f32[2,48,128]{2,1,0:T(8,128)S(1)}, u32[]{:S(2)}, u32[]{:S(2)}) collective-permute-start(f32[2,48,128]{2,1,0:T(8,128)S(1)} %get-tuple-element.43), channel_id=1, source_target_pairs={{0,2},{2,4},{6,0},{1,3},{3,5},{7,1},{8,10},{10,12},{14,8},{9,11},{... | collective-permute-start | bytes 147464 | tf_op jit(solution)/shard_map/ppermute | solution.py:246
  222.8 7.5 %collective-permute-start.31 = (f32[2,48,128]{2,1,0:T(8,128)S(1)}, f32[2,48,128]{2,1,0:T(8,128)S(1)}, u32[]{:S(2)}, u32[]{:S(2)}) collective-permute-start(f32[2,48,128]{2,1,0:T(8,128)S(1)} %get-tuple-element.44), channel_id=1, source_target_pairs={{0,4},{4,0},{6,2},{1,5},{5,1},{7,3},{8,12},{12,8},{14,10},{9,13},{... | collective-permute-start | bytes 147464 | tf_op jit(solution)/shard_map/ppermute | solution.py:246
  225.3 6.0 %collective-permute-start.30 = (f32[2,48,128]{2,1,0:T(8,128)S(1)}, f32[2,48,128]{2,1,0:T(8,128)S(1)}, u32[]{:S(2)}, u32[]{:S(2)}) collective-permute-start(f32[2,48,128]{2,1,0:T(8,128)S(1)} %get-tuple-element.45), channel_id=1, source_target_pairs={{2,0},{4,2},{6,4},{3,1},{5,3},{7,5},{10,8},{12,10},{14,12},{11,9},... | collective-permute-start | bytes 147464 | tf_op jit(solution)/shard_map/ppermute | solution.py:246
  231.4 5.8 %collective-permute-start.32 = (f32[128,128]{1,0:T(8,128)S(1)}, f32[128,128]{1,0:T(8,128)S(1)}, u32[]{:S(2)}, u32[]{:S(2)}) collective-permute-start(f32[128,128]{1,0:T(8,128)S(1)} %fusion.25), channel_id=1, source_target_pairs={{0,1},{1,0},{2,3},{3,2},{4,5},{5,4},{6,7},{7,6},{8,9},{9,8},{10,11... | collective-permute-start | bytes 196616 | tf_op jit(solution)/shard_map/ppermute | solution.py:18
  237.3 1.3 collective-permute-start.33

commit v6 on v5

--- a/solution.py
+++ b/solution.py
@@ -68,33 +68,56 @@
     return block.reshape(x, z * yh, comps // 2, 2 * n, sites)
 
 
-def front_kernel(owned, at, sols, vecs, out, lines, slab, sems):
+def hold_kernel(*refs):
+    pass
+
+
+def hold(value, *after):
+    return pl.pallas_call(
+        hold_kernel,
+        in_specs=[ANY] * (1 + len(after)),
+        out_specs=ANY,
+        out_shape=jax.ShapeDtypeStruct(value.shape, value.dtype),
+        input_output_aliases={0: 0},
+        cost_estimate=HINT,
+        name="hold",
+    )(value, *after)
+
+
+def front_kernel(owned, at, sols, vecs, out, lines, slab, held, sems):
     count, comps, rows, _ = lines.shape
-    whole = pltpu.make_async_copy(
-        sols.at[pl.ds(0, RAW * comps)], out.at[pl.ds(0, RAW * comps)], sems.at[count]
-    )
-    whole.start()
     group, time = at[0], at[1]
-    copies = []
-    for s in range(count):
-        copies.append(
-            pltpu.make_async_copy(
-                vecs.at[at[2 + s] % owned, :, pl.ds(pl.multiple_of(time // rows * rows, rows), rows)],
-                lines.at[s],
-                sems.at[s],
-            )
+    span = held.shape[0] // 4
+    part = lambda ref, i: ref.at[pl.ds(i * span, span)]
+    into = [
+        pltpu.make_async_copy(part(sols, i), part(held, i), sems.at[i]) for i in range(4)
+    ]
+    outof = [
+        pltpu.make_async_copy(part(held, i), part(out, i), sems.at[4 + i]) for i in range(4)
+    ]
+    first = pl.multiple_of(time // rows * rows, rows)
+    picks = [
+        pltpu.make_async_copy(
+            vecs.at[at[2 + s] % owned, :, pl.ds(first, rows)], lines.at[s], sems.at[8 + s]
         )
-        copies[s].start()
+        for s in range(count)
+    ]
+    last = pltpu.make_async_copy(slab, out.at[held.shape[0]], sems.at[8 + count])
+    for copy in into + picks:
+        copy.start()
+    for i in range(4):
+        into[i].wait()
+        outof[i].start()
     row = lax.broadcasted_iota(jnp.int32, lines.shape[1:], 1)
     for s in range(count):
-        copies[s].wait()
+        picks[s].wait()
         here = jnp.where(at[2 + s] // owned == group, time % rows, -1)
         kept = jnp.sum(jnp.where(row == here, lines[s].astype(jnp.float32), 0.0), axis=1)
         slab[s] = jnp.concatenate([kept, jnp.zeros_like(kept[:2])], axis=0).astype(slab.dtype)
-    last = pltpu.make_async_copy(slab, out.at[RAW * comps], sems.at[count + 1])
     last.start()
+    for i in range(4):
+        outof[i].wait()
     last.wait()
-    whole.wait()
 
 
 def front(sols, vecs, source_index, source_time, group):
@@ -109,7 +132,8 @@
         scratch_shapes=[
             pltpu.VMEM((count, comps, 16, sites), sols.dtype),
             pltpu.VMEM((count, times // count, sites), sols.dtype),
-            pltpu.SemaphoreType.DMA((count + 2,)),
+            pltpu.VMEM((RAW * comps, count, times // count, sites), sols.dtype),
+            pltpu.SemaphoreType.DMA((9 + count,)),
         ],
         compiler_params=pltpu.CompilerParams(vmem_limit_bytes=56 * 2**20),
         cost_estimate=HINT,
@@ -267,17 +291,31 @@
     other = swap(vecs, "c")
     sent = [(RAW, count, x, nx, 0, 2) for x, nx in ((0, 2), (2, 1), (3, 1))]
     mine, *send = by_time(sols, ((0, count, 0, 4, 0, 2), *sent), first_part)
-    got = [swap(rows_of(part), "yl") for part in send[:2]]
-    shared = [part.reshape(2, comps // 2, -1, sites) for part in share_z(send[2][0])]
-    got_last = [swap(part, "yl") for part in shared]
+    send = [rows_of(part) for part in send]
+    shared = share_z(send[2].reshape(4, 2, comps // 2, -1, sites))
 
     whole = (0, owned, 0, 4, 0, 2)
     late = (0, owned, 3, 1, 0, 2)
     own, own_late = by_time(vecs, (whole, late))
     other, other_late = by_time(other, (whole, late))
     own, other = rows_of(own), rows_of(other)
+    got = [swap(send[0], "yl"), swap(hold(send[1], raw, own, other), "yl")]
     lines = raw[RAW * comps] + first_part[RAW * comps]
     raw = rows_of(by_time(raw, ((0, RAW, 0, 4, 0, 2),), other)[0])
+
+    def rows(part):
+        x, inner, _, n, lanes = part.shape
+        return part.reshape(x, 4, inner // 4, 2 * n, lanes)
+
+    def against(part, x, y, step, *after):
+        return rows(project([part], own, other, x, y, step, *after)[0])
+
+    parts = project([rows_of(mine), raw], own, other, 0, 0, 8)
+    first_z = sum_z(jnp.concatenate([rows(p) for p in parts], axis=3))
+    first = sum_x(first_z, 0, 4)
+    most = swap(hold(jnp.concatenate(shared[:3]), got[0], first), "yl")
+    rest = swap(hold(shared[3], got[1]), "yl")
+    got_last = [most[:2], most[2:4], most[4:], rest]
 
     mine_z = share_z(own_late[0])
     theirs_z = [pick(other_late[0], lax.axis_index("z"))] + [swap(p, "c") for p in mine_z[1:]]
@@ -286,18 +324,8 @@
         for s, *pair in zip(got_last, mine_z, theirs_z)
     ]
 
-    def rows(part):
-        x, inner, _, n, lanes = part.shape
-        return part.reshape(x, 4, inner // 4, 2 * n, lanes)
-
-    def against(part, x, y, step, *after):
-        return rows(project([part], own, other, x, y, step, *after)[0])
-
-    parts = project([rows_of(mine), raw], own, other, 0, 0, 8, *shared[1:], *mine_z[1:])
-    first_z = sum_z(jnp.concatenate([rows(p) for p in parts], axis=3))
-    first = sum_x(first_z, 0, 4)
-    mid = [against(got[0], 0, 0, 8, first, *theirs_z[1:])]
-    mid.append(against(got[1], 2, 0, 4, mid[0]))
+    mid = [against(got[0], 0, 0, 8, first)]
+    mid.append(against(got[1], 2, 0, 4, mid[0], *theirs_z[1:]))
     mid = sum_x(sum_z(jnp.concatenate(mid, axis=0)), 0, 3)
     last = project_pieces(pieces[3:], project_pieces(pieces[:3]))
     last = sum_x(last.reshape(1, 2, -1, 2 * owned), 3, 1)

time: 242 us -> 205 us (0.85)
  Pallas kernels: 111 us -> 65.8 us
  waiting for transfers between devices: 49.9 us -> 54.9 us
    pallas_call x1, Pallas kernels: 49.5 us -> 2.96 us  [front(): pl.pallas_call(functools.partial(front_kernel, owned), in_specs=[pl.Block...]
    ppermute x12, waiting for transfers between devices: 27.8 us -> 42.2 us  [share_z(): lax.ppermute(pick(slabs, (me + k) % 4), 'z', [(i, (i + k) % 4) for i in r...]
    ppermute x14 -> x12, waiting for transfers between devices: 15.9 us -> 9.33 us  [swap(): return lax.ppermute(value, axis, SWAP)]
    ppermute x12, starting transfers between devices: 19.2 us -> 23.2 us  [share_z(): lax.ppermute(pick(slabs, (me + k) % 4), 'z', [(i, (i + k) % 4) for i in r...]
    dynamic_slice x3 -> x2, local copies, waits for them, and re-layouts: 6.68 us -> 2.86 us  [pick(): return lax.dynamic_index_in_dim(value, index, 0, keepdims=False)]
    ppermute x14 -> x12, starting transfers between devices: 12.8 us -> 9.27 us  [swap(): return lax.ppermute(value, axis, SWAP)]
    ppermute x9, waiting for transfers between devices: 6.23 us -> 3.38 us  [sum_x(): total = total + lax.ppermute(send, 'x', pairs)]
    unnamed x30 -> x38, local copies, waits for them, and re-layouts: 10.8 us -> 11 us
  transfers between devices with their start and end apart: 35 -> 33, of which waited for: 14 -> 11; matrix products, arithmetic and copies ran while one was open for 6% -> 7% of each run, Pallas kernels for 46% -> 33%
where the time goes in v6:
time: 205 us; the launch traced here: 201 us
  Pallas kernels  65.8 us (32%)
  waiting for transfers between devices  54.9 us (27%)
  starting transfers between devices  52 us (25%)
  local copies, waits for them, and re-layouts  17.8 us (9%)
  other arithmetic  8.76 us (4%)
    ppermute x12, waiting for transfers between devices, share_z(): lax.ppermute(pick(slabs, (me + k) % 4), 'z', [(i, (i + k) % 4) for i in r...  42.2 us
    pallas_call x4, Pallas kernels, by_time(): pl.pallas_call(functools.partial(by_time_kernel, cuts), grid=(4,), in_spe...  32.3 us
    pallas_call x3, Pallas kernels, project(): pl.pallas_call(functools.partial(dot_kernel, len(cols)), grid=(size, inne...  25.2 us
    ppermute x12, starting transfers between devices, share_z(): lax.ppermute(pick(slabs, (me + k) % 4), 'z', [(i, (i + k) % 4) for i in r...  23.2 us
    ppermute x9, starting transfers between devices, sum_x(): total = total + lax.ppermute(send, 'x', pairs)  19.6 us
    unnamed x38, local copies, waits for them, and re-layouts  11 us
    ppermute x12, waiting for transfers between devices, swap(): return lax.ppermute(value, axis, SWAP)  9.33 us
    ppermute x12, starting transfers between devices, swap(): return lax.ppermute(value, axis, SWAP)  9.27 us
  transfers between devices with their start and end apart: 33, of which 11 were waited for; matrix products, arithmetic and copies ran while one was open for 7% of the time, Pallas kernels for 33%

profile of v6, /device:TPU:0, one launch (start us, length us, event | category | flops | bytes accessed | tf_op | source)
XLA Modules:
  0.0 201.0 jit_solution(2190413995365391255)
XLA Ops:
  1.4 1.2 pad_add_fusion.at
  2.6 3.0 %front.1 = bf16[49,4,8,512]{3,2,1,0:T(8,128)(2,1)} custom-call(s32[6]{0:T(128)} %pad_add_fusion.at, bf16[192,4,8,512]{3,2,1,0:T(8,128)(2,1)} %bitcast.167, bf16[64,6,32,512]{3,2,1,0:T(8,128)(2,1)} %bitcast.165), custom_call_target="tpu_custom_call" | custom-call | flops 1000 | bytes 1000 | tf_op jit(solution)/shard_map/front/pallas_call | solution.py:127
  5.6 1.7 collective-permute-start
  7.3 7.6 %by_time.4 = (bf16[4,4,2,6,32,512]{5,4,3,2,1,0:T(8,128)(2,1)}, bf16[2,4,2,6,24,512]{5,4,3,2,1,0:T(8,128)(2,1)}, bf16[1,4,2,6,24,512]{5,4,3,2,1,0:T(8,128)(2,1)}, bf16[1,4,2,6,24,512]{5,4,3,2,1,0:T(8,128)(2,1)}) custom-call(bf16[32,6,32,512]{3,2,1,0:T(8,128)(2,1)} %bitcast.168, bf16[49,32,512]{2,1,0:T(8,128)(2,1)} %bitcast.170), custom_call_target="tpu_custom_call" | custom-call | flops 1000 | bytes 1000 | tf_op jit(solution)/shard_map/by_time/pallas_call | solution.py:48
  15.0 0.4 collective-permute-start.15
  15.3 11.1 %by_time.7 = (bf16[4,4,2,6,64,512]{5,4,3,2,1,0:T(8,128)(2,1)}, bf16[1,4,2,6,64,512]{5,4,3,2,1,0:T(8,128)(2,1)}) custom-call(bf16[64,6,32,512]{3,2,1,0:T(8,128)(2,1)} %bitcast.166), custom_call_target="tpu_custom_call" | custom-call | flops 1000 | bytes 1000 | tf_op jit(solution)/shard_map/by_time/pallas_call | solution.py:48
  26.4 11.2 %by_time.5 = (bf16[4,4,2,6,64,512]{5,4,3,2,1,0:T(8,128)(2,1)}, bf16[1,4,2,6,64,512]{5,4,3,2,1,0:T(8,128)(2,1)}) custom-call(bf16[64,6,32,512]{3,2,1,0:T(8,128)(2,1)} %collective-permute-done.1.block), custom_call_target="tpu_custom_call" | custom-call | flops 1000 | bytes 1000 | tf_op jit(solution)/shard_map/by_time/pallas_call | solution.py:48
  37.6 6.3 %collective-permute-done.block.refs_1_ = bf16[49,32,512]{2,1,0:T(8,128)(2,1)} collective-permute-done((bf16[49,32,512]{2,1,0:T(8,128)(2,1)}, bf16[49,32,512]{2,1,0:T(8,128)(2,1)}, u32[]{:S(2)}, u32[]{:S(2)}) %collective-permute-start) | collective-permute-done | bytes 1605664 | tf_op jit(solution)/shard_map/ppermute | solution.py:18
  43.9 4.6 %copy-done = bf16[4,4,2,6,64,512]{5,4,3,2,1,0:T(8,128)(2,1)S(1)} copy-done((bf16[4,4,2,6,64,512]{5,4,3,2,1,0:T(8,128)(2,1)S(1)}, bf16[4,4,2,6,64,512]{5,4,3,2,1,0:T(8,128)(2,1)}, u32[]{:S(2)}) %copy-start) | copy-done | bytes 12582936
  48.5 2.4 %by_time.6 = bf16[4,4,2,6,8,512]{5,4,3,2,1,0:T(8,128)(2,1)S(1)} custom-call(bf16[49,32,512]{2,1,0:T(8,128)(2,1)} %collective-permute-done.block.refs_1_, bf16[4,8,3,128,512]{4,3,2,1,0:T(8,128)(2,1)S(1)} %bitcast.144), custom_call_target="tpu_custom_call" | custom-call | flops 1000 | bytes 1000 | tf_op jit(solution)/shard_map/by_time/pallas_call | solution.py:48
  50.9 13.4 %project.3 = (f32[4,8,2,32,128]{4,3,2,1,0:T(8,128)S(1)}, f32[4,8,2,8,128]{4,3,2,1,0:T(8,128)S(1)}) custom-call(bf16[4,8,3,64,512]{4,3,2,1,0:T(8,128)(2,1)} %bitcast.171, bf16[4,8,3,16,512]{4,3,2,1,0:T(8,128)(2,1)S(1)} %bitcast.148, bf16[4,8,3,128,512]{4,3,2,1,0:T(8,128)(2,1)} %bitcast.160, bf16[4,8,3,128,512]{4,3,2,1,0:T(8,128)(2,1)} %bitcast.140), custom_call_target="tpu_custom_call" | custom-call | flops 1000 | bytes 1000 | tf_op jit(solution)/shard_map/project/pallas_call | solution.py:233
  64.4 2.1 %collective-permute-start.2 = (f32[4,2,80,128]{3,2,1,0:T(8,128)S(1)}, f32[4,2,80,128]{3,2,1,0:T(8,128)S(1)}, u32[]{:S(2)}, u32[]{:S(2)}) collective-permute-start(f32[4,2,80,128]{3,2,1,0:T(8,128)S(1)} %get-tuple-element.30), channel_id=1, source_target_pairs={{0,8},{8,16},{16,24},{24,0},{1,9},{9,17},{17,25},{25,1},{2,10},{10... | collective-permute-start | bytes 983048 | tf_op jit(solution)/shard_map/ppermute | solution.py:252
  66.5 0.9 dynamic-slice_bitcast_fusion.5
  67.4 3.7 %collective-permute-start.14 = (bf16[2,3,48,512]{3,2,1,0:T(8,128)(2,1)S(1)}, bf16[2,3,48,512]{3,2,1,0:T(8,128)(2,1)S(1)}, u32[]{:S(2)}, u32[]{:S(2)}) collective-permute-start(bf16[2,3,48,512]{3,2,1,0:T(8,128)(2,1)S(1)} %get-tuple-element.34), channel_id=1, source_target_pairs={{0,24},{8,0},{16,8},{24,16},{1,25},{9,1},{17,9},{25,17},{2,26},{10... | collective-permute-start | bytes 884744 | tf_op jit(solution)/shard_map/ppermute | solution.py:252
  71.1 3.2 %collective-permute-start.3 = (f32[4,2,80,128]{3,2,1,0:T(8,128)S(1)}, f32[4,2,80,128]{3,2,1,0:T(8,128)S(1)}, u32[]{:S(2)}, u32[]{:S(2)}) collective-permute-start(f32[4,2,80,128]{3,2,1,0:T(8,128)S(1)} %get-tuple-element.31), channel_id=1, source_target_pairs={{0,24},{8,0},{16,8},{24,16},{1,25},{9,1},{17,9},{25,17},{2,26},{10... | collective-permute-start | bytes 983048 | tf_op jit(solution)/shard_map/ppermute | solution.py:252
  74.3 1.7 constant_dynamic-slice_fusion.2
  76.0 2.5 %collective-permute-done.14 = bf16[2,3,48,512]{3,2,1,0:T(8,128)(2,1)S(1)} collective-permute-done((bf16[2,3,48,512]{3,2,1,0:T(8,128)(2,1)S(1)}, bf16[2,3,48,512]{3,2,1,0:T(8,128)(2,1)S(1)}, u32[]{:S(2)}, u32[]{:S(2)}) %collective-permute-start.14) | collective-permute-done | bytes 294944 | tf_op jit(solution)/shard_map/ppermute | solution.py:252
  78.6 3.7 %collective-permute-start.19 = (bf16[2,6,64,512]{3,2,1,0:T(8,128)(2,1)}, bf16[2,6,64,512]{3,2,1,0:T(8,128)(2,1)}, u32[]{:S(2)}, u32[]{:S(2)}) collective-permute-start(bf16[2,6,64,512]{3,2,1,0:T(8,128)(2,1)} %get-tuple-element.27), channel_id=1, source_target_pairs={{0,24},{8,0},{16,8},{24,16},{1,25},{9,1},{17,9},{25,17},{2,26},{10... | collective-permute-start | bytes 2359304 | tf_op jit(solution)/shard_map/ppermute | solution.py:252
  82.3 0.8 copy-done.12
  83.1 3.0 %collective-permute-start.11 = (bf16[2,6,64,512]{3,2,1,0:T(8,128)(2,1)}, bf16[2,6,64,512]{3,2,1,0:T(8,128)(2,1)}, u32[]{:S(2)}, u32[]{:S(2)}) collective-permute-start(bf16[2,6,64,512]{3,2,1,0:T(8,128)(2,1)} %get-tuple-element.29), channel_id=1, source_target_pairs={{0,16},{8,24},{16,0},{24,8},{1,17},{9,25},{17,1},{25,9},{2,18},{10... | collective-permute-start | bytes 2359304 | tf_op jit(solution)/shard_map/ppermute | solution.py:252
  86.2 1.8 collective-permute-start.4
  88.0 0.6 gather_fusion
  88.7 36.8 %collective-permute-done.4 = f32[4,2,80,128]{3,2,1,0:T(8,128)} collective-permute-done((f32[4,2,80,128]{3,2,1,0:T(8,128)S(1)}, f32[4,2,80,128]{3,2,1,0:T(8,128)}, u32[]{:S(2)}, u32[]{:S(2)}) %collective-permute-start.4) | collective-permute-done | bytes 327712 | tf_op jit(solution)/shard_map/ppermute | solution.py:252
  125.5 1.6 collective-permute-start.9
  127.0 1.3 fusion.6
  128.4 0.8 copy-done.10
  129.1 0.7 dynamic-slice_bitcast_fusion.9
  129.8 1.5 collective-permute-start.5
  131.3 2.7 %collective-permute-start.7 = (f32[2,80,128]{2,1,0:T(8,128)}, f32[2,80,128]{2,1,0:T(8,128)}, u32[]{:S(2)}, u32[]{:S(2)}) collective-permute-start(f32[2,80,128]{2,1,0:T(8,128)} %get-tuple-element.44), channel_id=1, source_target_pairs={{0,4},{2,6},{4,0},{6,2},{1,5},{3,7},{5,1},{7,3},{8,12},{10,14},{12... | collective-permute-start | bytes 245768 | tf_op jit(solution)/shard_map/ppermute | solution.py:270
  134.1 1.4 collective-permute-start.6
  135.8 1.8 collective-permute-done.7
  137.7 1.2 collective-permute-done.6
  138.8 2.2 %pad_maximum_fusion.refs_0_ = bf16[6,3,48,512]{3,2,1,0:T(8,128)(2,1)} fusion(bf16[2,3,48,512]{3,2,1,0:T(8,128)(2,1)} %copy-done.14, bf16[2,3,48,512]{3,2,1,0:T(8,128)(2,1)} %copy-done.15, bf16[2,3,48,512]{3,2,1,0:T(8,128)(2,1)} %get-tuple-element.33), kind=kLoop, calls=%fused_computation.13 | loop fusion | flops 884736 | bytes 1769472 | tf_op jit(solution)/shard_map/concatenate | solution.py:316
  141.0 1.7 fusion.23.refs_2_.refs_3_
  142.7 1.4 copy-done.1
  144.1 0.4 collective-permute-start.16
  144.6 1.7 copy-done.2
  146.3 0.9 copy-done.6
  147.1 7.1 %project.4 = f32[2,8,2,24,128]{4,3,2,1,0:T(8,128)S(1)} custom-call(bf16[2,8,3,48,512]{4,3,2,1,0:T(8,128)(2,1)S(1)} %copy-done.2, bf16[4,8,3,128,512]{4,3,2,1,0:T(8,128)(2,1)} %bitcast.162, bf16[4,8,3,128,512]{4,3,2,1,0:T(8,128)(2,1)} %bitcast.142, f32[2,80,128]{2,1,0:T(8,128)S(1)} %copy-done.6), custom_call_target="tpu_custom_call" | custom-call | flops 1000 | bytes 1000 | tf_op jit(solution)/shard_map/project/pallas_call | solution.py:233
  154.2 0.9 collective-permute-start.8
  155.2 4.7 %project.5 = f32[1,8,2,24,128]{4,3,2,1,0:T(8,128)S(1)} custom-call(bf16[1,8,3,48,512]{4,3,2,1,0:T(8,128)(2,1)S(1)} %collective-permute-done.9.refs_1_.refs_0_, bf16[4,8,3,128,512]{4,3,2,1,0:T(8,128)(2,1)} %bitcast.163, bf16[4,8,3,128,512]{4,3,2,1,0:T(8,128)(2,1)} %bitcast.143, f32[2,4,2,48,128]{4,3,2,1,0:T(8,128)S(1)} %bitcast.145, ...), custom_call_target="tpu_custom_call" | custom-call | flops 1000 | bytes 1000 | tf_op jit(solution)/shard_map/project/pallas_call | solution.py:233
  159.9 0.8 collective-permute-start.24
  160.8 2.5 %collective-permute-start.25 = (f32[3,2,48,128]{3,2,1,0:T(8,128)S(1)}, f32[3,2,48,128]{3,2,1,0:T(8,128)S(1)}, u32[]{:S(2)}, u32[]{:S(2)}) collective-permute-start(f32[3,2,48,128]{3,2,1,0:T(8,128)S(1)} %get-tuple-element.41), channel_id=1, source_target_pairs={{0,24},{8,0},{16,8},{24,16},{1,25},{9,1},{17,9},{25,17},{2,26},{10... | collective-permute-start | bytes 442376 | tf_op jit(solution)/shard_map/ppermute | solution.py:252
  163.2 1.5 collective-permute-start.26
  164.7 0.8 fusion.32
  165.5 1.2 constant_dynamic-slice_fusion.1
  166.8 2.1 %collective-permute-done.24 = f32[3,2,48,128]{3,2,1,0:T(8,128)S(1)} collective-permute-done((f32[3,2,48,128]{3,2,1,0:T(8,128)S(1)}, f32[3,2,48,128]{3,2,1,0:T(8,128)S(1)}, u32[]{:S(2)}, u32[]{:S(2)}) %collective-permute-start.24) | collective-permute-done | bytes 147488 | tf_op jit(solution)/shard_map/ppermute | solution.py:252
  169.0 1.6 collective-permute-start.10
  170.6 0.7 collective-permute-done.26
  171.4 2.7 %collective-permute-start.27 = (f32[2,48,128]{2,1,0:T(8,128)S(1)}, f32[2,48,128]{2,1,0:T(8,128)S(1)}, u32[]{:S(2)}, u32[]{:S(2)}) collective-permute-start(f32[2,48,128]{2,1,0:T(8,128)S(1)} %get-tuple-element.46), channel_id=1, source_target_pairs={{0,2},{2,4},{6,0},{1,3},{3,5},{7,1},{8,10},{10,12},{14,8},{9,11},{... | collective-permute-start | bytes 147464 | tf_op jit(solution)/shard_map/ppermute | solution.py:270
  174.0 1.2 fusion.35
  175.3 3.3 %project_pieces.2.refs_3_ = f32[2,2,24,128]{3,2,1,0:T(8,128)S(1)} custom-call(bf16[2,3,48,512]{3,2,1,0:T(8,128)(2,1)S(1)} %get-tuple-element.39.refs_0_, bf16[2,3,128,512]{3,2,1,0:T(8,128)(2,1)S(1)} %bitcast.152, bf16[2,3,128,512]{3,2,1,0:T(8,128)(2,1)S(1)} %bitcast.151, bf16[2,3,48,512]{3,2,1,0:T(8,128)(2,1)S(1)} %get-tuple-element.38.refs_3_, ...), custom_call_target="tpu_custom_call" | custom-call | flops 1000 | bytes 1000 | tf_op jit(solution)/shard_map/project_pieces/pallas_call | solution.py:206
  178.6 2.4 %collective-permute-start.29 = (f32[2,48,128]{2,1,0:T(8,128)S(1)}, f32[2,48,128]{2,1,0:T(8,128)S(1)}, u32[]{:S(2)}, u32[]{:S(2)}) collective-permute-start(f32[2,48,128]{2,1,0:T(8,128)S(1)} %get-tuple-element.47), channel_id=1, source_target_pairs={{0,4},{4,0},{6,2},{1,5},{5,1},{7,3},{8,12},{12,8},{14,10},{9,13},{... | collective-permute-start | bytes 147464 | tf_op jit(solution)/shard_map/ppermute | solution.py:270
  181.0 1.3 collective-permute-start.28
  182.3 2.1 %project_pieces.3 = f32[2,2,24,128]{3,2,1,0:T(8,128)S(1)} custom-call(bf16[2,3,48,512]{3,2,1,0:T(8,128)(2,1)S(1)} %collective-permute-done.10.refs_0_, bf16[2,3,128,512]{3,2,1,0:T(8,128)(2,1)} %bitcast.34.refs_1_, bf16[2,3,128,512]{3,2,1,0:T(8,128)(2,1)} %bitcast.35.refs_2_, f32[2,2,24,128]{3,2,1,0:T(8,128)S(1)} %project_pieces.2.refs_3_), custom_call_target="tpu_custom_call" | custom-call | flops 1000 | bytes 1000 | tf_op jit(solution)/shard_map/project_pieces/pallas_call | solution.py:206
  184.4 6.2 %collective-permute-start.22 = (f32[2,48,128]{2,1,0:T(8,128)S(1)}, f32[2,48,128]{2,1,0:T(8,128)S(1)}, u32[]{:S(2)}, u32[]{:S(2)}) collective-permute-start(f32[2,48,128]{2,1,0:T(8,128)S(1)} %bitcast.157), channel_id=1, source_target_pairs={{0,6},{1,7},{8,14},{9,15},{16,22},{17,23},{24,30},{25,31},{32,38},... | collective-permute-start | bytes 147464 | tf_op jit(solution)/shard_map/ppermute | solution.py:270
  190.6 0.7 collective-permute-start.23
  191.3 0.7 collective-permute-start.21
  192.0 0.3 collective-permute-done.22
  192.4 3.3 %collective-permute-start.30 = (f32[128,128]{1,0:T(8,128)S(1)}, f32[128,128]{1,0:T(8,128)S(1)}, u32[]{:S(2)}, u32[]{:S(2)}) collective-permute-start(f32[128,128]{1,0:T(8,128)S(1)} %fusion.25), channel_id=1, source_target_pairs={{0,1},{1,0},{2,3},{3,2},{4,5},{5,4},{6,7},{7,6},{8,9},{9,8},{10,11... | collective-permute-start | bytes 196616 | tf_op jit(solution)/shard_map/ppermute | solution.py:18
  195.7 0.7 broadcast_select_fusion
  196.4 1.8 collective-permute-done.30
  198.4 1.2 collective-permute-done.31
  200.3 0.7 copy.15
  (92 shorter events, 2.0 us)
Async XLA Ops:
  0.6 25.8 %collective-permute-start.1 = (bf16[64,6,32,512]{3,2,1,0:T(8,128)(2,1)}, bf16[64,6,32,512]{3,2,1,0:T(8,128)(2,1)}, u32[]{:S(2)}, u32[]{:S(2)}) collective-permute-start(bf16[64,6,32,512]{3,2,1,0:T(8,128)(2,1)} %bitcast.164), channel_id=1, source_target_pairs={{0,32},{32,0},{1,33},{33,1},{2,34},{34,2},{3,35},{35,3},{4,36},{36... | collective-permute-start | bytes 37748744 | tf_op jit(solution)/shard_map/ppermute | solution.py:18
  5.6 38.3 %collective-permute-start = (bf16[49,32,512]{2,1,0:T(8,128)(2,1)}, bf16[49,32,512]{2,1,0:T(8,128)(2,1)}, u32[]{:S(2)}, u32[]{:S(2)}) collective-permute-start(bf16[49,32,512]{2,1,0:T(8,128)(2,1)} %bitcast.169), channel_id=1, source_target_pairs={{0,64},{64,0},{1,65},{65,1},{2,66},{66,2},{3,67},{67,3},{4,68},{68... | collective-permute-start | bytes 4816904 | tf_op jit(solution)/shard_map/ppermute | solution.py:18
  15.0 127.7 %collective-permute-start.15 = (bf16[2,8,3,48,512]{4,3,2,1,0:T(8,128)(2,1)}, bf16[2,8,3,48,512]{4,3,2,1,0:T(8,128)(2,1)S(1)}, u32[]{:S(2)}, u32[]{:S(2)}) collective-permute-start(bf16[2,8,3,48,512]{4,3,2,1,0:T(8,128)(2,1)} %bitcast.184), channel_id=1, source_target_pairs={{0,64},{64,0},{1,65},{65,1},{2,66},{66,2},{3,67},{67,3},{4,68},{68... | collective-permute-start | bytes 7077896 | tf_op jit(solution)/shard_map/ppermute | solution.py:18
  43.9 4.6 %copy-start = (bf16[4,4,2,6,64,512]{5,4,3,2,1,0:T(8,128)(2,1)S(1)}, bf16[4,4,2,6,64,512]{5,4,3,2,1,0:T(8,128)(2,1)}, u32[]{:S(2)}) copy-start(bf16[4,4,2,6,64,512]{5,4,3,2,1,0:T(8,128)(2,1)} %get-tuple-element.13) | copy-start | bytes 37748740
  64.3 3.1 %copy-start.4 = (f32[4,8,2,32,128]{4,3,2,1,0:T(8,128)}, f32[4,8,2,32,128]{4,3,2,1,0:T(8,128)S(1)}, u32[]{:S(2)}) copy-start(f32[4,8,2,32,128]{4,3,2,1,0:T(8,128)S(1)} %get-tuple-element.15) | copy-start | bytes 3145732
  64.3 3.1 %copy-start.8 = (f32[4,8,2,8,128]{4,3,2,1,0:T(8,128)}, f32[4,8,2,8,128]{4,3,2,1,0:T(8,128)S(1)}, u32[]{:S(2)}) copy-start(f32[4,8,2,8,128]{4,3,2,1,0:T(8,128)S(1)} %get-tuple-element.16) | copy-start | bytes 786436
  64.3 2.2 %copy-start.11 = (bf16[1,4,2,6,24,512]{5,4,3,2,1,0:T(8,128)(2,1)S(1)}, bf16[1,4,2,6,24,512]{5,4,3,2,1,0:T(8,128)(2,1)}, u32[]{:S(2)}) copy-start(bf16[1,4,2,6,24,512]{5,4,3,2,1,0:T(8,128)(2,1)} %get-tuple-element.17) | copy-start | bytes 3538948
  64.3 10.0 %copy-start.9 = (bf16[1,4,2,6,64,512]{5,4,3,2,1,0:T(8,128)(2,1)S(1)}, bf16[1,4,2,6,64,512]{5,4,3,2,1,0:T(8,128)(2,1)}, u32[]{:S(2)}) copy-start(bf16[1,4,2,6,64,512]{5,4,3,2,1,0:T(8,128)(2,1)} %get-tuple-element.19) | copy-start | bytes 9437188
  64.4 17.8 %collective-permute-start.2 = (f32[4,2,80,128]{3,2,1,0:T(8,128)S(1)}, f32[4,2,80,128]{3,2,1,0:T(8,128)S(1)}, u32[]{:S(2)}, u32[]{:S(2)}) collective-permute-start(f32[4,2,80,128]{3,2,1,0:T(8,128)S(1)} %get-tuple-element.30), channel_id=1, source_target_pairs={{0,8},{8,16},{16,24},{24,0},{1,9},{9,17},{17,25},{25,1},{2,10},{10... | collective-permute-start | bytes 983048 | tf_op jit(solution)/shard_map/ppermute | solution.py:252
  67.4 11.1 %collective-permute-start.14 = (bf16[2,3,48,512]{3,2,1,0:T(8,128)(2,1)S(1)}, bf16[2,3,48,512]{3,2,1,0:T(8,128)(2,1)S(1)}, u32[]{:S(2)}, u32[]{:S(2)}) collective-permute-start(bf16[2,3,48,512]{3,2,1,0:T(8,128)(2,1)S(1)} %get-tuple-element.34), channel_id=1, source_target_pairs={{0,24},{8,0},{16,8},{24,16},{1,25},{9,1},{17,9},{25,17},{2,26},{10... | collective-permute-start | bytes 884744 | tf_op jit(solution)/shard_map/ppermute | solution.py:252
  71.1 11.2 %collective-permute-start.13 = (bf16[2,3,48,512]{3,2,1,0:T(8,128)(2,1)S(1)}, bf16[2,3,48,512]{3,2,1,0:T(8,128)(2,1)S(1)}, u32[]{:S(2)}, u32[]{:S(2)}) collective-permute-start(bf16[2,3,48,512]{3,2,1,0:T(8,128)(2,1)S(1)} %get-tuple-element.35), channel_id=1, source_target_pairs={{0,8},{8,16},{16,24},{24,0},{1,9},{9,17},{17,25},{25,1},{2,10},{10... | collective-permute-start | bytes 884744 | tf_op jit(solution)/shard_map/ppermute | solution.py:252
  71.1 15.1 %collective-permute-start.3 = (f32[4,2,80,128]{3,2,1,0:T(8,128)S(1)}, f32[4,2,80,128]{3,2,1,0:T(8,128)S(1)}, u32[]{:S(2)}, u32[]{:S(2)}) collective-permute-start(f32[4,2,80,128]{3,2,1,0:T(8,128)S(1)} %get-tuple-element.31), channel_id=1, source_target_pairs={{0,24},{8,0},{16,8},{24,16},{1,25},{9,1},{17,9},{25,17},{2,26},{10... | collective-permute-start | bytes 983048 | tf_op jit(solution)/shard_map/ppermute | solution.py:252
  74.3 11.8 %copy-start.17 = (s32[4,4]{1,0:T(4,128)S(1)}, s32[4,4]{1,0:T(4,128)}, u32[]{:S(2)}) copy-start(s32[4,4]{1,0:T(4,128)} %param.9) | copy-start | bytes 196
  78.5 4.5 %copy-start.14 = (bf16[2,3,48,512]{3,2,1,0:T(8,128)(2,1)}, bf16[2,3,48,512]{3,2,1,0:T(8,128)(2,1)S(1)}, u32[]{:S(2)}) copy-start(bf16[2,3,48,512]{3,2,1,0:T(8,128)(2,1)S(1)} %collective-permute-done.14) | copy-start | bytes 884740
  78.6 51.3 %collective-permute-start.19 = (bf16[2,6,64,512]{3,2,1,0:T(8,128)(2,1)}, bf16[2,6,64,512]{3,2,1,0:T(8,128)(2,1)}, u32[]{:S(2)}, u32[]{:S(2)}) collective-permute-start(bf16[2,6,64,512]{3,2,1,0:T(8,128)(2,1)} %get-tuple-element.27), channel_id=1, source_target_pairs={{0,24},{8,0},{16,8},{24,16},{1,25},{9,1},{17,9},{25,17},{2,26},{10... | collective-permute-start | bytes 2359304 | tf_op jit(solution)/shard_map/ppermute | solution.py:252
  82.2 0.8 copy-start.15
  82.2 49.1 %collective-permute-start.17 = (bf16[2,6,64,512]{3,2,1,0:T(8,128)(2,1)}, bf16[2,6,64,512]{3,2,1,0:T(8,128)(2,1)}, u32[]{:S(2)}, u32[]{:S(2)}) collective-permute-start(bf16[2,6,64,512]{3,2,1,0:T(8,128)(2,1)} %get-tuple-element.28), channel_id=1, source_target_pairs={{0,8},{8,16},{16,24},{24,0},{1,9},{9,17},{17,25},{25,1},{2,10},{10... | collective-permute-start | bytes 2359304 | tf_op jit(solution)/shard_map/ppermute | solution.py:252
  82.3 0.8 copy-start.12
  83.1 51.0 %collective-permute-start.11 = (bf16[2,6,64,512]{3,2,1,0:T(8,128)(2,1)}, bf16[2,6,64,512]{3,2,1,0:T(8,128)(2,1)}, u32[]{:S(2)}, u32[]{:S(2)}) collective-permute-start(bf16[2,6,64,512]{3,2,1,0:T(8,128)(2,1)} %get-tuple-element.29), channel_id=1, source_target_pairs={{0,16},{8,24},{16,0},{24,8},{1,17},{9,25},{17,1},{25,9},{2,18},{10... | collective-permute-start | bytes 2359304 | tf_op jit(solution)/shard_map/ppermute | solution.py:252
  86.2 2.5 %copy-start.13 = (f32[4,2,80,128]{3,2,1,0:T(8,128)}, f32[4,2,80,128]{3,2,1,0:T(8,128)S(1)}, u32[]{:S(2)}) copy-start(f32[4,2,80,128]{3,2,1,0:T(8,128)S(1)} %collective-permute-done.3) | copy-start | bytes 983044
  86.2 39.3 %collective-permute-start.4 = (f32[4,2,80,128]{3,2,1,0:T(8,128)S(1)}, f32[4,2,80,128]{3,2,1,0:T(8,128)}, u32[]{:S(2)}, u32[]{:S(2)}) collective-permute-start(f32[4,2,80,128]{3,2,1,0:T(8,128)S(1)} %get-tuple-element.32), channel_id=1, source_target_pairs={{0,16},{8,24},{16,0},{24,8},{1,17},{9,25},{17,1},{25,9},{2,18},{10... | collective-permute-start | bytes 983048 | tf_op jit(solution)/shard_map/ppermute | solution.py:252
  125.5 29.7 %collective-permute-start.9 = (bf16[1,8,3,48,512]{4,3,2,1,0:T(8,128)(2,1)}, bf16[1,8,3,48,512]{4,3,2,1,0:T(8,128)(2,1)S(1)}, u32[]{:S(2)}, u32[]{:S(2)}) collective-permute-start(bf16[1,8,3,48,512]{4,3,2,1,0:T(8,128)(2,1)} %hold.3), channel_id=1, source_target_pairs={{0,64},{64,0},{1,65},{65,1},{2,66},{66,2},{3,67},{67,3},{4,68},{68... | collective-permute-start | bytes 3538952 | tf_op jit(solution)/shard_map/ppermute | solution.py:18
  128.3 0.8 copy-start.10
  129.8 6.0 %collective-permute-start.5 = (f32[2,80,128]{2,1,0:T(8,128)}, f32[2,80,128]{2,1,0:T(8,128)}, u32[]{:S(2)}, u32[]{:S(2)}) collective-permute-start(f32[2,80,128]{2,1,0:T(8,128)} %get-tuple-element.43), channel_id=1, source_target_pairs={{0,2},{2,4},{4,6},{6,0},{1,3},{3,5},{5,7},{7,1},{8,10},{10,12},{12... | collective-permute-start | bytes 245768 | tf_op jit(solution)/shard_map/ppermute | solution.py:270
  131.3 6.3 %collective-permute-start.7 = (f32[2,80,128]{2,1,0:T(8,128)}, f32[2,80,128]{2,1,0:T(8,128)}, u32[]{:S(2)}, u32[]{:S(2)}) collective-permute-start(f32[2,80,128]{2,1,0:T(8,128)} %get-tuple-element.44), channel_id=1, source_target_pairs={{0,4},{2,6},{4,0},{6,2},{1,5},{3,7},{5,1},{7,3},{8,12},{10,14},{12... | collective-permute-start | bytes 245768 | tf_op jit(solution)/shard_map/ppermute | solution.py:270
  134.1 4.8 %collective-permute-start.6 = (f32[2,80,128]{2,1,0:T(8,128)}, f32[2,80,128]{2,1,0:T(8,128)}, u32[]{:S(2)}, u32[]{:S(2)}) collective-permute-start(f32[2,80,128]{2,1,0:T(8,128)} %get-tuple-element.45), channel_id=1, source_target_pairs={{0,6},{2,0},{4,2},{6,4},{1,7},{3,1},{5,3},{7,5},{8,14},{10,8},{12,... | collective-permute-start | bytes 245768 | tf_op jit(solution)/shard_map/ppermute | solution.py:270
  135.8 18.4 %collective-permute-start.20 = (bf16[2,6,64,512]{3,2,1,0:T(8,128)(2,1)}, bf16[2,6,64,512]{3,2,1,0:T(8,128)(2,1)}, u32[]{:S(2)}, u32[]{:S(2)}) collective-permute-start(bf16[2,6,64,512]{3,2,1,0:T(8,128)(2,1)} %collective-permute-done.19), channel_id=1, source_target_pairs={{0,32},{32,0},{1,33},{33,1},{2,34},{34,2},{3,35},{35,3},{4,36},{36... | collective-permute-start | bytes 2359304 | tf_op jit(solution)/shard_map/ppermute | solution.py:18
  137.7 17.5 %collective-permute-start.18 = (bf16[2,6,64,512]{3,2,1,0:T(8,128)(2,1)}, bf16[2,6,64,512]{3,2,1,0:T(8,128)(2,1)}, u32[]{:S(2)}, u32[]{:S(2)}) collective-permute-start(bf16[2,6,64,512]{3,2,1,0:T(8,128)(2,1)} %collective-permute-done.17), channel_id=1, source_target_pairs={{0,32},{32,0},{1,33},{33,1},{2,34},{34,2},{3,35},{35,3},{4,36},{36... | collective-permute-start | bytes 2359304 | tf_op jit(solution)/shard_map/ppermute | solution.py:18
  138.8 16.3 %collective-permute-start.12 = (bf16[2,6,64,512]{3,2,1,0:T(8,128)(2,1)}, bf16[2,6,64,512]{3,2,1,0:T(8,128)(2,1)}, u32[]{:S(2)}, u32[]{:S(2)}) collective-permute-start(bf16[2,6,64,512]{3,2,1,0:T(8,128)(2,1)} %collective-permute-done.11), channel_id=1, source_target_pairs={{0,32},{32,0},{1,33},{33,1},{2,34},{34,2},{3,35},{35,3},{4,36},{36... | collective-permute-start | bytes 2359304 | tf_op jit(solution)/shard_map/ppermute | solution.py:18
  142.7 1.4 copy-start.1
  144.1 30.0 %collective-permute-start.16 = (bf16[6,3,48,512]{3,2,1,0:T(8,128)(2,1)}, bf16[6,3,48,512]{3,2,1,0:T(8,128)(2,1)}, u32[]{:S(2)}, u32[]{:S(2)}) collective-permute-start(bf16[6,3,48,512]{3,2,1,0:T(8,128)(2,1)} %hold.5), channel_id=1, source_target_pairs={{0,64},{64,0},{1,65},{65,1},{2,66},{66,2},{3,67},{67,3},{4,68},{68... | collective-permute-start | bytes 2654216 | tf_op jit(solution)/shard_map/ppermute | solution.py:18
  144.6 1.7 copy-start.2
  146.3 0.9 copy-start.6
  147.1 7.1 %copy-start.16 = (bf16[2,3,48,512]{3,2,1,0:T(8,128)(2,1)S(1)}, bf16[2,3,48,512]{3,2,1,0:T(8,128)(2,1)}, u32[]{:S(2)}) copy-start(bf16[2,3,48,512]{3,2,1,0:T(8,128)(2,1)} %get-tuple-element.36) | copy-start | bytes 884740
  154.2 12.5 %collective-permute-start.8 = (bf16[2,3,48,512]{3,2,1,0:T(8,128)(2,1)S(1)}, bf16[2,3,48,512]{3,2,1,0:T(8,128)(2,1)}, u32[]{:S(2)}, u32[]{:S(2)}) collective-permute-start(bf16[2,3,48,512]{3,2,1,0:T(8,128)(2,1)S(1)} %copy-done.16), channel_id=1, source_target_pairs={{0,16},{8,24},{16,0},{24,8},{1,17},{9,25},{17,1},{25,9},{2,18},{10... | collective-permute-start | bytes 884744 | tf_op jit(solution)/shard_map/ppermute | solution.py:252
  155.1 4.7 %copy-start.3 = (bf16[1,8,3,48,512]{4,3,2,1,0:T(8,128)(2,1)}, bf16[1,8,3,48,512]{4,3,2,1,0:T(8,128)(2,1)S(1)}, u32[]{:S(2)}) copy-start(bf16[1,8,3,48,512]{4,3,2,1,0:T(8,128)(2,1)S(1)} %collective-permute-done.9.refs_1_.refs_0_) | copy-start | bytes 3538948
  159.9 9.1 %collective-permute-start.24 = (f32[3,2,48,128]{3,2,1,0:T(8,128)S(1)}, f32[3,2,48,128]{3,2,1,0:T(8,128)S(1)}, u32[]{:S(2)}, u32[]{:S(2)}) collective-permute-start(f32[3,2,48,128]{3,2,1,0:T(8,128)S(1)} %get-tuple-element.40), channel_id=1, source_target_pairs={{0,8},{8,16},{16,24},{24,0},{1,9},{9,17},{17,25},{25,1},{2,10},{10... | collective-permute-start | bytes 442376 | tf_op jit(solution)/shard_map/ppermute | solution.py:252
  160.8 9.8 %collective-permute-start.25 = (f32[3,2,48,128]{3,2,1,0:T(8,128)S(1)}, f32[3,2,48,128]{3,2,1,0:T(8,128)S(1)}, u32[]{:S(2)}, u32[]{:S(2)}) collective-permute-start(f32[3,2,48,128]{3,2,1,0:T(8,128)S(1)} %get-tuple-element.41), channel_id=1, source_target_pairs={{0,24},{8,0},{16,8},{24,16},{1,25},{9,1},{17,9},{25,17},{2,26},{10... | collective-permute-start | bytes 442376 | tf_op jit(solution)/shard_map/ppermute | solution.py:252
  163.2 8.1 %collective-permute-start.26 = (f32[3,2,48,128]{3,2,1,0:T(8,128)S(1)}, f32[3,2,48,128]{3,2,1,0:T(8,128)S(1)}, u32[]{:S(2)}, u32[]{:S(2)}) collective-permute-start(f32[3,2,48,128]{3,2,1,0:T(8,128)S(1)} %get-tuple-element.42), channel_id=1, source_target_pairs={{0,16},{8,24},{16,0},{24,8},{1,17},{9,25},{17,1},{25,9},{2,18},{10... | collective-permute-start | bytes 442376 | tf_op jit(solution)/shard_map/ppermute | solution.py:252
  166.7 23.9 %collective-permute-start.32 = (bf16[32,512]{1,0:T(8,128)(2,1)S(1)}, bf16[32,512]{1,0:T(8,128)(2,1)S(1)}, u32[]{:S(2)}, u32[]{:S(2)}) collective-permute-start(bf16[32,512]{1,0:T(8,128)(2,1)S(1)} %fusion.32), channel_id=1, source_target_pairs={{0,32},{32,0},{1,33},{33,1},{2,34},{34,2},{3,35},{35,3},{4,36},{36... | collective-permute-start | bytes 98312 | tf_op jit(solution)/shard_map/ppermute | solution.py:18
  166.8 8.4 %copy-start.5 = (bf16[1,1,2,6,64,512]{5,4,3,2,1,0:T(8,128)(2,1)S(1)}, bf16[1,1,2,6,64,512]{5,4,3,2,1,0:T(8,128)(2,1)}, u32[]{:S(2)}) copy-start(bf16[1,1,2,6,64,512]{5,4,3,2,1,0:T(8,128)(2,1)} %get-tuple-element.26) | copy-start | bytes 2359300
  169.0 13.3 %collective-permute-start.10 = (bf16[2,3,48,512]{3,2,1,0:T(8,128)(2,1)}, bf16[2,3,48,512]{3,2,1,0:T(8,128)(2,1)S(1)}, u32[]{:S(2)}, u32[]{:S(2)}) collective-permute-start(bf16[2,3,48,512]{3,2,1,0:T(8,128)(2,1)} %hold.4), channel_id=1, source_target_pairs={{0,64},{64,0},{1,65},{65,1},{2,66},{66,2},{3,67},{67,3},{4,68},{68... | collective-permute-start | bytes 884744 | tf_op jit(solution)/shard_map/ppermute | solution.py:18
  171.4 20.0 %collective-permute-start.27 = (f32[2,48,128]{2,1,0:T(8,128)S(1)}, f32[2,48,128]{2,1,0:T(8,128)S(1)}, u32[]{:S(2)}, u32[]{:S(2)}) collective-permute-start(f32[2,48,128]{2,1,0:T(8,128)S(1)} %get-tuple-element.46), channel_id=1, source_target_pairs={{0,2},{2,4},{6,0},{1,3},{3,5},{7,1},{8,10},{10,12},{14,8},{9,11},{... | collective-permute-start | bytes 147464 | tf_op jit(solution)/shard_map/ppermute | solution.py:270
  178.5 13.8 %copy-start.7 = (f32[2,80,128]{2,1,0:T(8,128)S(1)}, f32[2,80,128]{2,1,0:T(8,128)}, u32[]{:S(2)}) copy-start(f32[2,80,128]{2,1,0:T(8,128)} %fusion.23.refs_2_.refs_3_) | copy-start | bytes 245764
  178.6 13.4 %collective-permute-start.29 = (f32[2,48,128]{2,1,0:T(8,128)S(1)}, f32[2,48,128]{2,1,0:T(8,128)S(1)}, u32[]{:S(2)}, u32[]{:S(2)}) collective-permute-start(f32[2,48,128]{2,1,0:T(8,128)S(1)} %get-tuple-element.47), channel_id=1, source_target_pairs={{0,4},{4,0},{6,2},{1,5},{5,1},{7,3},{8,12},{12,8},{14,10},{9,13},{... | collective-permute-start | bytes 147464 | tf_op jit(solution)/shard_map/ppermute | solution.py:270
  181.0 11.0 %collective-permute-start.28 = (f32[2,48,128]{2,1,0:T(8,128)S(1)}, f32[2,48,128]{2,1,0:T(8,128)S(1)}, u32[]{:S(2)}, u32[]{:S(2)}) collective-permute-start(f32[2,48,128]{2,1,0:T(8,128)S(1)} %get-tuple-element.48), channel_id=1, source_target_pairs={{2,0},{4,2},{6,4},{3,1},{5,3},{7,5},{10,8},{12,10},{14,12},{11,9},... | collective-permute-start | bytes 147464 | tf_op jit(solution)/shard_map/ppermute | solution.py:270
  184.4 8.0 %collective-permute-start.22 = (f32[2,48,128]{2,1,0:T(8,128)S(1)}, f32[2,48,128]{2,1,0:T(8,128)S(1)}, u32[]{:S(2)}, u32[]{:S(2)}) collective-permute-start(f32[2,48,128]{2,1,0:T(8,128)S(1)} %bitcast.157), channel_id=1, source_target_pairs={{0,6},{1,7},{8,14},{9,15},{16,22},{17,23},{24,30},{25,31},{32,38},... | collective-permute-start | bytes 147464 | tf_op jit(solution)/shard_map/ppermute | solution.py:270
  190.6 1.7 collective-permute-start.23
  191.3 1.0 collective-permute-start.21
  192.4 5.8 %collective-permute-start.30 = (f32[128,128]{1,0:T(8,128)S(1)}, f32[128,128]{1,0:T(8,128)S(1)}, u32[]{:S(2)}, u32[]{:S(2)}) collective-permute-start(f32[128,128]{1,0:T(8,128)S(1)} %fusion.25), channel_id=1, source_target_pairs={{0,1},{1,0},{2,3},{3,2},{4,5},{5,4},{6,7},{7,6},{8,9},{9,8},{10,11... | collective-permute-start | bytes 196616 | tf_op jit(solution)/shard_map/ppermute | solution.py:18
  198.3 1.3 collective-permute-start.31

commit v7 on v6

--- a/solution.py
+++ b/solution.py
@@ -68,6 +68,12 @@
     return block.reshape(x, z * yh, comps // 2, 2 * n, sites)
 
 
+def mark(value):
+    while value.ndim > 2:
+        value = value[0]
+    return value
+
+
 def hold_kernel(*refs):
     pass
 
@@ -81,7 +87,7 @@
         input_output_aliases={0: 0},
         cost_estimate=HINT,
         name="hold",
-    )(value, *after)
+    )(value, *map(mark, after))
 
 
 def front_kernel(owned, at, sols, vecs, out, lines, slab, held, sems):
@@ -178,41 +184,30 @@
             row += 2 * n
 
 
-def pieces_kernel(count, *refs):
+def pieces_kernel(col, own, other, out):
     total = None
-    for at in range(count):
-        col, own, other = refs[3 * at : 3 * at + 3]
-        for colour in range(own.shape[1]):
-            term = product([col[0, colour]], own[0, colour], other[0, colour])
-            total = term if total is None else total + term
-    out = refs[-1]
-    n = out.shape[2]
-    parts = real_imag(total, 0, n)
-    for part in range(2):
-        if len(refs) == 3 * count + 1:
-            out[0, part] = parts[part]
-        else:
-            out[0, part] = refs[3 * count][0, part] + parts[part]
-
-
-def project_pieces(pieces, before=None):
-    inner, colours, n2, sites = pieces[0][0].shape
-    rows = pieces[0][1].shape[2]
-    spec = lambda shape: pl.BlockSpec((1,) + shape[1:], lambda j: (j, 0, 0, 0))
-    args = [array for piece in pieces for array in piece]
-    if before is not None:
-        args.append(before)
-    out = (inner, 2, n2 // 2, rows)
+    for colour in range(own.shape[1]):
+        term = product([col[0, colour]], own[0, colour], other[0, colour])
+        total = term if total is None else total + term
+    here = pl.program_id(0)
+    for part, value in enumerate(real_imag(total, 0, out.shape[1])):
+        out[part] = jnp.where(here == 0, value, out[part] + value)
+
+
+def project_pieces(cols, own, other, *after):
+    count, _, n2, _ = cols.shape
+    rows = own.shape[2]
+    spec = lambda v: pl.BlockSpec((1,) + v.shape[1:], lambda i: (i, 0, 0, 0))
     return pl.pallas_call(
-        functools.partial(pieces_kernel, len(pieces)),
-        grid=(inner,),
-        in_specs=[spec(array.shape) for array in args],
-        out_specs=spec(out),
-        out_shape=jax.ShapeDtypeStruct(out, jnp.float32),
+        pieces_kernel,
+        grid=(count,),
+        in_specs=[spec(cols), spec(own), spec(other)] + [ANY] * len(after),
+        out_specs=pl.BlockSpec((2, n2 // 2, rows), lambda i: (0, 0, 0)),
+        out_shape=jax.ShapeDtypeStruct((2, n2 // 2, rows), jnp.float32),
         compiler_params=pltpu.CompilerParams(vmem_limit_bytes=16 * 2**20),
         cost_estimate=HINT,
         name="project_pieces",
-    )(*args)
+    )(cols, own, other, *after)
 
 
 def project(cols, own, other, x, y, step, *after):
@@ -236,7 +231,7 @@
         in_specs=in_specs,
         out_specs=out_specs,
         out_shape=out_shape,
-        compiler_params=pltpu.CompilerParams(vmem_limit_bytes=48 * 2**20),
+        compiler_params=pltpu.CompilerParams(vmem_limit_bytes=(60 if size == 4 else 40) * 2**20),
         cost_estimate=HINT,
         name="project",
     )(*cols, own, other, *after)
@@ -255,19 +250,17 @@
     return [pick(slabs, me), *got]
 
 
-def sum_z(part):
-    got = share_z(jnp.swapaxes(part, 0, 1))
+def sum_z(slabs):
+    got = share_z(slabs)
     return got[0] + got[1] + got[2] + got[3]
 
 
-def sum_x(part, first, size):
+def sum_x(slabs):
     me = lax.axis_index("x")
-    clip = lambda i: jnp.clip(i - first, 0, size - 1)
-    total = pick(part, clip(me)) if size > 1 else part[0]
+    total = pick(slabs, me)
     for k in (1, 3, 2):
-        send = pick(part, clip((me + k) % 4)) if size > 1 else part[0]
-        pairs = [(i, (i + k) % 4) for i in range(4) if first <= (i + k) % 4 < first + size]
-        total = total + lax.ppermute(send, "x", pairs)
+        pairs = [(i, (i + k) % 4) for i in range(4)]
+        total = total + lax.ppermute(pick(slabs, (me + k) % 4), "x", pairs)
     return total
 
 
@@ -289,47 +282,46 @@
     first_part = front(sols, vecs, source_index, source_time, group)
     raw = swap(first_part, "yl")
     other = swap(vecs, "c")
-    sent = [(RAW, count, x, nx, 0, 2) for x, nx in ((0, 2), (2, 1), (3, 1))]
-    mine, *send = by_time(sols, ((0, count, 0, 4, 0, 2), *sent), first_part)
+    parts = ((0, 1, 0, 2), (1, 1, 0, 2), (2, 1, 0, 2), (3, 1, 0, 1), (3, 1, 1, 1))
+    sent = [(RAW, count, *part) for part in parts]
+    mine, *send = by_time(sols, ((0, count, 0, 4, 0, 2), *sent), mark(first_part))
     send = [rows_of(part) for part in send]
-    shared = share_z(send[2].reshape(4, 2, comps // 2, -1, sites))
-
-    whole = (0, owned, 0, 4, 0, 2)
-    late = (0, owned, 3, 1, 0, 2)
-    own, own_late = by_time(vecs, (whole, late))
-    other, other_late = by_time(other, (whole, late))
+    got = [swap(send[0], "yl"), swap(hold(send[1], raw), "yl")]
+    got += [swap(hold(send[2], got[0]), "yl"), swap(hold(send[3], got[1]), "yl")]
+
+    whole, late = (0, owned, 0, 4, 0, 2), (0, owned, 3, 1, 1, 1)
+    own, own_late = by_time(vecs, (whole, late), mark(send[0]))
+    other = by_time(other, (whole,))[0]
     own, other = rows_of(own), rows_of(other)
-    got = [swap(send[0], "yl"), swap(hold(send[1], raw, own, other), "yl")]
     lines = raw[RAW * comps] + first_part[RAW * comps]
-    raw = rows_of(by_time(raw, ((0, RAW, 0, 4, 0, 2),), other)[0])
-
-    def rows(part):
-        x, inner, _, n, lanes = part.shape
-        return part.reshape(x, 4, inner // 4, 2 * n, lanes)
+    lines = lines + swap(lines, "c")
+    raw_rows = rows_of(by_time(raw, ((0, RAW, 0, 4, 0, 2),), mark(other), lines)[0])
 
     def against(part, x, y, step, *after):
-        return rows(project([part], own, other, x, y, step, *after)[0])
-
-    parts = project([rows_of(mine), raw], own, other, 0, 0, 8)
-    first_z = sum_z(jnp.concatenate([rows(p) for p in parts], axis=3))
-    first = sum_x(first_z, 0, 4)
-    most = swap(hold(jnp.concatenate(shared[:3]), got[0], first), "yl")
-    rest = swap(hold(shared[3], got[1]), "yl")
-    got_last = [most[:2], most[2:4], most[4:], rest]
-
-    mine_z = share_z(own_late[0])
-    theirs_z = [pick(other_late[0], lax.axis_index("z"))] + [swap(p, "c") for p in mine_z[1:]]
-    pieces = [
-        (s, *(v.reshape(2, comps // 2, 2 * owned, sites) for v in pair))
-        for s, *pair in zip(got_last, mine_z, theirs_z)
-    ]
-
-    mid = [against(got[0], 0, 0, 8, first)]
-    mid.append(against(got[1], 2, 0, 4, mid[0], *theirs_z[1:]))
-    mid = sum_x(sum_z(jnp.concatenate(mid, axis=0)), 0, 3)
-    last = project_pieces(pieces[3:], project_pieces(pieces[:3]))
-    last = sum_x(last.reshape(1, 2, -1, 2 * owned), 3, 1)
-    late = jnp.where(lax.axis_index("x") == 3, last, mid)
+        out = project([part], own, other, x, y, step, *map(mark, after))[0]
+        return out.reshape(out.shape[0], 4, -1, 2 * (count - RAW), 2 * owned)
+
+    slabs = [v.reshape(4, comps // 2, -1, sites) for v in (send[4], own_late)]
+    spread = jnp.stack(share_z(hold(jnp.concatenate(slabs, axis=2), raw)))
+    cut = send[4].shape[3]
+    spread_s, spread_v = spread[:, :, :cut], spread[:, :, cut:]
+    spread_w = swap(spread_v, "c")
+
+    first = project([rows_of(mine), raw_rows], own, other, 0, 0, 8)
+    first = [v.reshape(4, 4, 2, -1, 2 * owned) for v in first]
+    first = sum_x(jnp.concatenate(first, axis=3))
+    first = sum_z(hold(first, spread_v))
+
+    early = [against(got[0], 0, 0, 4, first), against(got[1], 1, 0, 4, first, spread_w)]
+    early = sum_z(jnp.concatenate([v[0] for v in early], axis=1))
+    mid = [against(got[2], 2, 0, 4, early)[0]]
+    got.append(swap(hold(spread_s, mid[0]), "yl"))
+    mid.append(against(got[3], 3, 0, 1, mid[0])[0])
+    mid = sum_z(jnp.concatenate(mid, axis=1))
+    last = project_pieces(got[4], spread_v, spread_w)
+    last = last.reshape(1, -1, 2 * owned)
+    late = sum_x(jnp.concatenate([early, mid, last]).reshape(4, 2, -1, 2 * owned))
+
     here = sum_yh(jnp.concatenate([first, late], axis=1))
     there = swap(here, "c")
 
@@ -351,7 +343,6 @@
     result = jnp.sum(picked, axis=0).reshape(spins, 2, count, owned) * scale
     result = result.transpose(3, 0, 2, 1).reshape(1, owned, spins * count * 2)
 
-    lines = lines + swap(lines, "c")
     chosen = lines.reshape(nsources, -1, sites)[:, :comps]
     my_spins = lax.dynamic_index_in_dim(dilution, group, 1, keepdims=False)
     spin_mask = jnp.arange(spins, dtype=jnp.int32)[None, :] == my_spins[:, None]

time: 205 us -> 226 us (1.10)
  local copies, waits for them, and re-layouts: 17.8 us -> 34.5 us
  starting transfers between devices: 52 us -> 40.4 us
  waiting for transfers between devices: 54.9 us -> 64.1 us
  other arithmetic: 8.76 us -> 17.1 us
    ppermute x12 -> x11, waiting for transfers between devices: 9.33 us -> 20.9 us  [swap(): return lax.ppermute(value, axis, SWAP)]
    ppermute x12, waiting for transfers between devices: 42.2 us -> 30.8 us  [share_z(): lax.ppermute(pick(slabs, (me + k) % 4), 'z', [(i, (i + k) % 4) for i in r...]
    ppermute x9 -> x6, starting transfers between devices: 19.6 us -> 9.47 us  [sum_x(): total = total + lax.ppermute(pick(slabs, (me + k) % 4), 'x', pairs)]
    ppermute x9 -> x6, waiting for transfers between devices: 3.38 us -> 12.3 us  [sum_x(): total = total + lax.ppermute(pick(slabs, (me + k) % 4), 'x', pairs)]
    unnamed x38 -> x40, local copies, waits for them, and re-layouts: 11 us -> 19.4 us
    squeeze x0 -> x10, local copies, waits for them, and re-layouts: none -> 7.92 us  [mark(): value = value[0]]
    pallas_call x3 -> x5, Pallas kernels: 25.2 us -> 30.2 us  [project(): pl.pallas_call(functools.partial(dot_kernel, len(cols)), grid=(size, inne...]
    ppermute x12, starting transfers between devices: 23.2 us -> 19 us  [share_z(): lax.ppermute(pick(slabs, (me + k) % 4), 'z', [(i, (i + k) % 4) for i in r...]
  transfers between devices with their start and end apart: 33 -> 29, of which waited for: 11 -> 16; matrix products, arithmetic and copies ran while one was open for 7% -> 13% of each run, Pallas kernels for 33% -> 28%
where the time goes in v7:
time: 226 us; the launch traced here: 224 us
  Pallas kernels  66 us (29%)
  waiting for transfers between devices  64.1 us (28%)
  starting transfers between devices  40.4 us (18%)
  local copies, waits for them, and re-layouts  34.5 us (15%)
  other arithmetic  17.1 us (8%)
    ppermute x12, waiting for transfers between devices, share_z(): lax.ppermute(pick(slabs, (me + k) % 4), 'z', [(i, (i + k) % 4) for i in r...  30.8 us
    pallas_call x5, Pallas kernels, project(): pl.pallas_call(functools.partial(dot_kernel, len(cols)), grid=(size, inne...  30.2 us
    pallas_call x4, Pallas kernels, by_time(): pl.pallas_call(functools.partial(by_time_kernel, cuts), grid=(4,), in_spe...  29.5 us
    ppermute x11, waiting for transfers between devices, swap(): return lax.ppermute(value, axis, SWAP)  20.9 us
    unnamed x40, local copies, waits for them, and re-layouts  19.4 us
    ppermute x12, starting transfers between devices, share_z(): lax.ppermute(pick(slabs, (me + k) % 4), 'z', [(i, (i + k) % 4) for i in r...  19 us
    ppermute x6, waiting for transfers between devices, sum_x(): total = total + lax.ppermute(pick(slabs, (me + k) % 4), 'x', pairs)  12.3 us
    ppermute x11, starting transfers between devices, swap(): return lax.ppermute(value, axis, SWAP)  12 us
  transfers between devices with their start and end apart: 29, of which 16 were waited for; matrix products, arithmetic and copies ran while one was open for 13% of the time, Pallas kernels for 28%

profile of v7, /device:TPU:0, one launch (start us, length us, event | category | flops | bytes accessed | tf_op | source)
XLA Modules:
  0.0 223.9 jit_solution(7079582081179672275)
XLA Ops:
  1.4 1.2 pad_add_fusion.at
  2.6 2.9 %front.1 = bf16[49,4,8,512]{3,2,1,0:T(8,128)(2,1)} custom-call(s32[6]{0:T(128)} %pad_add_fusion.at, bf16[192,4,8,512]{3,2,1,0:T(8,128)(2,1)} %bitcast.195, bf16[64,6,32,512]{3,2,1,0:T(8,128)(2,1)} %bitcast.193), custom_call_target="tpu_custom_call" | custom-call | flops 1000 | bytes 1000 | tf_op jit(solution)/shard_map/front/pallas_call | solution.py:133
  5.6 1.7 collective-permute-start
  7.3 1.4 slice_bitcast_fusion.9.refs_0_
  8.7 7.7 %by_time.4 = (bf16[4,4,2,6,32,512]{5,4,3,2,1,0:T(8,128)(2,1)}, bf16[1,4,2,6,24,512]{5,4,3,2,1,0:T(8,128)(2,1)}, bf16[1,4,2,6,24,512]{5,4,3,2,1,0:T(8,128)(2,1)},...) custom-call(bf16[32,6,32,512]{3,2,1,0:T(8,128)(2,1)} %bitcast.196, ...), custom_call_target="tpu_custom_call" | custom-call | flops 1000 | bytes 1000 | tf_op jit(solution)/shard_map/by_time/pallas_call | solution.py:48
  16.4 1.4 slice_bitcast_fusion.4.refs_0_
  18.2 10.7 %by_time.7 = (bf16[4,4,2,6,64,512]{5,4,3,2,1,0:T(8,128)(2,1)}, bf16[1,4,1,6,64,512]{5,4,3,2,1,0:T(8,128)(2,1)}) custom-call(bf16[64,6,32,512]{3,2,1,0:T(8,128)(2,1)} %bitcast.194, bf16[48,512]{1,0:T(8,128)(2,1)} %slice_bitcast_fusion.4.refs_0_), custom_call_target="tpu_custom_call" | custom-call | flops 1000 | bytes 1000 | tf_op jit(solution)/shard_map/by_time/pallas_call | solution.py:48
  28.9 3.0 %pad_maximum_fusion.refs_0_ = bf16[4,3,176,512]{3,2,1,0:T(8,128)(2,1)} fusion(bf16[4,3,128,512]{3,2,1,0:T(8,128)(2,1)} %bitcast.207, bf16[4,3,48,512]{3,2,1,0:T(8,128)(2,1)S(1)} %bitcast.214), kind=kLoop, calls=%fused_computation.5 | loop fusion | flops 4325376 | bytes 4325376 | tf_op jit(solution)/shard_map/concatenate | solution.py:305
  31.9 11.9 %collective-permute-done.block = bf16[49,32,512]{2,1,0:T(8,128)(2,1)S(1)} collective-permute-done((bf16[49,32,512]{2,1,0:T(8,128)(2,1)}, bf16[49,32,512]{2,1,0:T(8,128)(2,1)S(1)}, u32[]{:S(2)}, u32[]{:S(2)}) %collective-permute-start) | collective-permute-done | bytes 1605664 | tf_op jit(solution)/shard_map/ppermute | solution.py:18
  45.2 2.5 %constant_dynamic-slice_fusion.1 = (bf16[1,3,176,512]{3,2,1,0:T(8,128)(2,1)S(1)}, bf16[3,176,512]{2,1,0:T(8,128)(2,1)}, bf16[3,176,512]{2,1,0:T(8,128)(2,1)S(1)}, bf16[3,176,512]{2,1,0:T(8,128)(2,1)S(1)}) fusion(bf16[4,3,176,512]{3,2,1,0:T(8,128)(2,1)} %hold.6, s32[]{:T(128)S(6)} %select_n.157, s32[]{:T(128)S(6)} %select_n.163, s32[]{:T(128)S(6)} %select_n.161, ...), kind=kLoop, calls=%fused_computation.106 | loop fusion | bytes 4325392 | tf_op jit(solution)/shard_map/jit(dynamic_index_in_dim)/dynamic_slice | solution.py:241
  47.7 4.0 %collective-permute-start.13 = (bf16[3,176,512]{2,1,0:T(8,128)(2,1)}, bf16[3,176,512]{2,1,0:T(8,128)(2,1)S(1)}, u32[]{:S(2)}, u32[]{:S(2)}) collective-permute-start(bf16[3,176,512]{2,1,0:T(8,128)(2,1)} %get-tuple-element.27), channel_id=1, source_target_pairs={{0,16},{8,24},{16,0},{24,8},{1,17},{9,25},{17,1},{25,9},{2,18},{10... | collective-permute-start | bytes 1622024 | tf_op jit(solution)/shard_map/ppermute | solution.py:247
  52.4 1.3 collective-permute-start.11
  54.0 11.1 %collective-permute-done.13 = bf16[3,176,512]{2,1,0:T(8,128)(2,1)S(1)} collective-permute-done((bf16[3,176,512]{2,1,0:T(8,128)(2,1)}, bf16[3,176,512]{2,1,0:T(8,128)(2,1)S(1)}, u32[]{:S(2)}, u32[]{:S(2)}) %collective-permute-start.13) | collective-permute-done | bytes 540704 | tf_op jit(solution)/shard_map/ppermute | solution.py:247
  65.0 12.1 %collective-permute-done.12 = bf16[3,176,512]{2,1,0:T(8,128)(2,1)S(1)} collective-permute-done((bf16[3,176,512]{2,1,0:T(8,128)(2,1)S(1)}, bf16[3,176,512]{2,1,0:T(8,128)(2,1)S(1)}, u32[]{:S(2)}, u32[]{:S(2)}) %collective-permute-start.12) | collective-permute-done | bytes 540704 | tf_op jit(solution)/shard_map/ppermute | solution.py:247
  78.7 10.4 %by_time.5 = bf16[4,4,2,6,64,512]{5,4,3,2,1,0:T(8,128)(2,1)} custom-call(bf16[64,6,32,512]{3,2,1,0:T(8,128)(2,1)} %collective-permute-done.1.block), custom_call_target="tpu_custom_call" | custom-call | flops 1000 | bytes 1000 | tf_op jit(solution)/shard_map/by_time/pallas_call | solution.py:48
  89.1 1.9 slice-done
  91.6 1.4 copy-done.5
  93.7 1.1 copy-done.3
  94.8 14.7 %project.5 = (f32[4,8,2,32,128]{4,3,2,1,0:T(8,128)}, f32[4,8,2,8,128]{4,3,2,1,0:T(8,128)}) custom-call(bf16[4,8,3,64,512]{4,3,2,1,0:T(8,128)(2,1)} %bitcast.197, bf16[4,8,3,16,512]{4,3,2,1,0:T(8,128)(2,1)} %bitcast.173, bf16[4,8,3,128,512]{4,3,2,1,0:T(8,128)(2,1)} %bitcast.168, bf16[4,8,3,128,512]{4,3,2,1,0:T(8,128)(2,1)} %bitcast.186), custom_call_target="tpu_custom_call" | custom-call | flops 1000 | bytes 1000 | tf_op jit(solution)/shard_map/project/pallas_call | solution.py:228
  109.5 2.1 fusion.8
  111.6 1.5 collective-permute-start.3
  113.1 1.7 collective-permute-start.4
  114.8 1.8 collective-permute-start.5
  116.6 1.4 slice_bitcast_fusion.3.refs_1_
  118.0 1.6 collective-permute-start.10
  119.6 1.6 dynamic-slice_bitcast_fusion.3.refs_1_
  121.2 2.0 collective-permute-done.3
  123.2 6.3 %collective-permute-done.4 = f32[4,2,80,128]{3,2,1,0:T(8,128)} collective-permute-done((f32[4,2,80,128]{3,2,1,0:T(8,128)}, f32[4,2,80,128]{3,2,1,0:T(8,128)}, u32[]{:S(2)}, u32[]{:S(2)}) %collective-permute-start.4) | collective-permute-done | bytes 327712 | tf_op jit(solution)/shard_map/ppermute | solution.py:263
  129.5 1.7 collective-permute-done.5
  131.2 2.1 fusion.6.refs_0_
  133.3 1.0 dynamic-slice_bitcast_fusion.6
  135.1 3.1 %collective-permute-start.8 = (f32[2,80,128]{2,1,0:T(8,128)S(1)}, f32[2,80,128]{2,1,0:T(8,128)S(1)}, u32[]{:S(2)}, u32[]{:S(2)}) collective-permute-start(f32[2,80,128]{2,1,0:T(8,128)S(1)} %get-tuple-element.37), channel_id=1, source_target_pairs={{0,16},{8,24},{16,0},{24,8},{1,17},{9,25},{17,1},{25,9},{2,18},{10... | collective-permute-start | bytes 245768 | tf_op jit(solution)/shard_map/ppermute | solution.py:247
  138.2 1.0 collective-permute-start.7
  139.2 2.0 pad_maximum_fusion.2.refs_0_
  141.2 1.6 collective-permute-start.18
  142.8 0.9 fusion.23
  144.3 4.6 %copy-done = bf16[4,4,2,6,64,512]{5,4,3,2,1,0:T(8,128)(2,1)S(1)} copy-done((bf16[4,4,2,6,64,512]{5,4,3,2,1,0:T(8,128)(2,1)S(1)}, bf16[4,4,2,6,64,512]{5,4,3,2,1,0:T(8,128)(2,1)}, u32[]{:S(2)}) %copy-start) | copy-done | bytes 12582936
  148.9 4.0 %project.6 = f32[1,8,2,24,128]{4,3,2,1,0:T(8,128)S(1)} custom-call(bf16[1,8,3,48,512]{4,3,2,1,0:T(8,128)(2,1)} %collective-permute-done.9.refs_0_, bf16[4,8,3,128,512]{4,3,2,1,0:T(8,128)(2,1)S(1)} %bitcast.169, bf16[4,8,3,128,512]{4,3,2,1,0:T(8,128)(2,1)} %bitcast.187, f32[80,128]{1,0:T(8,128)S(1)} %slice_bitcast_fusion.5.refs_3_), custom_call_target="tpu_custom_call" | custom-call | flops 1000 | bytes 1000 | tf_op jit(solution)/shard_map/project/pallas_call | solution.py:228
  152.9 4.0 %project.7 = f32[1,8,2,24,128]{4,3,2,1,0:T(8,128)S(1)} custom-call(bf16[1,8,3,48,512]{4,3,2,1,0:T(8,128)(2,1)} %collective-permute-done.10.refs_0_, bf16[4,8,3,128,512]{4,3,2,1,0:T(8,128)(2,1)S(1)} %bitcast.170, bf16[4,8,3,128,512]{4,3,2,1,0:T(8,128)(2,1)} %bitcast.188, f32[80,128]{1,0:T(8,128)S(1)} %slice_bitcast_fusion.5.refs_3_, ...), custom_call_target="tpu_custom_call" | custom-call | flops 1000 | bytes 1000 | tf_op jit(solution)/shard_map/project/pallas_call | solution.py:228
  157.6 1.0 collective-permute-start.15
  158.6 2.2 %collective-permute-start.16 = (f32[4,48,128]{2,1,0:T(8,128)}, f32[4,48,128]{2,1,0:T(8,128)}, u32[]{:S(2)}, u32[]{:S(2)}) collective-permute-start(f32[4,48,128]{2,1,0:T(8,128)} %get-tuple-element.34), channel_id=1, source_target_pairs={{0,24},{8,0},{16,8},{24,16},{1,25},{9,1},{17,9},{25,17},{2,26},{10... | collective-permute-start | bytes 294920 | tf_op jit(solution)/shard_map/ppermute | solution.py:247
  161.4 1.4 slice_bitcast_fusion.2.refs_1_
  162.8 1.6 collective-permute-start.19
  164.4 2.9 %collective-permute-done.17 = f32[4,48,128]{2,1,0:T(8,128)} collective-permute-done((f32[4,48,128]{2,1,0:T(8,128)}, f32[4,48,128]{2,1,0:T(8,128)}, u32[]{:S(2)}, u32[]{:S(2)}) %collective-permute-start.17) | collective-permute-done | bytes 98336 | tf_op jit(solution)/shard_map/ppermute | solution.py:247
  167.3 1.0 fusion.17
  168.3 4.2 %collective-permute-done.18.refs_0_ = bf16[1,8,3,48,512]{4,3,2,1,0:T(8,128)(2,1)} collective-permute-done((bf16[1,8,3,48,512]{4,3,2,1,0:T(8,128)(2,1)}, bf16[1,8,3,48,512]{4,3,2,1,0:T(8,128)(2,1)}, u32[]{:S(2)}, u32[]{:S(2)}) %collective-permute-start.18) | collective-permute-done | bytes 1179680 | tf_op jit(solution)/shard_map/ppermute | solution.py:18
  172.5 4.6 %copy-done.1 = bf16[4,4,2,6,64,512]{5,4,3,2,1,0:T(8,128)(2,1)S(1)} copy-done((bf16[4,4,2,6,64,512]{5,4,3,2,1,0:T(8,128)(2,1)S(1)}, bf16[4,4,2,6,64,512]{5,4,3,2,1,0:T(8,128)(2,1)}, u32[]{:S(2)}) %copy-start.1) | copy-done | bytes 12582936
  177.1 4.0 %project.8 = f32[1,8,2,24,128]{4,3,2,1,0:T(8,128)S(1)} custom-call(bf16[1,8,3,48,512]{4,3,2,1,0:T(8,128)(2,1)} %collective-permute-done.18.refs_0_, bf16[4,8,3,128,512]{4,3,2,1,0:T(8,128)(2,1)S(1)} %bitcast.171, bf16[4,8,3,128,512]{4,3,2,1,0:T(8,128)(2,1)} %bitcast.189, f32[48,128]{1,0:T(8,128)S(1)} %slice_bitcast_fusion.10.refs_3_), custom_call_target="tpu_custom_call" | custom-call | flops 1000 | bytes 1000 | tf_op jit(solution)/shard_map/project/pallas_call | solution.py:228
  181.7 1.6 collective-permute-start.23
  183.4 1.8 collective-permute-done.19.refs_0_
  185.2 4.6 %copy-done.2 = bf16[4,4,2,6,64,512]{5,4,3,2,1,0:T(8,128)(2,1)S(1)} copy-done((bf16[4,4,2,6,64,512]{5,4,3,2,1,0:T(8,128)(2,1)S(1)}, bf16[4,4,2,6,64,512]{5,4,3,2,1,0:T(8,128)(2,1)}, u32[]{:S(2)}) %copy-start.2) | copy-done | bytes 12582936
  190.5 3.6 %project.9 = f32[1,4,2,24,128]{4,3,2,1,0:T(8,128)S(1)} custom-call(bf16[1,4,3,48,512]{4,3,2,1,0:T(8,128)(2,1)} %collective-permute-done.19.refs_0_, bf16[4,8,3,128,512]{4,3,2,1,0:T(8,128)(2,1)S(1)} %bitcast.172, bf16[4,8,3,128,512]{4,3,2,1,0:T(8,128)(2,1)} %bitcast.190, f32[48,128]{1,0:T(8,128)S(1)} %bitcast.184), custom_call_target="tpu_custom_call" | custom-call | flops 1000 | bytes 1000 | tf_op jit(solution)/shard_map/project/pallas_call | solution.py:228
  195.6 2.5 %collective-permute-start.21 = (f32[3,48,128]{2,1,0:T(8,128)}, f32[3,48,128]{2,1,0:T(8,128)}, u32[]{:S(2)}, u32[]{:S(2)}) collective-permute-start(f32[3,48,128]{2,1,0:T(8,128)} %get-tuple-element.40), channel_id=1, source_target_pairs={{0,24},{8,0},{16,8},{24,16},{1,25},{9,1},{17,9},{25,17},{2,26},{10... | collective-permute-start | bytes 221192 | tf_op jit(solution)/shard_map/ppermute | solution.py:247
  198.0 1.0 collective-permute-start.22
  199.3 1.4 collective-permute-done.20
  200.7 3.3 %collective-permute-done.22 = f32[3,48,128]{2,1,0:T(8,128)} collective-permute-done((f32[3,48,128]{2,1,0:T(8,128)S(1)}, f32[3,48,128]{2,1,0:T(8,128)}, u32[]{:S(2)}, u32[]{:S(2)}) %collective-permute-start.22) | collective-permute-done | bytes 73760 | tf_op jit(solution)/shard_map/ppermute | solution.py:247
  204.0 1.0 fusion.30
  205.0 3.4 %project_pieces.1 = f32[2,24,128]{2,1,0:T(8,128)S(1)} custom-call(bf16[4,3,48,512]{3,2,1,0:T(8,128)(2,1)} %collective-permute-done.23.col, bf16[4,3,128,512]{3,2,1,0:T(8,128)(2,1)S(1)} %slice.143.own, bf16[4,3,128,512]{3,2,1,0:T(8,128)(2,1)S(1)} %collective-permute-done.14.other), custom_call_target="tpu_custom_call" | custom-call | flops 1000 | bytes 1000 | tf_op jit(solution)/shard_map/project_pieces/pallas_call | solution.py:201
  209.1 2.0 collective-permute-start.26
  211.1 1.8 collective-permute-start.25
  213.8 0.9 collective-permute-done.26
  215.3 3.3 %collective-permute-start.27 = (f32[128,128]{1,0:T(8,128)S(1)}, f32[128,128]{1,0:T(8,128)S(1)}, u32[]{:S(2)}, u32[]{:S(2)}) collective-permute-start(f32[128,128]{1,0:T(8,128)S(1)} %fusion.36), channel_id=1, source_target_pairs={{0,1},{1,0},{2,3},{3,2},{4,5},{5,4},{6,7},{7,6},{8,9},{9,8},{10,11... | collective-permute-start | bytes 196616 | tf_op jit(solution)/shard_map/ppermute | solution.py:18
  219.3 1.8 collective-permute-done.27
  221.3 1.2 collective-permute-done.28
  (106 shorter events, 15.8 us)
Async XLA Ops:
  0.6 78.0 %collective-permute-start.1 = (bf16[64,6,32,512]{3,2,1,0:T(8,128)(2,1)}, bf16[64,6,32,512]{3,2,1,0:T(8,128)(2,1)}, u32[]{:S(2)}, u32[]{:S(2)}) collective-permute-start(bf16[64,6,32,512]{3,2,1,0:T(8,128)(2,1)} %bitcast.192), channel_id=1, source_target_pairs={{0,32},{32,0},{1,33},{33,1},{2,34},{34,2},{3,35},{35,3},{4,36},{36... | collective-permute-start | bytes 37748744 | tf_op jit(solution)/shard_map/ppermute | solution.py:18
  5.6 38.2 %collective-permute-start = (bf16[49,32,512]{2,1,0:T(8,128)(2,1)}, bf16[49,32,512]{2,1,0:T(8,128)(2,1)S(1)}, u32[]{:S(2)}, u32[]{:S(2)}) collective-permute-start(bf16[49,32,512]{2,1,0:T(8,128)(2,1)} %bitcast.206), channel_id=1, source_target_pairs={{0,64},{64,0},{1,65},{65,1},{2,66},{66,2},{3,67},{67,3},{4,68},{68... | collective-permute-start | bytes 4816904 | tf_op jit(solution)/shard_map/ppermute | solution.py:18
  17.8 11.1 %copy-start.15 = (bf16[1,4,1,6,24,512]{5,4,3,2,1,0:T(8,128)(2,1)S(1)}, bf16[1,4,1,6,24,512]{5,4,3,2,1,0:T(8,128)(2,1)}, u32[]{:S(2)}) copy-start(bf16[1,4,1,6,24,512]{5,4,3,2,1,0:T(8,128)(2,1)} %get-tuple-element.17) | copy-start | bytes 1769476
  17.8 98.8 %collective-permute-start.9 = (bf16[1,8,3,48,512]{4,3,2,1,0:T(8,128)(2,1)}, bf16[1,8,3,48,512]{4,3,2,1,0:T(8,128)(2,1)}, u32[]{:S(2)}, u32[]{:S(2)}) collective-permute-start(bf16[1,8,3,48,512]{4,3,2,1,0:T(8,128)(2,1)} %bitcast.225), channel_id=1, source_target_pairs={{0,64},{64,0},{1,65},{65,1},{2,66},{66,2},{3,67},{67,3},{4,68},{68... | collective-permute-start | bytes 3538952 | tf_op jit(solution)/shard_map/ppermute | solution.py:18
  43.7 1.4 copy-start.4
  45.2 7.2 %collective-permute-start.2 = (bf16[32,512]{1,0:T(8,128)(2,1)S(1)}, bf16[32,512]{1,0:T(8,128)(2,1)S(1)}, u32[]{:S(2)}, u32[]{:S(2)}) collective-permute-start(bf16[32,512]{1,0:T(8,128)(2,1)S(1)} %fusion.42), channel_id=1, source_target_pairs={{0,32},{32,0},{1,33},{33,1},{2,34},{34,2},{3,35},{35,3},{4,36},{36... | collective-permute-start | bytes 98312 | tf_op jit(solution)/shard_map/ppermute | solution.py:18
  45.2 8.5 %copy-start.18 = (s32[4,4]{1,0:T(4,128)S(1)}, s32[4,4]{1,0:T(4,128)}, u32[]{:S(2)}) copy-start(s32[4,4]{1,0:T(4,128)} %param.9) | copy-start | bytes 196
  47.7 30.7 %copy-start.9 = (bf16[1,3,176,512]{3,2,1,0:T(8,128)(2,1)}, bf16[1,3,176,512]{3,2,1,0:T(8,128)(2,1)S(1)}, u32[]{:S(2)}) copy-start(bf16[1,3,176,512]{3,2,1,0:T(8,128)(2,1)S(1)} %get-tuple-element.26) | copy-start | bytes 1622020
  47.7 17.3 %collective-permute-start.13 = (bf16[3,176,512]{2,1,0:T(8,128)(2,1)}, bf16[3,176,512]{2,1,0:T(8,128)(2,1)S(1)}, u32[]{:S(2)}, u32[]{:S(2)}) collective-permute-start(bf16[3,176,512]{2,1,0:T(8,128)(2,1)} %get-tuple-element.27), channel_id=1, source_target_pairs={{0,16},{8,24},{16,0},{24,8},{1,17},{9,25},{17,1},{25,9},{2,18},{10... | collective-permute-start | bytes 1622024 | tf_op jit(solution)/shard_map/ppermute | solution.py:247
  51.7 25.5 %collective-permute-start.12 = (bf16[3,176,512]{2,1,0:T(8,128)(2,1)S(1)}, bf16[3,176,512]{2,1,0:T(8,128)(2,1)S(1)}, u32[]{:S(2)}, u32[]{:S(2)}) collective-permute-start(bf16[3,176,512]{2,1,0:T(8,128)(2,1)S(1)} %get-tuple-element.28), channel_id=1, source_target_pairs={{0,24},{8,0},{16,8},{24,16},{1,25},{9,1},{17,9},{25,17},{2,26},{10... | collective-permute-start | bytes 1622024 | tf_op jit(solution)/shard_map/ppermute | solution.py:247
  52.4 24.8 %collective-permute-start.11 = (bf16[3,176,512]{2,1,0:T(8,128)(2,1)S(1)}, bf16[3,176,512]{2,1,0:T(8,128)(2,1)S(1)}, u32[]{:S(2)}, u32[]{:S(2)}) collective-permute-start(bf16[3,176,512]{2,1,0:T(8,128)(2,1)S(1)} %get-tuple-element.29), channel_id=1, source_target_pairs={{0,8},{8,16},{16,24},{24,0},{1,9},{9,17},{17,25},{25,1},{2,10},{10... | collective-permute-start | bytes 1622024 | tf_op jit(solution)/shard_map/ppermute | solution.py:247
  54.0 37.6 %copy-start.6 = (bf16[32,512]{1,0:T(8,128)(2,1)}, bf16[32,512]{1,0:T(8,128)(2,1)S(1)}, u32[]{:S(2)}) copy-start(bf16[32,512]{1,0:T(8,128)(2,1)S(1)} %add.195.refs_1_) | copy-start | bytes 98308
  65.0 12.1 %copy-start.10 = (bf16[3,176,512]{2,1,0:T(8,128)(2,1)}, bf16[3,176,512]{2,1,0:T(8,128)(2,1)S(1)}, u32[]{:S(2)}) copy-start(bf16[3,176,512]{2,1,0:T(8,128)(2,1)S(1)} %collective-permute-done.13) | copy-start | bytes 1622020
  77.2 0.8 copy-start.11
  77.2 1.0 copy-start.12
  78.5 65.2 %collective-permute-start.14 = (bf16[4,3,128,512]{3,2,1,0:T(8,128)(2,1)S(1)}, bf16[4,3,128,512]{3,2,1,0:T(8,128)(2,1)S(1)}, u32[]{:S(2)}, u32[]{:S(2)}) collective-permute-start(bf16[4,3,128,512]{3,2,1,0:T(8,128)(2,1)S(1)} %slice.143.own), channel_id=1, source_target_pairs={{0,32},{32,0},{1,33},{33,1},{2,34},{34,2},{3,35},{35,3},{4,36},{36... | collective-permute-start | bytes 4718600 | tf_op jit(solution)/shard_map/ppermute | solution.py:18
  89.1 1.9 slice-start
  91.6 1.4 copy-start.5
  93.7 1.1 copy-start.3
  111.6 11.6 %collective-permute-start.3 = (f32[4,2,80,128]{3,2,1,0:T(8,128)}, f32[4,2,80,128]{3,2,1,0:T(8,128)}, u32[]{:S(2)}, u32[]{:S(2)}) collective-permute-start(f32[4,2,80,128]{3,2,1,0:T(8,128)} %get-tuple-element.30), channel_id=1, source_target_pairs={{0,2},{2,4},{4,6},{6,0},{1,3},{3,5},{5,7},{7,1},{8,10},{10,12},{12... | collective-permute-start | bytes 983048 | tf_op jit(solution)/shard_map/ppermute | solution.py:263
  113.1 16.4 %collective-permute-start.4 = (f32[4,2,80,128]{3,2,1,0:T(8,128)}, f32[4,2,80,128]{3,2,1,0:T(8,128)}, u32[]{:S(2)}, u32[]{:S(2)}) collective-permute-start(f32[4,2,80,128]{3,2,1,0:T(8,128)} %get-tuple-element.31), channel_id=1, source_target_pairs={{0,6},{2,0},{4,2},{6,4},{1,7},{3,1},{5,3},{7,5},{8,14},{10,8},{12,... | collective-permute-start | bytes 983048 | tf_op jit(solution)/shard_map/ppermute | solution.py:263
  114.8 16.4 %collective-permute-start.5 = (f32[4,2,80,128]{3,2,1,0:T(8,128)}, f32[4,2,80,128]{3,2,1,0:T(8,128)}, u32[]{:S(2)}, u32[]{:S(2)}) collective-permute-start(f32[4,2,80,128]{3,2,1,0:T(8,128)} %get-tuple-element.32), channel_id=1, source_target_pairs={{0,4},{2,6},{4,0},{6,2},{1,5},{3,7},{5,1},{7,3},{8,12},{10,14},{12... | collective-permute-start | bytes 983048 | tf_op jit(solution)/shard_map/ppermute | solution.py:263
  118.0 34.9 %collective-permute-start.10 = (bf16[1,8,3,48,512]{4,3,2,1,0:T(8,128)(2,1)}, bf16[1,8,3,48,512]{4,3,2,1,0:T(8,128)(2,1)}, u32[]{:S(2)}, u32[]{:S(2)}) collective-permute-start(bf16[1,8,3,48,512]{4,3,2,1,0:T(8,128)(2,1)} %hold.8), channel_id=1, source_target_pairs={{0,64},{64,0},{1,65},{65,1},{2,66},{66,2},{3,67},{67,3},{4,68},{68... | collective-permute-start | bytes 3538952 | tf_op jit(solution)/shard_map/ppermute | solution.py:18
  134.3 6.9 %collective-permute-start.6 = (f32[2,80,128]{2,1,0:T(8,128)S(1)}, f32[2,80,128]{2,1,0:T(8,128)S(1)}, u32[]{:S(2)}, u32[]{:S(2)}) collective-permute-start(f32[2,80,128]{2,1,0:T(8,128)S(1)} %get-tuple-element.36), channel_id=1, source_target_pairs={{0,8},{8,16},{16,24},{24,0},{1,9},{9,17},{17,25},{25,1},{2,10},{10... | collective-permute-start | bytes 245768 | tf_op jit(solution)/shard_map/ppermute | solution.py:247
  135.1 7.7 %collective-permute-start.8 = (f32[2,80,128]{2,1,0:T(8,128)S(1)}, f32[2,80,128]{2,1,0:T(8,128)S(1)}, u32[]{:S(2)}, u32[]{:S(2)}) collective-permute-start(f32[2,80,128]{2,1,0:T(8,128)S(1)} %get-tuple-element.37), channel_id=1, source_target_pairs={{0,16},{8,24},{16,0},{24,8},{1,17},{9,25},{17,1},{25,9},{2,18},{10... | collective-permute-start | bytes 245768 | tf_op jit(solution)/shard_map/ppermute | solution.py:247
  138.2 4.6 %collective-permute-start.7 = (f32[2,80,128]{2,1,0:T(8,128)S(1)}, f32[2,80,128]{2,1,0:T(8,128)S(1)}, u32[]{:S(2)}, u32[]{:S(2)}) collective-permute-start(f32[2,80,128]{2,1,0:T(8,128)S(1)} %get-tuple-element.38), channel_id=1, source_target_pairs={{0,24},{8,0},{16,8},{24,16},{1,25},{9,1},{17,9},{25,17},{2,26},{10... | collective-permute-start | bytes 245768 | tf_op jit(solution)/shard_map/ppermute | solution.py:247
  141.2 31.3 %collective-permute-start.18 = (bf16[1,8,3,48,512]{4,3,2,1,0:T(8,128)(2,1)}, bf16[1,8,3,48,512]{4,3,2,1,0:T(8,128)(2,1)}, u32[]{:S(2)}, u32[]{:S(2)}) collective-permute-start(bf16[1,8,3,48,512]{4,3,2,1,0:T(8,128)(2,1)} %hold.9), channel_id=1, source_target_pairs={{0,64},{64,0},{1,65},{65,1},{2,66},{66,2},{3,67},{67,3},{4,68},{68... | collective-permute-start | bytes 3538952 | tf_op jit(solution)/shard_map/ppermute | solution.py:18
  143.7 0.6 copy-start.13
  144.3 4.6 %copy-start = (bf16[4,4,2,6,64,512]{5,4,3,2,1,0:T(8,128)(2,1)S(1)}, bf16[4,4,2,6,64,512]{5,4,3,2,1,0:T(8,128)(2,1)}, u32[]{:S(2)}) copy-start(bf16[4,4,2,6,64,512]{5,4,3,2,1,0:T(8,128)(2,1)} %get-tuple-element.14) | copy-start | bytes 37748740
  157.6 6.7 %collective-permute-start.15 = (f32[4,48,128]{2,1,0:T(8,128)}, f32[4,48,128]{2,1,0:T(8,128)}, u32[]{:S(2)}, u32[]{:S(2)}) collective-permute-start(f32[4,48,128]{2,1,0:T(8,128)} %get-tuple-element.33), channel_id=1, source_target_pairs={{0,8},{8,16},{16,24},{24,0},{1,9},{9,17},{17,25},{25,1},{2,10},{10... | collective-permute-start | bytes 294920 | tf_op jit(solution)/shard_map/ppermute | solution.py:247
  158.6 5.8 %collective-permute-start.16 = (f32[4,48,128]{2,1,0:T(8,128)}, f32[4,48,128]{2,1,0:T(8,128)}, u32[]{:S(2)}, u32[]{:S(2)}) collective-permute-start(f32[4,48,128]{2,1,0:T(8,128)} %get-tuple-element.34), channel_id=1, source_target_pairs={{0,24},{8,0},{16,8},{24,16},{1,25},{9,1},{17,9},{25,17},{2,26},{10... | collective-permute-start | bytes 294920 | tf_op jit(solution)/shard_map/ppermute | solution.py:247
  160.9 6.4 %collective-permute-start.17 = (f32[4,48,128]{2,1,0:T(8,128)}, f32[4,48,128]{2,1,0:T(8,128)}, u32[]{:S(2)}, u32[]{:S(2)}) collective-permute-start(f32[4,48,128]{2,1,0:T(8,128)} %get-tuple-element.35), channel_id=1, source_target_pairs={{0,16},{8,24},{16,0},{24,8},{1,17},{9,25},{17,1},{25,9},{2,18},{10... | collective-permute-start | bytes 294920 | tf_op jit(solution)/shard_map/ppermute | solution.py:247
  162.8 22.4 %collective-permute-start.19 = (bf16[1,4,3,48,512]{4,3,2,1,0:T(8,128)(2,1)}, bf16[1,4,3,48,512]{4,3,2,1,0:T(8,128)(2,1)}, u32[]{:S(2)}, u32[]{:S(2)}) collective-permute-start(bf16[1,4,3,48,512]{4,3,2,1,0:T(8,128)(2,1)} %hold.10), channel_id=1, source_target_pairs={{0,64},{64,0},{1,65},{65,1},{2,66},{66,2},{3,67},{67,3},{4,68},{68... | collective-permute-start | bytes 1769480 | tf_op jit(solution)/shard_map/ppermute | solution.py:18
  168.3 12.8 %copy-start.16 = (f32[4,48,128]{2,1,0:T(8,128)}, f32[4,48,128]{2,1,0:T(8,128)S(1)}, u32[]{:S(2)}) copy-start(f32[4,48,128]{2,1,0:T(8,128)S(1)} %fusion.17) | copy-start | bytes 294916
  172.5 4.6 %copy-start.1 = (bf16[4,4,2,6,64,512]{5,4,3,2,1,0:T(8,128)(2,1)S(1)}, bf16[4,4,2,6,64,512]{5,4,3,2,1,0:T(8,128)(2,1)}, u32[]{:S(2)}) copy-start(bf16[4,4,2,6,64,512]{5,4,3,2,1,0:T(8,128)(2,1)} %get-tuple-element.14) | copy-start | bytes 37748740
  181.7 23.3 %collective-permute-start.23 = (bf16[4,3,48,512]{3,2,1,0:T(8,128)(2,1)}, bf16[4,3,48,512]{3,2,1,0:T(8,128)(2,1)}, u32[]{:S(2)}, u32[]{:S(2)}) collective-permute-start(bf16[4,3,48,512]{3,2,1,0:T(8,128)(2,1)} %hold.11), channel_id=1, source_target_pairs={{0,64},{64,0},{1,65},{65,1},{2,66},{66,2},{3,67},{67,3},{4,68},{68... | collective-permute-start | bytes 1769480 | tf_op jit(solution)/shard_map/ppermute | solution.py:18
  185.2 4.6 %copy-start.2 = (bf16[4,4,2,6,64,512]{5,4,3,2,1,0:T(8,128)(2,1)S(1)}, bf16[4,4,2,6,64,512]{5,4,3,2,1,0:T(8,128)(2,1)}, u32[]{:S(2)}) copy-start(bf16[4,4,2,6,64,512]{5,4,3,2,1,0:T(8,128)(2,1)} %get-tuple-element.14) | copy-start | bytes 37748740
  189.7 0.7 copy-start.8
  194.8 5.9 %collective-permute-start.20 = (f32[3,48,128]{2,1,0:T(8,128)}, f32[3,48,128]{2,1,0:T(8,128)}, u32[]{:S(2)}, u32[]{:S(2)}) collective-permute-start(f32[3,48,128]{2,1,0:T(8,128)} %get-tuple-element.39), channel_id=1, source_target_pairs={{0,8},{8,16},{16,24},{24,0},{1,9},{9,17},{17,25},{25,1},{2,10},{10... | collective-permute-start | bytes 221192 | tf_op jit(solution)/shard_map/ppermute | solution.py:247
  195.6 5.1 %collective-permute-start.21 = (f32[3,48,128]{2,1,0:T(8,128)}, f32[3,48,128]{2,1,0:T(8,128)}, u32[]{:S(2)}, u32[]{:S(2)}) collective-permute-start(f32[3,48,128]{2,1,0:T(8,128)} %get-tuple-element.40), channel_id=1, source_target_pairs={{0,24},{8,0},{16,8},{24,16},{1,25},{9,1},{17,9},{25,17},{2,26},{10... | collective-permute-start | bytes 221192 | tf_op jit(solution)/shard_map/ppermute | solution.py:247
  198.0 6.0 %collective-permute-start.22 = (f32[3,48,128]{2,1,0:T(8,128)S(1)}, f32[3,48,128]{2,1,0:T(8,128)}, u32[]{:S(2)}, u32[]{:S(2)}) collective-permute-start(f32[3,48,128]{2,1,0:T(8,128)S(1)} %get-tuple-element.41), channel_id=1, source_target_pairs={{0,16},{8,24},{16,0},{24,8},{1,17},{9,25},{17,1},{25,9},{2,18},{10... | collective-permute-start | bytes 221192 | tf_op jit(solution)/shard_map/ppermute | solution.py:247
  205.0 3.4 %copy-start.17 = (f32[4,48,128]{2,1,0:T(8,128)S(1)}, f32[4,48,128]{2,1,0:T(8,128)}, u32[]{:S(2)}) copy-start(f32[4,48,128]{2,1,0:T(8,128)} %copy-done.16) | copy-start | bytes 294916
  205.0 10.3 %copy-start.14 = (f32[2,80,128]{2,1,0:T(8,128)S(1)}, f32[2,80,128]{2,1,0:T(8,128)}, u32[]{:S(2)}) copy-start(f32[2,80,128]{2,1,0:T(8,128)} %copy-done.13) | copy-start | bytes 245764
  205.0 13.6 %copy-start.7 = (bf16[32,512]{1,0:T(8,128)(2,1)S(1)}, bf16[32,512]{1,0:T(8,128)(2,1)}, u32[]{:S(2)}) copy-start(bf16[32,512]{1,0:T(8,128)(2,1)} %copy-done.6) | copy-start | bytes 98308
  208.4 5.4 %collective-permute-start.24 = (f32[2,48,128]{2,1,0:T(8,128)S(1)}, f32[2,48,128]{2,1,0:T(8,128)S(1)}, u32[]{:S(2)}, u32[]{:S(2)}) collective-permute-start(f32[2,48,128]{2,1,0:T(8,128)S(1)} %get-tuple-element.42), channel_id=1, source_target_pairs={{0,2},{2,4},{4,6},{6,0},{1,3},{3,5},{5,7},{7,1},{8,10},{10,12},{12... | collective-permute-start | bytes 147464 | tf_op jit(solution)/shard_map/ppermute | solution.py:263
  209.1 5.6 %collective-permute-start.26 = (f32[2,48,128]{2,1,0:T(8,128)S(1)}, f32[2,48,128]{2,1,0:T(8,128)S(1)}, u32[]{:S(2)}, u32[]{:S(2)}) collective-permute-start(f32[2,48,128]{2,1,0:T(8,128)S(1)} %get-tuple-element.43), channel_id=1, source_target_pairs={{0,4},{2,6},{4,0},{6,2},{1,5},{3,7},{5,1},{7,3},{8,12},{10,14},{12... | collective-permute-start | bytes 147464 | tf_op jit(solution)/shard_map/ppermute | solution.py:263
  211.1 4.1 %collective-permute-start.25 = (f32[2,48,128]{2,1,0:T(8,128)S(1)}, f32[2,48,128]{2,1,0:T(8,128)S(1)}, u32[]{:S(2)}, u32[]{:S(2)}) collective-permute-start(f32[2,48,128]{2,1,0:T(8,128)S(1)} %get-tuple-element.44), channel_id=1, source_target_pairs={{0,6},{2,0},{4,2},{6,4},{1,7},{3,1},{5,3},{7,5},{8,14},{10,8},{12,... | collective-permute-start | bytes 147464 | tf_op jit(solution)/shard_map/ppermute | solution.py:263
  215.3 5.8 %collective-permute-start.27 = (f32[128,128]{1,0:T(8,128)S(1)}, f32[128,128]{1,0:T(8,128)S(1)}, u32[]{:S(2)}, u32[]{:S(2)}) collective-permute-start(f32[128,128]{1,0:T(8,128)S(1)} %fusion.36), channel_id=1, source_target_pairs={{0,1},{1,0},{2,3},{3,2},{4,5},{5,4},{6,7},{7,6},{8,9},{9,8},{10,11... | collective-permute-start | bytes 196616 | tf_op jit(solution)/shard_map/ppermute | solution.py:18
  221.2 1.3 collective-permute-start.28

commit v8 on v7

--- a/solution.py
+++ b/solution.py
@@ -231,7 +231,7 @@
         in_specs=in_specs,
         out_specs=out_specs,
         out_shape=out_shape,
-        compiler_params=pltpu.CompilerParams(vmem_limit_bytes=(60 if size == 4 else 40) * 2**20),
+        compiler_params=pltpu.CompilerParams(vmem_limit_bytes=60 * 2**20),
         cost_estimate=HINT,
         name="project",
     )(*cols, own, other, *after)
@@ -282,12 +282,11 @@
     first_part = front(sols, vecs, source_index, source_time, group)
     raw = swap(first_part, "yl")
     other = swap(vecs, "c")
-    parts = ((0, 1, 0, 2), (1, 1, 0, 2), (2, 1, 0, 2), (3, 1, 0, 1), (3, 1, 1, 1))
+    parts = ((0, 2, 0, 2), (2, 1, 0, 2), (3, 1, 0, 1), (3, 1, 1, 1))
     sent = [(RAW, count, *part) for part in parts]
     mine, *send = by_time(sols, ((0, count, 0, 4, 0, 2), *sent), mark(first_part))
     send = [rows_of(part) for part in send]
     got = [swap(send[0], "yl"), swap(hold(send[1], raw), "yl")]
-    got += [swap(hold(send[2], got[0]), "yl"), swap(hold(send[3], got[1]), "yl")]
 
     whole, late = (0, owned, 0, 4, 0, 2), (0, owned, 3, 1, 1, 1)
     own, own_late = by_time(vecs, (whole, late), mark(send[0]))
@@ -301,24 +300,28 @@
         out = project([part], own, other, x, y, step, *map(mark, after))[0]
         return out.reshape(out.shape[0], 4, -1, 2 * (count - RAW), 2 * owned)
 
-    slabs = [v.reshape(4, comps // 2, -1, sites) for v in (send[4], own_late)]
-    spread = jnp.stack(share_z(hold(jnp.concatenate(slabs, axis=2), raw)))
-    cut = send[4].shape[3]
+    first = project([rows_of(mine), raw_rows], own, other, 0, 0, 8)
+
+    slabs = [v.reshape(4, comps // 2, -1, sites) for v in (send[3], own_late)]
+    spread = share_z(hold(jnp.concatenate(slabs, axis=2), raw, other))
+    spread[1] = hold(spread[1], first[0])
+    spread = jnp.stack(spread)
+    cut = send[3].shape[3]
     spread_s, spread_v = spread[:, :, :cut], spread[:, :, cut:]
     spread_w = swap(spread_v, "c")
 
-    first = project([rows_of(mine), raw_rows], own, other, 0, 0, 8)
     first = [v.reshape(4, 4, 2, -1, 2 * owned) for v in first]
     first = sum_x(jnp.concatenate(first, axis=3))
     first = sum_z(hold(first, spread_v))
 
-    early = [against(got[0], 0, 0, 4, first), against(got[1], 1, 0, 4, first, spread_w)]
-    early = sum_z(jnp.concatenate([v[0] for v in early], axis=1))
-    mid = [against(got[2], 2, 0, 4, early)[0]]
+    got.append(swap(hold(send[2], got[0]), "yl"))
+    early = against(got[0], 0, 0, 8, first, spread_w)
+    early = sum_z(jnp.swapaxes(early, 0, 1)).reshape(4, -1, 2 * owned)
+    mid = [against(got[1], 2, 0, 4, early)[0]]
     got.append(swap(hold(spread_s, mid[0]), "yl"))
-    mid.append(against(got[3], 3, 0, 1, mid[0])[0])
+    mid.append(against(got[2], 3, 0, 1, mid[0])[0])
     mid = sum_z(jnp.concatenate(mid, axis=1))
-    last = project_pieces(got[4], spread_v, spread_w)
+    last = project_pieces(got[3], spread_v, spread_w)
     last = last.reshape(1, -1, 2 * owned)
     late = sum_x(jnp.concatenate([early, mid, last]).reshape(4, 2, -1, 2 * owned))
 

time: 226 us -> 195 us (0.86)
  waiting for transfers between devices: 64.1 us -> 40.2 us
  local copies, waits for them, and re-layouts: 34.5 us -> 25.4 us
  starting transfers between devices: 40.4 us -> 37.9 us
  other arithmetic: 17.1 us -> 19.4 us
    ppermute x12, waiting for transfers between devices: 30.8 us -> 9.55 us  [share_z(): lax.ppermute(pick(slabs, (me + k) % 4), 'z', [(i, (i + k) % 4) for i in r...]
    unnamed x40 -> x26, local copies, waits for them, and re-layouts: 19.4 us -> 3.37 us
    ppermute x11 -> x10, waiting for transfers between devices: 20.9 us -> 16.3 us  [swap(): return lax.ppermute(value, axis, SWAP)]
    ppermute x11 -> x10, starting transfers between devices: 12 us -> 8.95 us  [swap(): return lax.ppermute(value, axis, SWAP)]
    pallas_call x5 -> x4, Pallas kernels: 30.2 us -> 32.4 us  [project(): pl.pallas_call(functools.partial(dot_kernel, len(cols)), grid=(size, inne...]
    slice x3 -> x4, local copies, waits for them, and re-layouts: 2.5 us -> 4.58 us  [mark(): value = value[0]]
  transfers between devices with their start and end apart: 29 -> 28, of which waited for: 16 -> 17; matrix products, arithmetic and copies ran while one was open for 13% -> 20% of each run, Pallas kernels for 28% -> 34%
where the time goes in v8:
time: 195 us; the launch traced here: 193 us
  Pallas kernels  68.1 us (35%)
  waiting for transfers between devices  40.2 us (21%)
  starting transfers between devices  37.9 us (19%)
  local copies, waits for them, and re-layouts  25.4 us (13%)
  other arithmetic  19.4 us (10%)
    pallas_call x4, Pallas kernels, project(): pl.pallas_call(functools.partial(dot_kernel, len(cols)), grid=(size, inne...  32.4 us
    pallas_call x4, Pallas kernels, by_time(): pl.pallas_call(functools.partial(by_time_kernel, cuts), grid=(4,), in_spe...  29.4 us
    ppermute x12, starting transfers between devices, share_z(): lax.ppermute(pick(slabs, (me + k) % 4), 'z', [(i, (i + k) % 4) for i in r...  20.1 us
    ppermute x10, waiting for transfers between devices, swap(): return lax.ppermute(value, axis, SWAP)  16.3 us
    ppermute x6, waiting for transfers between devices, sum_x(): total = total + lax.ppermute(pick(slabs, (me + k) % 4), 'x', pairs)  14.3 us
    ppermute x12, waiting for transfers between devices, share_z(): lax.ppermute(pick(slabs, (me + k) % 4), 'z', [(i, (i + k) % 4) for i in r...  9.55 us
    squeeze x10, local copies, waits for them, and re-layouts, mark(): value = value[0]  9.52 us
    ppermute x10, starting transfers between devices, swap(): return lax.ppermute(value, axis, SWAP)  8.95 us
  transfers between devices with their start and end apart: 28, of which 17 were waited for; matrix products, arithmetic and copies ran while one was open for 20% of the time, Pallas kernels for 34%

profile of v8, /device:TPU:0, one launch (start us, length us, event | category | flops | bytes accessed | tf_op | source)
XLA Modules:
  0.0 192.6 jit_solution(5872229435875620936)
XLA Ops:
  1.4 1.2 pad_add_fusion.at
  2.6 2.9 %front.1 = bf16[49,4,8,512]{3,2,1,0:T(8,128)(2,1)} custom-call(s32[6]{0:T(128)} %pad_add_fusion.at, bf16[192,4,8,512]{3,2,1,0:T(8,128)(2,1)} %bitcast.180, bf16[64,6,32,512]{3,2,1,0:T(8,128)(2,1)} %bitcast.178), custom_call_target="tpu_custom_call" | custom-call | flops 1000 | bytes 1000 | tf_op jit(solution)/shard_map/front/pallas_call | solution.py:133
  5.6 1.7 collective-permute-start
  7.3 1.4 slice_bitcast_fusion.8.refs_0_
  8.7 7.6 %by_time.4 = (bf16[4,4,2,6,32,512]{5,4,3,2,1,0:T(8,128)(2,1)}, bf16[2,4,2,6,24,512]{5,4,3,2,1,0:T(8,128)(2,1)}, bf16[1,4,2,6,24,512]{5,4,3,2,1,0:T(8,128)(2,1)},...) custom-call(bf16[32,6,32,512]{3,2,1,0:T(8,128)(2,1)} %bitcast.181, ...), custom_call_target="tpu_custom_call" | custom-call | flops 1000 | bytes 1000 | tf_op jit(solution)/shard_map/by_time/pallas_call | solution.py:48
  16.4 1.3 slice.125
  18.7 10.6 %by_time.7 = (bf16[4,4,2,6,64,512]{5,4,3,2,1,0:T(8,128)(2,1)}, bf16[1,4,1,6,64,512]{5,4,3,2,1,0:T(8,128)(2,1)}) custom-call(bf16[64,6,32,512]{3,2,1,0:T(8,128)(2,1)} %bitcast.179, bf16[48,512]{1,0:T(8,128)(2,1)} %slice_bitcast_fusion.3.refs_0_), custom_call_target="tpu_custom_call" | custom-call | flops 1000 | bytes 1000 | tf_op jit(solution)/shard_map/by_time/pallas_call | solution.py:48
  29.4 2.9 %pad_maximum_fusion.refs_0_ = bf16[4,3,176,512]{3,2,1,0:T(8,128)(2,1)} fusion(bf16[4,3,128,512]{3,2,1,0:T(8,128)(2,1)} %bitcast.190, bf16[4,3,48,512]{3,2,1,0:T(8,128)(2,1)S(1)} %bitcast.201), kind=kLoop, calls=%fused_computation.5 | loop fusion | flops 4325376 | bytes 4325376 | tf_op jit(solution)/shard_map/concatenate | solution.py:306
  32.2 11.5 %collective-permute-done.block = bf16[49,32,512]{2,1,0:T(8,128)(2,1)S(1)} collective-permute-done((bf16[49,32,512]{2,1,0:T(8,128)(2,1)}, bf16[49,32,512]{2,1,0:T(8,128)(2,1)S(1)}, u32[]{:S(2)}, u32[]{:S(2)}) %collective-permute-start) | collective-permute-done | bytes 1605664 | tf_op jit(solution)/shard_map/ppermute | solution.py:18
  44.4 10.4 %by_time.5 = bf16[4,4,2,6,64,512]{5,4,3,2,1,0:T(8,128)(2,1)} custom-call(bf16[64,6,32,512]{3,2,1,0:T(8,128)(2,1)} %collective-permute-done.1.block), custom_call_target="tpu_custom_call" | custom-call | flops 1000 | bytes 1000 | tf_op jit(solution)/shard_map/by_time/pallas_call | solution.py:48
  54.8 1.9 slice-done
  57.4 2.8 %constant_dynamic-slice_fusion.1 = (bf16[1,3,176,512]{3,2,1,0:T(8,128)(2,1)S(1)}, bf16[3,176,512]{2,1,0:T(8,128)(2,1)}, bf16[3,176,512]{2,1,0:T(8,128)(2,1)}, bf16[3,176,512]{2,1,0:T(8,128)(2,1)}) fusion(bf16[4,3,176,512]{3,2,1,0:T(8,128)(2,1)} %hold.6, s32[]{:T(128)S(6)} %select_n.157, s32[]{:T(128)S(6)} %select_n.163, s32[]{:T(128)S(6)} %select_n.161, ...), kind=kLoop, calls=%fused_computation.93 | loop fusion | bytes 4325392 | tf_op jit(solution)/shard_map/jit(dynamic_index_in_dim)/dynamic_slice | solution.py:241
  60.2 2.0 %collective-permute-start.10 = (bf16[3,176,512]{2,1,0:T(8,128)(2,1)}, bf16[3,176,512]{2,1,0:T(8,128)(2,1)S(1)}, u32[]{:S(2)}, u32[]{:S(2)}) collective-permute-start(bf16[3,176,512]{2,1,0:T(8,128)(2,1)} %get-tuple-element.27), channel_id=1, source_target_pairs={{0,8},{8,16},{16,24},{24,0},{1,9},{9,17},{17,25},{25,1},{2,10},{10... | collective-permute-start | bytes 1622024 | tf_op jit(solution)/shard_map/ppermute | solution.py:247
  62.2 3.6 %collective-permute-start.12 = (bf16[3,176,512]{2,1,0:T(8,128)(2,1)}, bf16[3,176,512]{2,1,0:T(8,128)(2,1)}, u32[]{:S(2)}, u32[]{:S(2)}) collective-permute-start(bf16[3,176,512]{2,1,0:T(8,128)(2,1)} %get-tuple-element.25), channel_id=1, source_target_pairs={{0,16},{8,24},{16,0},{24,8},{1,17},{9,25},{17,1},{25,9},{2,18},{10... | collective-permute-start | bytes 1622024 | tf_op jit(solution)/shard_map/ppermute | solution.py:247
  65.8 1.0 collective-permute-start.11
  67.6 1.2 collective-permute-done.2
  69.5 1.2 copy-done
  70.7 14.7 %project.4 = (f32[4,8,2,32,128]{4,3,2,1,0:T(8,128)}, f32[4,8,2,8,128]{4,3,2,1,0:T(8,128)}) custom-call(bf16[4,8,3,64,512]{4,3,2,1,0:T(8,128)(2,1)} %bitcast.182, bf16[4,8,3,16,512]{4,3,2,1,0:T(8,128)(2,1)} %bitcast.165, bf16[4,8,3,128,512]{4,3,2,1,0:T(8,128)(2,1)} %bitcast.173, bf16[4,8,3,128,512]{4,3,2,1,0:T(8,128)(2,1)} %bitcast.168), custom_call_target="tpu_custom_call" | custom-call | flops 1000 | bytes 1000 | tf_op jit(solution)/shard_map/project/pallas_call | solution.py:228
  85.3 1.3 slice_bitcast_fusion.10.refs_1_
  87.5 1.7 collective-permute-done.12
  89.2 1.6 pad_maximum_fusion.1
  91.8 2.1 %fusion.8 = (f32[4,2,80,128]{3,2,1,0:T(8,128)}, f32[4,2,80,128]{3,2,1,0:T(8,128)}, f32[4,2,80,128]{3,2,1,0:T(8,128)}) fusion(s32[]{:T(128)S(6)} %select_n.152, f32[4,4,2,64,128]{4,3,2,1,0:T(8,128)} %bitcast.185, f32[4,4,2,16,128]{4,3,2,1,0:T(8,128)S(1)} %bitcast.194, s32[]{:T(128)S(6)} %select_n.154, s32[]{:T(128)S(6)} %select_n.156), kind=kLoop, calls=%fused_computation.32 | loop fusion | flops 245760 | bytes 2293772 | tf_op jit(solution)/shard_map/jit(dynamic_index_in_dim)/squeeze | solution.py:241
  93.9 1.5 collective-permute-start.3
  95.4 1.7 collective-permute-start.4
  97.1 1.8 collective-permute-start.5
  98.9 1.1 gather_fusion
  100.7 1.6 dynamic-slice_bitcast_fusion.3.refs_1_
  102.2 2.8 %collective-permute-done.3 = f32[4,2,80,128]{3,2,1,0:T(8,128)} collective-permute-done((f32[4,2,80,128]{3,2,1,0:T(8,128)}, f32[4,2,80,128]{3,2,1,0:T(8,128)}, u32[]{:S(2)}, u32[]{:S(2)}) %collective-permute-start.3) | collective-permute-done | bytes 327712 | tf_op jit(solution)/shard_map/ppermute | solution.py:263
  105.0 6.3 %collective-permute-done.4 = f32[4,2,80,128]{3,2,1,0:T(8,128)} collective-permute-done((f32[4,2,80,128]{3,2,1,0:T(8,128)}, f32[4,2,80,128]{3,2,1,0:T(8,128)}, u32[]{:S(2)}, u32[]{:S(2)}) %collective-permute-start.4) | collective-permute-done | bytes 327712 | tf_op jit(solution)/shard_map/ppermute | solution.py:263
  111.3 1.7 collective-permute-done.5
  113.0 2.0 %fusion.6.refs_0_ = f32[4,2,80,128]{3,2,1,0:T(8,128)} fusion(f32[4,2,80,128]{3,2,1,0:T(8,128)} %collective-permute-done.5, f32[4,2,80,128]{3,2,1,0:T(8,128)} %collective-permute-done.4, f32[4,2,80,128]{3,2,1,0:T(8,128)} %collective-permute-done.3, s32[]{:T(128)S(6)} %select_n.150, f32[4,4,2,64,128]{4,3,2,1,0:T(8,128)} %bitcast.186, ...), kind=kLoop, calls=%fused_computation.30 | loop fusion | flops 327680 | bytes 2621444 | tf_op jit(solution)/shard_map/add | solution.py:263
  115.0 1.6 collective-permute-start.17
  116.6 1.6 dynamic-slice_bitcast_fusion.9
  118.2 1.2 collective-permute-start.6
  119.3 2.5 %collective-permute-start.8 = (f32[2,80,128]{2,1,0:T(8,128)S(1)}, f32[2,80,128]{2,1,0:T(8,128)S(1)}, u32[]{:S(2)}, u32[]{:S(2)}) collective-permute-start(f32[2,80,128]{2,1,0:T(8,128)S(1)} %get-tuple-element.35), channel_id=1, source_target_pairs={{0,16},{8,24},{16,0},{24,8},{1,17},{9,25},{17,1},{25,9},{2,18},{10... | collective-permute-start | bytes 245768 | tf_op jit(solution)/shard_map/ppermute | solution.py:247
  121.8 1.2 collective-permute-start.7
  123.1 1.4 slice_bitcast_fusion.2.refs_1_
  125.3 1.0 collective-permute-done.7
  126.4 0.9 fusion.14
  129.1 8.1 %project.5 = f32[2,8,2,24,128]{4,3,2,1,0:T(8,128)} custom-call(bf16[2,8,3,48,512]{4,3,2,1,0:T(8,128)(2,1)} %collective-permute-done.9.refs_0_, bf16[4,8,3,128,512]{4,3,2,1,0:T(8,128)(2,1)} %bitcast.174, bf16[4,8,3,128,512]{4,3,2,1,0:T(8,128)(2,1)} %bitcast.169, f32[80,128]{1,0:T(8,128)} %slice_bitcast_fusion.4.refs_3_, ...), custom_call_target="tpu_custom_call" | custom-call | flops 1000 | bytes 1000 | tf_op jit(solution)/shard_map/project/pallas_call | solution.py:228
  137.2 1.0 dynamic-slice_bitcast_fusion.6
  138.2 1.0 collective-permute-start.14
  139.2 3.0 %collective-permute-start.16 = (f32[2,2,48,128]{3,2,1,0:T(8,128)S(1)}, f32[2,2,48,128]{3,2,1,0:T(8,128)S(1)}, u32[]{:S(2)}, u32[]{:S(2)}) collective-permute-start(f32[2,2,48,128]{3,2,1,0:T(8,128)S(1)} %get-tuple-element.32), channel_id=1, source_target_pairs={{0,16},{8,24},{16,0},{24,8},{1,17},{9,25},{17,1},{25,9},{2,18},{10... | collective-permute-start | bytes 294920 | tf_op jit(solution)/shard_map/ppermute | solution.py:247
  142.4 1.9 pad_maximum_fusion.2.refs_0_
  144.3 1.5 collective-permute-done.16
  145.8 1.0 collective-permute-done.15
  146.7 0.9 fusion.12
  148.3 5.1 %project.6 = f32[1,8,2,24,128]{4,3,2,1,0:T(8,128)} custom-call(bf16[1,8,3,48,512]{4,3,2,1,0:T(8,128)(2,1)} %collective-permute-done.17.refs_0_, bf16[4,8,3,128,512]{4,3,2,1,0:T(8,128)(2,1)} %bitcast.175, bf16[4,8,3,128,512]{4,3,2,1,0:T(8,128)(2,1)} %bitcast.170, f32[48,128]{1,0:T(8,128)} %slice_bitcast_fusion.9.refs_3_), custom_call_target="tpu_custom_call" | custom-call | flops 1000 | bytes 1000 | tf_op jit(solution)/shard_map/project/pallas_call | solution.py:228
  153.3 1.3 slice.158
  154.7 1.6 collective-permute-start.22
  156.6 4.6 %project.7 = f32[1,4,2,24,128]{4,3,2,1,0:T(8,128)} custom-call(bf16[1,4,3,48,512]{4,3,2,1,0:T(8,128)(2,1)} %collective-permute-done.18.refs_0_, bf16[4,8,3,128,512]{4,3,2,1,0:T(8,128)(2,1)} %bitcast.176, bf16[4,8,3,128,512]{4,3,2,1,0:T(8,128)(2,1)} %bitcast.171, f32[48,128]{1,0:T(8,128)} %bitcast.207), custom_call_target="tpu_custom_call" | custom-call | flops 1000 | bytes 1000 | tf_op jit(solution)/shard_map/project/pallas_call | solution.py:228
  161.2 1.5 fusion.23
  163.6 2.4 %collective-permute-start.20 = (f32[3,48,128]{2,1,0:T(8,128)}, f32[3,48,128]{2,1,0:T(8,128)}, u32[]{:S(2)}, u32[]{:S(2)}) collective-permute-start(f32[3,48,128]{2,1,0:T(8,128)} %get-tuple-element.38), channel_id=1, source_target_pairs={{0,24},{8,0},{16,8},{24,16},{1,25},{9,1},{17,9},{25,17},{2,26},{10... | collective-permute-start | bytes 221192 | tf_op jit(solution)/shard_map/ppermute | solution.py:247
  165.9 1.2 collective-permute-start.21
  168.6 3.5 %collective-permute-done.21 = f32[3,48,128]{2,1,0:T(8,128)} collective-permute-done((f32[3,48,128]{2,1,0:T(8,128)}, f32[3,48,128]{2,1,0:T(8,128)}, u32[]{:S(2)}, u32[]{:S(2)}) %collective-permute-start.21) | collective-permute-done | bytes 73760 | tf_op jit(solution)/shard_map/ppermute | solution.py:247
  172.1 1.0 fusion.21
  173.1 3.3 %project_pieces.1 = f32[2,24,128]{2,1,0:T(8,128)S(1)} custom-call(bf16[4,3,48,512]{3,2,1,0:T(8,128)(2,1)} %collective-permute-done.22.col, bf16[4,3,128,512]{3,2,1,0:T(8,128)(2,1)S(1)} %slice.154.own, bf16[4,3,128,512]{3,2,1,0:T(8,128)(2,1)S(1)} %collective-permute-done.13.other), custom_call_target="tpu_custom_call" | custom-call | flops 1000 | bytes 1000 | tf_op jit(solution)/shard_map/project_pieces/pallas_call | solution.py:201
  176.5 1.0 collective-permute-start.23
  177.5 2.3 %collective-permute-start.25 = (f32[2,48,128]{2,1,0:T(8,128)S(1)}, f32[2,48,128]{2,1,0:T(8,128)S(1)}, u32[]{:S(2)}, u32[]{:S(2)}) collective-permute-start(f32[2,48,128]{2,1,0:T(8,128)S(1)} %get-tuple-element.41), channel_id=1, source_target_pairs={{0,4},{2,6},{4,0},{6,2},{1,5},{3,7},{5,1},{7,3},{8,12},{10,14},{12... | collective-permute-start | bytes 147464 | tf_op jit(solution)/shard_map/ppermute | solution.py:263
  180.3 1.5 collective-permute-done.23
  181.9 1.2 collective-permute-done.25
  183.9 3.0 %collective-permute-start.26 = (f32[128,128]{1,0:T(8,128)S(1)}, f32[128,128]{1,0:T(8,128)S(1)}, u32[]{:S(2)}, u32[]{:S(2)}) collective-permute-start(f32[128,128]{1,0:T(8,128)S(1)} %fusion.27), channel_id=1, source_target_pairs={{0,1},{1,0},{2,3},{3,2},{4,5},{5,4},{6,7},{7,6},{8,9},{9,8},{10,11... | collective-permute-start | bytes 196616 | tf_op jit(solution)/shard_map/ppermute | solution.py:18
  187.7 2.1 %collective-permute-done.26 = f32[128,128]{1,0:T(8,128)S(1)} collective-permute-done((f32[128,128]{1,0:T(8,128)S(1)}, f32[128,128]{1,0:T(8,128)S(1)}, u32[]{:S(2)}, u32[]{:S(2)}) %collective-permute-start.26) | collective-permute-done | bytes 65568 | tf_op jit(solution)/shard_map/ppermute | solution.py:18
  189.9 1.2 collective-permute-done.27
  (90 shorter events, 15.9 us)
Async XLA Ops:
  0.6 43.7 %collective-permute-start.1 = (bf16[64,6,32,512]{3,2,1,0:T(8,128)(2,1)}, bf16[64,6,32,512]{3,2,1,0:T(8,128)(2,1)}, u32[]{:S(2)}, u32[]{:S(2)}) collective-permute-start(bf16[64,6,32,512]{3,2,1,0:T(8,128)(2,1)} %bitcast.177), channel_id=1, source_target_pairs={{0,32},{32,0},{1,33},{33,1},{2,34},{34,2},{3,35},{35,3},{4,36},{36... | collective-permute-start | bytes 37748744 | tf_op jit(solution)/shard_map/ppermute | solution.py:18
  5.6 38.2 %collective-permute-start = (bf16[49,32,512]{2,1,0:T(8,128)(2,1)}, bf16[49,32,512]{2,1,0:T(8,128)(2,1)S(1)}, u32[]{:S(2)}, u32[]{:S(2)}) collective-permute-start(bf16[49,32,512]{2,1,0:T(8,128)(2,1)} %bitcast.189), channel_id=1, source_target_pairs={{0,64},{64,0},{1,65},{65,1},{2,66},{66,2},{3,67},{67,3},{4,68},{68... | collective-permute-start | bytes 4816904 | tf_op jit(solution)/shard_map/ppermute | solution.py:18
  18.3 11.0 %copy-start.7 = (bf16[1,4,1,6,24,512]{5,4,3,2,1,0:T(8,128)(2,1)S(1)}, bf16[1,4,1,6,24,512]{5,4,3,2,1,0:T(8,128)(2,1)}, u32[]{:S(2)}) copy-start(bf16[1,4,1,6,24,512]{5,4,3,2,1,0:T(8,128)(2,1)} %get-tuple-element.16) | copy-start | bytes 1769476
  18.3 103.5 %collective-permute-start.9 = (bf16[2,8,3,48,512]{4,3,2,1,0:T(8,128)(2,1)}, bf16[2,8,3,48,512]{4,3,2,1,0:T(8,128)(2,1)}, u32[]{:S(2)}, u32[]{:S(2)}) collective-permute-start(bf16[2,8,3,48,512]{4,3,2,1,0:T(8,128)(2,1)} %bitcast.41), channel_id=1, source_target_pairs={{0,64},{64,0},{1,65},{65,1},{2,66},{66,2},{3,67},{67,3},{4,68},{68... | collective-permute-start | bytes 7077896 | tf_op jit(solution)/shard_map/ppermute | solution.py:18
  54.8 1.9 slice-start
  57.4 11.4 %copy-start.1 = (bf16[128,512]{1,0:T(8,128)(2,1)S(1)}, bf16[128,512]{1,0:T(8,128)(2,1)}, u32[]{:S(2)}) copy-start(bf16[128,512]{1,0:T(8,128)(2,1)} %slice_bitcast_fusion.1.refs_0_.refs_2_) | copy-start | bytes 393220
  60.2 29.0 %copy-start.4 = (bf16[1,3,176,512]{3,2,1,0:T(8,128)(2,1)}, bf16[1,3,176,512]{3,2,1,0:T(8,128)(2,1)S(1)}, u32[]{:S(2)}) copy-start(bf16[1,3,176,512]{3,2,1,0:T(8,128)(2,1)S(1)} %get-tuple-element.24) | copy-start | bytes 1622020
  60.2 26.4 %collective-permute-start.10 = (bf16[3,176,512]{2,1,0:T(8,128)(2,1)}, bf16[3,176,512]{2,1,0:T(8,128)(2,1)S(1)}, u32[]{:S(2)}, u32[]{:S(2)}) collective-permute-start(bf16[3,176,512]{2,1,0:T(8,128)(2,1)} %get-tuple-element.27), channel_id=1, source_target_pairs={{0,8},{8,16},{16,24},{24,0},{1,9},{9,17},{17,25},{25,1},{2,10},{10... | collective-permute-start | bytes 1622024 | tf_op jit(solution)/shard_map/ppermute | solution.py:247
  62.2 27.0 %collective-permute-start.12 = (bf16[3,176,512]{2,1,0:T(8,128)(2,1)}, bf16[3,176,512]{2,1,0:T(8,128)(2,1)}, u32[]{:S(2)}, u32[]{:S(2)}) collective-permute-start(bf16[3,176,512]{2,1,0:T(8,128)(2,1)} %get-tuple-element.25), channel_id=1, source_target_pairs={{0,16},{8,24},{16,0},{24,8},{1,17},{9,25},{17,1},{25,9},{2,18},{10... | collective-permute-start | bytes 1622024 | tf_op jit(solution)/shard_map/ppermute | solution.py:247
  65.8 23.4 %collective-permute-start.11 = (bf16[3,176,512]{2,1,0:T(8,128)(2,1)}, bf16[3,176,512]{2,1,0:T(8,128)(2,1)}, u32[]{:S(2)}, u32[]{:S(2)}) collective-permute-start(bf16[3,176,512]{2,1,0:T(8,128)(2,1)} %get-tuple-element.26), channel_id=1, source_target_pairs={{0,24},{8,0},{16,8},{24,16},{1,25},{9,1},{17,9},{25,17},{2,26},{10... | collective-permute-start | bytes 1622024 | tf_op jit(solution)/shard_map/ppermute | solution.py:247
  67.6 1.2 collective-permute-start.2
  69.5 1.2 copy-start
  86.7 0.8 copy-start.2
  90.8 0.7 copy-start.10
  90.8 1.0 copy-start.6
  91.0 37.0 %collective-permute-start.13 = (bf16[4,3,128,512]{3,2,1,0:T(8,128)(2,1)S(1)}, bf16[4,3,128,512]{3,2,1,0:T(8,128)(2,1)S(1)}, u32[]{:S(2)}, u32[]{:S(2)}) collective-permute-start(bf16[4,3,128,512]{3,2,1,0:T(8,128)(2,1)S(1)} %slice.154.own), channel_id=1, source_target_pairs={{0,32},{32,0},{1,33},{33,1},{2,34},{34,2},{3,35},{35,3},{4,36},{36... | collective-permute-start | bytes 4718600 | tf_op jit(solution)/shard_map/ppermute | solution.py:18
  93.9 11.1 %collective-permute-start.3 = (f32[4,2,80,128]{3,2,1,0:T(8,128)}, f32[4,2,80,128]{3,2,1,0:T(8,128)}, u32[]{:S(2)}, u32[]{:S(2)}) collective-permute-start(f32[4,2,80,128]{3,2,1,0:T(8,128)} %get-tuple-element.28), channel_id=1, source_target_pairs={{0,2},{2,4},{4,6},{6,0},{1,3},{3,5},{5,7},{7,1},{8,10},{10,12},{12... | collective-permute-start | bytes 983048 | tf_op jit(solution)/shard_map/ppermute | solution.py:263
  95.4 15.9 %collective-permute-start.4 = (f32[4,2,80,128]{3,2,1,0:T(8,128)}, f32[4,2,80,128]{3,2,1,0:T(8,128)}, u32[]{:S(2)}, u32[]{:S(2)}) collective-permute-start(f32[4,2,80,128]{3,2,1,0:T(8,128)} %get-tuple-element.29), channel_id=1, source_target_pairs={{0,6},{2,0},{4,2},{6,4},{1,7},{3,1},{5,3},{7,5},{8,14},{10,8},{12,... | collective-permute-start | bytes 983048 | tf_op jit(solution)/shard_map/ppermute | solution.py:263
  97.1 15.8 %collective-permute-start.5 = (f32[4,2,80,128]{3,2,1,0:T(8,128)}, f32[4,2,80,128]{3,2,1,0:T(8,128)}, u32[]{:S(2)}, u32[]{:S(2)}) collective-permute-start(f32[4,2,80,128]{3,2,1,0:T(8,128)} %get-tuple-element.30), channel_id=1, source_target_pairs={{0,4},{2,6},{4,0},{6,2},{1,5},{3,7},{5,1},{7,3},{8,12},{10,14},{12... | collective-permute-start | bytes 983048 | tf_op jit(solution)/shard_map/ppermute | solution.py:263
  115.0 33.3 %collective-permute-start.17 = (bf16[1,8,3,48,512]{4,3,2,1,0:T(8,128)(2,1)}, bf16[1,8,3,48,512]{4,3,2,1,0:T(8,128)(2,1)}, u32[]{:S(2)}, u32[]{:S(2)}) collective-permute-start(bf16[1,8,3,48,512]{4,3,2,1,0:T(8,128)(2,1)} %hold.9), channel_id=1, source_target_pairs={{0,64},{64,0},{1,65},{65,1},{2,66},{66,2},{3,67},{67,3},{4,68},{68... | collective-permute-start | bytes 3538952 | tf_op jit(solution)/shard_map/ppermute | solution.py:18
  118.2 6.3 %collective-permute-start.6 = (f32[2,80,128]{2,1,0:T(8,128)}, f32[2,80,128]{2,1,0:T(8,128)S(1)}, u32[]{:S(2)}, u32[]{:S(2)}) collective-permute-start(f32[2,80,128]{2,1,0:T(8,128)} %get-tuple-element.34), channel_id=1, source_target_pairs={{0,8},{8,16},{16,24},{24,0},{1,9},{9,17},{17,25},{25,1},{2,10},{10... | collective-permute-start | bytes 245768 | tf_op jit(solution)/shard_map/ppermute | solution.py:247
  119.3 6.0 %collective-permute-start.8 = (f32[2,80,128]{2,1,0:T(8,128)S(1)}, f32[2,80,128]{2,1,0:T(8,128)S(1)}, u32[]{:S(2)}, u32[]{:S(2)}) collective-permute-start(f32[2,80,128]{2,1,0:T(8,128)S(1)} %get-tuple-element.35), channel_id=1, source_target_pairs={{0,16},{8,24},{16,0},{24,8},{1,17},{9,25},{17,1},{25,9},{2,18},{10... | collective-permute-start | bytes 245768 | tf_op jit(solution)/shard_map/ppermute | solution.py:247
  121.8 4.5 %collective-permute-start.7 = (f32[2,80,128]{2,1,0:T(8,128)S(1)}, f32[2,80,128]{2,1,0:T(8,128)}, u32[]{:S(2)}, u32[]{:S(2)}) collective-permute-start(f32[2,80,128]{2,1,0:T(8,128)S(1)} %get-tuple-element.36), channel_id=1, source_target_pairs={{0,24},{8,0},{16,8},{24,16},{1,25},{9,1},{17,9},{25,17},{2,26},{10... | collective-permute-start | bytes 245768 | tf_op jit(solution)/shard_map/ppermute | solution.py:247
  128.6 13.8 %copy-start.3 = (bf16[3,176,512]{2,1,0:T(8,128)(2,1)S(1)}, bf16[3,176,512]{2,1,0:T(8,128)(2,1)}, u32[]{:S(2)}) copy-start(bf16[3,176,512]{2,1,0:T(8,128)(2,1)} %hold.8) | copy-start | bytes 1622020
  128.6 28.0 %collective-permute-start.18 = (bf16[1,4,3,48,512]{4,3,2,1,0:T(8,128)(2,1)}, bf16[1,4,3,48,512]{4,3,2,1,0:T(8,128)(2,1)}, u32[]{:S(2)}, u32[]{:S(2)}) collective-permute-start(bf16[1,4,3,48,512]{4,3,2,1,0:T(8,128)(2,1)} %hold.10), channel_id=1, source_target_pairs={{0,64},{64,0},{1,65},{65,1},{2,66},{66,2},{3,67},{67,3},{4,68},{68... | collective-permute-start | bytes 1769480 | tf_op jit(solution)/shard_map/ppermute | solution.py:18
  138.2 6.2 %collective-permute-start.14 = (f32[2,2,48,128]{3,2,1,0:T(8,128)S(1)}, f32[2,2,48,128]{3,2,1,0:T(8,128)S(1)}, u32[]{:S(2)}, u32[]{:S(2)}) collective-permute-start(f32[2,2,48,128]{3,2,1,0:T(8,128)S(1)} %get-tuple-element.31), channel_id=1, source_target_pairs={{0,8},{8,16},{16,24},{24,0},{1,9},{9,17},{17,25},{25,1},{2,10},{10... | collective-permute-start | bytes 294920 | tf_op jit(solution)/shard_map/ppermute | solution.py:247
  139.2 6.6 %collective-permute-start.16 = (f32[2,2,48,128]{3,2,1,0:T(8,128)S(1)}, f32[2,2,48,128]{3,2,1,0:T(8,128)S(1)}, u32[]{:S(2)}, u32[]{:S(2)}) collective-permute-start(f32[2,2,48,128]{3,2,1,0:T(8,128)S(1)} %get-tuple-element.32), channel_id=1, source_target_pairs={{0,16},{8,24},{16,0},{24,8},{1,17},{9,25},{17,1},{25,9},{2,18},{10... | collective-permute-start | bytes 294920 | tf_op jit(solution)/shard_map/ppermute | solution.py:247
  142.1 4.6 %collective-permute-start.15 = (f32[2,2,48,128]{3,2,1,0:T(8,128)S(1)}, f32[2,2,48,128]{3,2,1,0:T(8,128)S(1)}, u32[]{:S(2)}, u32[]{:S(2)}) collective-permute-start(f32[2,2,48,128]{3,2,1,0:T(8,128)S(1)} %get-tuple-element.33), channel_id=1, source_target_pairs={{0,24},{8,0},{16,8},{24,16},{1,25},{9,1},{17,9},{25,17},{2,26},{10... | collective-permute-start | bytes 294920 | tf_op jit(solution)/shard_map/ppermute | solution.py:247
  148.3 8.0 %copy-start.9 = (s32[4,4]{1,0:T(4,128)S(1)}, s32[4,4]{1,0:T(4,128)}, u32[]{:S(2)}) copy-start(s32[4,4]{1,0:T(4,128)} %gather_fusion) | copy-start | bytes 196
  148.3 8.0 %copy-start.11 = (pred[4]{0:T(512)(128)(4,1)S(1)}, pred[4]{0:T(512)(128)(4,1)}, u32[]{:S(2)}) copy-start(pred[4]{0:T(512)(128)(4,1)} %compare_and_fusion) | copy-start | bytes 16
  154.7 18.4 %collective-permute-start.22 = (bf16[4,3,48,512]{3,2,1,0:T(8,128)(2,1)}, bf16[4,3,48,512]{3,2,1,0:T(8,128)(2,1)}, u32[]{:S(2)}, u32[]{:S(2)}) collective-permute-start(bf16[4,3,48,512]{3,2,1,0:T(8,128)(2,1)} %hold.11), channel_id=1, source_target_pairs={{0,64},{64,0},{1,65},{65,1},{2,66},{66,2},{3,67},{67,3},{4,68},{68... | collective-permute-start | bytes 1769480 | tf_op jit(solution)/shard_map/ppermute | solution.py:18
  156.4 4.8 %copy-start.5 = (f32[1,8,2,24,128]{4,3,2,1,0:T(8,128)S(1)}, f32[1,8,2,24,128]{4,3,2,1,0:T(8,128)}, u32[]{:S(2)}) copy-start(f32[1,8,2,24,128]{4,3,2,1,0:T(8,128)} %project.6) | copy-start | bytes 589828
  162.7 5.9 %collective-permute-start.19 = (f32[3,48,128]{2,1,0:T(8,128)}, f32[3,48,128]{2,1,0:T(8,128)}, u32[]{:S(2)}, u32[]{:S(2)}) collective-permute-start(f32[3,48,128]{2,1,0:T(8,128)} %get-tuple-element.37), channel_id=1, source_target_pairs={{0,8},{8,16},{16,24},{24,0},{1,9},{9,17},{17,25},{25,1},{2,10},{10... | collective-permute-start | bytes 221192 | tf_op jit(solution)/shard_map/ppermute | solution.py:247
  163.6 5.0 %collective-permute-start.20 = (f32[3,48,128]{2,1,0:T(8,128)}, f32[3,48,128]{2,1,0:T(8,128)}, u32[]{:S(2)}, u32[]{:S(2)}) collective-permute-start(f32[3,48,128]{2,1,0:T(8,128)} %get-tuple-element.38), channel_id=1, source_target_pairs={{0,24},{8,0},{16,8},{24,16},{1,25},{9,1},{17,9},{25,17},{2,26},{10... | collective-permute-start | bytes 221192 | tf_op jit(solution)/shard_map/ppermute | solution.py:247
  165.9 6.2 %collective-permute-start.21 = (f32[3,48,128]{2,1,0:T(8,128)}, f32[3,48,128]{2,1,0:T(8,128)}, u32[]{:S(2)}, u32[]{:S(2)}) collective-permute-start(f32[3,48,128]{2,1,0:T(8,128)} %get-tuple-element.39), channel_id=1, source_target_pairs={{0,16},{8,24},{16,0},{24,8},{1,17},{9,25},{17,1},{25,9},{2,18},{10... | collective-permute-start | bytes 221192 | tf_op jit(solution)/shard_map/ppermute | solution.py:247
  176.4 15.0 %copy-start.8 = (pred[4,4,4]{2,1,0:T(4,128)(4,1)S(1)}, pred[4,4,4]{2,1,0:T(4,128)(4,1)}, u32[]{:S(2)}) copy-start(pred[4,4,4]{2,1,0:T(4,128)(4,1)} %iota_compare_fusion) | copy-start | bytes 196
  176.5 5.4 %collective-permute-start.23 = (f32[2,48,128]{2,1,0:T(8,128)S(1)}, f32[2,48,128]{2,1,0:T(8,128)S(1)}, u32[]{:S(2)}, u32[]{:S(2)}) collective-permute-start(f32[2,48,128]{2,1,0:T(8,128)S(1)} %get-tuple-element.40), channel_id=1, source_target_pairs={{0,2},{2,4},{4,6},{6,0},{1,3},{3,5},{5,7},{7,1},{8,10},{10,12},{12... | collective-permute-start | bytes 147464 | tf_op jit(solution)/shard_map/ppermute | solution.py:263
  177.5 5.6 %collective-permute-start.25 = (f32[2,48,128]{2,1,0:T(8,128)S(1)}, f32[2,48,128]{2,1,0:T(8,128)S(1)}, u32[]{:S(2)}, u32[]{:S(2)}) collective-permute-start(f32[2,48,128]{2,1,0:T(8,128)S(1)} %get-tuple-element.41), channel_id=1, source_target_pairs={{0,4},{2,6},{4,0},{6,2},{1,5},{3,7},{5,1},{7,3},{8,12},{10,14},{12... | collective-permute-start | bytes 147464 | tf_op jit(solution)/shard_map/ppermute | solution.py:263
  179.8 4.1 %collective-permute-start.24 = (f32[2,48,128]{2,1,0:T(8,128)S(1)}, f32[2,48,128]{2,1,0:T(8,128)S(1)}, u32[]{:S(2)}, u32[]{:S(2)}) collective-permute-start(f32[2,48,128]{2,1,0:T(8,128)S(1)} %get-tuple-element.42), channel_id=1, source_target_pairs={{0,6},{2,0},{4,2},{6,4},{1,7},{3,1},{5,3},{7,5},{8,14},{10,8},{12,... | collective-permute-start | bytes 147464 | tf_op jit(solution)/shard_map/ppermute | solution.py:263
  183.9 5.8 %collective-permute-start.26 = (f32[128,128]{1,0:T(8,128)S(1)}, f32[128,128]{1,0:T(8,128)S(1)}, u32[]{:S(2)}, u32[]{:S(2)}) collective-permute-start(f32[128,128]{1,0:T(8,128)S(1)} %fusion.27), channel_id=1, source_target_pairs={{0,1},{1,0},{2,3},{3,2},{4,5},{5,4},{6,7},{7,6},{8,9},{9,8},{10,11... | collective-permute-start | bytes 196616 | tf_op jit(solution)/shard_map/ppermute | solution.py:18
  189.8 1.3 collective-permute-start.27

commit v9 on v8

--- a/solution.py
+++ b/solution.py
@@ -282,14 +282,14 @@
     first_part = front(sols, vecs, source_index, source_time, group)
     raw = swap(first_part, "yl")
     other = swap(vecs, "c")
-    parts = ((0, 2, 0, 2), (2, 1, 0, 2), (3, 1, 0, 1), (3, 1, 1, 1))
+    parts = ((0, 3, 0, 2), (3, 1, 0, 1), (3, 1, 1, 1))
     sent = [(RAW, count, *part) for part in parts]
-    mine, *send = by_time(sols, ((0, count, 0, 4, 0, 2), *sent), mark(first_part))
+    mine, *send = by_time(sols, ((0, count, 0, 4, 0, 2), *sent), first_part)
     send = [rows_of(part) for part in send]
     got = [swap(send[0], "yl"), swap(hold(send[1], raw), "yl")]
 
     whole, late = (0, owned, 0, 4, 0, 2), (0, owned, 3, 1, 1, 1)
-    own, own_late = by_time(vecs, (whole, late), mark(send[0]))
+    own, own_late = by_time(vecs, (whole, late), send[0])
     other = by_time(other, (whole,))[0]
     own, other = rows_of(own), rows_of(other)
     lines = raw[RAW * comps] + first_part[RAW * comps]
@@ -302,28 +302,26 @@
 
     first = project([rows_of(mine), raw_rows], own, other, 0, 0, 8)
 
-    slabs = [v.reshape(4, comps // 2, -1, sites) for v in (send[3], own_late)]
-    spread = share_z(hold(jnp.concatenate(slabs, axis=2), raw, other))
+    slabs = [v.reshape(4, comps // 2, -1, sites) for v in (send[2], own_late)]
+    spread = share_z(jnp.concatenate(slabs, axis=2))
     spread[1] = hold(spread[1], first[0])
     spread = jnp.stack(spread)
-    cut = send[3].shape[3]
+    cut = send[2].shape[3]
     spread_s, spread_v = spread[:, :, :cut], spread[:, :, cut:]
     spread_w = swap(spread_v, "c")
 
     first = [v.reshape(4, 4, 2, -1, 2 * owned) for v in first]
     first = sum_x(jnp.concatenate(first, axis=3))
-    first = sum_z(hold(first, spread_v))
-
-    got.append(swap(hold(send[2], got[0]), "yl"))
-    early = against(got[0], 0, 0, 8, first, spread_w)
-    early = sum_z(jnp.swapaxes(early, 0, 1)).reshape(4, -1, 2 * owned)
-    mid = [against(got[1], 2, 0, 4, early)[0]]
-    got.append(swap(hold(spread_s, mid[0]), "yl"))
-    mid.append(against(got[2], 3, 0, 1, mid[0])[0])
-    mid = sum_z(jnp.concatenate(mid, axis=1))
-    last = project_pieces(got[3], spread_v, spread_w)
+    first = sum_z(hold(first, spread_v, spread_w))
+
+    late = [against(got[0], 0, 0, 8, first)]
+    got.append(swap(hold(spread_s, late[0]), "yl"))
+    late.append(against(got[1], 3, 0, 1, late[0]))
+    late = [jnp.swapaxes(v, 0, 1).reshape(4, -1, *v.shape[3:]) for v in late]
+    late = sum_z(jnp.concatenate(late, axis=1))
+    last = project_pieces(got[2], spread_v, spread_w)
     last = last.reshape(1, -1, 2 * owned)
-    late = sum_x(jnp.concatenate([early, mid, last]).reshape(4, 2, -1, 2 * owned))
+    late = sum_x(jnp.concatenate([late, last]).reshape(4, 2, -1, 2 * owned))
 
     here = sum_yh(jnp.concatenate([first, late], axis=1))
     there = swap(here, "c")

time: 195 us -> 181 us (0.928)
  local copies, waits for them, and re-layouts: 25.4 us -> 16.2 us
  starting transfers between devices: 37.9 us -> 29.9 us
  waiting for transfers between devices: 40.2 us -> 48.2 us
  other arithmetic: 19.4 us -> 16.6 us
    ppermute x12 -> x9, starting transfers between devices: 20.1 us -> 12.1 us  [share_z(): lax.ppermute(pick(slabs, (me + k) % 4), 'z', [(i, (i + k) % 4) for i in r...]
    ppermute x10 -> x9, waiting for transfers between devices: 16.3 us -> 20.7 us  [swap(): return lax.ppermute(value, axis, SWAP)]
    squeeze x10 -> x6, local copies, waits for them, and re-layouts: 9.52 us -> 5.58 us  [mark(): value = value[0]]
    concatenate x2 -> x1, other arithmetic: 2.89 us -> 0.02 us  [local(): late = sum_x(jnp.concatenate([late, last]).reshape(4, 2, -1, 2 * owned))]
    dynamic_slice x1 -> x0, local copies, waits for them, and re-layouts: 2.84 us -> none  [pick(): return lax.dynamic_index_in_dim(value, index, 0, keepdims=False)]
    squeeze x3 -> x4, other arithmetic: 3.59 us -> 5.74 us  [pick(): return lax.dynamic_index_in_dim(value, index, 0, keepdims=False)]
    pallas_call x4 -> x3, Pallas kernels: 32.4 us -> 30.6 us  [project(): pl.pallas_call(functools.partial(dot_kernel, len(cols)), grid=(size, inne...]
    ppermute x12 -> x9, waiting for transfers between devices: 9.55 us -> 11.2 us  [share_z(): lax.ppermute(pick(slabs, (me + k) % 4), 'z', [(i, (i + k) % 4) for i in r...]
  transfers between devices with their start and end apart: 28 -> 24, of which waited for: 17 -> 12; matrix products, arithmetic and copies ran while one was open for 20% -> 15% of each run, Pallas kernels for 34% -> 35%
where the time goes in v9:
time: 181 us; the launch traced here: 179 us
  Pallas kernels  66.5 us (37%)
  waiting for transfers between devices  48.2 us (27%)
  starting transfers between devices  29.9 us (17%)
  other arithmetic  16.6 us (9%)
  local copies, waits for them, and re-layouts  16.2 us (9%)
    pallas_call x3, Pallas kernels, project(): pl.pallas_call(functools.partial(dot_kernel, len(cols)), grid=(size, inne...  30.6 us
    pallas_call x4, Pallas kernels, by_time(): pl.pallas_call(functools.partial(by_time_kernel, cuts), grid=(4,), in_spe...  29.6 us
    ppermute x9, waiting for transfers between devices, swap(): return lax.ppermute(value, axis, SWAP)  20.7 us
    ppermute x6, waiting for transfers between devices, sum_x(): total = total + lax.ppermute(pick(slabs, (me + k) % 4), 'x', pairs)  16.2 us
    ppermute x9, starting transfers between devices, share_z(): lax.ppermute(pick(slabs, (me + k) % 4), 'z', [(i, (i + k) % 4) for i in r...  12.1 us
    ppermute x9, waiting for transfers between devices, share_z(): lax.ppermute(pick(slabs, (me + k) % 4), 'z', [(i, (i + k) % 4) for i in r...  11.2 us
    ppermute x6, starting transfers between devices, sum_x(): total = total + lax.ppermute(pick(slabs, (me + k) % 4), 'x', pairs)  10.1 us
    ppermute x9, starting transfers between devices, swap(): return lax.ppermute(value, axis, SWAP)  7.65 us
  transfers between devices with their start and end apart: 24, of which 12 were waited for; matrix products, arithmetic and copies ran while one was open for 15% of the time, Pallas kernels for 35%

profile of v9, /device:TPU:0, one launch (start us, length us, event | category | flops | bytes accessed | tf_op | source)
XLA Modules:
  0.0 178.9 jit_solution(13714514664143064220)
XLA Ops:
  1.4 1.2 pad_add_fusion.at
  2.6 2.9 %front.1 = bf16[49,4,8,512]{3,2,1,0:T(8,128)(2,1)} custom-call(s32[6]{0:T(128)} %pad_add_fusion.at, bf16[192,4,8,512]{3,2,1,0:T(8,128)(2,1)} %bitcast.157, bf16[64,6,32,512]{3,2,1,0:T(8,128)(2,1)} %bitcast.155), custom_call_target="tpu_custom_call" | custom-call | flops 1000 | bytes 1000 | tf_op jit(solution)/shard_map/front/pallas_call | solution.py:133
  5.6 1.7 collective-permute-start
  7.3 7.7 %by_time.4 = (bf16[4,4,2,6,32,512]{5,4,3,2,1,0:T(8,128)(2,1)}, bf16[3,4,2,6,24,512]{5,4,3,2,1,0:T(8,128)(2,1)}, bf16[1,4,1,6,24,512]{5,4,3,2,1,0:T(8,128)(2,1)}, bf16[1,4,1,6,24,512]{5,4,3,2,1,0:T(8,128)(2,1)}) custom-call(bf16[32,6,32,512]{3,2,1,0:T(8,128)(2,1)} %bitcast.158, bf16[49,32,512]{2,1,0:T(8,128)(2,1)} %bitcast.160), custom_call_target="tpu_custom_call" | custom-call | flops 1000 | bytes 1000 | tf_op jit(solution)/shard_map/by_time/pallas_call | solution.py:48
  15.0 0.4 collective-permute-start.13
  15.4 10.7 %by_time.7 = (bf16[4,4,2,6,64,512]{5,4,3,2,1,0:T(8,128)(2,1)}, bf16[1,4,1,6,64,512]{5,4,3,2,1,0:T(8,128)(2,1)}) custom-call(bf16[64,6,32,512]{3,2,1,0:T(8,128)(2,1)} %bitcast.156, bf16[3,8,3,48,512]{4,3,2,1,0:T(8,128)(2,1)} %bitcast.169), custom_call_target="tpu_custom_call" | custom-call | flops 1000 | bytes 1000 | tf_op jit(solution)/shard_map/by_time/pallas_call | solution.py:48
  26.1 17.7 %collective-permute-done.block = bf16[49,32,512]{2,1,0:T(8,128)(2,1)S(1)} collective-permute-done((bf16[49,32,512]{2,1,0:T(8,128)(2,1)}, bf16[49,32,512]{2,1,0:T(8,128)(2,1)S(1)}, u32[]{:S(2)}, u32[]{:S(2)}) %collective-permute-start) | collective-permute-done | bytes 1605664 | tf_op jit(solution)/shard_map/ppermute | solution.py:18
  43.7 0.8 fusion.38
  44.5 2.5 %fusion.4 = (bf16[3,176,512]{2,1,0:T(8,128)(2,1)S(1)}, bf16[1,3,176,512]{3,2,1,0:T(8,128)(2,1)S(1)}, bf16[3,176,512]{2,1,0:T(8,128)(2,1)}, bf16[3,176,512]{2,1,0:T(8,128)(2,1)}) fusion(s32[]{:T(128)S(6)} %select_n.148, bf16[4,3,128,512]{3,2,1,0:T(8,128)(2,1)} %bitcast.171, bf16[4,3,48,512]{3,2,1,0:T(8,128)(2,1)S(1)} %bitcast.178, s32[]{:T(128)S(6)} %select_n.146, ...), kind=kLoop, calls=%fused_computation.31 | loop fusion | flops 4325376 | bytes 4325392 | tf_op jit(solution)/shard_map/jit(dynamic_index_in_dim)/squeeze | solution.py:241
  47.0 4.0 %collective-permute-start.8 = (bf16[3,176,512]{2,1,0:T(8,128)(2,1)}, bf16[3,176,512]{2,1,0:T(8,128)(2,1)}, u32[]{:S(2)}, u32[]{:S(2)}) collective-permute-start(bf16[3,176,512]{2,1,0:T(8,128)(2,1)} %get-tuple-element.25), channel_id=1, source_target_pairs={{0,16},{8,24},{16,0},{24,8},{1,17},{9,25},{17,1},{25,9},{2,18},{10... | collective-permute-start | bytes 1622024 | tf_op jit(solution)/shard_map/ppermute | solution.py:247
  51.0 1.0 collective-permute-start.6
  52.0 2.2 %collective-permute-start.7 = (bf16[3,176,512]{2,1,0:T(8,128)(2,1)}, bf16[3,176,512]{2,1,0:T(8,128)(2,1)}, u32[]{:S(2)}, u32[]{:S(2)}) collective-permute-start(bf16[3,176,512]{2,1,0:T(8,128)(2,1)} %get-tuple-element.24), channel_id=1, source_target_pairs={{0,24},{8,0},{16,8},{24,16},{1,25},{9,1},{17,9},{25,17},{2,26},{10... | collective-permute-start | bytes 1622024 | tf_op jit(solution)/shard_map/ppermute | solution.py:247
  54.2 10.5 %by_time.5 = bf16[4,4,2,6,64,512]{5,4,3,2,1,0:T(8,128)(2,1)} custom-call(bf16[64,6,32,512]{3,2,1,0:T(8,128)(2,1)} %collective-permute-done.1.block), custom_call_target="tpu_custom_call" | custom-call | flops 1000 | bytes 1000 | tf_op jit(solution)/shard_map/by_time/pallas_call | solution.py:48
  64.8 1.9 %slice-done = bf16[1,4,2,6,64,512]{5,4,3,2,1,0:T(8,128)(2,1)S(1)} async-done(((bf16[4,4,2,6,64,512]{5,4,3,2,1,0:T(8,128)(2,1)}), bf16[1,4,2,6,64,512]{5,4,3,2,1,0:T(8,128)(2,1)S(1)}, s32[]{:S(2)}) %slice-start) | async-done | bytes 3145752 | tf_op jit(solution)/shard_map/slice | solution.py:73
  66.7 0.7 by_time.6
  67.4 1.2 copy-done
  68.5 14.7 %project.3 = (f32[4,8,2,32,128]{4,3,2,1,0:T(8,128)}, f32[4,8,2,8,128]{4,3,2,1,0:T(8,128)}) custom-call(bf16[4,8,3,64,512]{4,3,2,1,0:T(8,128)(2,1)} %bitcast.161, bf16[4,8,3,16,512]{4,3,2,1,0:T(8,128)(2,1)} %bitcast.144, bf16[4,8,3,128,512]{4,3,2,1,0:T(8,128)(2,1)} %bitcast.151, bf16[4,8,3,128,512]{4,3,2,1,0:T(8,128)(2,1)} %bitcast.147), custom_call_target="tpu_custom_call" | custom-call | flops 1000 | bytes 1000 | tf_op jit(solution)/shard_map/project/pallas_call | solution.py:228
  83.2 1.3 slice_bitcast_fusion.7.refs_1_
  84.5 0.8 copy-done.4
  85.4 1.6 pad_maximum_fusion
  87.3 0.4 copy-done.7
  87.9 0.6 gather_fusion
  88.5 1.6 slice_bitcast_fusion.1.refs_1_
  90.1 2.1 %fusion.15 = (f32[4,2,80,128]{3,2,1,0:T(8,128)}, f32[4,2,80,128]{3,2,1,0:T(8,128)}, f32[4,2,80,128]{3,2,1,0:T(8,128)}) fusion(s32[]{:T(128)S(6)} %select_n.141, f32[4,4,2,64,128]{4,3,2,1,0:T(8,128)} %bitcast.166, f32[4,4,2,16,128]{4,3,2,1,0:T(8,128)S(1)} %bitcast.172, s32[]{:T(128)S(6)} %select_n.143, s32[]{:T(128)S(6)} %select_n.145), kind=kLoop, calls=%fused_computation.43 | loop fusion | flops 245760 | bytes 2293772 | tf_op jit(solution)/shard_map/jit(dynamic_index_in_dim)/squeeze | solution.py:241
  92.2 3.0 %collective-permute-start.5 = (f32[4,2,80,128]{3,2,1,0:T(8,128)}, f32[4,2,80,128]{3,2,1,0:T(8,128)}, u32[]{:S(2)}, u32[]{:S(2)}) collective-permute-start(f32[4,2,80,128]{3,2,1,0:T(8,128)} %get-tuple-element.28), channel_id=1, source_target_pairs={{0,4},{2,6},{4,0},{6,2},{1,5},{3,7},{5,1},{7,3},{8,12},{10,14},{12... | collective-permute-start | bytes 983048 | tf_op jit(solution)/shard_map/ppermute | solution.py:263
  95.2 1.1 collective-permute-start.4
  96.4 0.9 collective-permute-start.3
  97.5 1.4 slice_bitcast_fusion.4.refs_1_
  98.9 5.8 %collective-permute-done.5 = f32[4,2,80,128]{3,2,1,0:T(8,128)} collective-permute-done((f32[4,2,80,128]{3,2,1,0:T(8,128)}, f32[4,2,80,128]{3,2,1,0:T(8,128)}, u32[]{:S(2)}, u32[]{:S(2)}) %collective-permute-start.5) | collective-permute-done | bytes 327712 | tf_op jit(solution)/shard_map/ppermute | solution.py:263
  104.6 6.2 %collective-permute-done.4 = f32[4,2,80,128]{3,2,1,0:T(8,128)} collective-permute-done((f32[4,2,80,128]{3,2,1,0:T(8,128)}, f32[4,2,80,128]{3,2,1,0:T(8,128)}, u32[]{:S(2)}, u32[]{:S(2)}) %collective-permute-start.4) | collective-permute-done | bytes 327712 | tf_op jit(solution)/shard_map/ppermute | solution.py:263
  110.8 2.0 %fusion.13.refs_0_ = f32[4,2,80,128]{3,2,1,0:T(8,128)} fusion(f32[4,2,80,128]{3,2,1,0:T(8,128)} %collective-permute-done.5, f32[4,2,80,128]{3,2,1,0:T(8,128)} %collective-permute-done.4, f32[4,2,80,128]{3,2,1,0:T(8,128)} %collective-permute-done.3, s32[]{:T(128)S(6)} %select_n.139, f32[4,4,2,64,128]{4,3,2,1,0:T(8,128)} %bitcast.167, ...), kind=kLoop, calls=%fused_computation.41 | loop fusion | flops 327680 | bytes 2621444 | tf_op jit(solution)/shard_map/add | solution.py:263
  112.9 0.7 slice_bitcast_fusion.refs_2_
  113.5 1.6 collective-permute-start.14
  115.1 1.0 dynamic-slice_bitcast_fusion.2
  116.2 2.5 %collective-permute-start.11 = (f32[2,80,128]{2,1,0:T(8,128)S(1)}, f32[2,80,128]{2,1,0:T(8,128)S(1)}, u32[]{:S(2)}, u32[]{:S(2)}) collective-permute-start(f32[2,80,128]{2,1,0:T(8,128)S(1)} %get-tuple-element.34), channel_id=1, source_target_pairs={{0,24},{8,0},{16,8},{24,16},{1,25},{9,1},{17,9},{25,17},{2,26},{10... | collective-permute-start | bytes 245768 | tf_op jit(solution)/shard_map/ppermute | solution.py:247
  118.7 2.0 %pad_maximum_fusion.1.refs_0_ = bf16[4,3,48,512]{3,2,1,0:T(8,128)(2,1)} fusion(bf16[1,3,176,512]{3,2,1,0:T(8,128)(2,1)} %bitcast.40, bf16[1,3,176,512]{3,2,1,0:T(8,128)(2,1)} %bitcast.38, bf16[1,3,176,512]{3,2,1,0:T(8,128)(2,1)} %bitcast.165, bf16[1,3,176,512]{3,2,1,0:T(8,128)(2,1)} %copy-done.2), kind=kLoop, calls=%fused_computation.26 | loop fusion | flops 2359296 | bytes 2752512 | tf_op jit(solution)/shard_map/slice | solution.py:310
  120.7 2.2 %collective-permute-done.12 = f32[2,80,128]{2,1,0:T(8,128)S(1)} collective-permute-done((f32[2,80,128]{2,1,0:T(8,128)S(1)}, f32[2,80,128]{2,1,0:T(8,128)S(1)}, u32[]{:S(2)}, u32[]{:S(2)}) %collective-permute-start.12) | collective-permute-done | bytes 81952 | tf_op jit(solution)/shard_map/ppermute | solution.py:247
  122.9 1.4 collective-permute-done.10
  124.3 0.9 fusion.30
  125.2 0.6 slice_bitcast_fusion.3.refs_3_
  125.8 11.3 %project.4 = f32[3,8,2,24,128]{4,3,2,1,0:T(8,128)} custom-call(bf16[3,8,3,48,512]{4,3,2,1,0:T(8,128)(2,1)} %collective-permute-done.13.refs_0_, bf16[4,8,3,128,512]{4,3,2,1,0:T(8,128)(2,1)} %bitcast.152, bf16[4,8,3,128,512]{4,3,2,1,0:T(8,128)(2,1)} %bitcast.148, f32[80,128]{1,0:T(8,128)} %slice_bitcast_fusion.3.refs_3_), custom_call_target="tpu_custom_call" | custom-call | flops 1000 | bytes 1000 | tf_op jit(solution)/shard_map/project/pallas_call | solution.py:228
  137.2 1.3 slice.124
  138.5 0.4 collective-permute-start.18
  139.0 1.9 %copy.18 = f32[3,4,2,48,128]{4,3,2,0,1:T(8,128)} copy(f32[3,4,2,48,128]{4,3,2,1,0:T(8,128)} %bitcast.170) | data formatting | bytes 1179648 | tf_op jit(solution)/shard_map/reshape | solution.py:301
  140.9 4.6 %project.5 = f32[1,4,2,24,128]{4,3,2,1,0:T(8,128)} custom-call(bf16[1,4,3,48,512]{4,3,2,1,0:T(8,128)(2,1)} %collective-permute-done.14.refs_0_, bf16[4,8,3,128,512]{4,3,2,1,0:T(8,128)(2,1)} %bitcast.153, bf16[4,8,3,128,512]{4,3,2,1,0:T(8,128)(2,1)} %bitcast.149, f32[48,128]{1,0:T(8,128)} %bitcast.182), custom_call_target="tpu_custom_call" | custom-call | flops 1000 | bytes 1000 | tf_op jit(solution)/shard_map/project/pallas_call | solution.py:228
  145.5 1.2 fusion.26
  146.8 1.6 collective-permute-start.16
  148.3 0.7 collective-permute-start.15
  149.1 5.8 %collective-permute-done.17 = f32[7,48,128]{2,1,0:T(8,128)S(1)} collective-permute-done((f32[7,48,128]{2,1,0:T(8,128)S(1)}, f32[7,48,128]{2,1,0:T(8,128)S(1)}, u32[]{:S(2)}, u32[]{:S(2)}) %collective-permute-start.17) | collective-permute-done | bytes 172064 | tf_op jit(solution)/shard_map/ppermute | solution.py:247
  154.9 1.8 collective-permute-done.15
  156.7 0.8 fusion.24
  157.5 3.3 %project_pieces.1 = f32[2,24,128]{2,1,0:T(8,128)S(1)} custom-call(bf16[4,3,48,512]{3,2,1,0:T(8,128)(2,1)} %collective-permute-done.18.col, bf16[4,3,128,512]{3,2,1,0:T(8,128)(2,1)S(1)} %slice.120.own, bf16[4,3,128,512]{3,2,1,0:T(8,128)(2,1)S(1)} %collective-permute-done.9.other), custom_call_target="tpu_custom_call" | custom-call | flops 1000 | bytes 1000 | tf_op jit(solution)/shard_map/project_pieces/pallas_call | solution.py:201
  160.8 3.1 %collective-permute-start.21 = (f32[2,48,128]{2,1,0:T(8,128)S(1)}, f32[2,48,128]{2,1,0:T(8,128)S(1)}, u32[]{:S(2)}, u32[]{:S(2)}) collective-permute-start(f32[2,48,128]{2,1,0:T(8,128)S(1)} %get-tuple-element.36), channel_id=1, source_target_pairs={{0,4},{2,6},{4,0},{6,2},{1,5},{3,7},{5,1},{7,3},{8,12},{10,14},{12... | collective-permute-start | bytes 147464 | tf_op jit(solution)/shard_map/ppermute | solution.py:263
  163.9 1.1 collective-permute-start.20
  165.0 1.0 collective-permute-start.19
  166.0 0.6 collective-permute-done.21
  166.6 1.4 collective-permute-done.20
  168.0 2.3 %collective-permute-done.19 = f32[2,48,128]{2,1,0:T(8,128)S(1)} collective-permute-done((f32[2,48,128]{2,1,0:T(8,128)S(1)}, f32[2,48,128]{2,1,0:T(8,128)S(1)}, u32[]{:S(2)}, u32[]{:S(2)}) %collective-permute-start.19) | collective-permute-done | bytes 49184 | tf_op jit(solution)/shard_map/ppermute | solution.py:263
  170.3 3.3 %collective-permute-start.22 = (f32[128,128]{1,0:T(8,128)S(1)}, f32[128,128]{1,0:T(8,128)S(1)}, u32[]{:S(2)}, u32[]{:S(2)}) collective-permute-start(f32[128,128]{1,0:T(8,128)S(1)} %fusion.32), channel_id=1, source_target_pairs={{0,1},{1,0},{2,3},{3,2},{4,5},{5,4},{6,7},{7,6},{8,9},{9,8},{10,11... | collective-permute-start | bytes 196616 | tf_op jit(solution)/shard_map/ppermute | solution.py:18
  173.6 0.7 broadcast_select_fusion
  174.3 1.8 %collective-permute-done.22 = f32[128,128]{1,0:T(8,128)S(1)} collective-permute-done((f32[128,128]{1,0:T(8,128)S(1)}, f32[128,128]{1,0:T(8,128)S(1)}, u32[]{:S(2)}, u32[]{:S(2)}) %collective-permute-start.22) | collective-permute-done | bytes 65568 | tf_op jit(solution)/shard_map/ppermute | solution.py:18
  176.3 1.2 collective-permute-done.23
  177.8 0.2 select_reduce_fusion
  178.2 0.7 copy.21
  (64 shorter events, 1.7 us)
Async XLA Ops:
  0.6 53.6 %collective-permute-start.1 = (bf16[64,6,32,512]{3,2,1,0:T(8,128)(2,1)}, bf16[64,6,32,512]{3,2,1,0:T(8,128)(2,1)}, u32[]{:S(2)}, u32[]{:S(2)}) collective-permute-start(bf16[64,6,32,512]{3,2,1,0:T(8,128)(2,1)} %bitcast.154), channel_id=1, source_target_pairs={{0,32},{32,0},{1,33},{33,1},{2,34},{34,2},{3,35},{35,3},{4,36},{36... | collective-permute-start | bytes 37748744 | tf_op jit(solution)/shard_map/ppermute | solution.py:18
  5.6 38.2 %collective-permute-start = (bf16[49,32,512]{2,1,0:T(8,128)(2,1)}, bf16[49,32,512]{2,1,0:T(8,128)(2,1)S(1)}, u32[]{:S(2)}, u32[]{:S(2)}) collective-permute-start(bf16[49,32,512]{2,1,0:T(8,128)(2,1)} %bitcast.159), channel_id=1, source_target_pairs={{0,64},{64,0},{1,65},{65,1},{2,66},{66,2},{3,67},{67,3},{4,68},{68... | collective-permute-start | bytes 4816904 | tf_op jit(solution)/shard_map/ppermute | solution.py:18
  15.0 29.5 %copy-start.6 = (bf16[1,4,1,6,24,512]{5,4,3,2,1,0:T(8,128)(2,1)S(1)}, bf16[1,4,1,6,24,512]{5,4,3,2,1,0:T(8,128)(2,1)}, u32[]{:S(2)}) copy-start(bf16[1,4,1,6,24,512]{5,4,3,2,1,0:T(8,128)(2,1)} %get-tuple-element.15) | copy-start | bytes 1769476
  15.0 110.8 %collective-permute-start.13 = (bf16[3,8,3,48,512]{4,3,2,1,0:T(8,128)(2,1)}, bf16[3,8,3,48,512]{4,3,2,1,0:T(8,128)(2,1)}, u32[]{:S(2)}, u32[]{:S(2)}) collective-permute-start(bf16[3,8,3,48,512]{4,3,2,1,0:T(8,128)(2,1)} %bitcast.168), channel_id=1, source_target_pairs={{0,64},{64,0},{1,65},{65,1},{2,66},{66,2},{3,67},{67,3},{4,68},{68... | collective-permute-start | bytes 10616840 | tf_op jit(solution)/shard_map/ppermute | solution.py:18
  43.7 22.9 %copy-start.1 = (bf16[49,32,512]{2,1,0:T(8,128)(2,1)}, bf16[49,32,512]{2,1,0:T(8,128)(2,1)S(1)}, u32[]{:S(2)}) copy-start(bf16[49,32,512]{2,1,0:T(8,128)(2,1)S(1)} %collective-permute-done.block) | copy-start | bytes 4816900
  44.5 7.5 %collective-permute-start.2 = (bf16[32,512]{1,0:T(8,128)(2,1)S(1)}, bf16[32,512]{1,0:T(8,128)(2,1)S(1)}, u32[]{:S(2)}, u32[]{:S(2)}) collective-permute-start(bf16[32,512]{1,0:T(8,128)(2,1)S(1)} %fusion.38), channel_id=1, source_target_pairs={{0,32},{32,0},{1,33},{33,1},{2,34},{34,2},{3,35},{35,3},{4,36},{36... | collective-permute-start | bytes 98312 | tf_op jit(solution)/shard_map/ppermute | solution.py:18
  47.0 38.4 %copy-start.2 = (bf16[1,3,176,512]{3,2,1,0:T(8,128)(2,1)}, bf16[1,3,176,512]{3,2,1,0:T(8,128)(2,1)S(1)}, u32[]{:S(2)}) copy-start(bf16[1,3,176,512]{3,2,1,0:T(8,128)(2,1)S(1)} %get-tuple-element.23) | copy-start | bytes 1622020
  47.0 38.4 %collective-permute-start.8 = (bf16[3,176,512]{2,1,0:T(8,128)(2,1)}, bf16[3,176,512]{2,1,0:T(8,128)(2,1)}, u32[]{:S(2)}, u32[]{:S(2)}) collective-permute-start(bf16[3,176,512]{2,1,0:T(8,128)(2,1)} %get-tuple-element.25), channel_id=1, source_target_pairs={{0,16},{8,24},{16,0},{24,8},{1,17},{9,25},{17,1},{25,9},{2,18},{10... | collective-permute-start | bytes 1622024 | tf_op jit(solution)/shard_map/ppermute | solution.py:247
  51.0 33.6 %collective-permute-start.6 = (bf16[3,176,512]{2,1,0:T(8,128)(2,1)S(1)}, bf16[3,176,512]{2,1,0:T(8,128)(2,1)S(1)}, u32[]{:S(2)}, u32[]{:S(2)}) collective-permute-start(bf16[3,176,512]{2,1,0:T(8,128)(2,1)S(1)} %get-tuple-element.22), channel_id=1, source_target_pairs={{0,8},{8,16},{16,24},{24,0},{1,9},{9,17},{17,25},{25,1},{2,10},{10... | collective-permute-start | bytes 1622024 | tf_op jit(solution)/shard_map/ppermute | solution.py:247
  52.0 33.4 %collective-permute-start.7 = (bf16[3,176,512]{2,1,0:T(8,128)(2,1)}, bf16[3,176,512]{2,1,0:T(8,128)(2,1)}, u32[]{:S(2)}, u32[]{:S(2)}) collective-permute-start(bf16[3,176,512]{2,1,0:T(8,128)(2,1)} %get-tuple-element.24), channel_id=1, source_target_pairs={{0,24},{8,0},{16,8},{24,16},{1,25},{9,1},{17,9},{25,17},{2,26},{10... | collective-permute-start | bytes 1622024 | tf_op jit(solution)/shard_map/ppermute | solution.py:247
  64.8 1.9 %slice-start = ((bf16[4,4,2,6,64,512]{5,4,3,2,1,0:T(8,128)(2,1)}), bf16[1,4,2,6,64,512]{5,4,3,2,1,0:T(8,128)(2,1)S(1)}, s32[]{:S(2)}) async-start(bf16[4,4,2,6,64,512]{5,4,3,2,1,0:T(8,128)(2,1)} %by_time.5), calls=%async_computation | async-start | bytes 6291456 | tf_op jit(solution)/shard_map/slice | solution.py:73
  67.4 1.2 copy-start
  84.5 0.8 copy-start.4
  87.0 0.7 copy-start.7
  87.0 3.1 %copy-start.5 = (f32[4,8,2,8,128]{4,3,2,1,0:T(8,128)S(1)}, f32[4,8,2,8,128]{4,3,2,1,0:T(8,128)}, u32[]{:S(2)}) copy-start(f32[4,8,2,8,128]{4,3,2,1,0:T(8,128)} %get-tuple-element.14) | copy-start | bytes 786436
  87.1 25.7 %collective-permute-start.9 = (bf16[4,3,128,512]{3,2,1,0:T(8,128)(2,1)S(1)}, bf16[4,3,128,512]{3,2,1,0:T(8,128)(2,1)S(1)}, u32[]{:S(2)}, u32[]{:S(2)}) collective-permute-start(bf16[4,3,128,512]{3,2,1,0:T(8,128)(2,1)S(1)} %slice.120.own), channel_id=1, source_target_pairs={{0,32},{32,0},{1,33},{33,1},{2,34},{34,2},{3,35},{35,3},{4,36},{36... | collective-permute-start | bytes 4718600 | tf_op jit(solution)/shard_map/ppermute | solution.py:18
  92.2 12.4 %collective-permute-start.5 = (f32[4,2,80,128]{3,2,1,0:T(8,128)}, f32[4,2,80,128]{3,2,1,0:T(8,128)}, u32[]{:S(2)}, u32[]{:S(2)}) collective-permute-start(f32[4,2,80,128]{3,2,1,0:T(8,128)} %get-tuple-element.28), channel_id=1, source_target_pairs={{0,4},{2,6},{4,0},{6,2},{1,5},{3,7},{5,1},{7,3},{8,12},{10,14},{12... | collective-permute-start | bytes 983048 | tf_op jit(solution)/shard_map/ppermute | solution.py:263
  95.2 15.6 %collective-permute-start.4 = (f32[4,2,80,128]{3,2,1,0:T(8,128)}, f32[4,2,80,128]{3,2,1,0:T(8,128)}, u32[]{:S(2)}, u32[]{:S(2)}) collective-permute-start(f32[4,2,80,128]{3,2,1,0:T(8,128)} %get-tuple-element.27), channel_id=1, source_target_pairs={{0,6},{2,0},{4,2},{6,4},{1,7},{3,1},{5,3},{7,5},{8,14},{10,8},{12,... | collective-permute-start | bytes 983048 | tf_op jit(solution)/shard_map/ppermute | solution.py:263
  96.4 14.5 %collective-permute-start.3 = (f32[4,2,80,128]{3,2,1,0:T(8,128)}, f32[4,2,80,128]{3,2,1,0:T(8,128)}, u32[]{:S(2)}, u32[]{:S(2)}) collective-permute-start(f32[4,2,80,128]{3,2,1,0:T(8,128)} %get-tuple-element.26), channel_id=1, source_target_pairs={{0,2},{2,4},{4,6},{6,0},{1,3},{3,5},{5,7},{7,1},{8,10},{10,12},{12... | collective-permute-start | bytes 983048 | tf_op jit(solution)/shard_map/ppermute | solution.py:263
  113.5 27.4 %collective-permute-start.14 = (bf16[1,4,3,48,512]{4,3,2,1,0:T(8,128)(2,1)}, bf16[1,4,3,48,512]{4,3,2,1,0:T(8,128)(2,1)}, u32[]{:S(2)}, u32[]{:S(2)}) collective-permute-start(bf16[1,4,3,48,512]{4,3,2,1,0:T(8,128)(2,1)} %hold.6), channel_id=1, source_target_pairs={{0,64},{64,0},{1,65},{65,1},{2,66},{66,2},{3,67},{67,3},{4,68},{68... | collective-permute-start | bytes 1769480 | tf_op jit(solution)/shard_map/ppermute | solution.py:18
  116.1 6.8 %collective-permute-start.12 = (f32[2,80,128]{2,1,0:T(8,128)S(1)}, f32[2,80,128]{2,1,0:T(8,128)S(1)}, u32[]{:S(2)}, u32[]{:S(2)}) collective-permute-start(f32[2,80,128]{2,1,0:T(8,128)S(1)} %get-tuple-element.33), channel_id=1, source_target_pairs={{0,16},{8,24},{16,0},{24,8},{1,17},{9,25},{17,1},{25,9},{2,18},{10... | collective-permute-start | bytes 245768 | tf_op jit(solution)/shard_map/ppermute | solution.py:247
  116.2 6.7 %collective-permute-start.11 = (f32[2,80,128]{2,1,0:T(8,128)S(1)}, f32[2,80,128]{2,1,0:T(8,128)S(1)}, u32[]{:S(2)}, u32[]{:S(2)}) collective-permute-start(f32[2,80,128]{2,1,0:T(8,128)S(1)} %get-tuple-element.34), channel_id=1, source_target_pairs={{0,24},{8,0},{16,8},{24,16},{1,25},{9,1},{17,9},{25,17},{2,26},{10... | collective-permute-start | bytes 245768 | tf_op jit(solution)/shard_map/ppermute | solution.py:247
  118.7 5.7 %collective-permute-start.10 = (f32[2,80,128]{2,1,0:T(8,128)S(1)}, f32[2,80,128]{2,1,0:T(8,128)S(1)}, u32[]{:S(2)}, u32[]{:S(2)}) collective-permute-start(f32[2,80,128]{2,1,0:T(8,128)S(1)} %get-tuple-element.32), channel_id=1, source_target_pairs={{0,8},{8,16},{16,24},{24,0},{1,9},{9,17},{17,25},{25,1},{2,10},{10... | collective-permute-start | bytes 245768 | tf_op jit(solution)/shard_map/ppermute | solution.py:247
  138.5 18.9 %collective-permute-start.18 = (bf16[4,3,48,512]{3,2,1,0:T(8,128)(2,1)}, bf16[4,3,48,512]{3,2,1,0:T(8,128)(2,1)}, u32[]{:S(2)}, u32[]{:S(2)}) collective-permute-start(bf16[4,3,48,512]{3,2,1,0:T(8,128)(2,1)} %hold.7), channel_id=1, source_target_pairs={{0,64},{64,0},{1,65},{65,1},{2,66},{66,2},{3,67},{67,3},{4,68},{68... | collective-permute-start | bytes 1769480 | tf_op jit(solution)/shard_map/ppermute | solution.py:18
  145.5 11.2 %copy-start.3 = (f32[3,4,2,48,128]{4,3,2,0,1:T(8,128)S(1)}, f32[3,4,2,48,128]{4,3,2,0,1:T(8,128)}, u32[]{:S(2)}) copy-start(f32[3,4,2,48,128]{4,3,2,0,1:T(8,128)} %copy.18) | copy-start | bytes 1769476
  146.7 8.2 %collective-permute-start.17 = (f32[7,48,128]{2,1,0:T(8,128)S(1)}, f32[7,48,128]{2,1,0:T(8,128)S(1)}, u32[]{:S(2)}, u32[]{:S(2)}) collective-permute-start(f32[7,48,128]{2,1,0:T(8,128)S(1)} %get-tuple-element.31), channel_id=1, source_target_pairs={{0,16},{8,24},{16,0},{24,8},{1,17},{9,25},{17,1},{25,9},{2,18},{10... | collective-permute-start | bytes 516104 | tf_op jit(solution)/shard_map/ppermute | solution.py:247
  146.8 8.1 %collective-permute-start.16 = (f32[7,48,128]{2,1,0:T(8,128)S(1)}, f32[7,48,128]{2,1,0:T(8,128)S(1)}, u32[]{:S(2)}, u32[]{:S(2)}) collective-permute-start(f32[7,48,128]{2,1,0:T(8,128)S(1)} %get-tuple-element.30), channel_id=1, source_target_pairs={{0,24},{8,0},{16,8},{24,16},{1,25},{9,1},{17,9},{25,17},{2,26},{10... | collective-permute-start | bytes 516104 | tf_op jit(solution)/shard_map/ppermute | solution.py:247
  148.3 8.3 %collective-permute-start.15 = (f32[7,48,128]{2,1,0:T(8,128)S(1)}, f32[7,48,128]{2,1,0:T(8,128)S(1)}, u32[]{:S(2)}, u32[]{:S(2)}) collective-permute-start(f32[7,48,128]{2,1,0:T(8,128)S(1)} %get-tuple-element.29), channel_id=1, source_target_pairs={{0,8},{8,16},{16,24},{24,0},{1,9},{9,17},{17,25},{25,1},{2,10},{10... | collective-permute-start | bytes 516104 | tf_op jit(solution)/shard_map/ppermute | solution.py:247
  160.8 5.8 %collective-permute-start.21 = (f32[2,48,128]{2,1,0:T(8,128)S(1)}, f32[2,48,128]{2,1,0:T(8,128)S(1)}, u32[]{:S(2)}, u32[]{:S(2)}) collective-permute-start(f32[2,48,128]{2,1,0:T(8,128)S(1)} %get-tuple-element.36), channel_id=1, source_target_pairs={{0,4},{2,6},{4,0},{6,2},{1,5},{3,7},{5,1},{7,3},{8,12},{10,14},{12... | collective-permute-start | bytes 147464 | tf_op jit(solution)/shard_map/ppermute | solution.py:263
  163.9 4.1 %collective-permute-start.20 = (f32[2,48,128]{2,1,0:T(8,128)S(1)}, f32[2,48,128]{2,1,0:T(8,128)S(1)}, u32[]{:S(2)}, u32[]{:S(2)}) collective-permute-start(f32[2,48,128]{2,1,0:T(8,128)S(1)} %get-tuple-element.37), channel_id=1, source_target_pairs={{0,6},{2,0},{4,2},{6,4},{1,7},{3,1},{5,3},{7,5},{8,14},{10,8},{12,... | collective-permute-start | bytes 147464 | tf_op jit(solution)/shard_map/ppermute | solution.py:263
  165.0 5.3 %collective-permute-start.19 = (f32[2,48,128]{2,1,0:T(8,128)S(1)}, f32[2,48,128]{2,1,0:T(8,128)S(1)}, u32[]{:S(2)}, u32[]{:S(2)}) collective-permute-start(f32[2,48,128]{2,1,0:T(8,128)S(1)} %get-tuple-element.35), channel_id=1, source_target_pairs={{0,2},{2,4},{4,6},{6,0},{1,3},{3,5},{5,7},{7,1},{8,10},{10,12},{12... | collective-permute-start | bytes 147464 | tf_op jit(solution)/shard_map/ppermute | solution.py:263
  170.3 5.8 %collective-permute-start.22 = (f32[128,128]{1,0:T(8,128)S(1)}, f32[128,128]{1,0:T(8,128)S(1)}, u32[]{:S(2)}, u32[]{:S(2)}) collective-permute-start(f32[128,128]{1,0:T(8,128)S(1)} %fusion.32), channel_id=1, source_target_pairs={{0,1},{1,0},{2,3},{3,2},{4,5},{5,4},{6,7},{7,6},{8,9},{9,8},{10,11... | collective-permute-start | bytes 196616 | tf_op jit(solution)/shard_map/ppermute | solution.py:18
  176.2 1.3 collective-permute-start.23

commit v10 on v9

--- a/solution.py
+++ b/solution.py
@@ -87,12 +87,12 @@
         input_output_aliases={0: 0},
         cost_estimate=HINT,
         name="hold",
-    )(value, *map(mark, after))
-
-
-def front_kernel(owned, at, sols, vecs, out, lines, slab, held, sems):
+    )(value, *after)
+
+
+def front_kernel(owned, index, when, sols, vecs, out, lines, slab, held, sems):
     count, comps, rows, _ = lines.shape
-    group, time = at[0], at[1]
+    group, time = 2 * lax.axis_index("yl") + lax.axis_index("c"), when[0]
     span = held.shape[0] // 4
     part = lambda ref, i: ref.at[pl.ds(i * span, span)]
     into = [
@@ -104,7 +104,7 @@
     first = pl.multiple_of(time // rows * rows, rows)
     picks = [
         pltpu.make_async_copy(
-            vecs.at[at[2 + s] % owned, :, pl.ds(first, rows)], lines.at[s], sems.at[8 + s]
+            vecs.at[index[s] % owned, :, pl.ds(first, rows)], lines.at[s], sems.at[8 + s]
         )
         for s in range(count)
     ]
@@ -117,7 +117,7 @@
     row = lax.broadcasted_iota(jnp.int32, lines.shape[1:], 1)
     for s in range(count):
         picks[s].wait()
-        here = jnp.where(at[2 + s] // owned == group, time % rows, -1)
+        here = jnp.where(index[s] // owned == group, time % rows, -1)
         kept = jnp.sum(jnp.where(row == here, lines[s].astype(jnp.float32), 0.0), axis=1)
         slab[s] = jnp.concatenate([kept, jnp.zeros_like(kept[:2])], axis=0).astype(slab.dtype)
     last.start()
@@ -126,13 +126,12 @@
     last.wait()
 
 
-def front(sols, vecs, source_index, source_time, group):
+def front(sols, vecs, source_index, source_time):
     owned, comps, times, sites = vecs.shape
     count = source_index.shape[0]
-    at = jnp.concatenate([group[None], source_time, source_index])
     out = pl.pallas_call(
         functools.partial(front_kernel, owned),
-        in_specs=[pl.BlockSpec(memory_space=pltpu.SMEM), ANY, ANY],
+        in_specs=[pl.BlockSpec(memory_space=pltpu.SMEM)] * 2 + [ANY] * 2,
         out_specs=ANY,
         out_shape=jax.ShapeDtypeStruct((RAW * comps + 1, count, times // count, sites), sols.dtype),
         scratch_shapes=[
@@ -144,7 +143,7 @@
         compiler_params=pltpu.CompilerParams(vmem_limit_bytes=56 * 2**20),
         cost_estimate=HINT,
         name="front",
-    )(at, sols.reshape(-1, count, times // count, sites), vecs)
+    )(source_index, source_time, sols.reshape(-1, count, times // count, sites), vecs)
     return out.reshape(RAW * comps + 1, times, sites)
 
 
@@ -279,14 +278,14 @@
     sols = solutions[0].transpose(0, 2, 1, 3)
     vecs = eigvecs.transpose(0, 2, 1, 3)
 
-    first_part = front(sols, vecs, source_index, source_time, group)
+    first_part = front(sols, vecs, source_index, source_time)
     raw = swap(first_part, "yl")
     other = swap(vecs, "c")
     parts = ((0, 3, 0, 2), (3, 1, 0, 1), (3, 1, 1, 1))
     sent = [(RAW, count, *part) for part in parts]
     mine, *send = by_time(sols, ((0, count, 0, 4, 0, 2), *sent), first_part)
     send = [rows_of(part) for part in send]
-    got = [swap(send[0], "yl"), swap(hold(send[1], raw), "yl")]
+    got = [swap(send[0], "yl"), swap(hold(send[1], mark(raw)), "yl")]
 
     whole, late = (0, owned, 0, 4, 0, 2), (0, owned, 3, 1, 1, 1)
     own, own_late = by_time(vecs, (whole, late), send[0])
@@ -294,17 +293,17 @@
     own, other = rows_of(own), rows_of(other)
     lines = raw[RAW * comps] + first_part[RAW * comps]
     lines = lines + swap(lines, "c")
-    raw_rows = rows_of(by_time(raw, ((0, RAW, 0, 4, 0, 2),), mark(other), lines)[0])
+    raw_rows = rows_of(by_time(raw, ((0, RAW, 0, 4, 0, 2),), lines)[0])
 
     def against(part, x, y, step, *after):
-        out = project([part], own, other, x, y, step, *map(mark, after))[0]
+        out = project([part], own, other, x, y, step, *after)[0]
         return out.reshape(out.shape[0], 4, -1, 2 * (count - RAW), 2 * owned)
 
     first = project([rows_of(mine), raw_rows], own, other, 0, 0, 8)
 
     slabs = [v.reshape(4, comps // 2, -1, sites) for v in (send[2], own_late)]
-    spread = share_z(jnp.concatenate(slabs, axis=2))
-    spread[1] = hold(spread[1], first[0])
+    spread = share_z(hold(jnp.concatenate(slabs, axis=2), mark(other)))
+    spread[1] = hold(spread[1], mark(first[0]))
     spread = jnp.stack(spread)
     cut = send[2].shape[3]
     spread_s, spread_v = spread[:, :, :cut], spread[:, :, cut:]
@@ -312,15 +311,16 @@
 
     first = [v.reshape(4, 4, 2, -1, 2 * owned) for v in first]
     first = sum_x(jnp.concatenate(first, axis=3))
-    first = sum_z(hold(first, spread_v, spread_w))
-
-    late = [against(got[0], 0, 0, 8, first)]
-    got.append(swap(hold(spread_s, late[0]), "yl"))
+    late = [against(got[0], 0, 0, 8, mark(first), mark(spread_w))]
+    got.append(swap(hold(spread_s, mark(first)), "yl"))
     late.append(against(got[1], 3, 0, 1, late[0]))
-    late = [jnp.swapaxes(v, 0, 1).reshape(4, -1, *v.shape[3:]) for v in late]
-    late = sum_z(jnp.concatenate(late, axis=1))
-    last = project_pieces(got[2], spread_v, spread_w)
-    last = last.reshape(1, -1, 2 * owned)
+    last = project_pieces(got[2], spread_v, spread_w).reshape(1, -1, 2 * owned)
+    late = [jnp.swapaxes(v, 0, 1).reshape(4, -1, 2 * owned) for v in late]
+    late = share_z(jnp.concatenate([first.reshape(4, -1, 2 * owned), *late], axis=1))
+    late = late[0] + late[1] + late[2] + hold(late[3], last)
+    cut = 4 * (count + RAW)
+    first = late[:cut].reshape(2, -1, 2 * owned)
+    late = late[cut:].reshape(7, -1, 2 * owned)
     late = sum_x(jnp.concatenate([late, last]).reshape(4, 2, -1, 2 * owned))
 
     here = sum_yh(jnp.concatenate([first, late], axis=1))

time: 181 us -> 177 us (0.978)
  waiting for transfers between devices: 48.2 us -> 40.9 us
  starting transfers between devices: 29.9 us -> 32.8 us
  local copies, waits for them, and re-layouts: 16.2 us -> 18.9 us
  other arithmetic: 16.6 us -> 14.6 us
    squeeze x4 -> x2, other arithmetic: 5.74 us -> 2.13 us  [pick(): return lax.dynamic_index_in_dim(value, index, 0, keepdims=False)]
    ppermute x9 -> x6, waiting for transfers between devices: 11.2 us -> 7.91 us  [share_z(): lax.ppermute(pick(slabs, (me + k) % 4), 'z', [(i, (i + k) % 4) for i in r...]
    concatenate x1 -> x2, other arithmetic: 1.24 us -> 4.06 us  [the longest x1 2.87 us: local(): spread = share_z(hold(jnp.concatenate(slabs, axis=2), mark(other)))]
    dynamic_slice x0 -> x1, local copies, waits for them, and re-layouts: none -> 2.74 us  [pick(): return lax.dynamic_index_in_dim(value, index, 0, keepdims=False)]
    ppermute x6, waiting for transfers between devices: 16.2 us -> 13.6 us  [sum_x(): total = total + lax.ppermute(pick(slabs, (me + k) % 4), 'x', pairs)]
    unnamed x18 -> x30, local copies, waits for them, and re-layouts: 3.23 us -> 5.59 us
    reshape x1 -> x0, local copies, waits for them, and re-layouts: 1.95 us -> none  [against(): return out.reshape(out.shape[0], 4, -1, 2 * (count - RAW), 2 * owned)]
    transpose x0 -> x1, local copies, waits for them, and re-layouts: none -> 1.93 us  [local(): late = [jnp.swapaxes(v, 0, 1).reshape(4, -1, 2 * owned) for v in late]]
  transfers between devices with their start and end apart: 24 -> 21, of which waited for: 12 -> 11; matrix products, arithmetic and copies ran while one was open for 15% -> 14% of each run, Pallas kernels for 35% -> 38%
where the time goes in v10:
time: 177 us; the launch traced here: 175 us
  Pallas kernels  66.4 us (38%)
  waiting for transfers between devices  40.9 us (23%)
  starting transfers between devices  32.8 us (19%)
  local copies, waits for them, and re-layouts  18.9 us (11%)
  other arithmetic  14.6 us (8%)
    pallas_call x3, Pallas kernels, project(): pl.pallas_call(functools.partial(dot_kernel, len(cols)), grid=(size, inne...  30.6 us
    pallas_call x4, Pallas kernels, by_time(): pl.pallas_call(functools.partial(by_time_kernel, cuts), grid=(4,), in_spe...  29.5 us
    ppermute x9, waiting for transfers between devices, swap(): return lax.ppermute(value, axis, SWAP)  19.4 us
    ppermute x6, waiting for transfers between devices, sum_x(): total = total + lax.ppermute(pick(slabs, (me + k) % 4), 'x', pairs)  13.6 us
    ppermute x6, starting transfers between devices, share_z(): lax.ppermute(pick(slabs, (me + k) % 4), 'z', [(i, (i + k) % 4) for i in r...  13.2 us
    ppermute x6, starting transfers between devices, sum_x(): total = total + lax.ppermute(pick(slabs, (me + k) % 4), 'x', pairs)  10.8 us
    ppermute x9, starting transfers between devices, swap(): return lax.ppermute(value, axis, SWAP)  8.82 us
    ppermute x6, waiting for transfers between devices, share_z(): lax.ppermute(pick(slabs, (me + k) % 4), 'z', [(i, (i + k) % 4) for i in r...  7.91 us
  transfers between devices with their start and end apart: 21, of which 11 were waited for; matrix products, arithmetic and copies ran while one was open for 14% of the time, Pallas kernels for 38%

profile of v10, /device:TPU:0, one launch (start us, length us, event | category | flops | bytes accessed | tf_op | source)
XLA Modules:
  0.0 175.2 jit_solution(1886341575881059172)
XLA Ops:
  1.4 3.0 %front.1 = bf16[49,4,8,512]{3,2,1,0:T(8,128)(2,1)} custom-call(s32[4]{0:T(128)} %index.1, s32[1]{0:T(128)S(6)} %copy.25.when, bf16[192,4,8,512]{3,2,1,0:T(8,128)(2,1)} %bitcast.142, bf16[64,6,32,512]{3,2,1,0:T(8,128)(2,1)} %bitcast.140), custom_call_target="tpu_custom_call" | custom-call | flops 1000 | bytes 1000 | tf_op jit(solution)/shard_map/front/pallas_call | solution.py:132
  4.3 1.7 collective-permute-start
  6.1 7.7 %by_time.4 = (bf16[4,4,2,6,32,512]{5,4,3,2,1,0:T(8,128)(2,1)}, bf16[3,4,2,6,24,512]{5,4,3,2,1,0:T(8,128)(2,1)}, bf16[1,4,1,6,24,512]{5,4,3,2,1,0:T(8,128)(2,1)}, bf16[1,4,1,6,24,512]{5,4,3,2,1,0:T(8,128)(2,1)}) custom-call(bf16[32,6,32,512]{3,2,1,0:T(8,128)(2,1)} %bitcast.143, bf16[49,32,512]{2,1,0:T(8,128)(2,1)} %bitcast.145), custom_call_target="tpu_custom_call" | custom-call | flops 1000 | bytes 1000 | tf_op jit(solution)/shard_map/by_time/pallas_call | solution.py:48
  13.7 0.4 collective-permute-start.6
  14.1 10.7 %by_time.6 = (bf16[4,4,2,6,64,512]{5,4,3,2,1,0:T(8,128)(2,1)}, bf16[1,4,1,6,64,512]{5,4,3,2,1,0:T(8,128)(2,1)}) custom-call(bf16[64,6,32,512]{3,2,1,0:T(8,128)(2,1)} %bitcast.141, bf16[3,8,3,48,512]{4,3,2,1,0:T(8,128)(2,1)} %bitcast.154), custom_call_target="tpu_custom_call" | custom-call | flops 1000 | bytes 1000 | tf_op jit(solution)/shard_map/by_time/pallas_call | solution.py:48
  24.8 2.9 %pad_maximum_fusion.refs_0_ = bf16[4,3,176,512]{3,2,1,0:T(8,128)(2,1)} fusion(bf16[4,3,128,512]{3,2,1,0:T(8,128)(2,1)} %bitcast.156, bf16[4,3,48,512]{3,2,1,0:T(8,128)(2,1)S(1)} %bitcast.166), kind=kLoop, calls=%fused_computation.5 | loop fusion | flops 4325376 | bytes 4325376 | tf_op jit(solution)/shard_map/concatenate | solution.py:305
  27.7 10.5 %by_time.7 = bf16[4,4,2,6,64,512]{5,4,3,2,1,0:T(8,128)(2,1)} custom-call(bf16[64,6,32,512]{3,2,1,0:T(8,128)(2,1)} %collective-permute-done.2.block), custom_call_target="tpu_custom_call" | custom-call | flops 1000 | bytes 1000 | tf_op jit(solution)/shard_map/by_time/pallas_call | solution.py:48
  38.2 1.9 %slice-done = bf16[1,4,2,6,64,512]{5,4,3,2,1,0:T(8,128)(2,1)S(1)} async-done(((bf16[4,4,2,6,64,512]{5,4,3,2,1,0:T(8,128)(2,1)}), bf16[1,4,2,6,64,512]{5,4,3,2,1,0:T(8,128)(2,1)S(1)}, s32[]{:S(2)}) %slice-start) | async-done | bytes 3145752 | tf_op jit(solution)/shard_map/slice | solution.py:73
  40.1 0.7 slice_bitcast_fusion.1.refs_1_
  40.8 2.7 %constant_dynamic-slice_fusion.1 = (bf16[1,3,176,512]{3,2,1,0:T(8,128)(2,1)S(1)}, bf16[3,176,512]{2,1,0:T(8,128)(2,1)}, bf16[3,176,512]{2,1,0:T(8,128)(2,1)}, bf16[3,176,512]{2,1,0:T(8,128)(2,1)S(1)}) fusion(bf16[4,3,176,512]{3,2,1,0:T(8,128)(2,1)} %hold.5, s32[]{:T(128)S(6)} %select_n.135, s32[]{:T(128)S(6)} %select_n.141, s32[]{:T(128)S(6)} %select_n.139, ...), kind=kLoop, calls=%fused_computation.67 | loop fusion | bytes 4325392 | tf_op jit(solution)/shard_map/jit(dynamic_index_in_dim)/dynamic_slice | solution.py:240
  43.5 2.0 %collective-permute-start.7 = (bf16[3,176,512]{2,1,0:T(8,128)(2,1)S(1)}, bf16[3,176,512]{2,1,0:T(8,128)(2,1)S(1)}, u32[]{:S(2)}, u32[]{:S(2)}) collective-permute-start(bf16[3,176,512]{2,1,0:T(8,128)(2,1)S(1)} %get-tuple-element.25), channel_id=1, source_target_pairs={{0,8},{8,16},{16,24},{24,0},{1,9},{9,17},{17,25},{25,1},{2,10},{10... | collective-permute-start | bytes 1622024 | tf_op jit(solution)/shard_map/ppermute | solution.py:246
  45.5 3.6 %collective-permute-start.9 = (bf16[3,176,512]{2,1,0:T(8,128)(2,1)}, bf16[3,176,512]{2,1,0:T(8,128)(2,1)}, u32[]{:S(2)}, u32[]{:S(2)}) collective-permute-start(bf16[3,176,512]{2,1,0:T(8,128)(2,1)} %get-tuple-element.23), channel_id=1, source_target_pairs={{0,16},{8,24},{16,0},{24,8},{1,17},{9,25},{17,1},{25,9},{2,18},{10... | collective-permute-start | bytes 1622024 | tf_op jit(solution)/shard_map/ppermute | solution.py:246
  49.1 1.0 collective-permute-start.8
  50.1 0.8 fusion.20
  50.9 1.2 collective-permute-done.1
  52.1 0.7 by_time.5
  52.8 1.2 copy-done
  53.9 14.7 %project.3 = (f32[4,8,2,32,128]{4,3,2,1,0:T(8,128)}, f32[4,8,2,8,128]{4,3,2,1,0:T(8,128)}) custom-call(bf16[4,8,3,64,512]{4,3,2,1,0:T(8,128)(2,1)} %bitcast.146, bf16[4,8,3,16,512]{4,3,2,1,0:T(8,128)(2,1)} %bitcast.128, bf16[4,8,3,128,512]{4,3,2,1,0:T(8,128)(2,1)} %bitcast.136, bf16[4,8,3,128,512]{4,3,2,1,0:T(8,128)(2,1)} %bitcast.132), custom_call_target="tpu_custom_call" | custom-call | flops 1000 | bytes 1000 | tf_op jit(solution)/shard_map/project/pallas_call | solution.py:227
  68.6 1.3 slice_bitcast_fusion.6.refs_1_
  70.0 0.8 copy-done.4
  70.8 2.1 %collective-permute-done.9 = bf16[3,176,512]{2,1,0:T(8,128)(2,1)} collective-permute-done((bf16[3,176,512]{2,1,0:T(8,128)(2,1)}, bf16[3,176,512]{2,1,0:T(8,128)(2,1)}, u32[]{:S(2)}, u32[]{:S(2)}) %collective-permute-start.9) | collective-permute-done | bytes 540704 | tf_op jit(solution)/shard_map/ppermute | solution.py:246
  72.9 1.6 pad_maximum_fusion.1
  74.8 0.4 copy-done.13
  75.5 2.1 %fusion.8 = (f32[4,2,80,128]{3,2,1,0:T(8,128)}, f32[4,2,80,128]{3,2,1,0:T(8,128)}, f32[4,2,80,128]{3,2,1,0:T(8,128)}) fusion(s32[]{:T(128)S(6)} %select_n.130, f32[4,4,2,64,128]{4,3,2,1,0:T(8,128)} %bitcast.151, f32[4,4,2,16,128]{4,3,2,1,0:T(8,128)S(1)} %bitcast.159, s32[]{:T(128)S(6)} %select_n.132, s32[]{:T(128)S(6)} %select_n.134), kind=kLoop, calls=%fused_computation.25 | loop fusion | flops 245760 | bytes 2293772 | tf_op jit(solution)/shard_map/jit(dynamic_index_in_dim)/squeeze | solution.py:240
  77.6 1.5 collective-permute-start.3
  79.1 1.7 collective-permute-start.4
  80.9 1.8 %collective-permute-start.5 = (f32[4,2,80,128]{3,2,1,0:T(8,128)}, f32[4,2,80,128]{3,2,1,0:T(8,128)}, u32[]{:S(2)}, u32[]{:S(2)}) collective-permute-start(f32[4,2,80,128]{3,2,1,0:T(8,128)} %get-tuple-element.28), channel_id=1, source_target_pairs={{0,4},{2,6},{4,0},{6,2},{1,5},{3,7},{5,1},{7,3},{8,12},{10,14},{12... | collective-permute-start | bytes 983048 | tf_op jit(solution)/shard_map/ppermute | solution.py:262
  82.8 1.4 slice_bitcast_fusion.3.refs_1_
  84.2 4.5 %collective-permute-done.3 = f32[4,2,80,128]{3,2,1,0:T(8,128)S(1)} collective-permute-done((f32[4,2,80,128]{3,2,1,0:T(8,128)}, f32[4,2,80,128]{3,2,1,0:T(8,128)S(1)}, u32[]{:S(2)}, u32[]{:S(2)}) %collective-permute-start.3) | collective-permute-done | bytes 327712 | tf_op jit(solution)/shard_map/ppermute | solution.py:262
  88.7 1.5 collective-permute-start.11
  90.2 4.8 %collective-permute-done.4 = f32[4,2,80,128]{3,2,1,0:T(8,128)} collective-permute-done((f32[4,2,80,128]{3,2,1,0:T(8,128)}, f32[4,2,80,128]{3,2,1,0:T(8,128)}, u32[]{:S(2)}, u32[]{:S(2)}) %collective-permute-start.4) | collective-permute-done | bytes 327712 | tf_op jit(solution)/shard_map/ppermute | solution.py:262
  95.1 1.7 collective-permute-done.5
  96.7 1.3 fusion.6
  98.1 0.6 slice_bitcast_fusion.2.refs_3_.refs_1_
  98.7 1.8 %pad_maximum_fusion.3.refs_0_ = bf16[4,3,48,512]{3,2,1,0:T(8,128)(2,1)} fusion(bf16[1,3,176,512]{3,2,1,0:T(8,128)(2,1)} %bitcast.41, bf16[1,3,176,512]{3,2,1,0:T(8,128)(2,1)} %bitcast.39, bf16[1,3,176,512]{3,2,1,0:T(8,128)(2,1)S(1)} %bitcast.150, bf16[1,3,176,512]{3,2,1,0:T(8,128)(2,1)S(1)} %copy-done.7), kind=kLoop, calls=%fused_computation.12 | loop fusion | flops 2359296 | bytes 2752512 | tf_op jit(solution)/shard_map/slice | solution.py:309
  100.5 0.6 gather_fusion
  101.1 1.6 collective-permute-start.15
  102.7 0.7 slice_bitcast_fusion.refs_4_
  103.4 15.1 %collective-permute-done.6.refs_0_ = bf16[3,8,3,48,512]{4,3,2,1,0:T(8,128)(2,1)} collective-permute-done((bf16[3,8,3,48,512]{4,3,2,1,0:T(8,128)(2,1)}, bf16[3,8,3,48,512]{4,3,2,1,0:T(8,128)(2,1)}, u32[]{:S(2)}, u32[]{:S(2)}) %collective-permute-start.6) | collective-permute-done | bytes 3538976 | tf_op jit(solution)/shard_map/ppermute | solution.py:18
  118.5 11.3 %project.4 = f32[3,8,2,24,128]{4,3,2,1,0:T(8,128)} custom-call(bf16[3,8,3,48,512]{4,3,2,1,0:T(8,128)(2,1)} %collective-permute-done.6.refs_0_, bf16[4,8,3,128,512]{4,3,2,1,0:T(8,128)(2,1)} %bitcast.137, bf16[4,8,3,128,512]{4,3,2,1,0:T(8,128)(2,1)} %bitcast.133, f32[80,128]{1,0:T(8,128)} %slice_bitcast_fusion.2.refs_3_.refs_1_, ...), custom_call_target="tpu_custom_call" | custom-call | flops 1000 | bytes 1000 | tf_op jit(solution)/shard_map/project/pallas_call | solution.py:227
  129.8 1.9 %copy.17 = f32[4,3,2,48,128]{4,3,2,1,0:T(8,128)} copy(f32[4,3,2,48,128]{4,3,2,0,1:T(8,128)} %bitcast.147) | data formatting | bytes 1179648 | tf_op jit(solution)/shard_map/transpose | solution.py:318
  131.7 4.6 %project.5 = f32[1,4,2,24,128]{4,3,2,1,0:T(8,128)} custom-call(bf16[1,4,3,48,512]{4,3,2,1,0:T(8,128)(2,1)} %collective-permute-done.11.refs_0_, bf16[4,8,3,128,512]{4,3,2,1,0:T(8,128)(2,1)} %bitcast.138, bf16[4,8,3,128,512]{4,3,2,1,0:T(8,128)(2,1)} %bitcast.134, f32[3,4,2,48,128]{4,3,2,1,0:T(8,128)} %bitcast.148), custom_call_target="tpu_custom_call" | custom-call | flops 1000 | bytes 1000 | tf_op jit(solution)/shard_map/project/pallas_call | solution.py:227
  136.3 1.2 pad_maximum_fusion.2
  137.5 1.0 copy-done.8
  138.5 0.9 dynamic-slice_bitcast_fusion.5
  139.4 2.0 %collective-permute-start.12 = (f32[496,128]{1,0:T(8,128)}, f32[496,128]{1,0:T(8,128)}, u32[]{:S(2)}, u32[]{:S(2)}) collective-permute-start(f32[496,128]{1,0:T(8,128)} %get-tuple-element.29), channel_id=1, source_target_pairs={{0,8},{8,16},{16,24},{24,0},{1,9},{9,17},{17,25},{25,1},{2,10},{10... | collective-permute-start | bytes 761864 | tf_op jit(solution)/shard_map/ppermute | solution.py:246
  141.4 3.6 %collective-permute-start.14 = (f32[496,128]{1,0:T(8,128)}, f32[496,128]{1,0:T(8,128)S(1)}, u32[]{:S(2)}, u32[]{:S(2)}) collective-permute-start(f32[496,128]{1,0:T(8,128)} %get-tuple-element.30), channel_id=1, source_target_pairs={{0,16},{8,24},{16,0},{24,8},{1,17},{9,25},{17,1},{25,9},{2,18},{10... | collective-permute-start | bytes 761864 | tf_op jit(solution)/shard_map/ppermute | solution.py:246
  145.0 1.0 collective-permute-start.13
  146.3 3.3 %project_pieces.1 = f32[2,24,128]{2,1,0:T(8,128)S(1)} custom-call(bf16[4,3,48,512]{3,2,1,0:T(8,128)(2,1)} %collective-permute-done.15.col, bf16[4,3,128,512]{3,2,1,0:T(8,128)(2,1)S(1)} %slice.110.own, bf16[4,3,128,512]{3,2,1,0:T(8,128)(2,1)S(1)} %collective-permute-done.10.other), custom_call_target="tpu_custom_call" | custom-call | flops 1000 | bytes 1000 | tf_op jit(solution)/shard_map/project_pieces/pallas_call | solution.py:200
  149.6 0.6 copy-done.2
  150.2 5.8 %collective-permute-done.14.refs_0_ = f32[496,128]{1,0:T(8,128)S(1)} collective-permute-done((f32[496,128]{1,0:T(8,128)}, f32[496,128]{1,0:T(8,128)S(1)}, u32[]{:S(2)}, u32[]{:S(2)}) %collective-permute-start.14) | collective-permute-done | bytes 253984 | tf_op jit(solution)/shard_map/ppermute | solution.py:246
  156.0 0.7 copy-done.10
  156.7 1.4 fusion.12
  158.1 1.6 collective-permute-start.16
  159.7 2.7 %collective-permute-start.18 = (f32[2,48,128]{2,1,0:T(8,128)S(1)}, f32[2,48,128]{2,1,0:T(8,128)S(1)}, u32[]{:S(2)}, u32[]{:S(2)}) collective-permute-start(f32[2,48,128]{2,1,0:T(8,128)S(1)} %get-tuple-element.33), channel_id=1, source_target_pairs={{0,4},{2,6},{4,0},{6,2},{1,5},{3,7},{5,1},{7,3},{8,12},{10,14},{12... | collective-permute-start | bytes 147464 | tf_op jit(solution)/shard_map/ppermute | solution.py:262
  162.4 1.4 collective-permute-start.17
  164.0 1.3 collective-permute-done.18
  165.3 1.2 collective-permute-done.17
  166.6 3.3 %collective-permute-start.19 = (f32[128,128]{1,0:T(8,128)S(1)}, f32[128,128]{1,0:T(8,128)S(1)}, u32[]{:S(2)}, u32[]{:S(2)}) collective-permute-start(f32[128,128]{1,0:T(8,128)S(1)} %fusion.14), channel_id=1, source_target_pairs={{0,1},{1,0},{2,3},{3,2},{4,5},{5,4},{6,7},{7,6},{8,9},{9,8},{10,11... | collective-permute-start | bytes 196616 | tf_op jit(solution)/shard_map/ppermute | solution.py:18
  169.8 0.7 broadcast_select_fusion
  170.6 1.8 %collective-permute-done.19 = f32[128,128]{1,0:T(8,128)S(1)} collective-permute-done((f32[128,128]{1,0:T(8,128)S(1)}, f32[128,128]{1,0:T(8,128)S(1)}, u32[]{:S(2)}, u32[]{:S(2)}) %collective-permute-start.19) | collective-permute-done | bytes 65568 | tf_op jit(solution)/shard_map/ppermute | solution.py:18
  172.6 1.2 collective-permute-done.20
  174.1 0.2 select_reduce_fusion
  174.5 0.7 copy.19
  (70 shorter events, 1.7 us)
Async XLA Ops:
  0.6 27.1 %collective-permute-start.2 = (bf16[64,6,32,512]{3,2,1,0:T(8,128)(2,1)}, bf16[64,6,32,512]{3,2,1,0:T(8,128)(2,1)}, u32[]{:S(2)}, u32[]{:S(2)}) collective-permute-start(bf16[64,6,32,512]{3,2,1,0:T(8,128)(2,1)} %bitcast.139), channel_id=1, source_target_pairs={{0,32},{32,0},{1,33},{33,1},{2,34},{34,2},{3,35},{35,3},{4,36},{36... | collective-permute-start | bytes 37748744 | tf_op jit(solution)/shard_map/ppermute | solution.py:18
  4.3 45.8 %collective-permute-start = (bf16[49,32,512]{2,1,0:T(8,128)(2,1)}, bf16[49,32,512]{2,1,0:T(8,128)(2,1)S(1)}, u32[]{:S(2)}, u32[]{:S(2)}) collective-permute-start(bf16[49,32,512]{2,1,0:T(8,128)(2,1)} %bitcast.144), channel_id=1, source_target_pairs={{0,64},{64,0},{1,65},{65,1},{2,66},{66,2},{3,67},{67,3},{4,68},{68... | collective-permute-start | bytes 4816904 | tf_op jit(solution)/shard_map/ppermute | solution.py:18
  13.7 11.1 %copy-start.11 = (bf16[1,4,1,6,24,512]{5,4,3,2,1,0:T(8,128)(2,1)S(1)}, bf16[1,4,1,6,24,512]{5,4,3,2,1,0:T(8,128)(2,1)}, u32[]{:S(2)}) copy-start(bf16[1,4,1,6,24,512]{5,4,3,2,1,0:T(8,128)(2,1)} %get-tuple-element.15) | copy-start | bytes 1769476
  13.7 104.7 %collective-permute-start.6 = (bf16[3,8,3,48,512]{4,3,2,1,0:T(8,128)(2,1)}, bf16[3,8,3,48,512]{4,3,2,1,0:T(8,128)(2,1)}, u32[]{:S(2)}, u32[]{:S(2)}) collective-permute-start(bf16[3,8,3,48,512]{4,3,2,1,0:T(8,128)(2,1)} %bitcast.153), channel_id=1, source_target_pairs={{0,64},{64,0},{1,65},{65,1},{2,66},{66,2},{3,67},{67,3},{4,68},{68... | collective-permute-start | bytes 10616840 | tf_op jit(solution)/shard_map/ppermute | solution.py:18
  38.2 1.9 %slice-start = ((bf16[4,4,2,6,64,512]{5,4,3,2,1,0:T(8,128)(2,1)}), bf16[1,4,2,6,64,512]{5,4,3,2,1,0:T(8,128)(2,1)S(1)}, s32[]{:S(2)}) async-start(bf16[4,4,2,6,64,512]{5,4,3,2,1,0:T(8,128)(2,1)} %by_time.7), calls=%async_computation | async-start | bytes 6291456 | tf_op jit(solution)/shard_map/slice | solution.py:73
  43.5 29.4 %copy-start.6 = (bf16[1,3,176,512]{3,2,1,0:T(8,128)(2,1)}, bf16[1,3,176,512]{3,2,1,0:T(8,128)(2,1)S(1)}, u32[]{:S(2)}) copy-start(bf16[1,3,176,512]{3,2,1,0:T(8,128)(2,1)S(1)} %get-tuple-element.22) | copy-start | bytes 1622020
  43.5 26.5 %collective-permute-start.7 = (bf16[3,176,512]{2,1,0:T(8,128)(2,1)S(1)}, bf16[3,176,512]{2,1,0:T(8,128)(2,1)S(1)}, u32[]{:S(2)}, u32[]{:S(2)}) collective-permute-start(bf16[3,176,512]{2,1,0:T(8,128)(2,1)S(1)} %get-tuple-element.25), channel_id=1, source_target_pairs={{0,8},{8,16},{16,24},{24,0},{1,9},{9,17},{17,25},{25,1},{2,10},{10... | collective-permute-start | bytes 1622024 | tf_op jit(solution)/shard_map/ppermute | solution.py:246
  45.5 27.4 %collective-permute-start.9 = (bf16[3,176,512]{2,1,0:T(8,128)(2,1)}, bf16[3,176,512]{2,1,0:T(8,128)(2,1)}, u32[]{:S(2)}, u32[]{:S(2)}) collective-permute-start(bf16[3,176,512]{2,1,0:T(8,128)(2,1)} %get-tuple-element.23), channel_id=1, source_target_pairs={{0,16},{8,24},{16,0},{24,8},{1,17},{9,25},{17,1},{25,9},{2,18},{10... | collective-permute-start | bytes 1622024 | tf_op jit(solution)/shard_map/ppermute | solution.py:246
  49.1 23.8 %collective-permute-start.8 = (bf16[3,176,512]{2,1,0:T(8,128)(2,1)}, bf16[3,176,512]{2,1,0:T(8,128)(2,1)}, u32[]{:S(2)}, u32[]{:S(2)}) collective-permute-start(bf16[3,176,512]{2,1,0:T(8,128)(2,1)} %get-tuple-element.24), channel_id=1, source_target_pairs={{0,24},{8,0},{16,8},{24,16},{1,25},{9,1},{17,9},{25,17},{2,26},{10... | collective-permute-start | bytes 1622024 | tf_op jit(solution)/shard_map/ppermute | solution.py:246
  50.1 18.5 %copy-start.1 = (bf16[49,32,512]{2,1,0:T(8,128)(2,1)}, bf16[49,32,512]{2,1,0:T(8,128)(2,1)S(1)}, u32[]{:S(2)}) copy-start(bf16[49,32,512]{2,1,0:T(8,128)(2,1)S(1)} %collective-permute-done.block) | copy-start | bytes 4816900
  50.9 1.2 collective-permute-start.1
  52.8 1.2 copy-start
  70.0 0.8 copy-start.4
  74.5 0.7 copy-start.13
  74.6 1.0 copy-start.9
  74.7 28.0 %collective-permute-start.10 = (bf16[4,3,128,512]{3,2,1,0:T(8,128)(2,1)S(1)}, bf16[4,3,128,512]{3,2,1,0:T(8,128)(2,1)S(1)}, u32[]{:S(2)}, u32[]{:S(2)}) collective-permute-start(bf16[4,3,128,512]{3,2,1,0:T(8,128)(2,1)S(1)} %slice.110.own), channel_id=1, source_target_pairs={{0,32},{32,0},{1,33},{33,1},{2,34},{34,2},{3,35},{35,3},{4,36},{36... | collective-permute-start | bytes 4718600 | tf_op jit(solution)/shard_map/ppermute | solution.py:18
  77.6 11.0 %collective-permute-start.3 = (f32[4,2,80,128]{3,2,1,0:T(8,128)}, f32[4,2,80,128]{3,2,1,0:T(8,128)S(1)}, u32[]{:S(2)}, u32[]{:S(2)}) collective-permute-start(f32[4,2,80,128]{3,2,1,0:T(8,128)} %get-tuple-element.26), channel_id=1, source_target_pairs={{0,2},{2,4},{4,6},{6,0},{1,3},{3,5},{5,7},{7,1},{8,10},{10,12},{12... | collective-permute-start | bytes 983048 | tf_op jit(solution)/shard_map/ppermute | solution.py:262
  79.1 15.9 %collective-permute-start.4 = (f32[4,2,80,128]{3,2,1,0:T(8,128)}, f32[4,2,80,128]{3,2,1,0:T(8,128)}, u32[]{:S(2)}, u32[]{:S(2)}) collective-permute-start(f32[4,2,80,128]{3,2,1,0:T(8,128)} %get-tuple-element.27), channel_id=1, source_target_pairs={{0,6},{2,0},{4,2},{6,4},{1,7},{3,1},{5,3},{7,5},{8,14},{10,8},{12,... | collective-permute-start | bytes 983048 | tf_op jit(solution)/shard_map/ppermute | solution.py:262
  80.9 15.9 %collective-permute-start.5 = (f32[4,2,80,128]{3,2,1,0:T(8,128)}, f32[4,2,80,128]{3,2,1,0:T(8,128)}, u32[]{:S(2)}, u32[]{:S(2)}) collective-permute-start(f32[4,2,80,128]{3,2,1,0:T(8,128)} %get-tuple-element.28), channel_id=1, source_target_pairs={{0,4},{2,6},{4,0},{6,2},{1,5},{3,7},{5,1},{7,3},{8,12},{10,14},{12... | collective-permute-start | bytes 983048 | tf_op jit(solution)/shard_map/ppermute | solution.py:262
  84.1 14.5 %copy-start.5 = (bf16[3,176,512]{2,1,0:T(8,128)(2,1)S(1)}, bf16[3,176,512]{2,1,0:T(8,128)(2,1)}, u32[]{:S(2)}) copy-start(bf16[3,176,512]{2,1,0:T(8,128)(2,1)} %hold.6) | copy-start | bytes 1622020
  84.1 14.5 %copy-start.7 = (bf16[1,3,176,512]{3,2,1,0:T(8,128)(2,1)S(1)}, bf16[1,3,176,512]{3,2,1,0:T(8,128)(2,1)}, u32[]{:S(2)}) copy-start(bf16[1,3,176,512]{3,2,1,0:T(8,128)(2,1)} %copy-done.6) | copy-start | bytes 1622020
  88.7 6.4 %copy-start.12 = (f32[4,2,80,128]{3,2,1,0:T(8,128)}, f32[4,2,80,128]{3,2,1,0:T(8,128)S(1)}, u32[]{:S(2)}) copy-start(f32[4,2,80,128]{3,2,1,0:T(8,128)S(1)} %collective-permute-done.3) | copy-start | bytes 983044
  88.7 43.1 %collective-permute-start.11 = (bf16[1,4,3,48,512]{4,3,2,1,0:T(8,128)(2,1)}, bf16[1,4,3,48,512]{4,3,2,1,0:T(8,128)(2,1)}, u32[]{:S(2)}, u32[]{:S(2)}) collective-permute-start(bf16[1,4,3,48,512]{4,3,2,1,0:T(8,128)(2,1)} %hold.7), channel_id=1, source_target_pairs={{0,64},{64,0},{1,65},{65,1},{2,66},{66,2},{3,67},{67,3},{4,68},{68... | collective-permute-start | bytes 1769480 | tf_op jit(solution)/shard_map/ppermute | solution.py:18
  101.1 45.2 %collective-permute-start.15 = (bf16[4,3,48,512]{3,2,1,0:T(8,128)(2,1)}, bf16[4,3,48,512]{3,2,1,0:T(8,128)(2,1)}, u32[]{:S(2)}, u32[]{:S(2)}) collective-permute-start(bf16[4,3,48,512]{3,2,1,0:T(8,128)(2,1)} %hold.8), channel_id=1, source_target_pairs={{0,64},{64,0},{1,65},{65,1},{2,66},{66,2},{3,67},{67,3},{4,68},{68... | collective-permute-start | bytes 1769480 | tf_op jit(solution)/shard_map/ppermute | solution.py:18
  137.5 1.0 copy-start.8
  139.4 17.3 %collective-permute-start.12 = (f32[496,128]{1,0:T(8,128)}, f32[496,128]{1,0:T(8,128)}, u32[]{:S(2)}, u32[]{:S(2)}) collective-permute-start(f32[496,128]{1,0:T(8,128)} %get-tuple-element.29), channel_id=1, source_target_pairs={{0,8},{8,16},{16,24},{24,0},{1,9},{9,17},{17,25},{25,1},{2,10},{10... | collective-permute-start | bytes 761864 | tf_op jit(solution)/shard_map/ppermute | solution.py:246
  141.4 14.6 %collective-permute-start.14 = (f32[496,128]{1,0:T(8,128)}, f32[496,128]{1,0:T(8,128)S(1)}, u32[]{:S(2)}, u32[]{:S(2)}) collective-permute-start(f32[496,128]{1,0:T(8,128)} %get-tuple-element.30), channel_id=1, source_target_pairs={{0,16},{8,24},{16,0},{24,8},{1,17},{9,25},{17,1},{25,9},{2,18},{10... | collective-permute-start | bytes 761864 | tf_op jit(solution)/shard_map/ppermute | solution.py:246
  145.0 11.7 %collective-permute-start.13 = (f32[496,128]{1,0:T(8,128)}, f32[496,128]{1,0:T(8,128)}, u32[]{:S(2)}, u32[]{:S(2)}) collective-permute-start(f32[496,128]{1,0:T(8,128)} %get-tuple-element.31), channel_id=1, source_target_pairs={{0,24},{8,0},{16,8},{24,16},{1,25},{9,1},{17,9},{25,17},{2,26},{10... | collective-permute-start | bytes 761864 | tf_op jit(solution)/shard_map/ppermute | solution.py:246
  149.6 0.6 copy-start.2
  156.0 0.7 copy-start.10
  156.0 2.1 %copy-start.3 = (f32[2,24,128]{2,1,0:T(8,128)S(1)}, f32[2,24,128]{2,1,0:T(8,128)}, u32[]{:S(2)}) copy-start(f32[2,24,128]{2,1,0:T(8,128)} %copy-done.2) | copy-start | bytes 73732
  158.1 5.8 %collective-permute-start.16 = (f32[2,48,128]{2,1,0:T(8,128)S(1)}, f32[2,48,128]{2,1,0:T(8,128)S(1)}, u32[]{:S(2)}, u32[]{:S(2)}) collective-permute-start(f32[2,48,128]{2,1,0:T(8,128)S(1)} %get-tuple-element.32), channel_id=1, source_target_pairs={{0,2},{2,4},{4,6},{6,0},{1,3},{3,5},{5,7},{7,1},{8,10},{10,12},{12... | collective-permute-start | bytes 147464 | tf_op jit(solution)/shard_map/ppermute | solution.py:262
  159.7 5.6 %collective-permute-start.18 = (f32[2,48,128]{2,1,0:T(8,128)S(1)}, f32[2,48,128]{2,1,0:T(8,128)S(1)}, u32[]{:S(2)}, u32[]{:S(2)}) collective-permute-start(f32[2,48,128]{2,1,0:T(8,128)S(1)} %get-tuple-element.33), channel_id=1, source_target_pairs={{0,4},{2,6},{4,0},{6,2},{1,5},{3,7},{5,1},{7,3},{8,12},{10,14},{12... | collective-permute-start | bytes 147464 | tf_op jit(solution)/shard_map/ppermute | solution.py:262
  162.4 4.1 %collective-permute-start.17 = (f32[2,48,128]{2,1,0:T(8,128)S(1)}, f32[2,48,128]{2,1,0:T(8,128)S(1)}, u32[]{:S(2)}, u32[]{:S(2)}) collective-permute-start(f32[2,48,128]{2,1,0:T(8,128)S(1)} %get-tuple-element.34), channel_id=1, source_target_pairs={{0,6},{2,0},{4,2},{6,4},{1,7},{3,1},{5,3},{7,5},{8,14},{10,8},{12,... | collective-permute-start | bytes 147464 | tf_op jit(solution)/shard_map/ppermute | solution.py:262
  166.6 5.8 %collective-permute-start.19 = (f32[128,128]{1,0:T(8,128)S(1)}, f32[128,128]{1,0:T(8,128)S(1)}, u32[]{:S(2)}, u32[]{:S(2)}) collective-permute-start(f32[128,128]{1,0:T(8,128)S(1)} %fusion.14), channel_id=1, source_target_pairs={{0,1},{1,0},{2,3},{3,2},{4,5},{5,4},{6,7},{7,6},{8,9},{9,8},{10,11... | collective-permute-start | bytes 196616 | tf_op jit(solution)/shard_map/ppermute | solution.py:18
  172.4 1.3 collective-permute-start.20

commit v11 on v10

--- a/solution.py
+++ b/solution.py
@@ -10,7 +10,6 @@
 from jax.sharding import PartitionSpec as P
 
 MASS = 2
-RAW = 8
 SWAP = [(0, 1), (1, 0)]
 
 
@@ -24,13 +23,8 @@
 
 def by_time_kernel(cuts, block, *refs):
     outs = refs[-len(cuts) :]
-    comps = refs[-1].shape[3]
-    for k in range(comps):
-        if len(block.shape) == 4:
-            part = block[:, k]
-        else:
-            part = jnp.stack([block[n * comps + k] for n in range(block.shape[0] // comps)])
-        turned = jnp.swapaxes(part, 0, 1)
+    for k in range(block.shape[1]):
+        turned = jnp.swapaxes(block[:, k], 0, 1)
         for (low, high, x, nx, y, ny), out in zip(cuts, outs):
             for i in range(nx):
                 for j in range(ny):
@@ -38,13 +32,8 @@
 
 
 def by_time(block, cuts, *after):
-    if block.ndim == 4:
-        n, comps, times, sites = block.shape
-        spec = pl.BlockSpec((n, comps, times // 4, sites), lambda z: (0, 0, z, 0))
-    else:
-        n, comps = RAW, block.shape[0] // RAW
-        _, times, sites = block.shape
-        spec = pl.BlockSpec((n * comps, times // 4, sites), lambda z: (0, z, 0))
+    n, comps, times, sites = block.shape
+    spec = pl.BlockSpec((n, comps, times // 4, sites), lambda z: (0, 0, z, 0))
     return pl.pallas_call(
         functools.partial(by_time_kernel, cuts),
         grid=(4,),
@@ -57,7 +46,7 @@
             jax.ShapeDtypeStruct((nx, 4, ny, comps, high - low, sites), block.dtype)
             for low, high, _, nx, _, ny in cuts
         ],
-        compiler_params=pltpu.CompilerParams(vmem_limit_bytes=(56 if n > RAW else 16) * 2**20),
+        compiler_params=pltpu.CompilerParams(vmem_limit_bytes=56 * 2**20),
         cost_estimate=HINT,
         name="by_time",
     )(block, *after)
@@ -90,61 +79,43 @@
     )(value, *after)
 
 
-def front_kernel(owned, index, when, sols, vecs, out, lines, slab, held, sems):
+def choose_kernel(owned, index, when, vecs, out, lines, sems):
     count, comps, rows, _ = lines.shape
     group, time = 2 * lax.axis_index("yl") + lax.axis_index("c"), when[0]
-    span = held.shape[0] // 4
-    part = lambda ref, i: ref.at[pl.ds(i * span, span)]
-    into = [
-        pltpu.make_async_copy(part(sols, i), part(held, i), sems.at[i]) for i in range(4)
-    ]
-    outof = [
-        pltpu.make_async_copy(part(held, i), part(out, i), sems.at[4 + i]) for i in range(4)
-    ]
     first = pl.multiple_of(time // rows * rows, rows)
     picks = [
         pltpu.make_async_copy(
-            vecs.at[index[s] % owned, :, pl.ds(first, rows)], lines.at[s], sems.at[8 + s]
+            vecs.at[index[s] % owned, :, pl.ds(first, rows)], lines.at[s], sems.at[s]
         )
         for s in range(count)
     ]
-    last = pltpu.make_async_copy(slab, out.at[held.shape[0]], sems.at[8 + count])
-    for copy in into + picks:
+    for copy in picks:
         copy.start()
-    for i in range(4):
-        into[i].wait()
-        outof[i].start()
     row = lax.broadcasted_iota(jnp.int32, lines.shape[1:], 1)
     for s in range(count):
         picks[s].wait()
         here = jnp.where(index[s] // owned == group, time % rows, -1)
         kept = jnp.sum(jnp.where(row == here, lines[s].astype(jnp.float32), 0.0), axis=1)
-        slab[s] = jnp.concatenate([kept, jnp.zeros_like(kept[:2])], axis=0).astype(slab.dtype)
-    last.start()
-    for i in range(4):
-        outof[i].wait()
-    last.wait()
-
-
-def front(sols, vecs, source_index, source_time):
+        out[s] = jnp.concatenate([kept, jnp.zeros_like(kept[:2])], axis=0).astype(out.dtype)
+
+
+def choose(vecs, source_index, source_time, after):
     owned, comps, times, sites = vecs.shape
     count = source_index.shape[0]
-    out = pl.pallas_call(
-        functools.partial(front_kernel, owned),
+    kernel = functools.partial(choose_kernel, owned)
+    return pl.pallas_call(
+        lambda index, when, vecs, after, *refs: kernel(index, when, vecs, *refs),
         in_specs=[pl.BlockSpec(memory_space=pltpu.SMEM)] * 2 + [ANY] * 2,
-        out_specs=ANY,
-        out_shape=jax.ShapeDtypeStruct((RAW * comps + 1, count, times // count, sites), sols.dtype),
+        out_specs=pl.BlockSpec(memory_space=pltpu.VMEM),
+        out_shape=jax.ShapeDtypeStruct((count, 8, sites), vecs.dtype),
         scratch_shapes=[
-            pltpu.VMEM((count, comps, 16, sites), sols.dtype),
-            pltpu.VMEM((count, times // count, sites), sols.dtype),
-            pltpu.VMEM((RAW * comps, count, times // count, sites), sols.dtype),
-            pltpu.SemaphoreType.DMA((9 + count,)),
+            pltpu.VMEM((count, comps, 16, sites), vecs.dtype),
+            pltpu.SemaphoreType.DMA((count,)),
         ],
-        compiler_params=pltpu.CompilerParams(vmem_limit_bytes=56 * 2**20),
-        cost_estimate=HINT,
-        name="front",
-    )(source_index, source_time, sols.reshape(-1, count, times // count, sites), vecs)
-    return out.reshape(RAW * comps + 1, times, sites)
+        compiler_params=pltpu.CompilerParams(vmem_limit_bytes=60 * 2**20),
+        cost_estimate=HINT,
+        name="choose",
+    )(source_index, source_time, vecs, after)
 
 
 def product(cols, own, other):
@@ -183,26 +154,28 @@
             row += 2 * n
 
 
-def pieces_kernel(col, own, other, out):
-    total = None
-    for colour in range(own.shape[1]):
-        term = product([col[0, colour]], own[0, colour], other[0, colour])
+def pieces_kernel(col, own, other, *refs):
+    total, out = None, refs[-1]
+    for colour in range(own.shape[2]):
+        pair = [col[2 * colour], col[2 * colour + 1]]
+        term = product(pair, own[0, 0, colour], other[0, 0, colour])
         total = term if total is None else total + term
     here = pl.program_id(0)
     for part, value in enumerate(real_imag(total, 0, out.shape[1])):
         out[part] = jnp.where(here == 0, value, out[part] + value)
 
 
-def project_pieces(cols, own, other, *after):
-    count, _, n2, _ = cols.shape
-    rows = own.shape[2]
-    spec = lambda v: pl.BlockSpec((1,) + v.shape[1:], lambda i: (i, 0, 0, 0))
+def project_pieces(cols, own, other, y, *after):
+    count, _, colours, rows, sites = own.shape
+    n = cols.shape[1]
+    vecs = pl.BlockSpec((1, 1, colours, rows, sites), lambda i: (i, y, 0, 0, 0))
     return pl.pallas_call(
         pieces_kernel,
         grid=(count,),
-        in_specs=[spec(cols), spec(own), spec(other)] + [ANY] * len(after),
-        out_specs=pl.BlockSpec((2, n2 // 2, rows), lambda i: (0, 0, 0)),
-        out_shape=jax.ShapeDtypeStruct((2, n2 // 2, rows), jnp.float32),
+        in_specs=[pl.BlockSpec((2 * colours, n, sites), lambda i: (i, 0, 0)), vecs, vecs]
+        + [ANY] * len(after),
+        out_specs=pl.BlockSpec((2, n, rows), lambda i: (0, 0, 0)),
+        out_shape=jax.ShapeDtypeStruct((2, n, rows), jnp.float32),
         compiler_params=pltpu.CompilerParams(vmem_limit_bytes=16 * 2**20),
         cost_estimate=HINT,
         name="project_pieces",
@@ -278,60 +251,55 @@
     sols = solutions[0].transpose(0, 2, 1, 3)
     vecs = eigvecs.transpose(0, 2, 1, 3)
 
-    first_part = front(sols, vecs, source_index, source_time)
-    raw = swap(first_part, "yl")
     other = swap(vecs, "c")
-    parts = ((0, 3, 0, 2), (3, 1, 0, 1), (3, 1, 1, 1))
-    sent = [(RAW, count, *part) for part in parts]
-    mine, *send = by_time(sols, ((0, count, 0, 4, 0, 2), *sent), first_part)
-    send = [rows_of(part) for part in send]
-    got = [swap(send[0], "yl"), swap(hold(send[1], mark(raw)), "yl")]
-
-    whole, late = (0, owned, 0, 4, 0, 2), (0, owned, 3, 1, 1, 1)
-    own, own_late = by_time(vecs, (whole, late), send[0])
+    mine = by_time(sols, ((0, count, 0, 3, 0, 2), (0, count, 3, 1, 0, 2)))
+    mine = [rows_of(part) for part in mine]
+    got = swap(mine[0], "yl")
+
+    whole, late = (0, owned, 0, 4, 0, 2), (0, owned, 3, 1, 0, 2)
+    own, own_late = by_time(vecs, (whole, late), mine[0])
     other = by_time(other, (whole,))[0]
     own, other = rows_of(own), rows_of(other)
-    lines = raw[RAW * comps] + first_part[RAW * comps]
-    lines = lines + swap(lines, "c")
-    raw_rows = rows_of(by_time(raw, ((0, RAW, 0, 4, 0, 2),), lines)[0])
-
-    def against(part, x, y, step, *after):
-        out = project([part], own, other, x, y, step, *after)[0]
-        return out.reshape(out.shape[0], 4, -1, 2 * (count - RAW), 2 * owned)
-
-    first = project([rows_of(mine), raw_rows], own, other, 0, 0, 8)
-
-    slabs = [v.reshape(4, comps // 2, -1, sites) for v in (send[2], own_late)]
-    spread = share_z(hold(jnp.concatenate(slabs, axis=2), mark(other)))
-    spread[1] = hold(spread[1], mark(first[0]))
+    lines = choose(vecs, source_index, source_time, mark(other)).reshape(1, -1, sites)
+
+    def against(part, x, *after):
+        out = project([part], own, other, x, 0, 8, *after)[0]
+        return out.reshape(out.shape[0], 4, 2, 2 * count, 2 * owned)
+
+    slabs = [v.reshape(4, 2, comps // 2, -1, sites) for v in (mine[1], own_late)]
+    spread = share_z(hold(jnp.concatenate(slabs, axis=3), mark(other)))
+    first = [against(mine[0], 0), against(mine[1], 3)]
+    spread[1] = hold(spread[1], mark(first[0]), mark(first[1]))
     spread = jnp.stack(spread)
-    cut = send[2].shape[3]
-    spread_s, spread_v = spread[:, :, :cut], spread[:, :, cut:]
+    cut = 2 * count
+    spread_s, spread_v = spread[:, :, :, :cut], spread[:, :, :, cut:]
     spread_w = swap(spread_v, "c")
-
-    first = [v.reshape(4, 4, 2, -1, 2 * owned) for v in first]
-    first = sum_x(jnp.concatenate(first, axis=3))
-    late = [against(got[0], 0, 0, 8, mark(first), mark(spread_w))]
-    got.append(swap(hold(spread_s, mark(first)), "yl"))
-    late.append(against(got[1], 3, 0, 1, late[0]))
-    last = project_pieces(got[2], spread_v, spread_w).reshape(1, -1, 2 * owned)
-    late = [jnp.swapaxes(v, 0, 1).reshape(4, -1, 2 * owned) for v in late]
-    late = share_z(jnp.concatenate([first.reshape(4, -1, 2 * owned), *late], axis=1))
-    late = late[0] + late[1] + late[2] + hold(late[3], last)
-    cut = 4 * (count + RAW)
+    spread_s = [spread_s[:, y].reshape(-1, count, sites) for y in range(2)]
+
+    first = sum_x(jnp.concatenate(first))
+    got_a = swap(hold(jnp.concatenate([spread_s[0], lines]), mark(first)), "yl")
+    late = against(got, 0)
+    got_b = swap(hold(spread_s[1], mark(late)), "yl")
+    last = [project_pieces(got_a, spread_v, spread_w, 0)]
+    last.append(project_pieces(got_b, spread_v, spread_w, 1, last[0]))
+    late = jnp.swapaxes(late, 0, 1).reshape(4, -1, 2 * owned)
+    late = share_z(jnp.concatenate([first.reshape(4, -1, 2 * owned), late], axis=1))
+    late = late[0] + late[1] + late[2] + hold(late[3], last[0])
+    cut = 4 * count
     first = late[:cut].reshape(2, -1, 2 * owned)
-    late = late[cut:].reshape(7, -1, 2 * owned)
-    late = sum_x(jnp.concatenate([late, last]).reshape(4, 2, -1, 2 * owned))
+    late = late[cut:].reshape(6, -1, 2 * owned)
+    late = jnp.concatenate([late, *(v.reshape(1, -1, 2 * owned) for v in last)])
+    late = sum_x(late.reshape(4, 2, -1, 2 * owned))
 
     here = sum_yh(jnp.concatenate([first, late], axis=1))
     there = swap(here, "c")
 
+    lines = lines[0] + got_a[-1]
+    lines = lines + swap(lines, "c")
+
     def assemble(sums, half):
-        sums = sums[:, half * owned : (half + 1) * owned]
-        view = lambda v: v.reshape(2, -1, owned)
-        cut = [2 * count, 2 * (count + RAW)]
-        away = [view(sums[cut[0] : cut[1]]), view(sums[cut[1] :])]
-        return view(sums[: cut[0]]), jnp.concatenate(away, axis=1)
+        sums = sums[:, half * owned : (half + 1) * owned].reshape(2, 2, count, owned)
+        return sums[0], sums[1]
 
     h0, y0 = assemble(here, 0)
     h1, y1 = assemble(there, 1)

time: 177 us -> 185 us (1.045)
  waiting for transfers between devices: 40.9 us -> 49.7 us
  starting transfers between devices: 32.8 us -> 25.6 us
  other arithmetic: 14.6 us -> 18.4 us
    ppermute x6, waiting for transfers between devices: 7.91 us -> 33.9 us  [share_z(): lax.ppermute(pick(slabs, (me + k) % 4), 'z', [(i, (i + k) % 4) for i in r...]
    ppermute x9 -> x8, waiting for transfers between devices: 19.4 us -> 4.16 us  [swap(): return lax.ppermute(value, axis, SWAP)]
    slice x2 -> x5, local copies, waits for them, and re-layouts: 1.89 us -> 6.01 us  [mark(): value = value[0]]
    pallas_call x2 -> x3, Pallas kernels: 6.28 us -> 9.9 us  [the longest x2 7.49 us: project_pieces(): pl.pallas_call(pieces_kernel, grid=(count,), in_specs=[pl.BlockSpec((2 *...]
    squeeze x5 -> x2, local copies, waits for them, and re-layouts: 4.65 us -> 1.26 us  [mark(): value = value[0]]
    ppermute x6, starting transfers between devices: 13.2 us -> 9.95 us  [share_z(): lax.ppermute(pick(slabs, (me + k) % 4), 'z', [(i, (i + k) % 4) for i in r...]
    ppermute x6, starting transfers between devices: 10.8 us -> 8.7 us  [sum_x(): total = total + lax.ppermute(pick(slabs, (me + k) % 4), 'x', pairs)]
    ppermute x6, waiting for transfers between devices: 13.6 us -> 11.6 us  [sum_x(): total = total + lax.ppermute(pick(slabs, (me + k) % 4), 'x', pairs)]
  transfers between devices with their start and end apart: 21 -> 20, of which waited for: 11 -> 13; matrix products, arithmetic and copies ran while one was open for 14% -> 17% of each run, Pallas kernels for 38% -> 37%
where the time goes in v11:
time: 185 us; the launch traced here: 183 us
  Pallas kernels  67.7 us (37%)
  waiting for transfers between devices  49.7 us (27%)
  starting transfers between devices  25.6 us (14%)
  local copies, waits for them, and re-layouts  19.6 us (11%)
  other arithmetic  18.4 us (10%)
    ppermute x6, waiting for transfers between devices, share_z(): lax.ppermute(pick(slabs, (me + k) % 4), 'z', [(i, (i + k) % 4) for i in r...  33.9 us
    pallas_call x3, Pallas kernels, project(): pl.pallas_call(functools.partial(dot_kernel, len(cols)), grid=(size, inne...  29.8 us
    pallas_call x3, Pallas kernels, by_time(): pl.pallas_call(functools.partial(by_time_kernel, cuts), grid=(4,), in_spe...  28 us
    ppermute x6, waiting for transfers between devices, sum_x(): total = total + lax.ppermute(pick(slabs, (me + k) % 4), 'x', pairs)  11.6 us
    ppermute x6, starting transfers between devices, share_z(): lax.ppermute(pick(slabs, (me + k) % 4), 'z', [(i, (i + k) % 4) for i in r...  9.95 us
    ppermute x6, starting transfers between devices, sum_x(): total = total + lax.ppermute(pick(slabs, (me + k) % 4), 'x', pairs)  8.7 us
    pallas_call x2, Pallas kernels, project_pieces(): pl.pallas_call(pieces_kernel, grid=(count,), in_specs=[pl.BlockSpec((2 *...  7.49 us
    ppermute x8, starting transfers between devices, swap(): return lax.ppermute(value, axis, SWAP)  7 us
  transfers between devices with their start and end apart: 20, of which 13 were waited for; matrix products, arithmetic and copies ran while one was open for 17% of the time, Pallas kernels for 37%

profile of v11, /device:TPU:0, one launch (start us, length us, event | category | flops | bytes accessed | tf_op | source)
XLA Modules:
  0.0 182.7 jit_solution(4159889684148589998)
XLA Ops:
  0.7 6.4 %by_time.3 = (bf16[3,4,2,6,32,512]{5,4,3,2,1,0:T(8,128)(2,1)}, bf16[1,4,2,6,32,512]{5,4,3,2,1,0:T(8,128)(2,1)}) custom-call(bf16[32,6,32,512]{3,2,1,0:T(8,128)(2,1)} %bitcast.141), custom_call_target="tpu_custom_call" | custom-call | flops 1000 | bytes 1000 | tf_op jit(solution)/shard_map/by_time/pallas_call | solution.py:37
  7.2 1.7 collective-permute-start.4
  8.8 11.1 %by_time.4 = (bf16[4,4,2,6,64,512]{5,4,3,2,1,0:T(8,128)(2,1)}, bf16[1,4,2,6,64,512]{5,4,3,2,1,0:T(8,128)(2,1)}) custom-call(bf16[64,6,32,512]{3,2,1,0:T(8,128)(2,1)} %bitcast.128, bf16[3,8,3,64,512]{4,3,2,1,0:T(8,128)(2,1)} %bitcast.131), custom_call_target="tpu_custom_call" | custom-call | flops 1000 | bytes 1000 | tf_op jit(solution)/shard_map/by_time/pallas_call | solution.py:37
  20.0 4.4 %pad_maximum_fusion.refs_0_ = bf16[4,2,3,192,512]{4,3,2,1,0:T(8,128)(2,1)} fusion(bf16[4,2,3,128,512]{4,3,2,1,0:T(8,128)(2,1)} %bitcast.147, bf16[4,2,3,64,512]{4,3,2,1,0:T(8,128)(2,1)S(1)} %bitcast.140), kind=kLoop, calls=%fused_computation.1 | loop fusion | flops 9437184 | bytes 9437184 | tf_op jit(solution)/shard_map/concatenate | solution.py:270
  24.4 10.5 %by_time.5 = bf16[4,4,2,6,64,512]{5,4,3,2,1,0:T(8,128)(2,1)} custom-call(bf16[64,6,32,512]{3,2,1,0:T(8,128)(2,1)} %collective-permute-done.block), custom_call_target="tpu_custom_call" | custom-call | flops 1000 | bytes 1000 | tf_op jit(solution)/shard_map/by_time/pallas_call | solution.py:37
  34.9 1.9 %slice-done = bf16[1,4,2,6,64,512]{5,4,3,2,1,0:T(8,128)(2,1)S(1)} async-done(((bf16[4,4,2,6,64,512]{5,4,3,2,1,0:T(8,128)(2,1)}), bf16[1,4,2,6,64,512]{5,4,3,2,1,0:T(8,128)(2,1)S(1)}, s32[]{:S(2)}) %slice-start) | async-done | bytes 3145752 | tf_op jit(solution)/shard_map/slice | solution.py:62
  36.8 0.6 slice_bitcast_fusion.refs_1_.after
  37.4 4.2 %constant_dynamic-slice_fusion.1 = (bf16[1,2,3,192,512]{4,3,2,1,0:T(8,128)(2,1)S(1)}, bf16[2,3,192,512]{3,2,1,0:T(8,128)(2,1)}, bf16[2,3,192,512]{3,2,1,0:T(8,128)(2,1)}, bf16[2,3,192,512]{3,2,1,0:T(8,128)(2,1)}) fusion(bf16[4,2,3,192,512]{4,3,2,1,0:T(8,128)(2,1)} %hold.5, s32[]{:T(128)S(6)} %select_n.135, s32[]{:T(128)S(6)} %select_n.141, ...), kind=kLoop, calls=%fused_computation.74 | loop fusion | bytes 9437200 | tf_op jit(solution)/shard_map/jit(dynamic_index_in_dim)/dynamic_slice | solution.py:213
  41.6 1.9 %collective-permute-start.8 = (bf16[2,3,192,512]{3,2,1,0:T(8,128)(2,1)}, bf16[2,3,192,512]{3,2,1,0:T(8,128)(2,1)S(1)}, u32[]{:S(2)}, u32[]{:S(2)}) collective-permute-start(bf16[2,3,192,512]{3,2,1,0:T(8,128)(2,1)} %get-tuple-element.19), channel_id=1, source_target_pairs={{0,8},{8,16},{16,24},{24,0},{1,9},{9,17},{17,25},{25,1},{2,10},{10... | collective-permute-start | bytes 3538952 | tf_op jit(solution)/shard_map/ppermute | solution.py:219
  43.5 3.6 %collective-permute-start.10 = (bf16[2,3,192,512]{3,2,1,0:T(8,128)(2,1)}, bf16[2,3,192,512]{3,2,1,0:T(8,128)(2,1)S(1)}, u32[]{:S(2)}, u32[]{:S(2)}) collective-permute-start(bf16[2,3,192,512]{3,2,1,0:T(8,128)(2,1)} %get-tuple-element.17), channel_id=1, source_target_pairs={{0,16},{8,24},{16,0},{24,8},{1,17},{9,25},{17,1},{25,9},{2,18},{10... | collective-permute-start | bytes 3538952 | tf_op jit(solution)/shard_map/ppermute | solution.py:219
  47.1 1.0 collective-permute-start.9
  48.1 11.8 %project.3 = f32[3,8,2,32,128]{4,3,2,1,0:T(8,128)} custom-call(bf16[3,8,3,64,512]{4,3,2,1,0:T(8,128)(2,1)} %bitcast.132, bf16[4,8,3,128,512]{4,3,2,1,0:T(8,128)(2,1)} %bitcast.124, bf16[4,8,3,128,512]{4,3,2,1,0:T(8,128)(2,1)} %bitcast.120), custom_call_target="tpu_custom_call" | custom-call | flops 1000 | bytes 1000 | tf_op jit(solution)/shard_map/project/pallas_call | solution.py:200
  59.9 6.2 %project.4 = f32[1,8,2,32,128]{4,3,2,1,0:T(8,128)} custom-call(bf16[1,8,3,64,512]{4,3,2,1,0:T(8,128)(2,1)} %bitcast.139, bf16[4,8,3,128,512]{4,3,2,1,0:T(8,128)(2,1)} %bitcast.125, bf16[4,8,3,128,512]{4,3,2,1,0:T(8,128)(2,1)} %bitcast.121), custom_call_target="tpu_custom_call" | custom-call | flops 1000 | bytes 1000 | tf_op jit(solution)/shard_map/project/pallas_call | solution.py:200
  66.1 1.4 slice.114
  67.5 1.4 slice.113
  68.8 3.4 %collective-permute-done.8.refs_0_ = bf16[2,3,192,512]{3,2,1,0:T(8,128)(2,1)S(1)} collective-permute-done((bf16[2,3,192,512]{3,2,1,0:T(8,128)(2,1)}, bf16[2,3,192,512]{3,2,1,0:T(8,128)(2,1)S(1)}, u32[]{:S(2)}, u32[]{:S(2)}) %collective-permute-start.8) | collective-permute-done | bytes 1179680 | tf_op jit(solution)/shard_map/ppermute | solution.py:219
  72.2 1.0 copy-done.4
  73.2 25.4 %collective-permute-done.10 = bf16[2,3,192,512]{3,2,1,0:T(8,128)(2,1)S(1)} collective-permute-done((bf16[2,3,192,512]{3,2,1,0:T(8,128)(2,1)}, bf16[2,3,192,512]{3,2,1,0:T(8,128)(2,1)S(1)}, u32[]{:S(2)}, u32[]{:S(2)}) %collective-permute-start.10) | collective-permute-done | bytes 1179680 | tf_op jit(solution)/shard_map/ppermute | solution.py:219
  98.7 1.1 copy-done.6
  99.7 1.9 %pad_maximum_fusion.1 = bf16[4,2,3,192,512]{4,3,2,1,0:T(8,128)(2,1)S(1)} fusion(bf16[1,2,3,192,512]{4,3,2,1,0:T(8,128)(2,1)S(1)} %bitcast.142, bf16[1,2,3,192,512]{4,3,2,1,0:T(8,128)(2,1)} %bitcast.40, bf16[1,2,3,192,512]{4,3,2,1,0:T(8,128)(2,1)} %bitcast.133, bf16[1,2,3,192,512]{4,3,2,1,0:T(8,128)(2,1)S(1)} %get-tuple-element.16), kind=kLoop, calls=%fused_computation.2 | loop fusion | flops 7077888 | bytes 9437184 | tf_op jit(solution)/shard_map/stack | solution.py:273
  101.7 0.3 slice.116.own
  102.1 0.5 copy-done.7
  102.6 2.0 %fusion.19 = (f32[4,2,64,128]{3,2,1,0:T(8,128)}, f32[4,2,64,128]{3,2,1,0:T(8,128)}, f32[4,2,64,128]{3,2,1,0:T(8,128)}) fusion(s32[]{:T(128)S(6)} %select_n.130, f32[3,4,2,64,128]{4,3,2,1,0:T(8,128)} %bitcast.135, f32[1,4,2,64,128]{4,3,2,1,0:T(8,128)S(1)} %bitcast.148, s32[]{:T(128)S(6)} %select_n.132, s32[]{:T(128)S(6)} %select_n.134), kind=kLoop, calls=%fused_computation.45 | loop fusion | flops 196608 | bytes 1835020 | tf_op jit(solution)/shard_map/jit(dynamic_index_in_dim)/squeeze | solution.py:213
  104.6 1.5 collective-permute-start.1
  106.1 1.7 collective-permute-start.2
  107.8 1.8 collective-permute-start.3
  110.3 2.4 %choose.1 = bf16[4,8,512]{2,1,0:T(8,128)(2,1)} custom-call(s32[4]{0:T(128)} %index.1, s32[1]{0:T(128)S(6)} %copy.26.when, bf16[64,6,32,512]{3,2,1,0:T(8,128)(2,1)} %bitcast.129, bf16[128,512]{1,0:T(8,128)(2,1)} %slice_bitcast_fusion.refs_1_.after), custom_call_target="tpu_custom_call" | custom-call | flops 1000 | bytes 1000 | tf_op jit(solution)/shard_map/choose/pallas_call | solution.py:106
  112.7 1.5 collective-permute-done.1
  114.2 4.9 %collective-permute-done.2 = f32[4,2,64,128]{3,2,1,0:T(8,128)} collective-permute-done((f32[4,2,64,128]{3,2,1,0:T(8,128)}, f32[4,2,64,128]{3,2,1,0:T(8,128)}, u32[]{:S(2)}, u32[]{:S(2)}) %collective-permute-start.2) | collective-permute-done | bytes 262176 | tf_op jit(solution)/shard_map/ppermute | solution.py:235
  119.1 1.8 collective-permute-done.3
  120.9 1.3 fusion.17
  122.2 0.7 copy-done.8
  122.9 0.6 slice_bitcast_fusion.2.refs_1_
  123.5 2.4 %pad_maximum_fusion.3 = (bf16[4,1,3,64,512]{4,3,2,1,0:T(8,128)(2,1)}, bf16[4,1,3,64,512]{4,3,2,1,0:T(8,128)(2,1)S(1)}) fusion(bf16[1,2,3,192,512]{4,3,2,1,0:T(8,128)(2,1)} %bitcast.143, bf16[1,2,3,192,512]{4,3,2,1,0:T(8,128)(2,1)} %bitcast.40, bf16[1,2,3,192,512]{4,3,2,1,0:T(8,128)(2,1)} %bitcast.134, bf16[1,2,3,192,512]{4,3,2,1,0:T(8,128)(2,1)S(1)} %copy-done.3), kind=kLoop, calls=%fused_computation.23 | loop fusion | flops 6291456 | bytes 6291456 | tf_op jit(solution)/shard_map/slice | solution.py:277
  125.9 1.0 pad_maximum_fusion.2.refs_0_
  126.9 0.5 collective-permute-start.11
  127.8 0.6 gather_fusion
  128.5 11.8 %project.5 = f32[3,8,2,32,128]{4,3,2,1,0:T(8,128)} custom-call(bf16[3,8,3,64,512]{4,3,2,1,0:T(8,128)(2,1)} %collective-permute-done.4.refs_0_, bf16[4,8,3,128,512]{4,3,2,1,0:T(8,128)(2,1)} %bitcast.126, bf16[4,8,3,128,512]{4,3,2,1,0:T(8,128)(2,1)} %bitcast.122), custom_call_target="tpu_custom_call" | custom-call | flops 1000 | bytes 1000 | tf_op jit(solution)/shard_map/project/pallas_call | solution.py:200
  140.3 1.4 slice.119
  141.7 2.2 %copy.18 = f32[4,3,2,64,128]{4,3,2,1,0:T(8,128)} copy(f32[4,3,2,64,128]{4,3,2,0,1:T(8,128)} %bitcast.144) | data formatting | bytes 1572864 | tf_op jit(solution)/shard_map/transpose | solution.py:285
  143.9 1.5 collective-permute-start.13
  145.4 2.0 %fusion.8 = (f32[512,128]{1,0:T(8,128)}, f32[512,128]{1,0:T(8,128)}, f32[512,128]{1,0:T(8,128)}) fusion(s32[]{:T(128)S(6)} %select_n.137, f32[4,384,128]{2,1,0:T(8,128)} %bitcast.137, f32[4,128,128]{2,1,0:T(8,128)S(1)} %bitcast.150, s32[]{:T(128)S(6)} %select_n.139, s32[]{:T(128)S(6)} %select_n.141), kind=kLoop, calls=%fused_computation.34 | loop fusion | flops 196608 | bytes 1835020 | tf_op jit(solution)/shard_map/jit(dynamic_index_in_dim)/squeeze | solution.py:213
  147.6 3.0 %collective-permute-start.6 = (f32[512,128]{1,0:T(8,128)}, f32[512,128]{1,0:T(8,128)}, u32[]{:S(2)}, u32[]{:S(2)}) collective-permute-start(f32[512,128]{1,0:T(8,128)} %get-tuple-element.21), channel_id=1, source_target_pairs={{0,24},{8,0},{16,8},{24,16},{1,25},{9,1},{17,9},{25,17},{2,26},{10... | collective-permute-start | bytes 786440 | tf_op jit(solution)/shard_map/ppermute | solution.py:219
  150.6 0.2 collective-permute-start.7
  150.9 0.8 fusion.29
  151.8 3.8 %project_pieces.2.refs_1_.refs_0_ = f32[2,32,128]{2,1,0:T(8,128)S(1)} custom-call(bf16[25,32,512]{2,1,0:T(8,128)(2,1)} %collective-permute-done.11.col, bf16[4,2,3,128,512]{4,3,2,1,0:T(8,128)(2,1)S(1)} %slice.116.own, bf16[4,2,3,128,512]{4,3,2,1,0:T(8,128)(2,1)} %collective-permute-done.12.other), custom_call_target="tpu_custom_call" | custom-call | flops 1000 | bytes 1000 | tf_op jit(solution)/shard_map/project_pieces/pallas_call | solution.py:172
  155.5 0.6 copy-done
  156.1 4.8 %collective-permute-done.7.refs_0_ = f32[512,128]{1,0:T(8,128)} collective-permute-done((f32[512,128]{1,0:T(8,128)}, f32[512,128]{1,0:T(8,128)}, u32[]{:S(2)}, u32[]{:S(2)}) %collective-permute-start.7) | collective-permute-done | bytes 262176 | tf_op jit(solution)/shard_map/ppermute | solution.py:219
  160.9 0.3 collective-permute-done.5
  161.2 1.2 fusion.6
  162.5 0.8 collective-permute-done.13.col
  163.3 3.7 %project_pieces.3 = f32[2,32,128]{2,1,0:T(8,128)S(1)} custom-call(bf16[24,32,512]{2,1,0:T(8,128)(2,1)} %collective-permute-done.13.col, bf16[4,2,3,128,512]{4,3,2,1,0:T(8,128)(2,1)S(1)} %slice.116.own, bf16[4,2,3,128,512]{4,3,2,1,0:T(8,128)(2,1)} %collective-permute-done.12.other, f32[2,32,128]{2,1,0:T(8,128)S(1)} %copy-done.1), custom_call_target="tpu_custom_call" | custom-call | flops 1000 | bytes 1000 | tf_op jit(solution)/shard_map/project_pieces/pallas_call | solution.py:172
  167.1 0.9 collective-permute-start.14
  168.0 1.9 %collective-permute-start.16 = (f32[2,64,128]{2,1,0:T(8,128)S(1)}, f32[2,64,128]{2,1,0:T(8,128)S(1)}, u32[]{:S(2)}, u32[]{:S(2)}) collective-permute-start(f32[2,64,128]{2,1,0:T(8,128)S(1)} %get-tuple-element.27), channel_id=1, source_target_pairs={{0,4},{2,6},{4,0},{6,2},{1,5},{3,7},{5,1},{7,3},{8,12},{10,14},{12... | collective-permute-start | bytes 196616 | tf_op jit(solution)/shard_map/ppermute | solution.py:235
  169.9 0.9 collective-permute-start.15
  170.8 1.9 %collective-permute-done.14 = f32[2,64,128]{2,1,0:T(8,128)S(1)} collective-permute-done((f32[2,64,128]{2,1,0:T(8,128)S(1)}, f32[2,64,128]{2,1,0:T(8,128)S(1)}, u32[]{:S(2)}, u32[]{:S(2)}) %collective-permute-start.14) | collective-permute-done | bytes 65568 | tf_op jit(solution)/shard_map/ppermute | solution.py:235
  172.6 1.1 collective-permute-done.16
  173.7 0.4 collective-permute-done.15
  174.2 3.0 %collective-permute-start.17 = (f32[128,128]{1,0:T(8,128)S(1)}, f32[128,128]{1,0:T(8,128)S(1)}, u32[]{:S(2)}, u32[]{:S(2)}) collective-permute-start(f32[128,128]{1,0:T(8,128)S(1)} %fusion.23), channel_id=1, source_target_pairs={{0,1},{1,0},{2,3},{3,2},{4,5},{5,4},{6,7},{7,6},{8,9},{9,8},{10,11... | collective-permute-start | bytes 196616 | tf_op jit(solution)/shard_map/ppermute | solution.py:17
  177.2 0.7 broadcast_select_fusion
  177.9 2.1 %collective-permute-done.17 = f32[128,128]{1,0:T(8,128)S(1)} collective-permute-done((f32[128,128]{1,0:T(8,128)S(1)}, f32[128,128]{1,0:T(8,128)S(1)}, u32[]{:S(2)}, u32[]{:S(2)}) %collective-permute-start.17) | collective-permute-done | bytes 65568 | tf_op jit(solution)/shard_map/ppermute | solution.py:17
  180.2 1.2 collective-permute-done.18
  181.6 0.2 select_reduce_fusion
  181.9 0.7 copy.20
  (58 shorter events, 1.6 us)
Async XLA Ops:
  0.6 23.8 %collective-permute-start = (bf16[64,6,32,512]{3,2,1,0:T(8,128)(2,1)}, bf16[64,6,32,512]{3,2,1,0:T(8,128)(2,1)}, u32[]{:S(2)}, u32[]{:S(2)}) collective-permute-start(bf16[64,6,32,512]{3,2,1,0:T(8,128)(2,1)} %bitcast.127), channel_id=1, source_target_pairs={{0,32},{32,0},{1,33},{33,1},{2,34},{34,2},{3,35},{35,3},{4,36},{36... | collective-permute-start | bytes 37748744 | tf_op jit(solution)/shard_map/ppermute | solution.py:17
  7.2 12.8 %copy-start.5 = (bf16[1,4,2,6,32,512]{5,4,3,2,1,0:T(8,128)(2,1)S(1)}, bf16[1,4,2,6,32,512]{5,4,3,2,1,0:T(8,128)(2,1)}, u32[]{:S(2)}) copy-start(bf16[1,4,2,6,32,512]{5,4,3,2,1,0:T(8,128)(2,1)} %get-tuple-element.8) | copy-start | bytes 4718596
  7.2 121.4 %collective-permute-start.4 = (bf16[3,8,3,64,512]{4,3,2,1,0:T(8,128)(2,1)}, bf16[3,8,3,64,512]{4,3,2,1,0:T(8,128)(2,1)}, u32[]{:S(2)}, u32[]{:S(2)}) collective-permute-start(bf16[3,8,3,64,512]{4,3,2,1,0:T(8,128)(2,1)} %bitcast.130), channel_id=1, source_target_pairs={{0,64},{64,0},{1,65},{65,1},{2,66},{66,2},{3,67},{67,3},{4,68},{68... | collective-permute-start | bytes 14155784 | tf_op jit(solution)/shard_map/ppermute | solution.py:17
  34.9 1.9 %slice-start = ((bf16[4,4,2,6,64,512]{5,4,3,2,1,0:T(8,128)(2,1)}), bf16[1,4,2,6,64,512]{5,4,3,2,1,0:T(8,128)(2,1)S(1)}, s32[]{:S(2)}) async-start(bf16[4,4,2,6,64,512]{5,4,3,2,1,0:T(8,128)(2,1)} %by_time.5), calls=%async_computation | async-start | bytes 6291456 | tf_op jit(solution)/shard_map/slice | solution.py:62
  41.6 57.1 %copy-start.2 = (bf16[1,2,3,192,512]{4,3,2,1,0:T(8,128)(2,1)}, bf16[1,2,3,192,512]{4,3,2,1,0:T(8,128)(2,1)S(1)}, u32[]{:S(2)}) copy-start(bf16[1,2,3,192,512]{4,3,2,1,0:T(8,128)(2,1)S(1)} %get-tuple-element.16) | copy-start | bytes 3538948
  41.6 30.6 %collective-permute-start.8 = (bf16[2,3,192,512]{3,2,1,0:T(8,128)(2,1)}, bf16[2,3,192,512]{3,2,1,0:T(8,128)(2,1)S(1)}, u32[]{:S(2)}, u32[]{:S(2)}) collective-permute-start(bf16[2,3,192,512]{3,2,1,0:T(8,128)(2,1)} %get-tuple-element.19), channel_id=1, source_target_pairs={{0,8},{8,16},{16,24},{24,0},{1,9},{9,17},{17,25},{25,1},{2,10},{10... | collective-permute-start | bytes 3538952 | tf_op jit(solution)/shard_map/ppermute | solution.py:219
  43.5 55.1 %collective-permute-start.10 = (bf16[2,3,192,512]{3,2,1,0:T(8,128)(2,1)}, bf16[2,3,192,512]{3,2,1,0:T(8,128)(2,1)S(1)}, u32[]{:S(2)}, u32[]{:S(2)}) collective-permute-start(bf16[2,3,192,512]{3,2,1,0:T(8,128)(2,1)} %get-tuple-element.17), channel_id=1, source_target_pairs={{0,16},{8,24},{16,0},{24,8},{1,17},{9,25},{17,1},{25,9},{2,18},{10... | collective-permute-start | bytes 3538952 | tf_op jit(solution)/shard_map/ppermute | solution.py:219
  47.1 51.5 %collective-permute-start.9 = (bf16[2,3,192,512]{3,2,1,0:T(8,128)(2,1)}, bf16[2,3,192,512]{3,2,1,0:T(8,128)(2,1)}, u32[]{:S(2)}, u32[]{:S(2)}) collective-permute-start(bf16[2,3,192,512]{3,2,1,0:T(8,128)(2,1)} %get-tuple-element.18), channel_id=1, source_target_pairs={{0,24},{8,0},{16,8},{24,16},{1,25},{9,1},{17,9},{25,17},{2,26},{10... | collective-permute-start | bytes 3538952 | tf_op jit(solution)/shard_map/ppermute | solution.py:219
  72.2 1.0 copy-start.4
  98.7 1.1 copy-start.6
  101.6 1.0 copy-start.7
  101.9 49.7 %collective-permute-start.12 = (bf16[4,2,3,128,512]{4,3,2,1,0:T(8,128)(2,1)S(1)}, bf16[4,2,3,128,512]{4,3,2,1,0:T(8,128)(2,1)}, u32[]{:S(2)}, u32[]{:S(2)}) collective-permute-start(bf16[4,2,3,128,512]{4,3,2,1,0:T(8,128)(2,1)S(1)} %slice.116.own), channel_id=1, source_target_pairs={{0,32},{32,0},{1,33},{33,1},{2,34},{34,2},{3,35},{35,3},{4,36},{36... | collective-permute-start | bytes 9437192 | tf_op jit(solution)/shard_map/ppermute | solution.py:17
  104.6 9.7 %collective-permute-start.1 = (f32[4,2,64,128]{3,2,1,0:T(8,128)}, f32[4,2,64,128]{3,2,1,0:T(8,128)}, u32[]{:S(2)}, u32[]{:S(2)}) collective-permute-start(f32[4,2,64,128]{3,2,1,0:T(8,128)} %get-tuple-element.23), channel_id=1, source_target_pairs={{0,2},{2,4},{4,6},{6,0},{1,3},{3,5},{5,7},{7,1},{8,10},{10,12},{12... | collective-permute-start | bytes 786440 | tf_op jit(solution)/shard_map/ppermute | solution.py:235
  106.1 13.1 %collective-permute-start.2 = (f32[4,2,64,128]{3,2,1,0:T(8,128)}, f32[4,2,64,128]{3,2,1,0:T(8,128)}, u32[]{:S(2)}, u32[]{:S(2)}) collective-permute-start(f32[4,2,64,128]{3,2,1,0:T(8,128)} %get-tuple-element.24), channel_id=1, source_target_pairs={{0,6},{2,0},{4,2},{6,4},{1,7},{3,1},{5,3},{7,5},{8,14},{10,8},{12,... | collective-permute-start | bytes 786440 | tf_op jit(solution)/shard_map/ppermute | solution.py:235
  107.8 13.1 %collective-permute-start.3 = (f32[4,2,64,128]{3,2,1,0:T(8,128)}, f32[4,2,64,128]{3,2,1,0:T(8,128)}, u32[]{:S(2)}, u32[]{:S(2)}) collective-permute-start(f32[4,2,64,128]{3,2,1,0:T(8,128)} %get-tuple-element.25), channel_id=1, source_target_pairs={{0,4},{2,6},{4,0},{6,2},{1,5},{3,7},{5,1},{7,3},{8,12},{10,14},{12... | collective-permute-start | bytes 786440 | tf_op jit(solution)/shard_map/ppermute | solution.py:235
  112.7 10.8 %copy-start.3 = (bf16[1,2,3,192,512]{4,3,2,1,0:T(8,128)(2,1)S(1)}, bf16[1,2,3,192,512]{4,3,2,1,0:T(8,128)(2,1)}, u32[]{:S(2)}) copy-start(bf16[1,2,3,192,512]{4,3,2,1,0:T(8,128)(2,1)} %copy-done.2) | copy-start | bytes 3538948
  122.2 0.7 copy-start.8
  123.5 2.4 %copy-start.10 = (bf16[4,8,512]{2,1,0:T(8,128)(2,1)S(1)}, bf16[4,8,512]{2,1,0:T(8,128)(2,1)}, u32[]{:S(2)}) copy-start(bf16[4,8,512]{2,1,0:T(8,128)(2,1)} %choose.1) | copy-start | bytes 98308
  125.9 1.6 copy-start.11
  126.9 23.7 %collective-permute-start.11 = (bf16[25,32,512]{2,1,0:T(8,128)(2,1)}, bf16[25,32,512]{2,1,0:T(8,128)(2,1)}, u32[]{:S(2)}, u32[]{:S(2)}) collective-permute-start(bf16[25,32,512]{2,1,0:T(8,128)(2,1)} %hold.7), channel_id=1, source_target_pairs={{0,64},{64,0},{1,65},{65,1},{2,66},{66,2},{3,67},{67,3},{4,68},{68... | collective-permute-start | bytes 2457608 | tf_op jit(solution)/shard_map/ppermute | solution.py:17
  141.7 3.7 %copy-start.9 = (f32[4,2,64,128]{3,2,1,0:T(8,128)S(1)}, f32[4,2,64,128]{3,2,1,0:T(8,128)}, u32[]{:S(2)}) copy-start(f32[4,2,64,128]{3,2,1,0:T(8,128)} %copy-done.8) | copy-start | bytes 786436
  143.9 19.4 %collective-permute-start.13 = (bf16[24,32,512]{2,1,0:T(8,128)(2,1)}, bf16[24,32,512]{2,1,0:T(8,128)(2,1)}, u32[]{:S(2)}, u32[]{:S(2)}) collective-permute-start(bf16[24,32,512]{2,1,0:T(8,128)(2,1)} %hold.9), channel_id=1, source_target_pairs={{0,64},{64,0},{1,65},{65,1},{2,66},{66,2},{3,67},{67,3},{4,68},{68... | collective-permute-start | bytes 2359304 | tf_op jit(solution)/shard_map/ppermute | solution.py:17
  147.4 13.9 %collective-permute-start.5 = (f32[512,128]{1,0:T(8,128)}, f32[512,128]{1,0:T(8,128)}, u32[]{:S(2)}, u32[]{:S(2)}) collective-permute-start(f32[512,128]{1,0:T(8,128)} %get-tuple-element.20), channel_id=1, source_target_pairs={{0,8},{8,16},{16,24},{24,0},{1,9},{9,17},{17,25},{25,1},{2,10},{10... | collective-permute-start | bytes 786440 | tf_op jit(solution)/shard_map/ppermute | solution.py:219
  147.6 13.7 %collective-permute-start.6 = (f32[512,128]{1,0:T(8,128)}, f32[512,128]{1,0:T(8,128)}, u32[]{:S(2)}, u32[]{:S(2)}) collective-permute-start(f32[512,128]{1,0:T(8,128)} %get-tuple-element.21), channel_id=1, source_target_pairs={{0,24},{8,0},{16,8},{24,16},{1,25},{9,1},{17,9},{25,17},{2,26},{10... | collective-permute-start | bytes 786440 | tf_op jit(solution)/shard_map/ppermute | solution.py:219
  150.6 10.3 %collective-permute-start.7 = (f32[512,128]{1,0:T(8,128)}, f32[512,128]{1,0:T(8,128)}, u32[]{:S(2)}, u32[]{:S(2)}) collective-permute-start(f32[512,128]{1,0:T(8,128)} %get-tuple-element.22), channel_id=1, source_target_pairs={{0,16},{8,24},{16,0},{24,8},{1,17},{9,25},{17,1},{25,9},{2,18},{10... | collective-permute-start | bytes 786440 | tf_op jit(solution)/shard_map/ppermute | solution.py:219
  151.7 19.1 %collective-permute-start.19 = (bf16[32,512]{1,0:T(8,128)(2,1)S(1)}, bf16[32,512]{1,0:T(8,128)(2,1)S(1)}, u32[]{:S(2)}, u32[]{:S(2)}) collective-permute-start(bf16[32,512]{1,0:T(8,128)(2,1)S(1)} %fusion.29), channel_id=1, source_target_pairs={{0,32},{32,0},{1,33},{33,1},{2,34},{34,2},{3,35},{35,3},{4,36},{36... | collective-permute-start | bytes 98312 | tf_op jit(solution)/shard_map/ppermute | solution.py:17
  155.5 0.6 copy-start
  160.9 2.4 %copy-start.1 = (f32[2,32,128]{2,1,0:T(8,128)S(1)}, f32[2,32,128]{2,1,0:T(8,128)}, u32[]{:S(2)}) copy-start(f32[2,32,128]{2,1,0:T(8,128)} %copy-done) | copy-start | bytes 98308
  167.1 5.5 %collective-permute-start.14 = (f32[2,64,128]{2,1,0:T(8,128)S(1)}, f32[2,64,128]{2,1,0:T(8,128)S(1)}, u32[]{:S(2)}, u32[]{:S(2)}) collective-permute-start(f32[2,64,128]{2,1,0:T(8,128)S(1)} %get-tuple-element.26), channel_id=1, source_target_pairs={{0,2},{2,4},{4,6},{6,0},{1,3},{3,5},{5,7},{7,1},{8,10},{10,12},{12... | collective-permute-start | bytes 196616 | tf_op jit(solution)/shard_map/ppermute | solution.py:235
  168.0 5.8 %collective-permute-start.16 = (f32[2,64,128]{2,1,0:T(8,128)S(1)}, f32[2,64,128]{2,1,0:T(8,128)S(1)}, u32[]{:S(2)}, u32[]{:S(2)}) collective-permute-start(f32[2,64,128]{2,1,0:T(8,128)S(1)} %get-tuple-element.27), channel_id=1, source_target_pairs={{0,4},{2,6},{4,0},{6,2},{1,5},{3,7},{5,1},{7,3},{8,12},{10,14},{12... | collective-permute-start | bytes 196616 | tf_op jit(solution)/shard_map/ppermute | solution.py:235
  169.9 4.3 %collective-permute-start.15 = (f32[2,64,128]{2,1,0:T(8,128)S(1)}, f32[2,64,128]{2,1,0:T(8,128)S(1)}, u32[]{:S(2)}, u32[]{:S(2)}) collective-permute-start(f32[2,64,128]{2,1,0:T(8,128)S(1)} %get-tuple-element.28), channel_id=1, source_target_pairs={{0,6},{2,0},{4,2},{6,4},{1,7},{3,1},{5,3},{7,5},{8,14},{10,8},{12,... | collective-permute-start | bytes 196616 | tf_op jit(solution)/shard_map/ppermute | solution.py:235
  174.2 5.8 %collective-permute-start.17 = (f32[128,128]{1,0:T(8,128)S(1)}, f32[128,128]{1,0:T(8,128)S(1)}, u32[]{:S(2)}, u32[]{:S(2)}) collective-permute-start(f32[128,128]{1,0:T(8,128)S(1)} %fusion.23), channel_id=1, source_target_pairs={{0,1},{1,0},{2,3},{3,2},{4,5},{5,4},{6,7},{7,6},{8,9},{9,8},{10,11... | collective-permute-start | bytes 196616 | tf_op jit(solution)/shard_map/ppermute | solution.py:17
  180.1 1.3 collective-permute-start.18

commit v12 on v11

--- a/solution.py
+++ b/solution.py
@@ -267,7 +267,7 @@
         return out.reshape(out.shape[0], 4, 2, 2 * count, 2 * owned)
 
     slabs = [v.reshape(4, 2, comps // 2, -1, sites) for v in (mine[1], own_late)]
-    spread = share_z(hold(jnp.concatenate(slabs, axis=3), mark(other)))
+    spread = share_z(jnp.concatenate(slabs, axis=3))
     first = [against(mine[0], 0), against(mine[1], 3)]
     spread[1] = hold(spread[1], mark(first[0]), mark(first[1]))
     spread = jnp.stack(spread)

time: 185 us -> 170 us (0.919)
  waiting for transfers between devices: 49.7 us -> 39.9 us
  local copies, waits for them, and re-layouts: 19.6 us -> 13.4 us
  starting transfers between devices: 25.6 us -> 29.8 us
  other arithmetic: 18.4 us -> 15.4 us
    ppermute x6, waiting for transfers between devices: 33.9 us -> 24.4 us  [share_z(): lax.ppermute(pick(slabs, (me + k) % 4), 'z', [(i, (i + k) % 4) for i in r...]
    dynamic_slice x1 -> x0, local copies, waits for them, and re-layouts: 4.22 us -> none  [pick(): return lax.dynamic_index_in_dim(value, index, 0, keepdims=False)]
    ppermute x6, waiting for transfers between devices: 11.6 us -> 7.95 us  [sum_x(): total = total + lax.ppermute(pick(slabs, (me + k) % 4), 'x', pairs)]
    ppermute x8, waiting for transfers between devices: 4.16 us -> 7.49 us  [swap(): return lax.ppermute(value, axis, SWAP)]
    squeeze x3, other arithmetic: 4.01 us -> 1.9 us  [pick(): return lax.dynamic_index_in_dim(value, index, 0, keepdims=False)]
    ppermute x6, starting transfers between devices: 8.7 us -> 10.8 us  [sum_x(): total = total + lax.ppermute(pick(slabs, (me + k) % 4), 'x', pairs)]
    ppermute x6, starting transfers between devices: 9.95 us -> 11.8 us  [share_z(): lax.ppermute(pick(slabs, (me + k) % 4), 'z', [(i, (i + k) % 4) for i in r...]
    unnamed x26 -> x28, local copies, waits for them, and re-layouts: 4.71 us -> 3.16 us
  transfers between devices with their start and end apart: 20 -> 20, of which waited for: 13 -> 10; matrix products, arithmetic and copies ran while one was open for 17% -> 15% of each run, Pallas kernels for 37% -> 40%
where the time goes in v12:
time: 170 us; the launch traced here: 168 us
  Pallas kernels  67.7 us (40%)
  waiting for transfers between devices  39.9 us (23%)
  starting transfers between devices  29.8 us (18%)
  other arithmetic  15.4 us (9%)
  local copies, waits for them, and re-layouts  13.4 us (8%)
    pallas_call x3, Pallas kernels, project(): pl.pallas_call(functools.partial(dot_kernel, len(cols)), grid=(size, inne...  29.7 us
    pallas_call x3, Pallas kernels, by_time(): pl.pallas_call(functools.partial(by_time_kernel, cuts), grid=(4,), in_spe...  28.1 us
    ppermute x6, waiting for transfers between devices, share_z(): lax.ppermute(pick(slabs, (me + k) % 4), 'z', [(i, (i + k) % 4) for i in r...  24.4 us
    ppermute x6, starting transfers between devices, share_z(): lax.ppermute(pick(slabs, (me + k) % 4), 'z', [(i, (i + k) % 4) for i in r...  11.8 us
    ppermute x6, starting transfers between devices, sum_x(): total = total + lax.ppermute(pick(slabs, (me + k) % 4), 'x', pairs)  10.8 us
    ppermute x6, waiting for transfers between devices, sum_x(): total = total + lax.ppermute(pick(slabs, (me + k) % 4), 'x', pairs)  7.95 us
    pallas_call x2, Pallas kernels, project_pieces(): pl.pallas_call(pieces_kernel, grid=(count,), in_specs=[pl.BlockSpec((2 *...  7.49 us
    ppermute x8, waiting for transfers between devices, swap(): return lax.ppermute(value, axis, SWAP)  7.49 us
  transfers between devices with their start and end apart: 20, of which 10 were waited for; matrix products, arithmetic and copies ran while one was open for 15% of the time, Pallas kernels for 40%

profile of v12, /device:TPU:0, one launch (start us, length us, event | category | flops | bytes accessed | tf_op | source)
XLA Modules:
  0.0 167.9 jit_solution(3361073148326119816)
XLA Ops:
  0.6 0.1 collective-permute-start
  0.7 6.4 %by_time.3 = (bf16[3,4,2,6,32,512]{5,4,3,2,1,0:T(8,128)(2,1)}, bf16[1,4,2,6,32,512]{5,4,3,2,1,0:T(8,128)(2,1)}) custom-call(bf16[32,6,32,512]{3,2,1,0:T(8,128)(2,1)} %bitcast.140), custom_call_target="tpu_custom_call" | custom-call | flops 1000 | bytes 1000 | tf_op jit(solution)/shard_map/by_time/pallas_call | solution.py:37
  7.1 1.7 collective-permute-start.4
  8.8 11.1 %by_time.4 = (bf16[4,4,2,6,64,512]{5,4,3,2,1,0:T(8,128)(2,1)}, bf16[1,4,2,6,64,512]{5,4,3,2,1,0:T(8,128)(2,1)}) custom-call(bf16[64,6,32,512]{3,2,1,0:T(8,128)(2,1)} %bitcast.127, bf16[3,8,3,64,512]{4,3,2,1,0:T(8,128)(2,1)} %bitcast.130), custom_call_target="tpu_custom_call" | custom-call | flops 1000 | bytes 1000 | tf_op jit(solution)/shard_map/by_time/pallas_call | solution.py:37
  19.9 3.2 %fusion.2 = (bf16[1,2,3,192,512]{4,3,2,1,0:T(8,128)(2,1)S(1)}, bf16[2,3,192,512]{3,2,1,0:T(8,128)(2,1)}, bf16[2,3,192,512]{3,2,1,0:T(8,128)(2,1)}, bf16[2,3,192,512]{3,2,1,0:T(8,128)(2,1)}) fusion(s32[]{:T(128)S(6)} %select_n.135, bf16[4,2,3,128,512]{4,3,2,1,0:T(8,128)(2,1)} %bitcast.143, bf16[4,2,3,64,512]{4,3,2,1,0:T(8,128)(2,1)S(1)} %bitcast.139, ...), kind=kLoop, calls=%fused_computation.28 | loop fusion | flops 9437184 | bytes 9437200 | tf_op jit(solution)/shard_map/concatenate | solution.py:270
  23.1 1.9 %collective-permute-start.8 = (bf16[2,3,192,512]{3,2,1,0:T(8,128)(2,1)}, bf16[2,3,192,512]{3,2,1,0:T(8,128)(2,1)S(1)}, u32[]{:S(2)}, u32[]{:S(2)}) collective-permute-start(bf16[2,3,192,512]{3,2,1,0:T(8,128)(2,1)} %get-tuple-element.17), channel_id=1, source_target_pairs={{0,8},{8,16},{16,24},{24,0},{1,9},{9,17},{17,25},{25,1},{2,10},{10... | collective-permute-start | bytes 3538952 | tf_op jit(solution)/shard_map/ppermute | solution.py:219
  25.0 2.2 %collective-permute-start.9 = (bf16[2,3,192,512]{3,2,1,0:T(8,128)(2,1)}, bf16[2,3,192,512]{3,2,1,0:T(8,128)(2,1)}, u32[]{:S(2)}, u32[]{:S(2)}) collective-permute-start(bf16[2,3,192,512]{3,2,1,0:T(8,128)(2,1)} %get-tuple-element.18), channel_id=1, source_target_pairs={{0,24},{8,0},{16,8},{24,16},{1,25},{9,1},{17,9},{25,17},{2,26},{10... | collective-permute-start | bytes 3538952 | tf_op jit(solution)/shard_map/ppermute | solution.py:219
  27.2 1.8 %collective-permute-start.10 = (bf16[2,3,192,512]{3,2,1,0:T(8,128)(2,1)}, bf16[2,3,192,512]{3,2,1,0:T(8,128)(2,1)}, u32[]{:S(2)}, u32[]{:S(2)}) collective-permute-start(bf16[2,3,192,512]{3,2,1,0:T(8,128)(2,1)} %get-tuple-element.19), channel_id=1, source_target_pairs={{0,16},{8,24},{16,0},{24,8},{1,17},{9,25},{17,1},{25,9},{2,18},{10... | collective-permute-start | bytes 3538952 | tf_op jit(solution)/shard_map/ppermute | solution.py:219
  29.0 10.5 %by_time.5 = bf16[4,4,2,6,64,512]{5,4,3,2,1,0:T(8,128)(2,1)} custom-call(bf16[64,6,32,512]{3,2,1,0:T(8,128)(2,1)} %collective-permute-done.block), custom_call_target="tpu_custom_call" | custom-call | flops 1000 | bytes 1000 | tf_op jit(solution)/shard_map/by_time/pallas_call | solution.py:37
  39.5 11.8 %project.3 = f32[3,8,2,32,128]{4,3,2,1,0:T(8,128)} custom-call(bf16[3,8,3,64,512]{4,3,2,1,0:T(8,128)(2,1)} %bitcast.131, bf16[4,8,3,128,512]{4,3,2,1,0:T(8,128)(2,1)} %bitcast.123, bf16[4,8,3,128,512]{4,3,2,1,0:T(8,128)(2,1)} %bitcast.120), custom_call_target="tpu_custom_call" | custom-call | flops 1000 | bytes 1000 | tf_op jit(solution)/shard_map/project/pallas_call | solution.py:200
  51.3 6.2 %project.4 = f32[1,8,2,32,128]{4,3,2,1,0:T(8,128)} custom-call(bf16[1,8,3,64,512]{4,3,2,1,0:T(8,128)(2,1)} %bitcast.138, bf16[4,8,3,128,512]{4,3,2,1,0:T(8,128)(2,1)} %bitcast.124, bf16[4,8,3,128,512]{4,3,2,1,0:T(8,128)(2,1)} %bitcast.121), custom_call_target="tpu_custom_call" | custom-call | flops 1000 | bytes 1000 | tf_op jit(solution)/shard_map/project/pallas_call | solution.py:200
  57.5 1.4 slice.109
  58.9 1.4 slice.108
  60.2 1.0 copy-done.3
  61.2 17.2 %collective-permute-done.9 = bf16[2,3,192,512]{3,2,1,0:T(8,128)(2,1)} collective-permute-done((bf16[2,3,192,512]{3,2,1,0:T(8,128)(2,1)}, bf16[2,3,192,512]{3,2,1,0:T(8,128)(2,1)}, u32[]{:S(2)}, u32[]{:S(2)}) %collective-permute-start.9) | collective-permute-done | bytes 1179680 | tf_op jit(solution)/shard_map/ppermute | solution.py:219
  78.4 1.8 %collective-permute-done.10 = bf16[2,3,192,512]{3,2,1,0:T(8,128)(2,1)} collective-permute-done((bf16[2,3,192,512]{3,2,1,0:T(8,128)(2,1)}, bf16[2,3,192,512]{3,2,1,0:T(8,128)(2,1)}, u32[]{:S(2)}, u32[]{:S(2)}) %collective-permute-start.10) | collective-permute-done | bytes 1179680 | tf_op jit(solution)/shard_map/ppermute | solution.py:219
  80.2 2.3 %pad_maximum_fusion = bf16[4,2,3,192,512]{4,3,2,1,0:T(8,128)(2,1)S(1)} fusion(bf16[1,2,3,192,512]{4,3,2,1,0:T(8,128)(2,1)} %bitcast.40, bf16[1,2,3,192,512]{4,3,2,1,0:T(8,128)(2,1)} %bitcast.38, bf16[1,2,3,192,512]{4,3,2,1,0:T(8,128)(2,1)} %bitcast.132, bf16[1,2,3,192,512]{4,3,2,1,0:T(8,128)(2,1)S(1)} %get-tuple-element.16), kind=kLoop, calls=%fused_computation.9 | loop fusion | flops 7077888 | bytes 9437184 | tf_op jit(solution)/shard_map/stack | solution.py:273
  82.5 0.3 slice.113.own
  82.8 0.1 collective-permute-start.12
  83.6 2.3 %slice.110 = bf16[1,4,2,6,64,512]{5,4,3,2,1,0:T(8,128)(2,1)S(1)} slice(bf16[4,4,2,6,64,512]{5,4,3,2,1,0:T(8,128)(2,1)} %by_time.5), slice={[0:1], [0:4], [0:2], [0:6], [0:64], [0:512]} | slice | bytes 6291456 | tf_op jit(solution)/shard_map/slice | solution.py:62
  86.0 1.0 fusion.26
  87.0 1.5 collective-permute-start.1
  88.4 1.7 %collective-permute-start.2 = (f32[4,2,64,128]{3,2,1,0:T(8,128)}, f32[4,2,64,128]{3,2,1,0:T(8,128)}, u32[]{:S(2)}, u32[]{:S(2)}) collective-permute-start(f32[4,2,64,128]{3,2,1,0:T(8,128)} %get-tuple-element.24), channel_id=1, source_target_pairs={{0,6},{2,0},{4,2},{6,4},{1,7},{3,1},{5,3},{7,5},{8,14},{10,8},{12,... | collective-permute-start | bytes 786440 | tf_op jit(solution)/shard_map/ppermute | solution.py:235
  90.2 1.8 %collective-permute-start.3 = (f32[4,2,64,128]{3,2,1,0:T(8,128)}, f32[4,2,64,128]{3,2,1,0:T(8,128)}, u32[]{:S(2)}, u32[]{:S(2)}) collective-permute-start(f32[4,2,64,128]{3,2,1,0:T(8,128)} %get-tuple-element.25), channel_id=1, source_target_pairs={{0,4},{2,6},{4,0},{6,2},{1,5},{3,7},{5,1},{7,3},{8,12},{10,14},{12... | collective-permute-start | bytes 786440 | tf_op jit(solution)/shard_map/ppermute | solution.py:235
  92.0 0.7 slice_bitcast_fusion.after
  92.7 2.4 %choose.1 = bf16[4,8,512]{2,1,0:T(8,128)(2,1)} custom-call(s32[4]{0:T(128)} %index.1, s32[1]{0:T(128)S(6)} %copy.24.when, bf16[64,6,32,512]{3,2,1,0:T(8,128)(2,1)} %bitcast.128, bf16[128,512]{1,0:T(8,128)(2,1)} %slice_bitcast_fusion.after), custom_call_target="tpu_custom_call" | custom-call | flops 1000 | bytes 1000 | tf_op jit(solution)/shard_map/choose/pallas_call | solution.py:106
  95.1 2.5 %pad_maximum_fusion.2 = (bf16[4,1,3,64,512]{4,3,2,1,0:T(8,128)(2,1)}, bf16[4,1,3,64,512]{4,3,2,1,0:T(8,128)(2,1)S(1)}) fusion(bf16[1,2,3,192,512]{4,3,2,1,0:T(8,128)(2,1)} %bitcast.40, bf16[1,2,3,192,512]{4,3,2,1,0:T(8,128)(2,1)} %bitcast.38, bf16[1,2,3,192,512]{4,3,2,1,0:T(8,128)(2,1)} %bitcast.133, bf16[1,2,3,192,512]{4,3,2,1,0:T(8,128)(2,1)} %copy-done.2), kind=kLoop, calls=%fused_computation.34 | loop fusion | flops 6291456 | bytes 6291456 | tf_op jit(solution)/shard_map/slice | solution.py:277
  97.6 1.0 pad_maximum_fusion.1.refs_0_
  98.6 3.5 %collective-permute-done.2 = f32[4,2,64,128]{3,2,1,0:T(8,128)} collective-permute-done((f32[4,2,64,128]{3,2,1,0:T(8,128)}, f32[4,2,64,128]{3,2,1,0:T(8,128)}, u32[]{:S(2)}, u32[]{:S(2)}) %collective-permute-start.2) | collective-permute-done | bytes 262176 | tf_op jit(solution)/shard_map/ppermute | solution.py:235
  102.1 1.7 %collective-permute-done.3 = f32[4,2,64,128]{3,2,1,0:T(8,128)} collective-permute-done((f32[4,2,64,128]{3,2,1,0:T(8,128)}, f32[4,2,64,128]{3,2,1,0:T(8,128)}, u32[]{:S(2)}, u32[]{:S(2)}) %collective-permute-start.3) | collective-permute-done | bytes 262176 | tf_op jit(solution)/shard_map/ppermute | solution.py:235
  103.8 1.2 fusion.24
  105.0 0.7 copy-done.9
  105.7 0.6 slice_bitcast_fusion.2.refs_1_
  106.3 0.5 collective-permute-start.11
  106.9 0.1 copy.16
  107.0 0.2 fusion.37
  107.2 0.6 gather_fusion
  107.9 4.1 %collective-permute-done.4.refs_0_ = bf16[3,8,3,64,512]{4,3,2,1,0:T(8,128)(2,1)} collective-permute-done((bf16[3,8,3,64,512]{4,3,2,1,0:T(8,128)(2,1)}, bf16[3,8,3,64,512]{4,3,2,1,0:T(8,128)(2,1)}, u32[]{:S(2)}, u32[]{:S(2)}) %collective-permute-start.4) | collective-permute-done | bytes 4718624 | tf_op jit(solution)/shard_map/ppermute | solution.py:17
  112.0 11.8 %project.5 = f32[3,8,2,32,128]{4,3,2,1,0:T(8,128)} custom-call(bf16[3,8,3,64,512]{4,3,2,1,0:T(8,128)(2,1)} %collective-permute-done.4.refs_0_, bf16[4,8,3,128,512]{4,3,2,1,0:T(8,128)(2,1)} %bitcast.125, bf16[4,8,3,128,512]{4,3,2,1,0:T(8,128)(2,1)} %bitcast.122), custom_call_target="tpu_custom_call" | custom-call | flops 1000 | bytes 1000 | tf_op jit(solution)/shard_map/project/pallas_call | solution.py:200
  123.8 1.4 slice.116
  125.2 1.2 copy.17
  126.5 1.7 %collective-permute-start.13 = (bf16[24,32,512]{2,1,0:T(8,128)(2,1)}, bf16[24,32,512]{2,1,0:T(8,128)(2,1)}, u32[]{:S(2)}, u32[]{:S(2)}) collective-permute-start(bf16[24,32,512]{2,1,0:T(8,128)(2,1)} %hold.7), channel_id=1, source_target_pairs={{0,64},{64,0},{1,65},{65,1},{2,66},{66,2},{3,67},{67,3},{4,68},{68... | collective-permute-start | bytes 2359304 | tf_op jit(solution)/shard_map/ppermute | solution.py:17
  128.2 0.9 fusion.15
  129.1 1.9 %collective-permute-start.5 = (f32[512,128]{1,0:T(8,128)}, f32[512,128]{1,0:T(8,128)}, u32[]{:S(2)}, u32[]{:S(2)}) collective-permute-start(f32[512,128]{1,0:T(8,128)} %get-tuple-element.20), channel_id=1, source_target_pairs={{0,8},{8,16},{16,24},{24,0},{1,9},{9,17},{17,25},{25,1},{2,10},{10... | collective-permute-start | bytes 786440 | tf_op jit(solution)/shard_map/ppermute | solution.py:219
  131.0 2.1 %collective-permute-start.6 = (f32[512,128]{1,0:T(8,128)}, f32[512,128]{1,0:T(8,128)}, u32[]{:S(2)}, u32[]{:S(2)}) collective-permute-start(f32[512,128]{1,0:T(8,128)} %get-tuple-element.21), channel_id=1, source_target_pairs={{0,24},{8,0},{16,8},{24,16},{1,25},{9,1},{17,9},{25,17},{2,26},{10... | collective-permute-start | bytes 786440 | tf_op jit(solution)/shard_map/ppermute | solution.py:219
  133.2 1.9 %collective-permute-start.7 = (f32[512,128]{1,0:T(8,128)}, f32[512,128]{1,0:T(8,128)}, u32[]{:S(2)}, u32[]{:S(2)}) collective-permute-start(f32[512,128]{1,0:T(8,128)} %get-tuple-element.22), channel_id=1, source_target_pairs={{0,16},{8,24},{16,0},{24,8},{1,17},{9,25},{17,1},{25,9},{2,18},{10... | collective-permute-start | bytes 786440 | tf_op jit(solution)/shard_map/ppermute | solution.py:219
  135.1 0.8 fusion.36
  135.9 3.8 %project_pieces.2.refs_1_.refs_0_ = f32[2,32,128]{2,1,0:T(8,128)S(1)} custom-call(bf16[25,32,512]{2,1,0:T(8,128)(2,1)} %collective-permute-done.11.col, bf16[4,2,3,128,512]{4,3,2,1,0:T(8,128)(2,1)S(1)} %slice.113.own, bf16[4,2,3,128,512]{4,3,2,1,0:T(8,128)(2,1)} %collective-permute-done.12.other), custom_call_target="tpu_custom_call" | custom-call | flops 1000 | bytes 1000 | tf_op jit(solution)/shard_map/project_pieces/pallas_call | solution.py:172
  139.7 0.6 copy-done
  140.3 5.4 %collective-permute-done.7.refs_0_ = f32[512,128]{1,0:T(8,128)} collective-permute-done((f32[512,128]{1,0:T(8,128)}, f32[512,128]{1,0:T(8,128)}, u32[]{:S(2)}, u32[]{:S(2)}) %collective-permute-start.7) | collective-permute-done | bytes 262176 | tf_op jit(solution)/shard_map/ppermute | solution.py:219
  145.8 1.2 fusion.13
  147.0 3.7 %project_pieces.3 = f32[2,32,128]{2,1,0:T(8,128)S(1)} custom-call(bf16[24,32,512]{2,1,0:T(8,128)(2,1)} %collective-permute-done.13.col, bf16[4,2,3,128,512]{4,3,2,1,0:T(8,128)(2,1)S(1)} %slice.113.own, bf16[4,2,3,128,512]{4,3,2,1,0:T(8,128)(2,1)} %collective-permute-done.12.other, f32[2,32,128]{2,1,0:T(8,128)S(1)} %copy-done.1), custom_call_target="tpu_custom_call" | custom-call | flops 1000 | bytes 1000 | tf_op jit(solution)/shard_map/project_pieces/pallas_call | solution.py:172
  150.8 1.6 collective-permute-start.14
  152.4 2.7 %collective-permute-start.16 = (f32[2,64,128]{2,1,0:T(8,128)S(1)}, f32[2,64,128]{2,1,0:T(8,128)S(1)}, u32[]{:S(2)}, u32[]{:S(2)}) collective-permute-start(f32[2,64,128]{2,1,0:T(8,128)S(1)} %get-tuple-element.27), channel_id=1, source_target_pairs={{0,4},{2,6},{4,0},{6,2},{1,5},{3,7},{5,1},{7,3},{8,12},{10,14},{12... | collective-permute-start | bytes 196616 | tf_op jit(solution)/shard_map/ppermute | solution.py:235
  155.1 1.4 collective-permute-start.15
  156.6 1.6 collective-permute-done.16
  158.2 1.2 collective-permute-done.15
  159.4 3.0 %collective-permute-start.17 = (f32[128,128]{1,0:T(8,128)S(1)}, f32[128,128]{1,0:T(8,128)S(1)}, u32[]{:S(2)}, u32[]{:S(2)}) collective-permute-start(f32[128,128]{1,0:T(8,128)S(1)} %fusion.30), channel_id=1, source_target_pairs={{0,1},{1,0},{2,3},{3,2},{4,5},{5,4},{6,7},{7,6},{8,9},{9,8},{10,11... | collective-permute-start | bytes 196616 | tf_op jit(solution)/shard_map/ppermute | solution.py:17
  162.4 0.7 broadcast_select_fusion
  163.2 2.1 %collective-permute-done.17 = f32[128,128]{1,0:T(8,128)S(1)} collective-permute-done((f32[128,128]{1,0:T(8,128)S(1)}, f32[128,128]{1,0:T(8,128)S(1)}, u32[]{:S(2)}, u32[]{:S(2)}) %collective-permute-start.17) | collective-permute-done | bytes 65568 | tf_op jit(solution)/shard_map/ppermute | solution.py:17
  165.4 1.2 collective-permute-done.18
  166.8 0.2 select_reduce_fusion
  167.0 0.1 copy.18
  167.2 0.7 copy.19
  (57 shorter events, 0.8 us)
Async XLA Ops:
  0.6 28.4 %collective-permute-start = (bf16[64,6,32,512]{3,2,1,0:T(8,128)(2,1)}, bf16[64,6,32,512]{3,2,1,0:T(8,128)(2,1)}, u32[]{:S(2)}, u32[]{:S(2)}) collective-permute-start(bf16[64,6,32,512]{3,2,1,0:T(8,128)(2,1)} %bitcast.126), channel_id=1, source_target_pairs={{0,32},{32,0},{1,33},{33,1},{2,34},{34,2},{3,35},{35,3},{4,36},{36... | collective-permute-start | bytes 37748744 | tf_op jit(solution)/shard_map/ppermute | solution.py:17
  7.1 12.8 %copy-start.6 = (bf16[1,4,2,6,32,512]{5,4,3,2,1,0:T(8,128)(2,1)S(1)}, bf16[1,4,2,6,32,512]{5,4,3,2,1,0:T(8,128)(2,1)}, u32[]{:S(2)}) copy-start(bf16[1,4,2,6,32,512]{5,4,3,2,1,0:T(8,128)(2,1)} %get-tuple-element.8) | copy-start | bytes 4718596
  7.1 104.9 %collective-permute-start.4 = (bf16[3,8,3,64,512]{4,3,2,1,0:T(8,128)(2,1)}, bf16[3,8,3,64,512]{4,3,2,1,0:T(8,128)(2,1)}, u32[]{:S(2)}, u32[]{:S(2)}) collective-permute-start(bf16[3,8,3,64,512]{4,3,2,1,0:T(8,128)(2,1)} %bitcast.129), channel_id=1, source_target_pairs={{0,64},{64,0},{1,65},{65,1},{2,66},{66,2},{3,67},{67,3},{4,68},{68... | collective-permute-start | bytes 14155784 | tf_op jit(solution)/shard_map/ppermute | solution.py:17
  23.1 57.2 %copy-start.2 = (bf16[1,2,3,192,512]{4,3,2,1,0:T(8,128)(2,1)}, bf16[1,2,3,192,512]{4,3,2,1,0:T(8,128)(2,1)S(1)}, u32[]{:S(2)}) copy-start(bf16[1,2,3,192,512]{4,3,2,1,0:T(8,128)(2,1)S(1)} %get-tuple-element.16) | copy-start | bytes 3538948
  23.1 37.1 %collective-permute-start.8 = (bf16[2,3,192,512]{3,2,1,0:T(8,128)(2,1)}, bf16[2,3,192,512]{3,2,1,0:T(8,128)(2,1)S(1)}, u32[]{:S(2)}, u32[]{:S(2)}) collective-permute-start(bf16[2,3,192,512]{3,2,1,0:T(8,128)(2,1)} %get-tuple-element.17), channel_id=1, source_target_pairs={{0,8},{8,16},{16,24},{24,0},{1,9},{9,17},{17,25},{25,1},{2,10},{10... | collective-permute-start | bytes 3538952 | tf_op jit(solution)/shard_map/ppermute | solution.py:219
  25.0 53.4 %collective-permute-start.9 = (bf16[2,3,192,512]{3,2,1,0:T(8,128)(2,1)}, bf16[2,3,192,512]{3,2,1,0:T(8,128)(2,1)}, u32[]{:S(2)}, u32[]{:S(2)}) collective-permute-start(bf16[2,3,192,512]{3,2,1,0:T(8,128)(2,1)} %get-tuple-element.18), channel_id=1, source_target_pairs={{0,24},{8,0},{16,8},{24,16},{1,25},{9,1},{17,9},{25,17},{2,26},{10... | collective-permute-start | bytes 3538952 | tf_op jit(solution)/shard_map/ppermute | solution.py:219
  27.2 53.0 %collective-permute-start.10 = (bf16[2,3,192,512]{3,2,1,0:T(8,128)(2,1)}, bf16[2,3,192,512]{3,2,1,0:T(8,128)(2,1)}, u32[]{:S(2)}, u32[]{:S(2)}) collective-permute-start(bf16[2,3,192,512]{3,2,1,0:T(8,128)(2,1)} %get-tuple-element.19), channel_id=1, source_target_pairs={{0,16},{8,24},{16,0},{24,8},{1,17},{9,25},{17,1},{25,9},{2,18},{10... | collective-permute-start | bytes 3538952 | tf_op jit(solution)/shard_map/ppermute | solution.py:219
  60.2 1.0 copy-start.3
  82.8 53.0 %collective-permute-start.12 = (bf16[4,2,3,128,512]{4,3,2,1,0:T(8,128)(2,1)S(1)}, bf16[4,2,3,128,512]{4,3,2,1,0:T(8,128)(2,1)}, u32[]{:S(2)}, u32[]{:S(2)}) collective-permute-start(bf16[4,2,3,128,512]{4,3,2,1,0:T(8,128)(2,1)S(1)} %slice.113.own), channel_id=1, source_target_pairs={{0,32},{32,0},{1,33},{33,1},{2,34},{34,2},{3,35},{35,3},{4,36},{36... | collective-permute-start | bytes 9437192 | tf_op jit(solution)/shard_map/ppermute | solution.py:17
  83.6 2.3 %copy-start.4 = (f32[3,8,2,32,128]{4,3,2,1,0:T(8,128)S(1)}, f32[3,8,2,32,128]{4,3,2,1,0:T(8,128)}, u32[]{:S(2)}) copy-start(f32[3,8,2,32,128]{4,3,2,1,0:T(8,128)} %project.3) | copy-start | bytes 2359300
  83.6 2.3 %copy-start.7 = (f32[1,8,2,32,128]{4,3,2,1,0:T(8,128)S(1)}, f32[1,8,2,32,128]{4,3,2,1,0:T(8,128)}, u32[]{:S(2)}) copy-start(f32[1,8,2,32,128]{4,3,2,1,0:T(8,128)} %project.4) | copy-start | bytes 786436
  87.0 11.7 %collective-permute-start.1 = (f32[4,2,64,128]{3,2,1,0:T(8,128)}, f32[4,2,64,128]{3,2,1,0:T(8,128)}, u32[]{:S(2)}, u32[]{:S(2)}) collective-permute-start(f32[4,2,64,128]{3,2,1,0:T(8,128)} %get-tuple-element.23), channel_id=1, source_target_pairs={{0,2},{2,4},{4,6},{6,0},{1,3},{3,5},{5,7},{7,1},{8,10},{10,12},{12... | collective-permute-start | bytes 786440 | tf_op jit(solution)/shard_map/ppermute | solution.py:235
  88.4 13.6 %collective-permute-start.2 = (f32[4,2,64,128]{3,2,1,0:T(8,128)}, f32[4,2,64,128]{3,2,1,0:T(8,128)}, u32[]{:S(2)}, u32[]{:S(2)}) collective-permute-start(f32[4,2,64,128]{3,2,1,0:T(8,128)} %get-tuple-element.24), channel_id=1, source_target_pairs={{0,6},{2,0},{4,2},{6,4},{1,7},{3,1},{5,3},{7,5},{8,14},{10,8},{12,... | collective-permute-start | bytes 786440 | tf_op jit(solution)/shard_map/ppermute | solution.py:235
  90.2 13.6 %collective-permute-start.3 = (f32[4,2,64,128]{3,2,1,0:T(8,128)}, f32[4,2,64,128]{3,2,1,0:T(8,128)}, u32[]{:S(2)}, u32[]{:S(2)}) collective-permute-start(f32[4,2,64,128]{3,2,1,0:T(8,128)} %get-tuple-element.25), channel_id=1, source_target_pairs={{0,4},{2,6},{4,0},{6,2},{1,5},{3,7},{5,1},{7,3},{8,12},{10,14},{12... | collective-permute-start | bytes 786440 | tf_op jit(solution)/shard_map/ppermute | solution.py:235
  95.1 2.5 %copy-start.11 = (bf16[4,8,512]{2,1,0:T(8,128)(2,1)S(1)}, bf16[4,8,512]{2,1,0:T(8,128)(2,1)}, u32[]{:S(2)}) copy-start(bf16[4,8,512]{2,1,0:T(8,128)(2,1)} %choose.1) | copy-start | bytes 98308
  97.6 6.2 %copy-start.8 = (f32[1,8,2,32,128]{4,3,2,1,0:T(8,128)S(1)}, f32[1,8,2,32,128]{4,3,2,1,0:T(8,128)}, u32[]{:S(2)}) copy-start(f32[1,8,2,32,128]{4,3,2,1,0:T(8,128)} %project.4) | copy-start | bytes 786436
  98.6 8.3 %copy-start.12 = (s32[4,4]{1,0:T(4,128)S(1)}, s32[4,4]{1,0:T(4,128)}, u32[]{:S(2)}) copy-start(s32[4,4]{1,0:T(4,128)} %param.9) | copy-start | bytes 196
  104.9 0.7 copy-start.9
  106.3 26.9 %collective-permute-start.11 = (bf16[25,32,512]{2,1,0:T(8,128)(2,1)}, bf16[25,32,512]{2,1,0:T(8,128)(2,1)}, u32[]{:S(2)}, u32[]{:S(2)}) collective-permute-start(bf16[25,32,512]{2,1,0:T(8,128)(2,1)} %hold.5), channel_id=1, source_target_pairs={{0,64},{64,0},{1,65},{65,1},{2,66},{66,2},{3,67},{67,3},{4,68},{68... | collective-permute-start | bytes 2457608 | tf_op jit(solution)/shard_map/ppermute | solution.py:17
  125.2 3.0 %copy-start.10 = (f32[4,2,64,128]{3,2,1,0:T(8,128)S(1)}, f32[4,2,64,128]{3,2,1,0:T(8,128)}, u32[]{:S(2)}) copy-start(f32[4,2,64,128]{3,2,1,0:T(8,128)} %copy-done.9) | copy-start | bytes 786436
  126.4 1.8 %copy-start.5 = (f32[4,3,2,64,128]{4,3,2,1,0:T(8,128)}, f32[4,3,2,64,128]{4,3,2,1,0:T(8,128)S(1)}, u32[]{:S(2)}) copy-start(f32[4,3,2,64,128]{4,3,2,1,0:T(8,128)S(1)} %copy.17) | copy-start | bytes 2359300
  126.5 20.6 %collective-permute-start.13 = (bf16[24,32,512]{2,1,0:T(8,128)(2,1)}, bf16[24,32,512]{2,1,0:T(8,128)(2,1)}, u32[]{:S(2)}, u32[]{:S(2)}) collective-permute-start(bf16[24,32,512]{2,1,0:T(8,128)(2,1)} %hold.7), channel_id=1, source_target_pairs={{0,64},{64,0},{1,65},{65,1},{2,66},{66,2},{3,67},{67,3},{4,68},{68... | collective-permute-start | bytes 2359304 | tf_op jit(solution)/shard_map/ppermute | solution.py:17
  129.1 16.6 %collective-permute-start.5 = (f32[512,128]{1,0:T(8,128)}, f32[512,128]{1,0:T(8,128)}, u32[]{:S(2)}, u32[]{:S(2)}) collective-permute-start(f32[512,128]{1,0:T(8,128)} %get-tuple-element.20), channel_id=1, source_target_pairs={{0,8},{8,16},{16,24},{24,0},{1,9},{9,17},{17,25},{25,1},{2,10},{10... | collective-permute-start | bytes 786440 | tf_op jit(solution)/shard_map/ppermute | solution.py:219
  131.0 14.7 %collective-permute-start.6 = (f32[512,128]{1,0:T(8,128)}, f32[512,128]{1,0:T(8,128)}, u32[]{:S(2)}, u32[]{:S(2)}) collective-permute-start(f32[512,128]{1,0:T(8,128)} %get-tuple-element.21), channel_id=1, source_target_pairs={{0,24},{8,0},{16,8},{24,16},{1,25},{9,1},{17,9},{25,17},{2,26},{10... | collective-permute-start | bytes 786440 | tf_op jit(solution)/shard_map/ppermute | solution.py:219
  133.2 12.6 %collective-permute-start.7 = (f32[512,128]{1,0:T(8,128)}, f32[512,128]{1,0:T(8,128)}, u32[]{:S(2)}, u32[]{:S(2)}) collective-permute-start(f32[512,128]{1,0:T(8,128)} %get-tuple-element.22), channel_id=1, source_target_pairs={{0,16},{8,24},{16,0},{24,8},{1,17},{9,25},{17,1},{25,9},{2,18},{10... | collective-permute-start | bytes 786440 | tf_op jit(solution)/shard_map/ppermute | solution.py:219
  135.9 20.7 %collective-permute-start.19 = (bf16[32,512]{1,0:T(8,128)(2,1)S(1)}, bf16[32,512]{1,0:T(8,128)(2,1)S(1)}, u32[]{:S(2)}, u32[]{:S(2)}) collective-permute-start(bf16[32,512]{1,0:T(8,128)(2,1)S(1)} %fusion.36), channel_id=1, source_target_pairs={{0,32},{32,0},{1,33},{33,1},{2,34},{34,2},{3,35},{35,3},{4,36},{36... | collective-permute-start | bytes 98312 | tf_op jit(solution)/shard_map/ppermute | solution.py:17
  139.7 0.6 copy-start
  145.8 1.3 copy-start.1
  150.8 5.8 %collective-permute-start.14 = (f32[2,64,128]{2,1,0:T(8,128)S(1)}, f32[2,64,128]{2,1,0:T(8,128)S(1)}, u32[]{:S(2)}, u32[]{:S(2)}) collective-permute-start(f32[2,64,128]{2,1,0:T(8,128)S(1)} %get-tuple-element.26), channel_id=1, source_target_pairs={{0,2},{2,4},{4,6},{6,0},{1,3},{3,5},{5,7},{7,1},{8,10},{10,12},{12... | collective-permute-start | bytes 196616 | tf_op jit(solution)/shard_map/ppermute | solution.py:235
  152.4 5.8 %collective-permute-start.16 = (f32[2,64,128]{2,1,0:T(8,128)S(1)}, f32[2,64,128]{2,1,0:T(8,128)S(1)}, u32[]{:S(2)}, u32[]{:S(2)}) collective-permute-start(f32[2,64,128]{2,1,0:T(8,128)S(1)} %get-tuple-element.27), channel_id=1, source_target_pairs={{0,4},{2,6},{4,0},{6,2},{1,5},{3,7},{5,1},{7,3},{8,12},{10,14},{12... | collective-permute-start | bytes 196616 | tf_op jit(solution)/shard_map/ppermute | solution.py:235
  155.1 4.3 %collective-permute-start.15 = (f32[2,64,128]{2,1,0:T(8,128)S(1)}, f32[2,64,128]{2,1,0:T(8,128)S(1)}, u32[]{:S(2)}, u32[]{:S(2)}) collective-permute-start(f32[2,64,128]{2,1,0:T(8,128)S(1)} %get-tuple-element.28), channel_id=1, source_target_pairs={{0,6},{2,0},{4,2},{6,4},{1,7},{3,1},{5,3},{7,5},{8,14},{10,8},{12,... | collective-permute-start | bytes 196616 | tf_op jit(solution)/shard_map/ppermute | solution.py:235
  159.4 5.8 %collective-permute-start.17 = (f32[128,128]{1,0:T(8,128)S(1)}, f32[128,128]{1,0:T(8,128)S(1)}, u32[]{:S(2)}, u32[]{:S(2)}) collective-permute-start(f32[128,128]{1,0:T(8,128)S(1)} %fusion.30), channel_id=1, source_target_pairs={{0,1},{1,0},{2,3},{3,2},{4,5},{5,4},{6,7},{7,6},{8,9},{9,8},{10,11... | collective-permute-start | bytes 196616 | tf_op jit(solution)/shard_map/ppermute | solution.py:17
  165.3 1.3 collective-permute-start.18

commit v13 on v12

--- a/solution.py
+++ b/solution.py
@@ -22,29 +22,45 @@
 
 
 def by_time_kernel(cuts, block, *refs):
-    outs = refs[-len(cuts) :]
-    for k in range(block.shape[1]):
-        turned = jnp.swapaxes(block[:, k], 0, 1)
+    outs, (given, turned, sems) = refs[-len(cuts) - 3 : -3], refs[-3:]
+    pairs, comps = given.shape[0], given.shape[2]
+    copies = [
+        pltpu.make_async_copy(block.at[:, :, pl.ds(16 * i, 16)], given.at[i], sems.at[i])
+        for i in range(pairs)
+    ]
+    for copy in copies:
+        copy.start()
+    sent = []
+    for z in range(2 * pairs):
+        if z % 2 == 0:
+            copies[z // 2].wait()
+        for k in range(comps):
+            eight = pl.ds(8 * (z % 2), 8)
+            turned[z, :, k] = jnp.swapaxes(given[z // 2, :, k, eight], 0, 1)
         for (low, high, x, nx, y, ny), out in zip(cuts, outs):
             for i in range(nx):
-                for j in range(ny):
-                    out[i, 0, j, k] = turned[2 * (x + i) + y + j, low:high]
+                at = len(sent)
+                source = turned.at[z, pl.ds(2 * (x + i) + y, ny), :, pl.ds(low, high - low)]
+                sent.append(pltpu.make_async_copy(source, out.at[i, z], sems.at[pairs + at]))
+                sent[at].start()
+    for copy in sent:
+        copy.wait()
 
 
 def by_time(block, cuts, *after):
     n, comps, times, sites = block.shape
-    spec = pl.BlockSpec((n, comps, times // 4, sites), lambda z: (0, 0, z, 0))
     return pl.pallas_call(
         functools.partial(by_time_kernel, cuts),
-        grid=(4,),
-        in_specs=[spec] + [ANY] * len(after),
-        out_specs=[
-            pl.BlockSpec((nx, 1, ny, comps, high - low, sites), lambda z: (0, z, 0, 0, 0, 0))
-            for low, high, _, nx, _, ny in cuts
-        ],
+        in_specs=[ANY] * (1 + len(after)),
+        out_specs=[ANY] * len(cuts),
         out_shape=[
             jax.ShapeDtypeStruct((nx, 4, ny, comps, high - low, sites), block.dtype)
             for low, high, _, nx, _, ny in cuts
+        ],
+        scratch_shapes=[
+            pltpu.VMEM((times // 16, n, comps, 16, sites), block.dtype),
+            pltpu.VMEM((times // 8, 8, comps, n, sites), block.dtype),
+            pltpu.SemaphoreType.DMA((times // 16 + sum(4 * cut[3] for cut in cuts),)),
         ],
         compiler_params=pltpu.CompilerParams(vmem_limit_bytes=56 * 2**20),
         cost_estimate=HINT,
@@ -139,7 +155,7 @@
 
 
 def dot_kernel(count, *refs):
-    cols, (own, other), outs = refs[:count], refs[count : count + 2], refs[-count:]
+    cols, (own, other), out = refs[:count], refs[count : count + 2], refs[-1]
     for at in range(own.shape[1]):
         total = None
         for colour in range(own.shape[2]):
@@ -148,35 +164,31 @@
             )
             total = term if total is None else total + term
         row = 0
-        for col, out in zip(cols, outs):
+        for col in cols:
             n = col.shape[3] // 2
-            out[0, at, 0], out[0, at, 1] = real_imag(total, row, n)
-            row += 2 * n
-
-
-def pieces_kernel(col, own, other, *refs):
+            real, imag = real_imag(total, 2 * row, n)
+            out[0, at, 0, row : row + n], out[0, at, 1, row : row + n] = real, imag
+            row += n
+
+
+def pieces_kernel(y, col, own, other, *refs):
     total, out = None, refs[-1]
-    for colour in range(own.shape[2]):
-        pair = [col[2 * colour], col[2 * colour + 1]]
-        term = product(pair, own[0, 0, colour], other[0, 0, colour])
-        total = term if total is None else total + term
-    here = pl.program_id(0)
-    for part, value in enumerate(real_imag(total, 0, out.shape[1])):
-        out[part] = jnp.where(here == 0, value, out[part] + value)
+    for block in range(own.shape[0]):
+        for colour in range(own.shape[2]):
+            at = 2 * (block * own.shape[2] + colour)
+            term = product([col[at], col[at + 1]], own[block, y, colour], other[block, y, colour])
+            total = term if total is None else total + term
+    out[0], out[1] = real_imag(total, 0, out.shape[1])
 
 
 def project_pieces(cols, own, other, y, *after):
-    count, _, colours, rows, sites = own.shape
-    n = cols.shape[1]
-    vecs = pl.BlockSpec((1, 1, colours, rows, sites), lambda i: (i, y, 0, 0, 0))
-    return pl.pallas_call(
-        pieces_kernel,
-        grid=(count,),
-        in_specs=[pl.BlockSpec((2 * colours, n, sites), lambda i: (i, 0, 0)), vecs, vecs]
-        + [ANY] * len(after),
-        out_specs=pl.BlockSpec((2, n, rows), lambda i: (0, 0, 0)),
-        out_shape=jax.ShapeDtypeStruct((2, n, rows), jnp.float32),
-        compiler_params=pltpu.CompilerParams(vmem_limit_bytes=16 * 2**20),
+    whole = pl.BlockSpec(memory_space=pltpu.VMEM)
+    return pl.pallas_call(
+        functools.partial(pieces_kernel, y),
+        in_specs=[whole] * 3 + [ANY] * len(after),
+        out_specs=whole,
+        out_shape=jax.ShapeDtypeStruct((2, cols.shape[1], own.shape[3]), jnp.float32),
+        compiler_params=pltpu.CompilerParams(vmem_limit_bytes=24 * 2**20),
         cost_estimate=HINT,
         name="project_pieces",
     )(cols, own, other, *after)
@@ -190,13 +202,9 @@
     )
     in_specs = [spec(c.shape[3]) for c in cols] + [spec(rows, stride, x, y)] * 2
     in_specs += [ANY] * len(after)
-    out_specs = [
-        pl.BlockSpec((1, step, 2, c.shape[3] // 2, rows), lambda i, j: (i, j, 0, 0, 0))
-        for c in cols
-    ]
-    out_shape = [
-        jax.ShapeDtypeStruct((size, inner, 2, c.shape[3] // 2, rows), jnp.float32) for c in cols
-    ]
+    total = sum(c.shape[3] for c in cols) // 2
+    out_specs = pl.BlockSpec((1, step, 2, total, rows), lambda i, j: (i, j, 0, 0, 0))
+    out_shape = jax.ShapeDtypeStruct((size, inner, 2, total, rows), jnp.float32)
     return pl.pallas_call(
         functools.partial(dot_kernel, len(cols)),
         grid=(size, inner // step),
@@ -262,13 +270,13 @@
     own, other = rows_of(own), rows_of(other)
     lines = choose(vecs, source_index, source_time, mark(other)).reshape(1, -1, sites)
 
-    def against(part, x, *after):
-        out = project([part], own, other, x, 0, 8, *after)[0]
+    def against(parts, x, *after):
+        out = project(parts, own, other, x, 0, 8, *after)
         return out.reshape(out.shape[0], 4, 2, 2 * count, 2 * owned)
 
     slabs = [v.reshape(4, 2, comps // 2, -1, sites) for v in (mine[1], own_late)]
     spread = share_z(jnp.concatenate(slabs, axis=3))
-    first = [against(mine[0], 0), against(mine[1], 3)]
+    first = [against(mine[:1], 0), against(mine[1:], 3)]
     spread[1] = hold(spread[1], mark(first[0]), mark(first[1]))
     spread = jnp.stack(spread)
     cut = 2 * count
@@ -278,7 +286,7 @@
 
     first = sum_x(jnp.concatenate(first))
     got_a = swap(hold(jnp.concatenate([spread_s[0], lines]), mark(first)), "yl")
-    late = against(got, 0)
+    late = against([got], 0)
     got_b = swap(hold(spread_s[1], mark(late)), "yl")
     last = [project_pieces(got_a, spread_v, spread_w, 0)]
     last.append(project_pieces(got_b, spread_v, spread_w, 1, last[0]))

time: 170 us -> 168 us (0.988)
  Pallas kernels: 67.7 us -> 61.6 us
  waiting for transfers between devices: 39.9 us -> 43.9 us
    pallas_call x5, Pallas kernels: 35.6 us -> 29.4 us  [the longest x3 22.7 us: by_time(): pl.pallas_call(functools.partial(by_time_kernel, cuts), in_specs=[ANY] *...]
    ppermute x6, waiting for transfers between devices: 24.4 us -> 26.7 us  [share_z(): lax.ppermute(pick(slabs, (me + k) % 4), 'z', [(i, (i + k) % 4) for i in r...]
    ppermute x8, waiting for transfers between devices: 7.49 us -> 9.22 us  [swap(): return lax.ppermute(value, axis, SWAP)]
  transfers between devices with their start and end apart: 20 -> 20, of which waited for: 10 -> 10; matrix products, arithmetic and copies ran while one was open for 15% -> 15% of each run, Pallas kernels for 40% -> 37%
where the time goes in v13:
time: 168 us; the launch traced here: 166 us
  Pallas kernels  61.6 us (37%)
  waiting for transfers between devices  43.9 us (26%)
  starting transfers between devices  30.2 us (18%)
  other arithmetic  15.5 us (9%)
  local copies, waits for them, and re-layouts  13.4 us (8%)
  between operations  1.71 us (1%)
    pallas_call x3, Pallas kernels, project(): pl.pallas_call(functools.partial(dot_kernel, len(cols)), grid=(size, inne...  29.7 us
    ppermute x6, waiting for transfers between devices, share_z(): lax.ppermute(pick(slabs, (me + k) % 4), 'z', [(i, (i + k) % 4) for i in r...  26.7 us
    pallas_call x3, Pallas kernels, by_time(): pl.pallas_call(functools.partial(by_time_kernel, cuts), in_specs=[ANY] *...  22.7 us
    ppermute x6, starting transfers between devices, share_z(): lax.ppermute(pick(slabs, (me + k) % 4), 'z', [(i, (i + k) % 4) for i in r...  11.8 us
    ppermute x6, starting transfers between devices, sum_x(): total = total + lax.ppermute(pick(slabs, (me + k) % 4), 'x', pairs)  10.8 us
    ppermute x8, waiting for transfers between devices, swap(): return lax.ppermute(value, axis, SWAP)  9.22 us
    ppermute x6, waiting for transfers between devices, sum_x(): total = total + lax.ppermute(pick(slabs, (me + k) % 4), 'x', pairs)  7.95 us
    ppermute x8, starting transfers between devices, swap(): return lax.ppermute(value, axis, SWAP)  7.59 us
  transfers between devices with their start and end apart: 20, of which 10 were waited for; matrix products, arithmetic and copies ran while one was open for 15% of the time, Pallas kernels for 37%

profile of v13, /device:TPU:0, one launch (start us, length us, event | category | flops | bytes accessed | tf_op | source)
XLA Modules:
  0.0 166.2 jit_solution(14247346649266391001)
XLA Ops:
  0.6 0.1 collective-permute-start
  0.7 5.1 %by_time.3 = (bf16[3,4,2,6,32,512]{5,4,3,2,1,0:T(8,128)(2,1)}, bf16[1,4,2,6,32,512]{5,4,3,2,1,0:T(8,128)(2,1)}) custom-call(bf16[32,6,32,512]{3,2,1,0:T(8,128)(2,1)} %bitcast.140), custom_call_target="tpu_custom_call" | custom-call | flops 1000 | bytes 1000 | tf_op jit(solution)/shard_map/by_time/pallas_call | solution.py:52
  5.8 1.7 %collective-permute-start.4 = (bf16[3,8,3,64,512]{4,3,2,1,0:T(8,128)(2,1)}, bf16[3,8,3,64,512]{4,3,2,1,0:T(8,128)(2,1)}, u32[]{:S(2)}, u32[]{:S(2)}) collective-permute-start(bf16[3,8,3,64,512]{4,3,2,1,0:T(8,128)(2,1)} %bitcast.129), channel_id=1, source_target_pairs={{0,64},{64,0},{1,65},{65,1},{2,66},{66,2},{3,67},{67,3},{4,68},{68... | collective-permute-start | bytes 14155784 | tf_op jit(solution)/shard_map/ppermute | solution.py:17
  7.5 9.3 %by_time.4 = (bf16[4,4,2,6,64,512]{5,4,3,2,1,0:T(8,128)(2,1)}, bf16[1,4,2,6,64,512]{5,4,3,2,1,0:T(8,128)(2,1)}) custom-call(bf16[64,6,32,512]{3,2,1,0:T(8,128)(2,1)} %bitcast.127, bf16[3,8,3,64,512]{4,3,2,1,0:T(8,128)(2,1)} %bitcast.130), custom_call_target="tpu_custom_call" | custom-call | flops 1000 | bytes 1000 | tf_op jit(solution)/shard_map/by_time/pallas_call | solution.py:52
  16.9 3.2 %fusion.2 = (bf16[1,2,3,192,512]{4,3,2,1,0:T(8,128)(2,1)S(1)}, bf16[2,3,192,512]{3,2,1,0:T(8,128)(2,1)}, bf16[2,3,192,512]{3,2,1,0:T(8,128)(2,1)}, bf16[2,3,192,512]{3,2,1,0:T(8,128)(2,1)}) fusion(s32[]{:T(128)S(6)} %select_n.135, bf16[4,2,3,128,512]{4,3,2,1,0:T(8,128)(2,1)} %bitcast.143, bf16[4,2,3,64,512]{4,3,2,1,0:T(8,128)(2,1)S(1)} %bitcast.139, ...), kind=kLoop, calls=%fused_computation.28 | loop fusion | flops 9437184 | bytes 9437200 | tf_op jit(solution)/shard_map/concatenate | solution.py:278
  20.1 1.9 %collective-permute-start.8 = (bf16[2,3,192,512]{3,2,1,0:T(8,128)(2,1)}, bf16[2,3,192,512]{3,2,1,0:T(8,128)(2,1)S(1)}, u32[]{:S(2)}, u32[]{:S(2)}) collective-permute-start(bf16[2,3,192,512]{3,2,1,0:T(8,128)(2,1)} %get-tuple-element.17), channel_id=1, source_target_pairs={{0,8},{8,16},{16,24},{24,0},{1,9},{9,17},{17,25},{25,1},{2,10},{10... | collective-permute-start | bytes 3538952 | tf_op jit(solution)/shard_map/ppermute | solution.py:227
  22.0 2.2 %collective-permute-start.9 = (bf16[2,3,192,512]{3,2,1,0:T(8,128)(2,1)}, bf16[2,3,192,512]{3,2,1,0:T(8,128)(2,1)}, u32[]{:S(2)}, u32[]{:S(2)}) collective-permute-start(bf16[2,3,192,512]{3,2,1,0:T(8,128)(2,1)} %get-tuple-element.18), channel_id=1, source_target_pairs={{0,24},{8,0},{16,8},{24,16},{1,25},{9,1},{17,9},{25,17},{2,26},{10... | collective-permute-start | bytes 3538952 | tf_op jit(solution)/shard_map/ppermute | solution.py:227
  24.2 1.8 %collective-permute-start.10 = (bf16[2,3,192,512]{3,2,1,0:T(8,128)(2,1)}, bf16[2,3,192,512]{3,2,1,0:T(8,128)(2,1)}, u32[]{:S(2)}, u32[]{:S(2)}) collective-permute-start(bf16[2,3,192,512]{3,2,1,0:T(8,128)(2,1)} %get-tuple-element.19), channel_id=1, source_target_pairs={{0,16},{8,24},{16,0},{24,8},{1,17},{9,25},{17,1},{25,9},{2,18},{10... | collective-permute-start | bytes 3538952 | tf_op jit(solution)/shard_map/ppermute | solution.py:227
  26.0 8.4 %by_time.5 = bf16[4,4,2,6,64,512]{5,4,3,2,1,0:T(8,128)(2,1)} custom-call(bf16[64,6,32,512]{3,2,1,0:T(8,128)(2,1)} %collective-permute-done.block), custom_call_target="tpu_custom_call" | custom-call | flops 1000 | bytes 1000 | tf_op jit(solution)/shard_map/by_time/pallas_call | solution.py:52
  34.4 11.8 %project.3 = f32[3,8,2,32,128]{4,3,2,1,0:T(8,128)} custom-call(bf16[3,8,3,64,512]{4,3,2,1,0:T(8,128)(2,1)} %bitcast.131, bf16[4,8,3,128,512]{4,3,2,1,0:T(8,128)(2,1)} %bitcast.123, bf16[4,8,3,128,512]{4,3,2,1,0:T(8,128)(2,1)} %bitcast.120), custom_call_target="tpu_custom_call" | custom-call | flops 1000 | bytes 1000 | tf_op jit(solution)/shard_map/project/pallas_call | solution.py:208
  46.2 6.2 %project.4 = f32[1,8,2,32,128]{4,3,2,1,0:T(8,128)} custom-call(bf16[1,8,3,64,512]{4,3,2,1,0:T(8,128)(2,1)} %bitcast.138, bf16[4,8,3,128,512]{4,3,2,1,0:T(8,128)(2,1)} %bitcast.124, bf16[4,8,3,128,512]{4,3,2,1,0:T(8,128)(2,1)} %bitcast.121), custom_call_target="tpu_custom_call" | custom-call | flops 1000 | bytes 1000 | tf_op jit(solution)/shard_map/project/pallas_call | solution.py:208
  52.4 1.4 slice.109
  53.7 1.4 slice.108
  55.1 1.0 copy-done.3
  56.1 19.3 %collective-permute-done.9 = bf16[2,3,192,512]{3,2,1,0:T(8,128)(2,1)} collective-permute-done((bf16[2,3,192,512]{3,2,1,0:T(8,128)(2,1)}, bf16[2,3,192,512]{3,2,1,0:T(8,128)(2,1)}, u32[]{:S(2)}, u32[]{:S(2)}) %collective-permute-start.9) | collective-permute-done | bytes 1179680 | tf_op jit(solution)/shard_map/ppermute | solution.py:227
  75.4 1.8 %collective-permute-done.10 = bf16[2,3,192,512]{3,2,1,0:T(8,128)(2,1)} collective-permute-done((bf16[2,3,192,512]{3,2,1,0:T(8,128)(2,1)}, bf16[2,3,192,512]{3,2,1,0:T(8,128)(2,1)}, u32[]{:S(2)}, u32[]{:S(2)}) %collective-permute-start.10) | collective-permute-done | bytes 1179680 | tf_op jit(solution)/shard_map/ppermute | solution.py:227
  77.2 2.3 %pad_maximum_fusion = bf16[4,2,3,192,512]{4,3,2,1,0:T(8,128)(2,1)S(1)} fusion(bf16[1,2,3,192,512]{4,3,2,1,0:T(8,128)(2,1)} %bitcast.40, bf16[1,2,3,192,512]{4,3,2,1,0:T(8,128)(2,1)} %bitcast.38, bf16[1,2,3,192,512]{4,3,2,1,0:T(8,128)(2,1)} %bitcast.132, bf16[1,2,3,192,512]{4,3,2,1,0:T(8,128)(2,1)S(1)} %get-tuple-element.16), kind=kLoop, calls=%fused_computation.9 | loop fusion | flops 7077888 | bytes 9437184 | tf_op jit(solution)/shard_map/stack | solution.py:281
  79.5 0.3 slice.113.own
  80.6 2.3 %slice.110 = bf16[1,4,2,6,64,512]{5,4,3,2,1,0:T(8,128)(2,1)S(1)} slice(bf16[4,4,2,6,64,512]{5,4,3,2,1,0:T(8,128)(2,1)} %by_time.5), slice={[0:1], [0:4], [0:2], [0:6], [0:64], [0:512]} | slice | bytes 6291456 | tf_op jit(solution)/shard_map/slice | solution.py:78
  83.0 1.0 fusion.26
  83.9 1.5 collective-permute-start.1
  85.4 1.7 %collective-permute-start.2 = (f32[4,2,64,128]{3,2,1,0:T(8,128)}, f32[4,2,64,128]{3,2,1,0:T(8,128)}, u32[]{:S(2)}, u32[]{:S(2)}) collective-permute-start(f32[4,2,64,128]{3,2,1,0:T(8,128)} %get-tuple-element.24), channel_id=1, source_target_pairs={{0,6},{2,0},{4,2},{6,4},{1,7},{3,1},{5,3},{7,5},{8,14},{10,8},{12,... | collective-permute-start | bytes 786440 | tf_op jit(solution)/shard_map/ppermute | solution.py:243
  87.2 1.8 %collective-permute-start.3 = (f32[4,2,64,128]{3,2,1,0:T(8,128)}, f32[4,2,64,128]{3,2,1,0:T(8,128)}, u32[]{:S(2)}, u32[]{:S(2)}) collective-permute-start(f32[4,2,64,128]{3,2,1,0:T(8,128)} %get-tuple-element.25), channel_id=1, source_target_pairs={{0,4},{2,6},{4,0},{6,2},{1,5},{3,7},{5,1},{7,3},{8,12},{10,14},{12... | collective-permute-start | bytes 786440 | tf_op jit(solution)/shard_map/ppermute | solution.py:243
  89.0 0.7 slice_bitcast_fusion.after
  89.7 2.4 %choose.1 = bf16[4,8,512]{2,1,0:T(8,128)(2,1)} custom-call(s32[4]{0:T(128)} %index.1, s32[1]{0:T(128)S(6)} %copy.24.when, bf16[64,6,32,512]{3,2,1,0:T(8,128)(2,1)} %bitcast.128, bf16[128,512]{1,0:T(8,128)(2,1)} %slice_bitcast_fusion.after), custom_call_target="tpu_custom_call" | custom-call | flops 1000 | bytes 1000 | tf_op jit(solution)/shard_map/choose/pallas_call | solution.py:122
  92.1 2.5 %pad_maximum_fusion.2 = (bf16[4,1,3,64,512]{4,3,2,1,0:T(8,128)(2,1)}, bf16[4,1,3,64,512]{4,3,2,1,0:T(8,128)(2,1)S(1)}) fusion(bf16[1,2,3,192,512]{4,3,2,1,0:T(8,128)(2,1)} %bitcast.40, bf16[1,2,3,192,512]{4,3,2,1,0:T(8,128)(2,1)} %bitcast.38, bf16[1,2,3,192,512]{4,3,2,1,0:T(8,128)(2,1)} %bitcast.133, bf16[1,2,3,192,512]{4,3,2,1,0:T(8,128)(2,1)} %copy-done.2), kind=kLoop, calls=%fused_computation.34 | loop fusion | flops 6291456 | bytes 6291456 | tf_op jit(solution)/shard_map/slice | solution.py:285
  94.6 1.0 pad_maximum_fusion.1.refs_0_
  95.6 3.5 %collective-permute-done.2 = f32[4,2,64,128]{3,2,1,0:T(8,128)} collective-permute-done((f32[4,2,64,128]{3,2,1,0:T(8,128)}, f32[4,2,64,128]{3,2,1,0:T(8,128)}, u32[]{:S(2)}, u32[]{:S(2)}) %collective-permute-start.2) | collective-permute-done | bytes 262176 | tf_op jit(solution)/shard_map/ppermute | solution.py:243
  99.0 1.7 %collective-permute-done.3 = f32[4,2,64,128]{3,2,1,0:T(8,128)} collective-permute-done((f32[4,2,64,128]{3,2,1,0:T(8,128)}, f32[4,2,64,128]{3,2,1,0:T(8,128)}, u32[]{:S(2)}, u32[]{:S(2)}) %collective-permute-start.3) | collective-permute-done | bytes 262176 | tf_op jit(solution)/shard_map/ppermute | solution.py:243
  100.7 1.2 fusion.24
  101.9 0.7 copy-done.9
  102.6 0.6 slice_bitcast_fusion.2.refs_1_
  103.3 0.6 collective-permute-start.11
  103.9 0.1 copy.16
  104.0 0.2 fusion.37
  104.2 0.6 gather_fusion
  104.9 5.9 %collective-permute-done.4.refs_0_ = bf16[3,8,3,64,512]{4,3,2,1,0:T(8,128)(2,1)} collective-permute-done((bf16[3,8,3,64,512]{4,3,2,1,0:T(8,128)(2,1)}, bf16[3,8,3,64,512]{4,3,2,1,0:T(8,128)(2,1)}, u32[]{:S(2)}, u32[]{:S(2)}) %collective-permute-start.4) | collective-permute-done | bytes 4718624 | tf_op jit(solution)/shard_map/ppermute | solution.py:17
  110.8 11.8 %project.5 = f32[3,8,2,32,128]{4,3,2,1,0:T(8,128)} custom-call(bf16[3,8,3,64,512]{4,3,2,1,0:T(8,128)(2,1)} %collective-permute-done.4.refs_0_, bf16[4,8,3,128,512]{4,3,2,1,0:T(8,128)(2,1)} %bitcast.125, bf16[4,8,3,128,512]{4,3,2,1,0:T(8,128)(2,1)} %bitcast.122), custom_call_target="tpu_custom_call" | custom-call | flops 1000 | bytes 1000 | tf_op jit(solution)/shard_map/project/pallas_call | solution.py:208
  122.6 1.4 slice.116
  124.0 1.2 copy.17
  125.2 1.7 %collective-permute-start.13 = (bf16[24,32,512]{2,1,0:T(8,128)(2,1)}, bf16[24,32,512]{2,1,0:T(8,128)(2,1)}, u32[]{:S(2)}, u32[]{:S(2)}) collective-permute-start(bf16[24,32,512]{2,1,0:T(8,128)(2,1)} %hold.7), channel_id=1, source_target_pairs={{0,64},{64,0},{1,65},{65,1},{2,66},{66,2},{3,67},{67,3},{4,68},{68... | collective-permute-start | bytes 2359304 | tf_op jit(solution)/shard_map/ppermute | solution.py:17
  127.0 0.9 fusion.15
  127.9 1.9 %collective-permute-start.5 = (f32[512,128]{1,0:T(8,128)}, f32[512,128]{1,0:T(8,128)}, u32[]{:S(2)}, u32[]{:S(2)}) collective-permute-start(f32[512,128]{1,0:T(8,128)} %get-tuple-element.20), channel_id=1, source_target_pairs={{0,8},{8,16},{16,24},{24,0},{1,9},{9,17},{17,25},{25,1},{2,10},{10... | collective-permute-start | bytes 786440 | tf_op jit(solution)/shard_map/ppermute | solution.py:227
  129.8 2.1 %collective-permute-start.6 = (f32[512,128]{1,0:T(8,128)}, f32[512,128]{1,0:T(8,128)}, u32[]{:S(2)}, u32[]{:S(2)}) collective-permute-start(f32[512,128]{1,0:T(8,128)} %get-tuple-element.21), channel_id=1, source_target_pairs={{0,24},{8,0},{16,8},{24,16},{1,25},{9,1},{17,9},{25,17},{2,26},{10... | collective-permute-start | bytes 786440 | tf_op jit(solution)/shard_map/ppermute | solution.py:227
  131.9 1.9 %collective-permute-start.7 = (f32[512,128]{1,0:T(8,128)}, f32[512,128]{1,0:T(8,128)}, u32[]{:S(2)}, u32[]{:S(2)}) collective-permute-start(f32[512,128]{1,0:T(8,128)} %get-tuple-element.22), channel_id=1, source_target_pairs={{0,16},{8,24},{16,0},{24,8},{1,17},{9,25},{17,1},{25,9},{2,18},{10... | collective-permute-start | bytes 786440 | tf_op jit(solution)/shard_map/ppermute | solution.py:227
  133.9 0.8 fusion.36
  134.6 0.3 collective-permute-start.19
  134.9 3.3 %project_pieces.2.refs_1_.refs_0_ = f32[2,32,128]{2,1,0:T(8,128)S(1)} custom-call(bf16[25,32,512]{2,1,0:T(8,128)(2,1)} %collective-permute-done.11.col, bf16[4,2,3,128,512]{4,3,2,1,0:T(8,128)(2,1)S(1)} %slice.113.own, bf16[4,2,3,128,512]{4,3,2,1,0:T(8,128)(2,1)} %collective-permute-done.12.other), custom_call_target="tpu_custom_call" | custom-call | flops 1000 | bytes 1000 | tf_op jit(solution)/shard_map/project_pieces/pallas_call | solution.py:186
  138.3 0.6 copy-done
  138.9 5.6 %collective-permute-done.7.refs_0_ = f32[512,128]{1,0:T(8,128)} collective-permute-done((f32[512,128]{1,0:T(8,128)}, f32[512,128]{1,0:T(8,128)}, u32[]{:S(2)}, u32[]{:S(2)}) %collective-permute-start.7) | collective-permute-done | bytes 262176 | tf_op jit(solution)/shard_map/ppermute | solution.py:227
  144.5 1.2 fusion.13
  145.8 3.3 %project_pieces.3 = f32[2,32,128]{2,1,0:T(8,128)S(1)} custom-call(bf16[24,32,512]{2,1,0:T(8,128)(2,1)} %collective-permute-done.13.col, bf16[4,2,3,128,512]{4,3,2,1,0:T(8,128)(2,1)S(1)} %slice.113.own, bf16[4,2,3,128,512]{4,3,2,1,0:T(8,128)(2,1)} %collective-permute-done.12.other, f32[2,32,128]{2,1,0:T(8,128)S(1)} %copy-done.1), custom_call_target="tpu_custom_call" | custom-call | flops 1000 | bytes 1000 | tf_op jit(solution)/shard_map/project_pieces/pallas_call | solution.py:186
  149.2 1.6 collective-permute-start.14
  150.8 2.7 %collective-permute-start.16 = (f32[2,64,128]{2,1,0:T(8,128)S(1)}, f32[2,64,128]{2,1,0:T(8,128)S(1)}, u32[]{:S(2)}, u32[]{:S(2)}) collective-permute-start(f32[2,64,128]{2,1,0:T(8,128)S(1)} %get-tuple-element.27), channel_id=1, source_target_pairs={{0,4},{2,6},{4,0},{6,2},{1,5},{3,7},{5,1},{7,3},{8,12},{10,14},{12... | collective-permute-start | bytes 196616 | tf_op jit(solution)/shard_map/ppermute | solution.py:243
  153.5 1.4 collective-permute-start.15
  155.0 1.6 collective-permute-done.16
  156.5 1.2 collective-permute-done.15
  157.8 3.0 %collective-permute-start.17 = (f32[128,128]{1,0:T(8,128)S(1)}, f32[128,128]{1,0:T(8,128)S(1)}, u32[]{:S(2)}, u32[]{:S(2)}) collective-permute-start(f32[128,128]{1,0:T(8,128)S(1)} %fusion.30), channel_id=1, source_target_pairs={{0,1},{1,0},{2,3},{3,2},{4,5},{5,4},{6,7},{7,6},{8,9},{9,8},{10,11... | collective-permute-start | bytes 196616 | tf_op jit(solution)/shard_map/ppermute | solution.py:17
  160.8 0.7 broadcast_select_fusion
  161.5 2.1 %collective-permute-done.17 = f32[128,128]{1,0:T(8,128)S(1)} collective-permute-done((f32[128,128]{1,0:T(8,128)S(1)}, f32[128,128]{1,0:T(8,128)S(1)}, u32[]{:S(2)}, u32[]{:S(2)}) %collective-permute-start.17) | collective-permute-done | bytes 65568 | tf_op jit(solution)/shard_map/ppermute | solution.py:17
  163.8 1.2 collective-permute-done.18
  165.1 0.2 select_reduce_fusion
  165.4 0.1 copy.18
  165.5 0.7 copy.19
  (57 shorter events, 0.8 us)
Async XLA Ops:
  0.6 25.4 %collective-permute-start = (bf16[64,6,32,512]{3,2,1,0:T(8,128)(2,1)}, bf16[64,6,32,512]{3,2,1,0:T(8,128)(2,1)}, u32[]{:S(2)}, u32[]{:S(2)}) collective-permute-start(bf16[64,6,32,512]{3,2,1,0:T(8,128)(2,1)} %bitcast.126), channel_id=1, source_target_pairs={{0,32},{32,0},{1,33},{33,1},{2,34},{34,2},{3,35},{35,3},{4,36},{36... | collective-permute-start | bytes 37748744 | tf_op jit(solution)/shard_map/ppermute | solution.py:17
  5.8 11.1 %copy-start.6 = (bf16[1,4,2,6,32,512]{5,4,3,2,1,0:T(8,128)(2,1)S(1)}, bf16[1,4,2,6,32,512]{5,4,3,2,1,0:T(8,128)(2,1)}, u32[]{:S(2)}) copy-start(bf16[1,4,2,6,32,512]{5,4,3,2,1,0:T(8,128)(2,1)} %get-tuple-element.8) | copy-start | bytes 4718596
  5.8 105.0 %collective-permute-start.4 = (bf16[3,8,3,64,512]{4,3,2,1,0:T(8,128)(2,1)}, bf16[3,8,3,64,512]{4,3,2,1,0:T(8,128)(2,1)}, u32[]{:S(2)}, u32[]{:S(2)}) collective-permute-start(bf16[3,8,3,64,512]{4,3,2,1,0:T(8,128)(2,1)} %bitcast.129), channel_id=1, source_target_pairs={{0,64},{64,0},{1,65},{65,1},{2,66},{66,2},{3,67},{67,3},{4,68},{68... | collective-permute-start | bytes 14155784 | tf_op jit(solution)/shard_map/ppermute | solution.py:17
  20.1 57.2 %copy-start.2 = (bf16[1,2,3,192,512]{4,3,2,1,0:T(8,128)(2,1)}, bf16[1,2,3,192,512]{4,3,2,1,0:T(8,128)(2,1)S(1)}, u32[]{:S(2)}) copy-start(bf16[1,2,3,192,512]{4,3,2,1,0:T(8,128)(2,1)S(1)} %get-tuple-element.16) | copy-start | bytes 3538948
  20.1 35.0 %collective-permute-start.8 = (bf16[2,3,192,512]{3,2,1,0:T(8,128)(2,1)}, bf16[2,3,192,512]{3,2,1,0:T(8,128)(2,1)S(1)}, u32[]{:S(2)}, u32[]{:S(2)}) collective-permute-start(bf16[2,3,192,512]{3,2,1,0:T(8,128)(2,1)} %get-tuple-element.17), channel_id=1, source_target_pairs={{0,8},{8,16},{16,24},{24,0},{1,9},{9,17},{17,25},{25,1},{2,10},{10... | collective-permute-start | bytes 3538952 | tf_op jit(solution)/shard_map/ppermute | solution.py:227
  22.0 53.4 %collective-permute-start.9 = (bf16[2,3,192,512]{3,2,1,0:T(8,128)(2,1)}, bf16[2,3,192,512]{3,2,1,0:T(8,128)(2,1)}, u32[]{:S(2)}, u32[]{:S(2)}) collective-permute-start(bf16[2,3,192,512]{3,2,1,0:T(8,128)(2,1)} %get-tuple-element.18), channel_id=1, source_target_pairs={{0,24},{8,0},{16,8},{24,16},{1,25},{9,1},{17,9},{25,17},{2,26},{10... | collective-permute-start | bytes 3538952 | tf_op jit(solution)/shard_map/ppermute | solution.py:227
  24.2 53.0 %collective-permute-start.10 = (bf16[2,3,192,512]{3,2,1,0:T(8,128)(2,1)}, bf16[2,3,192,512]{3,2,1,0:T(8,128)(2,1)}, u32[]{:S(2)}, u32[]{:S(2)}) collective-permute-start(bf16[2,3,192,512]{3,2,1,0:T(8,128)(2,1)} %get-tuple-element.19), channel_id=1, source_target_pairs={{0,16},{8,24},{16,0},{24,8},{1,17},{9,25},{17,1},{25,9},{2,18},{10... | collective-permute-start | bytes 3538952 | tf_op jit(solution)/shard_map/ppermute | solution.py:227
  55.1 1.0 copy-start.3
  79.8 54.8 %collective-permute-start.12 = (bf16[4,2,3,128,512]{4,3,2,1,0:T(8,128)(2,1)S(1)}, bf16[4,2,3,128,512]{4,3,2,1,0:T(8,128)(2,1)}, u32[]{:S(2)}, u32[]{:S(2)}) collective-permute-start(bf16[4,2,3,128,512]{4,3,2,1,0:T(8,128)(2,1)S(1)} %slice.113.own), channel_id=1, source_target_pairs={{0,32},{32,0},{1,33},{33,1},{2,34},{34,2},{3,35},{35,3},{4,36},{36... | collective-permute-start | bytes 9437192 | tf_op jit(solution)/shard_map/ppermute | solution.py:17
  80.6 2.3 %copy-start.4 = (f32[3,8,2,32,128]{4,3,2,1,0:T(8,128)S(1)}, f32[3,8,2,32,128]{4,3,2,1,0:T(8,128)}, u32[]{:S(2)}) copy-start(f32[3,8,2,32,128]{4,3,2,1,0:T(8,128)} %project.3) | copy-start | bytes 2359300
  80.6 2.3 %copy-start.7 = (f32[1,8,2,32,128]{4,3,2,1,0:T(8,128)S(1)}, f32[1,8,2,32,128]{4,3,2,1,0:T(8,128)}, u32[]{:S(2)}) copy-start(f32[1,8,2,32,128]{4,3,2,1,0:T(8,128)} %project.4) | copy-start | bytes 786436
  83.9 11.7 %collective-permute-start.1 = (f32[4,2,64,128]{3,2,1,0:T(8,128)}, f32[4,2,64,128]{3,2,1,0:T(8,128)}, u32[]{:S(2)}, u32[]{:S(2)}) collective-permute-start(f32[4,2,64,128]{3,2,1,0:T(8,128)} %get-tuple-element.23), channel_id=1, source_target_pairs={{0,2},{2,4},{4,6},{6,0},{1,3},{3,5},{5,7},{7,1},{8,10},{10,12},{12... | collective-permute-start | bytes 786440 | tf_op jit(solution)/shard_map/ppermute | solution.py:243
  85.4 13.6 %collective-permute-start.2 = (f32[4,2,64,128]{3,2,1,0:T(8,128)}, f32[4,2,64,128]{3,2,1,0:T(8,128)}, u32[]{:S(2)}, u32[]{:S(2)}) collective-permute-start(f32[4,2,64,128]{3,2,1,0:T(8,128)} %get-tuple-element.24), channel_id=1, source_target_pairs={{0,6},{2,0},{4,2},{6,4},{1,7},{3,1},{5,3},{7,5},{8,14},{10,8},{12,... | collective-permute-start | bytes 786440 | tf_op jit(solution)/shard_map/ppermute | solution.py:243
  87.2 13.6 %collective-permute-start.3 = (f32[4,2,64,128]{3,2,1,0:T(8,128)}, f32[4,2,64,128]{3,2,1,0:T(8,128)}, u32[]{:S(2)}, u32[]{:S(2)}) collective-permute-start(f32[4,2,64,128]{3,2,1,0:T(8,128)} %get-tuple-element.25), channel_id=1, source_target_pairs={{0,4},{2,6},{4,0},{6,2},{1,5},{3,7},{5,1},{7,3},{8,12},{10,14},{12... | collective-permute-start | bytes 786440 | tf_op jit(solution)/shard_map/ppermute | solution.py:243
  92.1 2.5 %copy-start.11 = (bf16[4,8,512]{2,1,0:T(8,128)(2,1)S(1)}, bf16[4,8,512]{2,1,0:T(8,128)(2,1)}, u32[]{:S(2)}) copy-start(bf16[4,8,512]{2,1,0:T(8,128)(2,1)} %choose.1) | copy-start | bytes 98308
  94.6 6.2 %copy-start.8 = (f32[1,8,2,32,128]{4,3,2,1,0:T(8,128)S(1)}, f32[1,8,2,32,128]{4,3,2,1,0:T(8,128)}, u32[]{:S(2)}) copy-start(f32[1,8,2,32,128]{4,3,2,1,0:T(8,128)} %project.4) | copy-start | bytes 786436
  95.6 8.3 %copy-start.12 = (s32[4,4]{1,0:T(4,128)S(1)}, s32[4,4]{1,0:T(4,128)}, u32[]{:S(2)}) copy-start(s32[4,4]{1,0:T(4,128)} %param.9) | copy-start | bytes 196
  101.9 0.7 copy-start.9
  103.3 28.7 %collective-permute-start.11 = (bf16[25,32,512]{2,1,0:T(8,128)(2,1)}, bf16[25,32,512]{2,1,0:T(8,128)(2,1)}, u32[]{:S(2)}, u32[]{:S(2)}) collective-permute-start(bf16[25,32,512]{2,1,0:T(8,128)(2,1)} %hold.5), channel_id=1, source_target_pairs={{0,64},{64,0},{1,65},{65,1},{2,66},{66,2},{3,67},{67,3},{4,68},{68... | collective-permute-start | bytes 2457608 | tf_op jit(solution)/shard_map/ppermute | solution.py:17
  124.0 3.0 %copy-start.10 = (f32[4,2,64,128]{3,2,1,0:T(8,128)S(1)}, f32[4,2,64,128]{3,2,1,0:T(8,128)}, u32[]{:S(2)}) copy-start(f32[4,2,64,128]{3,2,1,0:T(8,128)} %copy-done.9) | copy-start | bytes 786436
  125.2 1.8 %copy-start.5 = (f32[4,3,2,64,128]{4,3,2,1,0:T(8,128)}, f32[4,3,2,64,128]{4,3,2,1,0:T(8,128)S(1)}, u32[]{:S(2)}) copy-start(f32[4,3,2,64,128]{4,3,2,1,0:T(8,128)S(1)} %copy.17) | copy-start | bytes 2359300
  125.2 20.6 %collective-permute-start.13 = (bf16[24,32,512]{2,1,0:T(8,128)(2,1)}, bf16[24,32,512]{2,1,0:T(8,128)(2,1)}, u32[]{:S(2)}, u32[]{:S(2)}) collective-permute-start(bf16[24,32,512]{2,1,0:T(8,128)(2,1)} %hold.7), channel_id=1, source_target_pairs={{0,64},{64,0},{1,65},{65,1},{2,66},{66,2},{3,67},{67,3},{4,68},{68... | collective-permute-start | bytes 2359304 | tf_op jit(solution)/shard_map/ppermute | solution.py:17
  127.9 16.7 %collective-permute-start.5 = (f32[512,128]{1,0:T(8,128)}, f32[512,128]{1,0:T(8,128)}, u32[]{:S(2)}, u32[]{:S(2)}) collective-permute-start(f32[512,128]{1,0:T(8,128)} %get-tuple-element.20), channel_id=1, source_target_pairs={{0,8},{8,16},{16,24},{24,0},{1,9},{9,17},{17,25},{25,1},{2,10},{10... | collective-permute-start | bytes 786440 | tf_op jit(solution)/shard_map/ppermute | solution.py:227
  129.8 14.7 %collective-permute-start.6 = (f32[512,128]{1,0:T(8,128)}, f32[512,128]{1,0:T(8,128)}, u32[]{:S(2)}, u32[]{:S(2)}) collective-permute-start(f32[512,128]{1,0:T(8,128)} %get-tuple-element.21), channel_id=1, source_target_pairs={{0,24},{8,0},{16,8},{24,16},{1,25},{9,1},{17,9},{25,17},{2,26},{10... | collective-permute-start | bytes 786440 | tf_op jit(solution)/shard_map/ppermute | solution.py:227
  131.9 12.6 %collective-permute-start.7 = (f32[512,128]{1,0:T(8,128)}, f32[512,128]{1,0:T(8,128)}, u32[]{:S(2)}, u32[]{:S(2)}) collective-permute-start(f32[512,128]{1,0:T(8,128)} %get-tuple-element.22), channel_id=1, source_target_pairs={{0,16},{8,24},{16,0},{24,8},{1,17},{9,25},{17,1},{25,9},{2,18},{10... | collective-permute-start | bytes 786440 | tf_op jit(solution)/shard_map/ppermute | solution.py:227
  134.6 20.3 %collective-permute-start.19 = (bf16[32,512]{1,0:T(8,128)(2,1)S(1)}, bf16[32,512]{1,0:T(8,128)(2,1)S(1)}, u32[]{:S(2)}, u32[]{:S(2)}) collective-permute-start(bf16[32,512]{1,0:T(8,128)(2,1)S(1)} %fusion.36), channel_id=1, source_target_pairs={{0,32},{32,0},{1,33},{33,1},{2,34},{34,2},{3,35},{35,3},{4,36},{36... | collective-permute-start | bytes 98312 | tf_op jit(solution)/shard_map/ppermute | solution.py:17
  138.3 0.6 copy-start
  144.5 1.3 copy-start.1
  149.2 5.7 %collective-permute-start.14 = (f32[2,64,128]{2,1,0:T(8,128)S(1)}, f32[2,64,128]{2,1,0:T(8,128)S(1)}, u32[]{:S(2)}, u32[]{:S(2)}) collective-permute-start(f32[2,64,128]{2,1,0:T(8,128)S(1)} %get-tuple-element.26), channel_id=1, source_target_pairs={{0,2},{2,4},{4,6},{6,0},{1,3},{3,5},{5,7},{7,1},{8,10},{10,12},{12... | collective-permute-start | bytes 196616 | tf_op jit(solution)/shard_map/ppermute | solution.py:243
  150.8 5.8 %collective-permute-start.16 = (f32[2,64,128]{2,1,0:T(8,128)S(1)}, f32[2,64,128]{2,1,0:T(8,128)S(1)}, u32[]{:S(2)}, u32[]{:S(2)}) collective-permute-start(f32[2,64,128]{2,1,0:T(8,128)S(1)} %get-tuple-element.27), channel_id=1, source_target_pairs={{0,4},{2,6},{4,0},{6,2},{1,5},{3,7},{5,1},{7,3},{8,12},{10,14},{12... | collective-permute-start | bytes 196616 | tf_op jit(solution)/shard_map/ppermute | solution.py:243
  153.5 4.3 %collective-permute-start.15 = (f32[2,64,128]{2,1,0:T(8,128)S(1)}, f32[2,64,128]{2,1,0:T(8,128)S(1)}, u32[]{:S(2)}, u32[]{:S(2)}) collective-permute-start(f32[2,64,128]{2,1,0:T(8,128)S(1)} %get-tuple-element.28), channel_id=1, source_target_pairs={{0,6},{2,0},{4,2},{6,4},{1,7},{3,1},{5,3},{7,5},{8,14},{10,8},{12,... | collective-permute-start | bytes 196616 | tf_op jit(solution)/shard_map/ppermute | solution.py:243
  157.8 5.8 %collective-permute-start.17 = (f32[128,128]{1,0:T(8,128)S(1)}, f32[128,128]{1,0:T(8,128)S(1)}, u32[]{:S(2)}, u32[]{:S(2)}) collective-permute-start(f32[128,128]{1,0:T(8,128)S(1)} %fusion.30), channel_id=1, source_target_pairs={{0,1},{1,0},{2,3},{3,2},{4,5},{5,4},{6,7},{7,6},{8,9},{9,8},{10,11... | collective-permute-start | bytes 196616 | tf_op jit(solution)/shard_map/ppermute | solution.py:17
  163.7 1.3 collective-permute-start.18

commit v14 on v13

--- a/solution.py
+++ b/solution.py
@@ -171,22 +171,25 @@
             row += n
 
 
-def pieces_kernel(y, col, own, other, *refs):
+def pieces_kernel(col, own, other, *refs):
     total, out = None, refs[-1]
     for block in range(own.shape[0]):
         for colour in range(own.shape[2]):
             at = 2 * (block * own.shape[2] + colour)
-            term = product([col[at], col[at + 1]], own[block, y, colour], other[block, y, colour])
+            term = product([col[at], col[at + 1]], own[block, 0, colour], other[block, 0, colour])
             total = term if total is None else total + term
     out[0], out[1] = real_imag(total, 0, out.shape[1])
 
 
 def project_pieces(cols, own, other, y, *after):
-    whole = pl.BlockSpec(memory_space=pltpu.VMEM)
-    return pl.pallas_call(
-        functools.partial(pieces_kernel, y),
-        in_specs=[whole] * 3 + [ANY] * len(after),
-        out_specs=whole,
+    count, _, *rest = own.shape
+    vecs = pl.BlockSpec((count, 1, *rest), lambda i: (0, y, 0, 0, 0))
+    rows = pl.BlockSpec((2 * count * rest[0], *cols.shape[1:]), lambda i: (0, 0, 0))
+    return pl.pallas_call(
+        pieces_kernel,
+        grid=(1,),
+        in_specs=[rows, vecs, vecs] + [ANY] * len(after),
+        out_specs=pl.BlockSpec((2, cols.shape[1], own.shape[3]), lambda i: (0, 0, 0)),
         out_shape=jax.ShapeDtypeStruct((2, cols.shape[1], own.shape[3]), jnp.float32),
         compiler_params=pltpu.CompilerParams(vmem_limit_bytes=24 * 2**20),
         cost_estimate=HINT,

time: 168 us -> 167 us (level)
  no operation moved by 1% of the time
where the time goes in v14:
time: 167 us; the launch traced here: 166 us
  Pallas kernels  60.7 us (36%)
  waiting for transfers between devices  44.4 us (27%)
  starting transfers between devices  30.2 us (18%)
  other arithmetic  15.5 us (9%)
  local copies, waits for them, and re-layouts  13.4 us (8%)
  between operations  1.72 us (1%)
    pallas_call x3, Pallas kernels, project(): pl.pallas_call(functools.partial(dot_kernel, len(cols)), grid=(size, inne...  29.7 us
    ppermute x6, waiting for transfers between devices, share_z(): lax.ppermute(pick(slabs, (me + k) % 4), 'z', [(i, (i + k) % 4) for i in r...  27.2 us
    pallas_call x3, Pallas kernels, by_time(): pl.pallas_call(functools.partial(by_time_kernel, cuts), in_specs=[ANY] *...  22.7 us
    ppermute x6, starting transfers between devices, share_z(): lax.ppermute(pick(slabs, (me + k) % 4), 'z', [(i, (i + k) % 4) for i in r...  11.8 us
    ppermute x6, starting transfers between devices, sum_x(): total = total + lax.ppermute(pick(slabs, (me + k) % 4), 'x', pairs)  10.8 us
    ppermute x8, waiting for transfers between devices, swap(): return lax.ppermute(value, axis, SWAP)  9.23 us
    ppermute x6, waiting for transfers between devices, sum_x(): total = total + lax.ppermute(pick(slabs, (me + k) % 4), 'x', pairs)  7.94 us
    ppermute x8, starting transfers between devices, swap(): return lax.ppermute(value, axis, SWAP)  7.59 us
  transfers between devices with their start and end apart: 20, of which 10 were waited for; matrix products, arithmetic and copies ran while one was open for 15% of the time, Pallas kernels for 37%

profile of v14, /device:TPU:0, one launch (start us, length us, event | category | flops | bytes accessed | tf_op | source)
XLA Modules:
  0.0 165.8 jit_solution(2045597182765780248)
XLA Ops:
  0.6 0.1 collective-permute-start
  0.7 5.1 %by_time.3 = (bf16[3,4,2,6,32,512]{5,4,3,2,1,0:T(8,128)(2,1)}, bf16[1,4,2,6,32,512]{5,4,3,2,1,0:T(8,128)(2,1)}) custom-call(bf16[32,6,32,512]{3,2,1,0:T(8,128)(2,1)} %bitcast.140), custom_call_target="tpu_custom_call" | custom-call | flops 1000 | bytes 1000 | tf_op jit(solution)/shard_map/by_time/pallas_call | solution.py:52
  5.8 1.7 %collective-permute-start.4 = (bf16[3,8,3,64,512]{4,3,2,1,0:T(8,128)(2,1)}, bf16[3,8,3,64,512]{4,3,2,1,0:T(8,128)(2,1)}, u32[]{:S(2)}, u32[]{:S(2)}) collective-permute-start(bf16[3,8,3,64,512]{4,3,2,1,0:T(8,128)(2,1)} %bitcast.129), channel_id=1, source_target_pairs={{0,64},{64,0},{1,65},{65,1},{2,66},{66,2},{3,67},{67,3},{4,68},{68... | collective-permute-start | bytes 14155784 | tf_op jit(solution)/shard_map/ppermute | solution.py:17
  7.5 9.3 %by_time.4 = (bf16[4,4,2,6,64,512]{5,4,3,2,1,0:T(8,128)(2,1)}, bf16[1,4,2,6,64,512]{5,4,3,2,1,0:T(8,128)(2,1)}) custom-call(bf16[64,6,32,512]{3,2,1,0:T(8,128)(2,1)} %bitcast.127, bf16[3,8,3,64,512]{4,3,2,1,0:T(8,128)(2,1)} %bitcast.130), custom_call_target="tpu_custom_call" | custom-call | flops 1000 | bytes 1000 | tf_op jit(solution)/shard_map/by_time/pallas_call | solution.py:52
  16.9 3.2 %fusion.2 = (bf16[1,2,3,192,512]{4,3,2,1,0:T(8,128)(2,1)S(1)}, bf16[2,3,192,512]{3,2,1,0:T(8,128)(2,1)}, bf16[2,3,192,512]{3,2,1,0:T(8,128)(2,1)}, bf16[2,3,192,512]{3,2,1,0:T(8,128)(2,1)}) fusion(s32[]{:T(128)S(6)} %select_n.135, bf16[4,2,3,128,512]{4,3,2,1,0:T(8,128)(2,1)} %bitcast.143, bf16[4,2,3,64,512]{4,3,2,1,0:T(8,128)(2,1)S(1)} %bitcast.139, ...), kind=kLoop, calls=%fused_computation.28 | loop fusion | flops 9437184 | bytes 9437200 | tf_op jit(solution)/shard_map/concatenate | solution.py:281
  20.1 1.9 %collective-permute-start.8 = (bf16[2,3,192,512]{3,2,1,0:T(8,128)(2,1)}, bf16[2,3,192,512]{3,2,1,0:T(8,128)(2,1)S(1)}, u32[]{:S(2)}, u32[]{:S(2)}) collective-permute-start(bf16[2,3,192,512]{3,2,1,0:T(8,128)(2,1)} %get-tuple-element.17), channel_id=1, source_target_pairs={{0,8},{8,16},{16,24},{24,0},{1,9},{9,17},{17,25},{25,1},{2,10},{10... | collective-permute-start | bytes 3538952 | tf_op jit(solution)/shard_map/ppermute | solution.py:230
  22.0 2.2 %collective-permute-start.9 = (bf16[2,3,192,512]{3,2,1,0:T(8,128)(2,1)}, bf16[2,3,192,512]{3,2,1,0:T(8,128)(2,1)}, u32[]{:S(2)}, u32[]{:S(2)}) collective-permute-start(bf16[2,3,192,512]{3,2,1,0:T(8,128)(2,1)} %get-tuple-element.18), channel_id=1, source_target_pairs={{0,24},{8,0},{16,8},{24,16},{1,25},{9,1},{17,9},{25,17},{2,26},{10... | collective-permute-start | bytes 3538952 | tf_op jit(solution)/shard_map/ppermute | solution.py:230
  24.2 1.8 %collective-permute-start.10 = (bf16[2,3,192,512]{3,2,1,0:T(8,128)(2,1)}, bf16[2,3,192,512]{3,2,1,0:T(8,128)(2,1)}, u32[]{:S(2)}, u32[]{:S(2)}) collective-permute-start(bf16[2,3,192,512]{3,2,1,0:T(8,128)(2,1)} %get-tuple-element.19), channel_id=1, source_target_pairs={{0,16},{8,24},{16,0},{24,8},{1,17},{9,25},{17,1},{25,9},{2,18},{10... | collective-permute-start | bytes 3538952 | tf_op jit(solution)/shard_map/ppermute | solution.py:230
  26.0 8.4 %by_time.5 = bf16[4,4,2,6,64,512]{5,4,3,2,1,0:T(8,128)(2,1)} custom-call(bf16[64,6,32,512]{3,2,1,0:T(8,128)(2,1)} %collective-permute-done.block), custom_call_target="tpu_custom_call" | custom-call | flops 1000 | bytes 1000 | tf_op jit(solution)/shard_map/by_time/pallas_call | solution.py:52
  34.4 11.8 %project.3 = f32[3,8,2,32,128]{4,3,2,1,0:T(8,128)} custom-call(bf16[3,8,3,64,512]{4,3,2,1,0:T(8,128)(2,1)} %bitcast.131, bf16[4,8,3,128,512]{4,3,2,1,0:T(8,128)(2,1)} %bitcast.123, bf16[4,8,3,128,512]{4,3,2,1,0:T(8,128)(2,1)} %bitcast.120), custom_call_target="tpu_custom_call" | custom-call | flops 1000 | bytes 1000 | tf_op jit(solution)/shard_map/project/pallas_call | solution.py:211
  46.2 6.2 %project.4 = f32[1,8,2,32,128]{4,3,2,1,0:T(8,128)} custom-call(bf16[1,8,3,64,512]{4,3,2,1,0:T(8,128)(2,1)} %bitcast.138, bf16[4,8,3,128,512]{4,3,2,1,0:T(8,128)(2,1)} %bitcast.124, bf16[4,8,3,128,512]{4,3,2,1,0:T(8,128)(2,1)} %bitcast.121), custom_call_target="tpu_custom_call" | custom-call | flops 1000 | bytes 1000 | tf_op jit(solution)/shard_map/project/pallas_call | solution.py:211
  52.4 1.4 slice.109
  53.7 1.4 slice.108
  55.1 1.0 copy-done.3
  56.1 19.3 %collective-permute-done.9 = bf16[2,3,192,512]{3,2,1,0:T(8,128)(2,1)} collective-permute-done((bf16[2,3,192,512]{3,2,1,0:T(8,128)(2,1)}, bf16[2,3,192,512]{3,2,1,0:T(8,128)(2,1)}, u32[]{:S(2)}, u32[]{:S(2)}) %collective-permute-start.9) | collective-permute-done | bytes 1179680 | tf_op jit(solution)/shard_map/ppermute | solution.py:230
  75.4 1.8 %collective-permute-done.10 = bf16[2,3,192,512]{3,2,1,0:T(8,128)(2,1)} collective-permute-done((bf16[2,3,192,512]{3,2,1,0:T(8,128)(2,1)}, bf16[2,3,192,512]{3,2,1,0:T(8,128)(2,1)}, u32[]{:S(2)}, u32[]{:S(2)}) %collective-permute-start.10) | collective-permute-done | bytes 1179680 | tf_op jit(solution)/shard_map/ppermute | solution.py:230
  77.2 2.3 %pad_maximum_fusion = bf16[4,2,3,192,512]{4,3,2,1,0:T(8,128)(2,1)S(1)} fusion(bf16[1,2,3,192,512]{4,3,2,1,0:T(8,128)(2,1)} %bitcast.40, bf16[1,2,3,192,512]{4,3,2,1,0:T(8,128)(2,1)} %bitcast.38, bf16[1,2,3,192,512]{4,3,2,1,0:T(8,128)(2,1)} %bitcast.132, bf16[1,2,3,192,512]{4,3,2,1,0:T(8,128)(2,1)S(1)} %get-tuple-element.16), kind=kLoop, calls=%fused_computation.9 | loop fusion | flops 7077888 | bytes 9437184 | tf_op jit(solution)/shard_map/stack | solution.py:284
  79.5 0.3 slice.113.own
  80.6 2.3 %slice.110 = bf16[1,4,2,6,64,512]{5,4,3,2,1,0:T(8,128)(2,1)S(1)} slice(bf16[4,4,2,6,64,512]{5,4,3,2,1,0:T(8,128)(2,1)} %by_time.5), slice={[0:1], [0:4], [0:2], [0:6], [0:64], [0:512]} | slice | bytes 6291456 | tf_op jit(solution)/shard_map/slice | solution.py:78
  83.0 1.0 fusion.26
  83.9 1.5 collective-permute-start.1
  85.4 1.7 %collective-permute-start.2 = (f32[4,2,64,128]{3,2,1,0:T(8,128)}, f32[4,2,64,128]{3,2,1,0:T(8,128)}, u32[]{:S(2)}, u32[]{:S(2)}) collective-permute-start(f32[4,2,64,128]{3,2,1,0:T(8,128)} %get-tuple-element.24), channel_id=1, source_target_pairs={{0,6},{2,0},{4,2},{6,4},{1,7},{3,1},{5,3},{7,5},{8,14},{10,8},{12,... | collective-permute-start | bytes 786440 | tf_op jit(solution)/shard_map/ppermute | solution.py:246
  87.2 1.8 %collective-permute-start.3 = (f32[4,2,64,128]{3,2,1,0:T(8,128)}, f32[4,2,64,128]{3,2,1,0:T(8,128)}, u32[]{:S(2)}, u32[]{:S(2)}) collective-permute-start(f32[4,2,64,128]{3,2,1,0:T(8,128)} %get-tuple-element.25), channel_id=1, source_target_pairs={{0,4},{2,6},{4,0},{6,2},{1,5},{3,7},{5,1},{7,3},{8,12},{10,14},{12... | collective-permute-start | bytes 786440 | tf_op jit(solution)/shard_map/ppermute | solution.py:246
  89.0 0.7 slice_bitcast_fusion.after
  89.7 2.4 %choose.1 = bf16[4,8,512]{2,1,0:T(8,128)(2,1)} custom-call(s32[4]{0:T(128)} %index.1, s32[1]{0:T(128)S(6)} %copy.24.when, bf16[64,6,32,512]{3,2,1,0:T(8,128)(2,1)} %bitcast.128, bf16[128,512]{1,0:T(8,128)(2,1)} %slice_bitcast_fusion.after), custom_call_target="tpu_custom_call" | custom-call | flops 1000 | bytes 1000 | tf_op jit(solution)/shard_map/choose/pallas_call | solution.py:122
  92.1 2.5 %pad_maximum_fusion.2 = (bf16[4,1,3,64,512]{4,3,2,1,0:T(8,128)(2,1)}, bf16[4,1,3,64,512]{4,3,2,1,0:T(8,128)(2,1)S(1)}) fusion(bf16[1,2,3,192,512]{4,3,2,1,0:T(8,128)(2,1)} %bitcast.40, bf16[1,2,3,192,512]{4,3,2,1,0:T(8,128)(2,1)} %bitcast.38, bf16[1,2,3,192,512]{4,3,2,1,0:T(8,128)(2,1)} %bitcast.133, bf16[1,2,3,192,512]{4,3,2,1,0:T(8,128)(2,1)} %copy-done.2), kind=kLoop, calls=%fused_computation.34 | loop fusion | flops 6291456 | bytes 6291456 | tf_op jit(solution)/shard_map/slice | solution.py:288
  94.6 1.0 pad_maximum_fusion.1.refs_0_
  95.6 3.5 %collective-permute-done.2 = f32[4,2,64,128]{3,2,1,0:T(8,128)} collective-permute-done((f32[4,2,64,128]{3,2,1,0:T(8,128)}, f32[4,2,64,128]{3,2,1,0:T(8,128)}, u32[]{:S(2)}, u32[]{:S(2)}) %collective-permute-start.2) | collective-permute-done | bytes 262176 | tf_op jit(solution)/shard_map/ppermute | solution.py:246
  99.0 1.7 %collective-permute-done.3 = f32[4,2,64,128]{3,2,1,0:T(8,128)} collective-permute-done((f32[4,2,64,128]{3,2,1,0:T(8,128)}, f32[4,2,64,128]{3,2,1,0:T(8,128)}, u32[]{:S(2)}, u32[]{:S(2)}) %collective-permute-start.3) | collective-permute-done | bytes 262176 | tf_op jit(solution)/shard_map/ppermute | solution.py:246
  100.7 1.2 fusion.24
  101.9 0.7 copy-done.9
  102.6 0.6 slice_bitcast_fusion.2.refs_1_
  103.3 0.6 collective-permute-start.11
  103.9 0.1 copy.16
  104.0 0.2 fusion.37
  104.2 0.6 gather_fusion
  104.9 5.9 %collective-permute-done.4.refs_0_ = bf16[3,8,3,64,512]{4,3,2,1,0:T(8,128)(2,1)} collective-permute-done((bf16[3,8,3,64,512]{4,3,2,1,0:T(8,128)(2,1)}, bf16[3,8,3,64,512]{4,3,2,1,0:T(8,128)(2,1)}, u32[]{:S(2)}, u32[]{:S(2)}) %collective-permute-start.4) | collective-permute-done | bytes 4718624 | tf_op jit(solution)/shard_map/ppermute | solution.py:17
  110.8 11.8 %project.5 = f32[3,8,2,32,128]{4,3,2,1,0:T(8,128)} custom-call(bf16[3,8,3,64,512]{4,3,2,1,0:T(8,128)(2,1)} %collective-permute-done.4.refs_0_, bf16[4,8,3,128,512]{4,3,2,1,0:T(8,128)(2,1)} %bitcast.125, bf16[4,8,3,128,512]{4,3,2,1,0:T(8,128)(2,1)} %bitcast.122), custom_call_target="tpu_custom_call" | custom-call | flops 1000 | bytes 1000 | tf_op jit(solution)/shard_map/project/pallas_call | solution.py:211
  122.6 1.4 slice.116
  124.0 1.2 copy.17
  125.2 1.7 %collective-permute-start.13 = (bf16[24,32,512]{2,1,0:T(8,128)(2,1)}, bf16[24,32,512]{2,1,0:T(8,128)(2,1)}, u32[]{:S(2)}, u32[]{:S(2)}) collective-permute-start(bf16[24,32,512]{2,1,0:T(8,128)(2,1)} %hold.7), channel_id=1, source_target_pairs={{0,64},{64,0},{1,65},{65,1},{2,66},{66,2},{3,67},{67,3},{4,68},{68... | collective-permute-start | bytes 2359304 | tf_op jit(solution)/shard_map/ppermute | solution.py:17
  127.0 0.9 fusion.15
  127.9 1.9 %collective-permute-start.5 = (f32[512,128]{1,0:T(8,128)}, f32[512,128]{1,0:T(8,128)}, u32[]{:S(2)}, u32[]{:S(2)}) collective-permute-start(f32[512,128]{1,0:T(8,128)} %get-tuple-element.20), channel_id=1, source_target_pairs={{0,8},{8,16},{16,24},{24,0},{1,9},{9,17},{17,25},{25,1},{2,10},{10... | collective-permute-start | bytes 786440 | tf_op jit(solution)/shard_map/ppermute | solution.py:230
  129.8 2.1 %collective-permute-start.6 = (f32[512,128]{1,0:T(8,128)}, f32[512,128]{1,0:T(8,128)}, u32[]{:S(2)}, u32[]{:S(2)}) collective-permute-start(f32[512,128]{1,0:T(8,128)} %get-tuple-element.21), channel_id=1, source_target_pairs={{0,24},{8,0},{16,8},{24,16},{1,25},{9,1},{17,9},{25,17},{2,26},{10... | collective-permute-start | bytes 786440 | tf_op jit(solution)/shard_map/ppermute | solution.py:230
  131.9 1.9 %collective-permute-start.7 = (f32[512,128]{1,0:T(8,128)}, f32[512,128]{1,0:T(8,128)}, u32[]{:S(2)}, u32[]{:S(2)}) collective-permute-start(f32[512,128]{1,0:T(8,128)} %get-tuple-element.22), channel_id=1, source_target_pairs={{0,16},{8,24},{16,0},{24,8},{1,17},{9,25},{17,1},{25,9},{2,18},{10... | collective-permute-start | bytes 786440 | tf_op jit(solution)/shard_map/ppermute | solution.py:230
  133.9 0.8 fusion.36
  134.6 0.3 collective-permute-start.19
  134.9 2.9 %project_pieces.2.refs_1_.refs_0_ = f32[2,32,128]{2,1,0:T(8,128)S(1)} custom-call(bf16[25,32,512]{2,1,0:T(8,128)(2,1)} %collective-permute-done.11.col, bf16[4,2,3,128,512]{4,3,2,1,0:T(8,128)(2,1)S(1)} %slice.113.own, bf16[4,2,3,128,512]{4,3,2,1,0:T(8,128)(2,1)} %collective-permute-done.12.other), custom_call_target="tpu_custom_call" | custom-call | flops 1000 | bytes 1000 | tf_op jit(solution)/shard_map/project_pieces/pallas_call | solution.py:188
  137.8 0.6 copy-done
  138.4 6.1 %collective-permute-done.7.refs_0_ = f32[512,128]{1,0:T(8,128)} collective-permute-done((f32[512,128]{1,0:T(8,128)}, f32[512,128]{1,0:T(8,128)}, u32[]{:S(2)}, u32[]{:S(2)}) %collective-permute-start.7) | collective-permute-done | bytes 262176 | tf_op jit(solution)/shard_map/ppermute | solution.py:230
  144.5 1.2 fusion.13
  145.8 2.9 %project_pieces.3 = f32[2,32,128]{2,1,0:T(8,128)S(1)} custom-call(bf16[24,32,512]{2,1,0:T(8,128)(2,1)} %collective-permute-done.13.col, bf16[4,2,3,128,512]{4,3,2,1,0:T(8,128)(2,1)S(1)} %slice.113.own, bf16[4,2,3,128,512]{4,3,2,1,0:T(8,128)(2,1)} %collective-permute-done.12.other, f32[2,32,128]{2,1,0:T(8,128)S(1)} %copy-done.1), custom_call_target="tpu_custom_call" | custom-call | flops 1000 | bytes 1000 | tf_op jit(solution)/shard_map/project_pieces/pallas_call | solution.py:188
  148.8 1.6 collective-permute-start.14
  150.3 2.7 %collective-permute-start.16 = (f32[2,64,128]{2,1,0:T(8,128)S(1)}, f32[2,64,128]{2,1,0:T(8,128)S(1)}, u32[]{:S(2)}, u32[]{:S(2)}) collective-permute-start(f32[2,64,128]{2,1,0:T(8,128)S(1)} %get-tuple-element.27), channel_id=1, source_target_pairs={{0,4},{2,6},{4,0},{6,2},{1,5},{3,7},{5,1},{7,3},{8,12},{10,14},{12... | collective-permute-start | bytes 196616 | tf_op jit(solution)/shard_map/ppermute | solution.py:246
  153.0 1.4 collective-permute-start.15
  154.5 1.6 collective-permute-done.16
  156.1 1.2 collective-permute-done.15
  157.3 3.0 %collective-permute-start.17 = (f32[128,128]{1,0:T(8,128)S(1)}, f32[128,128]{1,0:T(8,128)S(1)}, u32[]{:S(2)}, u32[]{:S(2)}) collective-permute-start(f32[128,128]{1,0:T(8,128)S(1)} %fusion.30), channel_id=1, source_target_pairs={{0,1},{1,0},{2,3},{3,2},{4,5},{5,4},{6,7},{7,6},{8,9},{9,8},{10,11... | collective-permute-start | bytes 196616 | tf_op jit(solution)/shard_map/ppermute | solution.py:17
  160.3 0.7 broadcast_select_fusion
  161.1 2.1 %collective-permute-done.17 = f32[128,128]{1,0:T(8,128)S(1)} collective-permute-done((f32[128,128]{1,0:T(8,128)S(1)}, f32[128,128]{1,0:T(8,128)S(1)}, u32[]{:S(2)}, u32[]{:S(2)}) %collective-permute-start.17) | collective-permute-done | bytes 65568 | tf_op jit(solution)/shard_map/ppermute | solution.py:17
  163.3 1.2 collective-permute-done.18
  164.7 0.2 select_reduce_fusion
  165.0 0.1 copy.18
  165.1 0.7 copy.19
  (57 shorter events, 0.8 us)
Async XLA Ops:
  0.6 25.4 %collective-permute-start = (bf16[64,6,32,512]{3,2,1,0:T(8,128)(2,1)}, bf16[64,6,32,512]{3,2,1,0:T(8,128)(2,1)}, u32[]{:S(2)}, u32[]{:S(2)}) collective-permute-start(bf16[64,6,32,512]{3,2,1,0:T(8,128)(2,1)} %bitcast.126), channel_id=1, source_target_pairs={{0,32},{32,0},{1,33},{33,1},{2,34},{34,2},{3,35},{35,3},{4,36},{36... | collective-permute-start | bytes 37748744 | tf_op jit(solution)/shard_map/ppermute | solution.py:17
  5.8 11.1 %copy-start.6 = (bf16[1,4,2,6,32,512]{5,4,3,2,1,0:T(8,128)(2,1)S(1)}, bf16[1,4,2,6,32,512]{5,4,3,2,1,0:T(8,128)(2,1)}, u32[]{:S(2)}) copy-start(bf16[1,4,2,6,32,512]{5,4,3,2,1,0:T(8,128)(2,1)} %get-tuple-element.8) | copy-start | bytes 4718596
  5.8 105.0 %collective-permute-start.4 = (bf16[3,8,3,64,512]{4,3,2,1,0:T(8,128)(2,1)}, bf16[3,8,3,64,512]{4,3,2,1,0:T(8,128)(2,1)}, u32[]{:S(2)}, u32[]{:S(2)}) collective-permute-start(bf16[3,8,3,64,512]{4,3,2,1,0:T(8,128)(2,1)} %bitcast.129), channel_id=1, source_target_pairs={{0,64},{64,0},{1,65},{65,1},{2,66},{66,2},{3,67},{67,3},{4,68},{68... | collective-permute-start | bytes 14155784 | tf_op jit(solution)/shard_map/ppermute | solution.py:17
  20.1 57.2 %copy-start.2 = (bf16[1,2,3,192,512]{4,3,2,1,0:T(8,128)(2,1)}, bf16[1,2,3,192,512]{4,3,2,1,0:T(8,128)(2,1)S(1)}, u32[]{:S(2)}) copy-start(bf16[1,2,3,192,512]{4,3,2,1,0:T(8,128)(2,1)S(1)} %get-tuple-element.16) | copy-start | bytes 3538948
  20.1 35.0 %collective-permute-start.8 = (bf16[2,3,192,512]{3,2,1,0:T(8,128)(2,1)}, bf16[2,3,192,512]{3,2,1,0:T(8,128)(2,1)S(1)}, u32[]{:S(2)}, u32[]{:S(2)}) collective-permute-start(bf16[2,3,192,512]{3,2,1,0:T(8,128)(2,1)} %get-tuple-element.17), channel_id=1, source_target_pairs={{0,8},{8,16},{16,24},{24,0},{1,9},{9,17},{17,25},{25,1},{2,10},{10... | collective-permute-start | bytes 3538952 | tf_op jit(solution)/shard_map/ppermute | solution.py:230
  22.0 53.4 %collective-permute-start.9 = (bf16[2,3,192,512]{3,2,1,0:T(8,128)(2,1)}, bf16[2,3,192,512]{3,2,1,0:T(8,128)(2,1)}, u32[]{:S(2)}, u32[]{:S(2)}) collective-permute-start(bf16[2,3,192,512]{3,2,1,0:T(8,128)(2,1)} %get-tuple-element.18), channel_id=1, source_target_pairs={{0,24},{8,0},{16,8},{24,16},{1,25},{9,1},{17,9},{25,17},{2,26},{10... | collective-permute-start | bytes 3538952 | tf_op jit(solution)/shard_map/ppermute | solution.py:230
  24.2 53.0 %collective-permute-start.10 = (bf16[2,3,192,512]{3,2,1,0:T(8,128)(2,1)}, bf16[2,3,192,512]{3,2,1,0:T(8,128)(2,1)}, u32[]{:S(2)}, u32[]{:S(2)}) collective-permute-start(bf16[2,3,192,512]{3,2,1,0:T(8,128)(2,1)} %get-tuple-element.19), channel_id=1, source_target_pairs={{0,16},{8,24},{16,0},{24,8},{1,17},{9,25},{17,1},{25,9},{2,18},{10... | collective-permute-start | bytes 3538952 | tf_op jit(solution)/shard_map/ppermute | solution.py:230
  55.1 1.0 copy-start.3
  79.8 54.8 %collective-permute-start.12 = (bf16[4,2,3,128,512]{4,3,2,1,0:T(8,128)(2,1)S(1)}, bf16[4,2,3,128,512]{4,3,2,1,0:T(8,128)(2,1)}, u32[]{:S(2)}, u32[]{:S(2)}) collective-permute-start(bf16[4,2,3,128,512]{4,3,2,1,0:T(8,128)(2,1)S(1)} %slice.113.own), channel_id=1, source_target_pairs={{0,32},{32,0},{1,33},{33,1},{2,34},{34,2},{3,35},{35,3},{4,36},{36... | collective-permute-start | bytes 9437192 | tf_op jit(solution)/shard_map/ppermute | solution.py:17
  80.6 2.3 %copy-start.4 = (f32[3,8,2,32,128]{4,3,2,1,0:T(8,128)S(1)}, f32[3,8,2,32,128]{4,3,2,1,0:T(8,128)}, u32[]{:S(2)}) copy-start(f32[3,8,2,32,128]{4,3,2,1,0:T(8,128)} %project.3) | copy-start | bytes 2359300
  80.6 2.3 %copy-start.7 = (f32[1,8,2,32,128]{4,3,2,1,0:T(8,128)S(1)}, f32[1,8,2,32,128]{4,3,2,1,0:T(8,128)}, u32[]{:S(2)}) copy-start(f32[1,8,2,32,128]{4,3,2,1,0:T(8,128)} %project.4) | copy-start | bytes 786436
  83.9 11.7 %collective-permute-start.1 = (f32[4,2,64,128]{3,2,1,0:T(8,128)}, f32[4,2,64,128]{3,2,1,0:T(8,128)}, u32[]{:S(2)}, u32[]{:S(2)}) collective-permute-start(f32[4,2,64,128]{3,2,1,0:T(8,128)} %get-tuple-element.23), channel_id=1, source_target_pairs={{0,2},{2,4},{4,6},{6,0},{1,3},{3,5},{5,7},{7,1},{8,10},{10,12},{12... | collective-permute-start | bytes 786440 | tf_op jit(solution)/shard_map/ppermute | solution.py:246
  85.4 13.6 %collective-permute-start.2 = (f32[4,2,64,128]{3,2,1,0:T(8,128)}, f32[4,2,64,128]{3,2,1,0:T(8,128)}, u32[]{:S(2)}, u32[]{:S(2)}) collective-permute-start(f32[4,2,64,128]{3,2,1,0:T(8,128)} %get-tuple-element.24), channel_id=1, source_target_pairs={{0,6},{2,0},{4,2},{6,4},{1,7},{3,1},{5,3},{7,5},{8,14},{10,8},{12,... | collective-permute-start | bytes 786440 | tf_op jit(solution)/shard_map/ppermute | solution.py:246
  87.2 13.6 %collective-permute-start.3 = (f32[4,2,64,128]{3,2,1,0:T(8,128)}, f32[4,2,64,128]{3,2,1,0:T(8,128)}, u32[]{:S(2)}, u32[]{:S(2)}) collective-permute-start(f32[4,2,64,128]{3,2,1,0:T(8,128)} %get-tuple-element.25), channel_id=1, source_target_pairs={{0,4},{2,6},{4,0},{6,2},{1,5},{3,7},{5,1},{7,3},{8,12},{10,14},{12... | collective-permute-start | bytes 786440 | tf_op jit(solution)/shard_map/ppermute | solution.py:246
  92.1 2.5 %copy-start.11 = (bf16[4,8,512]{2,1,0:T(8,128)(2,1)S(1)}, bf16[4,8,512]{2,1,0:T(8,128)(2,1)}, u32[]{:S(2)}) copy-start(bf16[4,8,512]{2,1,0:T(8,128)(2,1)} %choose.1) | copy-start | bytes 98308
  94.6 6.2 %copy-start.8 = (f32[1,8,2,32,128]{4,3,2,1,0:T(8,128)S(1)}, f32[1,8,2,32,128]{4,3,2,1,0:T(8,128)}, u32[]{:S(2)}) copy-start(f32[1,8,2,32,128]{4,3,2,1,0:T(8,128)} %project.4) | copy-start | bytes 786436
  95.6 8.3 %copy-start.12 = (s32[4,4]{1,0:T(4,128)S(1)}, s32[4,4]{1,0:T(4,128)}, u32[]{:S(2)}) copy-start(s32[4,4]{1,0:T(4,128)} %param.9) | copy-start | bytes 196
  101.9 0.7 copy-start.9
  103.3 28.7 %collective-permute-start.11 = (bf16[25,32,512]{2,1,0:T(8,128)(2,1)}, bf16[25,32,512]{2,1,0:T(8,128)(2,1)}, u32[]{:S(2)}, u32[]{:S(2)}) collective-permute-start(bf16[25,32,512]{2,1,0:T(8,128)(2,1)} %hold.5), channel_id=1, source_target_pairs={{0,64},{64,0},{1,65},{65,1},{2,66},{66,2},{3,67},{67,3},{4,68},{68... | collective-permute-start | bytes 2457608 | tf_op jit(solution)/shard_map/ppermute | solution.py:17
  124.0 3.0 %copy-start.10 = (f32[4,2,64,128]{3,2,1,0:T(8,128)S(1)}, f32[4,2,64,128]{3,2,1,0:T(8,128)}, u32[]{:S(2)}) copy-start(f32[4,2,64,128]{3,2,1,0:T(8,128)} %copy-done.9) | copy-start | bytes 786436
  125.2 1.8 %copy-start.5 = (f32[4,3,2,64,128]{4,3,2,1,0:T(8,128)}, f32[4,3,2,64,128]{4,3,2,1,0:T(8,128)S(1)}, u32[]{:S(2)}) copy-start(f32[4,3,2,64,128]{4,3,2,1,0:T(8,128)S(1)} %copy.17) | copy-start | bytes 2359300
  125.2 20.6 %collective-permute-start.13 = (bf16[24,32,512]{2,1,0:T(8,128)(2,1)}, bf16[24,32,512]{2,1,0:T(8,128)(2,1)}, u32[]{:S(2)}, u32[]{:S(2)}) collective-permute-start(bf16[24,32,512]{2,1,0:T(8,128)(2,1)} %hold.7), channel_id=1, source_target_pairs={{0,64},{64,0},{1,65},{65,1},{2,66},{66,2},{3,67},{67,3},{4,68},{68... | collective-permute-start | bytes 2359304 | tf_op jit(solution)/shard_map/ppermute | solution.py:17
  127.9 16.7 %collective-permute-start.5 = (f32[512,128]{1,0:T(8,128)}, f32[512,128]{1,0:T(8,128)}, u32[]{:S(2)}, u32[]{:S(2)}) collective-permute-start(f32[512,128]{1,0:T(8,128)} %get-tuple-element.20), channel_id=1, source_target_pairs={{0,8},{8,16},{16,24},{24,0},{1,9},{9,17},{17,25},{25,1},{2,10},{10... | collective-permute-start | bytes 786440 | tf_op jit(solution)/shard_map/ppermute | solution.py:230
  129.8 14.7 %collective-permute-start.6 = (f32[512,128]{1,0:T(8,128)}, f32[512,128]{1,0:T(8,128)}, u32[]{:S(2)}, u32[]{:S(2)}) collective-permute-start(f32[512,128]{1,0:T(8,128)} %get-tuple-element.21), channel_id=1, source_target_pairs={{0,24},{8,0},{16,8},{24,16},{1,25},{9,1},{17,9},{25,17},{2,26},{10... | collective-permute-start | bytes 786440 | tf_op jit(solution)/shard_map/ppermute | solution.py:230
  131.9 12.6 %collective-permute-start.7 = (f32[512,128]{1,0:T(8,128)}, f32[512,128]{1,0:T(8,128)}, u32[]{:S(2)}, u32[]{:S(2)}) collective-permute-start(f32[512,128]{1,0:T(8,128)} %get-tuple-element.22), channel_id=1, source_target_pairs={{0,16},{8,24},{16,0},{24,8},{1,17},{9,25},{17,1},{25,9},{2,18},{10... | collective-permute-start | bytes 786440 | tf_op jit(solution)/shard_map/ppermute | solution.py:230
  134.6 19.9 %collective-permute-start.19 = (bf16[32,512]{1,0:T(8,128)(2,1)S(1)}, bf16[32,512]{1,0:T(8,128)(2,1)S(1)}, u32[]{:S(2)}, u32[]{:S(2)}) collective-permute-start(bf16[32,512]{1,0:T(8,128)(2,1)S(1)} %fusion.36), channel_id=1, source_target_pairs={{0,32},{32,0},{1,33},{33,1},{2,34},{34,2},{3,35},{35,3},{4,36},{36... | collective-permute-start | bytes 98312 | tf_op jit(solution)/shard_map/ppermute | solution.py:17
  137.8 0.6 copy-start
  144.5 1.3 copy-start.1
  148.8 5.7 %collective-permute-start.14 = (f32[2,64,128]{2,1,0:T(8,128)S(1)}, f32[2,64,128]{2,1,0:T(8,128)S(1)}, u32[]{:S(2)}, u32[]{:S(2)}) collective-permute-start(f32[2,64,128]{2,1,0:T(8,128)S(1)} %get-tuple-element.26), channel_id=1, source_target_pairs={{0,2},{2,4},{4,6},{6,0},{1,3},{3,5},{5,7},{7,1},{8,10},{10,12},{12... | collective-permute-start | bytes 196616 | tf_op jit(solution)/shard_map/ppermute | solution.py:246
  150.3 5.8 %collective-permute-start.16 = (f32[2,64,128]{2,1,0:T(8,128)S(1)}, f32[2,64,128]{2,1,0:T(8,128)S(1)}, u32[]{:S(2)}, u32[]{:S(2)}) collective-permute-start(f32[2,64,128]{2,1,0:T(8,128)S(1)} %get-tuple-element.27), channel_id=1, source_target_pairs={{0,4},{2,6},{4,0},{6,2},{1,5},{3,7},{5,1},{7,3},{8,12},{10,14},{12... | collective-permute-start | bytes 196616 | tf_op jit(solution)/shard_map/ppermute | solution.py:246
  153.0 4.3 %collective-permute-start.15 = (f32[2,64,128]{2,1,0:T(8,128)S(1)}, f32[2,64,128]{2,1,0:T(8,128)S(1)}, u32[]{:S(2)}, u32[]{:S(2)}) collective-permute-start(f32[2,64,128]{2,1,0:T(8,128)S(1)} %get-tuple-element.28), channel_id=1, source_target_pairs={{0,6},{2,0},{4,2},{6,4},{1,7},{3,1},{5,3},{7,5},{8,14},{10,8},{12,... | collective-permute-start | bytes 196616 | tf_op jit(solution)/shard_map/ppermute | solution.py:246
  157.3 5.8 %collective-permute-start.17 = (f32[128,128]{1,0:T(8,128)S(1)}, f32[128,128]{1,0:T(8,128)S(1)}, u32[]{:S(2)}, u32[]{:S(2)}) collective-permute-start(f32[128,128]{1,0:T(8,128)S(1)} %fusion.30), channel_id=1, source_target_pairs={{0,1},{1,0},{2,3},{3,2},{4,5},{5,4},{6,7},{7,6},{8,9},{9,8},{10,11... | collective-permute-start | bytes 196616 | tf_op jit(solution)/shard_map/ppermute | solution.py:17
  163.2 1.3 collective-permute-start.18

commit v15 on v14

--- a/solution.py
+++ b/solution.py
@@ -181,9 +181,10 @@
     out[0], out[1] = real_imag(total, 0, out.shape[1])
 
 
-def project_pieces(cols, own, other, y, *after):
-    count, _, *rest = own.shape
-    vecs = pl.BlockSpec((count, 1, *rest), lambda i: (0, y, 0, 0, 0))
+def project_pieces(cols, own, other, y, first, *after):
+    _, _, *rest = own.shape
+    count = cols.shape[0] // (2 * rest[0])
+    vecs = pl.BlockSpec((count, 1, *rest), lambda i: (first // count, y, 0, 0, 0))
     rows = pl.BlockSpec((2 * count * rest[0], *cols.shape[1:]), lambda i: (0, 0, 0))
     return pl.pallas_call(
         pieces_kernel,
@@ -288,25 +289,28 @@
     spread_s = [spread_s[:, y].reshape(-1, count, sites) for y in range(2)]
 
     first = sum_x(jnp.concatenate(first))
-    got_a = swap(hold(jnp.concatenate([spread_s[0], lines]), mark(first)), "yl")
+    cut = spread_s[1].shape[0] * 3 // 4
+    part_a = hold(jnp.concatenate([spread_s[0], lines]), mark(first))
+    part_b = hold(spread_s[1][:cut], mark(part_a))
+    got_a, got_b = swap(part_a, "yl"), swap(part_b, "yl")
     late = against([got], 0)
-    got_b = swap(hold(spread_s[1], mark(late)), "yl")
-    last = [project_pieces(got_a, spread_v, spread_w, 0)]
-    last.append(project_pieces(got_b, spread_v, spread_w, 1, last[0]))
+    last_a = project_pieces(got_a, spread_v, spread_w, 0, 0)
+    got_c = swap(hold(spread_s[1][cut:], mark(part_b)), "yl")
+    last_b = project_pieces(got_b, spread_v, spread_w, 1, 0, last_a)
+    lines = hold(lines[0] + got_a[-1], mark(last_b))
+    lines = lines + swap(lines, "c")
     late = jnp.swapaxes(late, 0, 1).reshape(4, -1, 2 * owned)
     late = share_z(jnp.concatenate([first.reshape(4, -1, 2 * owned), late], axis=1))
-    late = late[0] + late[1] + late[2] + hold(late[3], last[0])
+    late = late[0] + late[1] + late[2] + hold(late[3], last_b)
+    last_c = project_pieces(got_c, spread_v, spread_w, 1, 3, last_b, late[:8])
     cut = 4 * count
     first = late[:cut].reshape(2, -1, 2 * owned)
     late = late[cut:].reshape(6, -1, 2 * owned)
-    late = jnp.concatenate([late, *(v.reshape(1, -1, 2 * owned) for v in last)])
+    late = jnp.concatenate([late, *(v.reshape(1, -1, 2 * owned) for v in (last_a, last_b + last_c))])
     late = sum_x(late.reshape(4, 2, -1, 2 * owned))
 
     here = sum_yh(jnp.concatenate([first, late], axis=1))
     there = swap(here, "c")
-
-    lines = lines[0] + got_a[-1]
-    lines = lines + swap(lines, "c")
 
     def assemble(sums, half):
         sums = sums[:, half * owned : (half + 1) * owned].reshape(2, 2, count, owned)

time: 167 us -> 169 us (1.012)
  waiting for transfers between devices: 44.4 us -> 33.4 us
  local copies, waits for them, and re-layouts: 13.4 us -> 20.2 us
  other arithmetic: 15.5 us -> 18.7 us
    ppermute x6, waiting for transfers between devices: 27.2 us -> 20.5 us  [share_z(): lax.ppermute(pick(slabs, (me + k) % 4), 'z', [(i, (i + k) % 4) for i in r...]
    ppermute x8 -> x9, waiting for transfers between devices: 9.23 us -> 4.53 us  [swap(): return lax.ppermute(value, axis, SWAP)]
    squeeze x3 -> x4, other arithmetic: 1.9 us -> 5.47 us  [pick(): return lax.dynamic_index_in_dim(value, index, 0, keepdims=False)]
    squeeze x2 -> x5, local copies, waits for them, and re-layouts: 1.28 us -> 4.63 us  [mark(): value = value[0]]
    concatenate x3 -> x2, other arithmetic: 4.23 us -> 1.9 us  [the longest x1 0.95 us: local(): part_a = hold(jnp.concatenate([spread_s[0], lines]), mark(first))]
    unnamed x28 -> x30, local copies, waits for them, and re-layouts: 3.17 us -> 5.11 us
    another operation x1 -> x2, other arithmetic: 2.27 us -> 3.99 us  [local(): spread = jnp.stack(spread)]
    slice x4 -> x3, local copies, waits for them, and re-layouts: 6.44 us -> 5.07 us  [mark(): value = value[0]]
  transfers between devices with their start and end apart: 20 -> 21, of which waited for: 10 -> 8; matrix products, arithmetic and copies ran while one was open for 15% -> 20% of each run, Pallas kernels for 37% -> 36%
where the time goes in v15:
time: 169 us; the launch traced here: 167 us
  Pallas kernels  61.7 us (37%)
  waiting for transfers between devices  33.4 us (20%)
  starting transfers between devices  31.5 us (19%)
  local copies, waits for them, and re-layouts  20.2 us (12%)
  other arithmetic  18.7 us (11%)
  between operations  1.72 us (1%)
    pallas_call x3, Pallas kernels, project(): pl.pallas_call(functools.partial(dot_kernel, len(cols)), grid=(size, inne...  29.8 us
    pallas_call x3, Pallas kernels, by_time(): pl.pallas_call(functools.partial(by_time_kernel, cuts), in_specs=[ANY] *...  22.7 us
    ppermute x6, waiting for transfers between devices, share_z(): lax.ppermute(pick(slabs, (me + k) % 4), 'z', [(i, (i + k) % 4) for i in r...  20.5 us
    ppermute x6, starting transfers between devices, share_z(): lax.ppermute(pick(slabs, (me + k) % 4), 'z', [(i, (i + k) % 4) for i in r...  11.7 us
    ppermute x6, starting transfers between devices, sum_x(): total = total + lax.ppermute(pick(slabs, (me + k) % 4), 'x', pairs)  10.8 us
    ppermute x9, starting transfers between devices, swap(): return lax.ppermute(value, axis, SWAP)  8.96 us
    ppermute x6, waiting for transfers between devices, sum_x(): total = total + lax.ppermute(pick(slabs, (me + k) % 4), 'x', pairs)  8.41 us
    pallas_call x3, Pallas kernels, project_pieces(): pl.pallas_call(pieces_kernel, grid=(1,), in_specs=[rows, vecs, vecs] + [A...  6.8 us
  transfers between devices with their start and end apart: 21, of which 8 were waited for; matrix products, arithmetic and copies ran while one was open for 20% of the time, Pallas kernels for 36%

profile of v15, /device:TPU:0, one launch (start us, length us, event | category | flops | bytes accessed | tf_op | source)
XLA Modules:
  0.0 167.2 jit_solution(13778032084736137669)
XLA Ops:
  0.7 5.1 %by_time.3 = (bf16[3,4,2,6,32,512]{5,4,3,2,1,0:T(8,128)(2,1)}, bf16[1,4,2,6,32,512]{5,4,3,2,1,0:T(8,128)(2,1)}) custom-call(bf16[32,6,32,512]{3,2,1,0:T(8,128)(2,1)} %bitcast.149), custom_call_target="tpu_custom_call" | custom-call | flops 1000 | bytes 1000 | tf_op jit(solution)/shard_map/by_time/pallas_call | solution.py:52
  5.8 1.7 %collective-permute-start.4 = (bf16[3,8,3,64,512]{4,3,2,1,0:T(8,128)(2,1)}, bf16[3,8,3,64,512]{4,3,2,1,0:T(8,128)(2,1)}, u32[]{:S(2)}, u32[]{:S(2)}) collective-permute-start(bf16[3,8,3,64,512]{4,3,2,1,0:T(8,128)(2,1)} %bitcast.137), channel_id=1, source_target_pairs={{0,64},{64,0},{1,65},{65,1},{2,66},{66,2},{3,67},{67,3},{4,68},{68... | collective-permute-start | bytes 14155784 | tf_op jit(solution)/shard_map/ppermute | solution.py:17
  7.5 9.3 %by_time.4 = (bf16[4,4,2,6,64,512]{5,4,3,2,1,0:T(8,128)(2,1)}, bf16[1,4,2,6,64,512]{5,4,3,2,1,0:T(8,128)(2,1)}) custom-call(bf16[64,6,32,512]{3,2,1,0:T(8,128)(2,1)} %bitcast.132, bf16[3,8,3,64,512]{4,3,2,1,0:T(8,128)(2,1)} %bitcast.138), custom_call_target="tpu_custom_call" | custom-call | flops 1000 | bytes 1000 | tf_op jit(solution)/shard_map/by_time/pallas_call | solution.py:52
  16.9 3.6 %fusion.1 = (bf16[2,3,192,512]{3,2,1,0:T(8,128)(2,1)}, bf16[1,2,3,192,512]{4,3,2,1,0:T(8,128)(2,1)}, bf16[2,3,192,512]{3,2,1,0:T(8,128)(2,1)}, bf16[2,3,192,512]{3,2,1,0:T(8,128)(2,1)}) fusion(s32[]{:T(128)S(6)} %select_n.141, bf16[4,2,3,128,512]{4,3,2,1,0:T(8,128)(2,1)} %bitcast.151, bf16[4,2,3,64,512]{4,3,2,1,0:T(8,128)(2,1)S(1)} %bitcast.148, ...), kind=kLoop, calls=%fused_computation.29 | loop fusion | flops 9437184 | bytes 9437200 | tf_op jit(solution)/shard_map/jit(dynamic_index_in_dim)/squeeze | solution.py:225
  20.5 1.9 %collective-permute-start.8 = (bf16[2,3,192,512]{3,2,1,0:T(8,128)(2,1)}, bf16[2,3,192,512]{3,2,1,0:T(8,128)(2,1)S(1)}, u32[]{:S(2)}, u32[]{:S(2)}) collective-permute-start(bf16[2,3,192,512]{3,2,1,0:T(8,128)(2,1)} %get-tuple-element.16), channel_id=1, source_target_pairs={{0,8},{8,16},{16,24},{24,0},{1,9},{9,17},{17,25},{25,1},{2,10},{10... | collective-permute-start | bytes 3538952 | tf_op jit(solution)/shard_map/ppermute | solution.py:231
  22.4 3.6 %collective-permute-start.10 = (bf16[2,3,192,512]{3,2,1,0:T(8,128)(2,1)}, bf16[2,3,192,512]{3,2,1,0:T(8,128)(2,1)}, u32[]{:S(2)}, u32[]{:S(2)}) collective-permute-start(bf16[2,3,192,512]{3,2,1,0:T(8,128)(2,1)} %get-tuple-element.14), channel_id=1, source_target_pairs={{0,16},{8,24},{16,0},{24,8},{1,17},{9,25},{17,1},{25,9},{2,18},{10... | collective-permute-start | bytes 3538952 | tf_op jit(solution)/shard_map/ppermute | solution.py:231
  26.0 1.0 collective-permute-start.9
  27.0 8.4 %by_time.5 = bf16[4,4,2,6,64,512]{5,4,3,2,1,0:T(8,128)(2,1)} custom-call(bf16[64,6,32,512]{3,2,1,0:T(8,128)(2,1)} %collective-permute-done.block), custom_call_target="tpu_custom_call" | custom-call | flops 1000 | bytes 1000 | tf_op jit(solution)/shard_map/by_time/pallas_call | solution.py:52
  35.4 11.8 %project.3 = f32[3,8,2,32,128]{4,3,2,1,0:T(8,128)} custom-call(bf16[3,8,3,64,512]{4,3,2,1,0:T(8,128)(2,1)} %bitcast.139, bf16[4,8,3,128,512]{4,3,2,1,0:T(8,128)(2,1)} %bitcast.128, bf16[4,8,3,128,512]{4,3,2,1,0:T(8,128)(2,1)} %bitcast.125), custom_call_target="tpu_custom_call" | custom-call | flops 1000 | bytes 1000 | tf_op jit(solution)/shard_map/project/pallas_call | solution.py:212
  47.2 6.2 %project.4 = f32[1,8,2,32,128]{4,3,2,1,0:T(8,128)} custom-call(bf16[1,8,3,64,512]{4,3,2,1,0:T(8,128)(2,1)} %bitcast.147, bf16[4,8,3,128,512]{4,3,2,1,0:T(8,128)(2,1)} %bitcast.129, bf16[4,8,3,128,512]{4,3,2,1,0:T(8,128)(2,1)} %bitcast.126), custom_call_target="tpu_custom_call" | custom-call | flops 1000 | bytes 1000 | tf_op jit(solution)/shard_map/project/pallas_call | solution.py:212
  53.4 1.4 slice.131
  54.8 1.4 slice.130
  56.1 1.1 copy-done.2
  57.2 20.4 %collective-permute-done.10 = bf16[2,3,192,512]{3,2,1,0:T(8,128)(2,1)} collective-permute-done((bf16[2,3,192,512]{3,2,1,0:T(8,128)(2,1)}, bf16[2,3,192,512]{3,2,1,0:T(8,128)(2,1)}, u32[]{:S(2)}, u32[]{:S(2)}) %collective-permute-start.10) | collective-permute-done | bytes 1179680 | tf_op jit(solution)/shard_map/ppermute | solution.py:231
  77.7 1.0 copy-done.3
  78.7 2.0 %pad_maximum_fusion.own = bf16[4,2,3,128,512]{4,3,2,1,0:T(8,128)(2,1)S(1)} fusion(bf16[1,2,3,192,512]{4,3,2,1,0:T(8,128)(2,1)} %bitcast.41, bf16[1,2,3,192,512]{4,3,2,1,0:T(8,128)(2,1)} %bitcast.140, bf16[1,2,3,192,512]{4,3,2,1,0:T(8,128)(2,1)} %bitcast.134, bf16[1,2,3,192,512]{4,3,2,1,0:T(8,128)(2,1)} %get-tuple-element.15), kind=kLoop, calls=%fused_computation.9 | loop fusion | flops 12582912 | bytes 7864320 | tf_op jit(solution)/shard_map/stack | solution.py:285
  82.3 2.3 %slice.132 = bf16[1,4,2,6,64,512]{5,4,3,2,1,0:T(8,128)(2,1)S(1)} slice(bf16[4,4,2,6,64,512]{5,4,3,2,1,0:T(8,128)(2,1)} %by_time.5), slice={[0:1], [0:4], [0:2], [0:6], [0:64], [0:512]} | slice | bytes 6291456 | tf_op jit(solution)/shard_map/slice | solution.py:78
  84.6 0.9 fusion.26
  85.6 1.5 collective-permute-start.1
  87.1 1.7 %collective-permute-start.2 = (f32[4,2,64,128]{3,2,1,0:T(8,128)}, f32[4,2,64,128]{3,2,1,0:T(8,128)}, u32[]{:S(2)}, u32[]{:S(2)}) collective-permute-start(f32[4,2,64,128]{3,2,1,0:T(8,128)} %get-tuple-element.22), channel_id=1, source_target_pairs={{0,6},{2,0},{4,2},{6,4},{1,7},{3,1},{5,3},{7,5},{8,14},{10,8},{12,... | collective-permute-start | bytes 786440 | tf_op jit(solution)/shard_map/ppermute | solution.py:247
  88.8 1.8 %collective-permute-start.3 = (f32[4,2,64,128]{3,2,1,0:T(8,128)}, f32[4,2,64,128]{3,2,1,0:T(8,128)}, u32[]{:S(2)}, u32[]{:S(2)}) collective-permute-start(f32[4,2,64,128]{3,2,1,0:T(8,128)} %get-tuple-element.23), channel_id=1, source_target_pairs={{0,4},{2,6},{4,0},{6,2},{1,5},{3,7},{5,1},{7,3},{8,12},{10,14},{12... | collective-permute-start | bytes 786440 | tf_op jit(solution)/shard_map/ppermute | solution.py:247
  90.6 0.7 slice_bitcast_fusion.after
  91.3 2.4 %choose.1 = bf16[4,8,512]{2,1,0:T(8,128)(2,1)} custom-call(s32[4]{0:T(128)} %index.1, s32[1]{0:T(128)S(6)} %copy.28.when, bf16[64,6,32,512]{3,2,1,0:T(8,128)(2,1)} %bitcast.133, bf16[128,512]{1,0:T(8,128)(2,1)} %slice_bitcast_fusion.after), custom_call_target="tpu_custom_call" | custom-call | flops 1000 | bytes 1000 | tf_op jit(solution)/shard_map/choose/pallas_call | solution.py:122
  93.7 1.3 pad_maximum_fusion.4
  95.1 1.0 pad_maximum_fusion.3.refs_0_
  96.0 4.6 %collective-permute-done.2 = f32[4,2,64,128]{3,2,1,0:T(8,128)} collective-permute-done((f32[4,2,64,128]{3,2,1,0:T(8,128)}, f32[4,2,64,128]{3,2,1,0:T(8,128)}, u32[]{:S(2)}, u32[]{:S(2)}) %collective-permute-start.2) | collective-permute-done | bytes 262176 | tf_op jit(solution)/shard_map/ppermute | solution.py:247
  100.7 1.7 %collective-permute-done.3 = f32[4,2,64,128]{3,2,1,0:T(8,128)} collective-permute-done((f32[4,2,64,128]{3,2,1,0:T(8,128)}, f32[4,2,64,128]{3,2,1,0:T(8,128)}, u32[]{:S(2)}, u32[]{:S(2)}) %collective-permute-start.3) | collective-permute-done | bytes 262176 | tf_op jit(solution)/shard_map/ppermute | solution.py:247
  102.4 1.2 fusion.24
  103.6 0.7 copy-done.9
  104.3 0.6 slice_bitcast_fusion.4.refs_1_
  105.7 2.0 %pad_maximum_fusion.5 = bf16[3,1,3,64,512]{4,3,2,1,0:T(8,128)(2,1)} fusion(bf16[1,2,3,192,512]{4,3,2,1,0:T(8,128)(2,1)} %bitcast.142, bf16[1,2,3,192,512]{4,3,2,1,0:T(8,128)(2,1)} %bitcast.136, bf16[1,2,3,192,512]{4,3,2,1,0:T(8,128)(2,1)} %get-tuple-element.15), kind=kLoop, calls=%fused_computation.37 | loop fusion | flops 1769472 | bytes 4128768 | tf_op jit(solution)/shard_map/stack | solution.py:285
  107.7 1.4 slice_bitcast_fusion.3.refs_1_
  109.1 1.4 collective-permute-start.11
  110.6 1.6 slice.138
  112.2 11.8 %project.5 = f32[3,8,2,32,128]{4,3,2,1,0:T(8,128)} custom-call(bf16[3,8,3,64,512]{4,3,2,1,0:T(8,128)(2,1)} %collective-permute-done.4.refs_0_, bf16[4,8,3,128,512]{4,3,2,1,0:T(8,128)(2,1)} %bitcast.130, bf16[4,8,3,128,512]{4,3,2,1,0:T(8,128)(2,1)} %bitcast.127), custom_call_target="tpu_custom_call" | custom-call | flops 1000 | bytes 1000 | tf_op jit(solution)/shard_map/project/pallas_call | solution.py:212
  124.1 1.2 copy.19
  125.3 0.9 copy-done.5
  126.2 0.9 fusion.15
  127.1 1.1 collective-permute-start.5
  128.2 2.1 %collective-permute-start.6 = (f32[512,128]{1,0:T(8,128)}, f32[512,128]{1,0:T(8,128)}, u32[]{:S(2)}, u32[]{:S(2)}) collective-permute-start(f32[512,128]{1,0:T(8,128)} %get-tuple-element.19), channel_id=1, source_target_pairs={{0,24},{8,0},{16,8},{24,16},{1,25},{9,1},{17,9},{25,17},{2,26},{10... | collective-permute-start | bytes 786440 | tf_op jit(solution)/shard_map/ppermute | solution.py:231
  130.3 2.0 %collective-permute-start.7 = (f32[512,128]{1,0:T(8,128)}, f32[512,128]{1,0:T(8,128)}, u32[]{:S(2)}, u32[]{:S(2)}) collective-permute-start(f32[512,128]{1,0:T(8,128)} %get-tuple-element.20), channel_id=1, source_target_pairs={{0,16},{8,24},{16,0},{24,8},{1,17},{9,25},{17,1},{25,9},{2,18},{10... | collective-permute-start | bytes 786440 | tf_op jit(solution)/shard_map/ppermute | solution.py:231
  132.3 1.4 slice_bitcast_fusion.2.refs_1_
  133.7 1.4 fusion.36.refs_0_
  135.1 1.6 collective-permute-start.14
  136.6 2.9 %project_pieces.3.refs_0_ = f32[2,32,128]{2,1,0:T(8,128)S(1)} custom-call(bf16[25,32,512]{2,1,0:T(8,128)(2,1)} %collective-permute-done.13.col, bf16[4,2,3,128,512]{4,3,2,1,0:T(8,128)(2,1)S(1)} %pad_maximum_fusion.own, bf16[4,2,3,128,512]{4,3,2,1,0:T(8,128)(2,1)} %collective-permute-done.12.other), custom_call_target="tpu_custom_call" | custom-call | flops 1000 | bytes 1000 | tf_op jit(solution)/shard_map/project_pieces/pallas_call | solution.py:189
  139.5 1.5 collective-permute-done.11.col
  141.0 2.4 %project_pieces.4.refs_1_.refs_0_ = f32[2,32,128]{2,1,0:T(8,128)S(1)} custom-call(bf16[18,32,512]{2,1,0:T(8,128)(2,1)} %collective-permute-done.11.col, bf16[4,2,3,128,512]{4,3,2,1,0:T(8,128)(2,1)S(1)} %pad_maximum_fusion.own, bf16[4,2,3,128,512]{4,3,2,1,0:T(8,128)(2,1)} %collective-permute-done.12.other, f32[2,32,128]{2,1,0:T(8,128)S(1)} %project_pieces.3.refs_0_), custom_call_target="tpu_custom_call" | custom-call | flops 1000 | bytes 1000 | tf_op jit(solution)/shard_map/project_pieces/pallas_call | solution.py:189
  143.4 0.6 copy-done
  144.1 1.2 fusion.13
  145.3 0.7 slice.137
  146.1 0.6 slice_bitcast_fusion.5.refs_1_
  146.7 1.5 project_pieces.5
  148.3 0.9 pad_maximum_fusion.7
  149.3 0.8 slice.136
  150.1 1.6 collective-permute-start.15
  151.7 2.7 %collective-permute-start.17 = (f32[2,64,128]{2,1,0:T(8,128)S(1)}, f32[2,64,128]{2,1,0:T(8,128)S(1)}, u32[]{:S(2)}, u32[]{:S(2)}) collective-permute-start(f32[2,64,128]{2,1,0:T(8,128)S(1)} %get-tuple-element.25), channel_id=1, source_target_pairs={{0,4},{2,6},{4,0},{6,2},{1,5},{3,7},{5,1},{7,3},{8,12},{10,14},{12... | collective-permute-start | bytes 196616 | tf_op jit(solution)/shard_map/ppermute | solution.py:247
  154.4 1.4 collective-permute-start.16
  155.8 0.8 add_bitcast_fusion
  156.6 1.7 collective-permute-done.17
  158.7 3.3 %collective-permute-start.18 = (f32[128,128]{1,0:T(8,128)S(1)}, f32[128,128]{1,0:T(8,128)S(1)}, u32[]{:S(2)}, u32[]{:S(2)}) collective-permute-start(f32[128,128]{1,0:T(8,128)S(1)} %fusion.30), channel_id=1, source_target_pairs={{0,1},{1,0},{2,3},{3,2},{4,5},{5,4},{6,7},{7,6},{8,9},{9,8},{10,11... | collective-permute-start | bytes 196616 | tf_op jit(solution)/shard_map/ppermute | solution.py:17
  162.0 0.7 broadcast_select_fusion
  162.7 1.8 %collective-permute-done.18 = f32[128,128]{1,0:T(8,128)S(1)} collective-permute-done((f32[128,128]{1,0:T(8,128)S(1)}, f32[128,128]{1,0:T(8,128)S(1)}, u32[]{:S(2)}, u32[]{:S(2)}) %collective-permute-start.18) | collective-permute-done | bytes 65568 | tf_op jit(solution)/shard_map/ppermute | solution.py:17
  164.7 1.2 collective-permute-done.19
  166.4 0.7 copy.21
  (69 shorter events, 3.1 us)
Async XLA Ops:
  0.6 26.4 %collective-permute-start = (bf16[64,6,32,512]{3,2,1,0:T(8,128)(2,1)}, bf16[64,6,32,512]{3,2,1,0:T(8,128)(2,1)}, u32[]{:S(2)}, u32[]{:S(2)}) collective-permute-start(bf16[64,6,32,512]{3,2,1,0:T(8,128)(2,1)} %bitcast.131), channel_id=1, source_target_pairs={{0,32},{32,0},{1,33},{33,1},{2,34},{34,2},{3,35},{35,3},{4,36},{36... | collective-permute-start | bytes 37748744 | tf_op jit(solution)/shard_map/ppermute | solution.py:17
  5.8 11.1 %copy-start.6 = (bf16[1,4,2,6,32,512]{5,4,3,2,1,0:T(8,128)(2,1)S(1)}, bf16[1,4,2,6,32,512]{5,4,3,2,1,0:T(8,128)(2,1)}, u32[]{:S(2)}) copy-start(bf16[1,4,2,6,32,512]{5,4,3,2,1,0:T(8,128)(2,1)} %get-tuple-element.8) | copy-start | bytes 4718596
  5.8 106.4 %collective-permute-start.4 = (bf16[3,8,3,64,512]{4,3,2,1,0:T(8,128)(2,1)}, bf16[3,8,3,64,512]{4,3,2,1,0:T(8,128)(2,1)}, u32[]{:S(2)}, u32[]{:S(2)}) collective-permute-start(bf16[3,8,3,64,512]{4,3,2,1,0:T(8,128)(2,1)} %bitcast.137), channel_id=1, source_target_pairs={{0,64},{64,0},{1,65},{65,1},{2,66},{66,2},{3,67},{67,3},{4,68},{68... | collective-permute-start | bytes 14155784 | tf_op jit(solution)/shard_map/ppermute | solution.py:17
  20.5 35.6 %collective-permute-start.8 = (bf16[2,3,192,512]{3,2,1,0:T(8,128)(2,1)}, bf16[2,3,192,512]{3,2,1,0:T(8,128)(2,1)S(1)}, u32[]{:S(2)}, u32[]{:S(2)}) collective-permute-start(bf16[2,3,192,512]{3,2,1,0:T(8,128)(2,1)} %get-tuple-element.16), channel_id=1, source_target_pairs={{0,8},{8,16},{16,24},{24,0},{1,9},{9,17},{17,25},{25,1},{2,10},{10... | collective-permute-start | bytes 3538952 | tf_op jit(solution)/shard_map/ppermute | solution.py:231
  22.4 55.2 %collective-permute-start.10 = (bf16[2,3,192,512]{3,2,1,0:T(8,128)(2,1)}, bf16[2,3,192,512]{3,2,1,0:T(8,128)(2,1)}, u32[]{:S(2)}, u32[]{:S(2)}) collective-permute-start(bf16[2,3,192,512]{3,2,1,0:T(8,128)(2,1)} %get-tuple-element.14), channel_id=1, source_target_pairs={{0,16},{8,24},{16,0},{24,8},{1,17},{9,25},{17,1},{25,9},{2,18},{10... | collective-permute-start | bytes 3538952 | tf_op jit(solution)/shard_map/ppermute | solution.py:231
  26.0 51.7 %collective-permute-start.9 = (bf16[2,3,192,512]{3,2,1,0:T(8,128)(2,1)}, bf16[2,3,192,512]{3,2,1,0:T(8,128)(2,1)S(1)}, u32[]{:S(2)}, u32[]{:S(2)}) collective-permute-start(bf16[2,3,192,512]{3,2,1,0:T(8,128)(2,1)} %get-tuple-element.17), channel_id=1, source_target_pairs={{0,24},{8,0},{16,8},{24,16},{1,25},{9,1},{17,9},{25,17},{2,26},{10... | collective-permute-start | bytes 3538952 | tf_op jit(solution)/shard_map/ppermute | solution.py:231
  56.1 1.1 copy-start.2
  77.7 1.0 copy-start.3
  78.7 2.8 %copy-start.13 = (s32[4,4]{1,0:T(4,128)S(1)}, s32[4,4]{1,0:T(4,128)}, u32[]{:S(2)}) copy-start(s32[4,4]{1,0:T(4,128)} %param.9) | copy-start | bytes 196
  80.7 54.4 %collective-permute-start.12 = (bf16[4,2,3,128,512]{4,3,2,1,0:T(8,128)(2,1)S(1)}, bf16[4,2,3,128,512]{4,3,2,1,0:T(8,128)(2,1)}, u32[]{:S(2)}, u32[]{:S(2)}) collective-permute-start(bf16[4,2,3,128,512]{4,3,2,1,0:T(8,128)(2,1)S(1)} %pad_maximum_fusion.own), channel_id=1, source_target_pairs={{0,32},{32,0},{1,33},{33,1},{2,34},{34,2},{3,35},{35,3},{4,36},{36... | collective-permute-start | bytes 9437192 | tf_op jit(solution)/shard_map/ppermute | solution.py:17
  82.3 2.3 %copy-start.4 = (f32[3,8,2,32,128]{4,3,2,1,0:T(8,128)S(1)}, f32[3,8,2,32,128]{4,3,2,1,0:T(8,128)}, u32[]{:S(2)}) copy-start(f32[3,8,2,32,128]{4,3,2,1,0:T(8,128)} %project.3) | copy-start | bytes 2359300
  82.3 2.3 %copy-start.7 = (f32[1,8,2,32,128]{4,3,2,1,0:T(8,128)S(1)}, f32[1,8,2,32,128]{4,3,2,1,0:T(8,128)}, u32[]{:S(2)}) copy-start(f32[1,8,2,32,128]{4,3,2,1,0:T(8,128)} %project.4) | copy-start | bytes 786436
  85.6 10.5 %collective-permute-start.1 = (f32[4,2,64,128]{3,2,1,0:T(8,128)}, f32[4,2,64,128]{3,2,1,0:T(8,128)}, u32[]{:S(2)}, u32[]{:S(2)}) collective-permute-start(f32[4,2,64,128]{3,2,1,0:T(8,128)} %get-tuple-element.21), channel_id=1, source_target_pairs={{0,2},{2,4},{4,6},{6,0},{1,3},{3,5},{5,7},{7,1},{8,10},{10,12},{12... | collective-permute-start | bytes 786440 | tf_op jit(solution)/shard_map/ppermute | solution.py:247
  87.1 13.6 %collective-permute-start.2 = (f32[4,2,64,128]{3,2,1,0:T(8,128)}, f32[4,2,64,128]{3,2,1,0:T(8,128)}, u32[]{:S(2)}, u32[]{:S(2)}) collective-permute-start(f32[4,2,64,128]{3,2,1,0:T(8,128)} %get-tuple-element.22), channel_id=1, source_target_pairs={{0,6},{2,0},{4,2},{6,4},{1,7},{3,1},{5,3},{7,5},{8,14},{10,8},{12,... | collective-permute-start | bytes 786440 | tf_op jit(solution)/shard_map/ppermute | solution.py:247
  88.8 13.6 %collective-permute-start.3 = (f32[4,2,64,128]{3,2,1,0:T(8,128)}, f32[4,2,64,128]{3,2,1,0:T(8,128)}, u32[]{:S(2)}, u32[]{:S(2)}) collective-permute-start(f32[4,2,64,128]{3,2,1,0:T(8,128)} %get-tuple-element.23), channel_id=1, source_target_pairs={{0,4},{2,6},{4,0},{6,2},{1,5},{3,7},{5,1},{7,3},{8,12},{10,14},{12... | collective-permute-start | bytes 786440 | tf_op jit(solution)/shard_map/ppermute | solution.py:247
  93.7 1.4 copy-start.12
  93.7 8.7 %copy-start.8 = (f32[1,8,2,32,128]{4,3,2,1,0:T(8,128)S(1)}, f32[1,8,2,32,128]{4,3,2,1,0:T(8,128)}, u32[]{:S(2)}) copy-start(f32[1,8,2,32,128]{4,3,2,1,0:T(8,128)} %project.4) | copy-start | bytes 786436
  103.6 0.7 copy-start.9
  105.0 25.3 %collective-permute-start.13 = (bf16[25,32,512]{2,1,0:T(8,128)(2,1)}, bf16[25,32,512]{2,1,0:T(8,128)(2,1)}, u32[]{:S(2)}, u32[]{:S(2)}) collective-permute-start(bf16[25,32,512]{2,1,0:T(8,128)(2,1)} %hold.7), channel_id=1, source_target_pairs={{0,64},{64,0},{1,65},{65,1},{2,66},{66,2},{3,67},{67,3},{4,68},{68... | collective-permute-start | bytes 2457608 | tf_op jit(solution)/shard_map/ppermute | solution.py:17
  109.1 31.9 %collective-permute-start.11 = (bf16[18,32,512]{2,1,0:T(8,128)(2,1)}, bf16[18,32,512]{2,1,0:T(8,128)(2,1)}, u32[]{:S(2)}, u32[]{:S(2)}) collective-permute-start(bf16[18,32,512]{2,1,0:T(8,128)(2,1)} %hold.8), channel_id=1, source_target_pairs={{0,64},{64,0},{1,65},{65,1},{2,66},{66,2},{3,67},{67,3},{4,68},{68... | collective-permute-start | bytes 1769480 | tf_op jit(solution)/shard_map/ppermute | solution.py:17
  112.2 13.9 %copy-start.10 = (f32[4,2,64,128]{3,2,1,0:T(8,128)S(1)}, f32[4,2,64,128]{3,2,1,0:T(8,128)}, u32[]{:S(2)}) copy-start(f32[4,2,64,128]{3,2,1,0:T(8,128)} %copy-done.9) | copy-start | bytes 786436
  125.3 0.9 copy-start.5
  127.1 17.0 %collective-permute-start.5 = (f32[512,128]{1,0:T(8,128)}, f32[512,128]{1,0:T(8,128)}, u32[]{:S(2)}, u32[]{:S(2)}) collective-permute-start(f32[512,128]{1,0:T(8,128)} %get-tuple-element.18), channel_id=1, source_target_pairs={{0,8},{8,16},{16,24},{24,0},{1,9},{9,17},{17,25},{25,1},{2,10},{10... | collective-permute-start | bytes 786440 | tf_op jit(solution)/shard_map/ppermute | solution.py:231
  128.2 15.9 %collective-permute-start.6 = (f32[512,128]{1,0:T(8,128)}, f32[512,128]{1,0:T(8,128)}, u32[]{:S(2)}, u32[]{:S(2)}) collective-permute-start(f32[512,128]{1,0:T(8,128)} %get-tuple-element.19), channel_id=1, source_target_pairs={{0,24},{8,0},{16,8},{24,16},{1,25},{9,1},{17,9},{25,17},{2,26},{10... | collective-permute-start | bytes 786440 | tf_op jit(solution)/shard_map/ppermute | solution.py:231
  130.3 13.7 %collective-permute-start.7 = (f32[512,128]{1,0:T(8,128)}, f32[512,128]{1,0:T(8,128)}, u32[]{:S(2)}, u32[]{:S(2)}) collective-permute-start(f32[512,128]{1,0:T(8,128)} %get-tuple-element.20), channel_id=1, source_target_pairs={{0,16},{8,24},{16,0},{24,8},{1,17},{9,25},{17,1},{25,9},{2,18},{10... | collective-permute-start | bytes 786440 | tf_op jit(solution)/shard_map/ppermute | solution.py:231
  135.1 11.6 %collective-permute-start.14 = (bf16[6,32,512]{2,1,0:T(8,128)(2,1)}, bf16[6,32,512]{2,1,0:T(8,128)(2,1)S(1)}, u32[]{:S(2)}, u32[]{:S(2)}) collective-permute-start(bf16[6,32,512]{2,1,0:T(8,128)(2,1)} %hold.10), channel_id=1, source_target_pairs={{0,64},{64,0},{1,65},{65,1},{2,66},{66,2},{3,67},{67,3},{4,68},{68... | collective-permute-start | bytes 589832 | tf_op jit(solution)/shard_map/ppermute | solution.py:17
  143.4 0.6 copy-start
  144.1 2.0 %copy-start.1 = (f32[2,32,128]{2,1,0:T(8,128)S(1)}, f32[2,32,128]{2,1,0:T(8,128)}, u32[]{:S(2)}) copy-start(f32[2,32,128]{2,1,0:T(8,128)} %copy-done) | copy-start | bytes 98308
  145.3 1.4 copy-start.11
  148.2 7.7 %collective-permute-start.20 = (bf16[32,512]{1,0:T(8,128)(2,1)}, bf16[32,512]{1,0:T(8,128)(2,1)S(1)}, u32[]{:S(2)}, u32[]{:S(2)}) collective-permute-start(bf16[32,512]{1,0:T(8,128)(2,1)} %hold.11), channel_id=1, source_target_pairs={{0,32},{32,0},{1,33},{33,1},{2,34},{34,2},{3,35},{35,3},{4,36},{36... | collective-permute-start | bytes 98312 | tf_op jit(solution)/shard_map/ppermute | solution.py:17
  150.1 6.5 %collective-permute-start.15 = (f32[2,64,128]{2,1,0:T(8,128)S(1)}, f32[2,64,128]{2,1,0:T(8,128)S(1)}, u32[]{:S(2)}, u32[]{:S(2)}) collective-permute-start(f32[2,64,128]{2,1,0:T(8,128)S(1)} %get-tuple-element.24), channel_id=1, source_target_pairs={{0,2},{2,4},{4,6},{6,0},{1,3},{3,5},{5,7},{7,1},{8,10},{10,12},{12... | collective-permute-start | bytes 196616 | tf_op jit(solution)/shard_map/ppermute | solution.py:247
  151.7 6.6 %collective-permute-start.17 = (f32[2,64,128]{2,1,0:T(8,128)S(1)}, f32[2,64,128]{2,1,0:T(8,128)S(1)}, u32[]{:S(2)}, u32[]{:S(2)}) collective-permute-start(f32[2,64,128]{2,1,0:T(8,128)S(1)} %get-tuple-element.25), channel_id=1, source_target_pairs={{0,4},{2,6},{4,0},{6,2},{1,5},{3,7},{5,1},{7,3},{8,12},{10,14},{12... | collective-permute-start | bytes 196616 | tf_op jit(solution)/shard_map/ppermute | solution.py:247
  154.4 4.3 %collective-permute-start.16 = (f32[2,64,128]{2,1,0:T(8,128)S(1)}, f32[2,64,128]{2,1,0:T(8,128)S(1)}, u32[]{:S(2)}, u32[]{:S(2)}) collective-permute-start(f32[2,64,128]{2,1,0:T(8,128)S(1)} %get-tuple-element.26), channel_id=1, source_target_pairs={{0,6},{2,0},{4,2},{6,4},{1,7},{3,1},{5,3},{7,5},{8,14},{10,8},{12,... | collective-permute-start | bytes 196616 | tf_op jit(solution)/shard_map/ppermute | solution.py:247
  158.7 5.8 %collective-permute-start.18 = (f32[128,128]{1,0:T(8,128)S(1)}, f32[128,128]{1,0:T(8,128)S(1)}, u32[]{:S(2)}, u32[]{:S(2)}) collective-permute-start(f32[128,128]{1,0:T(8,128)S(1)} %fusion.30), channel_id=1, source_target_pairs={{0,1},{1,0},{2,3},{3,2},{4,5},{5,4},{6,7},{7,6},{8,9},{9,8},{10,11... | collective-permute-start | bytes 196616 | tf_op jit(solution)/shard_map/ppermute | solution.py:17
  164.6 1.3 collective-permute-start.19

commit v16 on v14

--- a/solution.py
+++ b/solution.py
@@ -28,12 +28,13 @@
         pltpu.make_async_copy(block.at[:, :, pl.ds(16 * i, 16)], given.at[i], sems.at[i])
         for i in range(pairs)
     ]
-    for copy in copies:
-        copy.start()
+    copies[0].start()
     sent = []
     for z in range(2 * pairs):
         if z % 2 == 0:
             copies[z // 2].wait()
+            if z // 2 + 1 < pairs:
+                copies[z // 2 + 1].start()
         for k in range(comps):
             eight = pl.ds(8 * (z % 2), 8)
             turned[z, :, k] = jnp.swapaxes(given[z // 2, :, k, eight], 0, 1)
@@ -288,9 +289,10 @@
     spread_s = [spread_s[:, y].reshape(-1, count, sites) for y in range(2)]
 
     first = sum_x(jnp.concatenate(first))
-    got_a = swap(hold(jnp.concatenate([spread_s[0], lines]), mark(first)), "yl")
+    part_a = hold(jnp.concatenate([spread_s[0], lines]), mark(first))
+    got_a = swap(part_a, "yl")
+    got_b = swap(hold(spread_s[1], mark(part_a)), "yl")
     late = against([got], 0)
-    got_b = swap(hold(spread_s[1], mark(late)), "yl")
     last = [project_pieces(got_a, spread_v, spread_w, 0)]
     last.append(project_pieces(got_b, spread_v, spread_w, 1, last[0]))
     late = jnp.swapaxes(late, 0, 1).reshape(4, -1, 2 * owned)

time: 167 us -> 172 us (1.030)
  Pallas kernels: 60.7 us -> 68.7 us
  waiting for transfers between devices: 44.4 us -> 38.7 us
    pallas_call x3, Pallas kernels: 22.7 us -> 30.8 us  [by_time(): pl.pallas_call(functools.partial(by_time_kernel, cuts), in_specs=[ANY] *...]
    ppermute x6, waiting for transfers between devices: 27.2 us -> 24 us  [share_z(): lax.ppermute(pick(slabs, (me + k) % 4), 'z', [(i, (i + k) % 4) for i in r...]
    ppermute x8, waiting for transfers between devices: 9.23 us -> 7.41 us  [swap(): return lax.ppermute(value, axis, SWAP)]
    slice x4 -> x3, local copies, waits for them, and re-layouts: 6.44 us -> 5.07 us  [mark(): value = value[0]]
  transfers between devices with their start and end apart: 20 -> 20, of which waited for: 10 -> 10; matrix products, arithmetic and copies ran while one was open for 15% -> 16% of each run, Pallas kernels for 37% -> 40%
where the time goes in v16:
time: 172 us; the launch traced here: 170 us
  Pallas kernels  68.7 us (40%)
  waiting for transfers between devices  38.7 us (23%)
  starting transfers between devices  30.1 us (18%)
  other arithmetic  16.2 us (9%)
  local copies, waits for them, and re-layouts  14.3 us (8%)
    pallas_call x3, Pallas kernels, by_time(): pl.pallas_call(functools.partial(by_time_kernel, cuts), in_specs=[ANY] *...  30.8 us
    pallas_call x3, Pallas kernels, project(): pl.pallas_call(functools.partial(dot_kernel, len(cols)), grid=(size, inne...  29.7 us
    ppermute x6, waiting for transfers between devices, share_z(): lax.ppermute(pick(slabs, (me + k) % 4), 'z', [(i, (i + k) % 4) for i in r...  24 us
    ppermute x6, starting transfers between devices, share_z(): lax.ppermute(pick(slabs, (me + k) % 4), 'z', [(i, (i + k) % 4) for i in r...  11.8 us
    ppermute x6, starting transfers between devices, sum_x(): total = total + lax.ppermute(pick(slabs, (me + k) % 4), 'x', pairs)  10.8 us
    ppermute x8, starting transfers between devices, swap(): return lax.ppermute(value, axis, SWAP)  7.52 us
    ppermute x8, waiting for transfers between devices, swap(): return lax.ppermute(value, axis, SWAP)  7.41 us
    ppermute x6, waiting for transfers between devices, sum_x(): total = total + lax.ppermute(pick(slabs, (me + k) % 4), 'x', pairs)  7.23 us
  transfers between devices with their start and end apart: 20, of which 10 were waited for; matrix products, arithmetic and copies ran while one was open for 16% of the time, Pallas kernels for 40%

profile of v16, /device:TPU:0, one launch (start us, length us, event | category | flops | bytes accessed | tf_op | source)
XLA Modules:
  0.0 169.7 jit_solution(1114592539151943291)
XLA Ops:
  0.6 0.1 collective-permute-start
  0.7 7.1 %by_time.3 = (bf16[3,4,2,6,32,512]{5,4,3,2,1,0:T(8,128)(2,1)}, bf16[1,4,2,6,32,512]{5,4,3,2,1,0:T(8,128)(2,1)}) custom-call(bf16[32,6,32,512]{3,2,1,0:T(8,128)(2,1)} %bitcast.141), custom_call_target="tpu_custom_call" | custom-call | flops 1000 | bytes 1000 | tf_op jit(solution)/shard_map/by_time/pallas_call | solution.py:53
  7.8 1.7 %collective-permute-start.4 = (bf16[3,8,3,64,512]{4,3,2,1,0:T(8,128)(2,1)}, bf16[3,8,3,64,512]{4,3,2,1,0:T(8,128)(2,1)}, u32[]{:S(2)}, u32[]{:S(2)}) collective-permute-start(bf16[3,8,3,64,512]{4,3,2,1,0:T(8,128)(2,1)} %bitcast.130), channel_id=1, source_target_pairs={{0,64},{64,0},{1,65},{65,1},{2,66},{66,2},{3,67},{67,3},{4,68},{68... | collective-permute-start | bytes 14155784 | tf_op jit(solution)/shard_map/ppermute | solution.py:17
  9.6 12.2 %by_time.4 = (bf16[4,4,2,6,64,512]{5,4,3,2,1,0:T(8,128)(2,1)}, bf16[1,4,2,6,64,512]{5,4,3,2,1,0:T(8,128)(2,1)}) custom-call(bf16[64,6,32,512]{3,2,1,0:T(8,128)(2,1)} %bitcast.128, bf16[3,8,3,64,512]{4,3,2,1,0:T(8,128)(2,1)} %bitcast.131), custom_call_target="tpu_custom_call" | custom-call | flops 1000 | bytes 1000 | tf_op jit(solution)/shard_map/by_time/pallas_call | solution.py:53
  21.8 3.3 %fusion.2 = (bf16[1,2,3,192,512]{4,3,2,1,0:T(8,128)(2,1)S(1)}, bf16[2,3,192,512]{3,2,1,0:T(8,128)(2,1)}, bf16[2,3,192,512]{3,2,1,0:T(8,128)(2,1)}, bf16[2,3,192,512]{3,2,1,0:T(8,128)(2,1)}) fusion(s32[]{:T(128)S(6)} %select_n.135, bf16[4,2,3,128,512]{4,3,2,1,0:T(8,128)(2,1)} %bitcast.145, bf16[4,2,3,64,512]{4,3,2,1,0:T(8,128)(2,1)S(1)} %bitcast.140, ...), kind=kLoop, calls=%fused_computation.28 | loop fusion | flops 9437184 | bytes 9437200 | tf_op jit(solution)/shard_map/concatenate | solution.py:282
  25.1 1.9 %collective-permute-start.8 = (bf16[2,3,192,512]{3,2,1,0:T(8,128)(2,1)}, bf16[2,3,192,512]{3,2,1,0:T(8,128)(2,1)S(1)}, u32[]{:S(2)}, u32[]{:S(2)}) collective-permute-start(bf16[2,3,192,512]{3,2,1,0:T(8,128)(2,1)} %get-tuple-element.17), channel_id=1, source_target_pairs={{0,8},{8,16},{16,24},{24,0},{1,9},{9,17},{17,25},{25,1},{2,10},{10... | collective-permute-start | bytes 3538952 | tf_op jit(solution)/shard_map/ppermute | solution.py:231
  27.0 2.2 %collective-permute-start.9 = (bf16[2,3,192,512]{3,2,1,0:T(8,128)(2,1)}, bf16[2,3,192,512]{3,2,1,0:T(8,128)(2,1)S(1)}, u32[]{:S(2)}, u32[]{:S(2)}) collective-permute-start(bf16[2,3,192,512]{3,2,1,0:T(8,128)(2,1)} %get-tuple-element.18), channel_id=1, source_target_pairs={{0,24},{8,0},{16,8},{24,16},{1,25},{9,1},{17,9},{25,17},{2,26},{10... | collective-permute-start | bytes 3538952 | tf_op jit(solution)/shard_map/ppermute | solution.py:231
  29.2 1.8 %collective-permute-start.10 = (bf16[2,3,192,512]{3,2,1,0:T(8,128)(2,1)}, bf16[2,3,192,512]{3,2,1,0:T(8,128)(2,1)}, u32[]{:S(2)}, u32[]{:S(2)}) collective-permute-start(bf16[2,3,192,512]{3,2,1,0:T(8,128)(2,1)} %get-tuple-element.19), channel_id=1, source_target_pairs={{0,16},{8,24},{16,0},{24,8},{1,17},{9,25},{17,1},{25,9},{2,18},{10... | collective-permute-start | bytes 3538952 | tf_op jit(solution)/shard_map/ppermute | solution.py:231
  31.0 11.5 %by_time.5 = bf16[4,4,2,6,64,512]{5,4,3,2,1,0:T(8,128)(2,1)} custom-call(bf16[64,6,32,512]{3,2,1,0:T(8,128)(2,1)} %collective-permute-done.block), custom_call_target="tpu_custom_call" | custom-call | flops 1000 | bytes 1000 | tf_op jit(solution)/shard_map/by_time/pallas_call | solution.py:53
  42.5 11.8 %project.3 = f32[3,8,2,32,128]{4,3,2,1,0:T(8,128)} custom-call(bf16[3,8,3,64,512]{4,3,2,1,0:T(8,128)(2,1)} %bitcast.132, bf16[4,8,3,128,512]{4,3,2,1,0:T(8,128)(2,1)} %bitcast.124, bf16[4,8,3,128,512]{4,3,2,1,0:T(8,128)(2,1)} %bitcast.121), custom_call_target="tpu_custom_call" | custom-call | flops 1000 | bytes 1000 | tf_op jit(solution)/shard_map/project/pallas_call | solution.py:212
  54.3 6.2 %project.4 = f32[1,8,2,32,128]{4,3,2,1,0:T(8,128)} custom-call(bf16[1,8,3,64,512]{4,3,2,1,0:T(8,128)(2,1)} %bitcast.139, bf16[4,8,3,128,512]{4,3,2,1,0:T(8,128)(2,1)} %bitcast.125, bf16[4,8,3,128,512]{4,3,2,1,0:T(8,128)(2,1)} %bitcast.122), custom_call_target="tpu_custom_call" | custom-call | flops 1000 | bytes 1000 | tf_op jit(solution)/shard_map/project/pallas_call | solution.py:212
  60.5 1.4 slice.102
  61.9 1.4 slice.101
  63.3 1.1 copy-done.3
  64.3 16.1 %collective-permute-done.9 = bf16[2,3,192,512]{3,2,1,0:T(8,128)(2,1)S(1)} collective-permute-done((bf16[2,3,192,512]{3,2,1,0:T(8,128)(2,1)}, bf16[2,3,192,512]{3,2,1,0:T(8,128)(2,1)S(1)}, u32[]{:S(2)}, u32[]{:S(2)}) %collective-permute-start.9) | collective-permute-done | bytes 1179680 | tf_op jit(solution)/shard_map/ppermute | solution.py:231
  80.4 1.8 %collective-permute-done.10 = bf16[2,3,192,512]{3,2,1,0:T(8,128)(2,1)} collective-permute-done((bf16[2,3,192,512]{3,2,1,0:T(8,128)(2,1)}, bf16[2,3,192,512]{3,2,1,0:T(8,128)(2,1)}, u32[]{:S(2)}, u32[]{:S(2)}) %collective-permute-start.10) | collective-permute-done | bytes 1179680 | tf_op jit(solution)/shard_map/ppermute | solution.py:231
  82.3 1.9 %pad_maximum_fusion = bf16[4,2,3,192,512]{4,3,2,1,0:T(8,128)(2,1)S(1)} fusion(bf16[1,2,3,192,512]{4,3,2,1,0:T(8,128)(2,1)} %bitcast.40, bf16[1,2,3,192,512]{4,3,2,1,0:T(8,128)(2,1)S(1)} %bitcast.142, bf16[1,2,3,192,512]{4,3,2,1,0:T(8,128)(2,1)} %bitcast.133, bf16[1,2,3,192,512]{4,3,2,1,0:T(8,128)(2,1)S(1)} %get-tuple-element.16), kind=kLoop, calls=%fused_computation.9 | loop fusion | flops 7077888 | bytes 9437184 | tf_op jit(solution)/shard_map/stack | solution.py:285
  84.2 0.3 slice.106.own
  85.3 2.3 %slice.103 = bf16[1,4,2,6,64,512]{5,4,3,2,1,0:T(8,128)(2,1)S(1)} slice(bf16[4,4,2,6,64,512]{5,4,3,2,1,0:T(8,128)(2,1)} %by_time.5), slice={[0:1], [0:4], [0:2], [0:6], [0:64], [0:512]} | slice | bytes 6291456 | tf_op jit(solution)/shard_map/slice | solution.py:79
  87.7 1.0 fusion.26
  88.6 1.5 collective-permute-start.1
  90.1 1.7 %collective-permute-start.2 = (f32[4,2,64,128]{3,2,1,0:T(8,128)}, f32[4,2,64,128]{3,2,1,0:T(8,128)S(1)}, u32[]{:S(2)}, u32[]{:S(2)}) collective-permute-start(f32[4,2,64,128]{3,2,1,0:T(8,128)} %get-tuple-element.24), channel_id=1, source_target_pairs={{0,6},{2,0},{4,2},{6,4},{1,7},{3,1},{5,3},{7,5},{8,14},{10,8},{12,... | collective-permute-start | bytes 786440 | tf_op jit(solution)/shard_map/ppermute | solution.py:247
  91.9 1.8 %collective-permute-start.3 = (f32[4,2,64,128]{3,2,1,0:T(8,128)}, f32[4,2,64,128]{3,2,1,0:T(8,128)}, u32[]{:S(2)}, u32[]{:S(2)}) collective-permute-start(f32[4,2,64,128]{3,2,1,0:T(8,128)} %get-tuple-element.25), channel_id=1, source_target_pairs={{0,4},{2,6},{4,0},{6,2},{1,5},{3,7},{5,1},{7,3},{8,12},{10,14},{12... | collective-permute-start | bytes 786440 | tf_op jit(solution)/shard_map/ppermute | solution.py:247
  93.7 0.7 slice_bitcast_fusion.after
  94.4 2.4 %choose.1 = bf16[4,8,512]{2,1,0:T(8,128)(2,1)} custom-call(s32[4]{0:T(128)} %index.1, s32[1]{0:T(128)S(6)} %copy.24.when, bf16[64,6,32,512]{3,2,1,0:T(8,128)(2,1)} %bitcast.129, bf16[128,512]{1,0:T(8,128)(2,1)} %slice_bitcast_fusion.after), custom_call_target="tpu_custom_call" | custom-call | flops 1000 | bytes 1000 | tf_op jit(solution)/shard_map/choose/pallas_call | solution.py:123
  96.8 2.5 %pad_maximum_fusion.2 = (bf16[4,1,3,64,512]{4,3,2,1,0:T(8,128)(2,1)}, bf16[4,1,3,64,512]{4,3,2,1,0:T(8,128)(2,1)S(1)}) fusion(bf16[1,2,3,192,512]{4,3,2,1,0:T(8,128)(2,1)} %bitcast.40, bf16[1,2,3,192,512]{4,3,2,1,0:T(8,128)(2,1)} %bitcast.143, bf16[1,2,3,192,512]{4,3,2,1,0:T(8,128)(2,1)} %bitcast.134, bf16[1,2,3,192,512]{4,3,2,1,0:T(8,128)(2,1)} %copy-done.2), kind=kLoop, calls=%fused_computation.34 | loop fusion | flops 6291456 | bytes 6291456 | tf_op jit(solution)/shard_map/slice | solution.py:289
  99.3 1.0 pad_maximum_fusion.1.refs_0_
  100.3 3.4 %collective-permute-done.2 = f32[4,2,64,128]{3,2,1,0:T(8,128)S(1)} collective-permute-done((f32[4,2,64,128]{3,2,1,0:T(8,128)}, f32[4,2,64,128]{3,2,1,0:T(8,128)S(1)}, u32[]{:S(2)}, u32[]{:S(2)}) %collective-permute-start.2) | collective-permute-done | bytes 262176 | tf_op jit(solution)/shard_map/ppermute | solution.py:247
  103.8 0.7 copy-done.10
  104.5 1.0 collective-permute-done.3
  105.4 1.1 fusion.24
  106.6 0.6 slice_bitcast_fusion.3.refs_1_
  107.2 0.6 collective-permute-start.11
  107.8 0.1 copy.16
  107.9 0.2 fusion.37
  108.1 0.6 gather_fusion
  108.8 4.0 %collective-permute-done.4.refs_0_ = bf16[3,8,3,64,512]{4,3,2,1,0:T(8,128)(2,1)} collective-permute-done((bf16[3,8,3,64,512]{4,3,2,1,0:T(8,128)(2,1)}, bf16[3,8,3,64,512]{4,3,2,1,0:T(8,128)(2,1)}, u32[]{:S(2)}, u32[]{:S(2)}) %collective-permute-start.4) | collective-permute-done | bytes 4718624 | tf_op jit(solution)/shard_map/ppermute | solution.py:17
  112.8 11.8 %project.5 = f32[3,8,2,32,128]{4,3,2,1,0:T(8,128)} custom-call(bf16[3,8,3,64,512]{4,3,2,1,0:T(8,128)(2,1)} %collective-permute-done.4.refs_0_, bf16[4,8,3,128,512]{4,3,2,1,0:T(8,128)(2,1)} %bitcast.126, bf16[4,8,3,128,512]{4,3,2,1,0:T(8,128)(2,1)} %bitcast.123), custom_call_target="tpu_custom_call" | custom-call | flops 1000 | bytes 1000 | tf_op jit(solution)/shard_map/project/pallas_call | solution.py:212
  124.6 2.1 %copy.17 = f32[4,3,2,64,128]{4,3,2,1,0:T(8,128)} copy(f32[4,3,2,64,128]{4,3,2,0,1:T(8,128)} %bitcast.148) | data formatting | bytes 1572864 | tf_op jit(solution)/shard_map/transpose | solution.py:298
  126.7 1.4 slice_bitcast_fusion.2.refs_1_
  128.1 1.7 collective-permute-start.13
  129.7 2.0 %fusion.15 = (f32[512,128]{1,0:T(8,128)}, f32[512,128]{1,0:T(8,128)}, f32[512,128]{1,0:T(8,128)}) fusion(s32[]{:T(128)S(6)} %select_n.137, f32[4,384,128]{2,1,0:T(8,128)} %bitcast.137, f32[4,128,128]{2,1,0:T(8,128)S(1)} %bitcast.151, s32[]{:T(128)S(6)} %select_n.139, s32[]{:T(128)S(6)} %select_n.141), kind=kLoop, calls=%fused_computation.45 | loop fusion | flops 196608 | bytes 1835020 | tf_op jit(solution)/shard_map/jit(dynamic_index_in_dim)/squeeze | solution.py:225
  131.7 1.9 %collective-permute-start.5 = (f32[512,128]{1,0:T(8,128)}, f32[512,128]{1,0:T(8,128)}, u32[]{:S(2)}, u32[]{:S(2)}) collective-permute-start(f32[512,128]{1,0:T(8,128)} %get-tuple-element.20), channel_id=1, source_target_pairs={{0,8},{8,16},{16,24},{24,0},{1,9},{9,17},{17,25},{25,1},{2,10},{10... | collective-permute-start | bytes 786440 | tf_op jit(solution)/shard_map/ppermute | solution.py:231
  133.7 2.1 %collective-permute-start.6 = (f32[512,128]{1,0:T(8,128)}, f32[512,128]{1,0:T(8,128)}, u32[]{:S(2)}, u32[]{:S(2)}) collective-permute-start(f32[512,128]{1,0:T(8,128)} %get-tuple-element.21), channel_id=1, source_target_pairs={{0,24},{8,0},{16,8},{24,16},{1,25},{9,1},{17,9},{25,17},{2,26},{10... | collective-permute-start | bytes 786440 | tf_op jit(solution)/shard_map/ppermute | solution.py:231
  135.8 1.9 %collective-permute-start.7 = (f32[512,128]{1,0:T(8,128)}, f32[512,128]{1,0:T(8,128)}, u32[]{:S(2)}, u32[]{:S(2)}) collective-permute-start(f32[512,128]{1,0:T(8,128)} %get-tuple-element.22), channel_id=1, source_target_pairs={{0,16},{8,24},{16,0},{24,8},{1,17},{9,25},{17,1},{25,9},{2,18},{10... | collective-permute-start | bytes 786440 | tf_op jit(solution)/shard_map/ppermute | solution.py:231
  137.7 0.8 fusion.36
  138.5 0.3 collective-permute-start.19
  138.8 2.9 %project_pieces.2.refs_1_.refs_0_ = f32[2,32,128]{2,1,0:T(8,128)S(1)} custom-call(bf16[25,32,512]{2,1,0:T(8,128)(2,1)} %collective-permute-done.11.col, bf16[4,2,3,128,512]{4,3,2,1,0:T(8,128)(2,1)S(1)} %slice.106.own, bf16[4,2,3,128,512]{4,3,2,1,0:T(8,128)(2,1)} %collective-permute-done.12.other), custom_call_target="tpu_custom_call" | custom-call | flops 1000 | bytes 1000 | tf_op jit(solution)/shard_map/project_pieces/pallas_call | solution.py:189
  141.7 0.6 copy-done
  142.3 6.1 %collective-permute-done.7.refs_0_ = f32[512,128]{1,0:T(8,128)} collective-permute-done((f32[512,128]{1,0:T(8,128)}, f32[512,128]{1,0:T(8,128)}, u32[]{:S(2)}, u32[]{:S(2)}) %collective-permute-start.7) | collective-permute-done | bytes 262176 | tf_op jit(solution)/shard_map/ppermute | solution.py:231
  148.4 1.2 fusion.13
  149.7 2.9 %project_pieces.3 = f32[2,32,128]{2,1,0:T(8,128)S(1)} custom-call(bf16[24,32,512]{2,1,0:T(8,128)(2,1)} %collective-permute-done.13.col, bf16[4,2,3,128,512]{4,3,2,1,0:T(8,128)(2,1)S(1)} %slice.106.own, bf16[4,2,3,128,512]{4,3,2,1,0:T(8,128)(2,1)} %collective-permute-done.12.other, f32[2,32,128]{2,1,0:T(8,128)S(1)} %copy-done.1), custom_call_target="tpu_custom_call" | custom-call | flops 1000 | bytes 1000 | tf_op jit(solution)/shard_map/project_pieces/pallas_call | solution.py:189
  152.6 1.6 collective-permute-start.14
  154.2 2.7 %collective-permute-start.16 = (f32[2,64,128]{2,1,0:T(8,128)S(1)}, f32[2,64,128]{2,1,0:T(8,128)S(1)}, u32[]{:S(2)}, u32[]{:S(2)}) collective-permute-start(f32[2,64,128]{2,1,0:T(8,128)S(1)} %get-tuple-element.27), channel_id=1, source_target_pairs={{0,4},{2,6},{4,0},{6,2},{1,5},{3,7},{5,1},{7,3},{8,12},{10,14},{12... | collective-permute-start | bytes 196616 | tf_op jit(solution)/shard_map/ppermute | solution.py:247
  156.9 1.4 collective-permute-start.15
  158.4 1.6 collective-permute-done.16
  160.0 1.2 collective-permute-done.15
  161.2 3.0 %collective-permute-start.17 = (f32[128,128]{1,0:T(8,128)S(1)}, f32[128,128]{1,0:T(8,128)S(1)}, u32[]{:S(2)}, u32[]{:S(2)}) collective-permute-start(f32[128,128]{1,0:T(8,128)S(1)} %fusion.30), channel_id=1, source_target_pairs={{0,1},{1,0},{2,3},{3,2},{4,5},{5,4},{6,7},{7,6},{8,9},{9,8},{10,11... | collective-permute-start | bytes 196616 | tf_op jit(solution)/shard_map/ppermute | solution.py:17
  164.2 0.7 broadcast_select_fusion
  165.0 2.1 %collective-permute-done.17 = f32[128,128]{1,0:T(8,128)S(1)} collective-permute-done((f32[128,128]{1,0:T(8,128)S(1)}, f32[128,128]{1,0:T(8,128)S(1)}, u32[]{:S(2)}, u32[]{:S(2)}) %collective-permute-start.17) | collective-permute-done | bytes 65568 | tf_op jit(solution)/shard_map/ppermute | solution.py:17
  167.2 1.2 collective-permute-done.18
  168.6 0.2 select_reduce_fusion
  168.8 0.1 copy.18
  169.0 0.7 copy.19
  (55 shorter events, 0.8 us)
Async XLA Ops:
  0.6 30.4 %collective-permute-start = (bf16[64,6,32,512]{3,2,1,0:T(8,128)(2,1)}, bf16[64,6,32,512]{3,2,1,0:T(8,128)(2,1)}, u32[]{:S(2)}, u32[]{:S(2)}) collective-permute-start(bf16[64,6,32,512]{3,2,1,0:T(8,128)(2,1)} %bitcast.127), channel_id=1, source_target_pairs={{0,32},{32,0},{1,33},{33,1},{2,34},{34,2},{3,35},{35,3},{4,36},{36... | collective-permute-start | bytes 37748744 | tf_op jit(solution)/shard_map/ppermute | solution.py:17
  7.8 14.0 %copy-start.6 = (bf16[1,4,2,6,32,512]{5,4,3,2,1,0:T(8,128)(2,1)S(1)}, bf16[1,4,2,6,32,512]{5,4,3,2,1,0:T(8,128)(2,1)}, u32[]{:S(2)}) copy-start(bf16[1,4,2,6,32,512]{5,4,3,2,1,0:T(8,128)(2,1)} %get-tuple-element.8) | copy-start | bytes 4718596
  7.8 105.0 %collective-permute-start.4 = (bf16[3,8,3,64,512]{4,3,2,1,0:T(8,128)(2,1)}, bf16[3,8,3,64,512]{4,3,2,1,0:T(8,128)(2,1)}, u32[]{:S(2)}, u32[]{:S(2)}) collective-permute-start(bf16[3,8,3,64,512]{4,3,2,1,0:T(8,128)(2,1)} %bitcast.130), channel_id=1, source_target_pairs={{0,64},{64,0},{1,65},{65,1},{2,66},{66,2},{3,67},{67,3},{4,68},{68... | collective-permute-start | bytes 14155784 | tf_op jit(solution)/shard_map/ppermute | solution.py:17
  25.1 57.2 %copy-start.2 = (bf16[1,2,3,192,512]{4,3,2,1,0:T(8,128)(2,1)}, bf16[1,2,3,192,512]{4,3,2,1,0:T(8,128)(2,1)S(1)}, u32[]{:S(2)}) copy-start(bf16[1,2,3,192,512]{4,3,2,1,0:T(8,128)(2,1)S(1)} %get-tuple-element.16) | copy-start | bytes 3538948
  25.1 38.2 %collective-permute-start.8 = (bf16[2,3,192,512]{3,2,1,0:T(8,128)(2,1)}, bf16[2,3,192,512]{3,2,1,0:T(8,128)(2,1)S(1)}, u32[]{:S(2)}, u32[]{:S(2)}) collective-permute-start(bf16[2,3,192,512]{3,2,1,0:T(8,128)(2,1)} %get-tuple-element.17), channel_id=1, source_target_pairs={{0,8},{8,16},{16,24},{24,0},{1,9},{9,17},{17,25},{25,1},{2,10},{10... | collective-permute-start | bytes 3538952 | tf_op jit(solution)/shard_map/ppermute | solution.py:231
  27.0 53.4 %collective-permute-start.9 = (bf16[2,3,192,512]{3,2,1,0:T(8,128)(2,1)}, bf16[2,3,192,512]{3,2,1,0:T(8,128)(2,1)S(1)}, u32[]{:S(2)}, u32[]{:S(2)}) collective-permute-start(bf16[2,3,192,512]{3,2,1,0:T(8,128)(2,1)} %get-tuple-element.18), channel_id=1, source_target_pairs={{0,24},{8,0},{16,8},{24,16},{1,25},{9,1},{17,9},{25,17},{2,26},{10... | collective-permute-start | bytes 3538952 | tf_op jit(solution)/shard_map/ppermute | solution.py:231
  29.2 53.0 %collective-permute-start.10 = (bf16[2,3,192,512]{3,2,1,0:T(8,128)(2,1)}, bf16[2,3,192,512]{3,2,1,0:T(8,128)(2,1)}, u32[]{:S(2)}, u32[]{:S(2)}) collective-permute-start(bf16[2,3,192,512]{3,2,1,0:T(8,128)(2,1)} %get-tuple-element.19), channel_id=1, source_target_pairs={{0,16},{8,24},{16,0},{24,8},{1,17},{9,25},{17,1},{25,9},{2,18},{10... | collective-permute-start | bytes 3538952 | tf_op jit(solution)/shard_map/ppermute | solution.py:231
  63.2 1.1 copy-start.3
  80.4 1.8 %copy-start.7 = (bf16[2,3,192,512]{3,2,1,0:T(8,128)(2,1)}, bf16[2,3,192,512]{3,2,1,0:T(8,128)(2,1)S(1)}, u32[]{:S(2)}) copy-start(bf16[2,3,192,512]{3,2,1,0:T(8,128)(2,1)S(1)} %collective-permute-done.9) | copy-start | bytes 3538948
  84.5 54.0 %collective-permute-start.12 = (bf16[4,2,3,128,512]{4,3,2,1,0:T(8,128)(2,1)S(1)}, bf16[4,2,3,128,512]{4,3,2,1,0:T(8,128)(2,1)}, u32[]{:S(2)}, u32[]{:S(2)}) collective-permute-start(bf16[4,2,3,128,512]{4,3,2,1,0:T(8,128)(2,1)S(1)} %slice.106.own), channel_id=1, source_target_pairs={{0,32},{32,0},{1,33},{33,1},{2,34},{34,2},{3,35},{35,3},{4,36},{36... | collective-permute-start | bytes 9437192 | tf_op jit(solution)/shard_map/ppermute | solution.py:17
  85.3 2.3 %copy-start.4 = (f32[3,8,2,32,128]{4,3,2,1,0:T(8,128)S(1)}, f32[3,8,2,32,128]{4,3,2,1,0:T(8,128)}, u32[]{:S(2)}) copy-start(f32[3,8,2,32,128]{4,3,2,1,0:T(8,128)} %project.3) | copy-start | bytes 2359300
  85.3 2.3 %copy-start.8 = (f32[1,8,2,32,128]{4,3,2,1,0:T(8,128)S(1)}, f32[1,8,2,32,128]{4,3,2,1,0:T(8,128)}, u32[]{:S(2)}) copy-start(f32[1,8,2,32,128]{4,3,2,1,0:T(8,128)} %project.4) | copy-start | bytes 786436
  88.6 11.7 %collective-permute-start.1 = (f32[4,2,64,128]{3,2,1,0:T(8,128)}, f32[4,2,64,128]{3,2,1,0:T(8,128)S(1)}, u32[]{:S(2)}, u32[]{:S(2)}) collective-permute-start(f32[4,2,64,128]{3,2,1,0:T(8,128)} %get-tuple-element.23), channel_id=1, source_target_pairs={{0,2},{2,4},{4,6},{6,0},{1,3},{3,5},{5,7},{7,1},{8,10},{10,12},{12... | collective-permute-start | bytes 786440 | tf_op jit(solution)/shard_map/ppermute | solution.py:247
  90.1 13.6 %collective-permute-start.2 = (f32[4,2,64,128]{3,2,1,0:T(8,128)}, f32[4,2,64,128]{3,2,1,0:T(8,128)S(1)}, u32[]{:S(2)}, u32[]{:S(2)}) collective-permute-start(f32[4,2,64,128]{3,2,1,0:T(8,128)} %get-tuple-element.24), channel_id=1, source_target_pairs={{0,6},{2,0},{4,2},{6,4},{1,7},{3,1},{5,3},{7,5},{8,14},{10,8},{12,... | collective-permute-start | bytes 786440 | tf_op jit(solution)/shard_map/ppermute | solution.py:247
  91.9 13.6 %collective-permute-start.3 = (f32[4,2,64,128]{3,2,1,0:T(8,128)}, f32[4,2,64,128]{3,2,1,0:T(8,128)}, u32[]{:S(2)}, u32[]{:S(2)}) collective-permute-start(f32[4,2,64,128]{3,2,1,0:T(8,128)} %get-tuple-element.25), channel_id=1, source_target_pairs={{0,4},{2,6},{4,0},{6,2},{1,5},{3,7},{5,1},{7,3},{8,12},{10,14},{12... | collective-permute-start | bytes 786440 | tf_op jit(solution)/shard_map/ppermute | solution.py:247
  96.8 2.5 %copy-start.9 = (bf16[4,8,512]{2,1,0:T(8,128)(2,1)S(1)}, bf16[4,8,512]{2,1,0:T(8,128)(2,1)}, u32[]{:S(2)}) copy-start(bf16[4,8,512]{2,1,0:T(8,128)(2,1)} %choose.1) | copy-start | bytes 98308
  99.3 6.2 %copy-start.5 = (f32[3,8,2,32,128]{4,3,2,1,0:T(8,128)S(1)}, f32[3,8,2,32,128]{4,3,2,1,0:T(8,128)}, u32[]{:S(2)}) copy-start(f32[3,8,2,32,128]{4,3,2,1,0:T(8,128)} %project.3) | copy-start | bytes 2359300
  100.3 7.5 %copy-start.11 = (s32[4,4]{1,0:T(4,128)S(1)}, s32[4,4]{1,0:T(4,128)}, u32[]{:S(2)}) copy-start(s32[4,4]{1,0:T(4,128)} %param.9) | copy-start | bytes 196
  103.8 0.7 copy-start.10
  107.2 28.6 %collective-permute-start.11 = (bf16[25,32,512]{2,1,0:T(8,128)(2,1)}, bf16[25,32,512]{2,1,0:T(8,128)(2,1)}, u32[]{:S(2)}, u32[]{:S(2)}) collective-permute-start(bf16[25,32,512]{2,1,0:T(8,128)(2,1)} %hold.5), channel_id=1, source_target_pairs={{0,64},{64,0},{1,65},{65,1},{2,66},{66,2},{3,67},{67,3},{4,68},{68... | collective-permute-start | bytes 2457608 | tf_op jit(solution)/shard_map/ppermute | solution.py:17
  128.1 21.6 %collective-permute-start.13 = (bf16[24,32,512]{2,1,0:T(8,128)(2,1)}, bf16[24,32,512]{2,1,0:T(8,128)(2,1)}, u32[]{:S(2)}, u32[]{:S(2)}) collective-permute-start(bf16[24,32,512]{2,1,0:T(8,128)(2,1)} %hold.7), channel_id=1, source_target_pairs={{0,64},{64,0},{1,65},{65,1},{2,66},{66,2},{3,67},{67,3},{4,68},{68... | collective-permute-start | bytes 2359304 | tf_op jit(solution)/shard_map/ppermute | solution.py:17
  131.7 16.7 %collective-permute-start.5 = (f32[512,128]{1,0:T(8,128)}, f32[512,128]{1,0:T(8,128)}, u32[]{:S(2)}, u32[]{:S(2)}) collective-permute-start(f32[512,128]{1,0:T(8,128)} %get-tuple-element.20), channel_id=1, source_target_pairs={{0,8},{8,16},{16,24},{24,0},{1,9},{9,17},{17,25},{25,1},{2,10},{10... | collective-permute-start | bytes 786440 | tf_op jit(solution)/shard_map/ppermute | solution.py:231
  133.7 14.7 %collective-permute-start.6 = (f32[512,128]{1,0:T(8,128)}, f32[512,128]{1,0:T(8,128)}, u32[]{:S(2)}, u32[]{:S(2)}) collective-permute-start(f32[512,128]{1,0:T(8,128)} %get-tuple-element.21), channel_id=1, source_target_pairs={{0,24},{8,0},{16,8},{24,16},{1,25},{9,1},{17,9},{25,17},{2,26},{10... | collective-permute-start | bytes 786440 | tf_op jit(solution)/shard_map/ppermute | solution.py:231
  135.8 12.6 %collective-permute-start.7 = (f32[512,128]{1,0:T(8,128)}, f32[512,128]{1,0:T(8,128)}, u32[]{:S(2)}, u32[]{:S(2)}) collective-permute-start(f32[512,128]{1,0:T(8,128)} %get-tuple-element.22), channel_id=1, source_target_pairs={{0,16},{8,24},{16,0},{24,8},{1,17},{9,25},{17,1},{25,9},{2,18},{10... | collective-permute-start | bytes 786440 | tf_op jit(solution)/shard_map/ppermute | solution.py:231
  138.5 19.9 %collective-permute-start.19 = (bf16[32,512]{1,0:T(8,128)(2,1)S(1)}, bf16[32,512]{1,0:T(8,128)(2,1)S(1)}, u32[]{:S(2)}, u32[]{:S(2)}) collective-permute-start(bf16[32,512]{1,0:T(8,128)(2,1)S(1)} %fusion.36), channel_id=1, source_target_pairs={{0,32},{32,0},{1,33},{33,1},{2,34},{34,2},{3,35},{35,3},{4,36},{36... | collective-permute-start | bytes 98312 | tf_op jit(solution)/shard_map/ppermute | solution.py:17
  141.7 0.6 copy-start
  148.4 1.3 copy-start.1
  152.6 5.8 %collective-permute-start.14 = (f32[2,64,128]{2,1,0:T(8,128)S(1)}, f32[2,64,128]{2,1,0:T(8,128)S(1)}, u32[]{:S(2)}, u32[]{:S(2)}) collective-permute-start(f32[2,64,128]{2,1,0:T(8,128)S(1)} %get-tuple-element.26), channel_id=1, source_target_pairs={{0,2},{2,4},{4,6},{6,0},{1,3},{3,5},{5,7},{7,1},{8,10},{10,12},{12... | collective-permute-start | bytes 196616 | tf_op jit(solution)/shard_map/ppermute | solution.py:247
  154.2 5.8 %collective-permute-start.16 = (f32[2,64,128]{2,1,0:T(8,128)S(1)}, f32[2,64,128]{2,1,0:T(8,128)S(1)}, u32[]{:S(2)}, u32[]{:S(2)}) collective-permute-start(f32[2,64,128]{2,1,0:T(8,128)S(1)} %get-tuple-element.27), channel_id=1, source_target_pairs={{0,4},{2,6},{4,0},{6,2},{1,5},{3,7},{5,1},{7,3},{8,12},{10,14},{12... | collective-permute-start | bytes 196616 | tf_op jit(solution)/shard_map/ppermute | solution.py:247
  156.9 4.3 %collective-permute-start.15 = (f32[2,64,128]{2,1,0:T(8,128)S(1)}, f32[2,64,128]{2,1,0:T(8,128)S(1)}, u32[]{:S(2)}, u32[]{:S(2)}) collective-permute-start(f32[2,64,128]{2,1,0:T(8,128)S(1)} %get-tuple-element.28), channel_id=1, source_target_pairs={{0,6},{2,0},{4,2},{6,4},{1,7},{3,1},{5,3},{7,5},{8,14},{10,8},{12,... | collective-permute-start | bytes 196616 | tf_op jit(solution)/shard_map/ppermute | solution.py:247
  161.2 5.8 %collective-permute-start.17 = (f32[128,128]{1,0:T(8,128)S(1)}, f32[128,128]{1,0:T(8,128)S(1)}, u32[]{:S(2)}, u32[]{:S(2)}) collective-permute-start(f32[128,128]{1,0:T(8,128)S(1)} %fusion.30), channel_id=1, source_target_pairs={{0,1},{1,0},{2,3},{3,2},{4,5},{5,4},{6,7},{7,6},{8,9},{9,8},{10,11... | collective-permute-start | bytes 196616 | tf_op jit(solution)/shard_map/ppermute | solution.py:17
  167.1 1.3 collective-permute-start.18

commit v17 on v13

--- a/solution.py
+++ b/solution.py
@@ -10,6 +10,7 @@
 from jax.sharding import PartitionSpec as P
 
 MASS = 2
+SPLIT = 4
 SWAP = [(0, 1), (1, 0)]
 
 
@@ -24,16 +25,23 @@
 def by_time_kernel(cuts, block, *refs):
     outs, (given, turned, sems) = refs[-len(cuts) - 3 : -3], refs[-3:]
     pairs, comps = given.shape[0], given.shape[2]
+    span = given.shape[1] // SPLIT
     copies = [
-        pltpu.make_async_copy(block.at[:, :, pl.ds(16 * i, 16)], given.at[i], sems.at[i])
+        pltpu.make_async_copy(
+            block.at[pl.ds(q * span, span), :, pl.ds(16 * i, 16)],
+            given.at[i, pl.ds(q * span, span)],
+            sems.at[SPLIT * i + q],
+        )
         for i in range(pairs)
+        for q in range(SPLIT)
     ]
     for copy in copies:
         copy.start()
     sent = []
     for z in range(2 * pairs):
         if z % 2 == 0:
-            copies[z // 2].wait()
+            for copy in copies[SPLIT * z // 2 : SPLIT * (z // 2 + 1)]:
+                copy.wait()
         for k in range(comps):
             eight = pl.ds(8 * (z % 2), 8)
             turned[z, :, k] = jnp.swapaxes(given[z // 2, :, k, eight], 0, 1)
@@ -41,7 +49,7 @@
             for i in range(nx):
                 at = len(sent)
                 source = turned.at[z, pl.ds(2 * (x + i) + y, ny), :, pl.ds(low, high - low)]
-                sent.append(pltpu.make_async_copy(source, out.at[i, z], sems.at[pairs + at]))
+                sent.append(pltpu.make_async_copy(source, out.at[i, z], sems.at[SPLIT * pairs + at]))
                 sent[at].start()
     for copy in sent:
         copy.wait()
@@ -60,7 +68,7 @@
         scratch_shapes=[
             pltpu.VMEM((times // 16, n, comps, 16, sites), block.dtype),
             pltpu.VMEM((times // 8, 8, comps, n, sites), block.dtype),
-            pltpu.SemaphoreType.DMA((times // 16 + sum(4 * cut[3] for cut in cuts),)),
+            pltpu.SemaphoreType.DMA((SPLIT * times // 16 + sum(4 * cut[3] for cut in cuts),)),
         ],
         compiler_params=pltpu.CompilerParams(vmem_limit_bytes=56 * 2**20),
         cost_estimate=HINT,

time: 168 us -> 168 us (level)
  no operation moved by 1% of the time
where the time goes in v17:
time: 168 us; the launch traced here: 166 us
  Pallas kernels  61.8 us (37%)
  waiting for transfers between devices  43.7 us (26%)
  starting transfers between devices  30.2 us (18%)
  other arithmetic  15.5 us (9%)
  local copies, waits for them, and re-layouts  13.4 us (8%)
  between operations  1.71 us (1%)
    pallas_call x3, Pallas kernels, project(): pl.pallas_call(functools.partial(dot_kernel, len(cols)), grid=(size, inne...  29.7 us
    ppermute x6, waiting for transfers between devices, share_z(): lax.ppermute(pick(slabs, (me + k) % 4), 'z', [(i, (i + k) % 4) for i in r...  26.6 us
    pallas_call x3, Pallas kernels, by_time(): pl.pallas_call(functools.partial(by_time_kernel, cuts), in_specs=[ANY] *...  22.9 us
    ppermute x6, starting transfers between devices, share_z(): lax.ppermute(pick(slabs, (me + k) % 4), 'z', [(i, (i + k) % 4) for i in r...  11.8 us
    ppermute x6, starting transfers between devices, sum_x(): total = total + lax.ppermute(pick(slabs, (me + k) % 4), 'x', pairs)  10.8 us
    ppermute x8, waiting for transfers between devices, swap(): return lax.ppermute(value, axis, SWAP)  9.12 us
    ppermute x6, waiting for transfers between devices, sum_x(): total = total + lax.ppermute(pick(slabs, (me + k) % 4), 'x', pairs)  7.94 us
    ppermute x8, starting transfers between devices, swap(): return lax.ppermute(value, axis, SWAP)  7.6 us
  transfers between devices with their start and end apart: 20, of which 10 were waited for; matrix products, arithmetic and copies ran while one was open for 15% of the time, Pallas kernels for 37%

profile of v17, /device:TPU:0, one launch (start us, length us, event | category | flops | bytes accessed | tf_op | source)
XLA Modules:
  0.0 166.2 jit_solution(8221842499989717612)
XLA Ops:
  0.6 0.1 collective-permute-start
  0.7 5.1 %by_time.3 = (bf16[3,4,2,6,32,512]{5,4,3,2,1,0:T(8,128)(2,1)}, bf16[1,4,2,6,32,512]{5,4,3,2,1,0:T(8,128)(2,1)}) custom-call(bf16[32,6,32,512]{3,2,1,0:T(8,128)(2,1)} %bitcast.140), custom_call_target="tpu_custom_call" | custom-call | flops 1000 | bytes 1000 | tf_op jit(solution)/shard_map/by_time/pallas_call | solution.py:60
  5.8 1.7 %collective-permute-start.4 = (bf16[3,8,3,64,512]{4,3,2,1,0:T(8,128)(2,1)}, bf16[3,8,3,64,512]{4,3,2,1,0:T(8,128)(2,1)}, u32[]{:S(2)}, u32[]{:S(2)}) collective-permute-start(bf16[3,8,3,64,512]{4,3,2,1,0:T(8,128)(2,1)} %bitcast.129), channel_id=1, source_target_pairs={{0,64},{64,0},{1,65},{65,1},{2,66},{66,2},{3,67},{67,3},{4,68},{68... | collective-permute-start | bytes 14155784 | tf_op jit(solution)/shard_map/ppermute | solution.py:18
  7.5 9.4 %by_time.4 = (bf16[4,4,2,6,64,512]{5,4,3,2,1,0:T(8,128)(2,1)}, bf16[1,4,2,6,64,512]{5,4,3,2,1,0:T(8,128)(2,1)}) custom-call(bf16[64,6,32,512]{3,2,1,0:T(8,128)(2,1)} %bitcast.127, bf16[3,8,3,64,512]{4,3,2,1,0:T(8,128)(2,1)} %bitcast.130), custom_call_target="tpu_custom_call" | custom-call | flops 1000 | bytes 1000 | tf_op jit(solution)/shard_map/by_time/pallas_call | solution.py:60
  17.0 3.2 %fusion.2 = (bf16[1,2,3,192,512]{4,3,2,1,0:T(8,128)(2,1)S(1)}, bf16[2,3,192,512]{3,2,1,0:T(8,128)(2,1)}, bf16[2,3,192,512]{3,2,1,0:T(8,128)(2,1)}, bf16[2,3,192,512]{3,2,1,0:T(8,128)(2,1)}) fusion(s32[]{:T(128)S(6)} %select_n.135, bf16[4,2,3,128,512]{4,3,2,1,0:T(8,128)(2,1)} %bitcast.143, bf16[4,2,3,64,512]{4,3,2,1,0:T(8,128)(2,1)S(1)} %bitcast.139, ...), kind=kLoop, calls=%fused_computation.28 | loop fusion | flops 9437184 | bytes 9437200 | tf_op jit(solution)/shard_map/concatenate | solution.py:286
  20.2 1.9 %collective-permute-start.8 = (bf16[2,3,192,512]{3,2,1,0:T(8,128)(2,1)}, bf16[2,3,192,512]{3,2,1,0:T(8,128)(2,1)S(1)}, u32[]{:S(2)}, u32[]{:S(2)}) collective-permute-start(bf16[2,3,192,512]{3,2,1,0:T(8,128)(2,1)} %get-tuple-element.17), channel_id=1, source_target_pairs={{0,8},{8,16},{16,24},{24,0},{1,9},{9,17},{17,25},{25,1},{2,10},{10... | collective-permute-start | bytes 3538952 | tf_op jit(solution)/shard_map/ppermute | solution.py:235
  22.1 2.2 %collective-permute-start.9 = (bf16[2,3,192,512]{3,2,1,0:T(8,128)(2,1)}, bf16[2,3,192,512]{3,2,1,0:T(8,128)(2,1)}, u32[]{:S(2)}, u32[]{:S(2)}) collective-permute-start(bf16[2,3,192,512]{3,2,1,0:T(8,128)(2,1)} %get-tuple-element.18), channel_id=1, source_target_pairs={{0,24},{8,0},{16,8},{24,16},{1,25},{9,1},{17,9},{25,17},{2,26},{10... | collective-permute-start | bytes 3538952 | tf_op jit(solution)/shard_map/ppermute | solution.py:235
  24.3 1.8 %collective-permute-start.10 = (bf16[2,3,192,512]{3,2,1,0:T(8,128)(2,1)}, bf16[2,3,192,512]{3,2,1,0:T(8,128)(2,1)}, u32[]{:S(2)}, u32[]{:S(2)}) collective-permute-start(bf16[2,3,192,512]{3,2,1,0:T(8,128)(2,1)} %get-tuple-element.19), channel_id=1, source_target_pairs={{0,16},{8,24},{16,0},{24,8},{1,17},{9,25},{17,1},{25,9},{2,18},{10... | collective-permute-start | bytes 3538952 | tf_op jit(solution)/shard_map/ppermute | solution.py:235
  26.1 8.5 %by_time.5 = bf16[4,4,2,6,64,512]{5,4,3,2,1,0:T(8,128)(2,1)} custom-call(bf16[64,6,32,512]{3,2,1,0:T(8,128)(2,1)} %collective-permute-done.block), custom_call_target="tpu_custom_call" | custom-call | flops 1000 | bytes 1000 | tf_op jit(solution)/shard_map/by_time/pallas_call | solution.py:60
  34.6 11.8 %project.3 = f32[3,8,2,32,128]{4,3,2,1,0:T(8,128)} custom-call(bf16[3,8,3,64,512]{4,3,2,1,0:T(8,128)(2,1)} %bitcast.131, bf16[4,8,3,128,512]{4,3,2,1,0:T(8,128)(2,1)} %bitcast.123, bf16[4,8,3,128,512]{4,3,2,1,0:T(8,128)(2,1)} %bitcast.120), custom_call_target="tpu_custom_call" | custom-call | flops 1000 | bytes 1000 | tf_op jit(solution)/shard_map/project/pallas_call | solution.py:216
  46.4 6.2 %project.4 = f32[1,8,2,32,128]{4,3,2,1,0:T(8,128)} custom-call(bf16[1,8,3,64,512]{4,3,2,1,0:T(8,128)(2,1)} %bitcast.138, bf16[4,8,3,128,512]{4,3,2,1,0:T(8,128)(2,1)} %bitcast.124, bf16[4,8,3,128,512]{4,3,2,1,0:T(8,128)(2,1)} %bitcast.121), custom_call_target="tpu_custom_call" | custom-call | flops 1000 | bytes 1000 | tf_op jit(solution)/shard_map/project/pallas_call | solution.py:216
  52.6 1.4 slice.109
  53.9 1.4 slice.108
  55.3 1.0 copy-done.3
  56.3 19.2 %collective-permute-done.9 = bf16[2,3,192,512]{3,2,1,0:T(8,128)(2,1)} collective-permute-done((bf16[2,3,192,512]{3,2,1,0:T(8,128)(2,1)}, bf16[2,3,192,512]{3,2,1,0:T(8,128)(2,1)}, u32[]{:S(2)}, u32[]{:S(2)}) %collective-permute-start.9) | collective-permute-done | bytes 1179680 | tf_op jit(solution)/shard_map/ppermute | solution.py:235
  75.5 1.8 %collective-permute-done.10 = bf16[2,3,192,512]{3,2,1,0:T(8,128)(2,1)} collective-permute-done((bf16[2,3,192,512]{3,2,1,0:T(8,128)(2,1)}, bf16[2,3,192,512]{3,2,1,0:T(8,128)(2,1)}, u32[]{:S(2)}, u32[]{:S(2)}) %collective-permute-start.10) | collective-permute-done | bytes 1179680 | tf_op jit(solution)/shard_map/ppermute | solution.py:235
  77.3 2.3 %pad_maximum_fusion = bf16[4,2,3,192,512]{4,3,2,1,0:T(8,128)(2,1)S(1)} fusion(bf16[1,2,3,192,512]{4,3,2,1,0:T(8,128)(2,1)} %bitcast.40, bf16[1,2,3,192,512]{4,3,2,1,0:T(8,128)(2,1)} %bitcast.38, bf16[1,2,3,192,512]{4,3,2,1,0:T(8,128)(2,1)} %bitcast.132, bf16[1,2,3,192,512]{4,3,2,1,0:T(8,128)(2,1)S(1)} %get-tuple-element.16), kind=kLoop, calls=%fused_computation.9 | loop fusion | flops 7077888 | bytes 9437184 | tf_op jit(solution)/shard_map/stack | solution.py:289
  79.6 0.3 slice.113.own
  80.7 2.3 %slice.110 = bf16[1,4,2,6,64,512]{5,4,3,2,1,0:T(8,128)(2,1)S(1)} slice(bf16[4,4,2,6,64,512]{5,4,3,2,1,0:T(8,128)(2,1)} %by_time.5), slice={[0:1], [0:4], [0:2], [0:6], [0:64], [0:512]} | slice | bytes 6291456 | tf_op jit(solution)/shard_map/slice | solution.py:86
  83.1 1.0 fusion.26
  84.0 1.5 collective-permute-start.1
  85.5 1.7 %collective-permute-start.2 = (f32[4,2,64,128]{3,2,1,0:T(8,128)}, f32[4,2,64,128]{3,2,1,0:T(8,128)}, u32[]{:S(2)}, u32[]{:S(2)}) collective-permute-start(f32[4,2,64,128]{3,2,1,0:T(8,128)} %get-tuple-element.24), channel_id=1, source_target_pairs={{0,6},{2,0},{4,2},{6,4},{1,7},{3,1},{5,3},{7,5},{8,14},{10,8},{12,... | collective-permute-start | bytes 786440 | tf_op jit(solution)/shard_map/ppermute | solution.py:251
  87.3 1.8 %collective-permute-start.3 = (f32[4,2,64,128]{3,2,1,0:T(8,128)}, f32[4,2,64,128]{3,2,1,0:T(8,128)}, u32[]{:S(2)}, u32[]{:S(2)}) collective-permute-start(f32[4,2,64,128]{3,2,1,0:T(8,128)} %get-tuple-element.25), channel_id=1, source_target_pairs={{0,4},{2,6},{4,0},{6,2},{1,5},{3,7},{5,1},{7,3},{8,12},{10,14},{12... | collective-permute-start | bytes 786440 | tf_op jit(solution)/shard_map/ppermute | solution.py:251
  89.1 0.7 slice_bitcast_fusion.after
  89.8 2.4 %choose.1 = bf16[4,8,512]{2,1,0:T(8,128)(2,1)} custom-call(s32[4]{0:T(128)} %index.1, s32[1]{0:T(128)S(6)} %copy.24.when, bf16[64,6,32,512]{3,2,1,0:T(8,128)(2,1)} %bitcast.128, bf16[128,512]{1,0:T(8,128)(2,1)} %slice_bitcast_fusion.after), custom_call_target="tpu_custom_call" | custom-call | flops 1000 | bytes 1000 | tf_op jit(solution)/shard_map/choose/pallas_call | solution.py:130
  92.2 2.5 %pad_maximum_fusion.2 = (bf16[4,1,3,64,512]{4,3,2,1,0:T(8,128)(2,1)}, bf16[4,1,3,64,512]{4,3,2,1,0:T(8,128)(2,1)S(1)}) fusion(bf16[1,2,3,192,512]{4,3,2,1,0:T(8,128)(2,1)} %bitcast.40, bf16[1,2,3,192,512]{4,3,2,1,0:T(8,128)(2,1)} %bitcast.38, bf16[1,2,3,192,512]{4,3,2,1,0:T(8,128)(2,1)} %bitcast.133, bf16[1,2,3,192,512]{4,3,2,1,0:T(8,128)(2,1)} %copy-done.2), kind=kLoop, calls=%fused_computation.34 | loop fusion | flops 6291456 | bytes 6291456 | tf_op jit(solution)/shard_map/slice | solution.py:293
  94.7 1.0 pad_maximum_fusion.1.refs_0_
  95.7 3.5 %collective-permute-done.2 = f32[4,2,64,128]{3,2,1,0:T(8,128)} collective-permute-done((f32[4,2,64,128]{3,2,1,0:T(8,128)}, f32[4,2,64,128]{3,2,1,0:T(8,128)}, u32[]{:S(2)}, u32[]{:S(2)}) %collective-permute-start.2) | collective-permute-done | bytes 262176 | tf_op jit(solution)/shard_map/ppermute | solution.py:251
  99.2 1.7 %collective-permute-done.3 = f32[4,2,64,128]{3,2,1,0:T(8,128)} collective-permute-done((f32[4,2,64,128]{3,2,1,0:T(8,128)}, f32[4,2,64,128]{3,2,1,0:T(8,128)}, u32[]{:S(2)}, u32[]{:S(2)}) %collective-permute-start.3) | collective-permute-done | bytes 262176 | tf_op jit(solution)/shard_map/ppermute | solution.py:251
  100.8 1.2 fusion.24
  102.1 0.7 copy-done.9
  102.8 0.6 slice_bitcast_fusion.2.refs_1_
  103.4 0.6 collective-permute-start.11
  104.0 0.1 copy.16
  104.1 0.2 fusion.37
  104.3 0.6 gather_fusion
  105.0 5.8 %collective-permute-done.4.refs_0_ = bf16[3,8,3,64,512]{4,3,2,1,0:T(8,128)(2,1)} collective-permute-done((bf16[3,8,3,64,512]{4,3,2,1,0:T(8,128)(2,1)}, bf16[3,8,3,64,512]{4,3,2,1,0:T(8,128)(2,1)}, u32[]{:S(2)}, u32[]{:S(2)}) %collective-permute-start.4) | collective-permute-done | bytes 4718624 | tf_op jit(solution)/shard_map/ppermute | solution.py:18
  110.8 11.8 %project.5 = f32[3,8,2,32,128]{4,3,2,1,0:T(8,128)} custom-call(bf16[3,8,3,64,512]{4,3,2,1,0:T(8,128)(2,1)} %collective-permute-done.4.refs_0_, bf16[4,8,3,128,512]{4,3,2,1,0:T(8,128)(2,1)} %bitcast.125, bf16[4,8,3,128,512]{4,3,2,1,0:T(8,128)(2,1)} %bitcast.122), custom_call_target="tpu_custom_call" | custom-call | flops 1000 | bytes 1000 | tf_op jit(solution)/shard_map/project/pallas_call | solution.py:216
  122.6 1.4 slice.116
  124.0 1.2 copy.17
  125.2 1.7 %collective-permute-start.13 = (bf16[24,32,512]{2,1,0:T(8,128)(2,1)}, bf16[24,32,512]{2,1,0:T(8,128)(2,1)}, u32[]{:S(2)}, u32[]{:S(2)}) collective-permute-start(bf16[24,32,512]{2,1,0:T(8,128)(2,1)} %hold.7), channel_id=1, source_target_pairs={{0,64},{64,0},{1,65},{65,1},{2,66},{66,2},{3,67},{67,3},{4,68},{68... | collective-permute-start | bytes 2359304 | tf_op jit(solution)/shard_map/ppermute | solution.py:18
  127.0 0.9 fusion.15
  127.9 1.9 %collective-permute-start.5 = (f32[512,128]{1,0:T(8,128)}, f32[512,128]{1,0:T(8,128)}, u32[]{:S(2)}, u32[]{:S(2)}) collective-permute-start(f32[512,128]{1,0:T(8,128)} %get-tuple-element.20), channel_id=1, source_target_pairs={{0,8},{8,16},{16,24},{24,0},{1,9},{9,17},{17,25},{25,1},{2,10},{10... | collective-permute-start | bytes 786440 | tf_op jit(solution)/shard_map/ppermute | solution.py:235
  129.8 2.1 %collective-permute-start.6 = (f32[512,128]{1,0:T(8,128)}, f32[512,128]{1,0:T(8,128)}, u32[]{:S(2)}, u32[]{:S(2)}) collective-permute-start(f32[512,128]{1,0:T(8,128)} %get-tuple-element.21), channel_id=1, source_target_pairs={{0,24},{8,0},{16,8},{24,16},{1,25},{9,1},{17,9},{25,17},{2,26},{10... | collective-permute-start | bytes 786440 | tf_op jit(solution)/shard_map/ppermute | solution.py:235
  131.9 1.9 %collective-permute-start.7 = (f32[512,128]{1,0:T(8,128)}, f32[512,128]{1,0:T(8,128)}, u32[]{:S(2)}, u32[]{:S(2)}) collective-permute-start(f32[512,128]{1,0:T(8,128)} %get-tuple-element.22), channel_id=1, source_target_pairs={{0,16},{8,24},{16,0},{24,8},{1,17},{9,25},{17,1},{25,9},{2,18},{10... | collective-permute-start | bytes 786440 | tf_op jit(solution)/shard_map/ppermute | solution.py:235
  133.9 0.8 fusion.36
  134.6 0.3 collective-permute-start.19
  134.9 3.3 %project_pieces.2.refs_1_.refs_0_ = f32[2,32,128]{2,1,0:T(8,128)S(1)} custom-call(bf16[25,32,512]{2,1,0:T(8,128)(2,1)} %collective-permute-done.11.col, bf16[4,2,3,128,512]{4,3,2,1,0:T(8,128)(2,1)S(1)} %slice.113.own, bf16[4,2,3,128,512]{4,3,2,1,0:T(8,128)(2,1)} %collective-permute-done.12.other), custom_call_target="tpu_custom_call" | custom-call | flops 1000 | bytes 1000 | tf_op jit(solution)/shard_map/project_pieces/pallas_call | solution.py:194
  138.3 0.6 copy-done
  138.9 5.6 %collective-permute-done.7.refs_0_ = f32[512,128]{1,0:T(8,128)} collective-permute-done((f32[512,128]{1,0:T(8,128)}, f32[512,128]{1,0:T(8,128)}, u32[]{:S(2)}, u32[]{:S(2)}) %collective-permute-start.7) | collective-permute-done | bytes 262176 | tf_op jit(solution)/shard_map/ppermute | solution.py:235
  144.5 1.2 fusion.13
  145.8 3.3 %project_pieces.3 = f32[2,32,128]{2,1,0:T(8,128)S(1)} custom-call(bf16[24,32,512]{2,1,0:T(8,128)(2,1)} %collective-permute-done.13.col, bf16[4,2,3,128,512]{4,3,2,1,0:T(8,128)(2,1)S(1)} %slice.113.own, bf16[4,2,3,128,512]{4,3,2,1,0:T(8,128)(2,1)} %collective-permute-done.12.other, f32[2,32,128]{2,1,0:T(8,128)S(1)} %copy-done.1), custom_call_target="tpu_custom_call" | custom-call | flops 1000 | bytes 1000 | tf_op jit(solution)/shard_map/project_pieces/pallas_call | solution.py:194
  149.2 1.6 collective-permute-start.14
  150.8 2.7 %collective-permute-start.16 = (f32[2,64,128]{2,1,0:T(8,128)S(1)}, f32[2,64,128]{2,1,0:T(8,128)S(1)}, u32[]{:S(2)}, u32[]{:S(2)}) collective-permute-start(f32[2,64,128]{2,1,0:T(8,128)S(1)} %get-tuple-element.27), channel_id=1, source_target_pairs={{0,4},{2,6},{4,0},{6,2},{1,5},{3,7},{5,1},{7,3},{8,12},{10,14},{12... | collective-permute-start | bytes 196616 | tf_op jit(solution)/shard_map/ppermute | solution.py:251
  153.5 1.4 collective-permute-start.15
  155.0 1.6 collective-permute-done.16
  156.5 1.2 collective-permute-done.15
  157.8 3.0 %collective-permute-start.17 = (f32[128,128]{1,0:T(8,128)S(1)}, f32[128,128]{1,0:T(8,128)S(1)}, u32[]{:S(2)}, u32[]{:S(2)}) collective-permute-start(f32[128,128]{1,0:T(8,128)S(1)} %fusion.30), channel_id=1, source_target_pairs={{0,1},{1,0},{2,3},{3,2},{4,5},{5,4},{6,7},{7,6},{8,9},{9,8},{10,11... | collective-permute-start | bytes 196616 | tf_op jit(solution)/shard_map/ppermute | solution.py:18
  160.8 0.7 broadcast_select_fusion
  161.5 2.1 %collective-permute-done.17 = f32[128,128]{1,0:T(8,128)S(1)} collective-permute-done((f32[128,128]{1,0:T(8,128)S(1)}, f32[128,128]{1,0:T(8,128)S(1)}, u32[]{:S(2)}, u32[]{:S(2)}) %collective-permute-start.17) | collective-permute-done | bytes 65568 | tf_op jit(solution)/shard_map/ppermute | solution.py:18
  163.8 1.2 collective-permute-done.18
  165.1 0.2 select_reduce_fusion
  165.4 0.1 copy.18
  165.5 0.7 copy.19
  (57 shorter events, 0.8 us)
Async XLA Ops:
  0.6 25.5 %collective-permute-start = (bf16[64,6,32,512]{3,2,1,0:T(8,128)(2,1)}, bf16[64,6,32,512]{3,2,1,0:T(8,128)(2,1)}, u32[]{:S(2)}, u32[]{:S(2)}) collective-permute-start(bf16[64,6,32,512]{3,2,1,0:T(8,128)(2,1)} %bitcast.126), channel_id=1, source_target_pairs={{0,32},{32,0},{1,33},{33,1},{2,34},{34,2},{3,35},{35,3},{4,36},{36... | collective-permute-start | bytes 37748744 | tf_op jit(solution)/shard_map/ppermute | solution.py:18
  5.8 11.2 %copy-start.6 = (bf16[1,4,2,6,32,512]{5,4,3,2,1,0:T(8,128)(2,1)S(1)}, bf16[1,4,2,6,32,512]{5,4,3,2,1,0:T(8,128)(2,1)}, u32[]{:S(2)}) copy-start(bf16[1,4,2,6,32,512]{5,4,3,2,1,0:T(8,128)(2,1)} %get-tuple-element.8) | copy-start | bytes 4718596
  5.8 105.0 %collective-permute-start.4 = (bf16[3,8,3,64,512]{4,3,2,1,0:T(8,128)(2,1)}, bf16[3,8,3,64,512]{4,3,2,1,0:T(8,128)(2,1)}, u32[]{:S(2)}, u32[]{:S(2)}) collective-permute-start(bf16[3,8,3,64,512]{4,3,2,1,0:T(8,128)(2,1)} %bitcast.129), channel_id=1, source_target_pairs={{0,64},{64,0},{1,65},{65,1},{2,66},{66,2},{3,67},{67,3},{4,68},{68... | collective-permute-start | bytes 14155784 | tf_op jit(solution)/shard_map/ppermute | solution.py:18
  20.2 57.2 %copy-start.2 = (bf16[1,2,3,192,512]{4,3,2,1,0:T(8,128)(2,1)}, bf16[1,2,3,192,512]{4,3,2,1,0:T(8,128)(2,1)S(1)}, u32[]{:S(2)}) copy-start(bf16[1,2,3,192,512]{4,3,2,1,0:T(8,128)(2,1)S(1)} %get-tuple-element.16) | copy-start | bytes 3538948
  20.2 35.1 %collective-permute-start.8 = (bf16[2,3,192,512]{3,2,1,0:T(8,128)(2,1)}, bf16[2,3,192,512]{3,2,1,0:T(8,128)(2,1)S(1)}, u32[]{:S(2)}, u32[]{:S(2)}) collective-permute-start(bf16[2,3,192,512]{3,2,1,0:T(8,128)(2,1)} %get-tuple-element.17), channel_id=1, source_target_pairs={{0,8},{8,16},{16,24},{24,0},{1,9},{9,17},{17,25},{25,1},{2,10},{10... | collective-permute-start | bytes 3538952 | tf_op jit(solution)/shard_map/ppermute | solution.py:235
  22.1 53.4 %collective-permute-start.9 = (bf16[2,3,192,512]{3,2,1,0:T(8,128)(2,1)}, bf16[2,3,192,512]{3,2,1,0:T(8,128)(2,1)}, u32[]{:S(2)}, u32[]{:S(2)}) collective-permute-start(bf16[2,3,192,512]{3,2,1,0:T(8,128)(2,1)} %get-tuple-element.18), channel_id=1, source_target_pairs={{0,24},{8,0},{16,8},{24,16},{1,25},{9,1},{17,9},{25,17},{2,26},{10... | collective-permute-start | bytes 3538952 | tf_op jit(solution)/shard_map/ppermute | solution.py:235
  24.3 53.0 %collective-permute-start.10 = (bf16[2,3,192,512]{3,2,1,0:T(8,128)(2,1)}, bf16[2,3,192,512]{3,2,1,0:T(8,128)(2,1)}, u32[]{:S(2)}, u32[]{:S(2)}) collective-permute-start(bf16[2,3,192,512]{3,2,1,0:T(8,128)(2,1)} %get-tuple-element.19), channel_id=1, source_target_pairs={{0,16},{8,24},{16,0},{24,8},{1,17},{9,25},{17,1},{25,9},{2,18},{10... | collective-permute-start | bytes 3538952 | tf_op jit(solution)/shard_map/ppermute | solution.py:235
  55.3 1.0 copy-start.3
  79.9 54.7 %collective-permute-start.12 = (bf16[4,2,3,128,512]{4,3,2,1,0:T(8,128)(2,1)S(1)}, bf16[4,2,3,128,512]{4,3,2,1,0:T(8,128)(2,1)}, u32[]{:S(2)}, u32[]{:S(2)}) collective-permute-start(bf16[4,2,3,128,512]{4,3,2,1,0:T(8,128)(2,1)S(1)} %slice.113.own), channel_id=1, source_target_pairs={{0,32},{32,0},{1,33},{33,1},{2,34},{34,2},{3,35},{35,3},{4,36},{36... | collective-permute-start | bytes 9437192 | tf_op jit(solution)/shard_map/ppermute | solution.py:18
  80.7 2.3 %copy-start.4 = (f32[3,8,2,32,128]{4,3,2,1,0:T(8,128)S(1)}, f32[3,8,2,32,128]{4,3,2,1,0:T(8,128)}, u32[]{:S(2)}) copy-start(f32[3,8,2,32,128]{4,3,2,1,0:T(8,128)} %project.3) | copy-start | bytes 2359300
  80.7 2.3 %copy-start.7 = (f32[1,8,2,32,128]{4,3,2,1,0:T(8,128)S(1)}, f32[1,8,2,32,128]{4,3,2,1,0:T(8,128)}, u32[]{:S(2)}) copy-start(f32[1,8,2,32,128]{4,3,2,1,0:T(8,128)} %project.4) | copy-start | bytes 786436
  84.0 11.7 %collective-permute-start.1 = (f32[4,2,64,128]{3,2,1,0:T(8,128)}, f32[4,2,64,128]{3,2,1,0:T(8,128)}, u32[]{:S(2)}, u32[]{:S(2)}) collective-permute-start(f32[4,2,64,128]{3,2,1,0:T(8,128)} %get-tuple-element.23), channel_id=1, source_target_pairs={{0,2},{2,4},{4,6},{6,0},{1,3},{3,5},{5,7},{7,1},{8,10},{10,12},{12... | collective-permute-start | bytes 786440 | tf_op jit(solution)/shard_map/ppermute | solution.py:251
  85.5 13.6 %collective-permute-start.2 = (f32[4,2,64,128]{3,2,1,0:T(8,128)}, f32[4,2,64,128]{3,2,1,0:T(8,128)}, u32[]{:S(2)}, u32[]{:S(2)}) collective-permute-start(f32[4,2,64,128]{3,2,1,0:T(8,128)} %get-tuple-element.24), channel_id=1, source_target_pairs={{0,6},{2,0},{4,2},{6,4},{1,7},{3,1},{5,3},{7,5},{8,14},{10,8},{12,... | collective-permute-start | bytes 786440 | tf_op jit(solution)/shard_map/ppermute | solution.py:251
  87.3 13.6 %collective-permute-start.3 = (f32[4,2,64,128]{3,2,1,0:T(8,128)}, f32[4,2,64,128]{3,2,1,0:T(8,128)}, u32[]{:S(2)}, u32[]{:S(2)}) collective-permute-start(f32[4,2,64,128]{3,2,1,0:T(8,128)} %get-tuple-element.25), channel_id=1, source_target_pairs={{0,4},{2,6},{4,0},{6,2},{1,5},{3,7},{5,1},{7,3},{8,12},{10,14},{12... | collective-permute-start | bytes 786440 | tf_op jit(solution)/shard_map/ppermute | solution.py:251
  92.2 2.5 %copy-start.11 = (bf16[4,8,512]{2,1,0:T(8,128)(2,1)S(1)}, bf16[4,8,512]{2,1,0:T(8,128)(2,1)}, u32[]{:S(2)}) copy-start(bf16[4,8,512]{2,1,0:T(8,128)(2,1)} %choose.1) | copy-start | bytes 98308
  94.7 6.2 %copy-start.8 = (f32[1,8,2,32,128]{4,3,2,1,0:T(8,128)S(1)}, f32[1,8,2,32,128]{4,3,2,1,0:T(8,128)}, u32[]{:S(2)}) copy-start(f32[1,8,2,32,128]{4,3,2,1,0:T(8,128)} %project.4) | copy-start | bytes 786436
  95.7 8.3 %copy-start.12 = (s32[4,4]{1,0:T(4,128)S(1)}, s32[4,4]{1,0:T(4,128)}, u32[]{:S(2)}) copy-start(s32[4,4]{1,0:T(4,128)} %param.9) | copy-start | bytes 196
  102.0 0.7 copy-start.9
  103.4 28.6 %collective-permute-start.11 = (bf16[25,32,512]{2,1,0:T(8,128)(2,1)}, bf16[25,32,512]{2,1,0:T(8,128)(2,1)}, u32[]{:S(2)}, u32[]{:S(2)}) collective-permute-start(bf16[25,32,512]{2,1,0:T(8,128)(2,1)} %hold.5), channel_id=1, source_target_pairs={{0,64},{64,0},{1,65},{65,1},{2,66},{66,2},{3,67},{67,3},{4,68},{68... | collective-permute-start | bytes 2457608 | tf_op jit(solution)/shard_map/ppermute | solution.py:18
  124.0 3.0 %copy-start.10 = (f32[4,2,64,128]{3,2,1,0:T(8,128)S(1)}, f32[4,2,64,128]{3,2,1,0:T(8,128)}, u32[]{:S(2)}) copy-start(f32[4,2,64,128]{3,2,1,0:T(8,128)} %copy-done.9) | copy-start | bytes 786436
  125.2 1.8 %copy-start.5 = (f32[4,3,2,64,128]{4,3,2,1,0:T(8,128)}, f32[4,3,2,64,128]{4,3,2,1,0:T(8,128)S(1)}, u32[]{:S(2)}) copy-start(f32[4,3,2,64,128]{4,3,2,1,0:T(8,128)S(1)} %copy.17) | copy-start | bytes 2359300
  125.2 20.6 %collective-permute-start.13 = (bf16[24,32,512]{2,1,0:T(8,128)(2,1)}, bf16[24,32,512]{2,1,0:T(8,128)(2,1)}, u32[]{:S(2)}, u32[]{:S(2)}) collective-permute-start(bf16[24,32,512]{2,1,0:T(8,128)(2,1)} %hold.7), channel_id=1, source_target_pairs={{0,64},{64,0},{1,65},{65,1},{2,66},{66,2},{3,67},{67,3},{4,68},{68... | collective-permute-start | bytes 2359304 | tf_op jit(solution)/shard_map/ppermute | solution.py:18
  127.9 16.6 %collective-permute-start.5 = (f32[512,128]{1,0:T(8,128)}, f32[512,128]{1,0:T(8,128)}, u32[]{:S(2)}, u32[]{:S(2)}) collective-permute-start(f32[512,128]{1,0:T(8,128)} %get-tuple-element.20), channel_id=1, source_target_pairs={{0,8},{8,16},{16,24},{24,0},{1,9},{9,17},{17,25},{25,1},{2,10},{10... | collective-permute-start | bytes 786440 | tf_op jit(solution)/shard_map/ppermute | solution.py:235
  129.8 14.7 %collective-permute-start.6 = (f32[512,128]{1,0:T(8,128)}, f32[512,128]{1,0:T(8,128)}, u32[]{:S(2)}, u32[]{:S(2)}) collective-permute-start(f32[512,128]{1,0:T(8,128)} %get-tuple-element.21), channel_id=1, source_target_pairs={{0,24},{8,0},{16,8},{24,16},{1,25},{9,1},{17,9},{25,17},{2,26},{10... | collective-permute-start | bytes 786440 | tf_op jit(solution)/shard_map/ppermute | solution.py:235
  131.9 12.6 %collective-permute-start.7 = (f32[512,128]{1,0:T(8,128)}, f32[512,128]{1,0:T(8,128)}, u32[]{:S(2)}, u32[]{:S(2)}) collective-permute-start(f32[512,128]{1,0:T(8,128)} %get-tuple-element.22), channel_id=1, source_target_pairs={{0,16},{8,24},{16,0},{24,8},{1,17},{9,25},{17,1},{25,9},{2,18},{10... | collective-permute-start | bytes 786440 | tf_op jit(solution)/shard_map/ppermute | solution.py:235
  134.6 20.3 %collective-permute-start.19 = (bf16[32,512]{1,0:T(8,128)(2,1)S(1)}, bf16[32,512]{1,0:T(8,128)(2,1)S(1)}, u32[]{:S(2)}, u32[]{:S(2)}) collective-permute-start(bf16[32,512]{1,0:T(8,128)(2,1)S(1)} %fusion.36), channel_id=1, source_target_pairs={{0,32},{32,0},{1,33},{33,1},{2,34},{34,2},{3,35},{35,3},{4,36},{36... | collective-permute-start | bytes 98312 | tf_op jit(solution)/shard_map/ppermute | solution.py:18
  138.3 0.6 copy-start
  144.5 1.3 copy-start.1
  149.2 5.8 %collective-permute-start.14 = (f32[2,64,128]{2,1,0:T(8,128)S(1)}, f32[2,64,128]{2,1,0:T(8,128)S(1)}, u32[]{:S(2)}, u32[]{:S(2)}) collective-permute-start(f32[2,64,128]{2,1,0:T(8,128)S(1)} %get-tuple-element.26), channel_id=1, source_target_pairs={{0,2},{2,4},{4,6},{6,0},{1,3},{3,5},{5,7},{7,1},{8,10},{10,12},{12... | collective-permute-start | bytes 196616 | tf_op jit(solution)/shard_map/ppermute | solution.py:251
  150.8 5.8 %collective-permute-start.16 = (f32[2,64,128]{2,1,0:T(8,128)S(1)}, f32[2,64,128]{2,1,0:T(8,128)S(1)}, u32[]{:S(2)}, u32[]{:S(2)}) collective-permute-start(f32[2,64,128]{2,1,0:T(8,128)S(1)} %get-tuple-element.27), channel_id=1, source_target_pairs={{0,4},{2,6},{4,0},{6,2},{1,5},{3,7},{5,1},{7,3},{8,12},{10,14},{12... | collective-permute-start | bytes 196616 | tf_op jit(solution)/shard_map/ppermute | solution.py:251
  153.5 4.3 %collective-permute-start.15 = (f32[2,64,128]{2,1,0:T(8,128)S(1)}, f32[2,64,128]{2,1,0:T(8,128)S(1)}, u32[]{:S(2)}, u32[]{:S(2)}) collective-permute-start(f32[2,64,128]{2,1,0:T(8,128)S(1)} %get-tuple-element.28), channel_id=1, source_target_pairs={{0,6},{2,0},{4,2},{6,4},{1,7},{3,1},{5,3},{7,5},{8,14},{10,8},{12,... | collective-permute-start | bytes 196616 | tf_op jit(solution)/shard_map/ppermute | solution.py:251
  157.8 5.8 %collective-permute-start.17 = (f32[128,128]{1,0:T(8,128)S(1)}, f32[128,128]{1,0:T(8,128)S(1)}, u32[]{:S(2)}, u32[]{:S(2)}) collective-permute-start(f32[128,128]{1,0:T(8,128)S(1)} %fusion.30), channel_id=1, source_target_pairs={{0,1},{1,0},{2,3},{3,2},{4,5},{5,4},{6,7},{7,6},{8,9},{9,8},{10,11... | collective-permute-start | bytes 196616 | tf_op jit(solution)/shard_map/ppermute | solution.py:18
  163.7 1.3 collective-permute-start.18

commit v18 on v14

--- a/solution.py
+++ b/solution.py
@@ -224,7 +224,7 @@
     return lax.dynamic_index_in_dim(value, index, 0, keepdims=False)
 
 
-def share_z(slabs):
+def share_z(slabs, pick=pick):
     me = lax.axis_index("z")
     got = [
         lax.ppermute(pick(slabs, (me + k) % 4), "z", [(i, (i + k) % 4) for i in range(4)])
@@ -293,8 +293,15 @@
     got_b = swap(hold(spread_s[1], mark(late)), "yl")
     last = [project_pieces(got_a, spread_v, spread_w, 0)]
     last.append(project_pieces(got_b, spread_v, spread_w, 1, last[0]))
-    late = jnp.swapaxes(late, 0, 1).reshape(4, -1, 2 * owned)
-    late = share_z(jnp.concatenate([first.reshape(4, -1, 2 * owned), late], axis=1))
+    late = share_z(
+        (first, late),
+        lambda v, z: jnp.concatenate(
+            [
+                pick(v[0], z).reshape(-1, 2 * owned),
+                lax.dynamic_index_in_dim(v[1], z, 1, keepdims=False).reshape(-1, 2 * owned),
+            ]
+        ),
+    )
     late = late[0] + late[1] + late[2] + hold(late[3], last[0])
     cut = 4 * count
     first = late[:cut].reshape(2, -1, 2 * owned)

time: 167 us -> 169 us (1.012)
  waiting for transfers between devices: 44.4 us -> 41.7 us
  other arithmetic: 15.5 us -> 18.1 us
    concatenate x0 -> x3, other arithmetic: none -> 2.15 us  [local(): jnp.concatenate([pick(v[0], z).reshape(-1, 2 * owned), lax.dynamic_index_...]
    dynamic_slice x0 -> x2, local copies, waits for them, and re-layouts: none -> 1.99 us  [the longest x1 1.97 us: local(): lax.dynamic_index_in_dim(v[1], z, 1, keepdims=False).reshape(-1, 2 * owned)]
    ppermute x6, waiting for transfers between devices: 27.2 us -> 25.4 us  [share_z(): lax.ppermute(pick(slabs, (me + k) % 4), 'z', [(i, (i + k) % 4) for i in r...]
  transfers between devices with their start and end apart: 20 -> 20, of which waited for: 10 -> 10; matrix products, arithmetic and copies ran while one was open for 15% -> 17% of each run, Pallas kernels for 37% -> 36%
where the time goes in v18:
time: 169 us; the launch traced here: 167 us
  Pallas kernels  60.6 us (36%)
  waiting for transfers between devices  41.7 us (25%)
  starting transfers between devices  29.9 us (18%)
  other arithmetic  18.1 us (11%)
  local copies, waits for them, and re-layouts  14.8 us (9%)
  between operations  1.69 us (1%)
    pallas_call x3, Pallas kernels, project(): pl.pallas_call(functools.partial(dot_kernel, len(cols)), grid=(size, inne...  29.7 us
    ppermute x6, waiting for transfers between devices, share_z(): lax.ppermute(pick(slabs, (me + k) % 4), 'z', [(i, (i + k) % 4) for i in r...  25.4 us
    pallas_call x3, Pallas kernels, by_time(): pl.pallas_call(functools.partial(by_time_kernel, cuts), in_specs=[ANY] *...  22.7 us
    ppermute x6, starting transfers between devices, share_z(): lax.ppermute(pick(slabs, (me + k) % 4), 'z', [(i, (i + k) % 4) for i in r...  11.8 us
    ppermute x6, starting transfers between devices, sum_x(): total = total + lax.ppermute(pick(slabs, (me + k) % 4), 'x', pairs)  10.8 us
    ppermute x8, waiting for transfers between devices, swap(): return lax.ppermute(value, axis, SWAP)  9.17 us
    ppermute x8, starting transfers between devices, swap(): return lax.ppermute(value, axis, SWAP)  7.3 us
    ppermute x6, waiting for transfers between devices, sum_x(): total = total + lax.ppermute(pick(slabs, (me + k) % 4), 'x', pairs)  7.19 us
  transfers between devices with their start and end apart: 20, of which 10 were waited for; matrix products, arithmetic and copies ran while one was open for 17% of the time, Pallas kernels for 36%

profile of v18, /device:TPU:0, one launch (start us, length us, event | category | flops | bytes accessed | tf_op | source)
XLA Modules:
  0.0 166.8 jit_solution(1407793294608771006)
XLA Ops:
  0.7 5.1 %by_time.3 = (bf16[3,4,2,6,32,512]{5,4,3,2,1,0:T(8,128)(2,1)}, bf16[1,4,2,6,32,512]{5,4,3,2,1,0:T(8,128)(2,1)}) custom-call(bf16[32,6,32,512]{3,2,1,0:T(8,128)(2,1)} %bitcast.136), custom_call_target="tpu_custom_call" | custom-call | flops 1000 | bytes 1000 | tf_op jit(solution)/shard_map/by_time/pallas_call | solution.py:52
  5.8 1.7 %collective-permute-start.4 = (bf16[3,8,3,64,512]{4,3,2,1,0:T(8,128)(2,1)}, bf16[3,8,3,64,512]{4,3,2,1,0:T(8,128)(2,1)}, u32[]{:S(2)}, u32[]{:S(2)}) collective-permute-start(bf16[3,8,3,64,512]{4,3,2,1,0:T(8,128)(2,1)} %bitcast.127), channel_id=1, source_target_pairs={{0,64},{64,0},{1,65},{65,1},{2,66},{66,2},{3,67},{67,3},{4,68},{68... | collective-permute-start | bytes 14155784 | tf_op jit(solution)/shard_map/ppermute | solution.py:17
  7.5 9.3 %by_time.4 = (bf16[4,4,2,6,64,512]{5,4,3,2,1,0:T(8,128)(2,1)}, bf16[1,4,2,6,64,512]{5,4,3,2,1,0:T(8,128)(2,1)}) custom-call(bf16[64,6,32,512]{3,2,1,0:T(8,128)(2,1)} %bitcast.125, bf16[3,8,3,64,512]{4,3,2,1,0:T(8,128)(2,1)} %bitcast.128), custom_call_target="tpu_custom_call" | custom-call | flops 1000 | bytes 1000 | tf_op jit(solution)/shard_map/by_time/pallas_call | solution.py:52
  16.9 3.2 %fusion.2 = (bf16[1,2,3,192,512]{4,3,2,1,0:T(8,128)(2,1)S(1)}, bf16[2,3,192,512]{3,2,1,0:T(8,128)(2,1)}, bf16[2,3,192,512]{3,2,1,0:T(8,128)(2,1)}, bf16[2,3,192,512]{3,2,1,0:T(8,128)(2,1)}) fusion(s32[]{:T(128)S(6)} %select_n.139, bf16[4,2,3,128,512]{4,3,2,1,0:T(8,128)(2,1)} %bitcast.139, bf16[4,2,3,64,512]{4,3,2,1,0:T(8,128)(2,1)S(1)} %bitcast.135, ...), kind=kLoop, calls=%fused_computation.20 | loop fusion | flops 9437184 | bytes 9437200 | tf_op jit(solution)/shard_map/concatenate | solution.py:281
  20.1 1.9 %collective-permute-start.8 = (bf16[2,3,192,512]{3,2,1,0:T(8,128)(2,1)}, bf16[2,3,192,512]{3,2,1,0:T(8,128)(2,1)S(1)}, u32[]{:S(2)}, u32[]{:S(2)}) collective-permute-start(bf16[2,3,192,512]{3,2,1,0:T(8,128)(2,1)} %get-tuple-element.17), channel_id=1, source_target_pairs={{0,8},{8,16},{16,24},{24,0},{1,9},{9,17},{17,25},{25,1},{2,10},{10... | collective-permute-start | bytes 3538952 | tf_op jit(solution)/shard_map/ppermute | solution.py:230
  22.0 2.2 %collective-permute-start.9 = (bf16[2,3,192,512]{3,2,1,0:T(8,128)(2,1)}, bf16[2,3,192,512]{3,2,1,0:T(8,128)(2,1)}, u32[]{:S(2)}, u32[]{:S(2)}) collective-permute-start(bf16[2,3,192,512]{3,2,1,0:T(8,128)(2,1)} %get-tuple-element.18), channel_id=1, source_target_pairs={{0,24},{8,0},{16,8},{24,16},{1,25},{9,1},{17,9},{25,17},{2,26},{10... | collective-permute-start | bytes 3538952 | tf_op jit(solution)/shard_map/ppermute | solution.py:230
  24.2 1.8 %collective-permute-start.10 = (bf16[2,3,192,512]{3,2,1,0:T(8,128)(2,1)}, bf16[2,3,192,512]{3,2,1,0:T(8,128)(2,1)}, u32[]{:S(2)}, u32[]{:S(2)}) collective-permute-start(bf16[2,3,192,512]{3,2,1,0:T(8,128)(2,1)} %get-tuple-element.19), channel_id=1, source_target_pairs={{0,16},{8,24},{16,0},{24,8},{1,17},{9,25},{17,1},{25,9},{2,18},{10... | collective-permute-start | bytes 3538952 | tf_op jit(solution)/shard_map/ppermute | solution.py:230
  26.0 8.4 %by_time.5 = bf16[4,4,2,6,64,512]{5,4,3,2,1,0:T(8,128)(2,1)} custom-call(bf16[64,6,32,512]{3,2,1,0:T(8,128)(2,1)} %collective-permute-done.block), custom_call_target="tpu_custom_call" | custom-call | flops 1000 | bytes 1000 | tf_op jit(solution)/shard_map/by_time/pallas_call | solution.py:52
  34.4 11.8 %project.3 = f32[3,8,2,32,128]{4,3,2,1,0:T(8,128)} custom-call(bf16[3,8,3,64,512]{4,3,2,1,0:T(8,128)(2,1)} %bitcast.129, bf16[4,8,3,128,512]{4,3,2,1,0:T(8,128)(2,1)} %bitcast.121, bf16[4,8,3,128,512]{4,3,2,1,0:T(8,128)(2,1)} %bitcast.118), custom_call_target="tpu_custom_call" | custom-call | flops 1000 | bytes 1000 | tf_op jit(solution)/shard_map/project/pallas_call | solution.py:211
  46.2 6.2 %project.4 = f32[1,8,2,32,128]{4,3,2,1,0:T(8,128)} custom-call(bf16[1,8,3,64,512]{4,3,2,1,0:T(8,128)(2,1)} %bitcast.134, bf16[4,8,3,128,512]{4,3,2,1,0:T(8,128)(2,1)} %bitcast.122, bf16[4,8,3,128,512]{4,3,2,1,0:T(8,128)(2,1)} %bitcast.119), custom_call_target="tpu_custom_call" | custom-call | flops 1000 | bytes 1000 | tf_op jit(solution)/shard_map/project/pallas_call | solution.py:211
  52.3 1.4 slice.109
  53.7 1.4 slice.108
  55.1 1.0 copy-done.3
  56.1 19.3 %collective-permute-done.9 = bf16[2,3,192,512]{3,2,1,0:T(8,128)(2,1)} collective-permute-done((bf16[2,3,192,512]{3,2,1,0:T(8,128)(2,1)}, bf16[2,3,192,512]{3,2,1,0:T(8,128)(2,1)}, u32[]{:S(2)}, u32[]{:S(2)}) %collective-permute-start.9) | collective-permute-done | bytes 1179680 | tf_op jit(solution)/shard_map/ppermute | solution.py:230
  75.4 1.8 %collective-permute-done.10 = bf16[2,3,192,512]{3,2,1,0:T(8,128)(2,1)} collective-permute-done((bf16[2,3,192,512]{3,2,1,0:T(8,128)(2,1)}, bf16[2,3,192,512]{3,2,1,0:T(8,128)(2,1)}, u32[]{:S(2)}, u32[]{:S(2)}) %collective-permute-start.10) | collective-permute-done | bytes 1179680 | tf_op jit(solution)/shard_map/ppermute | solution.py:230
  77.2 2.3 %pad_maximum_fusion = bf16[4,2,3,192,512]{4,3,2,1,0:T(8,128)(2,1)S(1)} fusion(bf16[1,2,3,192,512]{4,3,2,1,0:T(8,128)(2,1)} %bitcast.41, bf16[1,2,3,192,512]{4,3,2,1,0:T(8,128)(2,1)} %bitcast.39, bf16[1,2,3,192,512]{4,3,2,1,0:T(8,128)(2,1)} %bitcast.130, bf16[1,2,3,192,512]{4,3,2,1,0:T(8,128)(2,1)S(1)} %get-tuple-element.16), kind=kLoop, calls=%fused_computation.9 | loop fusion | flops 7077888 | bytes 9437184 | tf_op jit(solution)/shard_map/stack | solution.py:284
  79.5 0.3 slice.113.own
  80.8 0.6 gather_fusion
  81.5 2.3 %slice.110 = bf16[1,4,2,6,64,512]{5,4,3,2,1,0:T(8,128)(2,1)S(1)} slice(bf16[4,4,2,6,64,512]{5,4,3,2,1,0:T(8,128)(2,1)} %by_time.5), slice={[0:1], [0:4], [0:2], [0:6], [0:64], [0:512]} | slice | bytes 6291456 | tf_op jit(solution)/shard_map/slice | solution.py:78
  83.9 1.0 fusion.15
  84.8 1.5 collective-permute-start.1
  86.3 1.7 %collective-permute-start.2 = (f32[4,2,64,128]{3,2,1,0:T(8,128)}, f32[4,2,64,128]{3,2,1,0:T(8,128)}, u32[]{:S(2)}, u32[]{:S(2)}) collective-permute-start(f32[4,2,64,128]{3,2,1,0:T(8,128)} %get-tuple-element.21), channel_id=1, source_target_pairs={{0,6},{2,0},{4,2},{6,4},{1,7},{3,1},{5,3},{7,5},{8,14},{10,8},{12,... | collective-permute-start | bytes 786440 | tf_op jit(solution)/shard_map/ppermute | solution.py:246
  88.1 1.8 %collective-permute-start.3 = (f32[4,2,64,128]{3,2,1,0:T(8,128)}, f32[4,2,64,128]{3,2,1,0:T(8,128)}, u32[]{:S(2)}, u32[]{:S(2)}) collective-permute-start(f32[4,2,64,128]{3,2,1,0:T(8,128)} %get-tuple-element.22), channel_id=1, source_target_pairs={{0,4},{2,6},{4,0},{6,2},{1,5},{3,7},{5,1},{7,3},{8,12},{10,14},{12... | collective-permute-start | bytes 786440 | tf_op jit(solution)/shard_map/ppermute | solution.py:246
  89.9 0.7 slice_bitcast_fusion.after
  90.5 2.4 %choose.1 = bf16[4,8,512]{2,1,0:T(8,128)(2,1)} custom-call(s32[4]{0:T(128)} %index.1, s32[1]{0:T(128)S(6)} %copy.37.when, bf16[64,6,32,512]{3,2,1,0:T(8,128)(2,1)} %bitcast.126, bf16[128,512]{1,0:T(8,128)(2,1)} %slice_bitcast_fusion.after), custom_call_target="tpu_custom_call" | custom-call | flops 1000 | bytes 1000 | tf_op jit(solution)/shard_map/choose/pallas_call | solution.py:122
  93.0 2.5 %pad_maximum_fusion.2 = (bf16[4,1,3,64,512]{4,3,2,1,0:T(8,128)(2,1)}, bf16[4,1,3,64,512]{4,3,2,1,0:T(8,128)(2,1)S(1)}) fusion(bf16[1,2,3,192,512]{4,3,2,1,0:T(8,128)(2,1)} %bitcast.41, bf16[1,2,3,192,512]{4,3,2,1,0:T(8,128)(2,1)} %bitcast.39, bf16[1,2,3,192,512]{4,3,2,1,0:T(8,128)(2,1)} %bitcast.131, bf16[1,2,3,192,512]{4,3,2,1,0:T(8,128)(2,1)} %copy-done.2), kind=kLoop, calls=%fused_computation.26 | loop fusion | flops 6291456 | bytes 6291456 | tf_op jit(solution)/shard_map/slice | solution.py:288
  95.4 1.0 pad_maximum_fusion.1.refs_0_
  96.5 3.4 %collective-permute-done.2 = f32[4,2,64,128]{3,2,1,0:T(8,128)} collective-permute-done((f32[4,2,64,128]{3,2,1,0:T(8,128)}, f32[4,2,64,128]{3,2,1,0:T(8,128)}, u32[]{:S(2)}, u32[]{:S(2)}) %collective-permute-start.2) | collective-permute-done | bytes 262176 | tf_op jit(solution)/shard_map/ppermute | solution.py:246
  99.9 1.7 %collective-permute-done.3 = f32[4,2,64,128]{3,2,1,0:T(8,128)} collective-permute-done((f32[4,2,64,128]{3,2,1,0:T(8,128)}, f32[4,2,64,128]{3,2,1,0:T(8,128)}, u32[]{:S(2)}, u32[]{:S(2)}) %collective-permute-start.3) | collective-permute-done | bytes 262176 | tf_op jit(solution)/shard_map/ppermute | solution.py:246
  101.6 1.2 fusion.13
  102.8 0.7 copy-done.8
  103.5 0.6 slice_bitcast_fusion.2.refs_1_
  104.1 0.2 fusion.28
  104.3 0.7 collective-permute-start.11
  105.0 5.8 %collective-permute-done.4.refs_0_ = bf16[3,8,3,64,512]{4,3,2,1,0:T(8,128)(2,1)} collective-permute-done((bf16[3,8,3,64,512]{4,3,2,1,0:T(8,128)(2,1)}, bf16[3,8,3,64,512]{4,3,2,1,0:T(8,128)(2,1)}, u32[]{:S(2)}, u32[]{:S(2)}) %collective-permute-start.4) | collective-permute-done | bytes 4718624 | tf_op jit(solution)/shard_map/ppermute | solution.py:17
  110.8 11.8 %project.5 = f32[3,8,2,32,128]{4,3,2,1,0:T(8,128)} custom-call(bf16[3,8,3,64,512]{4,3,2,1,0:T(8,128)(2,1)} %collective-permute-done.4.refs_0_, bf16[4,8,3,128,512]{4,3,2,1,0:T(8,128)(2,1)} %bitcast.123, bf16[4,8,3,128,512]{4,3,2,1,0:T(8,128)(2,1)} %bitcast.120), custom_call_target="tpu_custom_call" | custom-call | flops 1000 | bytes 1000 | tf_op jit(solution)/shard_map/project/pallas_call | solution.py:211
  122.6 1.4 slice.116
  123.9 1.7 collective-permute-start.13
  125.6 2.0 %constant_dynamic-slice_fusion.7 = (f32[3,1,2,64,128]{4,3,2,1,0:T(8,128)}, f32[3,1,2,64,128]{4,3,2,1,0:T(8,128)S(1)}, f32[3,1,2,64,128]{4,3,2,1,0:T(8,128)S(1)}, f32[3,1,2,64,128]{4,3,2,1,0:T(8,128)S(1)}) fusion(f32[3,4,2,64,128]{4,3,2,1,0:T(8,128)} %bitcast.138, s32[]{:T(128)S(6)} %select_n.139, s32[]{:T(128)S(6)} %select_n.143, s32[]{:T(128)S(6)} %select_n.141, ...), kind=kLoop, calls=%fused_computation.77 | loop fusion | bytes 1572880 | tf_op jit(solution)/shard_map/jit(dynamic_index_in_dim)/dynamic_slice | solution.py:301
  127.6 0.7 pad_maximum_fusion.4
  128.3 1.9 %collective-permute-start.5 = (f32[512,128]{1,0:T(8,128)}, f32[512,128]{1,0:T(8,128)}, u32[]{:S(2)}, u32[]{:S(2)}) collective-permute-start(f32[512,128]{1,0:T(8,128)} %pad_maximum_fusion.4), channel_id=1, source_target_pairs={{0,8},{8,16},{16,24},{24,0},{1,9},{9,17},{17,25},{25,1},{2,10},{10... | collective-permute-start | bytes 786440 | tf_op jit(solution)/shard_map/ppermute | solution.py:230
  130.2 0.7 pad_maximum_fusion.5
  131.0 2.1 %collective-permute-start.6 = (f32[512,128]{1,0:T(8,128)}, f32[512,128]{1,0:T(8,128)}, u32[]{:S(2)}, u32[]{:S(2)}) collective-permute-start(f32[512,128]{1,0:T(8,128)} %pad_maximum_fusion.5), channel_id=1, source_target_pairs={{0,24},{8,0},{16,8},{24,16},{1,25},{9,1},{17,9},{25,17},{2,26},{10... | collective-permute-start | bytes 786440 | tf_op jit(solution)/shard_map/ppermute | solution.py:230
  133.1 0.7 pad_maximum_fusion.6
  133.8 1.9 %collective-permute-start.7 = (f32[512,128]{1,0:T(8,128)}, f32[512,128]{1,0:T(8,128)S(1)}, u32[]{:S(2)}, u32[]{:S(2)}) collective-permute-start(f32[512,128]{1,0:T(8,128)} %pad_maximum_fusion.6), channel_id=1, source_target_pairs={{0,16},{8,24},{16,0},{24,8},{1,17},{9,25},{17,1},{25,9},{2,18},{10... | collective-permute-start | bytes 786440 | tf_op jit(solution)/shard_map/ppermute | solution.py:230
  135.7 1.4 fusion.27
  137.1 2.9 %project_pieces.2.refs_1_.refs_0_ = f32[2,32,128]{2,1,0:T(8,128)S(1)} custom-call(bf16[25,32,512]{2,1,0:T(8,128)(2,1)} %collective-permute-done.11.col, bf16[4,2,3,128,512]{4,3,2,1,0:T(8,128)(2,1)S(1)} %slice.113.own, bf16[4,2,3,128,512]{4,3,2,1,0:T(8,128)(2,1)} %collective-permute-done.12.other), custom_call_target="tpu_custom_call" | custom-call | flops 1000 | bytes 1000 | tf_op jit(solution)/shard_map/project_pieces/pallas_call | solution.py:188
  140.0 0.6 copy-done
  140.6 4.2 %collective-permute-done.7.refs_0_ = f32[512,128]{1,0:T(8,128)S(1)} collective-permute-done((f32[512,128]{1,0:T(8,128)}, f32[512,128]{1,0:T(8,128)S(1)}, u32[]{:S(2)}, u32[]{:S(2)}) %collective-permute-start.7) | collective-permute-done | bytes 262176 | tf_op jit(solution)/shard_map/ppermute | solution.py:230
  144.9 0.7 copy-done.10
  145.6 1.2 fusion.19
  146.8 2.9 %project_pieces.3 = f32[2,32,128]{2,1,0:T(8,128)S(1)} custom-call(bf16[24,32,512]{2,1,0:T(8,128)(2,1)} %collective-permute-done.13.col, bf16[4,2,3,128,512]{4,3,2,1,0:T(8,128)(2,1)S(1)} %slice.113.own, bf16[4,2,3,128,512]{4,3,2,1,0:T(8,128)(2,1)} %collective-permute-done.12.other, f32[2,32,128]{2,1,0:T(8,128)S(1)} %copy-done.1), custom_call_target="tpu_custom_call" | custom-call | flops 1000 | bytes 1000 | tf_op jit(solution)/shard_map/project_pieces/pallas_call | solution.py:188
  149.8 1.6 collective-permute-start.14
  151.3 2.7 %collective-permute-start.16 = (f32[2,64,128]{2,1,0:T(8,128)S(1)}, f32[2,64,128]{2,1,0:T(8,128)S(1)}, u32[]{:S(2)}, u32[]{:S(2)}) collective-permute-start(f32[2,64,128]{2,1,0:T(8,128)S(1)} %get-tuple-element.28), channel_id=1, source_target_pairs={{0,4},{2,6},{4,0},{6,2},{1,5},{3,7},{5,1},{7,3},{8,12},{10,14},{12... | collective-permute-start | bytes 196616 | tf_op jit(solution)/shard_map/ppermute | solution.py:246
  154.1 1.4 collective-permute-start.15
  155.5 0.8 add_bitcast_fusion
  156.3 0.8 collective-permute-done.16
  157.1 1.2 collective-permute-done.15
  158.4 3.0 %collective-permute-start.17 = (f32[128,128]{1,0:T(8,128)S(1)}, f32[128,128]{1,0:T(8,128)S(1)}, u32[]{:S(2)}, u32[]{:S(2)}) collective-permute-start(f32[128,128]{1,0:T(8,128)S(1)} %fusion.21), channel_id=1, source_target_pairs={{0,1},{1,0},{2,3},{3,2},{4,5},{5,4},{6,7},{7,6},{8,9},{9,8},{10,11... | collective-permute-start | bytes 196616 | tf_op jit(solution)/shard_map/ppermute | solution.py:17
  161.3 0.7 broadcast_select_fusion
  162.1 2.1 %collective-permute-done.17 = f32[128,128]{1,0:T(8,128)S(1)} collective-permute-done((f32[128,128]{1,0:T(8,128)S(1)}, f32[128,128]{1,0:T(8,128)S(1)}, u32[]{:S(2)}, u32[]{:S(2)}) %collective-permute-start.17) | collective-permute-done | bytes 65568 | tf_op jit(solution)/shard_map/ppermute | solution.py:17
  164.3 1.2 collective-permute-done.18
  165.7 0.2 select_reduce_fusion
  166.1 0.7 copy.28
  (60 shorter events, 1.1 us)
Async XLA Ops:
  0.6 25.3 %collective-permute-start = (bf16[64,6,32,512]{3,2,1,0:T(8,128)(2,1)}, bf16[64,6,32,512]{3,2,1,0:T(8,128)(2,1)}, u32[]{:S(2)}, u32[]{:S(2)}) collective-permute-start(bf16[64,6,32,512]{3,2,1,0:T(8,128)(2,1)} %bitcast.124), channel_id=1, source_target_pairs={{0,32},{32,0},{1,33},{33,1},{2,34},{34,2},{3,35},{35,3},{4,36},{36... | collective-permute-start | bytes 37748744 | tf_op jit(solution)/shard_map/ppermute | solution.py:17
  5.8 11.1 %copy-start.5 = (bf16[1,4,2,6,32,512]{5,4,3,2,1,0:T(8,128)(2,1)S(1)}, bf16[1,4,2,6,32,512]{5,4,3,2,1,0:T(8,128)(2,1)}, u32[]{:S(2)}) copy-start(bf16[1,4,2,6,32,512]{5,4,3,2,1,0:T(8,128)(2,1)} %get-tuple-element.8) | copy-start | bytes 4718596
  5.8 105.0 %collective-permute-start.4 = (bf16[3,8,3,64,512]{4,3,2,1,0:T(8,128)(2,1)}, bf16[3,8,3,64,512]{4,3,2,1,0:T(8,128)(2,1)}, u32[]{:S(2)}, u32[]{:S(2)}) collective-permute-start(bf16[3,8,3,64,512]{4,3,2,1,0:T(8,128)(2,1)} %bitcast.127), channel_id=1, source_target_pairs={{0,64},{64,0},{1,65},{65,1},{2,66},{66,2},{3,67},{67,3},{4,68},{68... | collective-permute-start | bytes 14155784 | tf_op jit(solution)/shard_map/ppermute | solution.py:17
  20.1 57.2 %copy-start.2 = (bf16[1,2,3,192,512]{4,3,2,1,0:T(8,128)(2,1)}, bf16[1,2,3,192,512]{4,3,2,1,0:T(8,128)(2,1)S(1)}, u32[]{:S(2)}) copy-start(bf16[1,2,3,192,512]{4,3,2,1,0:T(8,128)(2,1)S(1)} %get-tuple-element.16) | copy-start | bytes 3538948
  20.1 35.0 %collective-permute-start.8 = (bf16[2,3,192,512]{3,2,1,0:T(8,128)(2,1)}, bf16[2,3,192,512]{3,2,1,0:T(8,128)(2,1)S(1)}, u32[]{:S(2)}, u32[]{:S(2)}) collective-permute-start(bf16[2,3,192,512]{3,2,1,0:T(8,128)(2,1)} %get-tuple-element.17), channel_id=1, source_target_pairs={{0,8},{8,16},{16,24},{24,0},{1,9},{9,17},{17,25},{25,1},{2,10},{10... | collective-permute-start | bytes 3538952 | tf_op jit(solution)/shard_map/ppermute | solution.py:230
  22.0 53.4 %collective-permute-start.9 = (bf16[2,3,192,512]{3,2,1,0:T(8,128)(2,1)}, bf16[2,3,192,512]{3,2,1,0:T(8,128)(2,1)}, u32[]{:S(2)}, u32[]{:S(2)}) collective-permute-start(bf16[2,3,192,512]{3,2,1,0:T(8,128)(2,1)} %get-tuple-element.18), channel_id=1, source_target_pairs={{0,24},{8,0},{16,8},{24,16},{1,25},{9,1},{17,9},{25,17},{2,26},{10... | collective-permute-start | bytes 3538952 | tf_op jit(solution)/shard_map/ppermute | solution.py:230
  24.2 53.0 %collective-permute-start.10 = (bf16[2,3,192,512]{3,2,1,0:T(8,128)(2,1)}, bf16[2,3,192,512]{3,2,1,0:T(8,128)(2,1)}, u32[]{:S(2)}, u32[]{:S(2)}) collective-permute-start(bf16[2,3,192,512]{3,2,1,0:T(8,128)(2,1)} %get-tuple-element.19), channel_id=1, source_target_pairs={{0,16},{8,24},{16,0},{24,8},{1,17},{9,25},{17,1},{25,9},{2,18},{10... | collective-permute-start | bytes 3538952 | tf_op jit(solution)/shard_map/ppermute | solution.py:230
  55.1 1.0 copy-start.3
  79.5 1.1 copy-start.12
  79.8 57.3 %collective-permute-start.12 = (bf16[4,2,3,128,512]{4,3,2,1,0:T(8,128)(2,1)S(1)}, bf16[4,2,3,128,512]{4,3,2,1,0:T(8,128)(2,1)}, u32[]{:S(2)}, u32[]{:S(2)}) collective-permute-start(bf16[4,2,3,128,512]{4,3,2,1,0:T(8,128)(2,1)S(1)} %slice.113.own), channel_id=1, source_target_pairs={{0,32},{32,0},{1,33},{33,1},{2,34},{34,2},{3,35},{35,3},{4,36},{36... | collective-permute-start | bytes 9437192 | tf_op jit(solution)/shard_map/ppermute | solution.py:17
  81.5 2.3 %copy-start.4 = (f32[3,8,2,32,128]{4,3,2,1,0:T(8,128)S(1)}, f32[3,8,2,32,128]{4,3,2,1,0:T(8,128)}, u32[]{:S(2)}) copy-start(f32[3,8,2,32,128]{4,3,2,1,0:T(8,128)} %project.3) | copy-start | bytes 2359300
  81.5 2.3 %copy-start.6 = (f32[1,8,2,32,128]{4,3,2,1,0:T(8,128)S(1)}, f32[1,8,2,32,128]{4,3,2,1,0:T(8,128)}, u32[]{:S(2)}) copy-start(f32[1,8,2,32,128]{4,3,2,1,0:T(8,128)} %project.4) | copy-start | bytes 786436
  84.8 11.7 %collective-permute-start.1 = (f32[4,2,64,128]{3,2,1,0:T(8,128)}, f32[4,2,64,128]{3,2,1,0:T(8,128)}, u32[]{:S(2)}, u32[]{:S(2)}) collective-permute-start(f32[4,2,64,128]{3,2,1,0:T(8,128)} %get-tuple-element.20), channel_id=1, source_target_pairs={{0,2},{2,4},{4,6},{6,0},{1,3},{3,5},{5,7},{7,1},{8,10},{10,12},{12... | collective-permute-start | bytes 786440 | tf_op jit(solution)/shard_map/ppermute | solution.py:246
  86.3 13.6 %collective-permute-start.2 = (f32[4,2,64,128]{3,2,1,0:T(8,128)}, f32[4,2,64,128]{3,2,1,0:T(8,128)}, u32[]{:S(2)}, u32[]{:S(2)}) collective-permute-start(f32[4,2,64,128]{3,2,1,0:T(8,128)} %get-tuple-element.21), channel_id=1, source_target_pairs={{0,6},{2,0},{4,2},{6,4},{1,7},{3,1},{5,3},{7,5},{8,14},{10,8},{12,... | collective-permute-start | bytes 786440 | tf_op jit(solution)/shard_map/ppermute | solution.py:246
  88.1 13.6 %collective-permute-start.3 = (f32[4,2,64,128]{3,2,1,0:T(8,128)}, f32[4,2,64,128]{3,2,1,0:T(8,128)}, u32[]{:S(2)}, u32[]{:S(2)}) collective-permute-start(f32[4,2,64,128]{3,2,1,0:T(8,128)} %get-tuple-element.22), channel_id=1, source_target_pairs={{0,4},{2,6},{4,0},{6,2},{1,5},{3,7},{5,1},{7,3},{8,12},{10,14},{12... | collective-permute-start | bytes 786440 | tf_op jit(solution)/shard_map/ppermute | solution.py:246
  92.9 2.5 %copy-start.11 = (bf16[4,8,512]{2,1,0:T(8,128)(2,1)S(1)}, bf16[4,8,512]{2,1,0:T(8,128)(2,1)}, u32[]{:S(2)}) copy-start(bf16[4,8,512]{2,1,0:T(8,128)(2,1)} %choose.1) | copy-start | bytes 98308
  95.4 6.2 %copy-start.7 = (f32[1,8,2,32,128]{4,3,2,1,0:T(8,128)S(1)}, f32[1,8,2,32,128]{4,3,2,1,0:T(8,128)}, u32[]{:S(2)}) copy-start(f32[1,8,2,32,128]{4,3,2,1,0:T(8,128)} %project.4) | copy-start | bytes 786436
  102.8 0.7 copy-start.8
  104.3 29.5 %collective-permute-start.11 = (bf16[25,32,512]{2,1,0:T(8,128)(2,1)}, bf16[25,32,512]{2,1,0:T(8,128)(2,1)}, u32[]{:S(2)}, u32[]{:S(2)}) collective-permute-start(bf16[25,32,512]{2,1,0:T(8,128)(2,1)} %hold.5), channel_id=1, source_target_pairs={{0,64},{64,0},{1,65},{65,1},{2,66},{66,2},{3,67},{67,3},{4,68},{68... | collective-permute-start | bytes 2457608 | tf_op jit(solution)/shard_map/ppermute | solution.py:17
  123.9 3.6 %copy-start.9 = (f32[4,2,64,128]{3,2,1,0:T(8,128)S(1)}, f32[4,2,64,128]{3,2,1,0:T(8,128)}, u32[]{:S(2)}) copy-start(f32[4,2,64,128]{3,2,1,0:T(8,128)} %copy-done.8) | copy-start | bytes 786436
  123.9 22.9 %collective-permute-start.13 = (bf16[24,32,512]{2,1,0:T(8,128)(2,1)}, bf16[24,32,512]{2,1,0:T(8,128)(2,1)}, u32[]{:S(2)}, u32[]{:S(2)}) collective-permute-start(bf16[24,32,512]{2,1,0:T(8,128)(2,1)} %hold.7), channel_id=1, source_target_pairs={{0,64},{64,0},{1,65},{65,1},{2,66},{66,2},{3,67},{67,3},{4,68},{68... | collective-permute-start | bytes 2359304 | tf_op jit(solution)/shard_map/ppermute | solution.py:17
  128.3 17.2 %collective-permute-start.5 = (f32[512,128]{1,0:T(8,128)}, f32[512,128]{1,0:T(8,128)}, u32[]{:S(2)}, u32[]{:S(2)}) collective-permute-start(f32[512,128]{1,0:T(8,128)} %pad_maximum_fusion.4), channel_id=1, source_target_pairs={{0,8},{8,16},{16,24},{24,0},{1,9},{9,17},{17,25},{25,1},{2,10},{10... | collective-permute-start | bytes 786440 | tf_op jit(solution)/shard_map/ppermute | solution.py:230
  131.0 14.6 %collective-permute-start.6 = (f32[512,128]{1,0:T(8,128)}, f32[512,128]{1,0:T(8,128)}, u32[]{:S(2)}, u32[]{:S(2)}) collective-permute-start(f32[512,128]{1,0:T(8,128)} %pad_maximum_fusion.5), channel_id=1, source_target_pairs={{0,24},{8,0},{16,8},{24,16},{1,25},{9,1},{17,9},{25,17},{2,26},{10... | collective-permute-start | bytes 786440 | tf_op jit(solution)/shard_map/ppermute | solution.py:230
  133.8 11.1 %collective-permute-start.7 = (f32[512,128]{1,0:T(8,128)}, f32[512,128]{1,0:T(8,128)S(1)}, u32[]{:S(2)}, u32[]{:S(2)}) collective-permute-start(f32[512,128]{1,0:T(8,128)} %pad_maximum_fusion.6), channel_id=1, source_target_pairs={{0,16},{8,24},{16,0},{24,8},{1,17},{9,25},{17,1},{25,9},{2,18},{10... | collective-permute-start | bytes 786440 | tf_op jit(solution)/shard_map/ppermute | solution.py:230
  137.1 18.4 %collective-permute-start.19 = (bf16[32,512]{1,0:T(8,128)(2,1)}, bf16[32,512]{1,0:T(8,128)(2,1)S(1)}, u32[]{:S(2)}, u32[]{:S(2)}) collective-permute-start(bf16[32,512]{1,0:T(8,128)(2,1)} %fusion.27), channel_id=1, source_target_pairs={{0,32},{32,0},{1,33},{33,1},{2,34},{34,2},{3,35},{35,3},{4,36},{36... | collective-permute-start | bytes 98312 | tf_op jit(solution)/shard_map/ppermute | solution.py:17
  140.0 0.6 copy-start
  144.9 0.7 copy-start.10
  145.6 1.3 copy-start.1
  149.8 6.5 %collective-permute-start.14 = (f32[2,64,128]{2,1,0:T(8,128)S(1)}, f32[2,64,128]{2,1,0:T(8,128)S(1)}, u32[]{:S(2)}, u32[]{:S(2)}) collective-permute-start(f32[2,64,128]{2,1,0:T(8,128)S(1)} %get-tuple-element.27), channel_id=1, source_target_pairs={{0,2},{2,4},{4,6},{6,0},{1,3},{3,5},{5,7},{7,1},{8,10},{10,12},{12... | collective-permute-start | bytes 196616 | tf_op jit(solution)/shard_map/ppermute | solution.py:246
  151.3 5.8 %collective-permute-start.16 = (f32[2,64,128]{2,1,0:T(8,128)S(1)}, f32[2,64,128]{2,1,0:T(8,128)S(1)}, u32[]{:S(2)}, u32[]{:S(2)}) collective-permute-start(f32[2,64,128]{2,1,0:T(8,128)S(1)} %get-tuple-element.28), channel_id=1, source_target_pairs={{0,4},{2,6},{4,0},{6,2},{1,5},{3,7},{5,1},{7,3},{8,12},{10,14},{12... | collective-permute-start | bytes 196616 | tf_op jit(solution)/shard_map/ppermute | solution.py:246
  154.1 4.3 %collective-permute-start.15 = (f32[2,64,128]{2,1,0:T(8,128)S(1)}, f32[2,64,128]{2,1,0:T(8,128)S(1)}, u32[]{:S(2)}, u32[]{:S(2)}) collective-permute-start(f32[2,64,128]{2,1,0:T(8,128)S(1)} %get-tuple-element.29), channel_id=1, source_target_pairs={{0,6},{2,0},{4,2},{6,4},{1,7},{3,1},{5,3},{7,5},{8,14},{10,8},{12,... | collective-permute-start | bytes 196616 | tf_op jit(solution)/shard_map/ppermute | solution.py:246
  158.4 5.8 %collective-permute-start.17 = (f32[128,128]{1,0:T(8,128)S(1)}, f32[128,128]{1,0:T(8,128)S(1)}, u32[]{:S(2)}, u32[]{:S(2)}) collective-permute-start(f32[128,128]{1,0:T(8,128)S(1)} %fusion.21), channel_id=1, source_target_pairs={{0,1},{1,0},{2,3},{3,2},{4,5},{5,4},{6,7},{7,6},{8,9},{9,8},{10,11... | collective-permute-start | bytes 196616 | tf_op jit(solution)/shard_map/ppermute | solution.py:17
  164.2 1.3 collective-permute-start.18
